TPU v7x, 32 devices: a whole 2x2x4 slice. The times are simulated.
32 devices in a mesh: dp: 4 (over x, core), ctx: 8 (over z, y).
Axes of the slice: x: 2, y: 2, z: 4, core: 2. Of those that a mesh axis runs over, the one named last changes fastest.
Arguments:
- activations: bfloat16 [4096, 4096], P(('dp', 'ctx')), parts along dimension 0
- routed: int32 [512], P('dp'), parts along dimension 0, may hold values from 0 to 1023, as said below
- balance: int32 [512], P('dp'), parts along dimension 0, may hold values from 0 to 7, as said below
- w_query: bfloat16 [4096, 4096], P(None, 'ctx')
- w_key: bfloat16 [4096, 1024], P(None, 'ctx')
- w_value: bfloat16 [4096, 1024], P(None, 'ctx'), may hold values from -0.09375 to 0.09375
- w_output: bfloat16 [4096, 4096], P('ctx'), may hold values from -0.09375 to 0.09375
- attn_gain: float32 [4096], replicated, may hold values from 0.25 to 1.75
- mlp_gain: float32 [4096], replicated, may hold values from 0.25 to 1.75
- w_gate: bfloat16 [4096, 8192], P(None, 'ctx'), may hold values from -0.09375 to 0.09375
- w_up: bfloat16 [4096, 8192], P(None, 'ctx'), may hold values from -0.09375 to 0.09375
- w_down: bfloat16 [8192, 4096], P('ctx'), may hold values from -0.0625 to 0.0625
- w_router: float32 [4096], replicated, may hold values from -0.09375 to 0.09375
Outputs:
- updated: bfloat16 [512, 4096], P(('dp', 'ctx')), parts along dimension 0
There are 4 independent parts, one for each index of `dp`. A program takes and returns all parts, laid end to end along the dimension named above; an argument that names none is the same for every part. Nothing has to cross between parts.
Inputs may be any that keep to these rules, and one draw needn't show every extreme that they name: `routed`: strictly increasing positions; one device's 128 positions hold at most 32 of them, and some device's hold exactly 32. `balance`: each device index appears exactly 16 times.
All inputs are finite; a program needn't handle non-finite values.
Results may differ from a plain program's by a relative error of at most 0.015.
Values may be sent and summed in bfloat16 or wider, within the bound.
No kernel may reach another device: no remote copies, remote signals or barrier semaphores. Data moves between devices by JAX's collectives and lax.ppermute only.
A program may use at most 128 MiB of HBM per device.

v0:
```python
import jax
import jax.numpy as jnp
from jax import lax
from jax.sharding import PartitionSpec as P

HEADS = 32
KV_HEADS = 8
HEAD_DIM = 128


rope_base = 500000.0
norm_eps = 1e-05


def rms_scale(values, gain):
    mean_sq = jnp.mean(values * values, axis=-1, keepdims=True)
    return values * lax.rsqrt(mean_sq + norm_eps) * gain


def rotary(values, positions):
    half = values.shape[-1] // 2
    steps_f = jnp.arange(half, dtype=jnp.float32)
    freqs = jnp.exp(-jnp.log(jnp.float32(rope_base)) * (2.0 * steps_f / values.shape[-1]))
    angles = positions.astype(jnp.float32)[:, None] * freqs[None, :]
    cosine = jnp.cos(angles)[:, None, :]
    sine = jnp.sin(angles)[:, None, :]
    first = values[..., :half]
    second = values[..., half:]
    return jnp.concatenate(
        [first * cosine - second * sine, second * cosine + first * sine], axis=-1
    )


def on_device(
    activations,
    routed,
    balance,
    w_query,
    w_key,
    w_value,
    w_output,
    attn_gain,
    mlp_gain,
    w_gate,
    w_up,
    w_down,
    w_router,
):
    shard_count = lax.axis_size("ctx")
    my_index = lax.axis_index("ctx")
    tok_shard = activations.shape[0]
    total = routed.shape[0]
    share = total // shard_count
    capacity = 2 * share
    local_heads = w_query.shape[1] // HEAD_DIM
    group_size = HEADS // KV_HEADS
    home_shard = routed // tok_shard
    shard_ids = jnp.arange(shard_count, dtype=jnp.int32)
    onehot = (home_shard[:, None] == shard_ids[None, :]).astype(jnp.int32)
    counts = jnp.sum(onehot, axis=0)
    first_rows = jnp.cumsum(counts) - counts
    my_first = lax.dynamic_index_in_dim(first_rows, my_index, 0, keepdims=False)
    my_count = lax.dynamic_index_in_dim(counts, my_index, 0, keepdims=False)
    padded = jnp.concatenate([routed, jnp.zeros((capacity,), jnp.int32)])
    picked = lax.dynamic_slice_in_dim(padded, my_first, capacity) - my_index * tok_shard
    is_valid = jnp.arange(capacity, dtype=jnp.int32) < my_count
    picked = jnp.where(is_valid, picked, 0)
    outgoing = jnp.where(
        is_valid[:, None], jnp.take(activations, picked, axis=0), jnp.zeros((), activations.dtype)
    )
    gathered = lax.all_gather(outgoing, "ctx", axis=0, tiled=True)
    first_of_row = jnp.sum(onehot * first_rows[None, :], axis=1)
    slot_index = home_shard * capacity + jnp.arange(total, dtype=jnp.int32) - first_of_row
    owner_order = jnp.argsort(balance, stable=True)
    positions = jnp.take(routed, owner_order)
    rows_f = jnp.take(gathered, jnp.take(slot_index, owner_order), axis=0).astype(jnp.float32)
    normed = rms_scale(rows_f, attn_gain).astype(jnp.bfloat16)
    query = jnp.dot(normed, w_query, preferred_element_type=jnp.float32).reshape(
        total, local_heads, HEAD_DIM
    )
    query = rotary(query, positions).astype(jnp.bfloat16)
    key_part = jnp.dot(normed, w_key, preferred_element_type=jnp.float32).astype(jnp.bfloat16)
    value_part = jnp.dot(normed, w_value, preferred_element_type=jnp.float32).astype(jnp.bfloat16)
    key_all, value_all = (
        lax.all_gather(key_part, "ctx", axis=1, tiled=True),
        lax.all_gather(value_part, "ctx", axis=1, tiled=True),
    )
    kv_local = max(1, local_heads // group_size)
    first_kv = my_index * local_heads // group_size
    key_heads = lax.dynamic_slice_in_dim(
        key_all.reshape(total, HEAD_DIM, KV_HEADS), first_kv, kv_local, 2
    )
    value_heads = lax.dynamic_slice_in_dim(
        value_all.reshape(total, HEAD_DIM, KV_HEADS), first_kv, kv_local, 2
    )
    key_heads = jnp.transpose(key_heads, (0, 2, 1))
    value_heads = jnp.transpose(value_heads, (0, 2, 1))
    key_heads = rotary(key_heads.astype(jnp.float32), positions).astype(jnp.bfloat16)
    repeats = local_heads // kv_local
    key_heads = jnp.repeat(key_heads, repeats, axis=1)
    value_heads = jnp.repeat(value_heads, repeats, axis=1)
    block_rows = min(total, 512)
    scale = HEAD_DIM ** (-0.5)

    def attend(block_start):
        scores = (
            jnp.einsum("qhd,khd->hqk", query, key_heads, preferred_element_type=jnp.float32) * scale
        )
        allowed = positions[None, :] <= positions[:, None]
        scores = jnp.where(allowed[None], scores, -1e30)
        row_max = jnp.max(scores, axis=-1, keepdims=True)
        exp_scores = jnp.exp(scores - row_max)
        probs = (exp_scores / jnp.sum(exp_scores, axis=-1, keepdims=True)).astype(jnp.bfloat16)
        return jnp.einsum(
            "hqk,khd->qhd", probs, value_heads, preferred_element_type=jnp.float32
        ).astype(jnp.bfloat16)

    block_starts = jnp.arange(total // block_rows, dtype=jnp.int32) * block_rows
    heads_out = lax.map(attend, block_starts).reshape(total, local_heads * HEAD_DIM)
    own_rows = lax.dynamic_slice_in_dim(rows_f, my_index * share, share, 0)
    attn_all = lax.psum(
        jnp.dot(heads_out, w_output, preferred_element_type=jnp.float32).astype(jnp.bfloat16), "ctx"
    ).astype(jnp.float32)
    hidden_all = rows_f + attn_all
    piece = rms_scale(hidden_all, mlp_gain).astype(jnp.bfloat16)
    gate = jnp.dot(piece, w_gate, preferred_element_type=jnp.float32)
    upward = jnp.dot(piece, w_up, preferred_element_type=jnp.float32)
    inner = (jax.nn.silu(gate) * upward).astype(jnp.bfloat16)
    attn_own = lax.dynamic_slice_in_dim(attn_all, my_index * share, share, 0)
    piece = inner
    mlp_own = lax.psum_scatter(
        jnp.dot(piece, w_down, preferred_element_type=jnp.float32).astype(jnp.bfloat16),
        "ctx",
        scatter_dimension=0,
        tiled=True,
    ).astype(jnp.float32)
    router_score = jnp.sum(own_rows * w_router[None, :], axis=1, keepdims=True)
    return (own_rows + router_score * (attn_own + mlp_own)).astype(jnp.bfloat16)


def solution(mesh):
    in_specs = (
        P(("dp", "ctx"), None),
        P("dp"),
        P("dp"),
        P(None, "ctx"),
        P(None, "ctx"),
        P(None, "ctx"),
        P("ctx", None),
        P(),
        P(),
        P(None, "ctx"),
        P(None, "ctx"),
        P("ctx", None),
        P(),
    )
    out_specs = P(("dp", "ctx"), None)
    return jax.shard_map(
        on_device, mesh=mesh, in_specs=in_specs, out_specs=out_specs, check_vma=False
    )
```

profile of v0, /device:TPU:0, one launch (start us, length us, event | category | flops | bytes accessed | tf_op | source)
XLA Modules:
  0.0 304.7 jit_solution(5056347241776898202)
XLA Ops:
  6.5 3.3 %sort.17 = (s32[128]{0:T(128)}, s32[128]{0:T(128)S(1)}) sort(s32[128]{0:T(128)} %param.17, s32[128]{0:T(128)S(1)} %iota.25), dimensions={0}, to_apply=%region_3.4 | sort | flops 896 | bytes 2048 | tf_op jit(solution)/shard_map/jit(argsort)/sort | solution.py:74
  9.8 0.7 compare_select_fusion
  10.6 0.7 dynamic_slice.22
  11.5 0.6 dynamic_slice.23
  13.3 0.7 iota_compare_fusion.1
  14.7 1.4 compare_and_fusion.1
  16.1 0.7 gather_fusion
  16.8 0.8 select_select_fusion
  17.8 1.2 gather_fusion.3
  19.1 1.2 gather_fusion.2
  20.5 0.3 multiply_cosine_fusion.1
  20.8 49.0 %all-gather.2.cloned.1.call-done = bf16[256,4096]{1,0:T(8,128)(2,1)} async-done(((bf16[32,4096]{1,0:T(8,128)(2,1)}), bf16[256,4096]{1,0:T(8,128)(2,1)}) %all-gather.2.cloned.1.call-update) | async-done | bytes 2097168 | tf_op jit(solution)/shard_map/all_gather | solution.py:71
  69.9 4.1 %gather_fusion.1 = bf16[128,4096]{1,0:T(8,128)(2,1)S(1)} fusion(bf16[256,4096]{1,0:T(8,128)(2,1)} %all-gather.2.cloned.1.call-done, s32[1024]{0:T(1024)S(1)} %pad_clamp_fusion), kind=kCustom, calls=%fused_computation.3 | custom fusion | bytes 2097664 | tf_op jit(solution)/shard_map/jit(_take)/gather | solution.py:76
  73.9 0.4 multiply_reduce_fusion.1
  74.4 1.8 convolution_convert_fusion.3
  76.2 26.5 %all_gather.11 = bf16[128,1024]{1,0:T(8,128)(2,1)S(1)} all-gather(bf16[128,128]{1,0:T(8,128)(2,1)S(1)} %convolution_convert_fusion.3), channel_id=1, replica_groups=mesh['dp'=4,'ctx'=8] {'ctx'}, dimensions={1}, use_global_device_ids=true | all-gather | bytes 294912 | tf_op jit(solution)/shard_map/all_gather | solution.py:85
  103.0 0.3 fusion.25
  103.4 2.9 fusion.40
  106.8 0.3 fusion.44
  107.1 0.3 fusion.3
  107.4 1.8 convolution_convert_fusion.4
  109.2 26.6 %all_gather.10 = bf16[128,1024]{1,0:T(8,128)(2,1)S(1)} all-gather(bf16[128,128]{1,0:T(8,128)(2,1)S(1)} %convolution_convert_fusion.4), channel_id=1, replica_groups=mesh['dp'=4,'ctx'=8] {'ctx'}, dimensions={1}, use_global_device_ids=true | all-gather | bytes 294912 | tf_op jit(solution)/shard_map/all_gather | solution.py:86
  136.3 4.0 %convolution_convert_fusion.1 = bf16[128,4096]{1,0:T(8,128)(2,1)} fusion(bf16[128,512]{0,1:T(8,128)(2,1)S(1)} %bitcast.32, bf16[512,4096]{1,0:T(8,128)(2,1)} %param.21), kind=kOutput, calls=%fused_computation.6 | convolution fusion | flops 537395200 | bytes 5373952 | tf_op jit(solution)/shard_map/dot_general | solution.py:122
  140.3 0.2 reduce-scatter.2.cloned.1.call-start
  140.5 75.2 %all-reduce.3.cloned.1.call-done = bf16[128,4096]{1,0:T(8,128)(2,1)} async-done(((bf16[128,4096]{1,0:T(8,128)(2,1)}), bf16[128,4096]{1,0:T(8,128)(2,1)}) %all-reduce.3.cloned.1.call-update) | async-done | bytes 1048592 | tf_op jit(solution)/shard_map/psum | solution.py:121
  215.7 1.9 multiply_reduce_fusion
  217.6 5.8 %fusion.39 = f32[128,1024]{1,0:T(8,128)} fusion(bf16[4096,1024]{1,0:T(8,128)(2,1)} %param.24, f32[4096]{0:T(1024)S(1)} %copy-done.6, f32[128]{0:T(128)S(1)} %add_rsqrt_fusion, bf16[128,4096]{1,0:T(8,128)(2,1)S(1)} %copy-done.2, bf16[128,4096]{1,0:T(8,128)(2,1)S(1)} %gather_fusion.1, pred[128]{0:T(512)(128)(4,1)S(1)} %get-tuple-element.28), kind=kOutput, calls=%fused_computation.91 | convolution fusion | flops 1077411840 | bytes 11027072 | tf_op jit(solution)/shard_map/dot_general | solution.py:126
  223.4 9.8 %convolution_convert_fusion = bf16[128,4096]{1,0:T(8,128)(2,1)} fusion(bf16[1024,4096]{1,0:T(8,128)(2,1)} %param.26, bf16[4096,1024]{1,0:T(8,128)(2,1)} %param.25, f32[128,1024]{1,0:T(8,128)} %fusion.39, f32[4096]{0:T(1024)S(1)} %copy-done.6, f32[128]{0:T(128)S(1)} %add_rsqrt_fusion, bf16[128,4096]{1,0:T(8,128)(2,1)S(1)} %copy-done.2, ...), kind=kOutput, calls=%fused_computation.5 | convolution fusion | flops 2152464384 | bytes 20464256 | tf_op jit(solution)/shard_map/dot_general | solution.py:132
  233.4 1.3 copy-done.3
  234.8 1.6 convert_element_type.82
  236.4 60.0 %reduce-scatter.2.cloned.1.call-done = bf16[16,4096]{1,0:T(8,128)(2,1)} async-done(((bf16[128,4096]{1,0:T(8,128)(2,1)}), bf16[16,4096]{1,0:T(8,128)(2,1)}) %reduce-scatter.2.cloned.1.call-update) | async-done | bytes 131088 | tf_op jit(solution)/shard_map/reduce_scatter | solution.py:131
  296.4 1.8 add_convert_fusion
  (47 shorter events, 2.3 us)
Async XLA Ops:
  6.5 9.6 %copy-start = (bf16[128,4096]{1,0:T(8,128)(2,1)S(1)}, bf16[128,4096]{1,0:T(8,128)(2,1)}, u32[]{:S(2)}) copy-start(bf16[128,4096]{1,0:T(8,128)(2,1)} %param.15) | copy-start | bytes 3145732
  6.5 11.2 %copy-start.1 = (s32[128]{0:T(128)S(1)}, s32[128]{0:T(128)}, u32[]{:S(2)}) copy-start(s32[128]{0:T(128)} %param.16) | copy-start | bytes 1540
  6.5 63.3 %all-gather.2.cloned.1.call-start = ((), (), s32[]{:S(2)}) async-start(), calls=%async_computation.1 | async-start | bytes 2359296 | tf_op jit(solution)/shard_map/all_gather | solution.py:71
  17.7 198.0 %all-reduce.3.cloned.1.call-start = ((), (), s32[]{:S(2)}) async-start(), calls=%async_computation.2 | async-start | bytes 2097152 | tf_op jit(solution)/shard_map/psum | solution.py:121
  20.8 53.5 %copy-start.5 = (f32[4096]{0:T(1024)S(1)}, f32[4096]{0:T(1024)}, u32[]{:S(2)}) copy-start(f32[4096]{0:T(1024)} %param.22) | copy-start | bytes 49156
  140.2 77.3 %copy-start.6 = (f32[4096]{0:T(1024)S(1)}, f32[4096]{0:T(1024)}, u32[]{:S(2)}) copy-start(f32[4096]{0:T(1024)} %param.23) | copy-start | bytes 49156
  140.3 156.1 %reduce-scatter.2.cloned.1.call-start = ((), (), s32[]{:S(2)}) async-start(), calls=%async_computation.3 | async-start | bytes 1179648 | tf_op jit(solution)/shard_map/reduce_scatter | solution.py:131
  215.7 1.9 copy-start.2
  233.1 1.5 copy-start.4
  233.4 1.3 copy-start.3
Sparse Core Ops, SparseCore 0:
  17.8 51.9 all-gather.1
  140.4 75.2 all-reduce.2
  233.3 63.0 reduce-scatter.1
where the time goes:
time: 305 us
  waiting for transfers between devices  184 us (60%)
  blocking collectives  53 us (17%)
  matrix products  26.9 us (9%)
  between operations  15.4 us (5%)
  other arithmetic  14.3 us (5%)
  local copies, waits for them, and re-layouts  10.7 us (4%)
    psum x1, waiting for transfers between devices, on_device(): lax.psum(jnp.dot(heads_out, w_output, preferred_element_type=jnp.float32)...  75.2 us
    reduce_scatter x1, waiting for transfers between devices, on_device(): lax.psum_scatter(jnp.dot(piece, w_down, preferred_element_type=jnp.float3...  60 us
    all_gather x1, waiting for transfers between devices, on_device(): gathered = lax.all_gather(outgoing, 'ctx', axis=0, tiled=True)  49 us
    all_gather x1, blocking collectives, on_device(): lax.all_gather(value_part, 'ctx', axis=1, tiled=True)  26.6 us
    all_gather x1, blocking collectives, on_device(): lax.all_gather(key_part, 'ctx', axis=1, tiled=True)  26.5 us
    dot_general x1, matrix products, on_device(): jnp.dot(piece, w_down, preferred_element_type=jnp.float32)  9.78 us
  transfers between devices with their start and end apart: 3, of which 3 were waited for; matrix products, arithmetic and copies ran while one was open for 2% of the time, Pallas kernels for 0%

commit v1 on v0

v1 whole, which is shorter than its diff:
```python
import jax
import jax.numpy as jnp
from jax import lax
from jax.sharding import PartitionSpec as P

HEADS = 32
KV_HEADS = 8
HEAD_DIM = 128

rope_base = 500000.0
norm_eps = 1e-05


def rms_scale(values, gain):
    mean_sq = jnp.mean(values * values, axis=-1, keepdims=True)
    return values * lax.rsqrt(mean_sq + norm_eps) * gain


def plane_of(count):
    wide = max(y for y in range(1, count + 1) if count % y == 0 and 2 * y * y <= max(count, 2))
    return count // wide, wide


def shift(block, tall, wide, dz, dy):
    pairs = [
        (z * wide + y, (z + dz) % tall * wide + (y + dy) % wide)
        for z in range(tall)
        for y in range(wide)
    ]
    return lax.ppermute(block, "ctx", pairs)


def gather_blocks(block, tall, wide):
    blocks = {}
    for dz in range(tall):
        blocks[dz, 0] = block if dz == 0 else shift(block, tall, wide, dz, 0)
    for dz in range(tall):
        for dy in range(1, wide):
            blocks[dz, dy] = shift(blocks[dz, 0], tall, wide, 0, dy)
    return [blocks[dz, dy] for dz in range(tall) for dy in range(wide)]


def scatter_sum(parts, tall, wide):
    total = None
    for dz in [*range(1, tall), 0]:
        lane = parts[dz * wide].astype(jnp.float32)
        for dy in range(1, wide):
            lane = lane + shift(parts[dz * wide + dy], tall, wide, 0, dy).astype(jnp.float32)
        if dz:
            lane = shift(lane.astype(jnp.bfloat16), tall, wide, dz, 0).astype(jnp.float32)
        total = lane if total is None else total + lane
    return total


def onehot_dot(onehot, values):
    return jnp.dot(onehot, values, preferred_element_type=jnp.float32).astype(values.dtype)


def on_device(
    activations,
    routed,
    balance,
    w_query,
    w_key,
    w_value,
    w_output,
    attn_gain,
    mlp_gain,
    w_gate,
    w_up,
    w_down,
    w_router,
):
    shard_count = lax.axis_size("ctx")
    tall, wide = plane_of(shard_count)
    me = lax.axis_index("ctx")
    my_z, my_y = me // wide, me % wide
    tok_shard = activations.shape[0]
    total = routed.shape[0]
    share = total // shard_count
    capacity = 2 * share
    local_heads = w_query.shape[1] // HEAD_DIM
    group_size = HEADS // KV_HEADS
    bf16, f32 = jnp.bfloat16, jnp.float32

    row_ids = jnp.arange(total, dtype=jnp.int32)
    low = me * tok_shard
    my_first = jnp.sum((routed < low).astype(jnp.int32))
    local = routed - low
    is_here = (local >= 0) & (local < tok_shard)
    slots = jnp.arange(capacity, dtype=jnp.int32)
    hit = is_here[None, :] & (row_ids[None, :] - my_first == slots[:, None])
    token = jnp.sum(jnp.where(hit, local[None, :] + 1, 0), axis=1) - 1
    pick_out = (token[:, None] == jnp.arange(tok_shard, dtype=jnp.int32)[None, :]).astype(bf16)
    outgoing = onehot_dot(pick_out, activations)
    blocks = gather_blocks(outgoing, tall, wide)

    home = routed // tok_shard
    before = home[None, :] < home[:, None]
    in_block = row_ids - jnp.sum(before.astype(jnp.int32), axis=1)
    from_z, from_y = (my_z - home // wide) % tall, (my_y - home % wide) % wide
    slot_of_row = (from_z * wide + from_y) * capacity + in_block
    same = (balance[None, :] == balance[:, None]) & (row_ids[None, :] < row_ids[:, None])
    rank = jnp.sum(same.astype(jnp.int32), axis=1)
    to_z, to_y = (balance // wide - my_z) % tall, (balance % wide - my_y) % wide
    place_of_row = (to_z * wide + to_y) * share + rank
    placed = place_of_row[None, :] == row_ids[:, None]
    slot_at = jnp.sum(jnp.where(placed, slot_of_row[None, :], 0), axis=1)
    positions = jnp.sum(jnp.where(placed, routed[None, :], 0), axis=1)
    pick_rows = (
        slot_at[:, None] == jnp.arange(shard_count * capacity, dtype=jnp.int32)[None, :]
    ).astype(bf16)

    rows = onehot_dot(pick_rows, jnp.concatenate(blocks, axis=0))
    normed = rms_scale(rows.astype(f32), attn_gain).astype(bf16)

    half = HEAD_DIM // 2
    steps_f = jnp.arange(half, dtype=f32)
    freqs = jnp.exp(-jnp.log(f32(rope_base)) * (2.0 * steps_f / HEAD_DIM))
    q_angles = positions.astype(f32)[:, None] * freqs[None, :]
    q_cos, q_sin = jnp.cos(q_angles)[:, None, :], jnp.sin(q_angles)[:, None, :]
    k_angles = freqs[:, None] * routed.astype(f32)[None, :]
    k_cos, k_sin = jnp.cos(k_angles), jnp.sin(k_angles)

    key_part = jnp.dot(normed, w_key, preferred_element_type=f32).astype(bf16)
    value_part = jnp.dot(normed, w_value, preferred_element_type=f32).astype(bf16)
    depth = w_key.shape[1] // KV_HEADS
    kv_local = max(1, local_heads // group_size)
    in_order = placed.astype(bf16)
    kv_t = lax.dot_general(
        jnp.concatenate([key_part, value_part], axis=1),
        in_order,
        (((0,), (0,)), ((), ())),
        preferred_element_type=f32,
    ).astype(bf16)
    kv_t = jnp.transpose(kv_t.reshape(2, depth, KV_HEADS, total), (2, 0, 1, 3))
    if kv_local * shard_count == KV_HEADS:
        outbound = kv_t.reshape(shard_count, kv_local, 2, depth, total)
    else:
        firsts = [p * local_heads // group_size for p in range(shard_count)]
        outbound = jnp.stack([kv_t[g : g + kv_local] for g in firsts])
    inbound = lax.all_to_all(outbound, "ctx", 0, 0, tiled=True)
    inbound = jnp.transpose(inbound, (2, 1, 0, 3, 4)).reshape(2, kv_local, HEAD_DIM, total)
    key_t, value_t = inbound[0].astype(f32), inbound[1]
    key_a, key_b = key_t[:, :half], key_t[:, half:]
    key_t = jnp.concatenate(
        [key_a * k_cos - key_b * k_sin, key_b * k_cos + key_a * k_sin], axis=1
    ).astype(bf16)

    query = jnp.dot(normed, w_query, preferred_element_type=f32).reshape(
        total, local_heads, HEAD_DIM
    )
    query_a, query_b = query[..., :half], query[..., half:]
    query = jnp.concatenate(
        [query_a * q_cos - query_b * q_sin, query_b * q_cos + query_a * q_sin], axis=-1
    ).astype(bf16)
    query = query.reshape(total, kv_local, local_heads // kv_local, HEAD_DIM)
    scores = jnp.einsum("qgrd,gdk->grqk", query, key_t, preferred_element_type=f32)
    scores = scores * HEAD_DIM ** (-0.5)
    allowed = routed[None, :] <= positions[:, None]
    scores = jnp.where(allowed, scores, -1e30)
    exp_scores = jnp.exp(scores - jnp.max(scores, axis=-1, keepdims=True))
    probs = (exp_scores / jnp.sum(exp_scores, axis=-1, keepdims=True)).astype(bf16)
    heads_out = jnp.einsum("grqk,gdk->qgrd", probs, value_t, preferred_element_type=f32)
    heads_out = heads_out.astype(bf16).reshape(total, local_heads * HEAD_DIM)

    def split(partial):
        return [partial[r * share : (r + 1) * share] for r in range(shard_count)]

    attn_part = jnp.dot(heads_out, w_output, preferred_element_type=f32).astype(bf16)
    attn_own = scatter_sum(split(attn_part), tall, wide)
    own_rows = rows[:share].astype(f32)
    mnorm = rms_scale(own_rows + attn_own, mlp_gain).astype(bf16)
    piece = jnp.concatenate(gather_blocks(mnorm, tall, wide), axis=0)
    gate = jnp.dot(piece, w_gate, preferred_element_type=f32)
    upward = jnp.dot(piece, w_up, preferred_element_type=f32)
    inner = (jax.nn.silu(gate) * upward).astype(bf16)
    mlp_part = split(jnp.dot(inner, w_down, preferred_element_type=f32).astype(bf16))
    back = [
        mlp_part[(-dz) % tall * wide + (-dy) % wide] for dz in range(tall) for dy in range(wide)
    ]
    mlp_own = scatter_sum(back, tall, wide)
    router_score = jnp.sum(own_rows * w_router[None, :], axis=1, keepdims=True)
    return (own_rows + router_score * (attn_own + mlp_own)).astype(bf16)


def solution(mesh):
    in_specs = (
        P(("dp", "ctx"), None),
        P("dp"),
        P("dp"),
        P(None, "ctx"),
        P(None, "ctx"),
        P(None, "ctx"),
        P("ctx", None),
        P(),
        P(),
        P(None, "ctx"),
        P(None, "ctx"),
        P("ctx", None),
        P(),
    )
    out_specs = P(("dp", "ctx"), None)
    return jax.shard_map(
        on_device, mesh=mesh, in_specs=in_specs, out_specs=out_specs, check_vma=False
    )
```

time: 305 us -> 134 us (0.44)
  waiting for transfers between devices: 184 us -> 54.4 us
  blocking collectives: 53 us -> 0 us
  starting transfers between devices: 0.27 us -> 45.2 us
  between operations: 15.4 us -> 0.42 us
  local copies, waits for them, and re-layouts: 10.7 us -> 1.46 us
  other arithmetic: 14.3 us -> 9.15 us
  matrix products: 26.9 us -> 22.6 us
    psum x1 -> x0, waiting for transfers between devices: 75.2 us -> none  [on_device(): lax.psum(jnp.dot(heads_out, w_output, preferred_element_type=jnp.float32)...]
    reduce_scatter x1 -> x0, waiting for transfers between devices: 60 us -> none  [on_device(): lax.psum_scatter(jnp.dot(piece, w_down, preferred_element_type=jnp.float3...]
    all_gather x2 -> x0, blocking collectives: 53 us -> none  [the longest x1 26.6 us: on_device(): lax.all_gather(value_part, 'ctx', axis=1, tiled=True)]
    ppermute x0 -> x28, waiting for transfers between devices: none -> 50.9 us  [shift(): return lax.ppermute(block, 'ctx', pairs)]
    all_gather x1 -> x0, waiting for transfers between devices: 49 us -> none  [on_device(): gathered = lax.all_gather(outgoing, 'ctx', axis=0, tiled=True)]
    ppermute x0 -> x28, starting transfers between devices: none -> 38.1 us  [shift(): return lax.ppermute(block, 'ctx', pairs)]
    gather x4 -> x0, local copies, waits for them, and re-layouts: 7.22 us -> none  [the longest x1 4.06 us: on_device(): jnp.take(gathered, jnp.take(slot_index, owner_order), axis=0)]
    all_to_all x0 -> x1, starting transfers between devices: none -> 7.1 us  [on_device(): inbound = lax.all_to_all(outbound, 'ctx', 0, 0, tiled=True)]
  transfers between devices with their start and end apart: 3 -> 29, of which waited for: 3 -> 19; matrix products, arithmetic and copies ran while one was open for 2% -> 5% of each run, Pallas kernels for 0% -> 0%
where the time goes in v1:
time: 134 us; the launch traced here: 133 us
  waiting for transfers between devices  54.4 us (41%)
  starting transfers between devices  45.2 us (34%)
  matrix products  22.6 us (17%)
  other arithmetic  9.15 us (7%)
  local copies, waits for them, and re-layouts  1.46 us (1%)
    ppermute x28, waiting for transfers between devices, shift(): return lax.ppermute(block, 'ctx', pairs)  50.9 us
    ppermute x28, starting transfers between devices, shift(): return lax.ppermute(block, 'ctx', pairs)  38.1 us
    dot_general x1, matrix products, on_device(): jnp.dot(inner, w_down, preferred_element_type=f32).astype(bf16)  8.4 us
    all_to_all x1, starting transfers between devices, on_device(): inbound = lax.all_to_all(outbound, 'ctx', 0, 0, tiled=True)  7.1 us
    dot_general x1, matrix products, on_device(): gate = jnp.dot(piece, w_gate, preferred_element_type=f32)  5.43 us
    all_to_all x1, waiting for transfers between devices, on_device(): inbound = lax.all_to_all(outbound, 'ctx', 0, 0, tiled=True)  3.58 us
    dot_general x1, matrix products, on_device(): jnp.dot(normed, w_query, preferred_element_type=f32)  2.94 us
    dot_general x1, matrix products, on_device(): jnp.dot(heads_out, w_output, preferred_element_type=f32).astype(bf16)  2.94 us
  transfers between devices with their start and end apart: 29, of which 19 were waited for; matrix products, arithmetic and copies ran while one was open for 5% of the time, Pallas kernels for 0%

profile of v1, /device:TPU:0, one launch (start us, length us, event | category | flops | bytes accessed | tf_op | source)
XLA Modules:
  0.0 133.3 jit_solution(9618280715836469462)
XLA Ops:
  3.4 3.0 %collective-permute-start = (bf16[32,4096]{1,0:T(8,128)(2,1)S(1)}, bf16[32,4096]{1,0:T(8,128)(2,1)S(1)}, u32[]{:S(2)}, u32[]{:S(2)}) collective-permute-start(bf16[32,4096]{1,0:T(8,128)(2,1)S(1)} %get-tuple-element.43), channel_id=1, source_target_pairs={{0,1},{1,0},{2,3},{3,2},{4,5},{5,4},{6,7},{7,6},{8,9},{9,8},{10,11... | collective-permute-start | bytes 786440 | tf_op jit(solution)/shard_map/ppermute | solution.py:30
  6.4 1.6 %collective-permute-start.1 = (bf16[32,4096]{1,0:T(8,128)(2,1)S(1)}, bf16[32,4096]{1,0:T(8,128)(2,1)S(1)}, u32[]{:S(2)}, u32[]{:S(2)}) collective-permute-start(bf16[32,4096]{1,0:T(8,128)(2,1)S(1)} %get-tuple-element.43), channel_id=1, source_target_pairs={{0,2},{1,3},{2,4},{3,5},{4,6},{5,7},{6,0},{7,1},{8,10},{9,11},{10,... | collective-permute-start | bytes 786440 | tf_op jit(solution)/shard_map/ppermute | solution.py:30
  8.0 2.6 %collective-permute-start.3 = (bf16[32,4096]{1,0:T(8,128)(2,1)S(1)}, bf16[32,4096]{1,0:T(8,128)(2,1)S(1)}, u32[]{:S(2)}, u32[]{:S(2)}) collective-permute-start(bf16[32,4096]{1,0:T(8,128)(2,1)S(1)} %get-tuple-element.43), channel_id=1, source_target_pairs={{0,4},{1,5},{2,6},{3,7},{4,0},{5,1},{6,2},{7,3},{8,12},{9,13},{10,... | collective-permute-start | bytes 786440 | tf_op jit(solution)/shard_map/ppermute | solution.py:30
  15.4 2.2 %collective-permute-done.1 = bf16[32,4096]{1,0:T(8,128)(2,1)S(1)} collective-permute-done((bf16[32,4096]{1,0:T(8,128)(2,1)S(1)}, bf16[32,4096]{1,0:T(8,128)(2,1)S(1)}, u32[]{:S(2)}, u32[]{:S(2)}) %collective-permute-start.1) | collective-permute-done | bytes 262176 | tf_op jit(solution)/shard_map/ppermute | solution.py:30
  17.8 9.6 %collective-permute-done.3 = bf16[32,4096]{1,0:T(8,128)(2,1)S(1)} collective-permute-done((bf16[32,4096]{1,0:T(8,128)(2,1)S(1)}, bf16[32,4096]{1,0:T(8,128)(2,1)S(1)}, u32[]{:S(2)}, u32[]{:S(2)}) %collective-permute-start.3) | collective-permute-done | bytes 262176 | tf_op jit(solution)/shard_map/ppermute | solution.py:30
  27.9 1.5 %collective-permute-start.6 = (bf16[32,4096]{1,0:T(8,128)(2,1)S(1)}, bf16[32,4096]{1,0:T(8,128)(2,1)S(1)}, u32[]{:S(2)}, u32[]{:S(2)}) collective-permute-start(bf16[32,4096]{1,0:T(8,128)(2,1)S(1)} %collective-permute-done.5), channel_id=1, source_target_pairs={{0,1},{1,0},{2,3},{3,2},{4,5},{5,4},{6,7},{7,6},{8,9},{9,8},{10,11... | collective-permute-start | bytes 786440 | tf_op jit(solution)/shard_map/ppermute | solution.py:30
  29.6 7.0 %collective-permute-done.4 = bf16[32,4096]{1,0:T(8,128)(2,1)S(1)} collective-permute-done((bf16[32,4096]{1,0:T(8,128)(2,1)S(1)}, bf16[32,4096]{1,0:T(8,128)(2,1)S(1)}, u32[]{:S(2)}, u32[]{:S(2)}) %collective-permute-start.4) | collective-permute-done | bytes 262176 | tf_op jit(solution)/shard_map/ppermute | solution.py:30
  36.7 4.5 %collective-permute-done.6 = bf16[32,4096]{1,0:T(8,128)(2,1)S(1)} collective-permute-done((bf16[32,4096]{1,0:T(8,128)(2,1)S(1)}, bf16[32,4096]{1,0:T(8,128)(2,1)S(1)}, u32[]{:S(2)}, u32[]{:S(2)}) %collective-permute-start.6) | collective-permute-done | bytes 262176 | tf_op jit(solution)/shard_map/ppermute | solution.py:30
  44.0 7.1 %all-to-all-start = ((bf16[8,1,2,16,128]{4,3,1,2,0:T(8,128)(2,1)}), bf16[8,1,2,16,128]{4,3,1,2,0:T(8,128)(2,1)S(1)}, u32[]{:S(2)}, u32[]{:S(2)}) async-start(bf16[8,1,2,16,128]{4,3,1,2,0:T(8,128)(2,1)} %bitcast.50), calls=%async_computation | async-start | bytes 131072 | tf_op jit(solution)/shard_map/all_to_all | solution.py:142
  51.1 2.9 %fusion.47 = f32[128,512]{1,0:T(8,128)S(1)} fusion(bf16[4096,512]{1,0:T(8,128)(2,1)} %param.16, bf16[128,4096]{1,0:T(8,128)(2,1)S(1)} %get-tuple-element.45, f32[4096]{0:T(1024)S(1)} %copy-done.6, f32[128]{0:T(128)S(1)} %add_rsqrt_fusion.1), kind=kOutput, calls=%fused_computation.146 | convolution fusion | flops 538968064 | bytes 5521920 | tf_op jit(solution)/shard_map/dot_general | solution.py:150
  54.5 3.6 %all-to-all-done = bf16[8,1,2,16,128]{4,3,1,2,0:T(8,128)(2,1)S(1)} async-done(((bf16[8,1,2,16,128]{4,3,1,2,0:T(8,128)(2,1)}), bf16[8,1,2,16,128]{4,3,1,2,0:T(8,128)(2,1)S(1)}, u32[]{:S(2)}, u32[]{:S(2)}) %all-to-all-start) | async-done | bytes 65568 | tf_op jit(solution)/shard_map/all_to_all | solution.py:142
  59.2 2.9 %convolution_convert_fusion.1 = bf16[128,4096]{1,0:T(8,128)(2,1)S(1)} fusion(bf16[128,512]{0,1:T(8,128)(2,1)S(1)} %bitcast.52, bf16[512,4096]{1,0:T(8,128)(2,1)} %param.19), kind=kOutput, calls=%fused_computation.1 | convolution fusion | flops 537395200 | bytes 5373952 | tf_op jit(solution)/shard_map/dot_general | solution.py:170
  62.6 1.6 %collective-permute-start.7 = (bf16[16,4096]{1,0:T(8,128)(2,1)S(1)}, bf16[16,4096]{1,0:T(8,128)(2,1)S(1)}, u32[]{:S(2)}, u32[]{:S(2)}) collective-permute-start(bf16[16,4096]{1,0:T(8,128)(2,1)S(1)} %get-tuple-element.22), channel_id=1, source_target_pairs={{0,1},{1,0},{2,3},{3,2},{4,5},{5,4},{6,7},{7,6},{8,9},{9,8},{10,11... | collective-permute-start | bytes 393224 | tf_op jit(solution)/shard_map/ppermute | solution.py:30
  64.7 1.6 %collective-permute-start.13 = (bf16[16,4096]{1,0:T(8,128)(2,1)S(1)}, bf16[16,4096]{1,0:T(8,128)(2,1)S(1)}, u32[]{:S(2)}, u32[]{:S(2)}) collective-permute-start(bf16[16,4096]{1,0:T(8,128)(2,1)S(1)} %get-tuple-element.23), channel_id=1, source_target_pairs={{0,1},{1,0},{2,3},{3,2},{4,5},{5,4},{6,7},{7,6},{8,9},{9,8},{10,11... | collective-permute-start | bytes 393224 | tf_op jit(solution)/shard_map/ppermute | solution.py:30
  66.3 1.9 %collective-permute-done.11 = bf16[16,4096]{1,0:T(8,128)(2,1)S(1)} collective-permute-done((bf16[16,4096]{1,0:T(8,128)(2,1)S(1)}, bf16[16,4096]{1,0:T(8,128)(2,1)S(1)}, u32[]{:S(2)}, u32[]{:S(2)}) %collective-permute-start.11) | collective-permute-done | bytes 131104 | tf_op jit(solution)/shard_map/ppermute | solution.py:30
  71.6 2.1 %collective-permute-start.12 = (bf16[16,4096]{1,0:T(8,128)(2,1)S(1)}, bf16[16,4096]{1,0:T(8,128)(2,1)S(1)}, u32[]{:S(2)}, u32[]{:S(2)}) collective-permute-start(bf16[16,4096]{1,0:T(8,128)(2,1)S(1)} %get-tuple-element.20), channel_id=1, source_target_pairs={{0,6},{1,7},{2,0},{3,1},{4,2},{5,3},{6,4},{7,5},{8,14},{9,15},{10,... | collective-permute-start | bytes 393224 | tf_op jit(solution)/shard_map/ppermute | solution.py:30
  73.7 4.5 %collective-permute-done.10 = bf16[16,4096]{1,0:T(8,128)(2,1)S(1)} collective-permute-done((bf16[16,4096]{1,0:T(8,128)(2,1)S(1)}, bf16[16,4096]{1,0:T(8,128)(2,1)S(1)}, u32[]{:S(2)}, u32[]{:S(2)}) %collective-permute-start.10) | collective-permute-done | bytes 131104 | tf_op jit(solution)/shard_map/ppermute | solution.py:30
  78.2 3.7 %collective-permute-done.8 = bf16[16,4096]{1,0:T(8,128)(2,1)S(1)} collective-permute-done((bf16[16,4096]{1,0:T(8,128)(2,1)S(1)}, bf16[16,4096]{1,0:T(8,128)(2,1)S(1)}, u32[]{:S(2)}, u32[]{:S(2)}) %collective-permute-start.8) | collective-permute-done | bytes 131104 | tf_op jit(solution)/shard_map/ppermute | solution.py:30
  82.3 3.5 %collective-permute-start.15 = (bf16[16,4096]{1,0:T(8,128)(2,1)S(1)}, bf16[16,4096]{1,0:T(8,128)(2,1)S(1)}, u32[]{:S(2)}, u32[]{:S(2)}) collective-permute-start(bf16[16,4096]{1,0:T(8,128)(2,1)S(1)} %get-tuple-element.10), channel_id=1, source_target_pairs={{0,2},{1,3},{2,4},{3,5},{4,6},{5,7},{6,0},{7,1},{8,10},{9,11},{10,... | collective-permute-start | bytes 393224 | tf_op jit(solution)/shard_map/ppermute | solution.py:30
  86.4 2.0 %collective-permute-start.17 = (bf16[16,4096]{1,0:T(8,128)(2,1)S(1)}, bf16[16,4096]{1,0:T(8,128)(2,1)S(1)}, u32[]{:S(2)}, u32[]{:S(2)}) collective-permute-start(bf16[16,4096]{1,0:T(8,128)(2,1)S(1)} %get-tuple-element.10), channel_id=1, source_target_pairs={{0,4},{1,5},{2,6},{3,7},{4,0},{5,1},{6,2},{7,3},{8,12},{9,13},{10,... | collective-permute-start | bytes 393224 | tf_op jit(solution)/shard_map/ppermute | solution.py:30
  88.3 2.8 %collective-permute-start.19 = (bf16[16,4096]{1,0:T(8,128)(2,1)S(1)}, bf16[16,4096]{1,0:T(8,128)(2,1)S(1)}, u32[]{:S(2)}, u32[]{:S(2)}) collective-permute-start(bf16[16,4096]{1,0:T(8,128)(2,1)S(1)} %get-tuple-element.10), channel_id=1, source_target_pairs={{0,6},{1,7},{2,0},{3,1},{4,2},{5,3},{6,4},{7,5},{8,14},{9,15},{10,... | collective-permute-start | bytes 393224 | tf_op jit(solution)/shard_map/ppermute | solution.py:30
  92.3 2.8 %collective-permute-start.18 = (bf16[16,4096]{1,0:T(8,128)(2,1)S(1)}, bf16[16,4096]{1,0:T(8,128)(2,1)S(1)}, u32[]{:S(2)}, u32[]{:S(2)}) collective-permute-start(bf16[16,4096]{1,0:T(8,128)(2,1)S(1)} %collective-permute-done.17), channel_id=1, source_target_pairs={{0,1},{1,0},{2,3},{3,2},{4,5},{5,4},{6,7},{7,6},{8,9},{9,8},{10,11... | collective-permute-start | bytes 393224 | tf_op jit(solution)/shard_map/ppermute | solution.py:30
  96.2 1.9 %collective-permute-done.18 = bf16[16,4096]{1,0:T(8,128)(2,1)S(1)} collective-permute-done((bf16[16,4096]{1,0:T(8,128)(2,1)S(1)}, bf16[16,4096]{1,0:T(8,128)(2,1)S(1)}, u32[]{:S(2)}, u32[]{:S(2)}) %collective-permute-start.18) | collective-permute-done | bytes 131104 | tf_op jit(solution)/shard_map/ppermute | solution.py:30
  98.1 2.0 %collective-permute-done.20 = bf16[16,4096]{1,0:T(8,128)(2,1)S(1)} collective-permute-done((bf16[16,4096]{1,0:T(8,128)(2,1)S(1)}, bf16[16,4096]{1,0:T(8,128)(2,1)S(1)}, u32[]{:S(2)}, u32[]{:S(2)}) %collective-permute-start.20) | collective-permute-done | bytes 131104 | tf_op jit(solution)/shard_map/ppermute | solution.py:30
  100.1 5.4 %fusion.60 = f32[128,1024]{1,0:T(8,128)} fusion(bf16[128,4096]{1,0:T(8,128)(2,1)S(1)} %constant_dynamic-update-slice_fusion.8, bf16[4096,1024]{1,0:T(8,128)(2,1)} %param.22), kind=kOutput, calls=%fused_computation.155 | convolution fusion | flops 1073741824 | bytes 9961472 | tf_op jit(solution)/shard_map/dot_general | solution.py:175
  105.5 8.4 %convolution_convert_fusion = bf16[128,4096]{1,0:T(8,128)(2,1)S(1)} fusion(bf16[1024,4096]{1,0:T(8,128)(2,1)} %param.24, f32[128,1024]{1,0:T(8,128)} %fusion.60, bf16[128,4096]{1,0:T(8,128)(2,1)S(1)} %constant_dynamic-update-slice_fusion.8, bf16[4096,1024]{1,0:T(8,128)(2,1)} %param.23), kind=kOutput, calls=%fused_computation | convolution fusion | flops 2148794368 | bytes 19398656 | tf_op jit(solution)/shard_map/dot_general | solution.py:178
  114.0 1.5 %collective-permute-start.21 = (bf16[16,4096]{1,0:T(8,128)(2,1)S(1)}, bf16[16,4096]{1,0:T(8,128)(2,1)S(1)}, u32[]{:S(2)}, u32[]{:S(2)}) collective-permute-start(bf16[16,4096]{1,0:T(8,128)(2,1)S(1)} %get-tuple-element.15), channel_id=1, source_target_pairs={{0,1},{1,0},{2,3},{3,2},{4,5},{5,4},{6,7},{7,6},{8,9},{9,8},{10,11... | collective-permute-start | bytes 393224 | tf_op jit(solution)/shard_map/ppermute | solution.py:30
  120.4 1.4 %collective-permute-done.25 = bf16[16,4096]{1,0:T(8,128)(2,1)S(1)} collective-permute-done((bf16[16,4096]{1,0:T(8,128)(2,1)S(1)}, bf16[16,4096]{1,0:T(8,128)(2,1)S(1)}, u32[]{:S(2)}, u32[]{:S(2)}) %collective-permute-start.25) | collective-permute-done | bytes 131104 | tf_op jit(solution)/shard_map/ppermute | solution.py:30
  123.1 2.3 %collective-permute-start.24 = (bf16[16,4096]{1,0:T(8,128)(2,1)S(1)}, bf16[16,4096]{1,0:T(8,128)(2,1)S(1)}, u32[]{:S(2)}, u32[]{:S(2)}) collective-permute-start(bf16[16,4096]{1,0:T(8,128)(2,1)S(1)} %get-tuple-element.14), channel_id=1, source_target_pairs={{0,4},{1,5},{2,6},{3,7},{4,0},{5,1},{6,2},{7,3},{8,12},{9,13},{10,... | collective-permute-start | bytes 393224 | tf_op jit(solution)/shard_map/ppermute | solution.py:30
  125.9 2.9 %collective-permute-done.22 = bf16[16,4096]{1,0:T(8,128)(2,1)S(1)} collective-permute-done((bf16[16,4096]{1,0:T(8,128)(2,1)S(1)}, bf16[16,4096]{1,0:T(8,128)(2,1)S(1)}, u32[]{:S(2)}, u32[]{:S(2)}) %collective-permute-start.22) | collective-permute-done | bytes 131104 | tf_op jit(solution)/shard_map/ppermute | solution.py:30
  128.8 2.8 %collective-permute-done.24 = bf16[16,4096]{1,0:T(8,128)(2,1)S(1)} collective-permute-done((bf16[16,4096]{1,0:T(8,128)(2,1)S(1)}, bf16[16,4096]{1,0:T(8,128)(2,1)S(1)}, u32[]{:S(2)}, u32[]{:S(2)}) %collective-permute-start.24) | collective-permute-done | bytes 131104 | tf_op jit(solution)/shard_map/ppermute | solution.py:30
  131.6 1.7 %fusion.6 = bf16[16,4096]{1,0:T(8,128)(2,1)} fusion(f32[16,4096]{1,0:T(8,128)S(1)} %get-tuple-element.11, bf16[16,4096]{1,0:T(8,128)(2,1)S(1)} %collective-permute-done.27, bf16[16,4096]{1,0:T(8,128)(2,1)S(1)} %collective-permute-done.26, bf16[16,4096]{1,0:T(8,128)(2,1)S(1)} %collective-permute-done.24, bf16[16,4096]{1,0:T(8,128)(2,1)S(1)} %collective-permute-done.22, ...), kind=kLoop, calls=%fused_computation.21 | loop fusion | flops 917504 | bytes 1179712 | tf_op jit(solution)/shard_map/convert_element_type | solution.py:184
  (99 shorter events, 27.5 us)
Async XLA Ops:
  3.4 26.1 %collective-permute-start = (bf16[32,4096]{1,0:T(8,128)(2,1)S(1)}, bf16[32,4096]{1,0:T(8,128)(2,1)S(1)}, u32[]{:S(2)}, u32[]{:S(2)}) collective-permute-start(bf16[32,4096]{1,0:T(8,128)(2,1)S(1)} %get-tuple-element.43), channel_id=1, source_target_pairs={{0,1},{1,0},{2,3},{3,2},{4,5},{5,4},{6,7},{7,6},{8,9},{9,8},{10,11... | collective-permute-start | bytes 786440 | tf_op jit(solution)/shard_map/ppermute | solution.py:30
  6.4 11.2 %collective-permute-start.1 = (bf16[32,4096]{1,0:T(8,128)(2,1)S(1)}, bf16[32,4096]{1,0:T(8,128)(2,1)S(1)}, u32[]{:S(2)}, u32[]{:S(2)}) collective-permute-start(bf16[32,4096]{1,0:T(8,128)(2,1)S(1)} %get-tuple-element.43), channel_id=1, source_target_pairs={{0,2},{1,3},{2,4},{3,5},{4,6},{5,7},{6,0},{7,1},{8,10},{9,11},{10,... | collective-permute-start | bytes 786440 | tf_op jit(solution)/shard_map/ppermute | solution.py:30
  8.0 19.4 %collective-permute-start.3 = (bf16[32,4096]{1,0:T(8,128)(2,1)S(1)}, bf16[32,4096]{1,0:T(8,128)(2,1)S(1)}, u32[]{:S(2)}, u32[]{:S(2)}) collective-permute-start(bf16[32,4096]{1,0:T(8,128)(2,1)S(1)} %get-tuple-element.43), channel_id=1, source_target_pairs={{0,4},{1,5},{2,6},{3,7},{4,0},{5,1},{6,2},{7,3},{8,12},{9,13},{10,... | collective-permute-start | bytes 786440 | tf_op jit(solution)/shard_map/ppermute | solution.py:30
  10.6 17.3 %collective-permute-start.5 = (bf16[32,4096]{1,0:T(8,128)(2,1)S(1)}, bf16[32,4096]{1,0:T(8,128)(2,1)S(1)}, u32[]{:S(2)}, u32[]{:S(2)}) collective-permute-start(bf16[32,4096]{1,0:T(8,128)(2,1)S(1)} %get-tuple-element.43), channel_id=1, source_target_pairs={{0,6},{1,7},{2,0},{3,1},{4,2},{5,3},{6,4},{7,5},{8,14},{9,15},{10,... | collective-permute-start | bytes 786440 | tf_op jit(solution)/shard_map/ppermute | solution.py:30
  17.6 11.9 %collective-permute-start.2 = (bf16[32,4096]{1,0:T(8,128)(2,1)S(1)}, bf16[32,4096]{1,0:T(8,128)(2,1)S(1)}, u32[]{:S(2)}, u32[]{:S(2)}) collective-permute-start(bf16[32,4096]{1,0:T(8,128)(2,1)S(1)} %collective-permute-done.1), channel_id=1, source_target_pairs={{0,1},{1,0},{2,3},{3,2},{4,5},{5,4},{6,7},{7,6},{8,9},{9,8},{10,11... | collective-permute-start | bytes 786440 | tf_op jit(solution)/shard_map/ppermute | solution.py:30
  27.4 9.2 %collective-permute-start.4 = (bf16[32,4096]{1,0:T(8,128)(2,1)S(1)}, bf16[32,4096]{1,0:T(8,128)(2,1)S(1)}, u32[]{:S(2)}, u32[]{:S(2)}) collective-permute-start(bf16[32,4096]{1,0:T(8,128)(2,1)S(1)} %collective-permute-done.3), channel_id=1, source_target_pairs={{0,1},{1,0},{2,3},{3,2},{4,5},{5,4},{6,7},{7,6},{8,9},{9,8},{10,11... | collective-permute-start | bytes 786440 | tf_op jit(solution)/shard_map/ppermute | solution.py:30
  27.9 13.2 %collective-permute-start.6 = (bf16[32,4096]{1,0:T(8,128)(2,1)S(1)}, bf16[32,4096]{1,0:T(8,128)(2,1)S(1)}, u32[]{:S(2)}, u32[]{:S(2)}) collective-permute-start(bf16[32,4096]{1,0:T(8,128)(2,1)S(1)} %collective-permute-done.5), channel_id=1, source_target_pairs={{0,1},{1,0},{2,3},{3,2},{4,5},{5,4},{6,7},{7,6},{8,9},{9,8},{10,11... | collective-permute-start | bytes 786440 | tf_op jit(solution)/shard_map/ppermute | solution.py:30
  41.8 40.3 %copy-start.1 = (bf16[128,4096]{1,0:T(8,128)(2,1)}, bf16[128,4096]{1,0:T(8,128)(2,1)S(1)}, u32[]{:S(2)}) copy-start(bf16[128,4096]{1,0:T(8,128)(2,1)S(1)} %get-tuple-element.45) | copy-start | bytes 3145732
  44.0 14.0 %all-to-all-start = ((bf16[8,1,2,16,128]{4,3,1,2,0:T(8,128)(2,1)}), bf16[8,1,2,16,128]{4,3,1,2,0:T(8,128)(2,1)S(1)}, u32[]{:S(2)}, u32[]{:S(2)}) async-start(bf16[8,1,2,16,128]{4,3,1,2,0:T(8,128)(2,1)} %bitcast.50), calls=%async_computation | async-start | bytes 131072 | tf_op jit(solution)/shard_map/all_to_all | solution.py:142
  62.1 19.8 %copy-start.2 = (f32[4096]{0:T(1024)S(1)}, f32[4096]{0:T(1024)}, u32[]{:S(2)}) copy-start(f32[4096]{0:T(1024)} %param.25) | copy-start | bytes 49156
  62.1 20.0 %copy-start.3 = (f32[4096]{0:T(1024)S(1)}, f32[4096]{0:T(1024)}, u32[]{:S(2)}) copy-start(f32[4096]{0:T(1024)} %param.21) | copy-start | bytes 49156
  62.2 6.0 %collective-permute-start.11 = (bf16[16,4096]{1,0:T(8,128)(2,1)S(1)}, bf16[16,4096]{1,0:T(8,128)(2,1)S(1)}, u32[]{:S(2)}, u32[]{:S(2)}) collective-permute-start(bf16[16,4096]{1,0:T(8,128)(2,1)S(1)} %get-tuple-element.24), channel_id=1, source_target_pairs={{0,1},{1,0},{2,3},{3,2},{4,5},{5,4},{6,7},{7,6},{8,9},{9,8},{10,11... | collective-permute-start | bytes 393224 | tf_op jit(solution)/shard_map/ppermute | solution.py:30
  62.6 6.9 %collective-permute-start.7 = (bf16[16,4096]{1,0:T(8,128)(2,1)S(1)}, bf16[16,4096]{1,0:T(8,128)(2,1)S(1)}, u32[]{:S(2)}, u32[]{:S(2)}) collective-permute-start(bf16[16,4096]{1,0:T(8,128)(2,1)S(1)} %get-tuple-element.22), channel_id=1, source_target_pairs={{0,1},{1,0},{2,3},{3,2},{4,5},{5,4},{6,7},{7,6},{8,9},{9,8},{10,11... | collective-permute-start | bytes 393224 | tf_op jit(solution)/shard_map/ppermute | solution.py:30
  64.3 6.7 %collective-permute-start.9 = (bf16[16,4096]{1,0:T(8,128)(2,1)S(1)}, bf16[16,4096]{1,0:T(8,128)(2,1)S(1)}, u32[]{:S(2)}, u32[]{:S(2)}) collective-permute-start(bf16[16,4096]{1,0:T(8,128)(2,1)S(1)} %get-tuple-element.25), channel_id=1, source_target_pairs={{0,1},{1,0},{2,3},{3,2},{4,5},{5,4},{6,7},{7,6},{8,9},{9,8},{10,11... | collective-permute-start | bytes 393224 | tf_op jit(solution)/shard_map/ppermute | solution.py:30
  64.7 9.0 %collective-permute-start.13 = (bf16[16,4096]{1,0:T(8,128)(2,1)S(1)}, bf16[16,4096]{1,0:T(8,128)(2,1)S(1)}, u32[]{:S(2)}, u32[]{:S(2)}) collective-permute-start(bf16[16,4096]{1,0:T(8,128)(2,1)S(1)} %get-tuple-element.23), channel_id=1, source_target_pairs={{0,1},{1,0},{2,3},{3,2},{4,5},{5,4},{6,7},{7,6},{8,9},{9,8},{10,11... | collective-permute-start | bytes 393224 | tf_op jit(solution)/shard_map/ppermute | solution.py:30
  71.1 7.2 %collective-permute-start.10 = (bf16[16,4096]{1,0:T(8,128)(2,1)S(1)}, bf16[16,4096]{1,0:T(8,128)(2,1)S(1)}, u32[]{:S(2)}, u32[]{:S(2)}) collective-permute-start(bf16[16,4096]{1,0:T(8,128)(2,1)S(1)} %get-tuple-element.21), channel_id=1, source_target_pairs={{0,4},{1,5},{2,6},{3,7},{4,0},{5,1},{6,2},{7,3},{8,12},{9,13},{10,... | collective-permute-start | bytes 393224 | tf_op jit(solution)/shard_map/ppermute | solution.py:30
  71.6 6.6 %collective-permute-start.12 = (bf16[16,4096]{1,0:T(8,128)(2,1)S(1)}, bf16[16,4096]{1,0:T(8,128)(2,1)S(1)}, u32[]{:S(2)}, u32[]{:S(2)}) collective-permute-start(bf16[16,4096]{1,0:T(8,128)(2,1)S(1)} %get-tuple-element.20), channel_id=1, source_target_pairs={{0,6},{1,7},{2,0},{3,1},{4,2},{5,3},{6,4},{7,5},{8,14},{9,15},{10,... | collective-permute-start | bytes 393224 | tf_op jit(solution)/shard_map/ppermute | solution.py:30
  73.7 8.2 %collective-permute-start.8 = (bf16[16,4096]{1,0:T(8,128)(2,1)S(1)}, bf16[16,4096]{1,0:T(8,128)(2,1)S(1)}, u32[]{:S(2)}, u32[]{:S(2)}) collective-permute-start(bf16[16,4096]{1,0:T(8,128)(2,1)S(1)} %get-tuple-element.19), channel_id=1, source_target_pairs={{0,2},{1,3},{2,4},{3,5},{4,6},{5,7},{6,0},{7,1},{8,10},{9,11},{10,... | collective-permute-start | bytes 393224 | tf_op jit(solution)/shard_map/ppermute | solution.py:30
  82.3 8.9 %collective-permute-start.15 = (bf16[16,4096]{1,0:T(8,128)(2,1)S(1)}, bf16[16,4096]{1,0:T(8,128)(2,1)S(1)}, u32[]{:S(2)}, u32[]{:S(2)}) collective-permute-start(bf16[16,4096]{1,0:T(8,128)(2,1)S(1)} %get-tuple-element.10), channel_id=1, source_target_pairs={{0,2},{1,3},{2,4},{3,5},{4,6},{5,7},{6,0},{7,1},{8,10},{9,11},{10,... | collective-permute-start | bytes 393224 | tf_op jit(solution)/shard_map/ppermute | solution.py:30
  85.8 6.0 %collective-permute-start.14 = (bf16[16,4096]{1,0:T(8,128)(2,1)S(1)}, bf16[16,4096]{1,0:T(8,128)(2,1)S(1)}, u32[]{:S(2)}, u32[]{:S(2)}) collective-permute-start(bf16[16,4096]{1,0:T(8,128)(2,1)S(1)} %get-tuple-element.10), channel_id=1, source_target_pairs={{0,1},{1,0},{2,3},{3,2},{4,5},{5,4},{6,7},{7,6},{8,9},{9,8},{10,11... | collective-permute-start | bytes 393224 | tf_op jit(solution)/shard_map/ppermute | solution.py:30
  86.4 5.9 %collective-permute-start.17 = (bf16[16,4096]{1,0:T(8,128)(2,1)S(1)}, bf16[16,4096]{1,0:T(8,128)(2,1)S(1)}, u32[]{:S(2)}, u32[]{:S(2)}) collective-permute-start(bf16[16,4096]{1,0:T(8,128)(2,1)S(1)} %get-tuple-element.10), channel_id=1, source_target_pairs={{0,4},{1,5},{2,6},{3,7},{4,0},{5,1},{6,2},{7,3},{8,12},{9,13},{10,... | collective-permute-start | bytes 393224 | tf_op jit(solution)/shard_map/ppermute | solution.py:30
  88.3 6.8 %collective-permute-start.19 = (bf16[16,4096]{1,0:T(8,128)(2,1)S(1)}, bf16[16,4096]{1,0:T(8,128)(2,1)S(1)}, u32[]{:S(2)}, u32[]{:S(2)}) collective-permute-start(bf16[16,4096]{1,0:T(8,128)(2,1)S(1)} %get-tuple-element.10), channel_id=1, source_target_pairs={{0,6},{1,7},{2,0},{3,1},{4,2},{5,3},{6,4},{7,5},{8,14},{9,15},{10,... | collective-permute-start | bytes 393224 | tf_op jit(solution)/shard_map/ppermute | solution.py:30
  91.2 5.0 %collective-permute-start.16 = (bf16[16,4096]{1,0:T(8,128)(2,1)S(1)}, bf16[16,4096]{1,0:T(8,128)(2,1)S(1)}, u32[]{:S(2)}, u32[]{:S(2)}) collective-permute-start(bf16[16,4096]{1,0:T(8,128)(2,1)S(1)} %collective-permute-done.15), channel_id=1, source_target_pairs={{0,1},{1,0},{2,3},{3,2},{4,5},{5,4},{6,7},{7,6},{8,9},{9,8},{10,11... | collective-permute-start | bytes 393224 | tf_op jit(solution)/shard_map/ppermute | solution.py:30
  92.3 5.8 %collective-permute-start.18 = (bf16[16,4096]{1,0:T(8,128)(2,1)S(1)}, bf16[16,4096]{1,0:T(8,128)(2,1)S(1)}, u32[]{:S(2)}, u32[]{:S(2)}) collective-permute-start(bf16[16,4096]{1,0:T(8,128)(2,1)S(1)} %collective-permute-done.17), channel_id=1, source_target_pairs={{0,1},{1,0},{2,3},{3,2},{4,5},{5,4},{6,7},{7,6},{8,9},{9,8},{10,11... | collective-permute-start | bytes 393224 | tf_op jit(solution)/shard_map/ppermute | solution.py:30
  95.1 5.0 %collective-permute-start.20 = (bf16[16,4096]{1,0:T(8,128)(2,1)S(1)}, bf16[16,4096]{1,0:T(8,128)(2,1)S(1)}, u32[]{:S(2)}, u32[]{:S(2)}) collective-permute-start(bf16[16,4096]{1,0:T(8,128)(2,1)S(1)} %collective-permute-done.19), channel_id=1, source_target_pairs={{0,1},{1,0},{2,3},{3,2},{4,5},{5,4},{6,7},{7,6},{8,9},{9,8},{10,11... | collective-permute-start | bytes 393224 | tf_op jit(solution)/shard_map/ppermute | solution.py:30
  114.0 5.0 %collective-permute-start.21 = (bf16[16,4096]{1,0:T(8,128)(2,1)S(1)}, bf16[16,4096]{1,0:T(8,128)(2,1)S(1)}, u32[]{:S(2)}, u32[]{:S(2)}) collective-permute-start(bf16[16,4096]{1,0:T(8,128)(2,1)S(1)} %get-tuple-element.15), channel_id=1, source_target_pairs={{0,1},{1,0},{2,3},{3,2},{4,5},{5,4},{6,7},{7,6},{8,9},{9,8},{10,11... | collective-permute-start | bytes 393224 | tf_op jit(solution)/shard_map/ppermute | solution.py:30
  115.4 5.0 %collective-permute-start.23 = (bf16[16,4096]{1,0:T(8,128)(2,1)S(1)}, bf16[16,4096]{1,0:T(8,128)(2,1)S(1)}, u32[]{:S(2)}, u32[]{:S(2)}) collective-permute-start(bf16[16,4096]{1,0:T(8,128)(2,1)S(1)} %get-tuple-element.18), channel_id=1, source_target_pairs={{0,1},{1,0},{2,3},{3,2},{4,5},{5,4},{6,7},{7,6},{8,9},{9,8},{10,11... | collective-permute-start | bytes 393224 | tf_op jit(solution)/shard_map/ppermute | solution.py:30
  116.1 5.8 %collective-permute-start.25 = (bf16[16,4096]{1,0:T(8,128)(2,1)S(1)}, bf16[16,4096]{1,0:T(8,128)(2,1)S(1)}, u32[]{:S(2)}, u32[]{:S(2)}) collective-permute-start(bf16[16,4096]{1,0:T(8,128)(2,1)S(1)} %get-tuple-element.17), channel_id=1, source_target_pairs={{0,1},{1,0},{2,3},{3,2},{4,5},{5,4},{6,7},{7,6},{8,9},{9,8},{10,11... | collective-permute-start | bytes 393224 | tf_op jit(solution)/shard_map/ppermute | solution.py:30
  117.5 8.4 %collective-permute-start.27 = (bf16[16,4096]{1,0:T(8,128)(2,1)S(1)}, bf16[16,4096]{1,0:T(8,128)(2,1)S(1)}, u32[]{:S(2)}, u32[]{:S(2)}) collective-permute-start(bf16[16,4096]{1,0:T(8,128)(2,1)S(1)} %get-tuple-element.16), channel_id=1, source_target_pairs={{0,1},{1,0},{2,3},{3,2},{4,5},{5,4},{6,7},{7,6},{8,9},{9,8},{10,11... | collective-permute-start | bytes 393224 | tf_op jit(solution)/shard_map/ppermute | solution.py:30
  121.9 6.9 %collective-permute-start.22 = (bf16[16,4096]{1,0:T(8,128)(2,1)S(1)}, bf16[16,4096]{1,0:T(8,128)(2,1)S(1)}, u32[]{:S(2)}, u32[]{:S(2)}) collective-permute-start(bf16[16,4096]{1,0:T(8,128)(2,1)S(1)} %get-tuple-element.12), channel_id=1, source_target_pairs={{0,2},{1,3},{2,4},{3,5},{4,6},{5,7},{6,0},{7,1},{8,10},{9,11},{10,... | collective-permute-start | bytes 393224 | tf_op jit(solution)/shard_map/ppermute | solution.py:30
  123.1 8.6 %collective-permute-start.24 = (bf16[16,4096]{1,0:T(8,128)(2,1)S(1)}, bf16[16,4096]{1,0:T(8,128)(2,1)S(1)}, u32[]{:S(2)}, u32[]{:S(2)}) collective-permute-start(bf16[16,4096]{1,0:T(8,128)(2,1)S(1)} %get-tuple-element.14), channel_id=1, source_target_pairs={{0,4},{1,5},{2,6},{3,7},{4,0},{5,1},{6,2},{7,3},{8,12},{9,13},{10,... | collective-permute-start | bytes 393224 | tf_op jit(solution)/shard_map/ppermute | solution.py:30
  125.4 6.3 %collective-permute-start.26 = (bf16[16,4096]{1,0:T(8,128)(2,1)S(1)}, bf16[16,4096]{1,0:T(8,128)(2,1)S(1)}, u32[]{:S(2)}, u32[]{:S(2)}) collective-permute-start(bf16[16,4096]{1,0:T(8,128)(2,1)S(1)} %get-tuple-element.13), channel_id=1, source_target_pairs={{0,6},{1,7},{2,0},{3,1},{4,2},{5,3},{6,4},{7,5},{8,14},{9,15},{10,... | collective-permute-start | bytes 393224 | tf_op jit(solution)/shard_map/ppermute | solution.py:30
  (4 other events, 14.9 us)

commit v2 on v1

v2 whole, which is shorter than its diff:
```python
import functools

import jax
import jax.numpy as jnp
from jax import lax
from jax.experimental import pallas as pl
from jax.experimental.pallas import tpu as pltpu
from jax.sharding import PartitionSpec as P

HEADS = 32
KV_HEADS = 8
HEAD_DIM = 128

rope_base = 500000.0
norm_eps = 1e-05

bf16, f32, i32 = jnp.bfloat16, jnp.float32, jnp.int32
VMEM = pl.BlockSpec(memory_space=pltpu.VMEM)


def plane_of(count):
    wide = max(y for y in range(1, count + 1) if count % y == 0 and 2 * y * y <= max(count, 2))
    return count // wide, wide


def shift(block, tall, wide, dz, dy):
    pairs = [
        (z * wide + y, (z + dz) % tall * wide + (y + dy) % wide)
        for z in range(tall)
        for y in range(wide)
    ]
    return lax.ppermute(block, "ctx", pairs)


def gather_blocks(block, tall, wide):
    blocks = {}
    for dz in range(tall):
        blocks[dz, 0] = block if dz == 0 else shift(block, tall, wide, dz, 0)
    for dz in range(tall):
        for dy in range(1, wide):
            blocks[dz, dy] = shift(blocks[dz, 0], tall, wide, 0, dy)
    return [blocks[dz, dy] for dz in range(tall) for dy in range(wide)]


def scatter_sum(parts, tall, wide):
    total = None
    for dz in [*range(1, tall), 0]:
        lane = parts[dz * wide].astype(f32)
        for dy in range(1, wide):
            lane = lane + shift(parts[dz * wide + dy], tall, wide, 0, dy).astype(f32)
        if dz:
            lane = shift(lane.astype(bf16), tall, wide, dz, 0).astype(f32)
        total = lane if total is None else total + lane
    return total


def exchange(parts, tall, wide):
    rows = [[parts[dz * wide + dy] for dz in range(tall)] for dy in range(wide)]
    lanes = [jnp.stack(rows[0])]
    lanes += [shift(jnp.stack(rows[dy]), tall, wide, 0, dy) for dy in range(1, wide)]
    lanes = jnp.stack(lanes, axis=1)
    out = [lanes[0]] + [shift(lanes[dz], tall, wide, dz, 0) for dz in range(1, tall)]
    return jnp.stack(out)


def dot(a, b):
    return jnp.dot(a, b, preferred_element_type=f32)


def fetched(weight):
    return pltpu.with_memory_space_constraint(weight, pltpu.VMEM)


def kernel_call(body, outs, args, scratch=(), limit=16, flops=0):
    return pl.pallas_call(
        body,
        out_shape=[jax.ShapeDtypeStruct(s, d) for s, d in outs],
        in_specs=[VMEM] * len(args),
        out_specs=[VMEM] * len(outs),
        scratch_shapes=list(scratch),
        compiler_params=pltpu.CompilerParams(vmem_limit_bytes=limit << 20),
        cost_estimate=pl.CostEstimate(flops=flops, bytes_accessed=1 << 20, transcendentals=0),
    )(*args)


def tile_of(width, most):
    return width if width <= most else most


def kv_body(count, *refs):
    blocks = refs[:count]
    pick, order, columns, gain, w_key, w_value, normed, own, kv_out, rows = refs[count:]
    total, width = normed.shape
    tile = tile_of(width, 512)
    square = jnp.zeros((total, 1), f32)
    for start in range(0, width, tile):
        span = slice(start, start + tile)
        part = dot(pick[...], jnp.concatenate([b[:, span] for b in blocks], axis=0))
        rows[:, span] = part.astype(bf16)
        square += jnp.sum(part * part, axis=1, keepdims=True)
    own[...] = rows[: own.shape[0], :]
    factor = lax.rsqrt(square / width + norm_eps)
    for start in range(0, width, tile):
        span = slice(start, start + tile)
        part = rows[:, span].astype(f32) * factor * gain[:, span]
        normed[:, span] = part.astype(bf16)
    keys = dot(normed[...], w_key[...]).astype(bf16)
    values = dot(normed[...], w_value[...]).astype(bf16)
    both = jnp.concatenate([keys, values], axis=1)
    turned = lax.dot_general(
        columns[...], both, (((1,), (1,)), ((), ())), preferred_element_type=f32
    ).astype(bf16)
    kv_out[...] = dot(turned, order[...]).astype(bf16)


def query_body(normed, w_query, cosine, sine, query):
    raw = dot(normed[...], w_query[...])
    for head in range(query.shape[1] // HEAD_DIM):
        span = slice(head * HEAD_DIM, (head + 1) * HEAD_DIM)
        one = raw[:, span]
        turned = one * cosine[...] + pltpu.roll(one, HEAD_DIM // 2, 1) * sine[...]
        query[:, span] = turned.astype(bf16)


def attend_body(kv_local, query, key_t, value_t, cosine, sine, key_pos, query_pos, w_output, *rest):
    parts, heads_out = rest[:-1], rest[-1]
    half = HEAD_DIM // 2
    heads = query.shape[1] // HEAD_DIM
    allowed = key_pos[...] <= query_pos[...]
    for group in range(kv_local):
        base = group * HEAD_DIM
        first = key_t[base : base + half, :].astype(f32)
        second = key_t[base + half : base + HEAD_DIM, :].astype(f32)
        keys = jnp.concatenate(
            [first * cosine[...] - second * sine[...], second * cosine[...] + first * sine[...]],
            axis=0,
        ).astype(bf16)
        values = value_t[base : base + HEAD_DIM, :]
        for head in range(group * heads // kv_local, (group + 1) * heads // kv_local):
            span = slice(head * HEAD_DIM, (head + 1) * HEAD_DIM)
            scores = dot(query[:, span], keys) * HEAD_DIM ** (-0.5)
            scores = jnp.where(allowed, scores, -1e30)
            weights = jnp.exp(scores - jnp.max(scores, axis=1, keepdims=True))
            probs = (weights / jnp.sum(weights, axis=1, keepdims=True)).astype(bf16)
            heads_out[:, span] = lax.dot_general(
                probs, values, (((1,), (1,)), ((), ())), preferred_element_type=f32
            ).astype(bf16)
    spread(heads_out, w_output, parts)


def spread(left, weight, parts):
    width = weight.shape[1]
    tile = tile_of(width, 512)
    share = parts[0].shape[0]
    for start in range(0, width, tile):
        span = slice(start, start + tile)
        product = dot(left[...], weight[:, span]).astype(bf16)
        for index, part in enumerate(parts):
            part[:, span] = product[index * share : (index + 1) * share, :]


def mlp_body(count, *refs):
    blocks, (w_gate, w_up, w_down) = refs[:count], refs[count : count + 3]
    parts, (piece, inner) = refs[count + 3 : -2], refs[-2:]
    share = blocks[0].shape[0]
    for index, block in enumerate(blocks):
        piece[index * share : (index + 1) * share, :] = block[...]
    width = w_gate.shape[1]
    tile = tile_of(width, 256)
    for start in range(0, width, tile):
        span = slice(start, start + tile)
        gate = dot(piece[...], w_gate[:, span])
        upward = dot(piece[...], w_up[:, span])
        inner[:, span] = (gate / (1.0 + jnp.exp(-gate)) * upward).astype(bf16)
    spread(inner, w_down, parts)


def onehot_dot(onehot, values):
    return dot(onehot, values).astype(values.dtype)


def on_device(
    activations,
    routed,
    balance,
    w_query,
    w_key,
    w_value,
    w_output,
    attn_gain,
    mlp_gain,
    w_gate,
    w_up,
    w_down,
    w_router,
):
    shard_count = lax.axis_size("ctx")
    tall, wide = plane_of(shard_count)
    me = lax.axis_index("ctx")
    my_z, my_y = me // wide, me % wide
    tok_shard, model = activations.shape
    total = routed.shape[0]
    share = total // shard_count
    capacity = 2 * share
    local_heads = w_query.shape[1] // HEAD_DIM
    group_size = HEADS // KV_HEADS

    row_ids = jnp.arange(total, dtype=i32)
    low = me * tok_shard
    my_first = jnp.sum((routed < low).astype(i32))
    local = routed - low
    is_here = (local >= 0) & (local < tok_shard)
    slots = jnp.arange(capacity, dtype=i32)
    hit = is_here[None, :] & (row_ids[None, :] - my_first == slots[:, None])
    token = jnp.sum(jnp.where(hit, local[None, :] + 1, 0), axis=1) - 1
    pick_out = (token[:, None] == jnp.arange(tok_shard, dtype=i32)[None, :]).astype(bf16)
    outgoing = onehot_dot(pick_out, activations)
    blocks = gather_blocks(outgoing, tall, wide)

    home = routed // tok_shard
    before = home[None, :] < home[:, None]
    in_block = row_ids - jnp.sum(before.astype(i32), axis=1)
    from_z, from_y = (my_z - home // wide) % tall, (my_y - home % wide) % wide
    slot_of_row = (from_z * wide + from_y) * capacity + in_block
    same = (balance[None, :] == balance[:, None]) & (row_ids[None, :] < row_ids[:, None])
    rank = jnp.sum(same.astype(i32), axis=1)
    to_z, to_y = (balance // wide - my_z) % tall, (balance % wide - my_y) % wide
    place_of_row = (to_z * wide + to_y) * share + rank
    placed = place_of_row[None, :] == row_ids[:, None]
    slot_at = jnp.sum(jnp.where(placed, slot_of_row[None, :], 0), axis=1)
    positions = jnp.sum(jnp.where(placed, routed[None, :], 0), axis=1)
    pick_rows = (
        slot_at[:, None] == jnp.arange(shard_count * capacity, dtype=i32)[None, :]
    ).astype(bf16)
    in_order = placed.astype(bf16)

    half = HEAD_DIM // 2
    steps_f = jnp.arange(half, dtype=f32)
    freqs = jnp.exp(-jnp.log(f32(rope_base)) * (2.0 * steps_f / HEAD_DIM))
    q_angles = positions.astype(f32)[:, None] * freqs[None, :]
    q_cos, q_sin = jnp.cos(q_angles), jnp.sin(q_angles)
    q_cos = jnp.concatenate([q_cos, q_cos], axis=1)
    q_sin = jnp.concatenate([-q_sin, q_sin], axis=1)
    k_angles = freqs[:, None] * routed.astype(f32)[None, :]
    k_cos, k_sin = jnp.cos(k_angles), jnp.sin(k_angles)

    key_cols = w_key.shape[1]
    depth = key_cols // KV_HEADS
    kv_local = max(1, local_heads // group_size)
    at = jnp.arange(2 * key_cols, dtype=i32)
    head_at, side_at, entry_at = at // (2 * depth), at // depth % 2, at % depth
    column_at = side_at * key_cols + entry_at * KV_HEADS + head_at
    columns = (column_at[:, None] == at[None, :]).astype(bf16)
    normed, own, kv_out = kernel_call(
        functools.partial(kv_body, len(blocks)),
        [((total, model), bf16), ((share, model), bf16), ((2 * key_cols, total), bf16)],
        [
            *blocks,
            pick_rows,
            in_order,
            columns,
            attn_gain.reshape(1, model),
            fetched(w_key),
            fetched(w_value),
        ],
        [pltpu.VMEM((total, model), bf16)],
        flops=2 * total * model * 512,
    )
    kv_heads = kv_out.reshape(KV_HEADS, 2 * depth, total)
    sent = []
    for dz in range(tall):
        for dy in range(wide):
            peer = (my_z + dz) % tall * wide + (my_y + dy) % wide
            first = peer * local_heads // group_size
            sent.append(lax.dynamic_slice_in_dim(kv_heads, first, kv_local, 0))
    arrived = exchange(sent, tall, wide)
    from_where = jnp.arange(shard_count, dtype=i32)
    arrived_at = (my_z - from_where // wide) % tall * wide + (my_y - from_where % wide) % wide
    arrived = arrived.reshape(shard_count, kv_local * 2 * depth * total)
    in_turn = (arrived_at[:, None] == from_where[None, :]).astype(bf16)
    arrived = onehot_dot(in_turn, arrived).reshape(shard_count, kv_local, 2, depth, total)
    arrived = jnp.transpose(arrived, (2, 1, 0, 3, 4)).reshape(2, kv_local * HEAD_DIM, total)

    (query,) = kernel_call(
        query_body,
        [((total, local_heads * HEAD_DIM), bf16)],
        [normed, fetched(w_query), q_cos, q_sin],
        flops=2 * total * model * local_heads * HEAD_DIM,
    )
    share_block = ((share, model), bf16)
    attn_parts = kernel_call(
        functools.partial(attend_body, kv_local),
        [share_block] * shard_count,
        [
            query,
            arrived[0],
            arrived[1],
            k_cos,
            k_sin,
            routed.reshape(1, total),
            positions.reshape(total, 1),
            fetched(w_output),
        ],
        [pltpu.VMEM((total, local_heads * HEAD_DIM), bf16)],
        flops=2 * total * model * local_heads * HEAD_DIM,
    )
    attn_own = scatter_sum(attn_parts, tall, wide)
    own_rows = own.astype(f32)
    hidden = own_rows + attn_own
    mean_sq = jnp.mean(hidden * hidden, axis=-1, keepdims=True)
    mnorm = (hidden * lax.rsqrt(mean_sq + norm_eps) * mlp_gain).astype(bf16)
    pieces = gather_blocks(mnorm, tall, wide)
    hidden_units = w_gate.shape[1]
    mlp_parts = kernel_call(
        functools.partial(mlp_body, shard_count),
        [share_block] * shard_count,
        [*pieces, fetched(w_gate), fetched(w_up), fetched(w_down)],
        [pltpu.VMEM((total, model), bf16), pltpu.VMEM((total, hidden_units), bf16)],
        flops=6 * total * model * hidden_units,
    )
    back = [
        mlp_parts[(-dz) % tall * wide + (-dy) % wide] for dz in range(tall) for dy in range(wide)
    ]
    mlp_own = scatter_sum(back, tall, wide)
    router_score = jnp.sum(own_rows * w_router[None, :], axis=1, keepdims=True)
    return (own_rows + router_score * (attn_own + mlp_own)).astype(bf16)


def solution(mesh):
    in_specs = (
        P(("dp", "ctx"), None),
        P("dp"),
        P("dp"),
        P(None, "ctx"),
        P(None, "ctx"),
        P(None, "ctx"),
        P("ctx", None),
        P(),
        P(),
        P(None, "ctx"),
        P(None, "ctx"),
        P("ctx", None),
        P(),
    )
    out_specs = P(("dp", "ctx"), None)
    return jax.shard_map(
        on_device, mesh=mesh, in_specs=in_specs, out_specs=out_specs, check_vma=False
    )
```

time: 134 us -> 129 us (0.963)
  matrix products: 22.6 us -> 0.52 us
  local copies, waits for them, and re-layouts: 1.46 us -> 11.1 us
  Pallas kernels: 0 us -> 7.61 us
  starting transfers between devices: 45.2 us -> 50.2 us
  waiting for transfers between devices: 54.4 us -> 50.8 us
  other arithmetic: 9.15 us -> 7.64 us
    dot_general x11 -> x2, matrix products: 22.6 us -> 0.52 us  [dot(): return jnp.dot(a, b, preferred_element_type=f32)]
    ppermute x28 -> x32, starting transfers between devices: 38.1 us -> 50.2 us  [shift(): return lax.ppermute(block, 'ctx', pairs)]
    unnamed x28 -> x26, local copies, waits for them, and re-layouts: 0.4 us -> 10.9 us
    pallas_call x0 -> x4, Pallas kernels: none -> 7.61 us  [kernel_call(): pl.pallas_call(body, out_shape=[jax.ShapeDtypeStruct(s, d) for s, d in ou...]
    all_to_all x1 -> x0, starting transfers between devices: 7.1 us -> none  [on_device(): inbound = lax.all_to_all(outbound, 'ctx', 0, 0, tiled=True)]
    all_to_all x1 -> x0, waiting for transfers between devices: 3.58 us -> none  [on_device(): inbound = lax.all_to_all(outbound, 'ctx', 0, 0, tiled=True)]
    ppermute x28 -> x32, waiting for transfers between devices: 50.9 us -> 50.8 us  [shift(): return lax.ppermute(block, 'ctx', pairs)]
  transfers between devices with their start and end apart: 29 -> 32, of which waited for: 19 -> 19; matrix products, arithmetic and copies ran while one was open for 5% -> 3% of each run, Pallas kernels for 0% -> 1%
where the time goes in v2:
time: 129 us
  waiting for transfers between devices  50.8 us (39%)
  starting transfers between devices  50.2 us (39%)
  local copies, waits for them, and re-layouts  11.1 us (9%)
  other arithmetic  7.64 us (6%)
  Pallas kernels  7.61 us (6%)
    ppermute x32, waiting for transfers between devices, shift(): return lax.ppermute(block, 'ctx', pairs)  50.8 us
    ppermute x32, starting transfers between devices, shift(): return lax.ppermute(block, 'ctx', pairs)  50.2 us
    unnamed x26, local copies, waits for them, and re-layouts  10.9 us
    pallas_call x4, Pallas kernels, kernel_call(): pl.pallas_call(body, out_shape=[jax.ShapeDtypeStruct(s, d) for s, d in ou...  7.61 us
  transfers between devices with their start and end apart: 32, of which 19 were waited for; matrix products, arithmetic and copies ran while one was open for 3% of the time, Pallas kernels for 1%

profile of v2, /device:TPU:0, one launch (start us, length us, event | category | flops | bytes accessed | tf_op | source)
XLA Modules:
  0.0 128.5 jit_solution(4180258984272654051)
XLA Ops:
  3.4 3.0 %collective-permute-start = (bf16[32,4096]{1,0:T(8,128)(2,1)S(1)}, bf16[32,4096]{1,0:T(8,128)(2,1)S(1)}, u32[]{:S(2)}, u32[]{:S(2)}) collective-permute-start(bf16[32,4096]{1,0:T(8,128)(2,1)S(1)} %convolution_convert_fusion.refs_0_), channel_id=1, source_target_pairs={{0,1},{1,0},{2,3},{3,2},{4,5},{5,4},{6,7},{7,6},{8,9},{9,8},{10,11... | collective-permute-start | bytes 786440 | tf_op jit(solution)/shard_map/ppermute | solution.py:32
  6.4 1.6 %collective-permute-start.1 = (bf16[32,4096]{1,0:T(8,128)(2,1)S(1)}, bf16[32,4096]{1,0:T(8,128)(2,1)S(1)}, u32[]{:S(2)}, u32[]{:S(2)}) collective-permute-start(bf16[32,4096]{1,0:T(8,128)(2,1)S(1)} %convolution_convert_fusion.refs_0_), channel_id=1, source_target_pairs={{0,2},{1,3},{2,4},{3,5},{4,6},{5,7},{6,0},{7,1},{8,10},{9,11},{10,... | collective-permute-start | bytes 786440 | tf_op jit(solution)/shard_map/ppermute | solution.py:32
  8.0 2.6 %collective-permute-start.3 = (bf16[32,4096]{1,0:T(8,128)(2,1)S(1)}, bf16[32,4096]{1,0:T(8,128)(2,1)S(1)}, u32[]{:S(2)}, u32[]{:S(2)}) collective-permute-start(bf16[32,4096]{1,0:T(8,128)(2,1)S(1)} %convolution_convert_fusion.refs_0_), channel_id=1, source_target_pairs={{0,4},{1,5},{2,6},{3,7},{4,0},{5,1},{6,2},{7,3},{8,12},{9,13},{10,... | collective-permute-start | bytes 786440 | tf_op jit(solution)/shard_map/ppermute | solution.py:32
  15.1 2.4 %collective-permute-done.1.refs_2_ = bf16[32,4096]{1,0:T(8,128)(2,1)S(1)} collective-permute-done((bf16[32,4096]{1,0:T(8,128)(2,1)S(1)}, bf16[32,4096]{1,0:T(8,128)(2,1)S(1)}, u32[]{:S(2)}, u32[]{:S(2)}) %collective-permute-start.1) | collective-permute-done | bytes 262176 | tf_op jit(solution)/shard_map/ppermute | solution.py:32
  17.8 9.6 %collective-permute-done.3.refs_4_ = bf16[32,4096]{1,0:T(8,128)(2,1)S(1)} collective-permute-done((bf16[32,4096]{1,0:T(8,128)(2,1)S(1)}, bf16[32,4096]{1,0:T(8,128)(2,1)S(1)}, u32[]{:S(2)}, u32[]{:S(2)}) %collective-permute-start.3) | collective-permute-done | bytes 262176 | tf_op jit(solution)/shard_map/ppermute | solution.py:32
  27.9 1.5 %collective-permute-start.6 = (bf16[32,4096]{1,0:T(8,128)(2,1)S(1)}, bf16[32,4096]{1,0:T(8,128)(2,1)S(1)}, u32[]{:S(2)}, u32[]{:S(2)}) collective-permute-start(bf16[32,4096]{1,0:T(8,128)(2,1)S(1)} %collective-permute-done.5.refs_6_), channel_id=1, source_target_pairs={{0,1},{1,0},{2,3},{3,2},{4,5},{5,4},{6,7},{7,6},{8,9},{9,8},{10,11... | collective-permute-start | bytes 786440 | tf_op jit(solution)/shard_map/ppermute | solution.py:32
  30.0 6.5 %collective-permute-done.4.refs_5_ = bf16[32,4096]{1,0:T(8,128)(2,1)S(1)} collective-permute-done((bf16[32,4096]{1,0:T(8,128)(2,1)S(1)}, bf16[32,4096]{1,0:T(8,128)(2,1)S(1)}, u32[]{:S(2)}, u32[]{:S(2)}) %collective-permute-start.4) | collective-permute-done | bytes 262176 | tf_op jit(solution)/shard_map/ppermute | solution.py:32
  36.6 4.6 %collective-permute-done.6.refs_7_ = bf16[32,4096]{1,0:T(8,128)(2,1)S(1)} collective-permute-done((bf16[32,4096]{1,0:T(8,128)(2,1)S(1)}, bf16[32,4096]{1,0:T(8,128)(2,1)S(1)}, u32[]{:S(2)}, u32[]{:S(2)}) %collective-permute-start.6) | collective-permute-done | bytes 262176 | tf_op jit(solution)/shard_map/ppermute | solution.py:32
  44.3 1.7 %shard_map.127 = (bf16[128,4096]{1,0:T(8,128)(2,1)S(1)}, bf16[16,4096]{1,0:T(8,128)(2,1)S(1)}, bf16[256,128]{1,0:T(8,128)(2,1)S(1)}) custom-call(bf16[32,4096]{1,0:T(8,128)(2,1)S(1)} %convolution_convert_fusion.refs_0_, bf16[32,4096]{1,0:T(8,128)(2,1)S(1)} %collective-permute-done.refs_1_, bf16[32,4096]{1,0:T(8,128)(2,1)S(1)} %collective-permute-done.1.refs_2_, ...), custom_call_target="tpu_custom_call" | custom-call | flops 536870912 | bytes 1048576 | tf_op jit(solution)/shard_map/pallas_call | solution.py:75
  46.7 3.4 %collective-permute-done.7 = bf16[4,1,32,128]{3,2,1,0:T(8,128)(2,1)S(1)} collective-permute-done((bf16[4,1,32,128]{3,2,1,0:T(8,128)(2,1)S(1)}, bf16[4,1,32,128]{3,2,1,0:T(8,128)(2,1)S(1)}, u32[]{:S(2)}, u32[]{:S(2)}) %collective-permute-start.7) | collective-permute-done | bytes 32800 | tf_op jit(solution)/shard_map/ppermute | solution.py:32
  50.1 5.9 %collective-permute-start.10 = (bf16[2,1,32,128]{3,2,0,1:T(8,128)(2,1)S(1)}, bf16[2,1,32,128]{3,2,0,1:T(8,128)(2,1)S(1)}, u32[]{:S(2)}, u32[]{:S(2)}) collective-permute-start(bf16[2,1,32,128]{3,2,0,1:T(8,128)(2,1)S(1)} %get-tuple-element.52), channel_id=1, source_target_pairs={{0,6},{1,7},{2,0},{3,1},{4,2},{5,3},{6,4},{7,5},{8,14},{9,15},{10,... | collective-permute-start | bytes 49160 | tf_op jit(solution)/shard_map/ppermute | solution.py:32
  56.7 2.2 %copy-done.4 = bf16[4096,512]{1,0:T(8,128)(2,1)S(1)} copy-done((bf16[4096,512]{1,0:T(8,128)(2,1)S(1)}, bf16[4096,512]{1,0:T(8,128)(2,1)}, u32[]{:S(2)}) %copy-start.4) | copy-done | bytes 4194328
  61.8 2.2 %copy-done.3 = bf16[512,4096]{1,0:T(8,128)(2,1)S(1)} copy-done((bf16[512,4096]{1,0:T(8,128)(2,1)S(1)}, bf16[512,4096]{1,0:T(8,128)(2,1)}, u32[]{:S(2)}) %copy-start.3) | copy-done | bytes 4194328
  64.0 1.5 %shard_map.129 = (bf16[16,4096]{1,0:T(8,128)(2,1)S(1)}, bf16[16,4096]{1,0:T(8,128)(2,1)S(1)}, bf16[16,4096]{1,0:T(8,128)(2,1)S(1)}, bf16[16,4096]{1,0:T(8,128)(2...) custom-call(bf16[128,512]{1,0:T(8,128)(2,1)S(1)} %shard_map.128.quer, ...), custom_call_target="tpu_custom_call" | custom-call | flops 536870912 | bytes 1048576 | tf_op jit(solution)/shard_map/pallas_call | solution.py:75
  66.1 1.5 %collective-permute-start.17 = (bf16[16,4096]{1,0:T(8,128)(2,1)S(1)}, bf16[16,4096]{1,0:T(8,128)(2,1)S(1)}, u32[]{:S(2)}, u32[]{:S(2)}) collective-permute-start(bf16[16,4096]{1,0:T(8,128)(2,1)S(1)} %get-tuple-element.34), channel_id=1, source_target_pairs={{0,1},{1,0},{2,3},{3,2},{4,5},{5,4},{6,7},{7,6},{8,9},{9,8},{10,11... | collective-permute-start | bytes 393224 | tf_op jit(solution)/shard_map/ppermute | solution.py:32
  68.1 1.5 %collective-permute-start.11 = (bf16[16,4096]{1,0:T(8,128)(2,1)S(1)}, bf16[16,4096]{1,0:T(8,128)(2,1)S(1)}, u32[]{:S(2)}, u32[]{:S(2)}) collective-permute-start(bf16[16,4096]{1,0:T(8,128)(2,1)S(1)} %get-tuple-element.28), channel_id=1, source_target_pairs={{0,1},{1,0},{2,3},{3,2},{4,5},{5,4},{6,7},{7,6},{8,9},{9,8},{10,11... | collective-permute-start | bytes 393224 | tf_op jit(solution)/shard_map/ppermute | solution.py:32
  70.7 2.4 %collective-permute-start.16 = (bf16[16,4096]{1,0:T(8,128)(2,1)S(1)}, bf16[16,4096]{1,0:T(8,128)(2,1)S(1)}, u32[]{:S(2)}, u32[]{:S(2)}) collective-permute-start(bf16[16,4096]{1,0:T(8,128)(2,1)S(1)} %add_convert_fusion.3), channel_id=1, source_target_pairs={{0,6},{1,7},{2,0},{3,1},{4,2},{5,3},{6,4},{7,5},{8,14},{9,15},{10,... | collective-permute-start | bytes 393224 | tf_op jit(solution)/shard_map/ppermute | solution.py:32
  74.9 1.7 %collective-permute-start.12 = (bf16[16,4096]{1,0:T(8,128)(2,1)S(1)}, bf16[16,4096]{1,0:T(8,128)(2,1)S(1)}, u32[]{:S(2)}, u32[]{:S(2)}) collective-permute-start(bf16[16,4096]{1,0:T(8,128)(2,1)S(1)} %add_convert_fusion.5), channel_id=1, source_target_pairs={{0,2},{1,3},{2,4},{3,5},{4,6},{5,7},{6,0},{7,1},{8,10},{9,11},{10,... | collective-permute-start | bytes 393224 | tf_op jit(solution)/shard_map/ppermute | solution.py:32
  76.8 8.6 %collective-permute-done.14 = bf16[16,4096]{1,0:T(8,128)(2,1)S(1)} collective-permute-done((bf16[16,4096]{1,0:T(8,128)(2,1)S(1)}, bf16[16,4096]{1,0:T(8,128)(2,1)S(1)}, u32[]{:S(2)}, u32[]{:S(2)}) %collective-permute-start.14) | collective-permute-done | bytes 131104 | tf_op jit(solution)/shard_map/ppermute | solution.py:32
  85.8 1.6 %collective-permute-start.19 = (bf16[16,4096]{1,0:T(8,128)(2,1)S(1)}, bf16[16,4096]{1,0:T(8,128)(2,1)S(1)}, u32[]{:S(2)}, u32[]{:S(2)}) collective-permute-start(bf16[16,4096]{1,0:T(8,128)(2,1)S(1)} %multiply_convert_fusion.refs_0_), channel_id=1, source_target_pairs={{0,2},{1,3},{2,4},{3,5},{4,6},{5,7},{6,0},{7,1},{8,10},{9,11},{10,... | collective-permute-start | bytes 393224 | tf_op jit(solution)/shard_map/ppermute | solution.py:32
  87.4 2.0 %collective-permute-start.21 = (bf16[16,4096]{1,0:T(8,128)(2,1)S(1)}, bf16[16,4096]{1,0:T(8,128)(2,1)S(1)}, u32[]{:S(2)}, u32[]{:S(2)}) collective-permute-start(bf16[16,4096]{1,0:T(8,128)(2,1)S(1)} %multiply_convert_fusion.refs_0_), channel_id=1, source_target_pairs={{0,4},{1,5},{2,6},{3,7},{4,0},{5,1},{6,2},{7,3},{8,12},{9,13},{10,... | collective-permute-start | bytes 393224 | tf_op jit(solution)/shard_map/ppermute | solution.py:32
  89.4 2.8 %collective-permute-start.23 = (bf16[16,4096]{1,0:T(8,128)(2,1)S(1)}, bf16[16,4096]{1,0:T(8,128)(2,1)S(1)}, u32[]{:S(2)}, u32[]{:S(2)}) collective-permute-start(bf16[16,4096]{1,0:T(8,128)(2,1)S(1)} %multiply_convert_fusion.refs_0_), channel_id=1, source_target_pairs={{0,6},{1,7},{2,0},{3,1},{4,2},{5,3},{6,4},{7,5},{8,14},{9,15},{10,... | collective-permute-start | bytes 393224 | tf_op jit(solution)/shard_map/ppermute | solution.py:32
  92.8 1.5 %collective-permute-start.20 = (bf16[16,4096]{1,0:T(8,128)(2,1)S(1)}, bf16[16,4096]{1,0:T(8,128)(2,1)S(1)}, u32[]{:S(2)}, u32[]{:S(2)}) collective-permute-start(bf16[16,4096]{1,0:T(8,128)(2,1)S(1)} %collective-permute-done.19.refs_2_), channel_id=1, source_target_pairs={{0,1},{1,0},{2,3},{3,2},{4,5},{5,4},{6,7},{7,6},{8,9},{9,8},{10,11... | collective-permute-start | bytes 393224 | tf_op jit(solution)/shard_map/ppermute | solution.py:32
  96.0 1.5 %collective-permute-start.24 = (bf16[16,4096]{1,0:T(8,128)(2,1)S(1)}, bf16[16,4096]{1,0:T(8,128)(2,1)S(1)}, u32[]{:S(2)}, u32[]{:S(2)}) collective-permute-start(bf16[16,4096]{1,0:T(8,128)(2,1)S(1)} %collective-permute-done.23.refs_6_), channel_id=1, source_target_pairs={{0,1},{1,0},{2,3},{3,2},{4,5},{5,4},{6,7},{7,6},{8,9},{9,8},{10,11... | collective-permute-start | bytes 393224 | tf_op jit(solution)/shard_map/ppermute | solution.py:32
  98.7 1.8 %collective-permute-done.22.refs_5_ = bf16[16,4096]{1,0:T(8,128)(2,1)S(1)} collective-permute-done((bf16[16,4096]{1,0:T(8,128)(2,1)S(1)}, bf16[16,4096]{1,0:T(8,128)(2,1)S(1)}, u32[]{:S(2)}, u32[]{:S(2)}) %collective-permute-start.22) | collective-permute-done | bytes 131104 | tf_op jit(solution)/shard_map/ppermute | solution.py:32
  100.4 1.7 %collective-permute-done.24.refs_7_ = bf16[16,4096]{1,0:T(8,128)(2,1)S(1)} collective-permute-done((bf16[16,4096]{1,0:T(8,128)(2,1)S(1)}, bf16[16,4096]{1,0:T(8,128)(2,1)S(1)}, u32[]{:S(2)}, u32[]{:S(2)}) %collective-permute-start.24) | collective-permute-done | bytes 131104 | tf_op jit(solution)/shard_map/ppermute | solution.py:32
  102.2 3.4 %copy-done.2 = bf16[1024,4096]{1,0:T(8,128)(2,1)S(1)} copy-done((bf16[1024,4096]{1,0:T(8,128)(2,1)S(1)}, bf16[1024,4096]{1,0:T(8,128)(2,1)}, u32[]{:S(2)}) %copy-start.2) | copy-done | bytes 8388632
  105.5 3.6 %shard_map.130 = (bf16[16,4096]{1,0:T(8,128)(2,1)S(1)}, bf16[16,4096]{1,0:T(8,128)(2,1)S(1)}, bf16[16,4096]{1,0:T(8,128)(2,1)S(1)}, bf16[16,4096]{1,0:T(8,128)(2...) custom-call(bf16[16,4096]{1,0:T(8,128)(2,1)S(1)} %multiply_convert_f, ...), custom_call_target="tpu_custom_call" | custom-call | flops 3221225472 | bytes 1048576 | tf_op jit(solution)/shard_map/pallas_call | solution.py:75
  114.2 4.9 %collective-permute-start.30 = (bf16[16,4096]{1,0:T(8,128)(2,1)S(1)}, bf16[16,4096]{1,0:T(8,128)(2,1)S(1)}, u32[]{:S(2)}, u32[]{:S(2)}) collective-permute-start(bf16[16,4096]{1,0:T(8,128)(2,1)S(1)} %add_convert_fusion), channel_id=1, source_target_pairs={{0,6},{1,7},{2,0},{3,1},{4,2},{5,3},{6,4},{7,5},{8,14},{9,15},{10,... | collective-permute-start | bytes 393224 | tf_op jit(solution)/shard_map/ppermute | solution.py:32
  119.2 1.7 %collective-permute-start.28 = (bf16[16,4096]{1,0:T(8,128)(2,1)S(1)}, bf16[16,4096]{1,0:T(8,128)(2,1)S(1)}, u32[]{:S(2)}, u32[]{:S(2)}) collective-permute-start(bf16[16,4096]{1,0:T(8,128)(2,1)S(1)} %add_convert_fusion.1), channel_id=1, source_target_pairs={{0,4},{1,5},{2,6},{3,7},{4,0},{5,1},{6,2},{7,3},{8,12},{9,13},{10,... | collective-permute-start | bytes 393224 | tf_op jit(solution)/shard_map/ppermute | solution.py:32
  120.9 1.7 %collective-permute-start.26 = (bf16[16,4096]{1,0:T(8,128)(2,1)S(1)}, bf16[16,4096]{1,0:T(8,128)(2,1)S(1)}, u32[]{:S(2)}, u32[]{:S(2)}) collective-permute-start(bf16[16,4096]{1,0:T(8,128)(2,1)S(1)} %add_convert_fusion.2), channel_id=1, source_target_pairs={{0,2},{1,3},{2,4},{3,5},{4,6},{5,7},{6,0},{7,1},{8,10},{9,11},{10,... | collective-permute-start | bytes 393224 | tf_op jit(solution)/shard_map/ppermute | solution.py:32
  122.6 3.7 %collective-permute-done.28 = bf16[16,4096]{1,0:T(8,128)(2,1)S(1)} collective-permute-done((bf16[16,4096]{1,0:T(8,128)(2,1)S(1)}, bf16[16,4096]{1,0:T(8,128)(2,1)S(1)}, u32[]{:S(2)}, u32[]{:S(2)}) %collective-permute-start.28) | collective-permute-done | bytes 131104 | tf_op jit(solution)/shard_map/ppermute | solution.py:32
  (103 shorter events, 31.6 us)
Async XLA Ops:
  3.4 26.6 %collective-permute-start = (bf16[32,4096]{1,0:T(8,128)(2,1)S(1)}, bf16[32,4096]{1,0:T(8,128)(2,1)S(1)}, u32[]{:S(2)}, u32[]{:S(2)}) collective-permute-start(bf16[32,4096]{1,0:T(8,128)(2,1)S(1)} %convolution_convert_fusion.refs_0_), channel_id=1, source_target_pairs={{0,1},{1,0},{2,3},{3,2},{4,5},{5,4},{6,7},{7,6},{8,9},{9,8},{10,11... | collective-permute-start | bytes 786440 | tf_op jit(solution)/shard_map/ppermute | solution.py:32
  6.4 11.2 %collective-permute-start.1 = (bf16[32,4096]{1,0:T(8,128)(2,1)S(1)}, bf16[32,4096]{1,0:T(8,128)(2,1)S(1)}, u32[]{:S(2)}, u32[]{:S(2)}) collective-permute-start(bf16[32,4096]{1,0:T(8,128)(2,1)S(1)} %convolution_convert_fusion.refs_0_), channel_id=1, source_target_pairs={{0,2},{1,3},{2,4},{3,5},{4,6},{5,7},{6,0},{7,1},{8,10},{9,11},{10,... | collective-permute-start | bytes 786440 | tf_op jit(solution)/shard_map/ppermute | solution.py:32
  8.0 19.4 %collective-permute-start.3 = (bf16[32,4096]{1,0:T(8,128)(2,1)S(1)}, bf16[32,4096]{1,0:T(8,128)(2,1)S(1)}, u32[]{:S(2)}, u32[]{:S(2)}) collective-permute-start(bf16[32,4096]{1,0:T(8,128)(2,1)S(1)} %convolution_convert_fusion.refs_0_), channel_id=1, source_target_pairs={{0,4},{1,5},{2,6},{3,7},{4,0},{5,1},{6,2},{7,3},{8,12},{9,13},{10,... | collective-permute-start | bytes 786440 | tf_op jit(solution)/shard_map/ppermute | solution.py:32
  10.6 17.3 %collective-permute-start.5 = (bf16[32,4096]{1,0:T(8,128)(2,1)S(1)}, bf16[32,4096]{1,0:T(8,128)(2,1)S(1)}, u32[]{:S(2)}, u32[]{:S(2)}) collective-permute-start(bf16[32,4096]{1,0:T(8,128)(2,1)S(1)} %convolution_convert_fusion.refs_0_), channel_id=1, source_target_pairs={{0,6},{1,7},{2,0},{3,1},{4,2},{5,3},{6,4},{7,5},{8,14},{9,15},{10,... | collective-permute-start | bytes 786440 | tf_op jit(solution)/shard_map/ppermute | solution.py:32
  17.6 12.5 %collective-permute-start.2 = (bf16[32,4096]{1,0:T(8,128)(2,1)S(1)}, bf16[32,4096]{1,0:T(8,128)(2,1)S(1)}, u32[]{:S(2)}, u32[]{:S(2)}) collective-permute-start(bf16[32,4096]{1,0:T(8,128)(2,1)S(1)} %collective-permute-done.1.refs_2_), channel_id=1, source_target_pairs={{0,1},{1,0},{2,3},{3,2},{4,5},{5,4},{6,7},{7,6},{8,9},{9,8},{10,11... | collective-permute-start | bytes 786440 | tf_op jit(solution)/shard_map/ppermute | solution.py:32
  27.4 9.2 %collective-permute-start.4 = (bf16[32,4096]{1,0:T(8,128)(2,1)S(1)}, bf16[32,4096]{1,0:T(8,128)(2,1)S(1)}, u32[]{:S(2)}, u32[]{:S(2)}) collective-permute-start(bf16[32,4096]{1,0:T(8,128)(2,1)S(1)} %collective-permute-done.3.refs_4_), channel_id=1, source_target_pairs={{0,1},{1,0},{2,3},{3,2},{4,5},{5,4},{6,7},{7,6},{8,9},{9,8},{10,11... | collective-permute-start | bytes 786440 | tf_op jit(solution)/shard_map/ppermute | solution.py:32
  27.9 13.2 %collective-permute-start.6 = (bf16[32,4096]{1,0:T(8,128)(2,1)S(1)}, bf16[32,4096]{1,0:T(8,128)(2,1)S(1)}, u32[]{:S(2)}, u32[]{:S(2)}) collective-permute-start(bf16[32,4096]{1,0:T(8,128)(2,1)S(1)} %collective-permute-done.5.refs_6_), channel_id=1, source_target_pairs={{0,1},{1,0},{2,3},{3,2},{4,5},{5,4},{6,7},{7,6},{8,9},{9,8},{10,11... | collective-permute-start | bytes 786440 | tf_op jit(solution)/shard_map/ppermute | solution.py:32
  46.1 4.0 %collective-permute-start.7 = (bf16[4,1,32,128]{3,2,1,0:T(8,128)(2,1)S(1)}, bf16[4,1,32,128]{3,2,1,0:T(8,128)(2,1)S(1)}, u32[]{:S(2)}, u32[]{:S(2)}) collective-permute-start(bf16[4,1,32,128]{3,2,1,0:T(8,128)(2,1)S(1)} %pad_maximum_fusion.3), channel_id=1, source_target_pairs={{0,1},{1,0},{2,3},{3,2},{4,5},{5,4},{6,7},{7,6},{8,9},{9,8},{10,11... | collective-permute-start | bytes 98312 | tf_op jit(solution)/shard_map/ppermute | solution.py:32
  50.1 9.6 %collective-permute-start.10 = (bf16[2,1,32,128]{3,2,0,1:T(8,128)(2,1)S(1)}, bf16[2,1,32,128]{3,2,0,1:T(8,128)(2,1)S(1)}, u32[]{:S(2)}, u32[]{:S(2)}) collective-permute-start(bf16[2,1,32,128]{3,2,0,1:T(8,128)(2,1)S(1)} %get-tuple-element.52), channel_id=1, source_target_pairs={{0,6},{1,7},{2,0},{3,1},{4,2},{5,3},{6,4},{7,5},{8,14},{9,15},{10,... | collective-permute-start | bytes 49160 | tf_op jit(solution)/shard_map/ppermute | solution.py:32
  56.0 4.6 %collective-permute-start.9 = (bf16[2,1,32,128]{3,2,0,1:T(8,128)(2,1)S(1)}, bf16[2,1,32,128]{3,2,0,1:T(8,128)(2,1)S(1)}, u32[]{:S(2)}, u32[]{:S(2)}) collective-permute-start(bf16[2,1,32,128]{3,2,0,1:T(8,128)(2,1)S(1)} %get-tuple-element.53), channel_id=1, source_target_pairs={{0,4},{1,5},{2,6},{3,7},{4,0},{5,1},{6,2},{7,3},{8,12},{9,13},{10,... | collective-permute-start | bytes 49160 | tf_op jit(solution)/shard_map/ppermute | solution.py:32
  56.0 5.5 %collective-permute-start.8 = (bf16[2,1,32,128]{3,2,0,1:T(8,128)(2,1)S(1)}, bf16[2,1,32,128]{3,2,0,1:T(8,128)(2,1)S(1)}, u32[]{:S(2)}, u32[]{:S(2)}) collective-permute-start(bf16[2,1,32,128]{3,2,0,1:T(8,128)(2,1)S(1)} %get-tuple-element.51), channel_id=1, source_target_pairs={{0,2},{1,3},{2,4},{3,5},{4,6},{5,7},{6,0},{7,1},{8,10},{9,11},{10,... | collective-permute-start | bytes 49160 | tf_op jit(solution)/shard_map/ppermute | solution.py:32
  65.5 5.1 %collective-permute-start.15 = (bf16[16,4096]{1,0:T(8,128)(2,1)S(1)}, bf16[16,4096]{1,0:T(8,128)(2,1)S(1)}, u32[]{:S(2)}, u32[]{:S(2)}) collective-permute-start(bf16[16,4096]{1,0:T(8,128)(2,1)S(1)} %get-tuple-element.32), channel_id=1, source_target_pairs={{0,1},{1,0},{2,3},{3,2},{4,5},{5,4},{6,7},{7,6},{8,9},{9,8},{10,11... | collective-permute-start | bytes 393224 | tf_op jit(solution)/shard_map/ppermute | solution.py:32
  66.1 10.5 %collective-permute-start.17 = (bf16[16,4096]{1,0:T(8,128)(2,1)S(1)}, bf16[16,4096]{1,0:T(8,128)(2,1)S(1)}, u32[]{:S(2)}, u32[]{:S(2)}) collective-permute-start(bf16[16,4096]{1,0:T(8,128)(2,1)S(1)} %get-tuple-element.34), channel_id=1, source_target_pairs={{0,1},{1,0},{2,3},{3,2},{4,5},{5,4},{6,7},{7,6},{8,9},{9,8},{10,11... | collective-permute-start | bytes 393224 | tf_op jit(solution)/shard_map/ppermute | solution.py:32
  67.6 5.9 %collective-permute-start.13 = (bf16[16,4096]{1,0:T(8,128)(2,1)S(1)}, bf16[16,4096]{1,0:T(8,128)(2,1)S(1)}, u32[]{:S(2)}, u32[]{:S(2)}) collective-permute-start(bf16[16,4096]{1,0:T(8,128)(2,1)S(1)} %get-tuple-element.30), channel_id=1, source_target_pairs={{0,1},{1,0},{2,3},{3,2},{4,5},{5,4},{6,7},{7,6},{8,9},{9,8},{10,11... | collective-permute-start | bytes 393224 | tf_op jit(solution)/shard_map/ppermute | solution.py:32
  68.1 6.8 %collective-permute-start.11 = (bf16[16,4096]{1,0:T(8,128)(2,1)S(1)}, bf16[16,4096]{1,0:T(8,128)(2,1)S(1)}, u32[]{:S(2)}, u32[]{:S(2)}) collective-permute-start(bf16[16,4096]{1,0:T(8,128)(2,1)S(1)} %get-tuple-element.28), channel_id=1, source_target_pairs={{0,1},{1,0},{2,3},{3,2},{4,5},{5,4},{6,7},{7,6},{8,9},{9,8},{10,11... | collective-permute-start | bytes 393224 | tf_op jit(solution)/shard_map/ppermute | solution.py:32
  70.7 6.2 %collective-permute-start.16 = (bf16[16,4096]{1,0:T(8,128)(2,1)S(1)}, bf16[16,4096]{1,0:T(8,128)(2,1)S(1)}, u32[]{:S(2)}, u32[]{:S(2)}) collective-permute-start(bf16[16,4096]{1,0:T(8,128)(2,1)S(1)} %add_convert_fusion.3), channel_id=1, source_target_pairs={{0,6},{1,7},{2,0},{3,1},{4,2},{5,3},{6,4},{7,5},{8,14},{9,15},{10,... | collective-permute-start | bytes 393224 | tf_op jit(solution)/shard_map/ppermute | solution.py:32
  73.5 12.0 %collective-permute-start.14 = (bf16[16,4096]{1,0:T(8,128)(2,1)S(1)}, bf16[16,4096]{1,0:T(8,128)(2,1)S(1)}, u32[]{:S(2)}, u32[]{:S(2)}) collective-permute-start(bf16[16,4096]{1,0:T(8,128)(2,1)S(1)} %add_convert_fusion.4), channel_id=1, source_target_pairs={{0,4},{1,5},{2,6},{3,7},{4,0},{5,1},{6,2},{7,3},{8,12},{9,13},{10,... | collective-permute-start | bytes 393224 | tf_op jit(solution)/shard_map/ppermute | solution.py:32
  74.9 10.6 %collective-permute-start.12 = (bf16[16,4096]{1,0:T(8,128)(2,1)S(1)}, bf16[16,4096]{1,0:T(8,128)(2,1)S(1)}, u32[]{:S(2)}, u32[]{:S(2)}) collective-permute-start(bf16[16,4096]{1,0:T(8,128)(2,1)S(1)} %add_convert_fusion.5), channel_id=1, source_target_pairs={{0,2},{1,3},{2,4},{3,5},{4,6},{5,7},{6,0},{7,1},{8,10},{9,11},{10,... | collective-permute-start | bytes 393224 | tf_op jit(solution)/shard_map/ppermute | solution.py:32
  85.8 7.0 %collective-permute-start.19 = (bf16[16,4096]{1,0:T(8,128)(2,1)S(1)}, bf16[16,4096]{1,0:T(8,128)(2,1)S(1)}, u32[]{:S(2)}, u32[]{:S(2)}) collective-permute-start(bf16[16,4096]{1,0:T(8,128)(2,1)S(1)} %multiply_convert_fusion.refs_0_), channel_id=1, source_target_pairs={{0,2},{1,3},{2,4},{3,5},{4,6},{5,7},{6,0},{7,1},{8,10},{9,11},{10,... | collective-permute-start | bytes 393224 | tf_op jit(solution)/shard_map/ppermute | solution.py:32
  87.4 8.0 %collective-permute-start.21 = (bf16[16,4096]{1,0:T(8,128)(2,1)S(1)}, bf16[16,4096]{1,0:T(8,128)(2,1)S(1)}, u32[]{:S(2)}, u32[]{:S(2)}) collective-permute-start(bf16[16,4096]{1,0:T(8,128)(2,1)S(1)} %multiply_convert_fusion.refs_0_), channel_id=1, source_target_pairs={{0,4},{1,5},{2,6},{3,7},{4,0},{5,1},{6,2},{7,3},{8,12},{9,13},{10,... | collective-permute-start | bytes 393224 | tf_op jit(solution)/shard_map/ppermute | solution.py:32
  89.4 6.6 %collective-permute-start.23 = (bf16[16,4096]{1,0:T(8,128)(2,1)S(1)}, bf16[16,4096]{1,0:T(8,128)(2,1)S(1)}, u32[]{:S(2)}, u32[]{:S(2)}) collective-permute-start(bf16[16,4096]{1,0:T(8,128)(2,1)S(1)} %multiply_convert_fusion.refs_0_), channel_id=1, source_target_pairs={{0,6},{1,7},{2,0},{3,1},{4,2},{5,3},{6,4},{7,5},{8,14},{9,15},{10,... | collective-permute-start | bytes 393224 | tf_op jit(solution)/shard_map/ppermute | solution.py:32
  92.3 5.2 %collective-permute-start.18 = (bf16[16,4096]{1,0:T(8,128)(2,1)S(1)}, bf16[16,4096]{1,0:T(8,128)(2,1)S(1)}, u32[]{:S(2)}, u32[]{:S(2)}) collective-permute-start(bf16[16,4096]{1,0:T(8,128)(2,1)S(1)} %multiply_convert_fusion.refs_0_), channel_id=1, source_target_pairs={{0,1},{1,0},{2,3},{3,2},{4,5},{5,4},{6,7},{7,6},{8,9},{9,8},{10,11... | collective-permute-start | bytes 393224 | tf_op jit(solution)/shard_map/ppermute | solution.py:32
  92.8 5.9 %collective-permute-start.20 = (bf16[16,4096]{1,0:T(8,128)(2,1)S(1)}, bf16[16,4096]{1,0:T(8,128)(2,1)S(1)}, u32[]{:S(2)}, u32[]{:S(2)}) collective-permute-start(bf16[16,4096]{1,0:T(8,128)(2,1)S(1)} %collective-permute-done.19.refs_2_), channel_id=1, source_target_pairs={{0,1},{1,0},{2,3},{3,2},{4,5},{5,4},{6,7},{7,6},{8,9},{9,8},{10,11... | collective-permute-start | bytes 393224 | tf_op jit(solution)/shard_map/ppermute | solution.py:32
  95.5 5.0 %collective-permute-start.22 = (bf16[16,4096]{1,0:T(8,128)(2,1)S(1)}, bf16[16,4096]{1,0:T(8,128)(2,1)S(1)}, u32[]{:S(2)}, u32[]{:S(2)}) collective-permute-start(bf16[16,4096]{1,0:T(8,128)(2,1)S(1)} %collective-permute-done.21.refs_4_), channel_id=1, source_target_pairs={{0,1},{1,0},{2,3},{3,2},{4,5},{5,4},{6,7},{7,6},{8,9},{9,8},{10,11... | collective-permute-start | bytes 393224 | tf_op jit(solution)/shard_map/ppermute | solution.py:32
  96.0 6.1 %collective-permute-start.24 = (bf16[16,4096]{1,0:T(8,128)(2,1)S(1)}, bf16[16,4096]{1,0:T(8,128)(2,1)S(1)}, u32[]{:S(2)}, u32[]{:S(2)}) collective-permute-start(bf16[16,4096]{1,0:T(8,128)(2,1)S(1)} %collective-permute-done.23.refs_6_), channel_id=1, source_target_pairs={{0,1},{1,0},{2,3},{3,2},{4,5},{5,4},{6,7},{7,6},{8,9},{9,8},{10,11... | collective-permute-start | bytes 393224 | tf_op jit(solution)/shard_map/ppermute | solution.py:32
  109.1 5.0 %collective-permute-start.29 = (bf16[16,4096]{1,0:T(8,128)(2,1)S(1)}, bf16[16,4096]{1,0:T(8,128)(2,1)S(1)}, u32[]{:S(2)}, u32[]{:S(2)}) collective-permute-start(bf16[16,4096]{1,0:T(8,128)(2,1)S(1)} %get-tuple-element.40), channel_id=1, source_target_pairs={{0,1},{1,0},{2,3},{3,2},{4,5},{5,4},{6,7},{7,6},{8,9},{9,8},{10,11... | collective-permute-start | bytes 393224 | tf_op jit(solution)/shard_map/ppermute | solution.py:32
  110.0 12.6 %collective-permute-start.31 = (bf16[16,4096]{1,0:T(8,128)(2,1)S(1)}, bf16[16,4096]{1,0:T(8,128)(2,1)S(1)}, u32[]{:S(2)}, u32[]{:S(2)}) collective-permute-start(bf16[16,4096]{1,0:T(8,128)(2,1)S(1)} %get-tuple-element.42), channel_id=1, source_target_pairs={{0,1},{1,0},{2,3},{3,2},{4,5},{5,4},{6,7},{7,6},{8,9},{9,8},{10,11... | collective-permute-start | bytes 393224 | tf_op jit(solution)/shard_map/ppermute | solution.py:32
  111.2 7.9 %collective-permute-start.27 = (bf16[16,4096]{1,0:T(8,128)(2,1)S(1)}, bf16[16,4096]{1,0:T(8,128)(2,1)S(1)}, u32[]{:S(2)}, u32[]{:S(2)}) collective-permute-start(bf16[16,4096]{1,0:T(8,128)(2,1)S(1)} %get-tuple-element.38), channel_id=1, source_target_pairs={{0,1},{1,0},{2,3},{3,2},{4,5},{5,4},{6,7},{7,6},{8,9},{9,8},{10,11... | collective-permute-start | bytes 393224 | tf_op jit(solution)/shard_map/ppermute | solution.py:32
  112.0 8.8 %collective-permute-start.25 = (bf16[16,4096]{1,0:T(8,128)(2,1)S(1)}, bf16[16,4096]{1,0:T(8,128)(2,1)S(1)}, u32[]{:S(2)}, u32[]{:S(2)}) collective-permute-start(bf16[16,4096]{1,0:T(8,128)(2,1)S(1)} %get-tuple-element.36), channel_id=1, source_target_pairs={{0,1},{1,0},{2,3},{3,2},{4,5},{5,4},{6,7},{7,6},{8,9},{9,8},{10,11... | collective-permute-start | bytes 393224 | tf_op jit(solution)/shard_map/ppermute | solution.py:32
  114.2 8.4 %collective-permute-start.30 = (bf16[16,4096]{1,0:T(8,128)(2,1)S(1)}, bf16[16,4096]{1,0:T(8,128)(2,1)S(1)}, u32[]{:S(2)}, u32[]{:S(2)}) collective-permute-start(bf16[16,4096]{1,0:T(8,128)(2,1)S(1)} %add_convert_fusion), channel_id=1, source_target_pairs={{0,6},{1,7},{2,0},{3,1},{4,2},{5,3},{6,4},{7,5},{8,14},{9,15},{10,... | collective-permute-start | bytes 393224 | tf_op jit(solution)/shard_map/ppermute | solution.py:32
  119.2 7.1 %collective-permute-start.28 = (bf16[16,4096]{1,0:T(8,128)(2,1)S(1)}, bf16[16,4096]{1,0:T(8,128)(2,1)S(1)}, u32[]{:S(2)}, u32[]{:S(2)}) collective-permute-start(bf16[16,4096]{1,0:T(8,128)(2,1)S(1)} %add_convert_fusion.1), channel_id=1, source_target_pairs={{0,4},{1,5},{2,6},{3,7},{4,0},{5,1},{6,2},{7,3},{8,12},{9,13},{10,... | collective-permute-start | bytes 393224 | tf_op jit(solution)/shard_map/ppermute | solution.py:32
  120.9 6.8 %collective-permute-start.26 = (bf16[16,4096]{1,0:T(8,128)(2,1)S(1)}, bf16[16,4096]{1,0:T(8,128)(2,1)S(1)}, u32[]{:S(2)}, u32[]{:S(2)}) collective-permute-start(bf16[16,4096]{1,0:T(8,128)(2,1)S(1)} %add_convert_fusion.2), channel_id=1, source_target_pairs={{0,2},{1,3},{2,4},{3,5},{4,6},{5,7},{6,0},{7,1},{8,10},{9,11},{10,... | collective-permute-start | bytes 393224 | tf_op jit(solution)/shard_map/ppermute | solution.py:32
  (13 other events, 346.1 us)

commit v3 on v2

v3 whole, which is shorter than its diff:
```python
import functools

import jax
import jax.numpy as jnp
import numpy as np
from jax import lax
from jax.experimental import pallas as pl
from jax.experimental.pallas import tpu as pltpu
from jax.sharding import PartitionSpec as P

HEADS = 32
KV_HEADS = 8
HEAD_DIM = 128

rope_base = 500000.0
norm_eps = 1e-05

bf16, f32, i32 = jnp.bfloat16, jnp.float32, jnp.int32
VMEM = pl.BlockSpec(memory_space=pltpu.VMEM)


def plane_of(count):
    wide = max(y for y in range(1, count + 1) if count % y == 0 and 2 * y * y <= max(count, 2))
    return count // wide, wide


def shift(block, tall, wide, dz, dy, keep=None):
    pairs = [
        (z * wide + y, (z + dz) % tall * wide + (y + dy) % wide)
        for z in range(tall)
        for y in range(wide)
        if keep is None or keep(z)
    ]
    return lax.ppermute(block, "ctx", pairs)


def gather_blocks(block, tall, wide, relay=False):
    blocks = {(0, 0): block}
    for dz in range(1, tall):
        if not (relay and tall == 4 and dz == 2):
            blocks[dz, 0] = shift(block, tall, wide, dz, 0)
    if relay and tall == 4:
        up = shift(blocks[1, 0], tall, wide, 1, 0, lambda z: z in (1, 2))
        down = shift(blocks[3, 0], tall, wide, -1, 0, lambda z: z in (1, 2))
        blocks[2, 0] = up + down
    for dz in [0, 1, *range(tall - 1, 1, -1)]:
        for dy in range(1, wide):
            blocks[dz, dy] = shift(blocks[dz, 0], tall, wide, 0, dy)
    return [blocks[dz, dy] for dz in range(tall) for dy in range(wide)]


def sum_order(tall):
    order = [tall // 2, *range(1, tall // 2), *range(tall // 2 + 1, tall), 0]
    return order[: tall // 2], order[tall // 2 :]


def sum_shapes(tall, wide, share, model):
    kept = [((share, model), bf16)] * tall
    return kept + [((tall // 2 * share, model), bf16)] * (2 * (wide - 1))


def store_parts(parts, tall, wide, span, product, back):
    share = parts[0].shape[0]
    sign = -1 if back else 1

    def rows(dz, dy):
        at = sign * dz % tall * wide + sign * dy % wide
        return product[at * share : (at + 1) * share, :]

    for dz in range(tall):
        parts[dz][:, span] = rows(dz, 0)
    for dy in range(1, wide):
        for which, group in enumerate(sum_order(tall)):
            out = parts[tall + 2 * (dy - 1) + which]
            for place, dz in enumerate(group):
                out[place * share : (place + 1) * share, span] = rows(dz, dy)


def scatter_sum(parts, tall, wide):
    share = parts[0].shape[0]
    crossed = [shift(p, tall, wide, 0, i // 2 + 1) for i, p in enumerate(parts[tall:])]
    total = None
    for which, group in enumerate(sum_order(tall)):
        for place, dz in enumerate(group):
            lane = parts[dz].astype(f32)
            for dy in range(1, wide):
                other = crossed[2 * (dy - 1) + which]
                lane = lane + other[place * share : (place + 1) * share].astype(f32)
            if dz:
                lane = shift(lane.astype(bf16), tall, wide, dz, 0).astype(f32)
            total = lane if total is None else total + lane
    return total


def dot(a, b):
    return jnp.dot(a, b, preferred_element_type=f32)


def fetched(weight):
    return pltpu.with_memory_space_constraint(weight, pltpu.VMEM)


def kernel_call(body, outs, args, scratch=(), limit=14, flops=0, specs=None):
    return pl.pallas_call(
        body,
        out_shape=[jax.ShapeDtypeStruct(s, d) for s, d in outs],
        in_specs=specs or [VMEM] * len(args),
        out_specs=[VMEM] * len(outs),
        scratch_shapes=list(scratch),
        compiler_params=pltpu.CompilerParams(vmem_limit_bytes=limit << 20),
        cost_estimate=pl.CostEstimate(flops=flops, bytes_accessed=1 << 20, transcendentals=0),
    )(*args)


def load_body(count, *refs):
    sources, copies, sems = refs[1 : 1 + count], refs[1 + count : -2], refs[-1]
    moves = [
        pltpu.make_async_copy(a, b, sems.at[i]) for i, (a, b) in enumerate(zip(sources, copies))
    ]
    for move in moves:
        move.start()
    for move in moves:
        move.wait()
    refs[-2][...] = jnp.zeros_like(refs[-2])


def load(after, *arrays):
    size = sum(a.size * a.dtype.itemsize for a in arrays)
    *copies, token = pl.pallas_call(
        functools.partial(load_body, len(arrays)),
        out_shape=[pltpu.VMEM(a.shape, a.dtype) for a in arrays]
        + [jax.ShapeDtypeStruct((8, 128), f32)],
        in_specs=[pl.BlockSpec(memory_space=pl.ANY)] * (1 + len(arrays)),
        out_specs=[VMEM] * (1 + len(arrays)),
        scratch_shapes=[pltpu.SemaphoreType.DMA((len(arrays),))],
        compiler_params=pltpu.CompilerParams(vmem_limit_bytes=2 << 20),
        cost_estimate=pl.CostEstimate(flops=0, bytes_accessed=2 * size, transcendentals=0),
    )(after, *[pltpu.with_memory_space_constraint(a, pltpu.HBM) for a in arrays])
    return [fetched(c) for c in copies] + [token]


def tile_of(width, most):
    return width if width <= most else most


def iota(shape, axis):
    return lax.broadcasted_iota(i32, shape, axis).astype(f32)


def pick(onehot, values):
    return dot(onehot, values).astype(values.dtype)


def send_body(me, routed, activations, outgoing):
    capacity, tokens, total = outgoing.shape[0], activations.shape[0], routed.shape[1]
    low = (me[0] * tokens).astype(f32)
    where = routed[...].astype(f32)
    first = jnp.sum(jnp.where(where < low, 1.0, 0.0), axis=1, keepdims=True)
    here = (where >= low) & (where < low + tokens)
    slot = jnp.where(here, iota((1, total), 1) - first, -1.0)
    hit = slot == iota((capacity, total), 0)
    token = jnp.sum(jnp.where(hit, where - low + 1.0, 0.0), axis=1, keepdims=True) - 1.0
    onehot = jnp.where(token == iota((capacity, tokens), 1), 1.0, 0.0).astype(bf16)
    width = activations.shape[1]
    tile = tile_of(width, 1024)
    for start in range(0, width, tile):
        span = slice(start, start + tile)
        outgoing[:, span] = pick(onehot, activations[:, span])


def map_body(tall, wide, tokens, heads_of, me, routed, balance, notes, *outs):
    pick_rows, in_order, columns, unmix, positions = outs
    count, total = tall * wide, routed.shape[1]
    share, capacity = total // count, pick_rows.shape[1] // count
    outbound, inbound = columns.shape[0], unmix.shape[0]
    my_z, my_y = lax.div(me[0], wide), lax.rem(me[0], wide)
    where, owner = routed[...].astype(f32), balance[...].astype(f32)
    lane = iota((1, total), 1)
    slot, place = jnp.zeros((1, total), f32), jnp.zeros((1, total), f32)
    out_base, out_block = notes[:outbound, 0:1], notes[:outbound, 1:2]
    in_base, in_source = notes[:inbound, 2:3], notes[:inbound, 3:4]
    for s in range(count):
        z, y = divmod(s, wide)
        from_block = lax.rem(my_z - z + tall, tall) * wide + lax.rem(my_y - y + wide, wide)
        to_block = lax.rem(z - my_z + tall, tall) * wide + lax.rem(y - my_y + wide, wide)
        peer = lax.rem(my_z + z, tall) * wide + lax.rem(my_y + y, wide)
        before = where < s * tokens
        first = jnp.sum(jnp.where(before, 1.0, 0.0), axis=1, keepdims=True)
        inside = (where < (s + 1) * tokens) & jnp.logical_not(before)
        start = (from_block * capacity).astype(f32)
        slot += jnp.where(inside, lane - first + start, 0.0)
        place += jnp.where(owner == s, (to_block * share).astype(f32), 0.0)
        out_base += jnp.where(out_block == s, heads_of(peer).astype(f32), 0.0)
        in_base += jnp.where(in_source == s, (from_block * (outbound // count)).astype(f32), 0.0)
    mine = owner == iota((count, total), 0)
    earlier = jnp.where(iota((total, total), 0) < iota((total, total), 1), 1.0, 0.0)
    rank = dot(jnp.where(mine, 1.0, 0.0).astype(bf16), earlier.astype(bf16))
    place += jnp.sum(jnp.where(mine, rank, 0.0), axis=0, keepdims=True)
    placed = place == iota((total, total), 0)
    in_order[...] = jnp.where(placed, 1.0, 0.0).astype(bf16)
    positions[...] = jnp.sum(jnp.where(placed, where, 0.0), axis=1, keepdims=True)
    slot_at = jnp.sum(jnp.where(placed, slot, 0.0), axis=1, keepdims=True)
    pick_rows[...] = jnp.where(slot_at == iota(pick_rows.shape, 1), 1.0, 0.0).astype(bf16)
    columns[...] = jnp.where(out_base == iota(columns.shape, 1), 1.0, 0.0).astype(bf16)
    unmix[...] = jnp.where(in_base == iota(unmix.shape, 1), 1.0, 0.0).astype(bf16)


def kv_body(count, *refs):
    blocks = refs[:count]
    pick_rows, order, columns, gain, w_key, w_value = refs[count : count + 6]
    (normed, own, *sent), rows = refs[-3 - count : -1], refs[-1]
    total, width = normed.shape
    tile = tile_of(width, 512)
    square = jnp.zeros((total, 1), f32)
    for start in range(0, width, tile):
        span = slice(start, start + tile)
        part = dot(pick_rows[...], jnp.concatenate([b[:, span] for b in blocks], axis=0))
        rows[:, span] = part.astype(bf16)
        square += jnp.sum(part * part, axis=1, keepdims=True)
    own[...] = rows[: own.shape[0], :]
    factor = lax.rsqrt(square / width + norm_eps)
    for start in range(0, width, tile):
        span = slice(start, start + tile)
        part = rows[:, span].astype(f32) * factor * gain[:, span]
        normed[:, span] = part.astype(bf16)
    keys = dot(normed[...], w_key[...]).astype(bf16)
    values = dot(normed[...], w_value[...]).astype(bf16)
    both = jnp.concatenate([keys, values], axis=1)
    turned = lax.dot_general(
        columns[...], both, (((1,), (1,)), ((), ())), preferred_element_type=f32
    ).astype(bf16)
    turned = dot(turned, order[...])
    each = turned.shape[0] // len(sent)
    for index, part in enumerate(sent):
        part[...] = turned[index * each : (index + 1) * each, :].astype(bf16)


def query_body(normed, w_query, cosine, sine, query):
    raw = dot(normed[...], w_query[...])
    for head in range(query.shape[1] // HEAD_DIM):
        span = slice(head * HEAD_DIM, (head + 1) * HEAD_DIM)
        one = raw[:, span]
        turned = one * cosine[...] + pltpu.roll(one, HEAD_DIM // 2, 1) * sine[...]
        query[:, span] = turned.astype(bf16)


def attend_body(plane, kv_local, *refs):
    count = plane[0] * plane[1]
    arrived, rest = refs[:count], refs[count:]
    query, unmix, cosine, sine, key_pos, query_pos, w_output = rest[:7]
    parts, heads_out = rest[7:-1], rest[-1]
    half = HEAD_DIM // 2
    heads = query.shape[1] // HEAD_DIM
    mixed = jnp.concatenate([a[...].astype(f32) for a in arrived], axis=0).astype(bf16)
    both = dot(unmix[...], mixed)
    allowed = key_pos[...].astype(f32) <= query_pos[...]
    for group in range(kv_local):
        base = group * HEAD_DIM
        first, second = both[base : base + half], both[base + half : base + HEAD_DIM]
        keys = jnp.concatenate(
            [first * cosine[...] - second * sine[...], second * cosine[...] + first * sine[...]],
            axis=0,
        ).astype(bf16)
        base += kv_local * HEAD_DIM
        values = both[base : base + HEAD_DIM].astype(bf16)
        for head in range(group * heads // kv_local, (group + 1) * heads // kv_local):
            span = slice(head * HEAD_DIM, (head + 1) * HEAD_DIM)
            scores = dot(query[:, span], keys) * HEAD_DIM ** (-0.5)
            scores = jnp.where(allowed, scores, -1e30)
            weights = jnp.exp(scores - jnp.max(scores, axis=1, keepdims=True))
            probs = (weights / jnp.sum(weights, axis=1, keepdims=True)).astype(bf16)
            heads_out[:, span] = lax.dot_general(
                probs, values, (((1,), (1,)), ((), ())), preferred_element_type=f32
            ).astype(bf16)
    spread(heads_out, w_output, parts, plane, False)


def spread(left, weight, parts, plane, back):
    width = weight.shape[1]
    tile = tile_of(width, 512)
    for start in range(0, width, tile):
        span = slice(start, start + tile)
        product = dot(left[...], weight[:, span]).astype(bf16)
        store_parts(parts, *plane, span, product, back)


def mlp_body(plane, *refs):
    count = plane[0] * plane[1]
    blocks, (w_gate, w_up, w_down) = refs[:count], refs[count : count + 3]
    parts, (piece, inner) = refs[count + 3 : -2], refs[-2:]
    share = blocks[0].shape[0]
    for index, block in enumerate(blocks):
        piece[index * share : (index + 1) * share, :] = block[...]
    width = w_gate.shape[1]
    tile = tile_of(width, 256)
    for start in range(0, width, tile):
        span = slice(start, start + tile)
        gate = dot(piece[...], w_gate[:, span])
        upward = dot(piece[...], w_up[:, span])
        inner[:, span] = (gate / (1.0 + jnp.exp(-gate)) * upward).astype(bf16)
    spread(inner, w_down, parts, plane, True)


def on_device(
    activations,
    routed,
    balance,
    w_query,
    w_key,
    w_value,
    w_output,
    attn_gain,
    mlp_gain,
    w_gate,
    w_up,
    w_down,
    w_router,
):
    count = lax.axis_size("ctx")
    plane = tall, wide = plane_of(count)
    me = lax.axis_index("ctx").astype(i32).reshape(1)
    tokens, model = activations.shape
    total = routed.shape[0]
    share = total // count
    capacity = 2 * share
    local_heads = w_query.shape[1] // HEAD_DIM
    group_size = HEADS // KV_HEADS
    kv_local = max(1, local_heads // group_size)
    key_cols = w_key.shape[1]
    depth = key_cols // KV_HEADS
    scalar = pl.BlockSpec(memory_space=pltpu.SMEM)
    routed, balance = routed.reshape(1, total), balance.reshape(1, total)

    (outgoing,) = kernel_call(
        send_body,
        [((capacity, model), bf16)],
        [me, routed, activations],
        specs=[scalar, VMEM, VMEM],
        flops=2 * capacity * tokens * model,
    )
    blocks = gather_blocks(outgoing, tall, wide, relay=True)
    attn_gain, w_key, w_value, w_query, _ = load(
        outgoing, attn_gain.reshape(1, model), w_key, w_value, w_query
    )
    near = blocks[wide]
    w_output, *tokens_1 = load(near, w_output)
    w_gate, *tokens_2 = load(near, w_gate)
    w_up, *tokens_3 = load(near, w_up)
    w_down, *tokens_4 = load(near, w_down)
    loaded = tokens_1 + tokens_2 + tokens_3 + tokens_4

    each = kv_local * 2 * depth
    notes = np.zeros((max(count * each, 2 * kv_local * HEAD_DIM), 4), np.float32)
    block, local, side, entry = np.indices((count, kv_local, 2, depth)).reshape(4, -1)
    notes[: count * each, 0] = side * key_cols + entry * KV_HEADS + local
    notes[: count * each, 1] = block
    side, local, source, entry = np.indices((2, kv_local, count, depth)).reshape(4, -1)
    notes[: 2 * kv_local * HEAD_DIM, 2] = (local * 2 + side) * depth + entry
    notes[: 2 * kv_local * HEAD_DIM, 3] = source
    pick_rows, in_order, columns, unmix, positions = kernel_call(
        functools.partial(
            map_body, tall, wide, tokens, lambda peer: lax.div(peer * local_heads, group_size)
        ),
        [
            ((total, count * capacity), bf16),
            ((total, total), bf16),
            ((count * each, 2 * key_cols), bf16),
            ((2 * kv_local * HEAD_DIM, count * each), bf16),
            ((total, 1), f32),
        ],
        [me, routed, balance, notes],
        specs=[scalar, VMEM, VMEM, VMEM],
    )

    half = HEAD_DIM // 2
    steps_f = jnp.arange(half, dtype=f32)
    freqs = jnp.exp(-jnp.log(f32(rope_base)) * (2.0 * steps_f / HEAD_DIM))
    q_angles = positions * freqs[None, :]
    q_cos, q_sin = jnp.cos(q_angles), jnp.sin(q_angles)
    q_cos = jnp.concatenate([q_cos, q_cos], axis=1)
    q_sin = jnp.concatenate([-q_sin, q_sin], axis=1)
    k_angles = freqs[:, None] * routed.astype(f32)
    k_cos, k_sin = jnp.cos(k_angles), jnp.sin(k_angles)

    normed, own, *sent = kernel_call(
        functools.partial(kv_body, count),
        [((total, model), bf16), ((share, model), bf16)] + [((each, total), bf16)] * count,
        [*blocks, pick_rows, in_order, columns, attn_gain, w_key, w_value, *loaded],
        [pltpu.VMEM((total, model), bf16)],
        flops=2 * total * model * 512,
    )
    arrived = [
        part if r == 0 else shift(part, tall, wide, *divmod(r, wide)) for r, part in enumerate(sent)
    ]
    (query,) = kernel_call(
        query_body,
        [((total, local_heads * HEAD_DIM), bf16)],
        [normed, w_query, q_cos, q_sin],
        flops=2 * total * model * local_heads * HEAD_DIM,
    )
    part_shapes = sum_shapes(tall, wide, share, model)
    attn_parts = kernel_call(
        functools.partial(attend_body, plane, kv_local),
        part_shapes,
        [*arrived, query, unmix, k_cos, k_sin, routed, positions, w_output],
        [pltpu.VMEM((total, local_heads * HEAD_DIM), bf16)],
        flops=2 * total * model * local_heads * HEAD_DIM,
    )
    attn_own = scatter_sum(attn_parts, tall, wide)
    own_rows = own.astype(f32)
    hidden = own_rows + attn_own
    mean_sq = jnp.mean(hidden * hidden, axis=-1, keepdims=True)
    mnorm = (hidden * lax.rsqrt(mean_sq + norm_eps) * mlp_gain).astype(bf16)
    pieces = gather_blocks(mnorm, tall, wide)
    hidden_units = w_gate.shape[1]
    mlp_parts = kernel_call(
        functools.partial(mlp_body, plane),
        part_shapes,
        [*pieces, w_gate, w_up, w_down],
        [pltpu.VMEM((total, model), bf16), pltpu.VMEM((total, hidden_units), bf16)],
        flops=6 * total * model * hidden_units,
    )
    mlp_own = scatter_sum(mlp_parts, tall, wide)
    router_score = jnp.sum(own_rows * w_router[None, :], axis=1, keepdims=True)
    return (own_rows + router_score * (attn_own + mlp_own)).astype(bf16)


def solution(mesh):
    in_specs = (
        P(("dp", "ctx"), None),
        P("dp"),
        P("dp"),
        P(None, "ctx"),
        P(None, "ctx"),
        P(None, "ctx"),
        P("ctx", None),
        P(),
        P(),
        P(None, "ctx"),
        P(None, "ctx"),
        P("ctx", None),
        P(),
    )
    out_specs = P(("dp", "ctx"), None)
    return jax.shard_map(
        on_device, mesh=mesh, in_specs=in_specs, out_specs=out_specs, check_vma=False
    )
```

time: 129 us -> 128 us (level)
  Pallas kernels: 7.61 us -> 25.1 us
  starting transfers between devices: 50.2 us -> 42.1 us
  local copies, waits for them, and re-layouts: 11.1 us -> 3.45 us
  other arithmetic: 7.64 us -> 2.12 us
  waiting for transfers between devices: 50.8 us -> 55.1 us
    pallas_call x0 -> x5, Pallas kernels: none -> 15.9 us  [load(): pl.pallas_call(functools.partial(load_body, len(arrays)), out_shape=[pltp...]
    ppermute x32, starting transfers between devices: 50.2 us -> 42.1 us  [shift(): return lax.ppermute(block, 'ctx', pairs)]
    unnamed x26 -> x14, local copies, waits for them, and re-layouts: 10.9 us -> 3.45 us
    ppermute x32, waiting for transfers between devices: 50.8 us -> 55.1 us  [shift(): return lax.ppermute(block, 'ctx', pairs)]
    reduce_sum x4 -> x0, other arithmetic: 1.94 us -> none  [the longest x1 0.9 us: on_device(): rank = jnp.sum(same.astype(i32), axis=1)]
    pallas_call x4 -> x6, Pallas kernels: 7.61 us -> 9.24 us  [kernel_call(): pl.pallas_call(body, out_shape=[jax.ShapeDtypeStruct(s, d) for s, d in ou...]
    convert_element_type x5 -> x1, other arithmetic: 1.61 us -> 0.01 us  [on_device(): k_angles = freqs[:, None] * routed.astype(f32)]
    add x4 -> x1, other arithmetic: 1.37 us -> 0.06 us  [gather_blocks(): blocks[2, 0] = up + down]
  transfers between devices with their start and end apart: 32 -> 32, of which waited for: 19 -> 17; matrix products, arithmetic and copies ran while one was open for 3% -> 1% of each run, Pallas kernels for 1% -> 14%
where the time goes in v3:
time: 128 us
  waiting for transfers between devices  55.1 us (43%)
  starting transfers between devices  42.1 us (33%)
  Pallas kernels  25.1 us (20%)
  local copies, waits for them, and re-layouts  3.45 us (3%)
  other arithmetic  2.12 us (2%)
    ppermute x32, waiting for transfers between devices, shift(): return lax.ppermute(block, 'ctx', pairs)  55.1 us
    ppermute x32, starting transfers between devices, shift(): return lax.ppermute(block, 'ctx', pairs)  42.1 us
    pallas_call x5, Pallas kernels, load(): pl.pallas_call(functools.partial(load_body, len(arrays)), out_shape=[pltp...  15.9 us
    pallas_call x6, Pallas kernels, kernel_call(): pl.pallas_call(body, out_shape=[jax.ShapeDtypeStruct(s, d) for s, d in ou...  9.24 us
    unnamed x14, local copies, waits for them, and re-layouts  3.45 us
  transfers between devices with their start and end apart: 32, of which 17 were waited for; matrix products, arithmetic and copies ran while one was open for 1% of the time, Pallas kernels for 14%

profile of v3, /device:TPU:0, one launch (start us, length us, event | category | flops | bytes accessed | tf_op | source)
XLA Modules:
  0.0 128.1 jit_solution(986822250597121835)
XLA Ops:
  2.3 3.1 %collective-permute-start.1 = (bf16[32,4096]{1,0:T(8,128)(2,1)S(1)}, bf16[32,4096]{1,0:T(8,128)(2,1)S(1)}, u32[]{:S(2)}, u32[]{:S(2)}) collective-permute-start(bf16[32,4096]{1,0:T(8,128)(2,1)S(1)} %shard_map.136.refs_0_), channel_id=1, source_target_pairs={{0,2},{1,3},{2,4},{3,5},{4,6},{5,7},{6,0},{7,1},{8,10},{9,11},{10,... | collective-permute-start | bytes 786440 | tf_op jit(solution)/shard_map/ppermute | solution.py:34
  5.4 2.1 %collective-permute-start.4 = (bf16[32,4096]{1,0:T(8,128)(2,1)S(1)}, bf16[32,4096]{1,0:T(8,128)(2,1)S(1)}, u32[]{:S(2)}, u32[]{:S(2)}) collective-permute-start(bf16[32,4096]{1,0:T(8,128)(2,1)S(1)} %shard_map.136.refs_0_), channel_id=1, source_target_pairs={{0,6},{1,7},{2,0},{3,1},{4,2},{5,3},{6,4},{7,5},{8,14},{9,15},{10,... | collective-permute-start | bytes 786440 | tf_op jit(solution)/shard_map/ppermute | solution.py:34
  7.5 7.1 %collective-permute-done.1.refs_0_.refs_2_ = bf16[32,4096]{1,0:T(8,128)(2,1)S(1)} collective-permute-done((bf16[32,4096]{1,0:T(8,128)(2,1)S(1)}, bf16[32,4096]{1,0:T(8,128)(2,1)S(1)}, u32[]{:S(2)}, u32[]{:S(2)}) %collective-permute-start.1) | collective-permute-done | bytes 262176 | tf_op jit(solution)/shard_map/ppermute | solution.py:34
  15.2 3.5 %collective-permute-done.4.refs_6_ = bf16[32,4096]{1,0:T(8,128)(2,1)S(1)} collective-permute-done((bf16[32,4096]{1,0:T(8,128)(2,1)S(1)}, bf16[32,4096]{1,0:T(8,128)(2,1)S(1)}, u32[]{:S(2)}, u32[]{:S(2)}) %collective-permute-start.4) | collective-permute-done | bytes 262176 | tf_op jit(solution)/shard_map/ppermute | solution.py:34
  23.7 5.1 %collective-permute-done.5 = bf16[32,4096]{1,0:T(8,128)(2,1)S(1)} collective-permute-done((bf16[32,4096]{1,0:T(8,128)(2,1)S(1)}, bf16[32,4096]{1,0:T(8,128)(2,1)S(1)}, u32[]{:S(2)}, u32[]{:S(2)}) %collective-permute-start.5) | collective-permute-done | bytes 262176 | tf_op jit(solution)/shard_map/ppermute | solution.py:34
  33.2 3.5 %shard_map.138 = (f32[1,4096]{1,0:T(1,128)S(1)}, bf16[4096,128]{1,0:T(8,128)(2,1)S(1)}, bf16[4096,128]{1,0:T(8,128)(2,1)S(1)}, bf16[4096,512]{1,0:T(8,128)(2,1)S(1)}, f32[8,128]{1,0:T(8,128)}) custom-call(bf16[32,4096]{1,0:T(8,128)(2,1)S(1)} %shard_map.136.refs_0_, f32[1,4096]{1,0:T(1,128)} %bitcast.8, bf16[4096,128]{1,0:T(8,128)(2,1)} %refs_2_.1, ...), custom_call_target="tpu_custom_call" | custom-call | bytes 12615680 | tf_op jit(solution)/shard_map/pallas_call | solution.py:129
  37.0 3.4 %shard_map.140 = (bf16[4096,1024]{1,0:T(8,128)(2,1)S(1)}, f32[8,128]{1,0:T(8,128)S(1)}) custom-call(bf16[32,4096]{1,0:T(8,128)(2,1)S(1)} %collective-permute-done.1.refs_0_.refs_2_, bf16[4096,1024]{1,0:T(8,128)(2,1)} %refs_1_.5), custom_call_target="tpu_custom_call" | custom-call | bytes 16777216 | tf_op jit(solution)/shard_map/pallas_call | solution.py:129
  40.4 3.4 %shard_map.141 = (bf16[4096,1024]{1,0:T(8,128)(2,1)S(1)}, f32[8,128]{1,0:T(8,128)S(1)}) custom-call(bf16[32,4096]{1,0:T(8,128)(2,1)S(1)} %collective-permute-done.1.refs_0_.refs_2_, bf16[4096,1024]{1,0:T(8,128)(2,1)} %refs_1_.6), custom_call_target="tpu_custom_call" | custom-call | bytes 16777216 | tf_op jit(solution)/shard_map/pallas_call | solution.py:129
  43.8 3.4 %shard_map.142 = (bf16[1024,4096]{1,0:T(8,128)(2,1)S(1)}, f32[8,128]{1,0:T(8,128)S(1)}) custom-call(bf16[32,4096]{1,0:T(8,128)(2,1)S(1)} %collective-permute-done.1.refs_0_.refs_2_, bf16[1024,4096]{1,0:T(8,128)(2,1)} %refs_1_.7), custom_call_target="tpu_custom_call" | custom-call | bytes 16777216 | tf_op jit(solution)/shard_map/pallas_call | solution.py:129
  47.2 2.2 %shard_map.139 = (bf16[512,4096]{1,0:T(8,128)(2,1)S(1)}, f32[8,128]{1,0:T(8,128)S(1)}) custom-call(bf16[32,4096]{1,0:T(8,128)(2,1)S(1)} %collective-permute-done.1.refs_0_.refs_2_, bf16[512,4096]{1,0:T(8,128)(2,1)} %refs_1_.4), custom_call_target="tpu_custom_call" | custom-call | bytes 8388608 | tf_op jit(solution)/shard_map/pallas_call | solution.py:129
  49.5 1.8 %shard_map.143 = (bf16[128,4096]{1,0:T(8,128)(2,1)S(1)}, bf16[16,4096]{1,0:T(8,128)(2,1)S(1)}, bf16[32,128]{1,0:T(8,128)(2,1)S(1)}, bf16[32,128]{1,0:T(8,128)(2,...) custom-call(bf16[32,4096]{1,0:T(8,128)(2,1)S(1)} %shard_map.136.refs, ...), custom_call_target="tpu_custom_call" | custom-call | flops 536870912 | bytes 1048576 | tf_op jit(solution)/shard_map/pallas_call | solution.py:104
  51.3 2.0 %collective-permute-start.10 = (bf16[32,128]{1,0:T(8,128)(2,1)S(1)}, bf16[32,128]{1,0:T(8,128)(2,1)S(1)}, u32[]{:S(2)}, u32[]{:S(2)}) collective-permute-start(bf16[32,128]{1,0:T(8,128)(2,1)S(1)} %get-tuple-element.58), channel_id=1, source_target_pairs={{0,3},{1,2},{2,5},{3,4},{4,7},{5,6},{6,1},{7,0},{8,11},{9,10},{10,... | collective-permute-start | bytes 24584 | tf_op jit(solution)/shard_map/ppermute | solution.py:34
  53.4 4.0 %collective-permute-start.12 = (bf16[32,128]{1,0:T(8,128)(2,1)S(1)}, bf16[32,128]{1,0:T(8,128)(2,1)S(1)}, u32[]{:S(2)}, u32[]{:S(2)}) collective-permute-start(bf16[32,128]{1,0:T(8,128)(2,1)S(1)} %get-tuple-element.60), channel_id=1, source_target_pairs={{0,5},{1,4},{2,7},{3,6},{4,1},{5,0},{6,3},{7,2},{8,13},{9,12},{10,... | collective-permute-start | bytes 24584 | tf_op jit(solution)/shard_map/ppermute | solution.py:34
  57.3 1.8 %collective-permute-start.13 = (bf16[32,128]{1,0:T(8,128)(2,1)S(1)}, bf16[32,128]{1,0:T(8,128)(2,1)S(1)}, u32[]{:S(2)}, u32[]{:S(2)}) collective-permute-start(bf16[32,128]{1,0:T(8,128)(2,1)S(1)} %get-tuple-element.61), channel_id=1, source_target_pairs={{0,6},{1,7},{2,0},{3,1},{4,2},{5,3},{6,4},{7,5},{8,14},{9,15},{10,... | collective-permute-start | bytes 24584 | tf_op jit(solution)/shard_map/ppermute | solution.py:34
  60.6 2.0 %collective-permute-start.9 = (bf16[32,128]{1,0:T(8,128)(2,1)S(1)}, bf16[32,128]{1,0:T(8,128)(2,1)S(1)}, u32[]{:S(2)}, u32[]{:S(2)}) collective-permute-start(bf16[32,128]{1,0:T(8,128)(2,1)S(1)} %get-tuple-element.57), channel_id=1, source_target_pairs={{0,2},{1,3},{2,4},{3,5},{4,6},{5,7},{6,0},{7,1},{8,10},{9,11},{10,... | collective-permute-start | bytes 24584 | tf_op jit(solution)/shard_map/ppermute | solution.py:34
  63.7 2.4 %collective-permute-done.9.refs_2_ = bf16[32,128]{1,0:T(8,128)(2,1)S(1)} collective-permute-done((bf16[32,128]{1,0:T(8,128)(2,1)S(1)}, bf16[32,128]{1,0:T(8,128)(2,1)S(1)}, u32[]{:S(2)}, u32[]{:S(2)}) %collective-permute-start.9) | collective-permute-done | bytes 8224 | tf_op jit(solution)/shard_map/ppermute | solution.py:34
  66.1 1.7 %shard_map.145 = (bf16[16,4096]{1,0:T(8,128)(2,1)S(1)}, bf16[16,4096]{1,0:T(8,128)(2,1)S(1)}, bf16[16,4096]{1,0:T(8,128)(2,1)S(1)}, bf16[16,4096]{1,0:T(8,128)(2...) custom-call(bf16[32,128]{1,0:T(8,128)(2,1)S(1)} %get-tuple-element.55.refs_0_, ...), custom_call_target="tpu_custom_call" | custom-call | flops 536870912 | bytes 1048576 | tf_op jit(solution)/shard_map/pallas_call | solution.py:104
  69.9 4.3 %collective-permute-done.15 = bf16[32,4096]{1,0:T(8,128)(2,1)S(1)} collective-permute-done((bf16[32,4096]{1,0:T(8,128)(2,1)S(1)}, bf16[32,4096]{1,0:T(8,128)(2,1)S(1)}, u32[]{:S(2)}, u32[]{:S(2)}) %collective-permute-start.15) | collective-permute-done | bytes 262176 | tf_op jit(solution)/shard_map/ppermute | solution.py:34
  74.7 2.4 %collective-permute-done.18 = bf16[32,4096]{1,0:T(8,128)(2,1)S(1)} collective-permute-done((bf16[32,4096]{1,0:T(8,128)(2,1)S(1)}, bf16[32,4096]{1,0:T(8,128)(2,1)S(1)}, u32[]{:S(2)}, u32[]{:S(2)}) %collective-permute-start.18) | collective-permute-done | bytes 262176 | tf_op jit(solution)/shard_map/ppermute | solution.py:34
  78.4 8.6 %collective-permute-done.16 = bf16[16,4096]{1,0:T(8,128)(2,1)S(1)} collective-permute-done((bf16[16,4096]{1,0:T(8,128)(2,1)S(1)}, bf16[16,4096]{1,0:T(8,128)(2,1)S(1)}, u32[]{:S(2)}, u32[]{:S(2)}) %collective-permute-start.16) | collective-permute-done | bytes 131104 | tf_op jit(solution)/shard_map/ppermute | solution.py:34
  88.7 2.0 %collective-permute-start.21 = (bf16[16,4096]{1,0:T(8,128)(2,1)S(1)}, bf16[16,4096]{1,0:T(8,128)(2,1)S(1)}, u32[]{:S(2)}, u32[]{:S(2)}) collective-permute-start(bf16[16,4096]{1,0:T(8,128)(2,1)S(1)} %multiply_convert_fusion.refs_0_), channel_id=1, source_target_pairs={{0,2},{1,3},{2,4},{3,5},{4,6},{5,7},{6,0},{7,1},{8,10},{9,11},{10,... | collective-permute-start | bytes 393224 | tf_op jit(solution)/shard_map/ppermute | solution.py:34
  90.7 2.4 %collective-permute-start.25 = (bf16[16,4096]{1,0:T(8,128)(2,1)S(1)}, bf16[16,4096]{1,0:T(8,128)(2,1)S(1)}, u32[]{:S(2)}, u32[]{:S(2)}) collective-permute-start(bf16[16,4096]{1,0:T(8,128)(2,1)S(1)} %multiply_convert_fusion.refs_0_), channel_id=1, source_target_pairs={{0,6},{1,7},{2,0},{3,1},{4,2},{5,3},{6,4},{7,5},{8,14},{9,15},{10,... | collective-permute-start | bytes 393224 | tf_op jit(solution)/shard_map/ppermute | solution.py:34
  93.6 2.0 %collective-permute-done.21.refs_2_ = bf16[16,4096]{1,0:T(8,128)(2,1)S(1)} collective-permute-done((bf16[16,4096]{1,0:T(8,128)(2,1)S(1)}, bf16[16,4096]{1,0:T(8,128)(2,1)S(1)}, u32[]{:S(2)}, u32[]{:S(2)}) %collective-permute-start.21) | collective-permute-done | bytes 131104 | tf_op jit(solution)/shard_map/ppermute | solution.py:34
  96.1 2.2 %collective-permute-done.23.refs_4_ = bf16[16,4096]{1,0:T(8,128)(2,1)S(1)} collective-permute-done((bf16[16,4096]{1,0:T(8,128)(2,1)S(1)}, bf16[16,4096]{1,0:T(8,128)(2,1)S(1)}, u32[]{:S(2)}, u32[]{:S(2)}) %collective-permute-start.23) | collective-permute-done | bytes 131104 | tf_op jit(solution)/shard_map/ppermute | solution.py:34
  100.3 1.6 %collective-permute-done.22.refs_3_ = bf16[16,4096]{1,0:T(8,128)(2,1)S(1)} collective-permute-done((bf16[16,4096]{1,0:T(8,128)(2,1)S(1)}, bf16[16,4096]{1,0:T(8,128)(2,1)S(1)}, u32[]{:S(2)}, u32[]{:S(2)}) %collective-permute-start.22) | collective-permute-done | bytes 131104 | tf_op jit(solution)/shard_map/ppermute | solution.py:34
  101.9 2.8 %collective-permute-done.24.refs_5_ = bf16[16,4096]{1,0:T(8,128)(2,1)S(1)} collective-permute-done((bf16[16,4096]{1,0:T(8,128)(2,1)S(1)}, bf16[16,4096]{1,0:T(8,128)(2,1)S(1)}, u32[]{:S(2)}, u32[]{:S(2)}) %collective-permute-start.24) | collective-permute-done | bytes 131104 | tf_op jit(solution)/shard_map/ppermute | solution.py:34
  104.7 2.8 %collective-permute-done.26.refs_7_ = bf16[16,4096]{1,0:T(8,128)(2,1)S(1)} collective-permute-done((bf16[16,4096]{1,0:T(8,128)(2,1)S(1)}, bf16[16,4096]{1,0:T(8,128)(2,1)S(1)}, u32[]{:S(2)}, u32[]{:S(2)}) %collective-permute-start.26) | collective-permute-done | bytes 131104 | tf_op jit(solution)/shard_map/ppermute | solution.py:34
  107.6 3.7 %shard_map.146 = (bf16[16,4096]{1,0:T(8,128)(2,1)S(1)}, bf16[16,4096]{1,0:T(8,128)(2,1)S(1)}, bf16[16,4096]{1,0:T(8,128)(2,1)S(1)}, bf16[16,4096]{1,0:T(8,128)(2...) custom-call(bf16[16,4096]{1,0:T(8,128)(2,1)S(1)} %multiply_convert_fusion.refs_0_, ...), custom_call_target="tpu_custom_call" | custom-call | flops 3221225472 | bytes 1048576 | tf_op jit(solution)/shard_map/pallas_call | solution.py:104
  113.3 4.3 %collective-permute-done.27 = bf16[32,4096]{1,0:T(8,128)(2,1)S(1)} collective-permute-done((bf16[32,4096]{1,0:T(8,128)(2,1)S(1)}, bf16[32,4096]{1,0:T(8,128)(2,1)S(1)}, u32[]{:S(2)}, u32[]{:S(2)}) %collective-permute-start.27) | collective-permute-done | bytes 262176 | tf_op jit(solution)/shard_map/ppermute | solution.py:34
  118.0 2.7 %collective-permute-start.29 = (bf16[16,4096]{1,0:T(8,128)(2,1)S(1)}, bf16[16,4096]{1,0:T(8,128)(2,1)S(1)}, u32[]{:S(2)}, u32[]{:S(2)}) collective-permute-start(bf16[16,4096]{1,0:T(8,128)(2,1)S(1)} %get-tuple-element.87), channel_id=1, source_target_pairs={{0,2},{1,3},{2,4},{3,5},{4,6},{5,7},{6,0},{7,1},{8,10},{9,11},{10,... | collective-permute-start | bytes 393224 | tf_op jit(solution)/shard_map/ppermute | solution.py:34
  120.7 2.2 %collective-permute-start.31 = (bf16[16,4096]{1,0:T(8,128)(2,1)S(1)}, bf16[16,4096]{1,0:T(8,128)(2,1)S(1)}, u32[]{:S(2)}, u32[]{:S(2)}) collective-permute-start(bf16[16,4096]{1,0:T(8,128)(2,1)S(1)} %add_convert_fusion), channel_id=1, source_target_pairs={{0,6},{1,7},{2,0},{3,1},{4,2},{5,3},{6,4},{7,5},{8,14},{9,15},{10,... | collective-permute-start | bytes 393224 | tf_op jit(solution)/shard_map/ppermute | solution.py:34
  122.9 3.2 %collective-permute-done.28 = bf16[16,4096]{1,0:T(8,128)(2,1)S(1)} collective-permute-done((bf16[16,4096]{1,0:T(8,128)(2,1)S(1)}, bf16[16,4096]{1,0:T(8,128)(2,1)S(1)}, u32[]{:S(2)}, u32[]{:S(2)}) %collective-permute-start.28) | collective-permute-done | bytes 131104 | tf_op jit(solution)/shard_map/ppermute | solution.py:34
  (72 shorter events, 28.3 us)
Async XLA Ops:
  2.3 12.3 %collective-permute-start.1 = (bf16[32,4096]{1,0:T(8,128)(2,1)S(1)}, bf16[32,4096]{1,0:T(8,128)(2,1)S(1)}, u32[]{:S(2)}, u32[]{:S(2)}) collective-permute-start(bf16[32,4096]{1,0:T(8,128)(2,1)S(1)} %shard_map.136.refs_0_), channel_id=1, source_target_pairs={{0,2},{1,3},{2,4},{3,5},{4,6},{5,7},{6,0},{7,1},{8,10},{9,11},{10,... | collective-permute-start | bytes 786440 | tf_op jit(solution)/shard_map/ppermute | solution.py:34
  5.4 13.4 %collective-permute-start.4 = (bf16[32,4096]{1,0:T(8,128)(2,1)S(1)}, bf16[32,4096]{1,0:T(8,128)(2,1)S(1)}, u32[]{:S(2)}, u32[]{:S(2)}) collective-permute-start(bf16[32,4096]{1,0:T(8,128)(2,1)S(1)} %shard_map.136.refs_0_), channel_id=1, source_target_pairs={{0,6},{1,7},{2,0},{3,1},{4,2},{5,3},{6,4},{7,5},{8,14},{9,15},{10,... | collective-permute-start | bytes 786440 | tf_op jit(solution)/shard_map/ppermute | solution.py:34
  14.6 9.2 %collective-permute-start.3 = (bf16[32,4096]{1,0:T(8,128)(2,1)S(1)}, bf16[32,4096]{1,0:T(8,128)(2,1)S(1)}, u32[]{:S(2)}, u32[]{:S(2)}) collective-permute-start(bf16[32,4096]{1,0:T(8,128)(2,1)S(1)} %collective-permute-done.1.refs_0_.refs_2_), channel_id=1, source_target_pairs={{2,4},{3,5},{4,6},{5,7},{10,12},{11,13},{12,14},{13,15},{18,20},{1... | collective-permute-start | bytes 786440 | tf_op jit(solution)/shard_map/ppermute | solution.py:34
  18.8 10.0 %collective-permute-start.5 = (bf16[32,4096]{1,0:T(8,128)(2,1)S(1)}, bf16[32,4096]{1,0:T(8,128)(2,1)S(1)}, u32[]{:S(2)}, u32[]{:S(2)}) collective-permute-start(bf16[32,4096]{1,0:T(8,128)(2,1)S(1)} %collective-permute-done.4.refs_6_), channel_id=1, source_target_pairs={{2,0},{3,1},{4,2},{5,3},{10,8},{11,9},{12,10},{13,11},{18,16},{19,... | collective-permute-start | bytes 786440 | tf_op jit(solution)/shard_map/ppermute | solution.py:34
  20.0 29.4 %collective-permute-start = (bf16[32,4096]{1,0:T(8,128)(2,1)S(1)}, bf16[32,4096]{1,0:T(8,128)(2,1)S(1)}, u32[]{:S(2)}, u32[]{:S(2)}) collective-permute-start(bf16[32,4096]{1,0:T(8,128)(2,1)S(1)} %shard_map.136.refs_0_), channel_id=1, source_target_pairs={{0,1},{1,0},{2,3},{3,2},{4,5},{5,4},{6,7},{7,6},{8,9},{9,8},{10,11... | collective-permute-start | bytes 786440 | tf_op jit(solution)/shard_map/ppermute | solution.py:34
  21.6 27.8 %collective-permute-start.2 = (bf16[32,4096]{1,0:T(8,128)(2,1)S(1)}, bf16[32,4096]{1,0:T(8,128)(2,1)S(1)}, u32[]{:S(2)}, u32[]{:S(2)}) collective-permute-start(bf16[32,4096]{1,0:T(8,128)(2,1)S(1)} %collective-permute-done.1.refs_0_.refs_2_), channel_id=1, source_target_pairs={{0,1},{1,0},{2,3},{3,2},{4,5},{5,4},{6,7},{7,6},{8,9},{9,8},{10,11... | collective-permute-start | bytes 786440 | tf_op jit(solution)/shard_map/ppermute | solution.py:34
  22.2 27.2 %collective-permute-start.7 = (bf16[32,4096]{1,0:T(8,128)(2,1)S(1)}, bf16[32,4096]{1,0:T(8,128)(2,1)S(1)}, u32[]{:S(2)}, u32[]{:S(2)}) collective-permute-start(bf16[32,4096]{1,0:T(8,128)(2,1)S(1)} %collective-permute-done.4.refs_6_), channel_id=1, source_target_pairs={{0,1},{1,0},{2,3},{3,2},{4,5},{5,4},{6,7},{7,6},{8,9},{9,8},{10,11... | collective-permute-start | bytes 786440 | tf_op jit(solution)/shard_map/ppermute | solution.py:34
  28.9 20.6 %collective-permute-start.6 = (bf16[32,4096]{1,0:T(8,128)(2,1)S(1)}, bf16[32,4096]{1,0:T(8,128)(2,1)S(1)}, u32[]{:S(2)}, u32[]{:S(2)}) collective-permute-start(bf16[32,4096]{1,0:T(8,128)(2,1)S(1)} %add.62.refs_4_), channel_id=1, source_target_pairs={{0,1},{1,0},{2,3},{3,2},{4,5},{5,4},{6,7},{7,6},{8,9},{9,8},{10,11... | collective-permute-start | bytes 786440 | tf_op jit(solution)/shard_map/ppermute | solution.py:34
  51.3 7.9 %collective-permute-start.10 = (bf16[32,128]{1,0:T(8,128)(2,1)S(1)}, bf16[32,128]{1,0:T(8,128)(2,1)S(1)}, u32[]{:S(2)}, u32[]{:S(2)}) collective-permute-start(bf16[32,128]{1,0:T(8,128)(2,1)S(1)} %get-tuple-element.58), channel_id=1, source_target_pairs={{0,3},{1,2},{2,5},{3,4},{4,7},{5,6},{6,1},{7,0},{8,11},{9,10},{10,... | collective-permute-start | bytes 24584 | tf_op jit(solution)/shard_map/ppermute | solution.py:34
  53.3 7.3 %collective-permute-start.11 = (bf16[32,128]{1,0:T(8,128)(2,1)S(1)}, bf16[32,128]{1,0:T(8,128)(2,1)S(1)}, u32[]{:S(2)}, u32[]{:S(2)}) collective-permute-start(bf16[32,128]{1,0:T(8,128)(2,1)S(1)} %get-tuple-element.59), channel_id=1, source_target_pairs={{0,4},{1,5},{2,6},{3,7},{4,0},{5,1},{6,2},{7,3},{8,12},{9,13},{10,... | collective-permute-start | bytes 24584 | tf_op jit(solution)/shard_map/ppermute | solution.py:34
  53.4 10.1 %collective-permute-start.12 = (bf16[32,128]{1,0:T(8,128)(2,1)S(1)}, bf16[32,128]{1,0:T(8,128)(2,1)S(1)}, u32[]{:S(2)}, u32[]{:S(2)}) collective-permute-start(bf16[32,128]{1,0:T(8,128)(2,1)S(1)} %get-tuple-element.60), channel_id=1, source_target_pairs={{0,5},{1,4},{2,7},{3,6},{4,1},{5,0},{6,3},{7,2},{8,13},{9,12},{10,... | collective-permute-start | bytes 24584 | tf_op jit(solution)/shard_map/ppermute | solution.py:34
  57.3 6.1 %collective-permute-start.13 = (bf16[32,128]{1,0:T(8,128)(2,1)S(1)}, bf16[32,128]{1,0:T(8,128)(2,1)S(1)}, u32[]{:S(2)}, u32[]{:S(2)}) collective-permute-start(bf16[32,128]{1,0:T(8,128)(2,1)S(1)} %get-tuple-element.61), channel_id=1, source_target_pairs={{0,6},{1,7},{2,0},{3,1},{4,2},{5,3},{6,4},{7,5},{8,14},{9,15},{10,... | collective-permute-start | bytes 24584 | tf_op jit(solution)/shard_map/ppermute | solution.py:34
  59.1 4.5 %collective-permute-start.14 = (bf16[32,128]{1,0:T(8,128)(2,1)S(1)}, bf16[32,128]{1,0:T(8,128)(2,1)S(1)}, u32[]{:S(2)}, u32[]{:S(2)}) collective-permute-start(bf16[32,128]{1,0:T(8,128)(2,1)S(1)} %get-tuple-element.62), channel_id=1, source_target_pairs={{0,7},{1,6},{2,1},{3,0},{4,3},{5,2},{6,5},{7,4},{8,15},{9,14},{10,... | collective-permute-start | bytes 24584 | tf_op jit(solution)/shard_map/ppermute | solution.py:34
  59.1 4.5 %collective-permute-start.8 = (bf16[32,128]{1,0:T(8,128)(2,1)S(1)}, bf16[32,128]{1,0:T(8,128)(2,1)S(1)}, u32[]{:S(2)}, u32[]{:S(2)}) collective-permute-start(bf16[32,128]{1,0:T(8,128)(2,1)S(1)} %get-tuple-element.56), channel_id=1, source_target_pairs={{0,1},{1,0},{2,3},{3,2},{4,5},{5,4},{6,7},{7,6},{8,9},{9,8},{10,11... | collective-permute-start | bytes 24584 | tf_op jit(solution)/shard_map/ppermute | solution.py:34
  60.6 5.4 %collective-permute-start.9 = (bf16[32,128]{1,0:T(8,128)(2,1)S(1)}, bf16[32,128]{1,0:T(8,128)(2,1)S(1)}, u32[]{:S(2)}, u32[]{:S(2)}) collective-permute-start(bf16[32,128]{1,0:T(8,128)(2,1)S(1)} %get-tuple-element.57), channel_id=1, source_target_pairs={{0,2},{1,3},{2,4},{3,5},{4,6},{5,7},{6,0},{7,1},{8,10},{9,11},{10,... | collective-permute-start | bytes 24584 | tf_op jit(solution)/shard_map/ppermute | solution.py:34
  67.8 6.4 %collective-permute-start.15 = (bf16[32,4096]{1,0:T(8,128)(2,1)S(1)}, bf16[32,4096]{1,0:T(8,128)(2,1)S(1)}, u32[]{:S(2)}, u32[]{:S(2)}) collective-permute-start(bf16[32,4096]{1,0:T(8,128)(2,1)S(1)} %get-tuple-element.69), channel_id=1, source_target_pairs={{0,1},{1,0},{2,3},{3,2},{4,5},{5,4},{6,7},{7,6},{8,9},{9,8},{10,11... | collective-permute-start | bytes 786440 | tf_op jit(solution)/shard_map/ppermute | solution.py:34
  68.4 8.6 %collective-permute-start.18 = (bf16[32,4096]{1,0:T(8,128)(2,1)S(1)}, bf16[32,4096]{1,0:T(8,128)(2,1)S(1)}, u32[]{:S(2)}, u32[]{:S(2)}) collective-permute-start(bf16[32,4096]{1,0:T(8,128)(2,1)S(1)} %get-tuple-element.72), channel_id=1, source_target_pairs={{0,1},{1,0},{2,3},{3,2},{4,5},{5,4},{6,7},{7,6},{8,9},{9,8},{10,11... | collective-permute-start | bytes 786440 | tf_op jit(solution)/shard_map/ppermute | solution.py:34
  74.3 12.6 %collective-permute-start.16 = (bf16[16,4096]{1,0:T(8,128)(2,1)S(1)}, bf16[16,4096]{1,0:T(8,128)(2,1)S(1)}, u32[]{:S(2)}, u32[]{:S(2)}) collective-permute-start(bf16[16,4096]{1,0:T(8,128)(2,1)S(1)} %get-tuple-element.88), channel_id=1, source_target_pairs={{0,4},{1,5},{2,6},{3,7},{4,0},{5,1},{6,2},{7,3},{8,12},{9,13},{10,... | collective-permute-start | bytes 393224 | tf_op jit(solution)/shard_map/ppermute | solution.py:34
  74.4 12.6 %collective-permute-start.17 = (bf16[16,4096]{1,0:T(8,128)(2,1)S(1)}, bf16[16,4096]{1,0:T(8,128)(2,1)S(1)}, u32[]{:S(2)}, u32[]{:S(2)}) collective-permute-start(bf16[16,4096]{1,0:T(8,128)(2,1)S(1)} %get-tuple-element.89), channel_id=1, source_target_pairs={{0,2},{1,3},{2,4},{3,5},{4,6},{5,7},{6,0},{7,1},{8,10},{9,11},{10,... | collective-permute-start | bytes 393224 | tf_op jit(solution)/shard_map/ppermute | solution.py:34
  77.1 11.2 %collective-permute-start.19 = (bf16[16,4096]{1,0:T(8,128)(2,1)S(1)}, bf16[16,4096]{1,0:T(8,128)(2,1)S(1)}, u32[]{:S(2)}, u32[]{:S(2)}) collective-permute-start(bf16[16,4096]{1,0:T(8,128)(2,1)S(1)} %add_convert_fusion.3), channel_id=1, source_target_pairs={{0,6},{1,7},{2,0},{3,1},{4,2},{5,3},{6,4},{7,5},{8,14},{9,15},{10,... | collective-permute-start | bytes 393224 | tf_op jit(solution)/shard_map/ppermute | solution.py:34
  88.7 6.9 %collective-permute-start.21 = (bf16[16,4096]{1,0:T(8,128)(2,1)S(1)}, bf16[16,4096]{1,0:T(8,128)(2,1)S(1)}, u32[]{:S(2)}, u32[]{:S(2)}) collective-permute-start(bf16[16,4096]{1,0:T(8,128)(2,1)S(1)} %multiply_convert_fusion.refs_0_), channel_id=1, source_target_pairs={{0,2},{1,3},{2,4},{3,5},{4,6},{5,7},{6,0},{7,1},{8,10},{9,11},{10,... | collective-permute-start | bytes 393224 | tf_op jit(solution)/shard_map/ppermute | solution.py:34
  90.7 7.6 %collective-permute-start.23 = (bf16[16,4096]{1,0:T(8,128)(2,1)S(1)}, bf16[16,4096]{1,0:T(8,128)(2,1)S(1)}, u32[]{:S(2)}, u32[]{:S(2)}) collective-permute-start(bf16[16,4096]{1,0:T(8,128)(2,1)S(1)} %multiply_convert_fusion.refs_0_), channel_id=1, source_target_pairs={{0,4},{1,5},{2,6},{3,7},{4,0},{5,1},{6,2},{7,3},{8,12},{9,13},{10,... | collective-permute-start | bytes 393224 | tf_op jit(solution)/shard_map/ppermute | solution.py:34
  90.7 8.1 %collective-permute-start.25 = (bf16[16,4096]{1,0:T(8,128)(2,1)S(1)}, bf16[16,4096]{1,0:T(8,128)(2,1)S(1)}, u32[]{:S(2)}, u32[]{:S(2)}) collective-permute-start(bf16[16,4096]{1,0:T(8,128)(2,1)S(1)} %multiply_convert_fusion.refs_0_), channel_id=1, source_target_pairs={{0,6},{1,7},{2,0},{3,1},{4,2},{5,3},{6,4},{7,5},{8,14},{9,15},{10,... | collective-permute-start | bytes 393224 | tf_op jit(solution)/shard_map/ppermute | solution.py:34
  93.1 7.2 %collective-permute-start.20 = (bf16[16,4096]{1,0:T(8,128)(2,1)S(1)}, bf16[16,4096]{1,0:T(8,128)(2,1)S(1)}, u32[]{:S(2)}, u32[]{:S(2)}) collective-permute-start(bf16[16,4096]{1,0:T(8,128)(2,1)S(1)} %multiply_convert_fusion.refs_0_), channel_id=1, source_target_pairs={{0,1},{1,0},{2,3},{3,2},{4,5},{5,4},{6,7},{7,6},{8,9},{9,8},{10,11... | collective-permute-start | bytes 393224 | tf_op jit(solution)/shard_map/ppermute | solution.py:34
  95.6 6.3 %collective-permute-start.22 = (bf16[16,4096]{1,0:T(8,128)(2,1)S(1)}, bf16[16,4096]{1,0:T(8,128)(2,1)S(1)}, u32[]{:S(2)}, u32[]{:S(2)}) collective-permute-start(bf16[16,4096]{1,0:T(8,128)(2,1)S(1)} %collective-permute-done.21.refs_2_), channel_id=1, source_target_pairs={{0,1},{1,0},{2,3},{3,2},{4,5},{5,4},{6,7},{7,6},{8,9},{9,8},{10,11... | collective-permute-start | bytes 393224 | tf_op jit(solution)/shard_map/ppermute | solution.py:34
  98.3 6.5 %collective-permute-start.24 = (bf16[16,4096]{1,0:T(8,128)(2,1)S(1)}, bf16[16,4096]{1,0:T(8,128)(2,1)S(1)}, u32[]{:S(2)}, u32[]{:S(2)}) collective-permute-start(bf16[16,4096]{1,0:T(8,128)(2,1)S(1)} %collective-permute-done.23.refs_4_), channel_id=1, source_target_pairs={{0,1},{1,0},{2,3},{3,2},{4,5},{5,4},{6,7},{7,6},{8,9},{9,8},{10,11... | collective-permute-start | bytes 393224 | tf_op jit(solution)/shard_map/ppermute | solution.py:34
  98.8 8.8 %collective-permute-start.26 = (bf16[16,4096]{1,0:T(8,128)(2,1)S(1)}, bf16[16,4096]{1,0:T(8,128)(2,1)S(1)}, u32[]{:S(2)}, u32[]{:S(2)}) collective-permute-start(bf16[16,4096]{1,0:T(8,128)(2,1)S(1)} %collective-permute-done.25.refs_6_), channel_id=1, source_target_pairs={{0,1},{1,0},{2,3},{3,2},{4,5},{5,4},{6,7},{7,6},{8,9},{9,8},{10,11... | collective-permute-start | bytes 393224 | tf_op jit(solution)/shard_map/ppermute | solution.py:34
  111.2 6.4 %collective-permute-start.27 = (bf16[32,4096]{1,0:T(8,128)(2,1)S(1)}, bf16[32,4096]{1,0:T(8,128)(2,1)S(1)}, u32[]{:S(2)}, u32[]{:S(2)}) collective-permute-start(bf16[32,4096]{1,0:T(8,128)(2,1)S(1)} %get-tuple-element.78), channel_id=1, source_target_pairs={{0,1},{1,0},{2,3},{3,2},{4,5},{5,4},{6,7},{7,6},{8,9},{9,8},{10,11... | collective-permute-start | bytes 786440 | tf_op jit(solution)/shard_map/ppermute | solution.py:34
  111.8 8.9 %collective-permute-start.30 = (bf16[32,4096]{1,0:T(8,128)(2,1)S(1)}, bf16[32,4096]{1,0:T(8,128)(2,1)S(1)}, u32[]{:S(2)}, u32[]{:S(2)}) collective-permute-start(bf16[32,4096]{1,0:T(8,128)(2,1)S(1)} %get-tuple-element.81), channel_id=1, source_target_pairs={{0,1},{1,0},{2,3},{3,2},{4,5},{5,4},{6,7},{7,6},{8,9},{9,8},{10,11... | collective-permute-start | bytes 786440 | tf_op jit(solution)/shard_map/ppermute | solution.py:34
  117.7 8.3 %collective-permute-start.28 = (bf16[16,4096]{1,0:T(8,128)(2,1)S(1)}, bf16[16,4096]{1,0:T(8,128)(2,1)S(1)}, u32[]{:S(2)}, u32[]{:S(2)}) collective-permute-start(bf16[16,4096]{1,0:T(8,128)(2,1)S(1)} %get-tuple-element.86), channel_id=1, source_target_pairs={{0,4},{1,5},{2,6},{3,7},{4,0},{5,1},{6,2},{7,3},{8,12},{9,13},{10,... | collective-permute-start | bytes 393224 | tf_op jit(solution)/shard_map/ppermute | solution.py:34
  118.0 8.1 %collective-permute-start.29 = (bf16[16,4096]{1,0:T(8,128)(2,1)S(1)}, bf16[16,4096]{1,0:T(8,128)(2,1)S(1)}, u32[]{:S(2)}, u32[]{:S(2)}) collective-permute-start(bf16[16,4096]{1,0:T(8,128)(2,1)S(1)} %get-tuple-element.87), channel_id=1, source_target_pairs={{0,2},{1,3},{2,4},{3,5},{4,6},{5,7},{6,0},{7,1},{8,10},{9,11},{10,... | collective-permute-start | bytes 393224 | tf_op jit(solution)/shard_map/ppermute | solution.py:34
  120.7 6.6 %collective-permute-start.31 = (bf16[16,4096]{1,0:T(8,128)(2,1)S(1)}, bf16[16,4096]{1,0:T(8,128)(2,1)S(1)}, u32[]{:S(2)}, u32[]{:S(2)}) collective-permute-start(bf16[16,4096]{1,0:T(8,128)(2,1)S(1)} %add_convert_fusion), channel_id=1, source_target_pairs={{0,6},{1,7},{2,0},{3,1},{4,2},{5,3},{6,4},{7,5},{8,14},{9,15},{10,... | collective-permute-start | bytes 393224 | tf_op jit(solution)/shard_map/ppermute | solution.py:34
  (7 other events, 100.2 us)

commit v4 on v3

--- a/solution.py
+++ b/solution.py
@@ -34,19 +34,69 @@
     return lax.ppermute(block, "ctx", pairs)
 
 
-def gather_blocks(block, tall, wide, relay=False):
+def tie_body(count, *refs):
+    total = refs[0][...]
+    for ref in refs[1:count]:
+        total = total + ref[...]
+    refs[-1][...] = total
+
+
+def tie(blocks, tokens):
+    return kernel_call(
+        functools.partial(tie_body, len(blocks)),
+        [(blocks[0].shape, blocks[0].dtype)],
+        [*blocks, *tokens],
+        specs=[VMEM] * len(blocks) + [pl.BlockSpec(memory_space=pl.ANY)] * len(tokens),
+    )[0]
+
+
+def gather_rows(block, tall, wide, tokens_1, tokens_2):
     blocks = {(0, 0): block}
     for dz in range(1, tall):
-        if not (relay and tall == 4 and dz == 2):
+        if tall != 4 or dz != 2:
             blocks[dz, 0] = shift(block, tall, wide, dz, 0)
-    if relay and tall == 4:
+    blocks[1, 0] = tie([blocks[1, 0]], tokens_1)
+    if tall == 4:
         up = shift(blocks[1, 0], tall, wide, 1, 0, lambda z: z in (1, 2))
         down = shift(blocks[3, 0], tall, wide, -1, 0, lambda z: z in (1, 2))
-        blocks[2, 0] = up + down
+        blocks[2, 0] = tie([up, down], tokens_2)
+    else:
+        blocks[tall - 1, 0] = tie([blocks[tall - 1, 0]], tokens_2)
     for dz in [0, 1, *range(tall - 1, 1, -1)]:
         for dy in range(1, wide):
             blocks[dz, dy] = shift(blocks[dz, 0], tall, wide, 0, dy)
     return [blocks[dz, dy] for dz in range(tall) for dy in range(wide)]
+
+
+def stack_body(count, *refs):
+    share = refs[0].shape[0]
+    for index, ref in enumerate(refs[:count]):
+        refs[-1][index * share : (index + 1) * share, :] = ref[...]
+
+
+def gather_half(block, tall, wide, tokens=()):
+    mine = [block if dz == 0 else shift(block, tall, wide, dz, 0) for dz in range(tall)]
+    share = block.shape[0]
+    shape = ((tall * share, block.shape[1]), block.dtype)
+    (mine,) = kernel_call(
+        functools.partial(stack_body, tall),
+        [shape],
+        [*mine, *tokens],
+        specs=[VMEM] * tall + [pl.BlockSpec(memory_space=pl.ANY)] * len(tokens),
+    )
+    return [mine] + [shift(mine, tall, wide, 0, dy) for dy in range(1, wide)]
+
+
+def sum_half(parts, tall, wide):
+    share = parts[0].shape[0] // tall
+    lanes = parts[0].astype(f32)
+    for dy in range(1, wide):
+        lanes = lanes + shift(parts[dy], tall, wide, 0, dy).astype(f32)
+    total = lanes[:share]
+    for dz in [tall // 2, *range(1, tall // 2), *range(tall // 2 + 1, tall)]:
+        one = lanes[dz * share : (dz + 1) * share].astype(bf16)
+        total = total + shift(one, tall, wide, dz, 0).astype(f32)
+    return total
 
 
 def sum_order(tall):
@@ -272,33 +322,70 @@
             heads_out[:, span] = lax.dot_general(
                 probs, values, (((1,), (1,)), ((), ())), preferred_element_type=f32
             ).astype(bf16)
-    spread(heads_out, w_output, parts, plane, False)
-
-
-def spread(left, weight, parts, plane, back):
-    width = weight.shape[1]
+    tall, wide = plane
+    width = w_output.shape[1]
+    tile = tile_of(width // 2, 512)
+    share = parts[0].shape[0] // tall
+    for start in range(0, width, tile):
+        product = dot(heads_out[...], w_output[:, start : start + tile]).astype(bf16)
+        which, local = divmod(start, width // 2)
+        for dy in range(wide):
+            for dz in range(tall):
+                block = product[(dz * wide + dy) * share : (dz * wide + dy + 1) * share, :]
+                part = parts[which * wide + dy]
+                part[dz * share : (dz + 1) * share, local : local + tile] = block
+
+
+def scale_body(hidden_1, hidden_2, gain, out):
+    width = hidden_2.shape[1]
+    square = jnp.sum(hidden_1[...] * hidden_1[...], axis=1, keepdims=True)
+    square += jnp.sum(hidden_2[...] * hidden_2[...], axis=1, keepdims=True)
+    factor = lax.rsqrt(square / (2 * width) + norm_eps)
+    high = factor.astype(bf16).astype(f32)
+    out[:, :width] = (hidden_2[...] * gain[...]).astype(bf16)
+    lane = lax.broadcasted_iota(i32, (out.shape[0], 128), 1)
+    out[:, width:] = jnp.where(lane < 64, high, factor - high).astype(bf16)
+
+
+def half_body(plane, *refs):
+    tall, wide = plane
+    blocks, (w_gate, w_up, gate, upward, piece) = refs[:wide], refs[wide:]
+    fill(blocks, piece, tall, wide)
+    depth, width = piece.shape[1], w_gate.shape[1]
+    tile = tile_of(width, 256)
+    for start in range(0, width, tile):
+        span = slice(start, start + tile)
+        gate[:, span] = dot(piece[...], w_gate[:depth, span])
+        upward[:, span] = dot(piece[...], w_up[:depth, span])
+
+
+def fill(blocks, piece, tall, wide):
+    share = blocks[0].shape[0] // tall
+    for dz in range(tall):
+        for dy in range(wide):
+            at = (dz * wide + dy) * share
+            piece[at : at + share, :] = blocks[dy][dz * share : (dz + 1) * share, :]
+
+
+def mlp_body(plane, *refs):
+    tall, wide = plane
+    blocks, (gate_1, up_1, w_gate, w_up, w_down) = refs[:wide], refs[wide : wide + 5]
+    parts, (piece, inner) = refs[wide + 5 : -2], refs[-2:]
+    fill(blocks, piece, tall, wide)
+    depth, width = w_gate.shape[0] // 2, w_gate.shape[1]
+    factor = piece[:, depth : depth + 1].astype(f32) + piece[:, depth + 64 : depth + 65].astype(f32)
+    tile = tile_of(width, 256)
+    for start in range(0, width, tile):
+        span = slice(start, start + tile)
+        gate = (gate_1[:, span] + dot(piece[:, :depth], w_gate[depth:, span])) * factor
+        upward = (up_1[:, span] + dot(piece[:, :depth], w_up[depth:, span])) * factor
+        inner[:, span] = (gate / (1.0 + jnp.exp(-gate)) * upward).astype(bf16)
+    width = w_down.shape[1]
     tile = tile_of(width, 512)
     for start in range(0, width, tile):
         span = slice(start, start + tile)
-        product = dot(left[...], weight[:, span]).astype(bf16)
-        store_parts(parts, *plane, span, product, back)
-
-
-def mlp_body(plane, *refs):
-    count = plane[0] * plane[1]
-    blocks, (w_gate, w_up, w_down) = refs[:count], refs[count : count + 3]
-    parts, (piece, inner) = refs[count + 3 : -2], refs[-2:]
-    share = blocks[0].shape[0]
-    for index, block in enumerate(blocks):
-        piece[index * share : (index + 1) * share, :] = block[...]
-    width = w_gate.shape[1]
-    tile = tile_of(width, 256)
-    for start in range(0, width, tile):
-        span = slice(start, start + tile)
-        gate = dot(piece[...], w_gate[:, span])
-        upward = dot(piece[...], w_up[:, span])
-        inner[:, span] = (gate / (1.0 + jnp.exp(-gate)) * upward).astype(bf16)
-    spread(inner, w_down, parts, plane, True)
+        product = dot(inner[...], w_down[:, span]).astype(bf16)
+        store_parts(parts, *plane, span, product, True)
 
 
 def on_device(
@@ -338,16 +425,12 @@
         specs=[scalar, VMEM, VMEM],
         flops=2 * capacity * tokens * model,
     )
-    blocks = gather_blocks(outgoing, tall, wide, relay=True)
-    attn_gain, w_key, w_value, w_query, _ = load(
+    attn_gain, w_key, w_value, w_query, token_1 = load(
         outgoing, attn_gain.reshape(1, model), w_key, w_value, w_query
     )
-    near = blocks[wide]
-    w_output, *tokens_1 = load(near, w_output)
-    w_gate, *tokens_2 = load(near, w_gate)
-    w_up, *tokens_3 = load(near, w_up)
-    w_down, *tokens_4 = load(near, w_down)
-    loaded = tokens_1 + tokens_2 + tokens_3 + tokens_4
+    w_gate, token_2 = load(outgoing, w_gate)
+    w_output, token_3 = load(token_2, w_output)
+    w_up, token_4 = load(token_3, w_up)
 
     each = kv_local * 2 * depth
     notes = np.zeros((max(count * each, 2 * kv_local * HEAD_DIM), 4), np.float32)
@@ -371,6 +454,7 @@
         [me, routed, balance, notes],
         specs=[scalar, VMEM, VMEM, VMEM],
     )
+    blocks = gather_rows(outgoing, tall, wide, [token_1, token_2, positions], [token_3, token_4])
 
     half = HEAD_DIM // 2
     steps_f = jnp.arange(half, dtype=f32)
@@ -385,7 +469,7 @@
     normed, own, *sent = kernel_call(
         functools.partial(kv_body, count),
         [((total, model), bf16), ((share, model), bf16)] + [((each, total), bf16)] * count,
-        [*blocks, pick_rows, in_order, columns, attn_gain, w_key, w_value, *loaded],
+        [*blocks, pick_rows, in_order, columns, attn_gain, w_key, w_value],
         [pltpu.VMEM((total, model), bf16)],
         flops=2 * total * model * 512,
     )
@@ -398,28 +482,44 @@
         [normed, w_query, q_cos, q_sin],
         flops=2 * total * model * local_heads * HEAD_DIM,
     )
-    part_shapes = sum_shapes(tall, wide, share, model)
-    attn_parts = kernel_call(
+    half_width = model // 2
+    parts = kernel_call(
         functools.partial(attend_body, plane, kv_local),
-        part_shapes,
+        [((tall * share, half_width), bf16)] * (2 * wide),
         [*arrived, query, unmix, k_cos, k_sin, routed, positions, w_output],
         [pltpu.VMEM((total, local_heads * HEAD_DIM), bf16)],
         flops=2 * total * model * local_heads * HEAD_DIM,
     )
-    attn_own = scatter_sum(attn_parts, tall, wide)
+    w_down, token_5 = load(parts[0], w_down)
     own_rows = own.astype(f32)
-    hidden = own_rows + attn_own
-    mean_sq = jnp.mean(hidden * hidden, axis=-1, keepdims=True)
-    mnorm = (hidden * lax.rsqrt(mean_sq + norm_eps) * mlp_gain).astype(bf16)
-    pieces = gather_blocks(mnorm, tall, wide)
+    attn_1 = sum_half(parts[:wide], tall, wide)
+    hidden_1 = own_rows[:, :half_width] + attn_1
+    scaled_1 = (hidden_1 * mlp_gain[:half_width]).astype(bf16)
+    pieces_1 = gather_half(scaled_1, tall, wide, [token_5])
+    attn_2 = sum_half(parts[wide:], tall, wide)
+    hidden_2 = own_rows[:, half_width:] + attn_2
+    (scaled_2,) = kernel_call(
+        scale_body,
+        [((share, half_width + 128), bf16)],
+        [hidden_1, hidden_2, mlp_gain[half_width:].reshape(1, half_width)],
+    )
+    pieces_2 = gather_half(scaled_2, tall, wide)
     hidden_units = w_gate.shape[1]
+    gate_1, up_1 = kernel_call(
+        functools.partial(half_body, plane),
+        [((total, hidden_units), f32)] * 2,
+        [*pieces_1, w_gate, w_up],
+        [pltpu.VMEM((total, half_width), bf16)],
+        flops=2 * total * model * hidden_units,
+    )
     mlp_parts = kernel_call(
         functools.partial(mlp_body, plane),
-        part_shapes,
-        [*pieces, w_gate, w_up, w_down],
-        [pltpu.VMEM((total, model), bf16), pltpu.VMEM((total, hidden_units), bf16)],
-        flops=6 * total * model * hidden_units,
-    )
+        sum_shapes(tall, wide, share, model),
+        [*pieces_2, gate_1, up_1, w_gate, w_up, w_down],
+        [pltpu.VMEM((total, half_width + 128), bf16), pltpu.VMEM((total, hidden_units), bf16)],
+        flops=4 * total * model * hidden_units,
+    )
+    attn_own = jnp.concatenate([attn_1, attn_2], axis=1)
     mlp_own = scatter_sum(mlp_parts, tall, wide)
     router_score = jnp.sum(own_rows * w_router[None, :], axis=1, keepdims=True)
     return (own_rows + router_score * (attn_own + mlp_own)).astype(bf16)

time: 128 us -> 145 us (1.13)
  local copies, waits for them, and re-layouts: 3.45 us -> 17.9 us
  waiting for transfers between devices: 55.1 us -> 44.8 us
  starting transfers between devices: 42.1 us -> 52.3 us
    unnamed x14 -> x50, local copies, waits for them, and re-layouts: 3.45 us -> 17.9 us
    ppermute x32 -> x36, waiting for transfers between devices: 55.1 us -> 44.8 us  [shift(): return lax.ppermute(block, 'ctx', pairs)]
    ppermute x32 -> x36, starting transfers between devices: 42.1 us -> 52.3 us  [shift(): return lax.ppermute(block, 'ctx', pairs)]
    pallas_call x6 -> x12, Pallas kernels: 9.24 us -> 10.8 us  [kernel_call(): pl.pallas_call(body, out_shape=[jax.ShapeDtypeStruct(s, d) for s, d in ou...]
  transfers between devices with their start and end apart: 32 -> 36, of which waited for: 17 -> 16; matrix products, arithmetic and copies ran while one was open for 1% -> 2% of each run, Pallas kernels for 14% -> 13%
where the time goes in v4:
time: 145 us
  starting transfers between devices  52.3 us (36%)
  waiting for transfers between devices  44.8 us (31%)
  Pallas kernels  26.1 us (18%)
  local copies, waits for them, and re-layouts  17.9 us (12%)
  other arithmetic  3.24 us (2%)
    ppermute x36, starting transfers between devices, shift(): return lax.ppermute(block, 'ctx', pairs)  52.3 us
    ppermute x36, waiting for transfers between devices, shift(): return lax.ppermute(block, 'ctx', pairs)  44.8 us
    unnamed x50, local copies, waits for them, and re-layouts  17.9 us
    pallas_call x5, Pallas kernels, load(): pl.pallas_call(functools.partial(load_body, len(arrays)), out_shape=[pltp...  15.4 us
    pallas_call x12, Pallas kernels, kernel_call(): pl.pallas_call(body, out_shape=[jax.ShapeDtypeStruct(s, d) for s, d in ou...  10.8 us
  transfers between devices with their start and end apart: 36, of which 16 were waited for; matrix products, arithmetic and copies ran while one was open for 2% of the time, Pallas kernels for 13%

profile of v4, /device:TPU:0, one launch (start us, length us, event | category | flops | bytes accessed | tf_op | source)
XLA Modules:
  0.0 144.8 jit_solution(13242675112248325584)
XLA Ops:
  2.3 3.1 %collective-permute-start.1 = (bf16[32,4096]{1,0:T(8,128)(2,1)S(1)}, bf16[32,4096]{1,0:T(8,128)(2,1)S(1)}, u32[]{:S(2)}, u32[]{:S(2)}) collective-permute-start(bf16[32,4096]{1,0:T(8,128)(2,1)S(1)} %shard_map.136.refs_0_), channel_id=1, source_target_pairs={{0,2},{1,3},{2,4},{3,5},{4,6},{5,7},{6,0},{7,1},{8,10},{9,11},{10,... | collective-permute-start | bytes 786440 | tf_op jit(solution)/shard_map/ppermute | solution.py:34
  5.4 2.1 %collective-permute-start.4 = (bf16[32,4096]{1,0:T(8,128)(2,1)S(1)}, bf16[32,4096]{1,0:T(8,128)(2,1)S(1)}, u32[]{:S(2)}, u32[]{:S(2)}) collective-permute-start(bf16[32,4096]{1,0:T(8,128)(2,1)S(1)} %shard_map.136.refs_0_), channel_id=1, source_target_pairs={{0,6},{1,7},{2,0},{3,1},{4,2},{5,3},{6,4},{7,5},{8,14},{9,15},{10,... | collective-permute-start | bytes 786440 | tf_op jit(solution)/shard_map/ppermute | solution.py:34
  7.5 3.4 %shard_map.138 = (bf16[4096,1024]{1,0:T(8,128)(2,1)S(1)}, f32[8,128]{1,0:T(8,128)S(1)}) custom-call(bf16[32,4096]{1,0:T(8,128)(2,1)S(1)} %shard_map.136.refs_0_, bf16[4096,1024]{1,0:T(8,128)(2,1)} %refs_1_.4), custom_call_target="tpu_custom_call" | custom-call | bytes 16777216 | tf_op jit(solution)/shard_map/pallas_call | solution.py:179
  10.9 3.3 %copy-done = bf16[4096,1024]{1,0:T(8,128)(2,1)} copy-done((bf16[4096,1024]{1,0:T(8,128)(2,1)}, bf16[4096,1024]{1,0:T(8,128)(2,1)S(1)}, u32[]{:S(2)}) %copy-start) | copy-done | bytes 8388632
  15.7 3.0 %shard_map.137 = (f32[1,4096]{1,0:T(1,128)S(1)}, bf16[4096,128]{1,0:T(8,128)(2,1)S(1)}, bf16[4096,128]{1,0:T(8,128)(2,1)S(1)}, bf16[4096,512]{1,0:T(8,128)(2,1)S(1)}, f32[8,128]{1,0:T(8,128)S(1)}) custom-call(bf16[32,4096]{1,0:T(8,128)(2,1)S(1)} %shard_map.136.refs_0_, f32[1,4096]{1,0:T(1,128)} %bitcast.12, bf16[4096,128]{1,0:T(8,128)(2,1)} %refs_2_.1, ...), custom_call_target="tpu_custom_call" | custom-call | bytes 12615680 | tf_op jit(solution)/shard_map/pallas_call | solution.py:179
  18.7 2.0 %copy-done.5 = bf16[4096,512]{1,0:T(8,128)(2,1)} copy-done((bf16[4096,512]{1,0:T(8,128)(2,1)}, bf16[4096,512]{1,0:T(8,128)(2,1)S(1)}, u32[]{:S(2)}) %copy-start.5) | copy-done | bytes 4194328
  22.7 1.7 %collective-permute-start = (bf16[32,4096]{1,0:T(8,128)(2,1)S(1)}, bf16[32,4096]{1,0:T(8,128)(2,1)S(1)}, u32[]{:S(2)}, u32[]{:S(2)}) collective-permute-start(bf16[32,4096]{1,0:T(8,128)(2,1)S(1)} %shard_map.136.refs_0_), channel_id=1, source_target_pairs={{0,1},{1,0},{2,3},{3,2},{4,5},{5,4},{6,7},{7,6},{8,9},{9,8},{10,11... | collective-permute-start | bytes 786440 | tf_op jit(solution)/shard_map/ppermute | solution.py:34
  24.5 2.2 %shard_map.141 = (bf16[512,4096]{1,0:T(8,128)(2,1)S(1)}, f32[8,128]{1,0:T(8,128)S(1)}) custom-call(f32[8,128]{1,0:T(8,128)S(1)} %get-tuple-element.46.refs_2_.refs_0_, bf16[512,4096]{1,0:T(8,128)(2,1)} %refs_1_.5), custom_call_target="tpu_custom_call" | custom-call | bytes 8388608 | tf_op jit(solution)/shard_map/pallas_call | solution.py:179
  26.7 2.0 %copy-done.3 = bf16[512,4096]{1,0:T(8,128)(2,1)} copy-done((bf16[512,4096]{1,0:T(8,128)(2,1)}, bf16[512,4096]{1,0:T(8,128)(2,1)S(1)}, u32[]{:S(2)}) %copy-start.3) | copy-done | bytes 4194328
  28.7 3.4 %shard_map.142 = (bf16[4096,1024]{1,0:T(8,128)(2,1)S(1)}, f32[8,128]{1,0:T(8,128)S(1)}) custom-call(f32[8,128]{1,0:T(8,128)S(1)} %get-tuple-element.48.refs_0_.refs_2_, bf16[4096,1024]{1,0:T(8,128)(2,1)} %refs_1_.6), custom_call_target="tpu_custom_call" | custom-call | bytes 16777216 | tf_op jit(solution)/shard_map/pallas_call | solution.py:179
  32.1 3.3 %copy-done.1 = bf16[4096,1024]{1,0:T(8,128)(2,1)} copy-done((bf16[4096,1024]{1,0:T(8,128)(2,1)}, bf16[4096,1024]{1,0:T(8,128)(2,1)S(1)}, u32[]{:S(2)}) %copy-start.1) | copy-done | bytes 8388632
  39.9 5.0 %collective-permute-done.2.refs_3_ = bf16[32,4096]{1,0:T(8,128)(2,1)} collective-permute-done((bf16[32,4096]{1,0:T(8,128)(2,1)S(1)}, bf16[32,4096]{1,0:T(8,128)(2,1)}, u32[]{:S(2)}, u32[]{:S(2)}) %collective-permute-start.2) | collective-permute-done | bytes 262176 | tf_op jit(solution)/shard_map/ppermute | solution.py:34
  44.8 5.6 %collective-permute-done.7.refs_7_ = bf16[32,4096]{1,0:T(8,128)(2,1)} collective-permute-done((bf16[32,4096]{1,0:T(8,128)(2,1)S(1)}, bf16[32,4096]{1,0:T(8,128)(2,1)}, u32[]{:S(2)}, u32[]{:S(2)}) %collective-permute-start.7) | collective-permute-done | bytes 262176 | tf_op jit(solution)/shard_map/ppermute | solution.py:34
  50.5 3.7 %collective-permute-done.6.refs_5_ = bf16[32,4096]{1,0:T(8,128)(2,1)} collective-permute-done((bf16[32,4096]{1,0:T(8,128)(2,1)S(1)}, bf16[32,4096]{1,0:T(8,128)(2,1)}, u32[]{:S(2)}, u32[]{:S(2)}) %collective-permute-start.6) | collective-permute-done | bytes 262176 | tf_op jit(solution)/shard_map/ppermute | solution.py:34
  56.7 2.9 %shard_map.144 = (bf16[128,4096]{1,0:T(8,128)(2,1)S(1)}, bf16[16,4096]{1,0:T(8,128)(2,1)S(1)}, bf16[32,128]{1,0:T(8,128)(2,1)S(1)}, bf16[32,128]{1,0:T(8,128)(2,...) custom-call(bf16[32,4096]{1,0:T(8,128)(2,1)S(1)} %shard_map.136.refs, ...), custom_call_target="tpu_custom_call" | custom-call | flops 536870912 | bytes 1048576 | tf_op jit(solution)/shard_map/pallas_call | solution.py:154
  59.6 2.8 %collective-permute-start.10 = (bf16[32,128]{1,0:T(8,128)(2,1)S(1)}, bf16[32,128]{1,0:T(8,128)(2,1)S(1)}, u32[]{:S(2)}, u32[]{:S(2)}) collective-permute-start(bf16[32,128]{1,0:T(8,128)(2,1)S(1)} %get-tuple-element.60), channel_id=1, source_target_pairs={{0,3},{1,2},{2,5},{3,4},{4,7},{5,6},{6,1},{7,0},{8,11},{9,10},{10,... | collective-permute-start | bytes 24584 | tf_op jit(solution)/shard_map/ppermute | solution.py:34
  63.8 2.6 %collective-permute-start.12 = (bf16[32,128]{1,0:T(8,128)(2,1)S(1)}, bf16[32,128]{1,0:T(8,128)(2,1)S(1)}, u32[]{:S(2)}, u32[]{:S(2)}) collective-permute-start(bf16[32,128]{1,0:T(8,128)(2,1)S(1)} %get-tuple-element.62), channel_id=1, source_target_pairs={{0,5},{1,4},{2,7},{3,6},{4,1},{5,0},{6,3},{7,2},{8,13},{9,12},{10,... | collective-permute-start | bytes 24584 | tf_op jit(solution)/shard_map/ppermute | solution.py:34
  71.2 2.2 %copy-done.6 = bf16[4096,512]{1,0:T(8,128)(2,1)S(1)} copy-done((bf16[4096,512]{1,0:T(8,128)(2,1)S(1)}, bf16[4096,512]{1,0:T(8,128)(2,1)}, u32[]{:S(2)}) %copy-start.6) | copy-done | bytes 4194328
  79.0 4.3 %collective-permute-done.19 = bf16[64,2048]{1,0:T(8,128)(2,1)S(1)} collective-permute-done((bf16[64,2048]{1,0:T(8,128)(2,1)S(1)}, bf16[64,2048]{1,0:T(8,128)(2,1)S(1)}, u32[]{:S(2)}, u32[]{:S(2)}) %collective-permute-start.19) | collective-permute-done | bytes 262176 | tf_op jit(solution)/shard_map/ppermute | solution.py:34
  86.0 2.6 %collective-permute-start.22 = (bf16[16,2048]{1,0:T(8,128)(2,1)S(1)}, bf16[16,2048]{1,0:T(8,128)(2,1)S(1)}, u32[]{:S(2)}, u32[]{:S(2)}) collective-permute-start(bf16[16,2048]{1,0:T(8,128)(2,1)S(1)} %get-tuple-element.102), channel_id=1, source_target_pairs={{0,6},{1,7},{2,0},{3,1},{4,2},{5,3},{6,4},{7,5},{8,14},{9,15},{10,... | collective-permute-start | bytes 196616 | tf_op jit(solution)/shard_map/ppermute | solution.py:34
  89.4 3.3 %collective-permute-start.18 = (bf16[16,2048]{1,0:T(8,128)(2,1)S(1)}, bf16[16,2048]{1,0:T(8,128)(2,1)S(1)}, u32[]{:S(2)}, u32[]{:S(2)}) collective-permute-start(bf16[16,2048]{1,0:T(8,128)(2,1)S(1)} %get-tuple-element.99), channel_id=1, source_target_pairs={{0,6},{1,7},{2,0},{3,1},{4,2},{5,3},{6,4},{7,5},{8,14},{9,15},{10,... | collective-permute-start | bytes 196616 | tf_op jit(solution)/shard_map/ppermute | solution.py:34
  92.7 3.7 %collective-permute-done.16 = bf16[16,2048]{1,0:T(8,128)(2,1)S(1)} collective-permute-done((bf16[16,2048]{1,0:T(8,128)(2,1)S(1)}, bf16[16,2048]{1,0:T(8,128)(2,1)S(1)}, u32[]{:S(2)}, u32[]{:S(2)}) %collective-permute-start.16) | collective-permute-done | bytes 65568 | tf_op jit(solution)/shard_map/ppermute | solution.py:34
  99.5 2.1 %collective-permute-start.29 = (bf16[16,2048]{1,0:T(8,128)(2,1)S(1)}, bf16[16,2048]{1,0:T(8,128)(2,1)S(1)}, u32[]{:S(2)}, u32[]{:S(2)}) collective-permute-start(bf16[16,2048]{1,0:T(8,128)(2,1)S(1)} %get-tuple-element.85.refs_0_), channel_id=1, source_target_pairs={{0,6},{1,7},{2,0},{3,1},{4,2},{5,3},{6,4},{7,5},{8,14},{9,15},{10,... | collective-permute-start | bytes 196616 | tf_op jit(solution)/shard_map/ppermute | solution.py:34
  101.7 3.4 %shard_map.149 = (bf16[1024,4096]{1,0:T(8,128)(2,1)S(1)}, f32[8,128]{1,0:T(8,128)S(1)}) custom-call(bf16[64,2048]{1,0:T(8,128)(2,1)S(1)} %get-tuple-element.69.refs_0_, bf16[1024,4096]{1,0:T(8,128)(2,1)} %refs_1_.7), custom_call_target="tpu_custom_call" | custom-call | bytes 16777216 | tf_op jit(solution)/shard_map/pallas_call | solution.py:179
  107.5 2.0 %collective-permute-start.23 = (bf16[16,2176]{1,0:T(8,128)(2,1)S(1)}, bf16[16,2176]{1,0:T(8,128)(2,1)S(1)}, u32[]{:S(2)}, u32[]{:S(2)}) collective-permute-start(bf16[16,2176]{1,0:T(8,128)(2,1)S(1)} %shard_map.147.refs_0_), channel_id=1, source_target_pairs={{0,2},{1,3},{2,4},{3,5},{4,6},{5,7},{6,0},{7,1},{8,10},{9,11},{10,... | collective-permute-start | bytes 208904 | tf_op jit(solution)/shard_map/ppermute | solution.py:34
  112.0 1.7 %collective-permute-done.23.refs_1_ = bf16[16,2176]{1,0:T(8,128)(2,1)S(1)} collective-permute-done((bf16[16,2176]{1,0:T(8,128)(2,1)S(1)}, bf16[16,2176]{1,0:T(8,128)(2,1)S(1)}, u32[]{:S(2)}, u32[]{:S(2)}) %collective-permute-start.23) | collective-permute-done | bytes 69664 | tf_op jit(solution)/shard_map/ppermute | solution.py:34
  118.2 7.3 %collective-permute-done.26.refs_1_ = bf16[64,2176]{1,0:T(8,128)(2,1)S(1)} collective-permute-done((bf16[64,2176]{1,0:T(8,128)(2,1)S(1)}, bf16[64,2176]{1,0:T(8,128)(2,1)S(1)}, u32[]{:S(2)}, u32[]{:S(2)}) %collective-permute-start.26) | collective-permute-done | bytes 278560 | tf_op jit(solution)/shard_map/ppermute | solution.py:34
  125.5 2.6 %shard_map.152 = (bf16[16,4096]{1,0:T(8,128)(2,1)S(1)}, bf16[16,4096]{1,0:T(8,128)(2,1)S(1)}, bf16[16,4096]{1,0:T(8,128)(2,1)S(1)}, bf16[16,4096]{1,0:T(8,128)(2...) custom-call(bf16[64,2176]{1,0:T(8,128)(2,1)S(1)} %shard_map.148.refs_0_, ...), custom_call_target="tpu_custom_call" | custom-call | flops 2147483648 | bytes 1048576 | tf_op jit(solution)/shard_map/pallas_call | solution.py:154
  130.2 4.3 %collective-permute-done.31 = bf16[32,4096]{1,0:T(8,128)(2,1)S(1)} collective-permute-done((bf16[32,4096]{1,0:T(8,128)(2,1)S(1)}, bf16[32,4096]{1,0:T(8,128)(2,1)S(1)}, u32[]{:S(2)}, u32[]{:S(2)}) %collective-permute-start.31) | collective-permute-done | bytes 262176 | tf_op jit(solution)/shard_map/ppermute | solution.py:34
  135.3 2.2 %collective-permute-start.33 = (bf16[16,4096]{1,0:T(8,128)(2,1)S(1)}, bf16[16,4096]{1,0:T(8,128)(2,1)S(1)}, u32[]{:S(2)}, u32[]{:S(2)}) collective-permute-start(bf16[16,4096]{1,0:T(8,128)(2,1)S(1)} %get-tuple-element.95), channel_id=1, source_target_pairs={{0,2},{1,3},{2,4},{3,5},{4,6},{5,7},{6,0},{7,1},{8,10},{9,11},{10,... | collective-permute-start | bytes 393224 | tf_op jit(solution)/shard_map/ppermute | solution.py:34
  137.5 2.2 %collective-permute-start.35 = (bf16[16,4096]{1,0:T(8,128)(2,1)S(1)}, bf16[16,4096]{1,0:T(8,128)(2,1)S(1)}, u32[]{:S(2)}, u32[]{:S(2)}) collective-permute-start(bf16[16,4096]{1,0:T(8,128)(2,1)S(1)} %add_convert_fusion), channel_id=1, source_target_pairs={{0,6},{1,7},{2,0},{3,1},{4,2},{5,3},{6,4},{7,5},{8,14},{9,15},{10,... | collective-permute-start | bytes 393224 | tf_op jit(solution)/shard_map/ppermute | solution.py:34
  139.8 2.9 %collective-permute-done.32 = bf16[16,4096]{1,0:T(8,128)(2,1)S(1)} collective-permute-done((bf16[16,4096]{1,0:T(8,128)(2,1)S(1)}, bf16[16,4096]{1,0:T(8,128)(2,1)S(1)}, u32[]{:S(2)}, u32[]{:S(2)}) %collective-permute-start.32) | collective-permute-done | bytes 131104 | tf_op jit(solution)/shard_map/ppermute | solution.py:34
  (125 shorter events, 45.5 us)
Async XLA Ops:
  2.3 18.4 %collective-permute-start.1 = (bf16[32,4096]{1,0:T(8,128)(2,1)S(1)}, bf16[32,4096]{1,0:T(8,128)(2,1)S(1)}, u32[]{:S(2)}, u32[]{:S(2)}) collective-permute-start(bf16[32,4096]{1,0:T(8,128)(2,1)S(1)} %shard_map.136.refs_0_), channel_id=1, source_target_pairs={{0,2},{1,3},{2,4},{3,5},{4,6},{5,7},{6,0},{7,1},{8,10},{9,11},{10,... | collective-permute-start | bytes 786440 | tf_op jit(solution)/shard_map/ppermute | solution.py:34
  5.4 16.0 %collective-permute-start.4 = (bf16[32,4096]{1,0:T(8,128)(2,1)S(1)}, bf16[32,4096]{1,0:T(8,128)(2,1)S(1)}, u32[]{:S(2)}, u32[]{:S(2)}) collective-permute-start(bf16[32,4096]{1,0:T(8,128)(2,1)S(1)} %shard_map.136.refs_0_), channel_id=1, source_target_pairs={{0,6},{1,7},{2,0},{3,1},{4,2},{5,3},{6,4},{7,5},{8,14},{9,15},{10,... | collective-permute-start | bytes 786440 | tf_op jit(solution)/shard_map/ppermute | solution.py:34
  20.7 16.8 %collective-permute-start.3 = (bf16[32,4096]{1,0:T(8,128)(2,1)S(1)}, bf16[32,4096]{1,0:T(8,128)(2,1)S(1)}, u32[]{:S(2)}, u32[]{:S(2)}) collective-permute-start(bf16[32,4096]{1,0:T(8,128)(2,1)S(1)} %shard_map.140.refs_2_), channel_id=1, source_target_pairs={{2,4},{3,5},{4,6},{5,7},{10,12},{11,13},{12,14},{13,15},{18,20},{1... | collective-permute-start | bytes 786440 | tf_op jit(solution)/shard_map/ppermute | solution.py:34
  21.4 16.1 %collective-permute-start.5 = (bf16[32,4096]{1,0:T(8,128)(2,1)S(1)}, bf16[32,4096]{1,0:T(8,128)(2,1)S(1)}, u32[]{:S(2)}, u32[]{:S(2)}) collective-permute-start(bf16[32,4096]{1,0:T(8,128)(2,1)S(1)} %collective-permute-done.4.refs_6_), channel_id=1, source_target_pairs={{2,0},{3,1},{4,2},{5,3},{10,8},{11,9},{12,10},{13,11},{18,16},{19,... | collective-permute-start | bytes 786440 | tf_op jit(solution)/shard_map/ppermute | solution.py:34
  22.7 17.1 %collective-permute-start = (bf16[32,4096]{1,0:T(8,128)(2,1)S(1)}, bf16[32,4096]{1,0:T(8,128)(2,1)S(1)}, u32[]{:S(2)}, u32[]{:S(2)}) collective-permute-start(bf16[32,4096]{1,0:T(8,128)(2,1)S(1)} %shard_map.136.refs_0_), channel_id=1, source_target_pairs={{0,1},{1,0},{2,3},{3,2},{4,5},{5,4},{6,7},{7,6},{8,9},{9,8},{10,11... | collective-permute-start | bytes 786440 | tf_op jit(solution)/shard_map/ppermute | solution.py:34
  35.4 9.4 %collective-permute-start.2 = (bf16[32,4096]{1,0:T(8,128)(2,1)S(1)}, bf16[32,4096]{1,0:T(8,128)(2,1)}, u32[]{:S(2)}, u32[]{:S(2)}) collective-permute-start(bf16[32,4096]{1,0:T(8,128)(2,1)S(1)} %shard_map.140.refs_2_), channel_id=1, source_target_pairs={{0,1},{1,0},{2,3},{3,2},{4,5},{5,4},{6,7},{7,6},{8,9},{9,8},{10,11... | collective-permute-start | bytes 786440 | tf_op jit(solution)/shard_map/ppermute | solution.py:34
  35.8 14.6 %collective-permute-start.7 = (bf16[32,4096]{1,0:T(8,128)(2,1)S(1)}, bf16[32,4096]{1,0:T(8,128)(2,1)}, u32[]{:S(2)}, u32[]{:S(2)}) collective-permute-start(bf16[32,4096]{1,0:T(8,128)(2,1)S(1)} %collective-permute-done.4.refs_6_), channel_id=1, source_target_pairs={{0,1},{1,0},{2,3},{3,2},{4,5},{5,4},{6,7},{7,6},{8,9},{9,8},{10,11... | collective-permute-start | bytes 786440 | tf_op jit(solution)/shard_map/ppermute | solution.py:34
  37.5 16.6 %collective-permute-start.6 = (bf16[32,4096]{1,0:T(8,128)(2,1)S(1)}, bf16[32,4096]{1,0:T(8,128)(2,1)}, u32[]{:S(2)}, u32[]{:S(2)}) collective-permute-start(bf16[32,4096]{1,0:T(8,128)(2,1)S(1)} %shard_map.143.refs_4_), channel_id=1, source_target_pairs={{0,1},{1,0},{2,3},{3,2},{4,5},{5,4},{6,7},{7,6},{8,9},{9,8},{10,11... | collective-permute-start | bytes 786440 | tf_op jit(solution)/shard_map/ppermute | solution.py:34
  59.6 9.6 %collective-permute-start.10 = (bf16[32,128]{1,0:T(8,128)(2,1)S(1)}, bf16[32,128]{1,0:T(8,128)(2,1)S(1)}, u32[]{:S(2)}, u32[]{:S(2)}) collective-permute-start(bf16[32,128]{1,0:T(8,128)(2,1)S(1)} %get-tuple-element.60), channel_id=1, source_target_pairs={{0,3},{1,2},{2,5},{3,4},{4,7},{5,6},{6,1},{7,0},{8,11},{9,10},{10,... | collective-permute-start | bytes 24584 | tf_op jit(solution)/shard_map/ppermute | solution.py:34
  62.4 7.3 %collective-permute-start.11 = (bf16[32,128]{1,0:T(8,128)(2,1)S(1)}, bf16[32,128]{1,0:T(8,128)(2,1)S(1)}, u32[]{:S(2)}, u32[]{:S(2)}) collective-permute-start(bf16[32,128]{1,0:T(8,128)(2,1)S(1)} %get-tuple-element.61), channel_id=1, source_target_pairs={{0,4},{1,5},{2,6},{3,7},{4,0},{5,1},{6,2},{7,3},{8,12},{9,13},{10,... | collective-permute-start | bytes 24584 | tf_op jit(solution)/shard_map/ppermute | solution.py:34
  63.8 10.3 %collective-permute-start.12 = (bf16[32,128]{1,0:T(8,128)(2,1)S(1)}, bf16[32,128]{1,0:T(8,128)(2,1)S(1)}, u32[]{:S(2)}, u32[]{:S(2)}) collective-permute-start(bf16[32,128]{1,0:T(8,128)(2,1)S(1)} %get-tuple-element.62), channel_id=1, source_target_pairs={{0,5},{1,4},{2,7},{3,6},{4,1},{5,0},{6,3},{7,2},{8,13},{9,12},{10,... | collective-permute-start | bytes 24584 | tf_op jit(solution)/shard_map/ppermute | solution.py:34
  66.5 7.7 %collective-permute-start.13 = (bf16[32,128]{1,0:T(8,128)(2,1)S(1)}, bf16[32,128]{1,0:T(8,128)(2,1)S(1)}, u32[]{:S(2)}, u32[]{:S(2)}) collective-permute-start(bf16[32,128]{1,0:T(8,128)(2,1)S(1)} %get-tuple-element.63), channel_id=1, source_target_pairs={{0,6},{1,7},{2,0},{3,1},{4,2},{5,3},{6,4},{7,5},{8,14},{9,15},{10,... | collective-permute-start | bytes 24584 | tf_op jit(solution)/shard_map/ppermute | solution.py:34
  67.7 6.5 %collective-permute-start.14 = (bf16[32,128]{1,0:T(8,128)(2,1)S(1)}, bf16[32,128]{1,0:T(8,128)(2,1)S(1)}, u32[]{:S(2)}, u32[]{:S(2)}) collective-permute-start(bf16[32,128]{1,0:T(8,128)(2,1)S(1)} %get-tuple-element.64), channel_id=1, source_target_pairs={{0,7},{1,6},{2,1},{3,0},{4,3},{5,2},{6,5},{7,4},{8,15},{9,14},{10,... | collective-permute-start | bytes 24584 | tf_op jit(solution)/shard_map/ppermute | solution.py:34
  76.9 6.4 %collective-permute-start.19 = (bf16[64,2048]{1,0:T(8,128)(2,1)S(1)}, bf16[64,2048]{1,0:T(8,128)(2,1)S(1)}, u32[]{:S(2)}, u32[]{:S(2)}) collective-permute-start(bf16[64,2048]{1,0:T(8,128)(2,1)S(1)} %get-tuple-element.72), channel_id=1, source_target_pairs={{0,1},{1,0},{2,3},{3,2},{4,5},{5,4},{6,7},{7,6},{8,9},{9,8},{10,11... | collective-permute-start | bytes 786440 | tf_op jit(solution)/shard_map/ppermute | solution.py:34
  78.4 10.1 %collective-permute-start.15 = (bf16[64,2048]{1,0:T(8,128)(2,1)S(1)}, bf16[64,2048]{1,0:T(8,128)(2,1)S(1)}, u32[]{:S(2)}, u32[]{:S(2)}) collective-permute-start(bf16[64,2048]{1,0:T(8,128)(2,1)S(1)} %get-tuple-element.70), channel_id=1, source_target_pairs={{0,1},{1,0},{2,3},{3,2},{4,5},{5,4},{6,7},{7,6},{8,9},{9,8},{10,11... | collective-permute-start | bytes 786440 | tf_op jit(solution)/shard_map/ppermute | solution.py:34
  83.4 6.0 %collective-permute-start.20 = (bf16[16,2048]{1,0:T(8,128)(2,1)S(1)}, bf16[16,2048]{1,0:T(8,128)(2,1)S(1)}, u32[]{:S(2)}, u32[]{:S(2)}) collective-permute-start(bf16[16,2048]{1,0:T(8,128)(2,1)S(1)} %get-tuple-element.101), channel_id=1, source_target_pairs={{0,4},{1,5},{2,6},{3,7},{4,0},{5,1},{6,2},{7,3},{8,12},{9,13},{10,... | collective-permute-start | bytes 196616 | tf_op jit(solution)/shard_map/ppermute | solution.py:34
  84.8 7.9 %collective-permute-start.21 = (bf16[16,2048]{1,0:T(8,128)(2,1)S(1)}, bf16[16,2048]{1,0:T(8,128)(2,1)S(1)}, u32[]{:S(2)}, u32[]{:S(2)}) collective-permute-start(bf16[16,2048]{1,0:T(8,128)(2,1)S(1)} %get-tuple-element.103), channel_id=1, source_target_pairs={{0,2},{1,3},{2,4},{3,5},{4,6},{5,7},{6,0},{7,1},{8,10},{9,11},{10,... | collective-permute-start | bytes 196616 | tf_op jit(solution)/shard_map/ppermute | solution.py:34
  86.0 6.7 %collective-permute-start.22 = (bf16[16,2048]{1,0:T(8,128)(2,1)S(1)}, bf16[16,2048]{1,0:T(8,128)(2,1)S(1)}, u32[]{:S(2)}, u32[]{:S(2)}) collective-permute-start(bf16[16,2048]{1,0:T(8,128)(2,1)S(1)} %get-tuple-element.102), channel_id=1, source_target_pairs={{0,6},{1,7},{2,0},{3,1},{4,2},{5,3},{6,4},{7,5},{8,14},{9,15},{10,... | collective-permute-start | bytes 196616 | tf_op jit(solution)/shard_map/ppermute | solution.py:34
  88.7 7.7 %collective-permute-start.16 = (bf16[16,2048]{1,0:T(8,128)(2,1)S(1)}, bf16[16,2048]{1,0:T(8,128)(2,1)S(1)}, u32[]{:S(2)}, u32[]{:S(2)}) collective-permute-start(bf16[16,2048]{1,0:T(8,128)(2,1)S(1)} %get-tuple-element.98), channel_id=1, source_target_pairs={{0,4},{1,5},{2,6},{3,7},{4,0},{5,1},{6,2},{7,3},{8,12},{9,13},{10,... | collective-permute-start | bytes 196616 | tf_op jit(solution)/shard_map/ppermute | solution.py:34
  88.8 7.6 %collective-permute-start.17 = (bf16[16,2048]{1,0:T(8,128)(2,1)S(1)}, bf16[16,2048]{1,0:T(8,128)(2,1)S(1)}, u32[]{:S(2)}, u32[]{:S(2)}) collective-permute-start(bf16[16,2048]{1,0:T(8,128)(2,1)S(1)} %get-tuple-element.100), channel_id=1, source_target_pairs={{0,2},{1,3},{2,4},{3,5},{4,6},{5,7},{6,0},{7,1},{8,10},{9,11},{10,... | collective-permute-start | bytes 196616 | tf_op jit(solution)/shard_map/ppermute | solution.py:34
  89.4 7.5 %collective-permute-start.18 = (bf16[16,2048]{1,0:T(8,128)(2,1)S(1)}, bf16[16,2048]{1,0:T(8,128)(2,1)S(1)}, u32[]{:S(2)}, u32[]{:S(2)}) collective-permute-start(bf16[16,2048]{1,0:T(8,128)(2,1)S(1)} %get-tuple-element.99), channel_id=1, source_target_pairs={{0,6},{1,7},{2,0},{3,1},{4,2},{5,3},{6,4},{7,5},{8,14},{9,15},{10,... | collective-permute-start | bytes 196616 | tf_op jit(solution)/shard_map/ppermute | solution.py:34
  97.0 8.1 %collective-permute-start.27 = (bf16[16,2048]{1,0:T(8,128)(2,1)S(1)}, bf16[16,2048]{1,0:T(8,128)(2,1)S(1)}, u32[]{:S(2)}, u32[]{:S(2)}) collective-permute-start(bf16[16,2048]{1,0:T(8,128)(2,1)S(1)} %get-tuple-element.85.refs_0_), channel_id=1, source_target_pairs={{0,2},{1,3},{2,4},{3,5},{4,6},{5,7},{6,0},{7,1},{8,10},{9,11},{10,... | collective-permute-start | bytes 196616 | tf_op jit(solution)/shard_map/ppermute | solution.py:34
  98.4 7.8 %collective-permute-start.28 = (bf16[16,2048]{1,0:T(8,128)(2,1)S(1)}, bf16[16,2048]{1,0:T(8,128)(2,1)S(1)}, u32[]{:S(2)}, u32[]{:S(2)}) collective-permute-start(bf16[16,2048]{1,0:T(8,128)(2,1)S(1)} %get-tuple-element.85.refs_0_), channel_id=1, source_target_pairs={{0,4},{1,5},{2,6},{3,7},{4,0},{5,1},{6,2},{7,3},{8,12},{9,13},{10,... | collective-permute-start | bytes 196616 | tf_op jit(solution)/shard_map/ppermute | solution.py:34
  99.5 6.7 %collective-permute-start.29 = (bf16[16,2048]{1,0:T(8,128)(2,1)S(1)}, bf16[16,2048]{1,0:T(8,128)(2,1)S(1)}, u32[]{:S(2)}, u32[]{:S(2)}) collective-permute-start(bf16[16,2048]{1,0:T(8,128)(2,1)S(1)} %get-tuple-element.85.refs_0_), channel_id=1, source_target_pairs={{0,6},{1,7},{2,0},{3,1},{4,2},{5,3},{6,4},{7,5},{8,14},{9,15},{10,... | collective-permute-start | bytes 196616 | tf_op jit(solution)/shard_map/ppermute | solution.py:34
  106.3 10.6 %collective-permute-start.30 = (bf16[64,2048]{1,0:T(8,128)(2,1)S(1)}, bf16[64,2048]{1,0:T(8,128)(2,1)S(1)}, u32[]{:S(2)}, u32[]{:S(2)}) collective-permute-start(bf16[64,2048]{1,0:T(8,128)(2,1)S(1)} %shard_map.150.refs_0_), channel_id=1, source_target_pairs={{0,1},{1,0},{2,3},{3,2},{4,5},{5,4},{6,7},{7,6},{8,9},{9,8},{10,11... | collective-permute-start | bytes 786440 | tf_op jit(solution)/shard_map/ppermute | solution.py:34
  107.5 6.2 %collective-permute-start.23 = (bf16[16,2176]{1,0:T(8,128)(2,1)S(1)}, bf16[16,2176]{1,0:T(8,128)(2,1)S(1)}, u32[]{:S(2)}, u32[]{:S(2)}) collective-permute-start(bf16[16,2176]{1,0:T(8,128)(2,1)S(1)} %shard_map.147.refs_0_), channel_id=1, source_target_pairs={{0,2},{1,3},{2,4},{3,5},{4,6},{5,7},{6,0},{7,1},{8,10},{9,11},{10,... | collective-permute-start | bytes 208904 | tf_op jit(solution)/shard_map/ppermute | solution.py:34
  115.9 9.6 %collective-permute-start.26 = (bf16[64,2176]{1,0:T(8,128)(2,1)S(1)}, bf16[64,2176]{1,0:T(8,128)(2,1)S(1)}, u32[]{:S(2)}, u32[]{:S(2)}) collective-permute-start(bf16[64,2176]{1,0:T(8,128)(2,1)S(1)} %shard_map.148.refs_0_), channel_id=1, source_target_pairs={{0,1},{1,0},{2,3},{3,2},{4,5},{5,4},{6,7},{7,6},{8,9},{9,8},{10,11... | collective-permute-start | bytes 835592 | tf_op jit(solution)/shard_map/ppermute | solution.py:34
  128.1 6.4 %collective-permute-start.31 = (bf16[32,4096]{1,0:T(8,128)(2,1)S(1)}, bf16[32,4096]{1,0:T(8,128)(2,1)S(1)}, u32[]{:S(2)}, u32[]{:S(2)}) collective-permute-start(bf16[32,4096]{1,0:T(8,128)(2,1)S(1)} %get-tuple-element.80), channel_id=1, source_target_pairs={{0,1},{1,0},{2,3},{3,2},{4,5},{5,4},{6,7},{7,6},{8,9},{9,8},{10,11... | collective-permute-start | bytes 786440 | tf_op jit(solution)/shard_map/ppermute | solution.py:34
  128.9 8.6 %collective-permute-start.34 = (bf16[32,4096]{1,0:T(8,128)(2,1)S(1)}, bf16[32,4096]{1,0:T(8,128)(2,1)S(1)}, u32[]{:S(2)}, u32[]{:S(2)}) collective-permute-start(bf16[32,4096]{1,0:T(8,128)(2,1)S(1)} %get-tuple-element.83), channel_id=1, source_target_pairs={{0,1},{1,0},{2,3},{3,2},{4,5},{5,4},{6,7},{7,6},{8,9},{9,8},{10,11... | collective-permute-start | bytes 786440 | tf_op jit(solution)/shard_map/ppermute | solution.py:34
  134.6 8.1 %collective-permute-start.32 = (bf16[16,4096]{1,0:T(8,128)(2,1)S(1)}, bf16[16,4096]{1,0:T(8,128)(2,1)S(1)}, u32[]{:S(2)}, u32[]{:S(2)}) collective-permute-start(bf16[16,4096]{1,0:T(8,128)(2,1)S(1)} %get-tuple-element.94), channel_id=1, source_target_pairs={{0,4},{1,5},{2,6},{3,7},{4,0},{5,1},{6,2},{7,3},{8,12},{9,13},{10,... | collective-permute-start | bytes 393224 | tf_op jit(solution)/shard_map/ppermute | solution.py:34
  135.3 7.5 %collective-permute-start.33 = (bf16[16,4096]{1,0:T(8,128)(2,1)S(1)}, bf16[16,4096]{1,0:T(8,128)(2,1)S(1)}, u32[]{:S(2)}, u32[]{:S(2)}) collective-permute-start(bf16[16,4096]{1,0:T(8,128)(2,1)S(1)} %get-tuple-element.95), channel_id=1, source_target_pairs={{0,2},{1,3},{2,4},{3,5},{4,6},{5,7},{6,0},{7,1},{8,10},{9,11},{10,... | collective-permute-start | bytes 393224 | tf_op jit(solution)/shard_map/ppermute | solution.py:34
  137.5 6.6 %collective-permute-start.35 = (bf16[16,4096]{1,0:T(8,128)(2,1)S(1)}, bf16[16,4096]{1,0:T(8,128)(2,1)S(1)}, u32[]{:S(2)}, u32[]{:S(2)}) collective-permute-start(bf16[16,4096]{1,0:T(8,128)(2,1)S(1)} %add_convert_fusion), channel_id=1, source_target_pairs={{0,6},{1,7},{2,0},{3,1},{4,2},{5,3},{6,4},{7,5},{8,14},{9,15},{10,... | collective-permute-start | bytes 393224 | tf_op jit(solution)/shard_map/ppermute | solution.py:34
  (29 other events, 326.9 us)

commit v5 on v3

--- a/solution.py
+++ b/solution.py
@@ -34,16 +34,43 @@
     return lax.ppermute(block, "ctx", pairs)
 
 
-def gather_blocks(block, tall, wide, relay=False):
+def tie_body(count, *refs):
+    total = refs[0][...]
+    for ref in refs[1:count]:
+        total = total + ref[...]
+    refs[-1][...] = total
+
+
+def tie(blocks, tokens):
+    return kernel_call(
+        functools.partial(tie_body, len(blocks)),
+        [(blocks[0].shape, blocks[0].dtype)],
+        [*blocks, *tokens],
+        specs=[VMEM] * len(blocks) + [pl.BlockSpec(memory_space=pl.ANY)] * len(tokens),
+    )[0]
+
+
+def gather_rows(block, tall, wide, tokens_1, tokens_2):
     blocks = {(0, 0): block}
     for dz in range(1, tall):
-        if not (relay and tall == 4 and dz == 2):
+        if tall != 4 or dz != 2:
             blocks[dz, 0] = shift(block, tall, wide, dz, 0)
-    if relay and tall == 4:
+    blocks[1, 0] = tie([blocks[1, 0]], tokens_1)
+    if tall == 4:
         up = shift(blocks[1, 0], tall, wide, 1, 0, lambda z: z in (1, 2))
         down = shift(blocks[3, 0], tall, wide, -1, 0, lambda z: z in (1, 2))
-        blocks[2, 0] = up + down
+        blocks[2, 0] = tie([up, down], tokens_2)
+    else:
+        blocks[tall - 1, 0] = tie([blocks[tall - 1, 0]], tokens_2)
     for dz in [0, 1, *range(tall - 1, 1, -1)]:
+        for dy in range(1, wide):
+            blocks[dz, dy] = shift(blocks[dz, 0], tall, wide, 0, dy)
+    return [blocks[dz, dy] for dz in range(tall) for dy in range(wide)]
+
+
+def gather_blocks(block, tall, wide):
+    blocks = {(dz, 0): shift(block, tall, wide, dz, 0) if dz else block for dz in range(tall)}
+    for dz in range(tall):
         for dy in range(1, wide):
             blocks[dz, dy] = shift(blocks[dz, 0], tall, wide, 0, dy)
     return [blocks[dz, dy] for dz in range(tall) for dy in range(wide)]
@@ -76,9 +103,11 @@
                 out[place * share : (place + 1) * share, span] = rows(dz, dy)
 
 
-def scatter_sum(parts, tall, wide):
+def scatter_sum(parts, tall, wide, tokens=()):
     share = parts[0].shape[0]
     crossed = [shift(p, tall, wide, 0, i // 2 + 1) for i, p in enumerate(parts[tall:])]
+    if tokens:
+        crossed[1] = tie([crossed[1]], tokens)
     total = None
     for which, group in enumerate(sum_order(tall)):
         for place, dz in enumerate(group):
@@ -198,7 +227,8 @@
     place += jnp.sum(jnp.where(mine, rank, 0.0), axis=0, keepdims=True)
     placed = place == iota((total, total), 0)
     in_order[...] = jnp.where(placed, 1.0, 0.0).astype(bf16)
-    positions[...] = jnp.sum(jnp.where(placed, where, 0.0), axis=1, keepdims=True)
+    at = jnp.sum(jnp.where(placed, where, 0.0), axis=1, keepdims=True)
+    positions[...] = jnp.broadcast_to(at, positions.shape)
     slot_at = jnp.sum(jnp.where(placed, slot, 0.0), axis=1, keepdims=True)
     pick_rows[...] = jnp.where(slot_at == iota(pick_rows.shape, 1), 1.0, 0.0).astype(bf16)
     columns[...] = jnp.where(out_base == iota(columns.shape, 1), 1.0, 0.0).astype(bf16)
@@ -253,7 +283,7 @@
     heads = query.shape[1] // HEAD_DIM
     mixed = jnp.concatenate([a[...].astype(f32) for a in arrived], axis=0).astype(bf16)
     both = dot(unmix[...], mixed)
-    allowed = key_pos[...].astype(f32) <= query_pos[...]
+    allowed = key_pos[...].astype(f32) <= query_pos[:, 0:1]
     for group in range(kv_local):
         base = group * HEAD_DIM
         first, second = both[base : base + half], both[base + half : base + HEAD_DIM]
@@ -338,16 +368,12 @@
         specs=[scalar, VMEM, VMEM],
         flops=2 * capacity * tokens * model,
     )
-    blocks = gather_blocks(outgoing, tall, wide, relay=True)
-    attn_gain, w_key, w_value, w_query, _ = load(
+    attn_gain, w_key, w_value, w_query, token_1 = load(
         outgoing, attn_gain.reshape(1, model), w_key, w_value, w_query
     )
-    near = blocks[wide]
-    w_output, *tokens_1 = load(near, w_output)
-    w_gate, *tokens_2 = load(near, w_gate)
-    w_up, *tokens_3 = load(near, w_up)
-    w_down, *tokens_4 = load(near, w_down)
-    loaded = tokens_1 + tokens_2 + tokens_3 + tokens_4
+    w_gate, token_2 = load(outgoing, w_gate)
+    w_output, token_3 = load(token_2, w_output)
+    w_up, token_4 = load(token_3, w_up)
 
     each = kv_local * 2 * depth
     notes = np.zeros((max(count * each, 2 * kv_local * HEAD_DIM), 4), np.float32)
@@ -366,11 +392,12 @@
             ((total, total), bf16),
             ((count * each, 2 * key_cols), bf16),
             ((2 * kv_local * HEAD_DIM, count * each), bf16),
-            ((total, 1), f32),
+            ((total, HEAD_DIM // 2), f32),
         ],
         [me, routed, balance, notes],
         specs=[scalar, VMEM, VMEM, VMEM],
     )
+    blocks = gather_rows(outgoing, tall, wide, [token_1, token_2, positions], [token_3, token_4])
 
     half = HEAD_DIM // 2
     steps_f = jnp.arange(half, dtype=f32)
@@ -385,7 +412,7 @@
     normed, own, *sent = kernel_call(
         functools.partial(kv_body, count),
         [((total, model), bf16), ((share, model), bf16)] + [((each, total), bf16)] * count,
-        [*blocks, pick_rows, in_order, columns, attn_gain, w_key, w_value, *loaded],
+        [*blocks, pick_rows, in_order, columns, attn_gain, w_key, w_value],
         [pltpu.VMEM((total, model), bf16)],
         flops=2 * total * model * 512,
     )
@@ -406,7 +433,8 @@
         [pltpu.VMEM((total, local_heads * HEAD_DIM), bf16)],
         flops=2 * total * model * local_heads * HEAD_DIM,
     )
-    attn_own = scatter_sum(attn_parts, tall, wide)
+    w_down, token_5 = load(attn_parts[0], w_down)
+    attn_own = scatter_sum(attn_parts, tall, wide, [token_5])
     own_rows = own.astype(f32)
     hidden = own_rows + attn_own
     mean_sq = jnp.mean(hidden * hidden, axis=-1, keepdims=True)

time: 128 us -> 125 us (0.977)
  waiting for transfers between devices: 55.1 us -> 52.5 us
  starting transfers between devices: 42.1 us -> 43.8 us
  local copies, waits for them, and re-layouts: 3.45 us -> 1.92 us
    ppermute x32, waiting for transfers between devices: 55.1 us -> 52.5 us  [shift(): return lax.ppermute(block, 'ctx', pairs)]
    ppermute x32, starting transfers between devices: 42.1 us -> 43.8 us  [shift(): return lax.ppermute(block, 'ctx', pairs)]
    unnamed x14, local copies, waits for them, and re-layouts: 3.45 us -> 1.92 us
    pallas_call x6 -> x9, Pallas kernels: 9.24 us -> 9.4 us  [kernel_call(): pl.pallas_call(body, out_shape=[jax.ShapeDtypeStruct(s, d) for s, d in ou...]
  transfers between devices with their start and end apart: 32 -> 32, of which waited for: 17 -> 19; matrix products, arithmetic and copies ran while one was open for 1% -> 1% of each run, Pallas kernels for 14% -> 14%
where the time goes in v5:
time: 125 us
  waiting for transfers between devices  52.5 us (42%)
  starting transfers between devices  43.8 us (35%)
  Pallas kernels  24.7 us (20%)
  local copies, waits for them, and re-layouts  1.92 us (2%)
  other arithmetic  1.9 us (2%)
    ppermute x32, waiting for transfers between devices, shift(): return lax.ppermute(block, 'ctx', pairs)  52.5 us
    ppermute x32, starting transfers between devices, shift(): return lax.ppermute(block, 'ctx', pairs)  43.8 us
    pallas_call x5, Pallas kernels, load(): pl.pallas_call(functools.partial(load_body, len(arrays)), out_shape=[pltp...  15.3 us
    pallas_call x9, Pallas kernels, kernel_call(): pl.pallas_call(body, out_shape=[jax.ShapeDtypeStruct(s, d) for s, d in ou...  9.4 us
  transfers between devices with their start and end apart: 32, of which 19 were waited for; matrix products, arithmetic and copies ran while one was open for 1% of the time, Pallas kernels for 14%

profile of v5, /device:TPU:0, one launch (start us, length us, event | category | flops | bytes accessed | tf_op | source)
XLA Modules:
  0.0 125.0 jit_solution(1452472238952801133)
XLA Ops:
  2.3 3.1 %collective-permute-start.1 = (bf16[32,4096]{1,0:T(8,128)(2,1)S(1)}, bf16[32,4096]{1,0:T(8,128)(2,1)S(1)}, u32[]{:S(2)}, u32[]{:S(2)}) collective-permute-start(bf16[32,4096]{1,0:T(8,128)(2,1)S(1)} %shard_map.136.refs_0_), channel_id=1, source_target_pairs={{0,2},{1,3},{2,4},{3,5},{4,6},{5,7},{6,0},{7,1},{8,10},{9,11},{10,... | collective-permute-start | bytes 786440 | tf_op jit(solution)/shard_map/ppermute | solution.py:34
  5.4 2.1 %collective-permute-start.4 = (bf16[32,4096]{1,0:T(8,128)(2,1)S(1)}, bf16[32,4096]{1,0:T(8,128)(2,1)S(1)}, u32[]{:S(2)}, u32[]{:S(2)}) collective-permute-start(bf16[32,4096]{1,0:T(8,128)(2,1)S(1)} %shard_map.136.refs_0_), channel_id=1, source_target_pairs={{0,6},{1,7},{2,0},{3,1},{4,2},{5,3},{6,4},{7,5},{8,14},{9,15},{10,... | collective-permute-start | bytes 786440 | tf_op jit(solution)/shard_map/ppermute | solution.py:34
  7.5 3.4 %shard_map.138 = (bf16[4096,1024]{1,0:T(8,128)(2,1)S(1)}, f32[8,128]{1,0:T(8,128)S(1)}) custom-call(bf16[32,4096]{1,0:T(8,128)(2,1)S(1)} %shard_map.136.refs_0_, bf16[4096,1024]{1,0:T(8,128)(2,1)} %refs_1_.4), custom_call_target="tpu_custom_call" | custom-call | bytes 16777216 | tf_op jit(solution)/shard_map/pallas_call | solution.py:158
  11.8 2.9 %shard_map.137 = (f32[1,4096]{1,0:T(1,128)S(1)}, bf16[4096,128]{1,0:T(8,128)(2,1)S(1)}, bf16[4096,128]{1,0:T(8,128)(2,1)S(1)}, bf16[4096,512]{1,0:T(8,128)(2,1)S(1)}, f32[8,128]{1,0:T(8,128)S(1)}) custom-call(bf16[32,4096]{1,0:T(8,128)(2,1)S(1)} %shard_map.136.refs_0_, f32[1,4096]{1,0:T(1,128)} %bitcast.8, bf16[4096,128]{1,0:T(8,128)(2,1)} %refs_2_.1, ...), custom_call_target="tpu_custom_call" | custom-call | bytes 12615680 | tf_op jit(solution)/shard_map/pallas_call | solution.py:158
  15.4 3.4 %collective-permute-done.4.refs_6_ = bf16[32,4096]{1,0:T(8,128)(2,1)S(1)} collective-permute-done((bf16[32,4096]{1,0:T(8,128)(2,1)S(1)}, bf16[32,4096]{1,0:T(8,128)(2,1)S(1)}, u32[]{:S(2)}, u32[]{:S(2)}) %collective-permute-start.4) | collective-permute-done | bytes 262176 | tf_op jit(solution)/shard_map/ppermute | solution.py:34
  20.1 1.6 %collective-permute-start = (bf16[32,4096]{1,0:T(8,128)(2,1)S(1)}, bf16[32,4096]{1,0:T(8,128)(2,1)S(1)}, u32[]{:S(2)}, u32[]{:S(2)}) collective-permute-start(bf16[32,4096]{1,0:T(8,128)(2,1)S(1)} %shard_map.136.refs_0_), channel_id=1, source_target_pairs={{0,1},{1,0},{2,3},{3,2},{4,5},{5,4},{6,7},{7,6},{8,9},{9,8},{10,11... | collective-permute-start | bytes 786440 | tf_op jit(solution)/shard_map/ppermute | solution.py:34
  21.6 2.2 %shard_map.141 = (bf16[512,4096]{1,0:T(8,128)(2,1)S(1)}, f32[8,128]{1,0:T(8,128)S(1)}) custom-call(f32[8,128]{1,0:T(8,128)S(1)} %get-tuple-element.46.refs_2_.refs_0_, bf16[512,4096]{1,0:T(8,128)(2,1)} %refs_1_.5), custom_call_target="tpu_custom_call" | custom-call | bytes 8388608 | tf_op jit(solution)/shard_map/pallas_call | solution.py:158
  23.9 3.4 %shard_map.142 = (bf16[4096,1024]{1,0:T(8,128)(2,1)S(1)}, f32[8,128]{1,0:T(8,128)S(1)}) custom-call(f32[8,128]{1,0:T(8,128)S(1)} %get-tuple-element.48.refs_0_.refs_2_, bf16[4096,1024]{1,0:T(8,128)(2,1)} %refs_1_.6), custom_call_target="tpu_custom_call" | custom-call | bytes 16777216 | tf_op jit(solution)/shard_map/pallas_call | solution.py:158
  27.9 1.5 %collective-permute-start.7 = (bf16[32,4096]{1,0:T(8,128)(2,1)S(1)}, bf16[32,4096]{1,0:T(8,128)(2,1)S(1)}, u32[]{:S(2)}, u32[]{:S(2)}) collective-permute-start(bf16[32,4096]{1,0:T(8,128)(2,1)S(1)} %collective-permute-done.4.refs_6_), channel_id=1, source_target_pairs={{0,1},{1,0},{2,3},{3,2},{4,5},{5,4},{6,7},{7,6},{8,9},{9,8},{10,11... | collective-permute-start | bytes 786440 | tf_op jit(solution)/shard_map/ppermute | solution.py:34
  30.9 5.7 %collective-permute-done.2.refs_3_ = bf16[32,4096]{1,0:T(8,128)(2,1)S(1)} collective-permute-done((bf16[32,4096]{1,0:T(8,128)(2,1)S(1)}, bf16[32,4096]{1,0:T(8,128)(2,1)S(1)}, u32[]{:S(2)}, u32[]{:S(2)}) %collective-permute-start.2) | collective-permute-done | bytes 262176 | tf_op jit(solution)/shard_map/ppermute | solution.py:34
  36.6 5.6 %collective-permute-done.7.refs_7_ = bf16[32,4096]{1,0:T(8,128)(2,1)S(1)} collective-permute-done((bf16[32,4096]{1,0:T(8,128)(2,1)S(1)}, bf16[32,4096]{1,0:T(8,128)(2,1)S(1)}, u32[]{:S(2)}, u32[]{:S(2)}) %collective-permute-start.7) | collective-permute-done | bytes 262176 | tf_op jit(solution)/shard_map/ppermute | solution.py:34
  42.2 3.7 %collective-permute-done.6.refs_5_ = bf16[32,4096]{1,0:T(8,128)(2,1)S(1)} collective-permute-done((bf16[32,4096]{1,0:T(8,128)(2,1)S(1)}, bf16[32,4096]{1,0:T(8,128)(2,1)S(1)}, u32[]{:S(2)}, u32[]{:S(2)}) %collective-permute-start.6) | collective-permute-done | bytes 262176 | tf_op jit(solution)/shard_map/ppermute | solution.py:34
  45.9 1.8 %shard_map.144 = (bf16[128,4096]{1,0:T(8,128)(2,1)S(1)}, bf16[16,4096]{1,0:T(8,128)(2,1)S(1)}, bf16[32,128]{1,0:T(8,128)(2,1)S(1)}, bf16[32,128]{1,0:T(8,128)(2,...) custom-call(bf16[32,4096]{1,0:T(8,128)(2,1)S(1)} %shard_map.136.refs, ...), custom_call_target="tpu_custom_call" | custom-call | flops 536870912 | bytes 1048576 | tf_op jit(solution)/shard_map/pallas_call | solution.py:133
  47.7 2.9 %collective-permute-start.10 = (bf16[32,128]{1,0:T(8,128)(2,1)S(1)}, bf16[32,128]{1,0:T(8,128)(2,1)S(1)}, u32[]{:S(2)}, u32[]{:S(2)}) collective-permute-start(bf16[32,128]{1,0:T(8,128)(2,1)S(1)} %get-tuple-element.60), channel_id=1, source_target_pairs={{0,3},{1,2},{2,5},{3,4},{4,7},{5,6},{6,1},{7,0},{8,11},{9,10},{10,... | collective-permute-start | bytes 24584 | tf_op jit(solution)/shard_map/ppermute | solution.py:34
  51.5 2.6 %collective-permute-start.12 = (bf16[32,128]{1,0:T(8,128)(2,1)S(1)}, bf16[32,128]{1,0:T(8,128)(2,1)S(1)}, u32[]{:S(2)}, u32[]{:S(2)}) collective-permute-start(bf16[32,128]{1,0:T(8,128)(2,1)S(1)} %get-tuple-element.62), channel_id=1, source_target_pairs={{0,5},{1,4},{2,7},{3,6},{4,1},{5,0},{6,3},{7,2},{8,13},{9,12},{10,... | collective-permute-start | bytes 24584 | tf_op jit(solution)/shard_map/ppermute | solution.py:34
  60.5 3.1 %collective-permute-done.9.refs_2_ = bf16[32,128]{1,0:T(8,128)(2,1)S(1)} collective-permute-done((bf16[32,128]{1,0:T(8,128)(2,1)S(1)}, bf16[32,128]{1,0:T(8,128)(2,1)S(1)}, u32[]{:S(2)}, u32[]{:S(2)}) %collective-permute-start.9) | collective-permute-done | bytes 8224 | tf_op jit(solution)/shard_map/ppermute | solution.py:34
  63.6 1.7 %shard_map.146 = (bf16[16,4096]{1,0:T(8,128)(2,1)S(1)}, bf16[16,4096]{1,0:T(8,128)(2,1)S(1)}, bf16[16,4096]{1,0:T(8,128)(2,1)S(1)}, bf16[16,4096]{1,0:T(8,128)(2...) custom-call(bf16[32,128]{1,0:T(8,128)(2,1)S(1)} %get-tuple-element.57.refs_0_, ...), custom_call_target="tpu_custom_call" | custom-call | flops 536870912 | bytes 1048576 | tf_op jit(solution)/shard_map/pallas_call | solution.py:133
  67.4 3.4 %shard_map.147 = (bf16[1024,4096]{1,0:T(8,128)(2,1)S(1)}, f32[8,128]{1,0:T(8,128)S(1)}) custom-call(bf16[16,4096]{1,0:T(8,128)(2,1)S(1)} %get-tuple-element.74.refs_0_, bf16[1024,4096]{1,0:T(8,128)(2,1)} %refs_1_.7), custom_call_target="tpu_custom_call" | custom-call | bytes 16777216 | tf_op jit(solution)/shard_map/pallas_call | solution.py:158
  72.8 1.8 %collective-permute-done.18.refs_0_ = bf16[32,4096]{1,0:T(8,128)(2,1)S(1)} collective-permute-done((bf16[32,4096]{1,0:T(8,128)(2,1)S(1)}, bf16[32,4096]{1,0:T(8,128)(2,1)S(1)}, u32[]{:S(2)}, u32[]{:S(2)}) %collective-permute-start.18) | collective-permute-done | bytes 262176 | tf_op jit(solution)/shard_map/ppermute | solution.py:34
  75.9 5.0 %collective-permute-done.16 = bf16[16,4096]{1,0:T(8,128)(2,1)S(1)} collective-permute-done((bf16[16,4096]{1,0:T(8,128)(2,1)S(1)}, bf16[16,4096]{1,0:T(8,128)(2,1)S(1)}, u32[]{:S(2)}, u32[]{:S(2)}) %collective-permute-start.16) | collective-permute-done | bytes 131104 | tf_op jit(solution)/shard_map/ppermute | solution.py:34
  80.9 4.0 %collective-permute-done.19 = bf16[16,4096]{1,0:T(8,128)(2,1)S(1)} collective-permute-done((bf16[16,4096]{1,0:T(8,128)(2,1)S(1)}, bf16[16,4096]{1,0:T(8,128)(2,1)S(1)}, u32[]{:S(2)}, u32[]{:S(2)}) %collective-permute-start.19) | collective-permute-done | bytes 131104 | tf_op jit(solution)/shard_map/ppermute | solution.py:34
  86.8 2.8 %collective-permute-start.25 = (bf16[16,4096]{1,0:T(8,128)(2,1)S(1)}, bf16[16,4096]{1,0:T(8,128)(2,1)S(1)}, u32[]{:S(2)}, u32[]{:S(2)}) collective-permute-start(bf16[16,4096]{1,0:T(8,128)(2,1)S(1)} %multiply_convert_fusion.refs_0_), channel_id=1, source_target_pairs={{0,6},{1,7},{2,0},{3,1},{4,2},{5,3},{6,4},{7,5},{8,14},{9,15},{10,... | collective-permute-start | bytes 393224 | tf_op jit(solution)/shard_map/ppermute | solution.py:34
  89.6 2.0 %collective-permute-start.20 = (bf16[16,4096]{1,0:T(8,128)(2,1)S(1)}, bf16[16,4096]{1,0:T(8,128)(2,1)S(1)}, u32[]{:S(2)}, u32[]{:S(2)}) collective-permute-start(bf16[16,4096]{1,0:T(8,128)(2,1)S(1)} %multiply_convert_fusion.refs_0_), channel_id=1, source_target_pairs={{0,1},{1,0},{2,3},{3,2},{4,5},{5,4},{6,7},{7,6},{8,9},{9,8},{10,11... | collective-permute-start | bytes 393224 | tf_op jit(solution)/shard_map/ppermute | solution.py:34
  93.1 1.9 %collective-permute-done.23.refs_4_ = bf16[16,4096]{1,0:T(8,128)(2,1)S(1)} collective-permute-done((bf16[16,4096]{1,0:T(8,128)(2,1)S(1)}, bf16[16,4096]{1,0:T(8,128)(2,1)S(1)}, u32[]{:S(2)}, u32[]{:S(2)}) %collective-permute-start.23) | collective-permute-done | bytes 131104 | tf_op jit(solution)/shard_map/ppermute | solution.py:34
  97.0 1.7 %collective-permute-done.22.refs_3_ = bf16[16,4096]{1,0:T(8,128)(2,1)S(1)} collective-permute-done((bf16[16,4096]{1,0:T(8,128)(2,1)S(1)}, bf16[16,4096]{1,0:T(8,128)(2,1)S(1)}, u32[]{:S(2)}, u32[]{:S(2)}) %collective-permute-start.22) | collective-permute-done | bytes 131104 | tf_op jit(solution)/shard_map/ppermute | solution.py:34
  98.7 2.8 %collective-permute-done.24.refs_5_ = bf16[16,4096]{1,0:T(8,128)(2,1)S(1)} collective-permute-done((bf16[16,4096]{1,0:T(8,128)(2,1)S(1)}, bf16[16,4096]{1,0:T(8,128)(2,1)S(1)}, u32[]{:S(2)}, u32[]{:S(2)}) %collective-permute-start.24) | collective-permute-done | bytes 131104 | tf_op jit(solution)/shard_map/ppermute | solution.py:34
  101.5 2.8 %collective-permute-done.26.refs_7_ = bf16[16,4096]{1,0:T(8,128)(2,1)S(1)} collective-permute-done((bf16[16,4096]{1,0:T(8,128)(2,1)S(1)}, bf16[16,4096]{1,0:T(8,128)(2,1)S(1)}, u32[]{:S(2)}, u32[]{:S(2)}) %collective-permute-start.26) | collective-permute-done | bytes 131104 | tf_op jit(solution)/shard_map/ppermute | solution.py:34
  104.3 3.7 %shard_map.149 = (bf16[16,4096]{1,0:T(8,128)(2,1)S(1)}, bf16[16,4096]{1,0:T(8,128)(2,1)S(1)}, bf16[16,4096]{1,0:T(8,128)(2,1)S(1)}, bf16[16,4096]{1,0:T(8,128)(2...) custom-call(bf16[16,4096]{1,0:T(8,128)(2,1)S(1)} %multiply_convert_fusion.refs_0_, ...), custom_call_target="tpu_custom_call" | custom-call | flops 3221225472 | bytes 1048576 | tf_op jit(solution)/shard_map/pallas_call | solution.py:133
  110.1 4.3 %collective-permute-done.27 = bf16[32,4096]{1,0:T(8,128)(2,1)S(1)} collective-permute-done((bf16[32,4096]{1,0:T(8,128)(2,1)S(1)}, bf16[32,4096]{1,0:T(8,128)(2,1)S(1)}, u32[]{:S(2)}, u32[]{:S(2)}) %collective-permute-start.27) | collective-permute-done | bytes 262176 | tf_op jit(solution)/shard_map/ppermute | solution.py:34
  115.2 2.4 %collective-permute-start.29 = (bf16[16,4096]{1,0:T(8,128)(2,1)S(1)}, bf16[16,4096]{1,0:T(8,128)(2,1)S(1)}, u32[]{:S(2)}, u32[]{:S(2)}) collective-permute-start(bf16[16,4096]{1,0:T(8,128)(2,1)S(1)} %get-tuple-element.91), channel_id=1, source_target_pairs={{0,2},{1,3},{2,4},{3,5},{4,6},{5,7},{6,0},{7,1},{8,10},{9,11},{10,... | collective-permute-start | bytes 393224 | tf_op jit(solution)/shard_map/ppermute | solution.py:34
  117.7 2.2 %collective-permute-start.31 = (bf16[16,4096]{1,0:T(8,128)(2,1)S(1)}, bf16[16,4096]{1,0:T(8,128)(2,1)S(1)}, u32[]{:S(2)}, u32[]{:S(2)}) collective-permute-start(bf16[16,4096]{1,0:T(8,128)(2,1)S(1)} %add_convert_fusion), channel_id=1, source_target_pairs={{0,6},{1,7},{2,0},{3,1},{4,2},{5,3},{6,4},{7,5},{8,14},{9,15},{10,... | collective-permute-start | bytes 393224 | tf_op jit(solution)/shard_map/ppermute | solution.py:34
  119.8 3.1 %collective-permute-done.28 = bf16[16,4096]{1,0:T(8,128)(2,1)S(1)} collective-permute-done((bf16[16,4096]{1,0:T(8,128)(2,1)S(1)}, bf16[16,4096]{1,0:T(8,128)(2,1)S(1)}, u32[]{:S(2)}, u32[]{:S(2)}) %collective-permute-start.28) | collective-permute-done | bytes 131104 | tf_op jit(solution)/shard_map/ppermute | solution.py:34
  (73 shorter events, 30.1 us)
Async XLA Ops:
  2.3 12.4 %collective-permute-start.1 = (bf16[32,4096]{1,0:T(8,128)(2,1)S(1)}, bf16[32,4096]{1,0:T(8,128)(2,1)S(1)}, u32[]{:S(2)}, u32[]{:S(2)}) collective-permute-start(bf16[32,4096]{1,0:T(8,128)(2,1)S(1)} %shard_map.136.refs_0_), channel_id=1, source_target_pairs={{0,2},{1,3},{2,4},{3,5},{4,6},{5,7},{6,0},{7,1},{8,10},{9,11},{10,... | collective-permute-start | bytes 786440 | tf_op jit(solution)/shard_map/ppermute | solution.py:34
  5.4 13.4 %collective-permute-start.4 = (bf16[32,4096]{1,0:T(8,128)(2,1)S(1)}, bf16[32,4096]{1,0:T(8,128)(2,1)S(1)}, u32[]{:S(2)}, u32[]{:S(2)}) collective-permute-start(bf16[32,4096]{1,0:T(8,128)(2,1)S(1)} %shard_map.136.refs_0_), channel_id=1, source_target_pairs={{0,6},{1,7},{2,0},{3,1},{4,2},{5,3},{6,4},{7,5},{8,14},{9,15},{10,... | collective-permute-start | bytes 786440 | tf_op jit(solution)/shard_map/ppermute | solution.py:34
  14.7 14.7 %collective-permute-start.3 = (bf16[32,4096]{1,0:T(8,128)(2,1)S(1)}, bf16[32,4096]{1,0:T(8,128)(2,1)S(1)}, u32[]{:S(2)}, u32[]{:S(2)}) collective-permute-start(bf16[32,4096]{1,0:T(8,128)(2,1)S(1)} %shard_map.140.refs_2_), channel_id=1, source_target_pairs={{2,4},{3,5},{4,6},{5,7},{10,12},{11,13},{12,14},{13,15},{18,20},{1... | collective-permute-start | bytes 786440 | tf_op jit(solution)/shard_map/ppermute | solution.py:34
  18.8 10.6 %collective-permute-start.5 = (bf16[32,4096]{1,0:T(8,128)(2,1)S(1)}, bf16[32,4096]{1,0:T(8,128)(2,1)S(1)}, u32[]{:S(2)}, u32[]{:S(2)}) collective-permute-start(bf16[32,4096]{1,0:T(8,128)(2,1)S(1)} %collective-permute-done.4.refs_6_), channel_id=1, source_target_pairs={{2,0},{3,1},{4,2},{5,3},{10,8},{11,9},{12,10},{13,11},{18,16},{19,... | collective-permute-start | bytes 786440 | tf_op jit(solution)/shard_map/ppermute | solution.py:34
  20.1 10.9 %collective-permute-start = (bf16[32,4096]{1,0:T(8,128)(2,1)S(1)}, bf16[32,4096]{1,0:T(8,128)(2,1)S(1)}, u32[]{:S(2)}, u32[]{:S(2)}) collective-permute-start(bf16[32,4096]{1,0:T(8,128)(2,1)S(1)} %shard_map.136.refs_0_), channel_id=1, source_target_pairs={{0,1},{1,0},{2,3},{3,2},{4,5},{5,4},{6,7},{7,6},{8,9},{9,8},{10,11... | collective-permute-start | bytes 786440 | tf_op jit(solution)/shard_map/ppermute | solution.py:34
  27.3 9.3 %collective-permute-start.2 = (bf16[32,4096]{1,0:T(8,128)(2,1)S(1)}, bf16[32,4096]{1,0:T(8,128)(2,1)S(1)}, u32[]{:S(2)}, u32[]{:S(2)}) collective-permute-start(bf16[32,4096]{1,0:T(8,128)(2,1)S(1)} %shard_map.140.refs_2_), channel_id=1, source_target_pairs={{0,1},{1,0},{2,3},{3,2},{4,5},{5,4},{6,7},{7,6},{8,9},{9,8},{10,11... | collective-permute-start | bytes 786440 | tf_op jit(solution)/shard_map/ppermute | solution.py:34
  27.9 14.4 %collective-permute-start.7 = (bf16[32,4096]{1,0:T(8,128)(2,1)S(1)}, bf16[32,4096]{1,0:T(8,128)(2,1)S(1)}, u32[]{:S(2)}, u32[]{:S(2)}) collective-permute-start(bf16[32,4096]{1,0:T(8,128)(2,1)S(1)} %collective-permute-done.4.refs_6_), channel_id=1, source_target_pairs={{0,1},{1,0},{2,3},{3,2},{4,5},{5,4},{6,7},{7,6},{8,9},{9,8},{10,11... | collective-permute-start | bytes 786440 | tf_op jit(solution)/shard_map/ppermute | solution.py:34
  29.4 16.5 %collective-permute-start.6 = (bf16[32,4096]{1,0:T(8,128)(2,1)S(1)}, bf16[32,4096]{1,0:T(8,128)(2,1)S(1)}, u32[]{:S(2)}, u32[]{:S(2)}) collective-permute-start(bf16[32,4096]{1,0:T(8,128)(2,1)S(1)} %shard_map.143.refs_4_), channel_id=1, source_target_pairs={{0,1},{1,0},{2,3},{3,2},{4,5},{5,4},{6,7},{7,6},{8,9},{9,8},{10,11... | collective-permute-start | bytes 786440 | tf_op jit(solution)/shard_map/ppermute | solution.py:34
  47.7 9.2 %collective-permute-start.10 = (bf16[32,128]{1,0:T(8,128)(2,1)S(1)}, bf16[32,128]{1,0:T(8,128)(2,1)S(1)}, u32[]{:S(2)}, u32[]{:S(2)}) collective-permute-start(bf16[32,128]{1,0:T(8,128)(2,1)S(1)} %get-tuple-element.60), channel_id=1, source_target_pairs={{0,3},{1,2},{2,5},{3,4},{4,7},{5,6},{6,1},{7,0},{8,11},{9,10},{10,... | collective-permute-start | bytes 24584 | tf_op jit(solution)/shard_map/ppermute | solution.py:34
  50.6 7.6 %collective-permute-start.11 = (bf16[32,128]{1,0:T(8,128)(2,1)S(1)}, bf16[32,128]{1,0:T(8,128)(2,1)S(1)}, u32[]{:S(2)}, u32[]{:S(2)}) collective-permute-start(bf16[32,128]{1,0:T(8,128)(2,1)S(1)} %get-tuple-element.61), channel_id=1, source_target_pairs={{0,4},{1,5},{2,6},{3,7},{4,0},{5,1},{6,2},{7,3},{8,12},{9,13},{10,... | collective-permute-start | bytes 24584 | tf_op jit(solution)/shard_map/ppermute | solution.py:34
  51.5 8.4 %collective-permute-start.12 = (bf16[32,128]{1,0:T(8,128)(2,1)S(1)}, bf16[32,128]{1,0:T(8,128)(2,1)S(1)}, u32[]{:S(2)}, u32[]{:S(2)}) collective-permute-start(bf16[32,128]{1,0:T(8,128)(2,1)S(1)} %get-tuple-element.62), channel_id=1, source_target_pairs={{0,5},{1,4},{2,7},{3,6},{4,1},{5,0},{6,3},{7,2},{8,13},{9,12},{10,... | collective-permute-start | bytes 24584 | tf_op jit(solution)/shard_map/ppermute | solution.py:34
  54.1 5.8 %collective-permute-start.13 = (bf16[32,128]{1,0:T(8,128)(2,1)S(1)}, bf16[32,128]{1,0:T(8,128)(2,1)S(1)}, u32[]{:S(2)}, u32[]{:S(2)}) collective-permute-start(bf16[32,128]{1,0:T(8,128)(2,1)S(1)} %get-tuple-element.63), channel_id=1, source_target_pairs={{0,6},{1,7},{2,0},{3,1},{4,2},{5,3},{6,4},{7,5},{8,14},{9,15},{10,... | collective-permute-start | bytes 24584 | tf_op jit(solution)/shard_map/ppermute | solution.py:34
  55.6 4.5 %collective-permute-start.14 = (bf16[32,128]{1,0:T(8,128)(2,1)S(1)}, bf16[32,128]{1,0:T(8,128)(2,1)S(1)}, u32[]{:S(2)}, u32[]{:S(2)}) collective-permute-start(bf16[32,128]{1,0:T(8,128)(2,1)S(1)} %get-tuple-element.64), channel_id=1, source_target_pairs={{0,7},{1,6},{2,1},{3,0},{4,3},{5,2},{6,5},{7,4},{8,15},{9,14},{10,... | collective-permute-start | bytes 24584 | tf_op jit(solution)/shard_map/ppermute | solution.py:34
  56.9 3.7 %collective-permute-start.8 = (bf16[32,128]{1,0:T(8,128)(2,1)S(1)}, bf16[32,128]{1,0:T(8,128)(2,1)S(1)}, u32[]{:S(2)}, u32[]{:S(2)}) collective-permute-start(bf16[32,128]{1,0:T(8,128)(2,1)S(1)} %get-tuple-element.58), channel_id=1, source_target_pairs={{0,1},{1,0},{2,3},{3,2},{4,5},{5,4},{6,7},{7,6},{8,9},{9,8},{10,11... | collective-permute-start | bytes 24584 | tf_op jit(solution)/shard_map/ppermute | solution.py:34
  58.2 5.4 %collective-permute-start.9 = (bf16[32,128]{1,0:T(8,128)(2,1)S(1)}, bf16[32,128]{1,0:T(8,128)(2,1)S(1)}, u32[]{:S(2)}, u32[]{:S(2)}) collective-permute-start(bf16[32,128]{1,0:T(8,128)(2,1)S(1)} %get-tuple-element.59), channel_id=1, source_target_pairs={{0,2},{1,3},{2,4},{3,5},{4,6},{5,7},{6,0},{7,1},{8,10},{9,11},{10,... | collective-permute-start | bytes 24584 | tf_op jit(solution)/shard_map/ppermute | solution.py:34
  65.4 6.4 %collective-permute-start.15 = (bf16[32,4096]{1,0:T(8,128)(2,1)S(1)}, bf16[32,4096]{1,0:T(8,128)(2,1)S(1)}, u32[]{:S(2)}, u32[]{:S(2)}) collective-permute-start(bf16[32,4096]{1,0:T(8,128)(2,1)S(1)} %get-tuple-element.70), channel_id=1, source_target_pairs={{0,1},{1,0},{2,3},{3,2},{4,5},{5,4},{6,7},{7,6},{8,9},{9,8},{10,11... | collective-permute-start | bytes 786440 | tf_op jit(solution)/shard_map/ppermute | solution.py:34
  66.1 8.5 %collective-permute-start.18 = (bf16[32,4096]{1,0:T(8,128)(2,1)S(1)}, bf16[32,4096]{1,0:T(8,128)(2,1)S(1)}, u32[]{:S(2)}, u32[]{:S(2)}) collective-permute-start(bf16[32,4096]{1,0:T(8,128)(2,1)S(1)} %get-tuple-element.73), channel_id=1, source_target_pairs={{0,1},{1,0},{2,3},{3,2},{4,5},{5,4},{6,7},{7,6},{8,9},{9,8},{10,11... | collective-permute-start | bytes 786440 | tf_op jit(solution)/shard_map/ppermute | solution.py:34
  71.9 9.1 %collective-permute-start.16 = (bf16[16,4096]{1,0:T(8,128)(2,1)S(1)}, bf16[16,4096]{1,0:T(8,128)(2,1)S(1)}, u32[]{:S(2)}, u32[]{:S(2)}) collective-permute-start(bf16[16,4096]{1,0:T(8,128)(2,1)S(1)} %get-tuple-element.92), channel_id=1, source_target_pairs={{0,4},{1,5},{2,6},{3,7},{4,0},{5,1},{6,2},{7,3},{8,12},{9,13},{10,... | collective-permute-start | bytes 393224 | tf_op jit(solution)/shard_map/ppermute | solution.py:34
  71.9 9.0 %collective-permute-start.17 = (bf16[16,4096]{1,0:T(8,128)(2,1)S(1)}, bf16[16,4096]{1,0:T(8,128)(2,1)S(1)}, u32[]{:S(2)}, u32[]{:S(2)}) collective-permute-start(bf16[16,4096]{1,0:T(8,128)(2,1)S(1)} %get-tuple-element.93), channel_id=1, source_target_pairs={{0,2},{1,3},{2,4},{3,5},{4,6},{5,7},{6,0},{7,1},{8,10},{9,11},{10,... | collective-permute-start | bytes 393224 | tf_op jit(solution)/shard_map/ppermute | solution.py:34
  74.7 10.3 %collective-permute-start.19 = (bf16[16,4096]{1,0:T(8,128)(2,1)S(1)}, bf16[16,4096]{1,0:T(8,128)(2,1)S(1)}, u32[]{:S(2)}, u32[]{:S(2)}) collective-permute-start(bf16[16,4096]{1,0:T(8,128)(2,1)S(1)} %add_convert_fusion.3), channel_id=1, source_target_pairs={{0,6},{1,7},{2,0},{3,1},{4,2},{5,3},{6,4},{7,5},{8,14},{9,15},{10,... | collective-permute-start | bytes 393224 | tf_op jit(solution)/shard_map/ppermute | solution.py:34
  85.3 7.0 %collective-permute-start.21 = (bf16[16,4096]{1,0:T(8,128)(2,1)S(1)}, bf16[16,4096]{1,0:T(8,128)(2,1)S(1)}, u32[]{:S(2)}, u32[]{:S(2)}) collective-permute-start(bf16[16,4096]{1,0:T(8,128)(2,1)S(1)} %multiply_convert_fusion.refs_0_), channel_id=1, source_target_pairs={{0,2},{1,3},{2,4},{3,5},{4,6},{5,7},{6,0},{7,1},{8,10},{9,11},{10,... | collective-permute-start | bytes 393224 | tf_op jit(solution)/shard_map/ppermute | solution.py:34
  86.6 8.4 %collective-permute-start.23 = (bf16[16,4096]{1,0:T(8,128)(2,1)S(1)}, bf16[16,4096]{1,0:T(8,128)(2,1)S(1)}, u32[]{:S(2)}, u32[]{:S(2)}) collective-permute-start(bf16[16,4096]{1,0:T(8,128)(2,1)S(1)} %multiply_convert_fusion.refs_0_), channel_id=1, source_target_pairs={{0,4},{1,5},{2,6},{3,7},{4,0},{5,1},{6,2},{7,3},{8,12},{9,13},{10,... | collective-permute-start | bytes 393224 | tf_op jit(solution)/shard_map/ppermute | solution.py:34
  86.8 9.0 %collective-permute-start.25 = (bf16[16,4096]{1,0:T(8,128)(2,1)S(1)}, bf16[16,4096]{1,0:T(8,128)(2,1)S(1)}, u32[]{:S(2)}, u32[]{:S(2)}) collective-permute-start(bf16[16,4096]{1,0:T(8,128)(2,1)S(1)} %multiply_convert_fusion.refs_0_), channel_id=1, source_target_pairs={{0,6},{1,7},{2,0},{3,1},{4,2},{5,3},{6,4},{7,5},{8,14},{9,15},{10,... | collective-permute-start | bytes 393224 | tf_op jit(solution)/shard_map/ppermute | solution.py:34
  89.6 7.4 %collective-permute-start.20 = (bf16[16,4096]{1,0:T(8,128)(2,1)S(1)}, bf16[16,4096]{1,0:T(8,128)(2,1)S(1)}, u32[]{:S(2)}, u32[]{:S(2)}) collective-permute-start(bf16[16,4096]{1,0:T(8,128)(2,1)S(1)} %multiply_convert_fusion.refs_0_), channel_id=1, source_target_pairs={{0,1},{1,0},{2,3},{3,2},{4,5},{5,4},{6,7},{7,6},{8,9},{9,8},{10,11... | collective-permute-start | bytes 393224 | tf_op jit(solution)/shard_map/ppermute | solution.py:34
  92.3 6.3 %collective-permute-start.22 = (bf16[16,4096]{1,0:T(8,128)(2,1)S(1)}, bf16[16,4096]{1,0:T(8,128)(2,1)S(1)}, u32[]{:S(2)}, u32[]{:S(2)}) collective-permute-start(bf16[16,4096]{1,0:T(8,128)(2,1)S(1)} %collective-permute-done.21.refs_2_), channel_id=1, source_target_pairs={{0,1},{1,0},{2,3},{3,2},{4,5},{5,4},{6,7},{7,6},{8,9},{9,8},{10,11... | collective-permute-start | bytes 393224 | tf_op jit(solution)/shard_map/ppermute | solution.py:34
  95.0 6.5 %collective-permute-start.24 = (bf16[16,4096]{1,0:T(8,128)(2,1)S(1)}, bf16[16,4096]{1,0:T(8,128)(2,1)S(1)}, u32[]{:S(2)}, u32[]{:S(2)}) collective-permute-start(bf16[16,4096]{1,0:T(8,128)(2,1)S(1)} %collective-permute-done.23.refs_4_), channel_id=1, source_target_pairs={{0,1},{1,0},{2,3},{3,2},{4,5},{5,4},{6,7},{7,6},{8,9},{9,8},{10,11... | collective-permute-start | bytes 393224 | tf_op jit(solution)/shard_map/ppermute | solution.py:34
  95.7 8.5 %collective-permute-start.26 = (bf16[16,4096]{1,0:T(8,128)(2,1)S(1)}, bf16[16,4096]{1,0:T(8,128)(2,1)S(1)}, u32[]{:S(2)}, u32[]{:S(2)}) collective-permute-start(bf16[16,4096]{1,0:T(8,128)(2,1)S(1)} %collective-permute-done.25.refs_6_), channel_id=1, source_target_pairs={{0,1},{1,0},{2,3},{3,2},{4,5},{5,4},{6,7},{7,6},{8,9},{9,8},{10,11... | collective-permute-start | bytes 393224 | tf_op jit(solution)/shard_map/ppermute | solution.py:34
  108.0 6.4 %collective-permute-start.27 = (bf16[32,4096]{1,0:T(8,128)(2,1)S(1)}, bf16[32,4096]{1,0:T(8,128)(2,1)S(1)}, u32[]{:S(2)}, u32[]{:S(2)}) collective-permute-start(bf16[32,4096]{1,0:T(8,128)(2,1)S(1)} %get-tuple-element.80), channel_id=1, source_target_pairs={{0,1},{1,0},{2,3},{3,2},{4,5},{5,4},{6,7},{7,6},{8,9},{9,8},{10,11... | collective-permute-start | bytes 786440 | tf_op jit(solution)/shard_map/ppermute | solution.py:34
  108.8 8.8 %collective-permute-start.30 = (bf16[32,4096]{1,0:T(8,128)(2,1)S(1)}, bf16[32,4096]{1,0:T(8,128)(2,1)S(1)}, u32[]{:S(2)}, u32[]{:S(2)}) collective-permute-start(bf16[32,4096]{1,0:T(8,128)(2,1)S(1)} %get-tuple-element.83), channel_id=1, source_target_pairs={{0,1},{1,0},{2,3},{3,2},{4,5},{5,4},{6,7},{7,6},{8,9},{9,8},{10,11... | collective-permute-start | bytes 786440 | tf_op jit(solution)/shard_map/ppermute | solution.py:34
  114.5 8.4 %collective-permute-start.28 = (bf16[16,4096]{1,0:T(8,128)(2,1)S(1)}, bf16[16,4096]{1,0:T(8,128)(2,1)S(1)}, u32[]{:S(2)}, u32[]{:S(2)}) collective-permute-start(bf16[16,4096]{1,0:T(8,128)(2,1)S(1)} %get-tuple-element.90), channel_id=1, source_target_pairs={{0,4},{1,5},{2,6},{3,7},{4,0},{5,1},{6,2},{7,3},{8,12},{9,13},{10,... | collective-permute-start | bytes 393224 | tf_op jit(solution)/shard_map/ppermute | solution.py:34
  115.2 7.7 %collective-permute-start.29 = (bf16[16,4096]{1,0:T(8,128)(2,1)S(1)}, bf16[16,4096]{1,0:T(8,128)(2,1)S(1)}, u32[]{:S(2)}, u32[]{:S(2)}) collective-permute-start(bf16[16,4096]{1,0:T(8,128)(2,1)S(1)} %get-tuple-element.91), channel_id=1, source_target_pairs={{0,2},{1,3},{2,4},{3,5},{4,6},{5,7},{6,0},{7,1},{8,10},{9,11},{10,... | collective-permute-start | bytes 393224 | tf_op jit(solution)/shard_map/ppermute | solution.py:34
  117.7 6.6 %collective-permute-start.31 = (bf16[16,4096]{1,0:T(8,128)(2,1)S(1)}, bf16[16,4096]{1,0:T(8,128)(2,1)S(1)}, u32[]{:S(2)}, u32[]{:S(2)}) collective-permute-start(bf16[16,4096]{1,0:T(8,128)(2,1)S(1)} %add_convert_fusion), channel_id=1, source_target_pairs={{0,6},{1,7},{2,0},{3,1},{4,2},{5,3},{6,4},{7,5},{8,14},{9,15},{10,... | collective-permute-start | bytes 393224 | tf_op jit(solution)/shard_map/ppermute | solution.py:34
  (7 other events, 111.9 us)

commit v6 on v5

--- a/solution.py
+++ b/solution.py
@@ -50,18 +50,16 @@
     )[0]
 
 
-def gather_rows(block, tall, wide, tokens_1, tokens_2):
+def gather_rows(block, tall, wide, tokens):
     blocks = {(0, 0): block}
     for dz in range(1, tall):
         if tall != 4 or dz != 2:
             blocks[dz, 0] = shift(block, tall, wide, dz, 0)
-    blocks[1, 0] = tie([blocks[1, 0]], tokens_1)
+    blocks[1, 0] = tie([blocks[1, 0]], tokens)
     if tall == 4:
         up = shift(blocks[1, 0], tall, wide, 1, 0, lambda z: z in (1, 2))
         down = shift(blocks[3, 0], tall, wide, -1, 0, lambda z: z in (1, 2))
-        blocks[2, 0] = tie([up, down], tokens_2)
-    else:
-        blocks[tall - 1, 0] = tie([blocks[tall - 1, 0]], tokens_2)
+        blocks[2, 0] = up + down
     for dz in [0, 1, *range(tall - 1, 1, -1)]:
         for dy in range(1, wide):
             blocks[dz, dy] = shift(blocks[dz, 0], tall, wide, 0, dy)
@@ -125,6 +123,10 @@
     return jnp.dot(a, b, preferred_element_type=f32)
 
 
+def from_hbm(weight):
+    return pltpu.with_memory_space_constraint(weight, pltpu.HBM)
+
+
 def fetched(weight):
     return pltpu.with_memory_space_constraint(weight, pltpu.VMEM)
 
@@ -164,7 +166,7 @@
         scratch_shapes=[pltpu.SemaphoreType.DMA((len(arrays),))],
         compiler_params=pltpu.CompilerParams(vmem_limit_bytes=2 << 20),
         cost_estimate=pl.CostEstimate(flops=0, bytes_accessed=2 * size, transcendentals=0),
-    )(after, *[pltpu.with_memory_space_constraint(a, pltpu.HBM) for a in arrays])
+    )(after, *[from_hbm(a) for a in arrays])
     return [fetched(c) for c in copies] + [token]
 
 
@@ -212,15 +214,14 @@
         z, y = divmod(s, wide)
         from_block = lax.rem(my_z - z + tall, tall) * wide + lax.rem(my_y - y + wide, wide)
         to_block = lax.rem(z - my_z + tall, tall) * wide + lax.rem(y - my_y + wide, wide)
-        peer = lax.rem(my_z + z, tall) * wide + lax.rem(my_y + y, wide)
         before = where < s * tokens
         first = jnp.sum(jnp.where(before, 1.0, 0.0), axis=1, keepdims=True)
         inside = (where < (s + 1) * tokens) & jnp.logical_not(before)
         start = (from_block * capacity).astype(f32)
         slot += jnp.where(inside, lane - first + start, 0.0)
         place += jnp.where(owner == s, (to_block * share).astype(f32), 0.0)
-        out_base += jnp.where(out_block == s, heads_of(peer).astype(f32), 0.0)
-        in_base += jnp.where(in_source == s, (from_block * (outbound // count)).astype(f32), 0.0)
+        out_base += jnp.where(out_block == s, float(heads_of(s)), 0.0)
+        in_base += jnp.where(in_source == s, float(s * (outbound // count)), 0.0)
     mine = owner == iota((count, total), 0)
     earlier = jnp.where(iota((total, total), 0) < iota((total, total), 1), 1.0, 0.0)
     rank = dot(jnp.where(mine, 1.0, 0.0).astype(bf16), earlier.astype(bf16))
@@ -238,7 +239,7 @@
 def kv_body(count, *refs):
     blocks = refs[:count]
     pick_rows, order, columns, gain, w_key, w_value = refs[count : count + 6]
-    (normed, own, *sent), rows = refs[-3 - count : -1], refs[-1]
+    normed, own, sent, rows = refs[-4:]
     total, width = normed.shape
     tile = tile_of(width, 512)
     square = jnp.zeros((total, 1), f32)
@@ -259,14 +260,23 @@
     turned = lax.dot_general(
         columns[...], both, (((1,), (1,)), ((), ())), preferred_element_type=f32
     ).astype(bf16)
-    turned = dot(turned, order[...])
-    each = turned.shape[0] // len(sent)
-    for index, part in enumerate(sent):
-        part[...] = turned[index * each : (index + 1) * each, :].astype(bf16)
-
-
-def query_body(normed, w_query, cosine, sine, query):
-    raw = dot(normed[...], w_query[...])
+    sent[...] = dot(turned, order[...]).astype(bf16)
+
+
+def query_body(normed, w_query, cosine, sine, query, weight, sems):
+    depth = weight.shape[0] // 4
+    moves = []
+    for index in range(4):
+        piece = pl.ds(index * depth, depth)
+        moves.append(
+            pltpu.make_async_copy(w_query.at[piece], weight.at[piece], sems.at[index])
+        )
+        moves[-1].start()
+    raw = jnp.zeros(query.shape, f32)
+    for index, move in enumerate(moves):
+        move.wait()
+        piece = slice(index * depth, (index + 1) * depth)
+        raw += dot(normed[:, piece], weight[piece, :])
     for head in range(query.shape[1] // HEAD_DIM):
         span = slice(head * HEAD_DIM, (head + 1) * HEAD_DIM)
         one = raw[:, span]
@@ -275,14 +285,19 @@
 
 
 def attend_body(plane, kv_local, *refs):
-    count = plane[0] * plane[1]
-    arrived, rest = refs[:count], refs[count:]
-    query, unmix, cosine, sine, key_pos, query_pos, w_output = rest[:7]
-    parts, heads_out = rest[7:-1], rest[-1]
+    arrived, query, unmix, cosine, sine, key_pos, query_pos, w_output = refs[:8]
+    parts, (heads_out, weight, sems) = refs[8:-3], refs[-3:]
+    width = weight.shape[1] // 4
+    moves = []
+    for index in range(4):
+        piece = pl.ds(index * width, width)
+        moves.append(
+            pltpu.make_async_copy(w_output.at[:, piece], weight.at[:, piece], sems.at[index])
+        )
+        moves[-1].start()
     half = HEAD_DIM // 2
     heads = query.shape[1] // HEAD_DIM
-    mixed = jnp.concatenate([a[...].astype(f32) for a in arrived], axis=0).astype(bf16)
-    both = dot(unmix[...], mixed)
+    both = dot(unmix[...], arrived[...])
     allowed = key_pos[...].astype(f32) <= query_pos[:, 0:1]
     for group in range(kv_local):
         base = group * HEAD_DIM
@@ -302,13 +317,15 @@
             heads_out[:, span] = lax.dot_general(
                 probs, values, (((1,), (1,)), ((), ())), preferred_element_type=f32
             ).astype(bf16)
-    spread(heads_out, w_output, parts, plane, False)
-
-
-def spread(left, weight, parts, plane, back):
+    spread(heads_out, weight, parts, plane, False, moves)
+
+
+def spread(left, weight, parts, plane, back, moves=()):
     width = weight.shape[1]
     tile = tile_of(width, 512)
     for start in range(0, width, tile):
+        if moves and start % (width // len(moves)) == 0:
+            moves[start // (width // len(moves))].wait()
         span = slice(start, start + tile)
         product = dot(left[...], weight[:, span]).astype(bf16)
         store_parts(parts, *plane, span, product, back)
@@ -368,12 +385,9 @@
         specs=[scalar, VMEM, VMEM],
         flops=2 * capacity * tokens * model,
     )
-    attn_gain, w_key, w_value, w_query, token_1 = load(
-        outgoing, attn_gain.reshape(1, model), w_key, w_value, w_query
-    )
-    w_gate, token_2 = load(outgoing, w_gate)
-    w_output, token_3 = load(token_2, w_output)
-    w_up, token_4 = load(token_3, w_up)
+    attn_gain, w_key, w_value, token_1 = load(
+        outgoing, attn_gain.reshape(1, model), w_key, w_value
+    )
 
     each = kv_local * 2 * depth
     notes = np.zeros((max(count * each, 2 * kv_local * HEAD_DIM), 4), np.float32)
@@ -385,7 +399,7 @@
     notes[: 2 * kv_local * HEAD_DIM, 3] = source
     pick_rows, in_order, columns, unmix, positions = kernel_call(
         functools.partial(
-            map_body, tall, wide, tokens, lambda peer: lax.div(peer * local_heads, group_size)
+            map_body, tall, wide, tokens, lambda peer: peer * local_heads // group_size
         ),
         [
             ((total, count * capacity), bf16),
@@ -397,7 +411,7 @@
         [me, routed, balance, notes],
         specs=[scalar, VMEM, VMEM, VMEM],
     )
-    blocks = gather_rows(outgoing, tall, wide, [token_1, token_2, positions], [token_3, token_4])
+    blocks = gather_rows(outgoing, tall, wide, [token_1, positions])
 
     half = HEAD_DIM // 2
     steps_f = jnp.arange(half, dtype=f32)
@@ -409,29 +423,37 @@
     k_angles = freqs[:, None] * routed.astype(f32)
     k_cos, k_sin = jnp.cos(k_angles), jnp.sin(k_angles)
 
-    normed, own, *sent = kernel_call(
+    normed, own, sent = kernel_call(
         functools.partial(kv_body, count),
-        [((total, model), bf16), ((share, model), bf16)] + [((each, total), bf16)] * count,
+        [((total, model), bf16), ((share, model), bf16), ((count * each, total), bf16)],
         [*blocks, pick_rows, in_order, columns, attn_gain, w_key, w_value],
         [pltpu.VMEM((total, model), bf16)],
         flops=2 * total * model * 512,
     )
-    arrived = [
-        part if r == 0 else shift(part, tall, wide, *divmod(r, wide)) for r, part in enumerate(sent)
-    ]
+    arrived = lax.all_to_all(sent.reshape(count, each, total), "ctx", 0, 0, tiled=True)
+    arrived = arrived.reshape(count * each, total)
+    in_hbm = pl.BlockSpec(memory_space=pl.ANY)
+    heads_wide = local_heads * HEAD_DIM
     (query,) = kernel_call(
         query_body,
-        [((total, local_heads * HEAD_DIM), bf16)],
-        [normed, w_query, q_cos, q_sin],
-        flops=2 * total * model * local_heads * HEAD_DIM,
+        [((total, heads_wide), bf16)],
+        [normed, from_hbm(w_query), q_cos, q_sin],
+        [pltpu.VMEM((model, heads_wide), bf16), pltpu.SemaphoreType.DMA((4,))],
+        flops=2 * total * model * heads_wide,
+        specs=[VMEM, in_hbm, VMEM, VMEM],
     )
     part_shapes = sum_shapes(tall, wide, share, model)
     attn_parts = kernel_call(
         functools.partial(attend_body, plane, kv_local),
         part_shapes,
-        [*arrived, query, unmix, k_cos, k_sin, routed, positions, w_output],
-        [pltpu.VMEM((total, local_heads * HEAD_DIM), bf16)],
-        flops=2 * total * model * local_heads * HEAD_DIM,
+        [arrived, query, unmix, k_cos, k_sin, routed, positions, from_hbm(w_output)],
+        [
+            pltpu.VMEM((total, heads_wide), bf16),
+            pltpu.VMEM((heads_wide, model), bf16),
+            pltpu.SemaphoreType.DMA((4,)),
+        ],
+        flops=2 * total * model * heads_wide,
+        specs=[VMEM] * 7 + [in_hbm],
     )
     w_down, token_5 = load(attn_parts[0], w_down)
     attn_own = scatter_sum(attn_parts, tall, wide, [token_5])
@@ -440,6 +462,8 @@
     mean_sq = jnp.mean(hidden * hidden, axis=-1, keepdims=True)
     mnorm = (hidden * lax.rsqrt(mean_sq + norm_eps) * mlp_gain).astype(bf16)
     pieces = gather_blocks(mnorm, tall, wide)
+    w_gate, _ = load(mnorm, w_gate)
+    w_up, _ = load(mnorm, w_up)
     hidden_units = w_gate.shape[1]
     mlp_parts = kernel_call(
         functools.partial(mlp_body, plane),

time: 125 us -> 124 us (level)
  starting transfers between devices: 43.8 us -> 34.8 us
  waiting for transfers between devices: 52.5 us -> 57.3 us
  local copies, waits for them, and re-layouts: 1.92 us -> 3.47 us
    ppermute x32 -> x25, starting transfers between devices: 43.8 us -> 29.7 us  [shift(): return lax.ppermute(block, 'ctx', pairs)]
    all_to_all x0 -> x1, starting transfers between devices: none -> 5.13 us  [on_device(): lax.all_to_all(sent.reshape(count, each, total), 'ctx', 0, 0, tiled=True)]
    all_to_all x0 -> x1, waiting for transfers between devices: none -> 4.13 us  [on_device(): lax.all_to_all(sent.reshape(count, each, total), 'ctx', 0, 0, tiled=True)]
    pallas_call x9 -> x8, Pallas kernels: 9.4 us -> 12.7 us  [kernel_call(): pl.pallas_call(body, out_shape=[jax.ShapeDtypeStruct(s, d) for s, d in ou...]
    pallas_call x5 -> x4, Pallas kernels: 15.3 us -> 12.9 us  [load(): pl.pallas_call(functools.partial(load_body, len(arrays)), out_shape=[pltp...]
    unnamed x14, local copies, waits for them, and re-layouts: 1.92 us -> 3.47 us
    ppermute x32 -> x25, waiting for transfers between devices: 52.5 us -> 53.2 us  [shift(): return lax.ppermute(block, 'ctx', pairs)]
  transfers between devices with their start and end apart: 32 -> 26, of which waited for: 19 -> 17; matrix products, arithmetic and copies ran while one was open for 1% -> 1% of each run, Pallas kernels for 14% -> 13%
where the time goes in v6:
time: 124 us; the launch traced here: 123 us
  waiting for transfers between devices  57.3 us (46%)
  starting transfers between devices  34.8 us (28%)
  Pallas kernels  25.6 us (21%)
  local copies, waits for them, and re-layouts  3.47 us (3%)
  other arithmetic  1.95 us (2%)
    ppermute x25, waiting for transfers between devices, shift(): return lax.ppermute(block, 'ctx', pairs)  53.2 us
    ppermute x25, starting transfers between devices, shift(): return lax.ppermute(block, 'ctx', pairs)  29.7 us
    pallas_call x4, Pallas kernels, load(): pl.pallas_call(functools.partial(load_body, len(arrays)), out_shape=[pltp...  12.9 us
    pallas_call x8, Pallas kernels, kernel_call(): pl.pallas_call(body, out_shape=[jax.ShapeDtypeStruct(s, d) for s, d in ou...  12.7 us
    all_to_all x1, starting transfers between devices, on_device(): lax.all_to_all(sent.reshape(count, each, total), 'ctx', 0, 0, tiled=True)  5.13 us
    all_to_all x1, waiting for transfers between devices, on_device(): lax.all_to_all(sent.reshape(count, each, total), 'ctx', 0, 0, tiled=True)  4.13 us
    unnamed x14, local copies, waits for them, and re-layouts  3.47 us
  transfers between devices with their start and end apart: 26, of which 17 were waited for; matrix products, arithmetic and copies ran while one was open for 1% of the time, Pallas kernels for 13%

profile of v6, /device:TPU:0, one launch (start us, length us, event | category | flops | bytes accessed | tf_op | source)
XLA Modules:
  0.0 123.4 jit_solution(5863637727138588340)
XLA Ops:
  2.3 5.1 %collective-permute-start.4 = (bf16[32,4096]{1,0:T(8,128)(2,1)S(1)}, bf16[32,4096]{1,0:T(8,128)(2,1)S(1)}, u32[]{:S(2)}, u32[]{:S(2)}) collective-permute-start(bf16[32,4096]{1,0:T(8,128)(2,1)S(1)} %shard_map.136.refs_0_), channel_id=1, source_target_pairs={{0,6},{1,7},{2,0},{3,1},{4,2},{5,3},{6,4},{7,5},{8,14},{9,15},{10,... | collective-permute-start | bytes 786440 | tf_op jit(solution)/shard_map/ppermute | solution.py:34
  9.5 1.6 %shard_map.137 = (f32[1,4096]{1,0:T(1,128)S(1)}, bf16[4096,128]{1,0:T(8,128)(2,1)S(1)}, bf16[4096,128]{1,0:T(8,128)(2,1)S(1)}, f32[8,128]{1,0:T(8,128)S(1)}) custom-call(bf16[32,4096]{1,0:T(8,128)(2,1)S(1)} %shard_map.136.refs_0_, f32[1,4096]{1,0:T(1,128)} %bitcast.11, bf16[4096,128]{1,0:T(8,128)(2,1)} %refs_2_.1, bf16[4096,128]{1,0:T(8,128)(2,1)} %refs_3_.1), custom_call_target="tpu_custom_call" | custom-call | bytes 4227072 | tf_op jit(solution)/shard_map/pallas_call | solution.py:160
  11.1 3.0 %collective-permute-done.4.refs_6_ = bf16[32,4096]{1,0:T(8,128)(2,1)S(1)} collective-permute-done((bf16[32,4096]{1,0:T(8,128)(2,1)S(1)}, bf16[32,4096]{1,0:T(8,128)(2,1)S(1)}, u32[]{:S(2)}, u32[]{:S(2)}) %collective-permute-start.4) | collective-permute-done | bytes 262176 | tf_op jit(solution)/shard_map/ppermute | solution.py:34
  15.4 4.2 %collective-permute-done.1.refs_0_ = bf16[32,4096]{1,0:T(8,128)(2,1)S(1)} collective-permute-done((bf16[32,4096]{1,0:T(8,128)(2,1)S(1)}, bf16[32,4096]{1,0:T(8,128)(2,1)S(1)}, u32[]{:S(2)}, u32[]{:S(2)}) %collective-permute-start.1) | collective-permute-done | bytes 262176 | tf_op jit(solution)/shard_map/ppermute | solution.py:34
  20.4 1.6 %collective-permute-start = (bf16[32,4096]{1,0:T(8,128)(2,1)S(1)}, bf16[32,4096]{1,0:T(8,128)(2,1)S(1)}, u32[]{:S(2)}, u32[]{:S(2)}) collective-permute-start(bf16[32,4096]{1,0:T(8,128)(2,1)S(1)} %shard_map.136.refs_0_), channel_id=1, source_target_pairs={{0,1},{1,0},{2,3},{3,2},{4,5},{5,4},{6,7},{7,6},{8,9},{9,8},{10,11... | collective-permute-start | bytes 786440 | tf_op jit(solution)/shard_map/ppermute | solution.py:34
  22.6 1.5 %collective-permute-start.7 = (bf16[32,4096]{1,0:T(8,128)(2,1)S(1)}, bf16[32,4096]{1,0:T(8,128)(2,1)S(1)}, u32[]{:S(2)}, u32[]{:S(2)}) collective-permute-start(bf16[32,4096]{1,0:T(8,128)(2,1)S(1)} %collective-permute-done.4.refs_6_), channel_id=1, source_target_pairs={{0,1},{1,0},{2,3},{3,2},{4,5},{5,4},{6,7},{7,6},{8,9},{9,8},{10,11... | collective-permute-start | bytes 786440 | tf_op jit(solution)/shard_map/ppermute | solution.py:34
  25.2 1.6 %collective-permute-start.6 = (bf16[32,4096]{1,0:T(8,128)(2,1)S(1)}, bf16[32,4096]{1,0:T(8,128)(2,1)S(1)}, u32[]{:S(2)}, u32[]{:S(2)}) collective-permute-start(bf16[32,4096]{1,0:T(8,128)(2,1)S(1)} %add.62.refs_4_), channel_id=1, source_target_pairs={{0,1},{1,0},{2,3},{3,2},{4,5},{5,4},{6,7},{7,6},{8,9},{9,8},{10,11... | collective-permute-start | bytes 786440 | tf_op jit(solution)/shard_map/ppermute | solution.py:34
  27.2 2.5 %collective-permute-done.refs_1_ = bf16[32,4096]{1,0:T(8,128)(2,1)S(1)} collective-permute-done((bf16[32,4096]{1,0:T(8,128)(2,1)S(1)}, bf16[32,4096]{1,0:T(8,128)(2,1)S(1)}, u32[]{:S(2)}, u32[]{:S(2)}) %collective-permute-start) | collective-permute-done | bytes 262176 | tf_op jit(solution)/shard_map/ppermute | solution.py:34
  29.7 11.2 %collective-permute-done.7.refs_7_ = bf16[32,4096]{1,0:T(8,128)(2,1)S(1)} collective-permute-done((bf16[32,4096]{1,0:T(8,128)(2,1)S(1)}, bf16[32,4096]{1,0:T(8,128)(2,1)S(1)}, u32[]{:S(2)}, u32[]{:S(2)}) %collective-permute-start.7) | collective-permute-done | bytes 262176 | tf_op jit(solution)/shard_map/ppermute | solution.py:34
  40.9 3.4 %collective-permute-done.6.refs_5_ = bf16[32,4096]{1,0:T(8,128)(2,1)S(1)} collective-permute-done((bf16[32,4096]{1,0:T(8,128)(2,1)S(1)}, bf16[32,4096]{1,0:T(8,128)(2,1)S(1)}, u32[]{:S(2)}, u32[]{:S(2)}) %collective-permute-start.6) | collective-permute-done | bytes 262176 | tf_op jit(solution)/shard_map/ppermute | solution.py:34
  44.3 2.4 %shard_map.140 = (bf16[128,4096]{1,0:T(8,128)(2,1)S(1)}, bf16[16,4096]{1,0:T(8,128)(2,1)S(1)}, bf16[256,128]{1,0:T(8,128)(2,1)}) custom-call(bf16[32,4096]{1,0:T(8,128)(2,1)S(1)} %shard_map.136.refs_0_, bf16[32,4096]{1,0:T(8,128)(2,1)S(1)} %collective-permute-done.refs_1_, bf16[32,4096]{1,0:T(8,128)(2,1)S(1)} %shard_map.139.refs_2_, ...), custom_call_target="tpu_custom_call" | custom-call | flops 536870912 | bytes 1048576 | tf_op jit(solution)/shard_map/pallas_call | solution.py:135
  46.8 5.1 %all-to-all-start = ((bf16[8,32,128]{2,1,0:T(8,128)(2,1)}), bf16[8,32,128]{2,1,0:T(8,128)(2,1)S(1)}, u32[]{:S(2)}, u32[]{:S(2)}) async-start(bf16[8,32,128]{2,1,0:T(8,128)(2,1)} %bitcast.4), calls=%async_computation | async-start | bytes 131072 | tf_op jit(solution)/shard_map/all_to_all | solution.py:433
  52.0 2.6 %shard_map.141.refs_1_ = bf16[128,512]{1,0:T(8,128)(2,1)S(1)} custom-call(bf16[128,4096]{1,0:T(8,128)(2,1)S(1)} %get-tuple-element.43.normed, bf16[4096,512]{1,0:T(8,128)(2,1)} %w_query.1, f32[128,128]{1,0:T(8,128)S(1)} %get-tuple-element.73.cosine, f32[128,128]{1,0:T(8,128)S(1)} %get-tuple-element.74.sine), custom_call_target="tpu_custom_call" | custom-call | flops 536870912 | bytes 1048576 | tf_op jit(solution)/shard_map/pallas_call | solution.py:135
  54.7 4.1 %all-to-all-done = bf16[8,32,128]{2,1,0:T(8,128)(2,1)S(1)} async-done(((bf16[8,32,128]{2,1,0:T(8,128)(2,1)}), bf16[8,32,128]{2,1,0:T(8,128)(2,1)S(1)}, u32[]{:S(2)}, u32[]{:S(2)}) %all-to-all-start) | async-done | bytes 65568 | tf_op jit(solution)/shard_map/all_to_all | solution.py:433
  58.8 3.1 %shard_map.142 = (bf16[16,4096]{1,0:T(8,128)(2,1)S(1)}, bf16[16,4096]{1,0:T(8,128)(2,1)S(1)}, bf16[16,4096]{1,0:T(8,128)(2,1)S(1)}, bf16[16,4096]{1,0:T(8,128)(2...) custom-call(bf16[256,128]{1,0:T(8,128)(2,1)S(1)} %bitcast.6, ...), custom_call_target="tpu_custom_call" | custom-call | flops 536870912 | bytes 1048576 | tf_op jit(solution)/shard_map/pallas_call | solution.py:135
  62.3 1.6 %collective-permute-start.11 = (bf16[32,4096]{1,0:T(8,128)(2,1)S(1)}, bf16[32,4096]{1,0:T(8,128)(2,1)S(1)}, u32[]{:S(2)}, u32[]{:S(2)}) collective-permute-start(bf16[32,4096]{1,0:T(8,128)(2,1)S(1)} %get-tuple-element.49), channel_id=1, source_target_pairs={{0,1},{1,0},{2,3},{3,2},{4,5},{5,4},{6,7},{7,6},{8,9},{9,8},{10,11... | collective-permute-start | bytes 786440 | tf_op jit(solution)/shard_map/ppermute | solution.py:34
  64.0 3.4 %shard_map.143 = (bf16[1024,4096]{1,0:T(8,128)(2,1)S(1)}, f32[8,128]{1,0:T(8,128)S(1)}) custom-call(bf16[16,4096]{1,0:T(8,128)(2,1)S(1)} %get-tuple-element.50.refs_0_, bf16[1024,4096]{1,0:T(8,128)(2,1)} %refs_1_.3), custom_call_target="tpu_custom_call" | custom-call | bytes 16777216 | tf_op jit(solution)/shard_map/pallas_call | solution.py:160
  67.4 1.6 %collective-permute-done.8 = bf16[32,4096]{1,0:T(8,128)(2,1)S(1)} collective-permute-done((bf16[32,4096]{1,0:T(8,128)(2,1)S(1)}, bf16[32,4096]{1,0:T(8,128)(2,1)S(1)}, u32[]{:S(2)}, u32[]{:S(2)}) %collective-permute-start.8) | collective-permute-done | bytes 262176 | tf_op jit(solution)/shard_map/ppermute | solution.py:34
  70.2 1.5 %collective-permute-done.11.refs_0_ = bf16[32,4096]{1,0:T(8,128)(2,1)S(1)} collective-permute-done((bf16[32,4096]{1,0:T(8,128)(2,1)S(1)}, bf16[32,4096]{1,0:T(8,128)(2,1)S(1)}, u32[]{:S(2)}, u32[]{:S(2)}) %collective-permute-start.11) | collective-permute-done | bytes 262176 | tf_op jit(solution)/shard_map/ppermute | solution.py:34
  71.8 1.7 %collective-permute-start.12 = (bf16[16,4096]{1,0:T(8,128)(2,1)S(1)}, bf16[16,4096]{1,0:T(8,128)(2,1)S(1)}, u32[]{:S(2)}, u32[]{:S(2)}) collective-permute-start(bf16[16,4096]{1,0:T(8,128)(2,1)S(1)} %add_convert_fusion.3), channel_id=1, source_target_pairs={{0,6},{1,7},{2,0},{3,1},{4,2},{5,3},{6,4},{7,5},{8,14},{9,15},{10,... | collective-permute-start | bytes 393224 | tf_op jit(solution)/shard_map/ppermute | solution.py:34
  73.5 6.5 %collective-permute-done.9 = bf16[16,4096]{1,0:T(8,128)(2,1)S(1)} collective-permute-done((bf16[16,4096]{1,0:T(8,128)(2,1)S(1)}, bf16[16,4096]{1,0:T(8,128)(2,1)S(1)}, u32[]{:S(2)}, u32[]{:S(2)}) %collective-permute-start.9) | collective-permute-done | bytes 131104 | tf_op jit(solution)/shard_map/ppermute | solution.py:34
  82.2 4.4 %collective-permute-start.16 = (bf16[16,4096]{1,0:T(8,128)(2,1)S(1)}, bf16[16,4096]{1,0:T(8,128)(2,1)S(1)}, u32[]{:S(2)}, u32[]{:S(2)}) collective-permute-start(bf16[16,4096]{1,0:T(8,128)(2,1)S(1)} %multiply_convert_fusion.refs_0_), channel_id=1, source_target_pairs={{0,4},{1,5},{2,6},{3,7},{4,0},{5,1},{6,2},{7,3},{8,12},{9,13},{10,... | collective-permute-start | bytes 393224 | tf_op jit(solution)/shard_map/ppermute | solution.py:34
  88.7 5.0 %collective-permute-done.16.refs_4_ = bf16[16,4096]{1,0:T(8,128)(2,1)S(1)} collective-permute-done((bf16[16,4096]{1,0:T(8,128)(2,1)S(1)}, bf16[16,4096]{1,0:T(8,128)(2,1)S(1)}, u32[]{:S(2)}, u32[]{:S(2)}) %collective-permute-start.16) | collective-permute-done | bytes 131104 | tf_op jit(solution)/shard_map/ppermute | solution.py:34
  94.4 1.4 %collective-permute-start.15 = (bf16[16,4096]{1,0:T(8,128)(2,1)S(1)}, bf16[16,4096]{1,0:T(8,128)(2,1)S(1)}, u32[]{:S(2)}, u32[]{:S(2)}) collective-permute-start(bf16[16,4096]{1,0:T(8,128)(2,1)S(1)} %collective-permute-done.14.refs_2_), channel_id=1, source_target_pairs={{0,1},{1,0},{2,3},{3,2},{4,5},{5,4},{6,7},{7,6},{8,9},{9,8},{10,11... | collective-permute-start | bytes 393224 | tf_op jit(solution)/shard_map/ppermute | solution.py:34
  95.8 4.0 %shard_map.146 = (bf16[4096,1024]{1,0:T(8,128)(2,1)S(1)}, f32[8,128]{1,0:T(8,128)}) custom-call(bf16[16,4096]{1,0:T(8,128)(2,1)S(1)} %multiply_convert_fusion.refs_0_, bf16[4096,1024]{1,0:T(8,128)(2,1)} %refs_1_.5), custom_call_target="tpu_custom_call" | custom-call | bytes 16777216 | tf_op jit(solution)/shard_map/pallas_call | solution.py:160
  99.8 4.0 %shard_map.145 = (bf16[4096,1024]{1,0:T(8,128)(2,1)S(1)}, f32[8,128]{1,0:T(8,128)}) custom-call(bf16[16,4096]{1,0:T(8,128)(2,1)S(1)} %multiply_convert_fusion.refs_0_, bf16[4096,1024]{1,0:T(8,128)(2,1)} %refs_1_.4), custom_call_target="tpu_custom_call" | custom-call | bytes 16777216 | tf_op jit(solution)/shard_map/pallas_call | solution.py:160
  103.8 3.6 %shard_map.147 = (bf16[16,4096]{1,0:T(8,128)(2,1)S(1)}, bf16[16,4096]{1,0:T(8,128)(2,1)S(1)}, bf16[16,4096]{1,0:T(8,128)(2,1)S(1)}, bf16[16,4096]{1,0:T(8,128)(2...) custom-call(bf16[16,4096]{1,0:T(8,128)(2,1)S(1)} %multiply_convert_fusion.refs_0_, ...), custom_call_target="tpu_custom_call" | custom-call | flops 3221225472 | bytes 1048576 | tf_op jit(solution)/shard_map/pallas_call | solution.py:135
  108.1 1.4 %collective-permute-start.23 = (bf16[32,4096]{1,0:T(8,128)(2,1)S(1)}, bf16[32,4096]{1,0:T(8,128)(2,1)S(1)}, u32[]{:S(2)}, u32[]{:S(2)}) collective-permute-start(bf16[32,4096]{1,0:T(8,128)(2,1)S(1)} %get-tuple-element.59), channel_id=1, source_target_pairs={{0,1},{1,0},{2,3},{3,2},{4,5},{5,4},{6,7},{7,6},{8,9},{9,8},{10,11... | collective-permute-start | bytes 786440 | tf_op jit(solution)/shard_map/ppermute | solution.py:34
  109.5 4.3 %collective-permute-done.20 = bf16[32,4096]{1,0:T(8,128)(2,1)S(1)} collective-permute-done((bf16[32,4096]{1,0:T(8,128)(2,1)S(1)}, bf16[32,4096]{1,0:T(8,128)(2,1)S(1)}, u32[]{:S(2)}, u32[]{:S(2)}) %collective-permute-start.20) | collective-permute-done | bytes 262176 | tf_op jit(solution)/shard_map/ppermute | solution.py:34
  114.1 2.6 %collective-permute-done.23 = bf16[32,4096]{1,0:T(8,128)(2,1)S(1)} collective-permute-done((bf16[32,4096]{1,0:T(8,128)(2,1)S(1)}, bf16[32,4096]{1,0:T(8,128)(2,1)S(1)}, u32[]{:S(2)}, u32[]{:S(2)}) %collective-permute-start.23) | collective-permute-done | bytes 262176 | tf_op jit(solution)/shard_map/ppermute | solution.py:34
  118.0 3.4 %collective-permute-done.21 = bf16[16,4096]{1,0:T(8,128)(2,1)S(1)} collective-permute-done((bf16[16,4096]{1,0:T(8,128)(2,1)S(1)}, bf16[16,4096]{1,0:T(8,128)(2,1)S(1)}, u32[]{:S(2)}, u32[]{:S(2)}) %collective-permute-start.21) | collective-permute-done | bytes 131104 | tf_op jit(solution)/shard_map/ppermute | solution.py:34
  121.4 1.3 %collective-permute-done.24 = bf16[16,4096]{1,0:T(8,128)(2,1)S(1)} collective-permute-done((bf16[16,4096]{1,0:T(8,128)(2,1)S(1)}, bf16[16,4096]{1,0:T(8,128)(2,1)S(1)}, u32[]{:S(2)}, u32[]{:S(2)}) %collective-permute-start.24) | collective-permute-done | bytes 131104 | tf_op jit(solution)/shard_map/ppermute | solution.py:34
  (60 shorter events, 18.4 us)
Async XLA Ops:
  0.0 58.8 %copy-start.3 = (s32[128]{0:T(128)S(1)}, s32[128]{0:T(128)}, u32[]{:S(2)}) copy-start(s32[128]{0:T(128)} %param.15) | copy-start | bytes 1540
  0.0 1.2 %copy-start = (bf16[128,4096]{1,0:T(8,128)(2,1)S(1)}, bf16[128,4096]{1,0:T(8,128)(2,1)}, u32[]{:S(2)}) copy-start(bf16[128,4096]{1,0:T(8,128)(2,1)} %activations.1) | copy-start | bytes 3145732
  1.2 0.7 copy-start.2
  2.3 11.8 %collective-permute-start.4 = (bf16[32,4096]{1,0:T(8,128)(2,1)S(1)}, bf16[32,4096]{1,0:T(8,128)(2,1)S(1)}, u32[]{:S(2)}, u32[]{:S(2)}) collective-permute-start(bf16[32,4096]{1,0:T(8,128)(2,1)S(1)} %shard_map.136.refs_0_), channel_id=1, source_target_pairs={{0,6},{1,7},{2,0},{3,1},{4,2},{5,3},{6,4},{7,5},{8,14},{9,15},{10,... | collective-permute-start | bytes 786440 | tf_op jit(solution)/shard_map/ppermute | solution.py:34
  7.4 12.2 %collective-permute-start.1 = (bf16[32,4096]{1,0:T(8,128)(2,1)S(1)}, bf16[32,4096]{1,0:T(8,128)(2,1)S(1)}, u32[]{:S(2)}, u32[]{:S(2)}) collective-permute-start(bf16[32,4096]{1,0:T(8,128)(2,1)S(1)} %shard_map.136.refs_0_), channel_id=1, source_target_pairs={{0,2},{1,3},{2,4},{3,5},{4,6},{5,7},{6,0},{7,1},{8,10},{9,11},{10,... | collective-permute-start | bytes 786440 | tf_op jit(solution)/shard_map/ppermute | solution.py:34
  7.4 0.9 copy-start.1
  14.1 11.0 %collective-permute-start.5 = (bf16[32,4096]{1,0:T(8,128)(2,1)S(1)}, bf16[32,4096]{1,0:T(8,128)(2,1)S(1)}, u32[]{:S(2)}, u32[]{:S(2)}) collective-permute-start(bf16[32,4096]{1,0:T(8,128)(2,1)S(1)} %collective-permute-done.4.refs_6_), channel_id=1, source_target_pairs={{2,0},{3,1},{4,2},{5,3},{10,8},{11,9},{12,10},{13,11},{18,16},{19,... | collective-permute-start | bytes 786440 | tf_op jit(solution)/shard_map/ppermute | solution.py:34
  19.7 5.5 %collective-permute-start.3 = (bf16[32,4096]{1,0:T(8,128)(2,1)S(1)}, bf16[32,4096]{1,0:T(8,128)(2,1)S(1)}, u32[]{:S(2)}, u32[]{:S(2)}) collective-permute-start(bf16[32,4096]{1,0:T(8,128)(2,1)S(1)} %shard_map.139.refs_2_), channel_id=1, source_target_pairs={{2,4},{3,5},{4,6},{5,7},{10,12},{11,13},{12,14},{13,15},{18,20},{1... | collective-permute-start | bytes 786440 | tf_op jit(solution)/shard_map/ppermute | solution.py:34
  20.4 9.3 %collective-permute-start = (bf16[32,4096]{1,0:T(8,128)(2,1)S(1)}, bf16[32,4096]{1,0:T(8,128)(2,1)S(1)}, u32[]{:S(2)}, u32[]{:S(2)}) collective-permute-start(bf16[32,4096]{1,0:T(8,128)(2,1)S(1)} %shard_map.136.refs_0_), channel_id=1, source_target_pairs={{0,1},{1,0},{2,3},{3,2},{4,5},{5,4},{6,7},{7,6},{8,9},{9,8},{10,11... | collective-permute-start | bytes 786440 | tf_op jit(solution)/shard_map/ppermute | solution.py:34
  22.0 19.0 %collective-permute-start.2 = (bf16[32,4096]{1,0:T(8,128)(2,1)S(1)}, bf16[32,4096]{1,0:T(8,128)(2,1)S(1)}, u32[]{:S(2)}, u32[]{:S(2)}) collective-permute-start(bf16[32,4096]{1,0:T(8,128)(2,1)S(1)} %shard_map.139.refs_2_), channel_id=1, source_target_pairs={{0,1},{1,0},{2,3},{3,2},{4,5},{5,4},{6,7},{7,6},{8,9},{9,8},{10,11... | collective-permute-start | bytes 786440 | tf_op jit(solution)/shard_map/ppermute | solution.py:34
  22.6 18.4 %collective-permute-start.7 = (bf16[32,4096]{1,0:T(8,128)(2,1)S(1)}, bf16[32,4096]{1,0:T(8,128)(2,1)S(1)}, u32[]{:S(2)}, u32[]{:S(2)}) collective-permute-start(bf16[32,4096]{1,0:T(8,128)(2,1)S(1)} %collective-permute-done.4.refs_6_), channel_id=1, source_target_pairs={{0,1},{1,0},{2,3},{3,2},{4,5},{5,4},{6,7},{7,6},{8,9},{9,8},{10,11... | collective-permute-start | bytes 786440 | tf_op jit(solution)/shard_map/ppermute | solution.py:34
  25.2 19.1 %collective-permute-start.6 = (bf16[32,4096]{1,0:T(8,128)(2,1)S(1)}, bf16[32,4096]{1,0:T(8,128)(2,1)S(1)}, u32[]{:S(2)}, u32[]{:S(2)}) collective-permute-start(bf16[32,4096]{1,0:T(8,128)(2,1)S(1)} %add.62.refs_4_), channel_id=1, source_target_pairs={{0,1},{1,0},{2,3},{3,2},{4,5},{5,4},{6,7},{7,6},{8,9},{9,8},{10,11... | collective-permute-start | bytes 786440 | tf_op jit(solution)/shard_map/ppermute | solution.py:34
  46.8 12.0 %all-to-all-start = ((bf16[8,32,128]{2,1,0:T(8,128)(2,1)}), bf16[8,32,128]{2,1,0:T(8,128)(2,1)S(1)}, u32[]{:S(2)}, u32[]{:S(2)}) async-start(bf16[8,32,128]{2,1,0:T(8,128)(2,1)} %bitcast.4), calls=%async_computation | async-start | bytes 131072 | tf_op jit(solution)/shard_map/all_to_all | solution.py:433
  54.6 26.0 %copy-start.5 = (f32[4096]{0:T(1024)S(1)}, f32[4096]{0:T(1024)}, u32[]{:S(2)}) copy-start(f32[4096]{0:T(1024)} %param.26) | copy-start | bytes 49156
  54.6 26.3 %copy-start.6 = (f32[4096]{0:T(1024)S(1)}, f32[4096]{0:T(1024)}, u32[]{:S(2)}) copy-start(f32[4096]{0:T(1024)} %param.22) | copy-start | bytes 49156
  61.9 7.1 %collective-permute-start.8 = (bf16[32,4096]{1,0:T(8,128)(2,1)S(1)}, bf16[32,4096]{1,0:T(8,128)(2,1)S(1)}, u32[]{:S(2)}, u32[]{:S(2)}) collective-permute-start(bf16[32,4096]{1,0:T(8,128)(2,1)S(1)} %get-tuple-element.46), channel_id=1, source_target_pairs={{0,1},{1,0},{2,3},{3,2},{4,5},{5,4},{6,7},{7,6},{8,9},{9,8},{10,11... | collective-permute-start | bytes 786440 | tf_op jit(solution)/shard_map/ppermute | solution.py:34
  62.3 9.5 %collective-permute-start.11 = (bf16[32,4096]{1,0:T(8,128)(2,1)S(1)}, bf16[32,4096]{1,0:T(8,128)(2,1)S(1)}, u32[]{:S(2)}, u32[]{:S(2)}) collective-permute-start(bf16[32,4096]{1,0:T(8,128)(2,1)S(1)} %get-tuple-element.49), channel_id=1, source_target_pairs={{0,1},{1,0},{2,3},{3,2},{4,5},{5,4},{6,7},{7,6},{8,9},{9,8},{10,11... | collective-permute-start | bytes 786440 | tf_op jit(solution)/shard_map/ppermute | solution.py:34
  69.0 10.9 %collective-permute-start.9 = (bf16[16,4096]{1,0:T(8,128)(2,1)S(1)}, bf16[16,4096]{1,0:T(8,128)(2,1)S(1)}, u32[]{:S(2)}, u32[]{:S(2)}) collective-permute-start(bf16[16,4096]{1,0:T(8,128)(2,1)S(1)} %get-tuple-element.68), channel_id=1, source_target_pairs={{0,4},{1,5},{2,6},{3,7},{4,0},{5,1},{6,2},{7,3},{8,12},{9,13},{10,... | collective-permute-start | bytes 393224 | tf_op jit(solution)/shard_map/ppermute | solution.py:34
  69.6 10.4 %collective-permute-start.10 = (bf16[16,4096]{1,0:T(8,128)(2,1)S(1)}, bf16[16,4096]{1,0:T(8,128)(2,1)S(1)}, u32[]{:S(2)}, u32[]{:S(2)}) collective-permute-start(bf16[16,4096]{1,0:T(8,128)(2,1)S(1)} %get-tuple-element.69), channel_id=1, source_target_pairs={{0,2},{1,3},{2,4},{3,5},{4,6},{5,7},{6,0},{7,1},{8,10},{9,11},{10,... | collective-permute-start | bytes 393224 | tf_op jit(solution)/shard_map/ppermute | solution.py:34
  71.8 8.8 %collective-permute-start.12 = (bf16[16,4096]{1,0:T(8,128)(2,1)S(1)}, bf16[16,4096]{1,0:T(8,128)(2,1)S(1)}, u32[]{:S(2)}, u32[]{:S(2)}) collective-permute-start(bf16[16,4096]{1,0:T(8,128)(2,1)S(1)} %add_convert_fusion.3), channel_id=1, source_target_pairs={{0,6},{1,7},{2,0},{3,1},{4,2},{5,3},{6,4},{7,5},{8,14},{9,15},{10,... | collective-permute-start | bytes 393224 | tf_op jit(solution)/shard_map/ppermute | solution.py:34
  81.0 7.1 %collective-permute-start.18 = (bf16[16,4096]{1,0:T(8,128)(2,1)S(1)}, bf16[16,4096]{1,0:T(8,128)(2,1)S(1)}, u32[]{:S(2)}, u32[]{:S(2)}) collective-permute-start(bf16[16,4096]{1,0:T(8,128)(2,1)S(1)} %multiply_convert_fusion.refs_0_), channel_id=1, source_target_pairs={{0,6},{1,7},{2,0},{3,1},{4,2},{5,3},{6,4},{7,5},{8,14},{9,15},{10,... | collective-permute-start | bytes 393224 | tf_op jit(solution)/shard_map/ppermute | solution.py:34
  82.2 11.6 %collective-permute-start.16 = (bf16[16,4096]{1,0:T(8,128)(2,1)S(1)}, bf16[16,4096]{1,0:T(8,128)(2,1)S(1)}, u32[]{:S(2)}, u32[]{:S(2)}) collective-permute-start(bf16[16,4096]{1,0:T(8,128)(2,1)S(1)} %multiply_convert_fusion.refs_0_), channel_id=1, source_target_pairs={{0,4},{1,5},{2,6},{3,7},{4,0},{5,1},{6,2},{7,3},{8,12},{9,13},{10,... | collective-permute-start | bytes 393224 | tf_op jit(solution)/shard_map/ppermute | solution.py:34
  86.6 7.8 %collective-permute-start.14 = (bf16[16,4096]{1,0:T(8,128)(2,1)S(1)}, bf16[16,4096]{1,0:T(8,128)(2,1)S(1)}, u32[]{:S(2)}, u32[]{:S(2)}) collective-permute-start(bf16[16,4096]{1,0:T(8,128)(2,1)S(1)} %multiply_convert_fusion.refs_0_), channel_id=1, source_target_pairs={{0,2},{1,3},{2,4},{3,5},{4,6},{5,7},{6,0},{7,1},{8,10},{9,11},{10,... | collective-permute-start | bytes 393224 | tf_op jit(solution)/shard_map/ppermute | solution.py:34
  86.6 17.2 %collective-permute-start.13 = (bf16[16,4096]{1,0:T(8,128)(2,1)S(1)}, bf16[16,4096]{1,0:T(8,128)(2,1)S(1)}, u32[]{:S(2)}, u32[]{:S(2)}) collective-permute-start(bf16[16,4096]{1,0:T(8,128)(2,1)S(1)} %multiply_convert_fusion.refs_0_), channel_id=1, source_target_pairs={{0,1},{1,0},{2,3},{3,2},{4,5},{5,4},{6,7},{7,6},{8,9},{9,8},{10,11... | collective-permute-start | bytes 393224 | tf_op jit(solution)/shard_map/ppermute | solution.py:34
  88.1 15.7 %collective-permute-start.19 = (bf16[16,4096]{1,0:T(8,128)(2,1)S(1)}, bf16[16,4096]{1,0:T(8,128)(2,1)S(1)}, u32[]{:S(2)}, u32[]{:S(2)}) collective-permute-start(bf16[16,4096]{1,0:T(8,128)(2,1)S(1)} %collective-permute-done.18.refs_6_), channel_id=1, source_target_pairs={{0,1},{1,0},{2,3},{3,2},{4,5},{5,4},{6,7},{7,6},{8,9},{9,8},{10,11... | collective-permute-start | bytes 393224 | tf_op jit(solution)/shard_map/ppermute | solution.py:34
  93.8 10.0 %collective-permute-start.17 = (bf16[16,4096]{1,0:T(8,128)(2,1)S(1)}, bf16[16,4096]{1,0:T(8,128)(2,1)S(1)}, u32[]{:S(2)}, u32[]{:S(2)}) collective-permute-start(bf16[16,4096]{1,0:T(8,128)(2,1)S(1)} %collective-permute-done.16.refs_4_), channel_id=1, source_target_pairs={{0,1},{1,0},{2,3},{3,2},{4,5},{5,4},{6,7},{7,6},{8,9},{9,8},{10,11... | collective-permute-start | bytes 393224 | tf_op jit(solution)/shard_map/ppermute | solution.py:34
  94.4 9.4 %collective-permute-start.15 = (bf16[16,4096]{1,0:T(8,128)(2,1)S(1)}, bf16[16,4096]{1,0:T(8,128)(2,1)S(1)}, u32[]{:S(2)}, u32[]{:S(2)}) collective-permute-start(bf16[16,4096]{1,0:T(8,128)(2,1)S(1)} %collective-permute-done.14.refs_2_), channel_id=1, source_target_pairs={{0,1},{1,0},{2,3},{3,2},{4,5},{5,4},{6,7},{7,6},{8,9},{9,8},{10,11... | collective-permute-start | bytes 393224 | tf_op jit(solution)/shard_map/ppermute | solution.py:34
  107.4 6.4 %collective-permute-start.20 = (bf16[32,4096]{1,0:T(8,128)(2,1)S(1)}, bf16[32,4096]{1,0:T(8,128)(2,1)S(1)}, u32[]{:S(2)}, u32[]{:S(2)}) collective-permute-start(bf16[32,4096]{1,0:T(8,128)(2,1)S(1)} %get-tuple-element.56), channel_id=1, source_target_pairs={{0,1},{1,0},{2,3},{3,2},{4,5},{5,4},{6,7},{7,6},{8,9},{9,8},{10,11... | collective-permute-start | bytes 786440 | tf_op jit(solution)/shard_map/ppermute | solution.py:34
  108.1 8.5 %collective-permute-start.23 = (bf16[32,4096]{1,0:T(8,128)(2,1)S(1)}, bf16[32,4096]{1,0:T(8,128)(2,1)S(1)}, u32[]{:S(2)}, u32[]{:S(2)}) collective-permute-start(bf16[32,4096]{1,0:T(8,128)(2,1)S(1)} %get-tuple-element.59), channel_id=1, source_target_pairs={{0,1},{1,0},{2,3},{3,2},{4,5},{5,4},{6,7},{7,6},{8,9},{9,8},{10,11... | collective-permute-start | bytes 786440 | tf_op jit(solution)/shard_map/ppermute | solution.py:34
  113.9 7.4 %collective-permute-start.21 = (bf16[16,4096]{1,0:T(8,128)(2,1)S(1)}, bf16[16,4096]{1,0:T(8,128)(2,1)S(1)}, u32[]{:S(2)}, u32[]{:S(2)}) collective-permute-start(bf16[16,4096]{1,0:T(8,128)(2,1)S(1)} %get-tuple-element.66), channel_id=1, source_target_pairs={{0,4},{1,5},{2,6},{3,7},{4,0},{5,1},{6,2},{7,3},{8,12},{9,13},{10,... | collective-permute-start | bytes 393224 | tf_op jit(solution)/shard_map/ppermute | solution.py:34
  114.0 7.4 %collective-permute-start.22 = (bf16[16,4096]{1,0:T(8,128)(2,1)S(1)}, bf16[16,4096]{1,0:T(8,128)(2,1)S(1)}, u32[]{:S(2)}, u32[]{:S(2)}) collective-permute-start(bf16[16,4096]{1,0:T(8,128)(2,1)S(1)} %get-tuple-element.67), channel_id=1, source_target_pairs={{0,2},{1,3},{2,4},{3,5},{4,6},{5,7},{6,0},{7,1},{8,10},{9,11},{10,... | collective-permute-start | bytes 393224 | tf_op jit(solution)/shard_map/ppermute | solution.py:34
  116.7 6.0 %collective-permute-start.24 = (bf16[16,4096]{1,0:T(8,128)(2,1)S(1)}, bf16[16,4096]{1,0:T(8,128)(2,1)S(1)}, u32[]{:S(2)}, u32[]{:S(2)}) collective-permute-start(bf16[16,4096]{1,0:T(8,128)(2,1)S(1)} %add_convert_fusion), channel_id=1, source_target_pairs={{0,6},{1,7},{2,0},{3,1},{4,2},{5,3},{6,4},{7,5},{8,14},{9,15},{10,... | collective-permute-start | bytes 393224 | tf_op jit(solution)/shard_map/ppermute | solution.py:34
  (1 other events, 0.7 us)

commit v7 on v6

--- a/solution.py
+++ b/solution.py
@@ -55,12 +55,14 @@
     for dz in range(1, tall):
         if tall != 4 or dz != 2:
             blocks[dz, 0] = shift(block, tall, wide, dz, 0)
-    blocks[1, 0] = tie([blocks[1, 0]], tokens)
+    for dy in range(1, wide):
+        blocks[0, dy] = shift(block, tall, wide, 0, dy)
+    blocks[1, 0] = tie([blocks[1, 0]], [*tokens, *(blocks[0, dy] for dy in range(1, wide))])
     if tall == 4:
         up = shift(blocks[1, 0], tall, wide, 1, 0, lambda z: z in (1, 2))
         down = shift(blocks[3, 0], tall, wide, -1, 0, lambda z: z in (1, 2))
         blocks[2, 0] = up + down
-    for dz in [0, 1, *range(tall - 1, 1, -1)]:
+    for dz in [1, *range(tall - 1, 1, -1)]:
         for dy in range(1, wide):
             blocks[dz, dy] = shift(blocks[dz, 0], tall, wide, 0, dy)
     return [blocks[dz, dy] for dz in range(tall) for dy in range(wide)]
@@ -101,11 +103,14 @@
                 out[place * share : (place + 1) * share, span] = rows(dz, dy)
 
 
-def scatter_sum(parts, tall, wide, tokens=()):
+def scatter_sum(parts, tall, wide, loads=()):
     share = parts[0].shape[0]
+    loaded = []
     crossed = [shift(p, tall, wide, 0, i // 2 + 1) for i, p in enumerate(parts[tall:])]
-    if tokens:
-        crossed[1] = tie([crossed[1]], tokens)
+    if loads:
+        *copy, token = load(parts[0], loads[0])
+        loaded += copy
+        crossed[1] = tie([crossed[1]], [token])
     total = None
     for which, group in enumerate(sum_order(tall)):
         for place, dz in enumerate(group):
@@ -114,9 +119,15 @@
                 other = crossed[2 * (dy - 1) + which]
                 lane = lane + other[place * share : (place + 1) * share].astype(f32)
             if dz:
-                lane = shift(lane.astype(bf16), tall, wide, dz, 0).astype(f32)
+                sent = lane.astype(bf16)
+                lane = shift(sent, tall, wide, dz, 0)
+                if loads and dz == tall - 1:
+                    *copy, token = load(sent, loads[1])
+                    loaded += copy
+                    lane = tie([lane], [token])
+                lane = lane.astype(f32)
             total = lane if total is None else total + lane
-    return total
+    return (total, *loaded) if loads else total
 
 
 def dot(a, b):
@@ -182,7 +193,12 @@
     return dot(onehot, values).astype(values.dtype)
 
 
-def send_body(me, routed, activations, outgoing):
+def send_body(me, routed_in, activations_in, outgoing, routed, activations, sems):
+    first_move = pltpu.make_async_copy(routed_in, routed, sems.at[0])
+    second_move = pltpu.make_async_copy(activations_in, activations, sems.at[1])
+    first_move.start()
+    second_move.start()
+    first_move.wait()
     capacity, tokens, total = outgoing.shape[0], activations.shape[0], routed.shape[1]
     low = (me[0] * tokens).astype(f32)
     where = routed[...].astype(f32)
@@ -192,6 +208,7 @@
     hit = slot == iota((capacity, total), 0)
     token = jnp.sum(jnp.where(hit, where - low + 1.0, 0.0), axis=1, keepdims=True) - 1.0
     onehot = jnp.where(token == iota((capacity, tokens), 1), 1.0, 0.0).astype(bf16)
+    second_move.wait()
     width = activations.shape[1]
     tile = tile_of(width, 1024)
     for start in range(0, width, tile):
@@ -376,13 +393,19 @@
     key_cols = w_key.shape[1]
     depth = key_cols // KV_HEADS
     scalar = pl.BlockSpec(memory_space=pltpu.SMEM)
+    in_hbm = pl.BlockSpec(memory_space=pl.ANY)
     routed, balance = routed.reshape(1, total), balance.reshape(1, total)
 
     (outgoing,) = kernel_call(
         send_body,
         [((capacity, model), bf16)],
-        [me, routed, activations],
-        specs=[scalar, VMEM, VMEM],
+        [me, from_hbm(routed), from_hbm(activations)],
+        [
+            pltpu.VMEM(routed.shape, i32),
+            pltpu.VMEM(activations.shape, bf16),
+            pltpu.SemaphoreType.DMA((2,)),
+        ],
+        specs=[scalar, in_hbm, in_hbm],
         flops=2 * capacity * tokens * model,
     )
     attn_gain, w_key, w_value, token_1 = load(
@@ -432,7 +455,6 @@
     )
     arrived = lax.all_to_all(sent.reshape(count, each, total), "ctx", 0, 0, tiled=True)
     arrived = arrived.reshape(count * each, total)
-    in_hbm = pl.BlockSpec(memory_space=pl.ANY)
     heads_wide = local_heads * HEAD_DIM
     (query,) = kernel_call(
         query_body,
@@ -455,14 +477,12 @@
         flops=2 * total * model * heads_wide,
         specs=[VMEM] * 7 + [in_hbm],
     )
-    w_down, token_5 = load(attn_parts[0], w_down)
-    attn_own = scatter_sum(attn_parts, tall, wide, [token_5])
+    attn_own, w_down, w_gate = scatter_sum(attn_parts, tall, wide, [w_down, w_gate])
     own_rows = own.astype(f32)
     hidden = own_rows + attn_own
     mean_sq = jnp.mean(hidden * hidden, axis=-1, keepdims=True)
     mnorm = (hidden * lax.rsqrt(mean_sq + norm_eps) * mlp_gain).astype(bf16)
     pieces = gather_blocks(mnorm, tall, wide)
-    w_gate, _ = load(mnorm, w_gate)
     w_up, _ = load(mnorm, w_up)
     hidden_units = w_gate.shape[1]
     mlp_parts = kernel_call(

time: 124 us -> 115 us (0.927)
  waiting for transfers between devices: 57.3 us -> 49.5 us
  local copies, waits for them, and re-layouts: 3.47 us -> 2.22 us
    ppermute x25, waiting for transfers between devices: 53.2 us -> 45.3 us  [shift(): return lax.ppermute(block, 'ctx', pairs)]
    unnamed x14 -> x12, local copies, waits for them, and re-layouts: 3.47 us -> 2.22 us
    pallas_call x8 -> x9, Pallas kernels: 12.7 us -> 13.9 us  [kernel_call(): pl.pallas_call(body, out_shape=[jax.ShapeDtypeStruct(s, d) for s, d in ou...]
  transfers between devices with their start and end apart: 26 -> 26, of which waited for: 17 -> 15; matrix products, arithmetic and copies ran while one was open for 1% -> 1% of each run, Pallas kernels for 13% -> 14%
where the time goes in v7:
time: 115 us
  waiting for transfers between devices  49.5 us (43%)
  starting transfers between devices  34.3 us (30%)
  Pallas kernels  26.3 us (23%)
  local copies, waits for them, and re-layouts  2.22 us (2%)
  other arithmetic  1.96 us (2%)
    ppermute x25, waiting for transfers between devices, shift(): return lax.ppermute(block, 'ctx', pairs)  45.3 us
    ppermute x25, starting transfers between devices, shift(): return lax.ppermute(block, 'ctx', pairs)  29.2 us
    pallas_call x9, Pallas kernels, kernel_call(): pl.pallas_call(body, out_shape=[jax.ShapeDtypeStruct(s, d) for s, d in ou...  13.9 us
    pallas_call x4, Pallas kernels, load(): pl.pallas_call(functools.partial(load_body, len(arrays)), out_shape=[pltp...  12.4 us
    all_to_all x1, starting transfers between devices, on_device(): lax.all_to_all(sent.reshape(count, each, total), 'ctx', 0, 0, tiled=True)  5.13 us
    all_to_all x1, waiting for transfers between devices, on_device(): lax.all_to_all(sent.reshape(count, each, total), 'ctx', 0, 0, tiled=True)  4.16 us
  transfers between devices with their start and end apart: 26, of which 15 were waited for; matrix products, arithmetic and copies ran while one was open for 1% of the time, Pallas kernels for 14%

profile of v7, /device:TPU:0, one launch (start us, length us, event | category | flops | bytes accessed | tf_op | source)
XLA Modules:
  0.0 114.5 jit_solution(25548299129685747)
XLA Ops:
  0.0 1.6 %shard_map.136.refs_0_ = bf16[32,4096]{1,0:T(8,128)(2,1)S(1)} custom-call(s32[1]{0:T(128)} %bitcast.me, s32[1,128]{1,0:T(1,128)} %bitcast.7, bf16[128,4096]{1,0:T(8,128)(2,1)} %activations_in.1), custom_call_target="tpu_custom_call" | custom-call | flops 33554432 | bytes 1048576 | tf_op jit(solution)/shard_map/pallas_call | solution.py:146
  1.6 5.1 %collective-permute-start.4 = (bf16[32,4096]{1,0:T(8,128)(2,1)S(1)}, bf16[32,4096]{1,0:T(8,128)(2,1)S(1)}, u32[]{:S(2)}, u32[]{:S(2)}) collective-permute-start(bf16[32,4096]{1,0:T(8,128)(2,1)S(1)} %shard_map.136.refs_0_), channel_id=1, source_target_pairs={{0,6},{1,7},{2,0},{3,1},{4,2},{5,3},{6,4},{7,5},{8,14},{9,15},{10,... | collective-permute-start | bytes 786440 | tf_op jit(solution)/shard_map/ppermute | solution.py:34
  11.0 1.6 %shard_map.137 = (f32[1,4096]{1,0:T(1,128)S(1)}, bf16[4096,128]{1,0:T(8,128)(2,1)S(1)}, bf16[4096,128]{1,0:T(8,128)(2,1)S(1)}, f32[8,128]{1,0:T(8,128)S(1)}) custom-call(bf16[32,4096]{1,0:T(8,128)(2,1)S(1)} %shard_map.136.refs_0_, f32[1,4096]{1,0:T(1,128)} %bitcast.11, bf16[4096,128]{1,0:T(8,128)(2,1)} %refs_2_.1, bf16[4096,128]{1,0:T(8,128)(2,1)} %refs_3_.1), custom_call_target="tpu_custom_call" | custom-call | bytes 4227072 | tf_op jit(solution)/shard_map/pallas_call | solution.py:171
  14.7 4.3 %collective-permute-done.1.refs_0_ = bf16[32,4096]{1,0:T(8,128)(2,1)S(1)} collective-permute-done((bf16[32,4096]{1,0:T(8,128)(2,1)S(1)}, bf16[32,4096]{1,0:T(8,128)(2,1)S(1)}, u32[]{:S(2)}, u32[]{:S(2)}) %collective-permute-start.1) | collective-permute-done | bytes 262176 | tf_op jit(solution)/shard_map/ppermute | solution.py:34
  19.7 1.6 %collective-permute-start.2 = (bf16[32,4096]{1,0:T(8,128)(2,1)S(1)}, bf16[32,4096]{1,0:T(8,128)(2,1)S(1)}, u32[]{:S(2)}, u32[]{:S(2)}) collective-permute-start(bf16[32,4096]{1,0:T(8,128)(2,1)S(1)} %shard_map.139.refs_2_), channel_id=1, source_target_pairs={{0,1},{1,0},{2,3},{3,2},{4,5},{5,4},{6,7},{7,6},{8,9},{9,8},{10,11... | collective-permute-start | bytes 786440 | tf_op jit(solution)/shard_map/ppermute | solution.py:34
  21.8 2.7 %collective-permute-done.5 = bf16[32,4096]{1,0:T(8,128)(2,1)S(1)} collective-permute-done((bf16[32,4096]{1,0:T(8,128)(2,1)S(1)}, bf16[32,4096]{1,0:T(8,128)(2,1)S(1)}, u32[]{:S(2)}, u32[]{:S(2)}) %collective-permute-start.5) | collective-permute-done | bytes 262176 | tf_op jit(solution)/shard_map/ppermute | solution.py:34
  24.5 1.5 %collective-permute-start.6 = (bf16[32,4096]{1,0:T(8,128)(2,1)S(1)}, bf16[32,4096]{1,0:T(8,128)(2,1)S(1)}, u32[]{:S(2)}, u32[]{:S(2)}) collective-permute-start(bf16[32,4096]{1,0:T(8,128)(2,1)S(1)} %add.62.refs_4_), channel_id=1, source_target_pairs={{0,1},{1,0},{2,3},{3,2},{4,5},{5,4},{6,7},{7,6},{8,9},{9,8},{10,11... | collective-permute-start | bytes 786440 | tf_op jit(solution)/shard_map/ppermute | solution.py:34
  26.5 8.1 %collective-permute-done.7.refs_7_ = bf16[32,4096]{1,0:T(8,128)(2,1)S(1)} collective-permute-done((bf16[32,4096]{1,0:T(8,128)(2,1)S(1)}, bf16[32,4096]{1,0:T(8,128)(2,1)S(1)}, u32[]{:S(2)}, u32[]{:S(2)}) %collective-permute-start.7) | collective-permute-done | bytes 262176 | tf_op jit(solution)/shard_map/ppermute | solution.py:34
  34.6 3.4 %collective-permute-done.6.refs_5_ = bf16[32,4096]{1,0:T(8,128)(2,1)S(1)} collective-permute-done((bf16[32,4096]{1,0:T(8,128)(2,1)S(1)}, bf16[32,4096]{1,0:T(8,128)(2,1)S(1)}, u32[]{:S(2)}, u32[]{:S(2)}) %collective-permute-start.6) | collective-permute-done | bytes 262176 | tf_op jit(solution)/shard_map/ppermute | solution.py:34
  38.0 2.4 %shard_map.140 = (bf16[128,4096]{1,0:T(8,128)(2,1)S(1)}, bf16[16,4096]{1,0:T(8,128)(2,1)S(1)}, bf16[256,128]{1,0:T(8,128)(2,1)}) custom-call(bf16[32,4096]{1,0:T(8,128)(2,1)S(1)} %shard_map.136.refs_0_, bf16[32,4096]{1,0:T(8,128)(2,1)S(1)} %collective-permute-done.refs_3_.refs_1_, bf16[32,4096]{1,0:T(8,128)(2,1)S(1)} %shard_map.139.refs_2_, ...), custom_call_target="tpu_custom_call" | custom-call | flops 536870912 | bytes 1048576 | tf_op jit(solution)/shard_map/pallas_call | solution.py:146
  40.4 5.1 %all-to-all-start = ((bf16[8,32,128]{2,1,0:T(8,128)(2,1)}), bf16[8,32,128]{2,1,0:T(8,128)(2,1)S(1)}, u32[]{:S(2)}, u32[]{:S(2)}) async-start(bf16[8,32,128]{2,1,0:T(8,128)(2,1)} %bitcast.4), calls=%async_computation | async-start | bytes 131072 | tf_op jit(solution)/shard_map/all_to_all | solution.py:456
  45.7 2.6 %shard_map.141.refs_1_ = bf16[128,512]{1,0:T(8,128)(2,1)S(1)} custom-call(bf16[128,4096]{1,0:T(8,128)(2,1)S(1)} %get-tuple-element.44.normed, bf16[4096,512]{1,0:T(8,128)(2,1)} %w_query.1, f32[128,128]{1,0:T(8,128)S(1)} %get-tuple-element.75.cosine, f32[128,128]{1,0:T(8,128)S(1)} %get-tuple-element.76.sine), custom_call_target="tpu_custom_call" | custom-call | flops 536870912 | bytes 1048576 | tf_op jit(solution)/shard_map/pallas_call | solution.py:146
  48.3 4.2 %all-to-all-done = bf16[8,32,128]{2,1,0:T(8,128)(2,1)S(1)} async-done(((bf16[8,32,128]{2,1,0:T(8,128)(2,1)}), bf16[8,32,128]{2,1,0:T(8,128)(2,1)S(1)}, u32[]{:S(2)}, u32[]{:S(2)}) %all-to-all-start) | async-done | bytes 65568 | tf_op jit(solution)/shard_map/all_to_all | solution.py:456
  52.5 3.1 %shard_map.142 = (bf16[16,4096]{1,0:T(8,128)(2,1)S(1)}, bf16[16,4096]{1,0:T(8,128)(2,1)S(1)}, bf16[16,4096]{1,0:T(8,128)(2,1)S(1)}, bf16[16,4096]{1,0:T(8,128)(2...) custom-call(bf16[256,128]{1,0:T(8,128)(2,1)S(1)} %bitcast.6, ...), custom_call_target="tpu_custom_call" | custom-call | flops 536870912 | bytes 1048576 | tf_op jit(solution)/shard_map/pallas_call | solution.py:146
  56.0 1.6 %collective-permute-start.8 = (bf16[32,4096]{1,0:T(8,128)(2,1)S(1)}, bf16[32,4096]{1,0:T(8,128)(2,1)S(1)}, u32[]{:S(2)}, u32[]{:S(2)}) collective-permute-start(bf16[32,4096]{1,0:T(8,128)(2,1)S(1)} %get-tuple-element.47), channel_id=1, source_target_pairs={{0,1},{1,0},{2,3},{3,2},{4,5},{5,4},{6,7},{7,6},{8,9},{9,8},{10,11... | collective-permute-start | bytes 786440 | tf_op jit(solution)/shard_map/ppermute | solution.py:34
  57.6 3.4 %shard_map.143 = (bf16[1024,4096]{1,0:T(8,128)(2,1)S(1)}, f32[8,128]{1,0:T(8,128)S(1)}) custom-call(bf16[16,4096]{1,0:T(8,128)(2,1)S(1)} %get-tuple-element.51.refs_0_, bf16[1024,4096]{1,0:T(8,128)(2,1)} %refs_1_.3), custom_call_target="tpu_custom_call" | custom-call | bytes 16777216 | tf_op jit(solution)/shard_map/pallas_call | solution.py:171
  61.0 1.6 %collective-permute-done.11.refs_0_ = bf16[32,4096]{1,0:T(8,128)(2,1)S(1)} collective-permute-done((bf16[32,4096]{1,0:T(8,128)(2,1)S(1)}, bf16[32,4096]{1,0:T(8,128)(2,1)S(1)}, u32[]{:S(2)}, u32[]{:S(2)}) %collective-permute-start.11) | collective-permute-done | bytes 262176 | tf_op jit(solution)/shard_map/ppermute | solution.py:34
  63.3 2.1 %collective-permute-done.8 = bf16[32,4096]{1,0:T(8,128)(2,1)S(1)} collective-permute-done((bf16[32,4096]{1,0:T(8,128)(2,1)S(1)}, bf16[32,4096]{1,0:T(8,128)(2,1)S(1)}, u32[]{:S(2)}, u32[]{:S(2)}) %collective-permute-start.8) | collective-permute-done | bytes 262176 | tf_op jit(solution)/shard_map/ppermute | solution.py:34
  66.7 3.4 %shard_map.145 = (bf16[4096,1024]{1,0:T(8,128)(2,1)S(1)}, f32[8,128]{1,0:T(8,128)S(1)}) custom-call(bf16[16,4096]{1,0:T(8,128)(2,1)S(1)} %add_convert_fusion.3.refs_0_, bf16[4096,1024]{1,0:T(8,128)(2,1)} %refs_1_.4), custom_call_target="tpu_custom_call" | custom-call | bytes 16777216 | tf_op jit(solution)/shard_map/pallas_call | solution.py:171
  70.1 7.9 %collective-permute-done.9 = bf16[16,4096]{1,0:T(8,128)(2,1)S(1)} collective-permute-done((bf16[16,4096]{1,0:T(8,128)(2,1)S(1)}, bf16[16,4096]{1,0:T(8,128)(2,1)S(1)}, u32[]{:S(2)}, u32[]{:S(2)}) %collective-permute-start.9) | collective-permute-done | bytes 131104 | tf_op jit(solution)/shard_map/ppermute | solution.py:34
  78.6 1.9 %collective-permute-start.14 = (bf16[16,4096]{1,0:T(8,128)(2,1)S(1)}, bf16[16,4096]{1,0:T(8,128)(2,1)S(1)}, u32[]{:S(2)}, u32[]{:S(2)}) collective-permute-start(bf16[16,4096]{1,0:T(8,128)(2,1)S(1)} %multiply_convert_fusion.refs_0_), channel_id=1, source_target_pairs={{0,2},{1,3},{2,4},{3,5},{4,6},{5,7},{6,0},{7,1},{8,10},{9,11},{10,... | collective-permute-start | bytes 393224 | tf_op jit(solution)/shard_map/ppermute | solution.py:34
  80.7 4.1 %collective-permute-done.18.refs_6_ = bf16[16,4096]{1,0:T(8,128)(2,1)S(1)} collective-permute-done((bf16[16,4096]{1,0:T(8,128)(2,1)S(1)}, bf16[16,4096]{1,0:T(8,128)(2,1)S(1)}, u32[]{:S(2)}, u32[]{:S(2)}) %collective-permute-start.18) | collective-permute-done | bytes 131104 | tf_op jit(solution)/shard_map/ppermute | solution.py:34
  84.9 2.0 %collective-permute-start.17 = (bf16[16,4096]{1,0:T(8,128)(2,1)S(1)}, bf16[16,4096]{1,0:T(8,128)(2,1)S(1)}, u32[]{:S(2)}, u32[]{:S(2)}) collective-permute-start(bf16[16,4096]{1,0:T(8,128)(2,1)S(1)} %collective-permute-done.16.refs_4_), channel_id=1, source_target_pairs={{0,1},{1,0},{2,3},{3,2},{4,5},{5,4},{6,7},{7,6},{8,9},{9,8},{10,11... | collective-permute-start | bytes 393224 | tf_op jit(solution)/shard_map/ppermute | solution.py:34
  87.3 4.0 %shard_map.147 = (bf16[4096,1024]{1,0:T(8,128)(2,1)S(1)}, f32[8,128]{1,0:T(8,128)}) custom-call(bf16[16,4096]{1,0:T(8,128)(2,1)S(1)} %multiply_convert_fusion.refs_0_, bf16[4096,1024]{1,0:T(8,128)(2,1)} %refs_1_.5), custom_call_target="tpu_custom_call" | custom-call | bytes 16777216 | tf_op jit(solution)/shard_map/pallas_call | solution.py:171
  91.3 2.1 %collective-permute-done.15.refs_3_ = bf16[16,4096]{1,0:T(8,128)(2,1)S(1)} collective-permute-done((bf16[16,4096]{1,0:T(8,128)(2,1)S(1)}, bf16[16,4096]{1,0:T(8,128)(2,1)S(1)}, u32[]{:S(2)}, u32[]{:S(2)}) %collective-permute-start.15) | collective-permute-done | bytes 131104 | tf_op jit(solution)/shard_map/ppermute | solution.py:34
  93.4 3.6 %shard_map.148 = (bf16[16,4096]{1,0:T(8,128)(2,1)S(1)}, bf16[16,4096]{1,0:T(8,128)(2,1)S(1)}, bf16[16,4096]{1,0:T(8,128)(2,1)S(1)}, bf16[16,4096]{1,0:T(8,128)(2...) custom-call(bf16[16,4096]{1,0:T(8,128)(2,1)S(1)} %multiply_convert_fusion.refs_0_, ...), custom_call_target="tpu_custom_call" | custom-call | flops 3221225472 | bytes 1048576 | tf_op jit(solution)/shard_map/pallas_call | solution.py:146
  97.2 2.0 %collective-permute-start.23 = (bf16[32,4096]{1,0:T(8,128)(2,1)S(1)}, bf16[32,4096]{1,0:T(8,128)(2,1)S(1)}, u32[]{:S(2)}, u32[]{:S(2)}) collective-permute-start(bf16[32,4096]{1,0:T(8,128)(2,1)S(1)} %get-tuple-element.61), channel_id=1, source_target_pairs={{0,1},{1,0},{2,3},{3,2},{4,5},{5,4},{6,7},{7,6},{8,9},{9,8},{10,11... | collective-permute-start | bytes 786440 | tf_op jit(solution)/shard_map/ppermute | solution.py:34
  99.2 4.3 %collective-permute-done.20 = bf16[32,4096]{1,0:T(8,128)(2,1)S(1)} collective-permute-done((bf16[32,4096]{1,0:T(8,128)(2,1)S(1)}, bf16[32,4096]{1,0:T(8,128)(2,1)S(1)}, u32[]{:S(2)}, u32[]{:S(2)}) %collective-permute-start.20) | collective-permute-done | bytes 262176 | tf_op jit(solution)/shard_map/ppermute | solution.py:34
  103.6 1.6 %collective-permute-start.21 = (bf16[16,4096]{1,0:T(8,128)(2,1)S(1)}, bf16[16,4096]{1,0:T(8,128)(2,1)S(1)}, u32[]{:S(2)}, u32[]{:S(2)}) collective-permute-start(bf16[16,4096]{1,0:T(8,128)(2,1)S(1)} %get-tuple-element.68), channel_id=1, source_target_pairs={{0,4},{1,5},{2,6},{3,7},{4,0},{5,1},{6,2},{7,3},{8,12},{9,13},{10,... | collective-permute-start | bytes 393224 | tf_op jit(solution)/shard_map/ppermute | solution.py:34
  105.2 2.9 %collective-permute-start.22 = (bf16[16,4096]{1,0:T(8,128)(2,1)S(1)}, bf16[16,4096]{1,0:T(8,128)(2,1)S(1)}, u32[]{:S(2)}, u32[]{:S(2)}) collective-permute-start(bf16[16,4096]{1,0:T(8,128)(2,1)S(1)} %get-tuple-element.69), channel_id=1, source_target_pairs={{0,2},{1,3},{2,4},{3,5},{4,6},{5,7},{6,0},{7,1},{8,10},{9,11},{10,... | collective-permute-start | bytes 393224 | tf_op jit(solution)/shard_map/ppermute | solution.py:34
  108.2 2.2 %collective-permute-start.24 = (bf16[16,4096]{1,0:T(8,128)(2,1)S(1)}, bf16[16,4096]{1,0:T(8,128)(2,1)S(1)}, u32[]{:S(2)}, u32[]{:S(2)}) collective-permute-start(bf16[16,4096]{1,0:T(8,128)(2,1)S(1)} %add_convert_fusion), channel_id=1, source_target_pairs={{0,6},{1,7},{2,0},{3,1},{4,2},{5,3},{6,4},{7,5},{8,14},{9,15},{10,... | collective-permute-start | bytes 393224 | tf_op jit(solution)/shard_map/ppermute | solution.py:34
  110.4 2.0 %collective-permute-done.21 = bf16[16,4096]{1,0:T(8,128)(2,1)S(1)} collective-permute-done((bf16[16,4096]{1,0:T(8,128)(2,1)S(1)}, bf16[16,4096]{1,0:T(8,128)(2,1)S(1)}, u32[]{:S(2)}, u32[]{:S(2)}) %collective-permute-start.21) | collective-permute-done | bytes 131104 | tf_op jit(solution)/shard_map/ppermute | solution.py:34
  (59 shorter events, 14.1 us)
Async XLA Ops:
  0.0 52.5 %copy-start.2 = (s32[128]{0:T(128)S(1)}, s32[128]{0:T(128)}, u32[]{:S(2)}) copy-start(s32[128]{0:T(128)} %param.15) | copy-start | bytes 1540
  1.6 11.8 %collective-permute-start.4 = (bf16[32,4096]{1,0:T(8,128)(2,1)S(1)}, bf16[32,4096]{1,0:T(8,128)(2,1)S(1)}, u32[]{:S(2)}, u32[]{:S(2)}) collective-permute-start(bf16[32,4096]{1,0:T(8,128)(2,1)S(1)} %shard_map.136.refs_0_), channel_id=1, source_target_pairs={{0,6},{1,7},{2,0},{3,1},{4,2},{5,3},{6,4},{7,5},{8,14},{9,15},{10,... | collective-permute-start | bytes 786440 | tf_op jit(solution)/shard_map/ppermute | solution.py:34
  6.7 12.3 %collective-permute-start.1 = (bf16[32,4096]{1,0:T(8,128)(2,1)S(1)}, bf16[32,4096]{1,0:T(8,128)(2,1)S(1)}, u32[]{:S(2)}, u32[]{:S(2)}) collective-permute-start(bf16[32,4096]{1,0:T(8,128)(2,1)S(1)} %shard_map.136.refs_0_), channel_id=1, source_target_pairs={{0,2},{1,3},{2,4},{3,5},{4,6},{5,7},{6,0},{7,1},{8,10},{9,11},{10,... | collective-permute-start | bytes 786440 | tf_op jit(solution)/shard_map/ppermute | solution.py:34
  6.7 12.3 %collective-permute-start = (bf16[32,4096]{1,0:T(8,128)(2,1)S(1)}, bf16[32,4096]{1,0:T(8,128)(2,1)S(1)}, u32[]{:S(2)}, u32[]{:S(2)}) collective-permute-start(bf16[32,4096]{1,0:T(8,128)(2,1)S(1)} %shard_map.136.refs_0_), channel_id=1, source_target_pairs={{0,1},{1,0},{2,3},{3,2},{4,5},{5,4},{6,7},{7,6},{8,9},{9,8},{10,11... | collective-permute-start | bytes 786440 | tf_op jit(solution)/shard_map/ppermute | solution.py:34
  8.2 0.9 copy-start
  9.1 0.7 copy-start.1
  9.7 0.7 copy-start.3
  13.4 11.1 %collective-permute-start.5 = (bf16[32,4096]{1,0:T(8,128)(2,1)S(1)}, bf16[32,4096]{1,0:T(8,128)(2,1)S(1)}, u32[]{:S(2)}, u32[]{:S(2)}) collective-permute-start(bf16[32,4096]{1,0:T(8,128)(2,1)S(1)} %collective-permute-done.4.refs_6_), channel_id=1, source_target_pairs={{2,0},{3,1},{4,2},{5,3},{10,8},{11,9},{12,10},{13,11},{18,16},{19,... | collective-permute-start | bytes 786440 | tf_op jit(solution)/shard_map/ppermute | solution.py:34
  19.0 5.5 %collective-permute-start.3 = (bf16[32,4096]{1,0:T(8,128)(2,1)S(1)}, bf16[32,4096]{1,0:T(8,128)(2,1)S(1)}, u32[]{:S(2)}, u32[]{:S(2)}) collective-permute-start(bf16[32,4096]{1,0:T(8,128)(2,1)S(1)} %shard_map.139.refs_2_), channel_id=1, source_target_pairs={{2,4},{3,5},{4,6},{5,7},{10,12},{11,13},{12,14},{13,15},{18,20},{1... | collective-permute-start | bytes 786440 | tf_op jit(solution)/shard_map/ppermute | solution.py:34
  19.7 14.9 %collective-permute-start.2 = (bf16[32,4096]{1,0:T(8,128)(2,1)S(1)}, bf16[32,4096]{1,0:T(8,128)(2,1)S(1)}, u32[]{:S(2)}, u32[]{:S(2)}) collective-permute-start(bf16[32,4096]{1,0:T(8,128)(2,1)S(1)} %shard_map.139.refs_2_), channel_id=1, source_target_pairs={{0,1},{1,0},{2,3},{3,2},{4,5},{5,4},{6,7},{7,6},{8,9},{9,8},{10,11... | collective-permute-start | bytes 786440 | tf_op jit(solution)/shard_map/ppermute | solution.py:34
  21.2 13.4 %collective-permute-start.7 = (bf16[32,4096]{1,0:T(8,128)(2,1)S(1)}, bf16[32,4096]{1,0:T(8,128)(2,1)S(1)}, u32[]{:S(2)}, u32[]{:S(2)}) collective-permute-start(bf16[32,4096]{1,0:T(8,128)(2,1)S(1)} %collective-permute-done.4.refs_6_), channel_id=1, source_target_pairs={{0,1},{1,0},{2,3},{3,2},{4,5},{5,4},{6,7},{7,6},{8,9},{9,8},{10,11... | collective-permute-start | bytes 786440 | tf_op jit(solution)/shard_map/ppermute | solution.py:34
  24.5 13.5 %collective-permute-start.6 = (bf16[32,4096]{1,0:T(8,128)(2,1)S(1)}, bf16[32,4096]{1,0:T(8,128)(2,1)S(1)}, u32[]{:S(2)}, u32[]{:S(2)}) collective-permute-start(bf16[32,4096]{1,0:T(8,128)(2,1)S(1)} %add.62.refs_4_), channel_id=1, source_target_pairs={{0,1},{1,0},{2,3},{3,2},{4,5},{5,4},{6,7},{7,6},{8,9},{9,8},{10,11... | collective-permute-start | bytes 786440 | tf_op jit(solution)/shard_map/ppermute | solution.py:34
  40.4 12.0 %all-to-all-start = ((bf16[8,32,128]{2,1,0:T(8,128)(2,1)}), bf16[8,32,128]{2,1,0:T(8,128)(2,1)S(1)}, u32[]{:S(2)}, u32[]{:S(2)}) async-start(bf16[8,32,128]{2,1,0:T(8,128)(2,1)} %bitcast.4), calls=%async_computation | async-start | bytes 131072 | tf_op jit(solution)/shard_map/all_to_all | solution.py:456
  55.5 7.1 %collective-permute-start.11 = (bf16[32,4096]{1,0:T(8,128)(2,1)S(1)}, bf16[32,4096]{1,0:T(8,128)(2,1)S(1)}, u32[]{:S(2)}, u32[]{:S(2)}) collective-permute-start(bf16[32,4096]{1,0:T(8,128)(2,1)S(1)} %get-tuple-element.50), channel_id=1, source_target_pairs={{0,1},{1,0},{2,3},{3,2},{4,5},{5,4},{6,7},{7,6},{8,9},{9,8},{10,11... | collective-permute-start | bytes 786440 | tf_op jit(solution)/shard_map/ppermute | solution.py:34
  56.0 9.4 %collective-permute-start.8 = (bf16[32,4096]{1,0:T(8,128)(2,1)S(1)}, bf16[32,4096]{1,0:T(8,128)(2,1)S(1)}, u32[]{:S(2)}, u32[]{:S(2)}) collective-permute-start(bf16[32,4096]{1,0:T(8,128)(2,1)S(1)} %get-tuple-element.47), channel_id=1, source_target_pairs={{0,1},{1,0},{2,3},{3,2},{4,5},{5,4},{6,7},{7,6},{8,9},{9,8},{10,11... | collective-permute-start | bytes 786440 | tf_op jit(solution)/shard_map/ppermute | solution.py:34
  57.6 20.4 %copy-start.4 = (f32[4096]{0:T(1024)S(1)}, f32[4096]{0:T(1024)}, u32[]{:S(2)}) copy-start(f32[4096]{0:T(1024)} %param.26) | copy-start | bytes 49156
  57.6 20.7 %copy-start.5 = (f32[4096]{0:T(1024)S(1)}, f32[4096]{0:T(1024)}, u32[]{:S(2)}) copy-start(f32[4096]{0:T(1024)} %param.22) | copy-start | bytes 49156
  62.7 7.4 %collective-permute-start.12 = (bf16[16,4096]{1,0:T(8,128)(2,1)S(1)}, bf16[16,4096]{1,0:T(8,128)(2,1)S(1)}, u32[]{:S(2)}, u32[]{:S(2)}) collective-permute-start(bf16[16,4096]{1,0:T(8,128)(2,1)S(1)} %add_convert_fusion.3.refs_0_), channel_id=1, source_target_pairs={{0,6},{1,7},{2,0},{3,1},{4,2},{5,3},{6,4},{7,5},{8,14},{9,15},{10,... | collective-permute-start | bytes 393224 | tf_op jit(solution)/shard_map/ppermute | solution.py:34
  65.5 12.6 %collective-permute-start.9 = (bf16[16,4096]{1,0:T(8,128)(2,1)S(1)}, bf16[16,4096]{1,0:T(8,128)(2,1)S(1)}, u32[]{:S(2)}, u32[]{:S(2)}) collective-permute-start(bf16[16,4096]{1,0:T(8,128)(2,1)S(1)} %get-tuple-element.70), channel_id=1, source_target_pairs={{0,4},{1,5},{2,6},{3,7},{4,0},{5,1},{6,2},{7,3},{8,12},{9,13},{10,... | collective-permute-start | bytes 393224 | tf_op jit(solution)/shard_map/ppermute | solution.py:34
  66.0 12.0 %collective-permute-start.10 = (bf16[16,4096]{1,0:T(8,128)(2,1)S(1)}, bf16[16,4096]{1,0:T(8,128)(2,1)S(1)}, u32[]{:S(2)}, u32[]{:S(2)}) collective-permute-start(bf16[16,4096]{1,0:T(8,128)(2,1)S(1)} %get-tuple-element.71), channel_id=1, source_target_pairs={{0,2},{1,3},{2,4},{3,5},{4,6},{5,7},{6,0},{7,1},{8,10},{9,11},{10,... | collective-permute-start | bytes 393224 | tf_op jit(solution)/shard_map/ppermute | solution.py:34
  78.4 6.4 %collective-permute-start.18 = (bf16[16,4096]{1,0:T(8,128)(2,1)S(1)}, bf16[16,4096]{1,0:T(8,128)(2,1)S(1)}, u32[]{:S(2)}, u32[]{:S(2)}) collective-permute-start(bf16[16,4096]{1,0:T(8,128)(2,1)S(1)} %multiply_convert_fusion.refs_0_), channel_id=1, source_target_pairs={{0,6},{1,7},{2,0},{3,1},{4,2},{5,3},{6,4},{7,5},{8,14},{9,15},{10,... | collective-permute-start | bytes 393224 | tf_op jit(solution)/shard_map/ppermute | solution.py:34
  78.5 6.4 %collective-permute-start.16 = (bf16[16,4096]{1,0:T(8,128)(2,1)S(1)}, bf16[16,4096]{1,0:T(8,128)(2,1)S(1)}, u32[]{:S(2)}, u32[]{:S(2)}) collective-permute-start(bf16[16,4096]{1,0:T(8,128)(2,1)S(1)} %multiply_convert_fusion.refs_0_), channel_id=1, source_target_pairs={{0,4},{1,5},{2,6},{3,7},{4,0},{5,1},{6,2},{7,3},{8,12},{9,13},{10,... | collective-permute-start | bytes 393224 | tf_op jit(solution)/shard_map/ppermute | solution.py:34
  78.6 8.7 %collective-permute-start.14 = (bf16[16,4096]{1,0:T(8,128)(2,1)S(1)}, bf16[16,4096]{1,0:T(8,128)(2,1)S(1)}, u32[]{:S(2)}, u32[]{:S(2)}) collective-permute-start(bf16[16,4096]{1,0:T(8,128)(2,1)S(1)} %multiply_convert_fusion.refs_0_), channel_id=1, source_target_pairs={{0,2},{1,3},{2,4},{3,5},{4,6},{5,7},{6,0},{7,1},{8,10},{9,11},{10,... | collective-permute-start | bytes 393224 | tf_op jit(solution)/shard_map/ppermute | solution.py:34
  80.5 10.8 %collective-permute-start.13 = (bf16[16,4096]{1,0:T(8,128)(2,1)S(1)}, bf16[16,4096]{1,0:T(8,128)(2,1)S(1)}, u32[]{:S(2)}, u32[]{:S(2)}) collective-permute-start(bf16[16,4096]{1,0:T(8,128)(2,1)S(1)} %multiply_convert_fusion.refs_0_), channel_id=1, source_target_pairs={{0,1},{1,0},{2,3},{3,2},{4,5},{5,4},{6,7},{7,6},{8,9},{9,8},{10,11... | collective-permute-start | bytes 393224 | tf_op jit(solution)/shard_map/ppermute | solution.py:34
  84.9 6.4 %collective-permute-start.19 = (bf16[16,4096]{1,0:T(8,128)(2,1)S(1)}, bf16[16,4096]{1,0:T(8,128)(2,1)S(1)}, u32[]{:S(2)}, u32[]{:S(2)}) collective-permute-start(bf16[16,4096]{1,0:T(8,128)(2,1)S(1)} %collective-permute-done.18.refs_6_), channel_id=1, source_target_pairs={{0,1},{1,0},{2,3},{3,2},{4,5},{5,4},{6,7},{7,6},{8,9},{9,8},{10,11... | collective-permute-start | bytes 393224 | tf_op jit(solution)/shard_map/ppermute | solution.py:34
  84.9 6.4 %collective-permute-start.17 = (bf16[16,4096]{1,0:T(8,128)(2,1)S(1)}, bf16[16,4096]{1,0:T(8,128)(2,1)S(1)}, u32[]{:S(2)}, u32[]{:S(2)}) collective-permute-start(bf16[16,4096]{1,0:T(8,128)(2,1)S(1)} %collective-permute-done.16.refs_4_), channel_id=1, source_target_pairs={{0,1},{1,0},{2,3},{3,2},{4,5},{5,4},{6,7},{7,6},{8,9},{9,8},{10,11... | collective-permute-start | bytes 393224 | tf_op jit(solution)/shard_map/ppermute | solution.py:34
  87.3 6.1 %collective-permute-start.15 = (bf16[16,4096]{1,0:T(8,128)(2,1)S(1)}, bf16[16,4096]{1,0:T(8,128)(2,1)S(1)}, u32[]{:S(2)}, u32[]{:S(2)}) collective-permute-start(bf16[16,4096]{1,0:T(8,128)(2,1)S(1)} %collective-permute-done.14.refs_2_), channel_id=1, source_target_pairs={{0,1},{1,0},{2,3},{3,2},{4,5},{5,4},{6,7},{7,6},{8,9},{9,8},{10,11... | collective-permute-start | bytes 393224 | tf_op jit(solution)/shard_map/ppermute | solution.py:34
  97.1 6.4 %collective-permute-start.20 = (bf16[32,4096]{1,0:T(8,128)(2,1)S(1)}, bf16[32,4096]{1,0:T(8,128)(2,1)S(1)}, u32[]{:S(2)}, u32[]{:S(2)}) collective-permute-start(bf16[32,4096]{1,0:T(8,128)(2,1)S(1)} %get-tuple-element.58), channel_id=1, source_target_pairs={{0,1},{1,0},{2,3},{3,2},{4,5},{5,4},{6,7},{7,6},{8,9},{9,8},{10,11... | collective-permute-start | bytes 786440 | tf_op jit(solution)/shard_map/ppermute | solution.py:34
  97.2 11.0 %collective-permute-start.23 = (bf16[32,4096]{1,0:T(8,128)(2,1)S(1)}, bf16[32,4096]{1,0:T(8,128)(2,1)S(1)}, u32[]{:S(2)}, u32[]{:S(2)}) collective-permute-start(bf16[32,4096]{1,0:T(8,128)(2,1)S(1)} %get-tuple-element.61), channel_id=1, source_target_pairs={{0,1},{1,0},{2,3},{3,2},{4,5},{5,4},{6,7},{7,6},{8,9},{9,8},{10,11... | collective-permute-start | bytes 786440 | tf_op jit(solution)/shard_map/ppermute | solution.py:34
  103.6 8.8 %collective-permute-start.21 = (bf16[16,4096]{1,0:T(8,128)(2,1)S(1)}, bf16[16,4096]{1,0:T(8,128)(2,1)S(1)}, u32[]{:S(2)}, u32[]{:S(2)}) collective-permute-start(bf16[16,4096]{1,0:T(8,128)(2,1)S(1)} %get-tuple-element.68), channel_id=1, source_target_pairs={{0,4},{1,5},{2,6},{3,7},{4,0},{5,1},{6,2},{7,3},{8,12},{9,13},{10,... | collective-permute-start | bytes 393224 | tf_op jit(solution)/shard_map/ppermute | solution.py:34
  105.2 7.2 %collective-permute-start.22 = (bf16[16,4096]{1,0:T(8,128)(2,1)S(1)}, bf16[16,4096]{1,0:T(8,128)(2,1)S(1)}, u32[]{:S(2)}, u32[]{:S(2)}) collective-permute-start(bf16[16,4096]{1,0:T(8,128)(2,1)S(1)} %get-tuple-element.69), channel_id=1, source_target_pairs={{0,2},{1,3},{2,4},{3,5},{4,6},{5,7},{6,0},{7,1},{8,10},{9,11},{10,... | collective-permute-start | bytes 393224 | tf_op jit(solution)/shard_map/ppermute | solution.py:34
  108.2 5.5 %collective-permute-start.24 = (bf16[16,4096]{1,0:T(8,128)(2,1)S(1)}, bf16[16,4096]{1,0:T(8,128)(2,1)S(1)}, u32[]{:S(2)}, u32[]{:S(2)}) collective-permute-start(bf16[16,4096]{1,0:T(8,128)(2,1)S(1)} %add_convert_fusion), channel_id=1, source_target_pairs={{0,6},{1,7},{2,0},{3,1},{4,2},{5,3},{6,4},{7,5},{8,14},{9,15},{10,... | collective-permute-start | bytes 393224 | tf_op jit(solution)/shard_map/ppermute | solution.py:34

commit v8 on v7

--- a/solution.py
+++ b/solution.py
@@ -20,13 +20,15 @@
 
 
 def plane_of(count):
-    wide = max(y for y in range(1, count + 1) if count % y == 0 and 2 * y * y <= max(count, 2))
+    wide = 1
+    while 8 * wide * wide <= count:
+        wide *= 2
     return count // wide, wide
 
 
-def shift(block, tall, wide, dz, dy, keep=None):
+def swap(block, tall, wide, kz, ky, keep=None):
     pairs = [
-        (z * wide + y, (z + dz) % tall * wide + (y + dy) % wide)
+        (z * wide + y, (z ^ kz) * wide + (y ^ ky))
         for z in range(tall)
         for y in range(wide)
         if keep is None or keep(z)
@@ -52,32 +54,40 @@
 
 def gather_rows(block, tall, wide, tokens):
     blocks = {(0, 0): block}
-    for dz in range(1, tall):
-        if tall != 4 or dz != 2:
-            blocks[dz, 0] = shift(block, tall, wide, dz, 0)
-    for dy in range(1, wide):
-        blocks[0, dy] = shift(block, tall, wide, 0, dy)
-    blocks[1, 0] = tie([blocks[1, 0]], [*tokens, *(blocks[0, dy] for dy in range(1, wide))])
+    for ky in range(1, wide):
+        blocks[0, ky] = swap(block, tall, wide, 0, ky)
+    first = [*tokens, *(blocks[0, ky] for ky in range(1, wide))]
     if tall == 4:
-        up = shift(blocks[1, 0], tall, wide, 1, 0, lambda z: z in (1, 2))
-        down = shift(blocks[3, 0], tall, wide, -1, 0, lambda z: z in (1, 2))
-        blocks[2, 0] = up + down
-    for dz in [1, *range(tall - 1, 1, -1)]:
-        for dy in range(1, wide):
-            blocks[dz, dy] = shift(blocks[dz, 0], tall, wide, 0, dy)
-    return [blocks[dz, dy] for dz in range(tall) for dy in range(wide)]
+        blocks[1, 0] = tie([swap(block, tall, wide, 1, 0)], first)
+        blocks[3, 0] = swap(block, tall, wide, 3, 0)
+        inner = swap(blocks[1, 0], tall, wide, 3, 0, lambda z: z in (1, 2))
+        outer = swap(blocks[3, 0], tall, wide, 1, 0, lambda z: z in (1, 2))
+        for ky in range(1, wide):
+            blocks[1, ky] = swap(blocks[1, 0], tall, wide, 0, ky)
+            blocks[3, ky] = swap(blocks[3, 0], tall, wide, 0, ky)
+        blocks[2, 0] = tie([inner, outer], [blocks[1, ky] for ky in range(1, wide)])
+        rest = [2]
+    else:
+        for kz in range(1, tall):
+            blocks[kz, 0] = swap(block, tall, wide, kz, 0)
+        blocks[1, 0] = tie([blocks[1, 0]], first)
+        rest = range(1, tall)
+    for kz in rest:
+        for ky in range(1, wide):
+            blocks[kz, ky] = swap(blocks[kz, 0], tall, wide, 0, ky)
+    return [blocks[kz, ky] for kz in range(tall) for ky in range(wide)]
 
 
 def gather_blocks(block, tall, wide):
-    blocks = {(dz, 0): shift(block, tall, wide, dz, 0) if dz else block for dz in range(tall)}
-    for dz in range(tall):
-        for dy in range(1, wide):
-            blocks[dz, dy] = shift(blocks[dz, 0], tall, wide, 0, dy)
-    return [blocks[dz, dy] for dz in range(tall) for dy in range(wide)]
+    blocks = {(kz, 0): swap(block, tall, wide, kz, 0) if kz else block for kz in range(tall)}
+    for kz in range(tall):
+        for ky in range(1, wide):
+            blocks[kz, ky] = swap(blocks[kz, 0], tall, wide, 0, ky)
+    return [blocks[kz, ky] for kz in range(tall) for ky in range(wide)]
 
 
 def sum_order(tall):
-    order = [tall // 2, *range(1, tall // 2), *range(tall // 2 + 1, tall), 0]
+    order = [*range(tall - 1, -1, -1)]
     return order[: tall // 2], order[tall // 2 :]
 
 
@@ -86,42 +96,41 @@
     return kept + [((tall // 2 * share, model), bf16)] * (2 * (wide - 1))
 
 
-def store_parts(parts, tall, wide, span, product, back):
+def store_parts(parts, tall, wide, span, product):
     share = parts[0].shape[0]
-    sign = -1 if back else 1
-
-    def rows(dz, dy):
-        at = sign * dz % tall * wide + sign * dy % wide
+
+    def rows(kz, ky):
+        at = kz * wide + ky
         return product[at * share : (at + 1) * share, :]
 
-    for dz in range(tall):
-        parts[dz][:, span] = rows(dz, 0)
-    for dy in range(1, wide):
+    for kz in range(tall):
+        parts[kz][:, span] = rows(kz, 0)
+    for ky in range(1, wide):
         for which, group in enumerate(sum_order(tall)):
-            out = parts[tall + 2 * (dy - 1) + which]
-            for place, dz in enumerate(group):
-                out[place * share : (place + 1) * share, span] = rows(dz, dy)
+            out = parts[tall + 2 * (ky - 1) + which]
+            for place, kz in enumerate(group):
+                out[place * share : (place + 1) * share, span] = rows(kz, ky)
 
 
 def scatter_sum(parts, tall, wide, loads=()):
     share = parts[0].shape[0]
     loaded = []
-    crossed = [shift(p, tall, wide, 0, i // 2 + 1) for i, p in enumerate(parts[tall:])]
+    crossed = [swap(p, tall, wide, 0, i // 2 + 1) for i, p in enumerate(parts[tall:])]
     if loads:
         *copy, token = load(parts[0], loads[0])
         loaded += copy
-        crossed[1] = tie([crossed[1]], [token])
+        crossed[0] = tie([crossed[0]], [token])
     total = None
     for which, group in enumerate(sum_order(tall)):
-        for place, dz in enumerate(group):
-            lane = parts[dz].astype(f32)
-            for dy in range(1, wide):
-                other = crossed[2 * (dy - 1) + which]
+        for place, kz in enumerate(group):
+            lane = parts[kz].astype(f32)
+            for ky in range(1, wide):
+                other = crossed[2 * (ky - 1) + which]
                 lane = lane + other[place * share : (place + 1) * share].astype(f32)
-            if dz:
+            if kz:
                 sent = lane.astype(bf16)
-                lane = shift(sent, tall, wide, dz, 0)
-                if loads and dz == tall - 1:
+                lane = swap(sent, tall, wide, kz, 0)
+                if loads and kz == 1:
                     *copy, token = load(sent, loads[1])
                     loaded += copy
                     lane = tie([lane], [token])
@@ -229,14 +238,13 @@
     in_base, in_source = notes[:inbound, 2:3], notes[:inbound, 3:4]
     for s in range(count):
         z, y = divmod(s, wide)
-        from_block = lax.rem(my_z - z + tall, tall) * wide + lax.rem(my_y - y + wide, wide)
-        to_block = lax.rem(z - my_z + tall, tall) * wide + lax.rem(y - my_y + wide, wide)
+        pair = (my_z ^ z) * wide + (my_y ^ y)
         before = where < s * tokens
         first = jnp.sum(jnp.where(before, 1.0, 0.0), axis=1, keepdims=True)
         inside = (where < (s + 1) * tokens) & jnp.logical_not(before)
-        start = (from_block * capacity).astype(f32)
+        start = (pair * capacity).astype(f32)
         slot += jnp.where(inside, lane - first + start, 0.0)
-        place += jnp.where(owner == s, (to_block * share).astype(f32), 0.0)
+        place += jnp.where(owner == s, (pair * share).astype(f32), 0.0)
         out_base += jnp.where(out_block == s, float(heads_of(s)), 0.0)
         in_base += jnp.where(in_source == s, float(s * (outbound // count)), 0.0)
     mine = owner == iota((count, total), 0)
@@ -334,10 +342,10 @@
             heads_out[:, span] = lax.dot_general(
                 probs, values, (((1,), (1,)), ((), ())), preferred_element_type=f32
             ).astype(bf16)
-    spread(heads_out, weight, parts, plane, False, moves)
-
-
-def spread(left, weight, parts, plane, back, moves=()):
+    spread(heads_out, weight, parts, plane, moves)
+
+
+def spread(left, weight, parts, plane, moves=()):
     width = weight.shape[1]
     tile = tile_of(width, 512)
     for start in range(0, width, tile):
@@ -345,7 +353,7 @@
             moves[start // (width // len(moves))].wait()
         span = slice(start, start + tile)
         product = dot(left[...], weight[:, span]).astype(bf16)
-        store_parts(parts, *plane, span, product, back)
+        store_parts(parts, *plane, span, product)
 
 
 def mlp_body(plane, *refs):
@@ -362,7 +370,7 @@
         gate = dot(piece[...], w_gate[:, span])
         upward = dot(piece[...], w_up[:, span])
         inner[:, span] = (gate / (1.0 + jnp.exp(-gate)) * upward).astype(bf16)
-    spread(inner, w_down, parts, plane, True)
+    spread(inner, w_down, parts, plane)
 
 
 def on_device(

time: 115 us -> 121 us (1.052)
  waiting for transfers between devices: 49.5 us -> 54.8 us
    ppermute x25, waiting for transfers between devices: 45.3 us -> 50.7 us  [swap(): return lax.ppermute(block, 'ctx', pairs)]
    pallas_call x9 -> x10, Pallas kernels: 13.9 us -> 13.8 us  [kernel_call(): pl.pallas_call(body, out_shape=[jax.ShapeDtypeStruct(s, d) for s, d in ou...]
  transfers between devices with their start and end apart: 26 -> 26, of which waited for: 15 -> 19; matrix products, arithmetic and copies ran while one was open for 1% -> 1% of each run, Pallas kernels for 14% -> 13%
where the time goes in v8:
time: 121 us; the launch traced here: 120 us
  waiting for transfers between devices  54.8 us (45%)
  starting transfers between devices  35 us (29%)
  Pallas kernels  26.2 us (22%)
  local copies, waits for them, and re-layouts  2.22 us (2%)
  other arithmetic  1.88 us (2%)
    ppermute x25, waiting for transfers between devices, swap(): return lax.ppermute(block, 'ctx', pairs)  50.7 us
    ppermute x25, starting transfers between devices, swap(): return lax.ppermute(block, 'ctx', pairs)  29.7 us
    pallas_call x10, Pallas kernels, kernel_call(): pl.pallas_call(body, out_shape=[jax.ShapeDtypeStruct(s, d) for s, d in ou...  13.8 us
    pallas_call x4, Pallas kernels, load(): pl.pallas_call(functools.partial(load_body, len(arrays)), out_shape=[pltp...  12.4 us
    all_to_all x1, starting transfers between devices, on_device(): lax.all_to_all(sent.reshape(count, each, total), 'ctx', 0, 0, tiled=True)  5.32 us
    all_to_all x1, waiting for transfers between devices, on_device(): lax.all_to_all(sent.reshape(count, each, total), 'ctx', 0, 0, tiled=True)  4.16 us
  transfers between devices with their start and end apart: 26, of which 19 were waited for; matrix products, arithmetic and copies ran while one was open for 1% of the time, Pallas kernels for 13%

profile of v8, /device:TPU:0, one launch (start us, length us, event | category | flops | bytes accessed | tf_op | source)
XLA Modules:
  0.0 120.3 jit_solution(14889194422179116404)
XLA Ops:
  1.6 5.1 %collective-permute-start.4 = (bf16[32,4096]{1,0:T(8,128)(2,1)S(1)}, bf16[32,4096]{1,0:T(8,128)(2,1)S(1)}, u32[]{:S(2)}, u32[]{:S(2)}) collective-permute-start(bf16[32,4096]{1,0:T(8,128)(2,1)S(1)} %shard_map.136.refs_0_), channel_id=1, source_target_pairs={{0,6},{1,7},{2,4},{3,5},{4,2},{5,3},{6,0},{7,1},{8,14},{9,15},{10,... | collective-permute-start | bytes 786440 | tf_op jit(solution)/shard_map/ppermute | solution.py:36
  11.0 1.6 %shard_map.137 = (f32[1,4096]{1,0:T(1,128)S(1)}, bf16[4096,128]{1,0:T(8,128)(2,1)S(1)}, bf16[4096,128]{1,0:T(8,128)(2,1)S(1)}, f32[8,128]{1,0:T(8,128)S(1)}) custom-call(bf16[32,4096]{1,0:T(8,128)(2,1)S(1)} %shard_map.136.refs_0_, f32[1,4096]{1,0:T(1,128)} %bitcast.11, bf16[4096,128]{1,0:T(8,128)(2,1)} %refs_2_.1, bf16[4096,128]{1,0:T(8,128)(2,1)} %refs_3_.1), custom_call_target="tpu_custom_call" | custom-call | bytes 4227072 | tf_op jit(solution)/shard_map/pallas_call | solution.py:180
  15.2 3.5 %collective-permute-done.1.refs_0_ = bf16[32,4096]{1,0:T(8,128)(2,1)S(1)} collective-permute-done((bf16[32,4096]{1,0:T(8,128)(2,1)S(1)}, bf16[32,4096]{1,0:T(8,128)(2,1)S(1)}, u32[]{:S(2)}, u32[]{:S(2)}) %collective-permute-start.1) | collective-permute-done | bytes 262176 | tf_op jit(solution)/shard_map/ppermute | solution.py:36
  21.6 3.6 %collective-permute-done.5.refs_1_ = bf16[32,4096]{1,0:T(8,128)(2,1)S(1)} collective-permute-done((bf16[32,4096]{1,0:T(8,128)(2,1)S(1)}, bf16[32,4096]{1,0:T(8,128)(2,1)S(1)}, u32[]{:S(2)}, u32[]{:S(2)}) %collective-permute-start.5) | collective-permute-done | bytes 262176 | tf_op jit(solution)/shard_map/ppermute | solution.py:36
  25.2 3.4 %collective-permute-done.2.refs_2_.refs_3_ = bf16[32,4096]{1,0:T(8,128)(2,1)S(1)} collective-permute-done((bf16[32,4096]{1,0:T(8,128)(2,1)S(1)}, bf16[32,4096]{1,0:T(8,128)(2,1)S(1)}, u32[]{:S(2)}, u32[]{:S(2)}) %collective-permute-start.2) | collective-permute-done | bytes 262176 | tf_op jit(solution)/shard_map/ppermute | solution.py:36
  28.7 1.6 %collective-permute-start.6 = (bf16[32,4096]{1,0:T(8,128)(2,1)S(1)}, bf16[32,4096]{1,0:T(8,128)(2,1)S(1)}, u32[]{:S(2)}, u32[]{:S(2)}) collective-permute-start(bf16[32,4096]{1,0:T(8,128)(2,1)S(1)} %shard_map.140.refs_4_), channel_id=1, source_target_pairs={{0,1},{1,0},{2,3},{3,2},{4,5},{5,4},{6,7},{7,6},{8,9},{9,8},{10,11... | collective-permute-start | bytes 786440 | tf_op jit(solution)/shard_map/ppermute | solution.py:36
  30.7 3.5 %collective-permute-done.7.refs_7_ = bf16[32,4096]{1,0:T(8,128)(2,1)S(1)} collective-permute-done((bf16[32,4096]{1,0:T(8,128)(2,1)S(1)}, bf16[32,4096]{1,0:T(8,128)(2,1)S(1)}, u32[]{:S(2)}, u32[]{:S(2)}) %collective-permute-start.7) | collective-permute-done | bytes 262176 | tf_op jit(solution)/shard_map/ppermute | solution.py:36
  34.3 4.7 %collective-permute-done.6.refs_5_ = bf16[32,4096]{1,0:T(8,128)(2,1)S(1)} collective-permute-done((bf16[32,4096]{1,0:T(8,128)(2,1)S(1)}, bf16[32,4096]{1,0:T(8,128)(2,1)S(1)}, u32[]{:S(2)}, u32[]{:S(2)}) %collective-permute-start.6) | collective-permute-done | bytes 262176 | tf_op jit(solution)/shard_map/ppermute | solution.py:36
  38.9 2.4 %shard_map.141 = (bf16[128,4096]{1,0:T(8,128)(2,1)S(1)}, bf16[16,4096]{1,0:T(8,128)(2,1)S(1)}, bf16[256,128]{1,0:T(8,128)(2,1)}) custom-call(bf16[32,4096]{1,0:T(8,128)(2,1)S(1)} %shard_map.136.refs_0_, bf16[32,4096]{1,0:T(8,128)(2,1)S(1)} %collective-permute-done.refs_3_.refs_1_, bf16[32,4096]{1,0:T(8,128)(2,1)S(1)} %shard_map.139.refs_2_, ...), custom_call_target="tpu_custom_call" | custom-call | flops 536870912 | bytes 1048576 | tf_op jit(solution)/shard_map/pallas_call | solution.py:155
  41.3 5.3 %all-to-all-start = ((bf16[8,32,128]{2,1,0:T(8,128)(2,1)}), bf16[8,32,128]{2,1,0:T(8,128)(2,1)S(1)}, u32[]{:S(2)}, u32[]{:S(2)}) async-start(bf16[8,32,128]{2,1,0:T(8,128)(2,1)} %bitcast.4), calls=%async_computation | async-start | bytes 131072 | tf_op jit(solution)/shard_map/all_to_all | solution.py:464
  46.8 2.6 %shard_map.142.refs_1_ = bf16[128,512]{1,0:T(8,128)(2,1)S(1)} custom-call(bf16[128,4096]{1,0:T(8,128)(2,1)S(1)} %get-tuple-element.44.normed, bf16[4096,512]{1,0:T(8,128)(2,1)} %w_query.1, f32[128,128]{1,0:T(8,128)S(1)} %get-tuple-element.75.cosine, f32[128,128]{1,0:T(8,128)S(1)} %get-tuple-element.76.sine), custom_call_target="tpu_custom_call" | custom-call | flops 536870912 | bytes 1048576 | tf_op jit(solution)/shard_map/pallas_call | solution.py:155
  49.4 4.2 %all-to-all-done = bf16[8,32,128]{2,1,0:T(8,128)(2,1)S(1)} async-done(((bf16[8,32,128]{2,1,0:T(8,128)(2,1)}), bf16[8,32,128]{2,1,0:T(8,128)(2,1)S(1)}, u32[]{:S(2)}, u32[]{:S(2)}) %all-to-all-start) | async-done | bytes 65568 | tf_op jit(solution)/shard_map/all_to_all | solution.py:464
  53.6 3.1 %shard_map.143 = (bf16[16,4096]{1,0:T(8,128)(2,1)S(1)}, bf16[16,4096]{1,0:T(8,128)(2,1)S(1)}, bf16[16,4096]{1,0:T(8,128)(2,1)S(1)}, bf16[16,4096]{1,0:T(8,128)(2...) custom-call(bf16[256,128]{1,0:T(8,128)(2,1)S(1)} %bitcast.6, ...), custom_call_target="tpu_custom_call" | custom-call | flops 536870912 | bytes 1048576 | tf_op jit(solution)/shard_map/pallas_call | solution.py:155
  57.1 1.6 %collective-permute-start.8 = (bf16[32,4096]{1,0:T(8,128)(2,1)S(1)}, bf16[32,4096]{1,0:T(8,128)(2,1)S(1)}, u32[]{:S(2)}, u32[]{:S(2)}) collective-permute-start(bf16[32,4096]{1,0:T(8,128)(2,1)S(1)} %get-tuple-element.47), channel_id=1, source_target_pairs={{0,1},{1,0},{2,3},{3,2},{4,5},{5,4},{6,7},{7,6},{8,9},{9,8},{10,11... | collective-permute-start | bytes 786440 | tf_op jit(solution)/shard_map/ppermute | solution.py:36
  58.7 3.4 %shard_map.144 = (bf16[1024,4096]{1,0:T(8,128)(2,1)S(1)}, f32[8,128]{1,0:T(8,128)S(1)}) custom-call(bf16[16,4096]{1,0:T(8,128)(2,1)S(1)} %get-tuple-element.48.refs_0_, bf16[1024,4096]{1,0:T(8,128)(2,1)} %refs_1_.3), custom_call_target="tpu_custom_call" | custom-call | bytes 16777216 | tf_op jit(solution)/shard_map/pallas_call | solution.py:180
  62.1 2.0 %collective-permute-done.11 = bf16[32,4096]{1,0:T(8,128)(2,1)S(1)} collective-permute-done((bf16[32,4096]{1,0:T(8,128)(2,1)S(1)}, bf16[32,4096]{1,0:T(8,128)(2,1)S(1)}, u32[]{:S(2)}, u32[]{:S(2)}) %collective-permute-start.11) | collective-permute-done | bytes 262176 | tf_op jit(solution)/shard_map/ppermute | solution.py:36
  64.4 2.5 %collective-permute-done.8.refs_0_ = bf16[32,4096]{1,0:T(8,128)(2,1)S(1)} collective-permute-done((bf16[32,4096]{1,0:T(8,128)(2,1)S(1)}, bf16[32,4096]{1,0:T(8,128)(2,1)S(1)}, u32[]{:S(2)}, u32[]{:S(2)}) %collective-permute-start.8) | collective-permute-done | bytes 262176 | tf_op jit(solution)/shard_map/ppermute | solution.py:36
  68.7 3.4 %shard_map.146 = (bf16[4096,1024]{1,0:T(8,128)(2,1)S(1)}, f32[8,128]{1,0:T(8,128)S(1)}) custom-call(bf16[16,4096]{1,0:T(8,128)(2,1)S(1)} %add_convert_fusion.3.refs_0_, bf16[4096,1024]{1,0:T(8,128)(2,1)} %refs_1_.4), custom_call_target="tpu_custom_call" | custom-call | bytes 16777216 | tf_op jit(solution)/shard_map/pallas_call | solution.py:180
  72.2 1.8 %collective-permute-done.9 = bf16[16,4096]{1,0:T(8,128)(2,1)S(1)} collective-permute-done((bf16[16,4096]{1,0:T(8,128)(2,1)S(1)}, bf16[16,4096]{1,0:T(8,128)(2,1)S(1)}, u32[]{:S(2)}, u32[]{:S(2)}) %collective-permute-start.9) | collective-permute-done | bytes 131104 | tf_op jit(solution)/shard_map/ppermute | solution.py:36
  73.9 6.8 %collective-permute-done.10 = bf16[16,4096]{1,0:T(8,128)(2,1)S(1)} collective-permute-done((bf16[16,4096]{1,0:T(8,128)(2,1)S(1)}, bf16[16,4096]{1,0:T(8,128)(2,1)S(1)}, u32[]{:S(2)}, u32[]{:S(2)}) %collective-permute-start.10) | collective-permute-done | bytes 131104 | tf_op jit(solution)/shard_map/ppermute | solution.py:36
  81.1 1.6 %collective-permute-start.18 = (bf16[16,4096]{1,0:T(8,128)(2,1)S(1)}, bf16[16,4096]{1,0:T(8,128)(2,1)S(1)}, u32[]{:S(2)}, u32[]{:S(2)}) collective-permute-start(bf16[16,4096]{1,0:T(8,128)(2,1)S(1)} %multiply_convert_fusion.refs_0_), channel_id=1, source_target_pairs={{0,6},{1,7},{2,4},{3,5},{4,2},{5,3},{6,0},{7,1},{8,14},{9,15},{10,... | collective-permute-start | bytes 393224 | tf_op jit(solution)/shard_map/ppermute | solution.py:36
  82.7 2.8 %collective-permute-start.14 = (bf16[16,4096]{1,0:T(8,128)(2,1)S(1)}, bf16[16,4096]{1,0:T(8,128)(2,1)S(1)}, u32[]{:S(2)}, u32[]{:S(2)}) collective-permute-start(bf16[16,4096]{1,0:T(8,128)(2,1)S(1)} %multiply_convert_fusion.refs_0_), channel_id=1, source_target_pairs={{0,2},{1,3},{2,0},{3,1},{4,6},{5,7},{6,4},{7,5},{8,10},{9,11},{10,... | collective-permute-start | bytes 393224 | tf_op jit(solution)/shard_map/ppermute | solution.py:36
  86.2 1.9 %collective-permute-done.18.refs_6_ = bf16[16,4096]{1,0:T(8,128)(2,1)S(1)} collective-permute-done((bf16[16,4096]{1,0:T(8,128)(2,1)S(1)}, bf16[16,4096]{1,0:T(8,128)(2,1)S(1)}, u32[]{:S(2)}, u32[]{:S(2)}) %collective-permute-start.18) | collective-permute-done | bytes 131104 | tf_op jit(solution)/shard_map/ppermute | solution.py:36
  88.6 2.1 %collective-permute-done.16.refs_4_ = bf16[16,4096]{1,0:T(8,128)(2,1)S(1)} collective-permute-done((bf16[16,4096]{1,0:T(8,128)(2,1)S(1)}, bf16[16,4096]{1,0:T(8,128)(2,1)S(1)}, u32[]{:S(2)}, u32[]{:S(2)}) %collective-permute-start.16) | collective-permute-done | bytes 131104 | tf_op jit(solution)/shard_map/ppermute | solution.py:36
  92.8 4.0 %shard_map.148 = (bf16[4096,1024]{1,0:T(8,128)(2,1)S(1)}, f32[8,128]{1,0:T(8,128)}) custom-call(bf16[16,4096]{1,0:T(8,128)(2,1)S(1)} %multiply_convert_fusion.refs_0_, bf16[4096,1024]{1,0:T(8,128)(2,1)} %refs_1_.5), custom_call_target="tpu_custom_call" | custom-call | bytes 16777216 | tf_op jit(solution)/shard_map/pallas_call | solution.py:180
  97.0 2.8 %collective-permute-done.15.refs_3_ = bf16[16,4096]{1,0:T(8,128)(2,1)S(1)} collective-permute-done((bf16[16,4096]{1,0:T(8,128)(2,1)S(1)}, bf16[16,4096]{1,0:T(8,128)(2,1)S(1)}, u32[]{:S(2)}, u32[]{:S(2)}) %collective-permute-start.15) | collective-permute-done | bytes 131104 | tf_op jit(solution)/shard_map/ppermute | solution.py:36
  99.8 3.6 %shard_map.149 = (bf16[16,4096]{1,0:T(8,128)(2,1)S(1)}, bf16[16,4096]{1,0:T(8,128)(2,1)S(1)}, bf16[16,4096]{1,0:T(8,128)(2,1)S(1)}, bf16[16,4096]{1,0:T(8,128)(2...) custom-call(bf16[16,4096]{1,0:T(8,128)(2,1)S(1)} %multiply_convert_fusion.refs_0_, ...), custom_call_target="tpu_custom_call" | custom-call | flops 3221225472 | bytes 1048576 | tf_op jit(solution)/shard_map/pallas_call | solution.py:155
  105.5 4.3 %collective-permute-done.20 = bf16[32,4096]{1,0:T(8,128)(2,1)S(1)} collective-permute-done((bf16[32,4096]{1,0:T(8,128)(2,1)S(1)}, bf16[32,4096]{1,0:T(8,128)(2,1)S(1)}, u32[]{:S(2)}, u32[]{:S(2)}) %collective-permute-start.20) | collective-permute-done | bytes 262176 | tf_op jit(solution)/shard_map/ppermute | solution.py:36
  109.9 1.7 %collective-permute-start.21 = (bf16[16,4096]{1,0:T(8,128)(2,1)S(1)}, bf16[16,4096]{1,0:T(8,128)(2,1)S(1)}, u32[]{:S(2)}, u32[]{:S(2)}) collective-permute-start(bf16[16,4096]{1,0:T(8,128)(2,1)S(1)} %get-tuple-element.68), channel_id=1, source_target_pairs={{0,6},{1,7},{2,4},{3,5},{4,2},{5,3},{6,0},{7,1},{8,14},{9,15},{10,... | collective-permute-start | bytes 393224 | tf_op jit(solution)/shard_map/ppermute | solution.py:36
  112.7 1.8 %collective-permute-start.24 = (bf16[16,4096]{1,0:T(8,128)(2,1)S(1)}, bf16[16,4096]{1,0:T(8,128)(2,1)S(1)}, u32[]{:S(2)}, u32[]{:S(2)}) collective-permute-start(bf16[16,4096]{1,0:T(8,128)(2,1)S(1)} %add_convert_fusion), channel_id=1, source_target_pairs={{0,2},{1,3},{2,0},{3,1},{4,6},{5,7},{6,4},{7,5},{8,10},{9,11},{10,... | collective-permute-start | bytes 393224 | tf_op jit(solution)/shard_map/ppermute | solution.py:36
  114.5 2.4 %collective-permute-done.21 = bf16[16,4096]{1,0:T(8,128)(2,1)S(1)} collective-permute-done((bf16[16,4096]{1,0:T(8,128)(2,1)S(1)}, bf16[16,4096]{1,0:T(8,128)(2,1)S(1)}, u32[]{:S(2)}, u32[]{:S(2)}) %collective-permute-start.21) | collective-permute-done | bytes 131104 | tf_op jit(solution)/shard_map/ppermute | solution.py:36
  116.9 2.7 %collective-permute-done.22 = bf16[16,4096]{1,0:T(8,128)(2,1)S(1)} collective-permute-done((bf16[16,4096]{1,0:T(8,128)(2,1)S(1)}, bf16[16,4096]{1,0:T(8,128)(2,1)S(1)}, u32[]{:S(2)}, u32[]{:S(2)}) %collective-permute-start.22) | collective-permute-done | bytes 131104 | tf_op jit(solution)/shard_map/ppermute | solution.py:36
  (59 shorter events, 22.3 us)
Async XLA Ops:
  0.0 53.6 %copy-start.2 = (s32[128]{0:T(128)S(1)}, s32[128]{0:T(128)}, u32[]{:S(2)}) copy-start(s32[128]{0:T(128)} %param.15) | copy-start | bytes 1540
  1.6 12.3 %collective-permute-start.4 = (bf16[32,4096]{1,0:T(8,128)(2,1)S(1)}, bf16[32,4096]{1,0:T(8,128)(2,1)S(1)}, u32[]{:S(2)}, u32[]{:S(2)}) collective-permute-start(bf16[32,4096]{1,0:T(8,128)(2,1)S(1)} %shard_map.136.refs_0_), channel_id=1, source_target_pairs={{0,6},{1,7},{2,4},{3,5},{4,2},{5,3},{6,0},{7,1},{8,14},{9,15},{10,... | collective-permute-start | bytes 786440 | tf_op jit(solution)/shard_map/ppermute | solution.py:36
  6.7 12.0 %collective-permute-start.1 = (bf16[32,4096]{1,0:T(8,128)(2,1)S(1)}, bf16[32,4096]{1,0:T(8,128)(2,1)S(1)}, u32[]{:S(2)}, u32[]{:S(2)}) collective-permute-start(bf16[32,4096]{1,0:T(8,128)(2,1)S(1)} %shard_map.136.refs_0_), channel_id=1, source_target_pairs={{0,2},{1,3},{2,0},{3,1},{4,6},{5,7},{6,4},{7,5},{8,10},{9,11},{10,... | collective-permute-start | bytes 786440 | tf_op jit(solution)/shard_map/ppermute | solution.py:36
  6.7 12.0 %collective-permute-start = (bf16[32,4096]{1,0:T(8,128)(2,1)S(1)}, bf16[32,4096]{1,0:T(8,128)(2,1)S(1)}, u32[]{:S(2)}, u32[]{:S(2)}) collective-permute-start(bf16[32,4096]{1,0:T(8,128)(2,1)S(1)} %shard_map.136.refs_0_), channel_id=1, source_target_pairs={{0,1},{1,0},{2,3},{3,2},{4,5},{5,4},{6,7},{7,6},{8,9},{9,8},{10,11... | collective-permute-start | bytes 786440 | tf_op jit(solution)/shard_map/ppermute | solution.py:36
  8.2 0.9 copy-start
  9.1 0.7 copy-start.1
  9.8 0.7 copy-start.3
  13.9 11.3 %collective-permute-start.5 = (bf16[32,4096]{1,0:T(8,128)(2,1)S(1)}, bf16[32,4096]{1,0:T(8,128)(2,1)S(1)}, u32[]{:S(2)}, u32[]{:S(2)}) collective-permute-start(bf16[32,4096]{1,0:T(8,128)(2,1)S(1)} %collective-permute-done.4.refs_6_), channel_id=1, source_target_pairs={{2,0},{3,1},{4,6},{5,7},{10,8},{11,9},{12,14},{13,15},{18,16},{19,... | collective-permute-start | bytes 786440 | tf_op jit(solution)/shard_map/ppermute | solution.py:36
  18.7 6.5 %collective-permute-start.3 = (bf16[32,4096]{1,0:T(8,128)(2,1)S(1)}, bf16[32,4096]{1,0:T(8,128)(2,1)S(1)}, u32[]{:S(2)}, u32[]{:S(2)}) collective-permute-start(bf16[32,4096]{1,0:T(8,128)(2,1)S(1)} %shard_map.139.refs_2_), channel_id=1, source_target_pairs={{2,4},{3,5},{4,2},{5,3},{10,12},{11,13},{12,10},{13,11},{18,20},{1... | collective-permute-start | bytes 786440 | tf_op jit(solution)/shard_map/ppermute | solution.py:36
  19.4 9.2 %collective-permute-start.2 = (bf16[32,4096]{1,0:T(8,128)(2,1)S(1)}, bf16[32,4096]{1,0:T(8,128)(2,1)S(1)}, u32[]{:S(2)}, u32[]{:S(2)}) collective-permute-start(bf16[32,4096]{1,0:T(8,128)(2,1)S(1)} %shard_map.139.refs_2_), channel_id=1, source_target_pairs={{0,1},{1,0},{2,3},{3,2},{4,5},{5,4},{6,7},{7,6},{8,9},{9,8},{10,11... | collective-permute-start | bytes 786440 | tf_op jit(solution)/shard_map/ppermute | solution.py:36
  21.0 13.2 %collective-permute-start.7 = (bf16[32,4096]{1,0:T(8,128)(2,1)S(1)}, bf16[32,4096]{1,0:T(8,128)(2,1)S(1)}, u32[]{:S(2)}, u32[]{:S(2)}) collective-permute-start(bf16[32,4096]{1,0:T(8,128)(2,1)S(1)} %collective-permute-done.4.refs_6_), channel_id=1, source_target_pairs={{0,1},{1,0},{2,3},{3,2},{4,5},{5,4},{6,7},{7,6},{8,9},{9,8},{10,11... | collective-permute-start | bytes 786440 | tf_op jit(solution)/shard_map/ppermute | solution.py:36
  28.7 10.3 %collective-permute-start.6 = (bf16[32,4096]{1,0:T(8,128)(2,1)S(1)}, bf16[32,4096]{1,0:T(8,128)(2,1)S(1)}, u32[]{:S(2)}, u32[]{:S(2)}) collective-permute-start(bf16[32,4096]{1,0:T(8,128)(2,1)S(1)} %shard_map.140.refs_4_), channel_id=1, source_target_pairs={{0,1},{1,0},{2,3},{3,2},{4,5},{5,4},{6,7},{7,6},{8,9},{9,8},{10,11... | collective-permute-start | bytes 786440 | tf_op jit(solution)/shard_map/ppermute | solution.py:36
  41.3 12.2 %all-to-all-start = ((bf16[8,32,128]{2,1,0:T(8,128)(2,1)}), bf16[8,32,128]{2,1,0:T(8,128)(2,1)S(1)}, u32[]{:S(2)}, u32[]{:S(2)}) async-start(bf16[8,32,128]{2,1,0:T(8,128)(2,1)} %bitcast.4), calls=%async_computation | async-start | bytes 131072 | tf_op jit(solution)/shard_map/all_to_all | solution.py:464
  56.6 7.5 %collective-permute-start.11 = (bf16[32,4096]{1,0:T(8,128)(2,1)S(1)}, bf16[32,4096]{1,0:T(8,128)(2,1)S(1)}, u32[]{:S(2)}, u32[]{:S(2)}) collective-permute-start(bf16[32,4096]{1,0:T(8,128)(2,1)S(1)} %get-tuple-element.52), channel_id=1, source_target_pairs={{0,1},{1,0},{2,3},{3,2},{4,5},{5,4},{6,7},{7,6},{8,9},{9,8},{10,11... | collective-permute-start | bytes 786440 | tf_op jit(solution)/shard_map/ppermute | solution.py:36
  57.1 9.8 %collective-permute-start.8 = (bf16[32,4096]{1,0:T(8,128)(2,1)S(1)}, bf16[32,4096]{1,0:T(8,128)(2,1)S(1)}, u32[]{:S(2)}, u32[]{:S(2)}) collective-permute-start(bf16[32,4096]{1,0:T(8,128)(2,1)S(1)} %get-tuple-element.47), channel_id=1, source_target_pairs={{0,1},{1,0},{2,3},{3,2},{4,5},{5,4},{6,7},{7,6},{8,9},{9,8},{10,11... | collective-permute-start | bytes 786440 | tf_op jit(solution)/shard_map/ppermute | solution.py:36
  58.7 22.0 %copy-start.4 = (f32[4096]{0:T(1024)S(1)}, f32[4096]{0:T(1024)}, u32[]{:S(2)}) copy-start(f32[4096]{0:T(1024)} %param.26) | copy-start | bytes 49156
  58.7 22.3 %copy-start.5 = (f32[4096]{0:T(1024)S(1)}, f32[4096]{0:T(1024)}, u32[]{:S(2)}) copy-start(f32[4096]{0:T(1024)} %param.22) | copy-start | bytes 49156
  64.1 8.0 %collective-permute-start.12 = (bf16[16,4096]{1,0:T(8,128)(2,1)S(1)}, bf16[16,4096]{1,0:T(8,128)(2,1)S(1)}, u32[]{:S(2)}, u32[]{:S(2)}) collective-permute-start(bf16[16,4096]{1,0:T(8,128)(2,1)S(1)} %add_convert_fusion.3.refs_0_), channel_id=1, source_target_pairs={{0,2},{1,3},{2,0},{3,1},{4,6},{5,7},{6,4},{7,5},{8,10},{9,11},{10,... | collective-permute-start | bytes 393224 | tf_op jit(solution)/shard_map/ppermute | solution.py:36
  67.0 6.9 %collective-permute-start.9 = (bf16[16,4096]{1,0:T(8,128)(2,1)S(1)}, bf16[16,4096]{1,0:T(8,128)(2,1)S(1)}, u32[]{:S(2)}, u32[]{:S(2)}) collective-permute-start(bf16[16,4096]{1,0:T(8,128)(2,1)S(1)} %get-tuple-element.70), channel_id=1, source_target_pairs={{0,6},{1,7},{2,4},{3,5},{4,2},{5,3},{6,0},{7,1},{8,14},{9,15},{10,... | collective-permute-start | bytes 393224 | tf_op jit(solution)/shard_map/ppermute | solution.py:36
  67.6 13.1 %collective-permute-start.10 = (bf16[16,4096]{1,0:T(8,128)(2,1)S(1)}, bf16[16,4096]{1,0:T(8,128)(2,1)S(1)}, u32[]{:S(2)}, u32[]{:S(2)}) collective-permute-start(bf16[16,4096]{1,0:T(8,128)(2,1)S(1)} %get-tuple-element.71), channel_id=1, source_target_pairs={{0,4},{1,5},{2,6},{3,7},{4,0},{5,1},{6,2},{7,3},{8,12},{9,13},{10,... | collective-permute-start | bytes 393224 | tf_op jit(solution)/shard_map/ppermute | solution.py:36
  81.1 7.0 %collective-permute-start.18 = (bf16[16,4096]{1,0:T(8,128)(2,1)S(1)}, bf16[16,4096]{1,0:T(8,128)(2,1)S(1)}, u32[]{:S(2)}, u32[]{:S(2)}) collective-permute-start(bf16[16,4096]{1,0:T(8,128)(2,1)S(1)} %multiply_convert_fusion.refs_0_), channel_id=1, source_target_pairs={{0,6},{1,7},{2,4},{3,5},{4,2},{5,3},{6,0},{7,1},{8,14},{9,15},{10,... | collective-permute-start | bytes 393224 | tf_op jit(solution)/shard_map/ppermute | solution.py:36
  82.7 8.0 %collective-permute-start.16 = (bf16[16,4096]{1,0:T(8,128)(2,1)S(1)}, bf16[16,4096]{1,0:T(8,128)(2,1)S(1)}, u32[]{:S(2)}, u32[]{:S(2)}) collective-permute-start(bf16[16,4096]{1,0:T(8,128)(2,1)S(1)} %multiply_convert_fusion.refs_0_), channel_id=1, source_target_pairs={{0,4},{1,5},{2,6},{3,7},{4,0},{5,1},{6,2},{7,3},{8,12},{9,13},{10,... | collective-permute-start | bytes 393224 | tf_op jit(solution)/shard_map/ppermute | solution.py:36
  82.7 8.6 %collective-permute-start.14 = (bf16[16,4096]{1,0:T(8,128)(2,1)S(1)}, bf16[16,4096]{1,0:T(8,128)(2,1)S(1)}, u32[]{:S(2)}, u32[]{:S(2)}) collective-permute-start(bf16[16,4096]{1,0:T(8,128)(2,1)S(1)} %multiply_convert_fusion.refs_0_), channel_id=1, source_target_pairs={{0,2},{1,3},{2,0},{3,1},{4,6},{5,7},{6,4},{7,5},{8,10},{9,11},{10,... | collective-permute-start | bytes 393224 | tf_op jit(solution)/shard_map/ppermute | solution.py:36
  85.5 11.2 %collective-permute-start.13 = (bf16[16,4096]{1,0:T(8,128)(2,1)S(1)}, bf16[16,4096]{1,0:T(8,128)(2,1)S(1)}, u32[]{:S(2)}, u32[]{:S(2)}) collective-permute-start(bf16[16,4096]{1,0:T(8,128)(2,1)S(1)} %multiply_convert_fusion.refs_0_), channel_id=1, source_target_pairs={{0,1},{1,0},{2,3},{3,2},{4,5},{5,4},{6,7},{7,6},{8,9},{9,8},{10,11... | collective-permute-start | bytes 393224 | tf_op jit(solution)/shard_map/ppermute | solution.py:36
  88.1 8.7 %collective-permute-start.19 = (bf16[16,4096]{1,0:T(8,128)(2,1)S(1)}, bf16[16,4096]{1,0:T(8,128)(2,1)S(1)}, u32[]{:S(2)}, u32[]{:S(2)}) collective-permute-start(bf16[16,4096]{1,0:T(8,128)(2,1)S(1)} %collective-permute-done.18.refs_6_), channel_id=1, source_target_pairs={{0,1},{1,0},{2,3},{3,2},{4,5},{5,4},{6,7},{7,6},{8,9},{9,8},{10,11... | collective-permute-start | bytes 393224 | tf_op jit(solution)/shard_map/ppermute | solution.py:36
  90.7 6.3 %collective-permute-start.17 = (bf16[16,4096]{1,0:T(8,128)(2,1)S(1)}, bf16[16,4096]{1,0:T(8,128)(2,1)S(1)}, u32[]{:S(2)}, u32[]{:S(2)}) collective-permute-start(bf16[16,4096]{1,0:T(8,128)(2,1)S(1)} %collective-permute-done.16.refs_4_), channel_id=1, source_target_pairs={{0,1},{1,0},{2,3},{3,2},{4,5},{5,4},{6,7},{7,6},{8,9},{9,8},{10,11... | collective-permute-start | bytes 393224 | tf_op jit(solution)/shard_map/ppermute | solution.py:36
  91.4 8.5 %collective-permute-start.15 = (bf16[16,4096]{1,0:T(8,128)(2,1)S(1)}, bf16[16,4096]{1,0:T(8,128)(2,1)S(1)}, u32[]{:S(2)}, u32[]{:S(2)}) collective-permute-start(bf16[16,4096]{1,0:T(8,128)(2,1)S(1)} %collective-permute-done.14.refs_2_), channel_id=1, source_target_pairs={{0,1},{1,0},{2,3},{3,2},{4,5},{5,4},{6,7},{7,6},{8,9},{9,8},{10,11... | collective-permute-start | bytes 393224 | tf_op jit(solution)/shard_map/ppermute | solution.py:36
  103.4 6.4 %collective-permute-start.20 = (bf16[32,4096]{1,0:T(8,128)(2,1)S(1)}, bf16[32,4096]{1,0:T(8,128)(2,1)S(1)}, u32[]{:S(2)}, u32[]{:S(2)}) collective-permute-start(bf16[32,4096]{1,0:T(8,128)(2,1)S(1)} %get-tuple-element.58), channel_id=1, source_target_pairs={{0,1},{1,0},{2,3},{3,2},{4,5},{5,4},{6,7},{7,6},{8,9},{9,8},{10,11... | collective-permute-start | bytes 786440 | tf_op jit(solution)/shard_map/ppermute | solution.py:36
  104.1 8.5 %collective-permute-start.23 = (bf16[32,4096]{1,0:T(8,128)(2,1)S(1)}, bf16[32,4096]{1,0:T(8,128)(2,1)S(1)}, u32[]{:S(2)}, u32[]{:S(2)}) collective-permute-start(bf16[32,4096]{1,0:T(8,128)(2,1)S(1)} %get-tuple-element.61), channel_id=1, source_target_pairs={{0,1},{1,0},{2,3},{3,2},{4,5},{5,4},{6,7},{7,6},{8,9},{9,8},{10,11... | collective-permute-start | bytes 786440 | tf_op jit(solution)/shard_map/ppermute | solution.py:36
  109.9 7.0 %collective-permute-start.21 = (bf16[16,4096]{1,0:T(8,128)(2,1)S(1)}, bf16[16,4096]{1,0:T(8,128)(2,1)S(1)}, u32[]{:S(2)}, u32[]{:S(2)}) collective-permute-start(bf16[16,4096]{1,0:T(8,128)(2,1)S(1)} %get-tuple-element.68), channel_id=1, source_target_pairs={{0,6},{1,7},{2,4},{3,5},{4,2},{5,3},{6,0},{7,1},{8,14},{9,15},{10,... | collective-permute-start | bytes 393224 | tf_op jit(solution)/shard_map/ppermute | solution.py:36
  111.6 7.9 %collective-permute-start.22 = (bf16[16,4096]{1,0:T(8,128)(2,1)S(1)}, bf16[16,4096]{1,0:T(8,128)(2,1)S(1)}, u32[]{:S(2)}, u32[]{:S(2)}) collective-permute-start(bf16[16,4096]{1,0:T(8,128)(2,1)S(1)} %get-tuple-element.69), channel_id=1, source_target_pairs={{0,4},{1,5},{2,6},{3,7},{4,0},{5,1},{6,2},{7,3},{8,12},{9,13},{10,... | collective-permute-start | bytes 393224 | tf_op jit(solution)/shard_map/ppermute | solution.py:36
  112.7 6.9 %collective-permute-start.24 = (bf16[16,4096]{1,0:T(8,128)(2,1)S(1)}, bf16[16,4096]{1,0:T(8,128)(2,1)S(1)}, u32[]{:S(2)}, u32[]{:S(2)}) collective-permute-start(bf16[16,4096]{1,0:T(8,128)(2,1)S(1)} %add_convert_fusion), channel_id=1, source_target_pairs={{0,2},{1,3},{2,0},{3,1},{4,6},{5,7},{6,4},{7,5},{8,10},{9,11},{10,... | collective-permute-start | bytes 393224 | tf_op jit(solution)/shard_map/ppermute | solution.py:36

commit v9 on v7

--- a/solution.py
+++ b/solution.py
@@ -57,15 +57,34 @@
             blocks[dz, 0] = shift(block, tall, wide, dz, 0)
     for dy in range(1, wide):
         blocks[0, dy] = shift(block, tall, wide, 0, dy)
-    blocks[1, 0] = tie([blocks[1, 0]], [*tokens, *(blocks[0, dy] for dy in range(1, wide))])
+        if tall == 4:
+            blocks[3, dy] = shift(blocks[3, 0], tall, wide, 0, dy)
+    early = [b for (_, dy), b in blocks.items() if dy]
+    blocks[1, 0] = tie([blocks[1, 0]], [*tokens, *early])
     if tall == 4:
         up = shift(blocks[1, 0], tall, wide, 1, 0, lambda z: z in (1, 2))
         down = shift(blocks[3, 0], tall, wide, -1, 0, lambda z: z in (1, 2))
         blocks[2, 0] = up + down
-    for dz in [1, *range(tall - 1, 1, -1)]:
+    for dz in range(1, tall):
         for dy in range(1, wide):
-            blocks[dz, dy] = shift(blocks[dz, 0], tall, wide, 0, dy)
+            if (dz, dy) not in blocks:
+                blocks[dz, dy] = shift(blocks[dz, 0], tall, wide, 0, dy)
     return [blocks[dz, dy] for dz in range(tall) for dy in range(wide)]
+
+
+def pack_body(tall, *refs):
+    wide = len(refs) - tall
+    each = refs[0].shape[0] // tall
+    for dz in range(tall):
+        values = [ref[...].astype(f32)[dz * each : (dz + 1) * each] for ref in refs[:wide]]
+        refs[wide + dz][...] = jnp.concatenate(values, axis=0).astype(bf16)
+
+
+def exchange(parts, tall, wide):
+    shape = ((parts[0].shape[0] // tall * wide, parts[0].shape[1]), bf16)
+    crossed = [parts[0]] + [shift(parts[dy], tall, wide, 0, dy) for dy in range(1, wide)]
+    packed = kernel_call(functools.partial(pack_body, tall), [shape] * tall, crossed)
+    return [packed[0]] + [shift(packed[dz], tall, wide, dz, 0) for dz in range(1, tall)]
 
 
 def gather_blocks(block, tall, wide):
@@ -121,7 +140,7 @@
             if dz:
                 sent = lane.astype(bf16)
                 lane = shift(sent, tall, wide, dz, 0)
-                if loads and dz == tall - 1:
+                if len(loads) > 1 and dz == tall - 1:
                     *copy, token = load(sent, loads[1])
                     loaded += copy
                     lane = tie([lane], [token])
@@ -231,14 +250,15 @@
         z, y = divmod(s, wide)
         from_block = lax.rem(my_z - z + tall, tall) * wide + lax.rem(my_y - y + wide, wide)
         to_block = lax.rem(z - my_z + tall, tall) * wide + lax.rem(y - my_y + wide, wide)
+        peer = lax.rem(my_z + z, tall) * wide + lax.rem(my_y + y, wide)
         before = where < s * tokens
         first = jnp.sum(jnp.where(before, 1.0, 0.0), axis=1, keepdims=True)
         inside = (where < (s + 1) * tokens) & jnp.logical_not(before)
         start = (from_block * capacity).astype(f32)
         slot += jnp.where(inside, lane - first + start, 0.0)
         place += jnp.where(owner == s, (to_block * share).astype(f32), 0.0)
-        out_base += jnp.where(out_block == s, float(heads_of(s)), 0.0)
-        in_base += jnp.where(in_source == s, float(s * (outbound // count)), 0.0)
+        out_base += jnp.where(out_block == y * tall + z, heads_of(peer).astype(f32), 0.0)
+        in_base += jnp.where(in_source == s, (from_block * (outbound // count)).astype(f32), 0.0)
     mine = owner == iota((count, total), 0)
     earlier = jnp.where(iota((total, total), 0) < iota((total, total), 1), 1.0, 0.0)
     rank = dot(jnp.where(mine, 1.0, 0.0).astype(bf16), earlier.astype(bf16))
@@ -253,10 +273,11 @@
     unmix[...] = jnp.where(in_base == iota(unmix.shape, 1), 1.0, 0.0).astype(bf16)
 
 
-def kv_body(count, *refs):
+def kv_body(count, extra, *refs):
     blocks = refs[:count]
     pick_rows, order, columns, gain, w_key, w_value = refs[count : count + 6]
-    normed, own, sent, rows = refs[-4:]
+    wide = len(refs) - count - 9 - extra
+    normed, own, *sent, rows = refs[-3 - wide :]
     total, width = normed.shape
     tile = tile_of(width, 512)
     square = jnp.zeros((total, 1), f32)
@@ -277,23 +298,14 @@
     turned = lax.dot_general(
         columns[...], both, (((1,), (1,)), ((), ())), preferred_element_type=f32
     ).astype(bf16)
-    sent[...] = dot(turned, order[...]).astype(bf16)
-
-
-def query_body(normed, w_query, cosine, sine, query, weight, sems):
-    depth = weight.shape[0] // 4
-    moves = []
-    for index in range(4):
-        piece = pl.ds(index * depth, depth)
-        moves.append(
-            pltpu.make_async_copy(w_query.at[piece], weight.at[piece], sems.at[index])
-        )
-        moves[-1].start()
-    raw = jnp.zeros(query.shape, f32)
-    for index, move in enumerate(moves):
-        move.wait()
-        piece = slice(index * depth, (index + 1) * depth)
-        raw += dot(normed[:, piece], weight[piece, :])
+    turned = dot(turned, order[...])
+    each = turned.shape[0] // wide
+    for dy in range(wide):
+        sent[dy][...] = turned[dy * each : (dy + 1) * each].astype(bf16)
+
+
+def query_body(normed, w_query, cosine, sine, query):
+    raw = dot(normed[...], w_query[...])
     for head in range(query.shape[1] // HEAD_DIM):
         span = slice(head * HEAD_DIM, (head + 1) * HEAD_DIM)
         one = raw[:, span]
@@ -302,19 +314,14 @@
 
 
 def attend_body(plane, kv_local, *refs):
-    arrived, query, unmix, cosine, sine, key_pos, query_pos, w_output = refs[:8]
-    parts, (heads_out, weight, sems) = refs[8:-3], refs[-3:]
-    width = weight.shape[1] // 4
-    moves = []
-    for index in range(4):
-        piece = pl.ds(index * width, width)
-        moves.append(
-            pltpu.make_async_copy(w_output.at[:, piece], weight.at[:, piece], sems.at[index])
-        )
-        moves[-1].start()
+    tall = plane[0]
+    arrived, rest = refs[:tall], refs[tall:]
+    query, unmix, cosine, sine, key_pos, query_pos, w_output = rest[:7]
+    parts, heads_out = rest[7:-1], rest[-1]
     half = HEAD_DIM // 2
     heads = query.shape[1] // HEAD_DIM
-    both = dot(unmix[...], arrived[...])
+    mixed = jnp.concatenate([a[...].astype(f32) for a in arrived], axis=0).astype(bf16)
+    both = dot(unmix[...], mixed)
     allowed = key_pos[...].astype(f32) <= query_pos[:, 0:1]
     for group in range(kv_local):
         base = group * HEAD_DIM
@@ -334,15 +341,13 @@
             heads_out[:, span] = lax.dot_general(
                 probs, values, (((1,), (1,)), ((), ())), preferred_element_type=f32
             ).astype(bf16)
-    spread(heads_out, weight, parts, plane, False, moves)
-
-
-def spread(left, weight, parts, plane, back, moves=()):
+    spread(heads_out, w_output, parts, plane, False)
+
+
+def spread(left, weight, parts, plane, back):
     width = weight.shape[1]
     tile = tile_of(width, 512)
     for start in range(0, width, tile):
-        if moves and start % (width // len(moves)) == 0:
-            moves[start // (width // len(moves))].wait()
         span = slice(start, start + tile)
         product = dot(left[...], weight[:, span]).astype(bf16)
         store_parts(parts, *plane, span, product, back)
@@ -408,8 +413,8 @@
         specs=[scalar, in_hbm, in_hbm],
         flops=2 * capacity * tokens * model,
     )
-    attn_gain, w_key, w_value, token_1 = load(
-        outgoing, attn_gain.reshape(1, model), w_key, w_value
+    attn_gain, w_key, w_value, w_query, token_1 = load(
+        outgoing, attn_gain.reshape(1, model), w_key, w_value, w_query
     )
 
     each = kv_local * 2 * depth
@@ -422,7 +427,7 @@
     notes[: 2 * kv_local * HEAD_DIM, 3] = source
     pick_rows, in_order, columns, unmix, positions = kernel_call(
         functools.partial(
-            map_body, tall, wide, tokens, lambda peer: peer * local_heads // group_size
+            map_body, tall, wide, tokens, lambda peer: lax.div(peer * local_heads, group_size)
         ),
         [
             ((total, count * capacity), bf16),
@@ -435,6 +440,11 @@
         specs=[scalar, VMEM, VMEM, VMEM],
     )
     blocks = gather_rows(outgoing, tall, wide, [token_1, positions])
+    near = blocks[2 * wide]
+    w_output, *token_2 = load(near, w_output)
+    w_gate, *token_3 = load(near, w_gate)
+    w_up, *token_4 = load(near, w_up)
+    loaded = token_2 + token_3 + token_4
 
     half = HEAD_DIM // 2
     steps_f = jnp.arange(half, dtype=f32)
@@ -446,44 +456,35 @@
     k_angles = freqs[:, None] * routed.astype(f32)
     k_cos, k_sin = jnp.cos(k_angles), jnp.sin(k_angles)
 
-    normed, own, sent = kernel_call(
-        functools.partial(kv_body, count),
-        [((total, model), bf16), ((share, model), bf16), ((count * each, total), bf16)],
-        [*blocks, pick_rows, in_order, columns, attn_gain, w_key, w_value],
+    normed, own, *sent = kernel_call(
+        functools.partial(kv_body, count, len(loaded)),
+        [((total, model), bf16), ((share, model), bf16)] + [((tall * each, total), bf16)] * wide,
+        [*blocks, pick_rows, in_order, columns, attn_gain, w_key, w_value, *loaded],
         [pltpu.VMEM((total, model), bf16)],
         flops=2 * total * model * 512,
     )
-    arrived = lax.all_to_all(sent.reshape(count, each, total), "ctx", 0, 0, tiled=True)
-    arrived = arrived.reshape(count * each, total)
+    arrived = exchange(sent, tall, wide)
     heads_wide = local_heads * HEAD_DIM
     (query,) = kernel_call(
         query_body,
         [((total, heads_wide), bf16)],
-        [normed, from_hbm(w_query), q_cos, q_sin],
-        [pltpu.VMEM((model, heads_wide), bf16), pltpu.SemaphoreType.DMA((4,))],
+        [normed, w_query, q_cos, q_sin],
         flops=2 * total * model * heads_wide,
-        specs=[VMEM, in_hbm, VMEM, VMEM],
     )
     part_shapes = sum_shapes(tall, wide, share, model)
     attn_parts = kernel_call(
         functools.partial(attend_body, plane, kv_local),
         part_shapes,
-        [arrived, query, unmix, k_cos, k_sin, routed, positions, from_hbm(w_output)],
-        [
-            pltpu.VMEM((total, heads_wide), bf16),
-            pltpu.VMEM((heads_wide, model), bf16),
-            pltpu.SemaphoreType.DMA((4,)),
-        ],
+        [*arrived, query, unmix, k_cos, k_sin, routed, positions, w_output],
+        [pltpu.VMEM((total, heads_wide), bf16)],
         flops=2 * total * model * heads_wide,
-        specs=[VMEM] * 7 + [in_hbm],
-    )
-    attn_own, w_down, w_gate = scatter_sum(attn_parts, tall, wide, [w_down, w_gate])
+    )
+    attn_own, w_down = scatter_sum(attn_parts, tall, wide, [w_down])
     own_rows = own.astype(f32)
     hidden = own_rows + attn_own
     mean_sq = jnp.mean(hidden * hidden, axis=-1, keepdims=True)
     mnorm = (hidden * lax.rsqrt(mean_sq + norm_eps) * mlp_gain).astype(bf16)
     pieces = gather_blocks(mnorm, tall, wide)
-    w_up, _ = load(mnorm, w_up)
     hidden_units = w_gate.shape[1]
     mlp_parts = kernel_call(
         functools.partial(mlp_body, plane),

time: 115 us -> 118 us (1.026)
  starting transfers between devices: 34.3 us -> 40.3 us
  waiting for transfers between devices: 49.5 us -> 46.8 us
    ppermute x25 -> x29, starting transfers between devices: 29.2 us -> 40.3 us  [shift(): return lax.ppermute(block, 'ctx', pairs)]
    all_to_all x1 -> x0, starting transfers between devices: 5.13 us -> none  [on_device(): lax.all_to_all(sent.reshape(count, each, total), 'ctx', 0, 0, tiled=True)]
    all_to_all x1 -> x0, waiting for transfers between devices: 4.16 us -> none  [on_device(): lax.all_to_all(sent.reshape(count, each, total), 'ctx', 0, 0, tiled=True)]
    pallas_call x9, Pallas kernels: 13.9 us -> 10.5 us  [kernel_call(): pl.pallas_call(body, out_shape=[jax.ShapeDtypeStruct(s, d) for s, d in ou...]
    pallas_call x4 -> x5, Pallas kernels: 12.4 us -> 15.3 us  [load(): pl.pallas_call(functools.partial(load_body, len(arrays)), out_shape=[pltp...]
    ppermute x25 -> x29, waiting for transfers between devices: 45.3 us -> 46.8 us  [shift(): return lax.ppermute(block, 'ctx', pairs)]
  transfers between devices with their start and end apart: 26 -> 29, of which waited for: 15 -> 17; matrix products, arithmetic and copies ran while one was open for 1% -> 1% of each run, Pallas kernels for 14% -> 14%
where the time goes in v9:
time: 118 us; the launch traced here: 117 us
  waiting for transfers between devices  46.8 us (40%)
  starting transfers between devices  40.3 us (34%)
  Pallas kernels  25.7 us (22%)
  local copies, waits for them, and re-layouts  2.23 us (2%)
  other arithmetic  1.97 us (2%)
    ppermute x29, waiting for transfers between devices, shift(): return lax.ppermute(block, 'ctx', pairs)  46.8 us
    ppermute x29, starting transfers between devices, shift(): return lax.ppermute(block, 'ctx', pairs)  40.3 us
    pallas_call x5, Pallas kernels, load(): pl.pallas_call(functools.partial(load_body, len(arrays)), out_shape=[pltp...  15.3 us
    pallas_call x9, Pallas kernels, kernel_call(): pl.pallas_call(body, out_shape=[jax.ShapeDtypeStruct(s, d) for s, d in ou...  10.5 us
  transfers between devices with their start and end apart: 29, of which 17 were waited for; matrix products, arithmetic and copies ran while one was open for 1% of the time, Pallas kernels for 14%

profile of v9, /device:TPU:0, one launch (start us, length us, event | category | flops | bytes accessed | tf_op | source)
XLA Modules:
  0.0 117.4 jit_solution(17797745845965984449)
XLA Ops:
  0.0 1.5 %shard_map.136.refs_0_ = bf16[32,4096]{1,0:T(8,128)(2,1)S(1)} custom-call(s32[1]{0:T(128)} %bitcast.me, s32[1,128]{1,0:T(1,128)} %bitcast.4, bf16[128,4096]{1,0:T(8,128)(2,1)} %activations_in.1), custom_call_target="tpu_custom_call" | custom-call | flops 33554432 | bytes 1048576 | tf_op jit(solution)/shard_map/pallas_call | solution.py:165
  1.5 5.1 %collective-permute-start.2 = (bf16[32,4096]{1,0:T(8,128)(2,1)S(1)}, bf16[32,4096]{1,0:T(8,128)(2,1)S(1)}, u32[]{:S(2)}, u32[]{:S(2)}) collective-permute-start(bf16[32,4096]{1,0:T(8,128)(2,1)S(1)} %shard_map.136.refs_0_), channel_id=1, source_target_pairs={{0,6},{1,7},{2,0},{3,1},{4,2},{5,3},{6,4},{7,5},{8,14},{9,15},{10,... | collective-permute-start | bytes 786440 | tf_op jit(solution)/shard_map/ppermute | solution.py:34
  8.2 5.2 %collective-permute-done.2.refs_6_ = bf16[32,4096]{1,0:T(8,128)(2,1)S(1)} collective-permute-done((bf16[32,4096]{1,0:T(8,128)(2,1)S(1)}, bf16[32,4096]{1,0:T(8,128)(2,1)S(1)}, u32[]{:S(2)}, u32[]{:S(2)}) %collective-permute-start.2) | collective-permute-done | bytes 262176 | tf_op jit(solution)/shard_map/ppermute | solution.py:34
  18.0 2.9 %shard_map.137 = (f32[1,4096]{1,0:T(1,128)S(1)}, bf16[4096,128]{1,0:T(8,128)(2,1)S(1)}, bf16[4096,128]{1,0:T(8,128)(2,1)S(1)}, bf16[4096,512]{1,0:T(8,128)(2,1)S(1)}, f32[8,128]{1,0:T(8,128)S(1)}) custom-call(bf16[32,4096]{1,0:T(8,128)(2,1)S(1)} %shard_map.136.refs_0_, f32[1,4096]{1,0:T(1,128)} %bitcast.8, bf16[4096,128]{1,0:T(8,128)(2,1)} %refs_2_.1, ...), custom_call_target="tpu_custom_call" | custom-call | bytes 12615680 | tf_op jit(solution)/shard_map/pallas_call | solution.py:190
  23.5 5.6 %collective-permute-done.6 = bf16[32,4096]{1,0:T(8,128)(2,1)S(1)} collective-permute-done((bf16[32,4096]{1,0:T(8,128)(2,1)S(1)}, bf16[32,4096]{1,0:T(8,128)(2,1)S(1)}, u32[]{:S(2)}, u32[]{:S(2)}) %collective-permute-start.6) | collective-permute-done | bytes 262176 | tf_op jit(solution)/shard_map/ppermute | solution.py:34
  30.2 3.4 %shard_map.141 = (bf16[4096,1024]{1,0:T(8,128)(2,1)S(1)}, f32[8,128]{1,0:T(8,128)S(1)}) custom-call(bf16[32,4096]{1,0:T(8,128)(2,1)S(1)} %add.62.refs_0_.refs_4_, bf16[4096,1024]{1,0:T(8,128)(2,1)} %refs_1_.5), custom_call_target="tpu_custom_call" | custom-call | bytes 16777216 | tf_op jit(solution)/shard_map/pallas_call | solution.py:190
  33.6 3.4 %shard_map.142 = (bf16[4096,1024]{1,0:T(8,128)(2,1)S(1)}, f32[8,128]{1,0:T(8,128)S(1)}) custom-call(bf16[32,4096]{1,0:T(8,128)(2,1)S(1)} %add.62.refs_0_.refs_4_, bf16[4096,1024]{1,0:T(8,128)(2,1)} %refs_1_.6), custom_call_target="tpu_custom_call" | custom-call | bytes 16777216 | tf_op jit(solution)/shard_map/pallas_call | solution.py:190
  37.1 2.2 %shard_map.140 = (bf16[512,4096]{1,0:T(8,128)(2,1)S(1)}, f32[8,128]{1,0:T(8,128)S(1)}) custom-call(bf16[32,4096]{1,0:T(8,128)(2,1)S(1)} %add.62.refs_0_.refs_4_, bf16[512,4096]{1,0:T(8,128)(2,1)} %refs_1_.4), custom_call_target="tpu_custom_call" | custom-call | bytes 8388608 | tf_op jit(solution)/shard_map/pallas_call | solution.py:190
  39.3 1.8 %shard_map.143 = (bf16[128,4096]{1,0:T(8,128)(2,1)S(1)}, bf16[16,4096]{1,0:T(8,128)(2,1)S(1)}, bf16[128,128]{1,0:T(8,128)(2,1)S(1)}, bf16[128,128]{1,0:T(8,128)(2,1)S(1)}) custom-call(bf16[32,4096]{1,0:T(8,128)(2,1)S(1)} %shard_map.136.refs_0_, bf16[32,4096]{1,0:T(8,128)(2,1)S(1)} %collective-permute-done.refs_3_.refs_1_, ...), custom_call_target="tpu_custom_call" | custom-call | flops 536870912 | bytes 1048576 | tf_op jit(solution)/shard_map/pallas_call | solution.py:165
  41.1 1.6 %collective-permute-start.8 = (bf16[128,128]{1,0:T(8,128)(2,1)S(1)}, bf16[128,128]{1,0:T(8,128)(2,1)S(1)}, u32[]{:S(2)}, u32[]{:S(2)}) collective-permute-start(bf16[128,128]{1,0:T(8,128)(2,1)S(1)} %get-tuple-element.56), channel_id=1, source_target_pairs={{0,1},{1,0},{2,3},{3,2},{4,5},{5,4},{6,7},{7,6},{8,9},{9,8},{10,11... | collective-permute-start | bytes 98312 | tf_op jit(solution)/shard_map/ppermute | solution.py:34
  42.8 2.3 %collective-permute-done.8.refs_1_ = bf16[128,128]{1,0:T(8,128)(2,1)S(1)} collective-permute-done((bf16[128,128]{1,0:T(8,128)(2,1)S(1)}, bf16[128,128]{1,0:T(8,128)(2,1)S(1)}, u32[]{:S(2)}, u32[]{:S(2)}) %collective-permute-start.8) | collective-permute-done | bytes 32800 | tf_op jit(solution)/shard_map/ppermute | solution.py:34
  45.1 3.2 %collective-permute-start.10 = (bf16[64,128]{1,0:T(8,128)(2,1)S(1)}, bf16[64,128]{1,0:T(8,128)(2,1)S(1)}, u32[]{:S(2)}, u32[]{:S(2)}) collective-permute-start(bf16[64,128]{1,0:T(8,128)(2,1)S(1)} %get-tuple-element.59), channel_id=1, source_target_pairs={{0,4},{1,5},{2,6},{3,7},{4,0},{5,1},{6,2},{7,3},{8,12},{9,13},{10,... | collective-permute-start | bytes 49160 | tf_op jit(solution)/shard_map/ppermute | solution.py:34
  48.2 2.0 %collective-permute-start.11 = (bf16[64,128]{1,0:T(8,128)(2,1)S(1)}, bf16[64,128]{1,0:T(8,128)(2,1)S(1)}, u32[]{:S(2)}, u32[]{:S(2)}) collective-permute-start(bf16[64,128]{1,0:T(8,128)(2,1)S(1)} %get-tuple-element.60), channel_id=1, source_target_pairs={{0,6},{1,7},{2,0},{3,1},{4,2},{5,3},{6,4},{7,5},{8,14},{9,15},{10,... | collective-permute-start | bytes 49160 | tf_op jit(solution)/shard_map/ppermute | solution.py:34
  52.4 3.3 %collective-permute-done.9.refs_1_ = bf16[64,128]{1,0:T(8,128)(2,1)S(1)} collective-permute-done((bf16[64,128]{1,0:T(8,128)(2,1)S(1)}, bf16[64,128]{1,0:T(8,128)(2,1)S(1)}, u32[]{:S(2)}, u32[]{:S(2)}) %collective-permute-start.9) | collective-permute-done | bytes 16416 | tf_op jit(solution)/shard_map/ppermute | solution.py:34
  55.8 1.7 %shard_map.146 = (bf16[16,4096]{1,0:T(8,128)(2,1)S(1)}, bf16[16,4096]{1,0:T(8,128)(2,1)S(1)}, bf16[16,4096]{1,0:T(8,128)(2,1)S(1)}, bf16[16,4096]{1,0:T(8,128)(2...) custom-call(bf16[64,128]{1,0:T(8,128)(2,1)S(1)} %get-tuple-element.57.refs_0_, ...), custom_call_target="tpu_custom_call" | custom-call | flops 536870912 | bytes 1048576 | tf_op jit(solution)/shard_map/pallas_call | solution.py:165
  57.5 1.6 %collective-permute-start.12 = (bf16[32,4096]{1,0:T(8,128)(2,1)S(1)}, bf16[32,4096]{1,0:T(8,128)(2,1)S(1)}, u32[]{:S(2)}, u32[]{:S(2)}) collective-permute-start(bf16[32,4096]{1,0:T(8,128)(2,1)S(1)} %get-tuple-element.66), channel_id=1, source_target_pairs={{0,1},{1,0},{2,3},{3,2},{4,5},{5,4},{6,7},{7,6},{8,9},{9,8},{10,11... | collective-permute-start | bytes 786440 | tf_op jit(solution)/shard_map/ppermute | solution.py:34
  59.6 3.4 %shard_map.147 = (bf16[1024,4096]{1,0:T(8,128)(2,1)S(1)}, f32[8,128]{1,0:T(8,128)S(1)}) custom-call(bf16[16,4096]{1,0:T(8,128)(2,1)S(1)} %get-tuple-element.70.refs_0_, bf16[1024,4096]{1,0:T(8,128)(2,1)} %refs_1_.7), custom_call_target="tpu_custom_call" | custom-call | bytes 16777216 | tf_op jit(solution)/shard_map/pallas_call | solution.py:190
  64.6 2.1 %collective-permute-done.15.refs_0_ = bf16[32,4096]{1,0:T(8,128)(2,1)S(1)} collective-permute-done((bf16[32,4096]{1,0:T(8,128)(2,1)S(1)}, bf16[32,4096]{1,0:T(8,128)(2,1)S(1)}, u32[]{:S(2)}, u32[]{:S(2)}) %collective-permute-start.15) | collective-permute-done | bytes 262176 | tf_op jit(solution)/shard_map/ppermute | solution.py:34
  68.2 7.4 %collective-permute-done.13 = bf16[16,4096]{1,0:T(8,128)(2,1)S(1)} collective-permute-done((bf16[16,4096]{1,0:T(8,128)(2,1)S(1)}, bf16[16,4096]{1,0:T(8,128)(2,1)S(1)}, u32[]{:S(2)}, u32[]{:S(2)}) %collective-permute-start.13) | collective-permute-done | bytes 131104 | tf_op jit(solution)/shard_map/ppermute | solution.py:34
  77.3 2.0 %collective-permute-start.18 = (bf16[16,4096]{1,0:T(8,128)(2,1)S(1)}, bf16[16,4096]{1,0:T(8,128)(2,1)S(1)}, u32[]{:S(2)}, u32[]{:S(2)}) collective-permute-start(bf16[16,4096]{1,0:T(8,128)(2,1)S(1)} %multiply_convert_fusion.refs_0_), channel_id=1, source_target_pairs={{0,2},{1,3},{2,4},{3,5},{4,6},{5,7},{6,0},{7,1},{8,10},{9,11},{10,... | collective-permute-start | bytes 393224 | tf_op jit(solution)/shard_map/ppermute | solution.py:34
  79.4 2.8 %collective-permute-start.22 = (bf16[16,4096]{1,0:T(8,128)(2,1)S(1)}, bf16[16,4096]{1,0:T(8,128)(2,1)S(1)}, u32[]{:S(2)}, u32[]{:S(2)}) collective-permute-start(bf16[16,4096]{1,0:T(8,128)(2,1)S(1)} %multiply_convert_fusion.refs_0_), channel_id=1, source_target_pairs={{0,6},{1,7},{2,0},{3,1},{4,2},{5,3},{6,4},{7,5},{8,14},{9,15},{10,... | collective-permute-start | bytes 393224 | tf_op jit(solution)/shard_map/ppermute | solution.py:34
  84.3 1.5 %collective-permute-start.19 = (bf16[16,4096]{1,0:T(8,128)(2,1)S(1)}, bf16[16,4096]{1,0:T(8,128)(2,1)S(1)}, u32[]{:S(2)}, u32[]{:S(2)}) collective-permute-start(bf16[16,4096]{1,0:T(8,128)(2,1)S(1)} %collective-permute-done.18.refs_2_), channel_id=1, source_target_pairs={{0,1},{1,0},{2,3},{3,2},{4,5},{5,4},{6,7},{7,6},{8,9},{9,8},{10,11... | collective-permute-start | bytes 393224 | tf_op jit(solution)/shard_map/ppermute | solution.py:34
  87.0 1.5 %collective-permute-start.21 = (bf16[16,4096]{1,0:T(8,128)(2,1)S(1)}, bf16[16,4096]{1,0:T(8,128)(2,1)S(1)}, u32[]{:S(2)}, u32[]{:S(2)}) collective-permute-start(bf16[16,4096]{1,0:T(8,128)(2,1)S(1)} %collective-permute-done.20.refs_4_), channel_id=1, source_target_pairs={{0,1},{1,0},{2,3},{3,2},{4,5},{5,4},{6,7},{7,6},{8,9},{9,8},{10,11... | collective-permute-start | bytes 393224 | tf_op jit(solution)/shard_map/ppermute | solution.py:34
  89.0 1.6 %collective-permute-done.19.refs_3_ = bf16[16,4096]{1,0:T(8,128)(2,1)S(1)} collective-permute-done((bf16[16,4096]{1,0:T(8,128)(2,1)S(1)}, bf16[16,4096]{1,0:T(8,128)(2,1)S(1)}, u32[]{:S(2)}, u32[]{:S(2)}) %collective-permute-start.19) | collective-permute-done | bytes 131104 | tf_op jit(solution)/shard_map/ppermute | solution.py:34
  90.6 2.8 %collective-permute-done.21.refs_5_ = bf16[16,4096]{1,0:T(8,128)(2,1)S(1)} collective-permute-done((bf16[16,4096]{1,0:T(8,128)(2,1)S(1)}, bf16[16,4096]{1,0:T(8,128)(2,1)S(1)}, u32[]{:S(2)}, u32[]{:S(2)}) %collective-permute-start.21) | collective-permute-done | bytes 131104 | tf_op jit(solution)/shard_map/ppermute | solution.py:34
  93.4 2.8 %collective-permute-done.23.refs_7_ = bf16[16,4096]{1,0:T(8,128)(2,1)S(1)} collective-permute-done((bf16[16,4096]{1,0:T(8,128)(2,1)S(1)}, bf16[16,4096]{1,0:T(8,128)(2,1)S(1)}, u32[]{:S(2)}, u32[]{:S(2)}) %collective-permute-start.23) | collective-permute-done | bytes 131104 | tf_op jit(solution)/shard_map/ppermute | solution.py:34
  96.2 3.7 %shard_map.149 = (bf16[16,4096]{1,0:T(8,128)(2,1)S(1)}, bf16[16,4096]{1,0:T(8,128)(2,1)S(1)}, bf16[16,4096]{1,0:T(8,128)(2,1)S(1)}, bf16[16,4096]{1,0:T(8,128)(2...) custom-call(bf16[16,4096]{1,0:T(8,128)(2,1)S(1)} %multiply_convert_fusion.refs_0_, ...), custom_call_target="tpu_custom_call" | custom-call | flops 3221225472 | bytes 1048576 | tf_op jit(solution)/shard_map/pallas_call | solution.py:165
  99.9 1.6 %collective-permute-start.24 = (bf16[32,4096]{1,0:T(8,128)(2,1)S(1)}, bf16[32,4096]{1,0:T(8,128)(2,1)S(1)}, u32[]{:S(2)}, u32[]{:S(2)}) collective-permute-start(bf16[32,4096]{1,0:T(8,128)(2,1)S(1)} %get-tuple-element.76), channel_id=1, source_target_pairs={{0,1},{1,0},{2,3},{3,2},{4,5},{5,4},{6,7},{7,6},{8,9},{9,8},{10,11... | collective-permute-start | bytes 786440 | tf_op jit(solution)/shard_map/ppermute | solution.py:34
  102.0 4.3 %collective-permute-done.24 = bf16[32,4096]{1,0:T(8,128)(2,1)S(1)} collective-permute-done((bf16[32,4096]{1,0:T(8,128)(2,1)S(1)}, bf16[32,4096]{1,0:T(8,128)(2,1)S(1)}, u32[]{:S(2)}, u32[]{:S(2)}) %collective-permute-start.24) | collective-permute-done | bytes 262176 | tf_op jit(solution)/shard_map/ppermute | solution.py:34
  107.0 2.9 %collective-permute-start.26 = (bf16[16,4096]{1,0:T(8,128)(2,1)S(1)}, bf16[16,4096]{1,0:T(8,128)(2,1)S(1)}, u32[]{:S(2)}, u32[]{:S(2)}) collective-permute-start(bf16[16,4096]{1,0:T(8,128)(2,1)S(1)} %get-tuple-element.87), channel_id=1, source_target_pairs={{0,2},{1,3},{2,4},{3,5},{4,6},{5,7},{6,0},{7,1},{8,10},{9,11},{10,... | collective-permute-start | bytes 393224 | tf_op jit(solution)/shard_map/ppermute | solution.py:34
  110.0 2.2 %collective-permute-start.28 = (bf16[16,4096]{1,0:T(8,128)(2,1)S(1)}, bf16[16,4096]{1,0:T(8,128)(2,1)S(1)}, u32[]{:S(2)}, u32[]{:S(2)}) collective-permute-start(bf16[16,4096]{1,0:T(8,128)(2,1)S(1)} %add_convert_fusion), channel_id=1, source_target_pairs={{0,6},{1,7},{2,0},{3,1},{4,2},{5,3},{6,4},{7,5},{8,14},{9,15},{10,... | collective-permute-start | bytes 393224 | tf_op jit(solution)/shard_map/ppermute | solution.py:34
  112.2 3.1 %collective-permute-done.25 = bf16[16,4096]{1,0:T(8,128)(2,1)S(1)} collective-permute-done((bf16[16,4096]{1,0:T(8,128)(2,1)S(1)}, bf16[16,4096]{1,0:T(8,128)(2,1)S(1)}, u32[]{:S(2)}, u32[]{:S(2)}) %collective-permute-start.25) | collective-permute-done | bytes 131104 | tf_op jit(solution)/shard_map/ppermute | solution.py:34
  (66 shorter events, 24.4 us)
Async XLA Ops:
  1.5 11.8 %collective-permute-start.2 = (bf16[32,4096]{1,0:T(8,128)(2,1)S(1)}, bf16[32,4096]{1,0:T(8,128)(2,1)S(1)}, u32[]{:S(2)}, u32[]{:S(2)}) collective-permute-start(bf16[32,4096]{1,0:T(8,128)(2,1)S(1)} %shard_map.136.refs_0_), channel_id=1, source_target_pairs={{0,6},{1,7},{2,0},{3,1},{4,2},{5,3},{6,4},{7,5},{8,14},{9,15},{10,... | collective-permute-start | bytes 786440 | tf_op jit(solution)/shard_map/ppermute | solution.py:34
  6.6 15.5 %collective-permute-start = (bf16[32,4096]{1,0:T(8,128)(2,1)S(1)}, bf16[32,4096]{1,0:T(8,128)(2,1)S(1)}, u32[]{:S(2)}, u32[]{:S(2)}) collective-permute-start(bf16[32,4096]{1,0:T(8,128)(2,1)S(1)} %shard_map.136.refs_0_), channel_id=1, source_target_pairs={{0,1},{1,0},{2,3},{3,2},{4,5},{5,4},{6,7},{7,6},{8,9},{9,8},{10,11... | collective-permute-start | bytes 786440 | tf_op jit(solution)/shard_map/ppermute | solution.py:34
  8.2 14.0 %collective-permute-start.1 = (bf16[32,4096]{1,0:T(8,128)(2,1)S(1)}, bf16[32,4096]{1,0:T(8,128)(2,1)S(1)}, u32[]{:S(2)}, u32[]{:S(2)}) collective-permute-start(bf16[32,4096]{1,0:T(8,128)(2,1)S(1)} %shard_map.136.refs_0_), channel_id=1, source_target_pairs={{0,2},{1,3},{2,4},{3,5},{4,6},{5,7},{6,0},{7,1},{8,10},{9,11},{10,... | collective-permute-start | bytes 786440 | tf_op jit(solution)/shard_map/ppermute | solution.py:34
  13.4 8.8 %collective-permute-start.3 = (bf16[32,4096]{1,0:T(8,128)(2,1)S(1)}, bf16[32,4096]{1,0:T(8,128)(2,1)S(1)}, u32[]{:S(2)}, u32[]{:S(2)}) collective-permute-start(bf16[32,4096]{1,0:T(8,128)(2,1)S(1)} %collective-permute-done.2.refs_6_), channel_id=1, source_target_pairs={{0,1},{1,0},{2,3},{3,2},{4,5},{5,4},{6,7},{7,6},{8,9},{9,8},{10,11... | collective-permute-start | bytes 786440 | tf_op jit(solution)/shard_map/ppermute | solution.py:34
  20.9 8.3 %collective-permute-start.6 = (bf16[32,4096]{1,0:T(8,128)(2,1)S(1)}, bf16[32,4096]{1,0:T(8,128)(2,1)S(1)}, u32[]{:S(2)}, u32[]{:S(2)}) collective-permute-start(bf16[32,4096]{1,0:T(8,128)(2,1)S(1)} %collective-permute-done.2.refs_6_), channel_id=1, source_target_pairs={{2,0},{3,1},{4,2},{5,3},{10,8},{11,9},{12,10},{13,11},{18,16},{19,... | collective-permute-start | bytes 786440 | tf_op jit(solution)/shard_map/ppermute | solution.py:34
  22.2 6.9 %collective-permute-start.5 = (bf16[32,4096]{1,0:T(8,128)(2,1)S(1)}, bf16[32,4096]{1,0:T(8,128)(2,1)S(1)}, u32[]{:S(2)}, u32[]{:S(2)}) collective-permute-start(bf16[32,4096]{1,0:T(8,128)(2,1)S(1)} %shard_map.139.refs_2_), channel_id=1, source_target_pairs={{2,4},{3,5},{4,6},{5,7},{10,12},{11,13},{12,14},{13,15},{18,20},{1... | collective-permute-start | bytes 786440 | tf_op jit(solution)/shard_map/ppermute | solution.py:34
  22.9 16.3 %collective-permute-start.4 = (bf16[32,4096]{1,0:T(8,128)(2,1)S(1)}, bf16[32,4096]{1,0:T(8,128)(2,1)S(1)}, u32[]{:S(2)}, u32[]{:S(2)}) collective-permute-start(bf16[32,4096]{1,0:T(8,128)(2,1)S(1)} %shard_map.139.refs_2_), channel_id=1, source_target_pairs={{0,1},{1,0},{2,3},{3,2},{4,5},{5,4},{6,7},{7,6},{8,9},{9,8},{10,11... | collective-permute-start | bytes 786440 | tf_op jit(solution)/shard_map/ppermute | solution.py:34
  29.2 10.1 %collective-permute-start.7 = (bf16[32,4096]{1,0:T(8,128)(2,1)S(1)}, bf16[32,4096]{1,0:T(8,128)(2,1)S(1)}, u32[]{:S(2)}, u32[]{:S(2)}) collective-permute-start(bf16[32,4096]{1,0:T(8,128)(2,1)S(1)} %add.62.refs_0_.refs_4_), channel_id=1, source_target_pairs={{0,1},{1,0},{2,3},{3,2},{4,5},{5,4},{6,7},{7,6},{8,9},{9,8},{10,11... | collective-permute-start | bytes 786440 | tf_op jit(solution)/shard_map/ppermute | solution.py:34
  37.0 18.7 %copy-start.2 = (s32[128]{0:T(128)S(1)}, s32[128]{0:T(128)}, u32[]{:S(2)}) copy-start(s32[128]{0:T(128)} %param.15) | copy-start | bytes 1540
  41.1 4.0 %collective-permute-start.8 = (bf16[128,128]{1,0:T(8,128)(2,1)S(1)}, bf16[128,128]{1,0:T(8,128)(2,1)S(1)}, u32[]{:S(2)}, u32[]{:S(2)}) collective-permute-start(bf16[128,128]{1,0:T(8,128)(2,1)S(1)} %get-tuple-element.56), channel_id=1, source_target_pairs={{0,1},{1,0},{2,3},{3,2},{4,5},{5,4},{6,7},{7,6},{8,9},{9,8},{10,11... | collective-permute-start | bytes 98312 | tf_op jit(solution)/shard_map/ppermute | solution.py:34
  45.1 6.5 %collective-permute-start.10 = (bf16[64,128]{1,0:T(8,128)(2,1)S(1)}, bf16[64,128]{1,0:T(8,128)(2,1)S(1)}, u32[]{:S(2)}, u32[]{:S(2)}) collective-permute-start(bf16[64,128]{1,0:T(8,128)(2,1)S(1)} %get-tuple-element.59), channel_id=1, source_target_pairs={{0,4},{1,5},{2,6},{3,7},{4,0},{5,1},{6,2},{7,3},{8,12},{9,13},{10,... | collective-permute-start | bytes 49160 | tf_op jit(solution)/shard_map/ppermute | solution.py:34
  48.2 4.2 %collective-permute-start.11 = (bf16[64,128]{1,0:T(8,128)(2,1)S(1)}, bf16[64,128]{1,0:T(8,128)(2,1)S(1)}, u32[]{:S(2)}, u32[]{:S(2)}) collective-permute-start(bf16[64,128]{1,0:T(8,128)(2,1)S(1)} %get-tuple-element.60), channel_id=1, source_target_pairs={{0,6},{1,7},{2,0},{3,1},{4,2},{5,3},{6,4},{7,5},{8,14},{9,15},{10,... | collective-permute-start | bytes 49160 | tf_op jit(solution)/shard_map/ppermute | solution.py:34
  50.2 5.5 %collective-permute-start.9 = (bf16[64,128]{1,0:T(8,128)(2,1)S(1)}, bf16[64,128]{1,0:T(8,128)(2,1)S(1)}, u32[]{:S(2)}, u32[]{:S(2)}) collective-permute-start(bf16[64,128]{1,0:T(8,128)(2,1)S(1)} %get-tuple-element.58), channel_id=1, source_target_pairs={{0,2},{1,3},{2,4},{3,5},{4,6},{5,7},{6,0},{7,1},{8,10},{9,11},{10,... | collective-permute-start | bytes 49160 | tf_op jit(solution)/shard_map/ppermute | solution.py:34
  51.6 25.4 %copy-start.4 = (f32[4096]{0:T(1024)S(1)}, f32[4096]{0:T(1024)}, u32[]{:S(2)}) copy-start(f32[4096]{0:T(1024)} %param.26) | copy-start | bytes 49156
  51.6 25.7 %copy-start.5 = (f32[4096]{0:T(1024)S(1)}, f32[4096]{0:T(1024)}, u32[]{:S(2)}) copy-start(f32[4096]{0:T(1024)} %param.22) | copy-start | bytes 49156
  57.5 6.4 %collective-permute-start.12 = (bf16[32,4096]{1,0:T(8,128)(2,1)S(1)}, bf16[32,4096]{1,0:T(8,128)(2,1)S(1)}, u32[]{:S(2)}, u32[]{:S(2)}) collective-permute-start(bf16[32,4096]{1,0:T(8,128)(2,1)S(1)} %get-tuple-element.66), channel_id=1, source_target_pairs={{0,1},{1,0},{2,3},{3,2},{4,5},{5,4},{6,7},{7,6},{8,9},{9,8},{10,11... | collective-permute-start | bytes 786440 | tf_op jit(solution)/shard_map/ppermute | solution.py:34
  59.1 7.7 %collective-permute-start.15 = (bf16[32,4096]{1,0:T(8,128)(2,1)S(1)}, bf16[32,4096]{1,0:T(8,128)(2,1)S(1)}, u32[]{:S(2)}, u32[]{:S(2)}) collective-permute-start(bf16[32,4096]{1,0:T(8,128)(2,1)S(1)} %get-tuple-element.69), channel_id=1, source_target_pairs={{0,1},{1,0},{2,3},{3,2},{4,5},{5,4},{6,7},{7,6},{8,9},{9,8},{10,11... | collective-permute-start | bytes 786440 | tf_op jit(solution)/shard_map/ppermute | solution.py:34
  64.0 11.6 %collective-permute-start.13 = (bf16[16,4096]{1,0:T(8,128)(2,1)S(1)}, bf16[16,4096]{1,0:T(8,128)(2,1)S(1)}, u32[]{:S(2)}, u32[]{:S(2)}) collective-permute-start(bf16[16,4096]{1,0:T(8,128)(2,1)S(1)} %get-tuple-element.88), channel_id=1, source_target_pairs={{0,4},{1,5},{2,6},{3,7},{4,0},{5,1},{6,2},{7,3},{8,12},{9,13},{10,... | collective-permute-start | bytes 393224 | tf_op jit(solution)/shard_map/ppermute | solution.py:34
  64.2 11.4 %collective-permute-start.14 = (bf16[16,4096]{1,0:T(8,128)(2,1)S(1)}, bf16[16,4096]{1,0:T(8,128)(2,1)S(1)}, u32[]{:S(2)}, u32[]{:S(2)}) collective-permute-start(bf16[16,4096]{1,0:T(8,128)(2,1)S(1)} %get-tuple-element.89), channel_id=1, source_target_pairs={{0,2},{1,3},{2,4},{3,5},{4,6},{5,7},{6,0},{7,1},{8,10},{9,11},{10,... | collective-permute-start | bytes 393224 | tf_op jit(solution)/shard_map/ppermute | solution.py:34
  66.8 10.1 %collective-permute-start.16 = (bf16[16,4096]{1,0:T(8,128)(2,1)S(1)}, bf16[16,4096]{1,0:T(8,128)(2,1)S(1)}, u32[]{:S(2)}, u32[]{:S(2)}) collective-permute-start(bf16[16,4096]{1,0:T(8,128)(2,1)S(1)} %add_convert_fusion.3), channel_id=1, source_target_pairs={{0,6},{1,7},{2,0},{3,1},{4,2},{5,3},{6,4},{7,5},{8,14},{9,15},{10,... | collective-permute-start | bytes 393224 | tf_op jit(solution)/shard_map/ppermute | solution.py:34
  77.3 6.9 %collective-permute-start.18 = (bf16[16,4096]{1,0:T(8,128)(2,1)S(1)}, bf16[16,4096]{1,0:T(8,128)(2,1)S(1)}, u32[]{:S(2)}, u32[]{:S(2)}) collective-permute-start(bf16[16,4096]{1,0:T(8,128)(2,1)S(1)} %multiply_convert_fusion.refs_0_), channel_id=1, source_target_pairs={{0,2},{1,3},{2,4},{3,5},{4,6},{5,7},{6,0},{7,1},{8,10},{9,11},{10,... | collective-permute-start | bytes 393224 | tf_op jit(solution)/shard_map/ppermute | solution.py:34
  79.4 7.6 %collective-permute-start.20 = (bf16[16,4096]{1,0:T(8,128)(2,1)S(1)}, bf16[16,4096]{1,0:T(8,128)(2,1)S(1)}, u32[]{:S(2)}, u32[]{:S(2)}) collective-permute-start(bf16[16,4096]{1,0:T(8,128)(2,1)S(1)} %multiply_convert_fusion.refs_0_), channel_id=1, source_target_pairs={{0,4},{1,5},{2,6},{3,7},{4,0},{5,1},{6,2},{7,3},{8,12},{9,13},{10,... | collective-permute-start | bytes 393224 | tf_op jit(solution)/shard_map/ppermute | solution.py:34
  79.4 9.1 %collective-permute-start.22 = (bf16[16,4096]{1,0:T(8,128)(2,1)S(1)}, bf16[16,4096]{1,0:T(8,128)(2,1)S(1)}, u32[]{:S(2)}, u32[]{:S(2)}) collective-permute-start(bf16[16,4096]{1,0:T(8,128)(2,1)S(1)} %multiply_convert_fusion.refs_0_), channel_id=1, source_target_pairs={{0,6},{1,7},{2,0},{3,1},{4,2},{5,3},{6,4},{7,5},{8,14},{9,15},{10,... | collective-permute-start | bytes 393224 | tf_op jit(solution)/shard_map/ppermute | solution.py:34
  82.2 6.8 %collective-permute-start.17 = (bf16[16,4096]{1,0:T(8,128)(2,1)S(1)}, bf16[16,4096]{1,0:T(8,128)(2,1)S(1)}, u32[]{:S(2)}, u32[]{:S(2)}) collective-permute-start(bf16[16,4096]{1,0:T(8,128)(2,1)S(1)} %multiply_convert_fusion.refs_0_), channel_id=1, source_target_pairs={{0,1},{1,0},{2,3},{3,2},{4,5},{5,4},{6,7},{7,6},{8,9},{9,8},{10,11... | collective-permute-start | bytes 393224 | tf_op jit(solution)/shard_map/ppermute | solution.py:34
  84.3 6.3 %collective-permute-start.19 = (bf16[16,4096]{1,0:T(8,128)(2,1)S(1)}, bf16[16,4096]{1,0:T(8,128)(2,1)S(1)}, u32[]{:S(2)}, u32[]{:S(2)}) collective-permute-start(bf16[16,4096]{1,0:T(8,128)(2,1)S(1)} %collective-permute-done.18.refs_2_), channel_id=1, source_target_pairs={{0,1},{1,0},{2,3},{3,2},{4,5},{5,4},{6,7},{7,6},{8,9},{9,8},{10,11... | collective-permute-start | bytes 393224 | tf_op jit(solution)/shard_map/ppermute | solution.py:34
  87.0 6.5 %collective-permute-start.21 = (bf16[16,4096]{1,0:T(8,128)(2,1)S(1)}, bf16[16,4096]{1,0:T(8,128)(2,1)S(1)}, u32[]{:S(2)}, u32[]{:S(2)}) collective-permute-start(bf16[16,4096]{1,0:T(8,128)(2,1)S(1)} %collective-permute-done.20.refs_4_), channel_id=1, source_target_pairs={{0,1},{1,0},{2,3},{3,2},{4,5},{5,4},{6,7},{7,6},{8,9},{9,8},{10,11... | collective-permute-start | bytes 393224 | tf_op jit(solution)/shard_map/ppermute | solution.py:34
  88.5 7.7 %collective-permute-start.23 = (bf16[16,4096]{1,0:T(8,128)(2,1)S(1)}, bf16[16,4096]{1,0:T(8,128)(2,1)S(1)}, u32[]{:S(2)}, u32[]{:S(2)}) collective-permute-start(bf16[16,4096]{1,0:T(8,128)(2,1)S(1)} %collective-permute-done.22.refs_6_), channel_id=1, source_target_pairs={{0,1},{1,0},{2,3},{3,2},{4,5},{5,4},{6,7},{7,6},{8,9},{9,8},{10,11... | collective-permute-start | bytes 393224 | tf_op jit(solution)/shard_map/ppermute | solution.py:34
  99.9 6.4 %collective-permute-start.24 = (bf16[32,4096]{1,0:T(8,128)(2,1)S(1)}, bf16[32,4096]{1,0:T(8,128)(2,1)S(1)}, u32[]{:S(2)}, u32[]{:S(2)}) collective-permute-start(bf16[32,4096]{1,0:T(8,128)(2,1)S(1)} %get-tuple-element.76), channel_id=1, source_target_pairs={{0,1},{1,0},{2,3},{3,2},{4,5},{5,4},{6,7},{7,6},{8,9},{9,8},{10,11... | collective-permute-start | bytes 786440 | tf_op jit(solution)/shard_map/ppermute | solution.py:34
  101.5 8.5 %collective-permute-start.27 = (bf16[32,4096]{1,0:T(8,128)(2,1)S(1)}, bf16[32,4096]{1,0:T(8,128)(2,1)S(1)}, u32[]{:S(2)}, u32[]{:S(2)}) collective-permute-start(bf16[32,4096]{1,0:T(8,128)(2,1)S(1)} %get-tuple-element.79), channel_id=1, source_target_pairs={{0,1},{1,0},{2,3},{3,2},{4,5},{5,4},{6,7},{7,6},{8,9},{9,8},{10,11... | collective-permute-start | bytes 786440 | tf_op jit(solution)/shard_map/ppermute | solution.py:34
  106.4 8.8 %collective-permute-start.25 = (bf16[16,4096]{1,0:T(8,128)(2,1)S(1)}, bf16[16,4096]{1,0:T(8,128)(2,1)S(1)}, u32[]{:S(2)}, u32[]{:S(2)}) collective-permute-start(bf16[16,4096]{1,0:T(8,128)(2,1)S(1)} %get-tuple-element.86), channel_id=1, source_target_pairs={{0,4},{1,5},{2,6},{3,7},{4,0},{5,1},{6,2},{7,3},{8,12},{9,13},{10,... | collective-permute-start | bytes 393224 | tf_op jit(solution)/shard_map/ppermute | solution.py:34
  107.0 8.2 %collective-permute-start.26 = (bf16[16,4096]{1,0:T(8,128)(2,1)S(1)}, bf16[16,4096]{1,0:T(8,128)(2,1)S(1)}, u32[]{:S(2)}, u32[]{:S(2)}) collective-permute-start(bf16[16,4096]{1,0:T(8,128)(2,1)S(1)} %get-tuple-element.87), channel_id=1, source_target_pairs={{0,2},{1,3},{2,4},{3,5},{4,6},{5,7},{6,0},{7,1},{8,10},{9,11},{10,... | collective-permute-start | bytes 393224 | tf_op jit(solution)/shard_map/ppermute | solution.py:34
  110.0 6.6 %collective-permute-start.28 = (bf16[16,4096]{1,0:T(8,128)(2,1)S(1)}, bf16[16,4096]{1,0:T(8,128)(2,1)S(1)}, u32[]{:S(2)}, u32[]{:S(2)}) collective-permute-start(bf16[16,4096]{1,0:T(8,128)(2,1)S(1)} %add_convert_fusion), channel_id=1, source_target_pairs={{0,6},{1,7},{2,0},{3,1},{4,2},{5,3},{6,4},{7,5},{8,14},{9,15},{10,... | collective-permute-start | bytes 393224 | tf_op jit(solution)/shard_map/ppermute | solution.py:34
  (3 other events, 2.2 us)

commit v10 on v9

--- a/solution.py
+++ b/solution.py
@@ -52,19 +52,19 @@
 
 def gather_rows(block, tall, wide, tokens):
     blocks = {(0, 0): block}
-    for dz in range(1, tall):
+    for dy in range(1, wide):
+        blocks[0, dy] = shift(block, tall, wide, 0, dy)
+    first = [*tokens, *(blocks[0, dy] for dy in range(1, wide))]
+    for dz in range(tall - 1, 0, -1):
         if tall != 4 or dz != 2:
             blocks[dz, 0] = shift(block, tall, wide, dz, 0)
-    for dy in range(1, wide):
-        blocks[0, dy] = shift(block, tall, wide, 0, dy)
-        if tall == 4:
+    blocks[tall - 1, 0] = tie([blocks[tall - 1, 0]], first)
+    if tall == 4:
+        for dy in range(1, wide):
             blocks[3, dy] = shift(blocks[3, 0], tall, wide, 0, dy)
-    early = [b for (_, dy), b in blocks.items() if dy]
-    blocks[1, 0] = tie([blocks[1, 0]], [*tokens, *early])
-    if tall == 4:
         up = shift(blocks[1, 0], tall, wide, 1, 0, lambda z: z in (1, 2))
         down = shift(blocks[3, 0], tall, wide, -1, 0, lambda z: z in (1, 2))
-        blocks[2, 0] = up + down
+        blocks[2, 0] = tie([up, down], [blocks[3, dy] for dy in range(1, wide)])
     for dz in range(1, tall):
         for dy in range(1, wide):
             if (dz, dy) not in blocks:
@@ -443,8 +443,7 @@
     near = blocks[2 * wide]
     w_output, *token_2 = load(near, w_output)
     w_gate, *token_3 = load(near, w_gate)
-    w_up, *token_4 = load(near, w_up)
-    loaded = token_2 + token_3 + token_4
+    loaded = token_2 + token_3
 
     half = HEAD_DIM // 2
     steps_f = jnp.arange(half, dtype=f32)
@@ -485,6 +484,7 @@
     mean_sq = jnp.mean(hidden * hidden, axis=-1, keepdims=True)
     mnorm = (hidden * lax.rsqrt(mean_sq + norm_eps) * mlp_gain).astype(bf16)
     pieces = gather_blocks(mnorm, tall, wide)
+    w_up, _ = load(mnorm, w_up)
     hidden_units = w_gate.shape[1]
     mlp_parts = kernel_call(
         functools.partial(mlp_body, plane),

time: 118 us -> 112 us (0.949)
  waiting for transfers between devices: 46.8 us -> 36.4 us
  starting transfers between devices: 40.3 us -> 44.9 us
    ppermute x29, waiting for transfers between devices: 46.8 us -> 36.4 us  [shift(): return lax.ppermute(block, 'ctx', pairs)]
    ppermute x29, starting transfers between devices: 40.3 us -> 44.9 us  [shift(): return lax.ppermute(block, 'ctx', pairs)]
    pallas_call x9 -> x10, Pallas kernels: 10.5 us -> 10.3 us  [kernel_call(): pl.pallas_call(body, out_shape=[jax.ShapeDtypeStruct(s, d) for s, d in ou...]
  transfers between devices with their start and end apart: 29 -> 29, of which waited for: 17 -> 17; matrix products, arithmetic and copies ran while one was open for 1% -> 1% of each run, Pallas kernels for 14% -> 16%
where the time goes in v10:
time: 112 us
  starting transfers between devices  44.9 us (40%)
  waiting for transfers between devices  36.4 us (32%)
  Pallas kernels  26.2 us (23%)
  local copies, waits for them, and re-layouts  2.23 us (2%)
  other arithmetic  1.88 us (2%)
    ppermute x29, starting transfers between devices, shift(): return lax.ppermute(block, 'ctx', pairs)  44.9 us
    ppermute x29, waiting for transfers between devices, shift(): return lax.ppermute(block, 'ctx', pairs)  36.4 us
    pallas_call x5, Pallas kernels, load(): pl.pallas_call(functools.partial(load_body, len(arrays)), out_shape=[pltp...  15.9 us
    pallas_call x10, Pallas kernels, kernel_call(): pl.pallas_call(body, out_shape=[jax.ShapeDtypeStruct(s, d) for s, d in ou...  10.3 us
  transfers between devices with their start and end apart: 29, of which 17 were waited for; matrix products, arithmetic and copies ran while one was open for 1% of the time, Pallas kernels for 16%

profile of v10, /device:TPU:0, one launch (start us, length us, event | category | flops | bytes accessed | tf_op | source)
XLA Modules:
  0.0 111.9 jit_solution(14809264392824824712)
XLA Ops:
  0.0 1.6 %shard_map.136.refs_0_ = bf16[32,4096]{1,0:T(8,128)(2,1)S(1)} custom-call(s32[1]{0:T(128)} %bitcast.me, s32[1,128]{1,0:T(1,128)} %bitcast.4, bf16[128,4096]{1,0:T(8,128)(2,1)} %activations_in.1), custom_call_target="tpu_custom_call" | custom-call | flops 33554432 | bytes 1048576 | tf_op jit(solution)/shard_map/pallas_call | solution.py:165
  1.6 3.1 %collective-permute-start.1 = (bf16[32,4096]{1,0:T(8,128)(2,1)S(1)}, bf16[32,4096]{1,0:T(8,128)(2,1)S(1)}, u32[]{:S(2)}, u32[]{:S(2)}) collective-permute-start(bf16[32,4096]{1,0:T(8,128)(2,1)S(1)} %shard_map.136.refs_0_), channel_id=1, source_target_pairs={{0,2},{1,3},{2,4},{3,5},{4,6},{5,7},{6,0},{7,1},{8,10},{9,11},{10,... | collective-permute-start | bytes 786440 | tf_op jit(solution)/shard_map/ppermute | solution.py:34
  4.6 2.1 %collective-permute-start.4 = (bf16[32,4096]{1,0:T(8,128)(2,1)S(1)}, bf16[32,4096]{1,0:T(8,128)(2,1)S(1)}, u32[]{:S(2)}, u32[]{:S(2)}) collective-permute-start(bf16[32,4096]{1,0:T(8,128)(2,1)S(1)} %shard_map.136.refs_0_), channel_id=1, source_target_pairs={{0,6},{1,7},{2,0},{3,1},{4,2},{5,3},{6,4},{7,5},{8,14},{9,15},{10,... | collective-permute-start | bytes 786440 | tf_op jit(solution)/shard_map/ppermute | solution.py:34
  6.7 1.7 %collective-permute-start = (bf16[32,4096]{1,0:T(8,128)(2,1)S(1)}, bf16[32,4096]{1,0:T(8,128)(2,1)S(1)}, u32[]{:S(2)}, u32[]{:S(2)}) collective-permute-start(bf16[32,4096]{1,0:T(8,128)(2,1)S(1)} %shard_map.136.refs_0_), channel_id=1, source_target_pairs={{0,1},{1,0},{2,3},{3,2},{4,5},{5,4},{6,7},{7,6},{8,9},{9,8},{10,11... | collective-permute-start | bytes 786440 | tf_op jit(solution)/shard_map/ppermute | solution.py:34
  11.5 2.9 %shard_map.137 = (f32[1,4096]{1,0:T(1,128)S(1)}, bf16[4096,128]{1,0:T(8,128)(2,1)S(1)}, bf16[4096,128]{1,0:T(8,128)(2,1)S(1)}, bf16[4096,512]{1,0:T(8,128)(2,1)S(1)}, f32[8,128]{1,0:T(8,128)S(1)}) custom-call(bf16[32,4096]{1,0:T(8,128)(2,1)S(1)} %shard_map.136.refs_0_, f32[1,4096]{1,0:T(1,128)} %bitcast.8, bf16[4096,128]{1,0:T(8,128)(2,1)} %refs_2_.1, ...), custom_call_target="tpu_custom_call" | custom-call | bytes 12615680 | tf_op jit(solution)/shard_map/pallas_call | solution.py:190
  15.1 2.9 %collective-permute-done.4.refs_0_ = bf16[32,4096]{1,0:T(8,128)(2,1)S(1)} collective-permute-done((bf16[32,4096]{1,0:T(8,128)(2,1)S(1)}, bf16[32,4096]{1,0:T(8,128)(2,1)S(1)}, u32[]{:S(2)}, u32[]{:S(2)}) %collective-permute-start.4) | collective-permute-done | bytes 262176 | tf_op jit(solution)/shard_map/ppermute | solution.py:34
  18.0 1.6 %collective-permute-start.6 = (bf16[32,4096]{1,0:T(8,128)(2,1)S(1)}, bf16[32,4096]{1,0:T(8,128)(2,1)S(1)}, u32[]{:S(2)}, u32[]{:S(2)}) collective-permute-start(bf16[32,4096]{1,0:T(8,128)(2,1)S(1)} %shard_map.139.refs_6_), channel_id=1, source_target_pairs={{0,1},{1,0},{2,3},{3,2},{4,5},{5,4},{6,7},{7,6},{8,9},{9,8},{10,11... | collective-permute-start | bytes 786440 | tf_op jit(solution)/shard_map/ppermute | solution.py:34
  21.5 5.8 %collective-permute-done.6.refs_2_.refs_7_ = bf16[32,4096]{1,0:T(8,128)(2,1)S(1)} collective-permute-done((bf16[32,4096]{1,0:T(8,128)(2,1)S(1)}, bf16[32,4096]{1,0:T(8,128)(2,1)S(1)}, u32[]{:S(2)}, u32[]{:S(2)}) %collective-permute-start.6) | collective-permute-done | bytes 262176 | tf_op jit(solution)/shard_map/ppermute | solution.py:34
  27.4 2.3 %collective-permute-done.5.refs_1_ = bf16[32,4096]{1,0:T(8,128)(2,1)S(1)} collective-permute-done((bf16[32,4096]{1,0:T(8,128)(2,1)S(1)}, bf16[32,4096]{1,0:T(8,128)(2,1)S(1)}, u32[]{:S(2)}, u32[]{:S(2)}) %collective-permute-start.5) | collective-permute-done | bytes 262176 | tf_op jit(solution)/shard_map/ppermute | solution.py:34
  30.7 2.2 %shard_map.141 = (bf16[512,4096]{1,0:T(8,128)(2,1)S(1)}, f32[8,128]{1,0:T(8,128)S(1)}) custom-call(bf16[32,4096]{1,0:T(8,128)(2,1)S(1)} %shard_map.140.refs_0_.refs_4_, bf16[512,4096]{1,0:T(8,128)(2,1)} %refs_1_.4), custom_call_target="tpu_custom_call" | custom-call | bytes 8388608 | tf_op jit(solution)/shard_map/pallas_call | solution.py:190
  32.9 3.4 %shard_map.142 = (bf16[4096,1024]{1,0:T(8,128)(2,1)S(1)}, f32[8,128]{1,0:T(8,128)S(1)}) custom-call(bf16[32,4096]{1,0:T(8,128)(2,1)S(1)} %shard_map.140.refs_0_.refs_4_, bf16[4096,1024]{1,0:T(8,128)(2,1)} %refs_1_.5), custom_call_target="tpu_custom_call" | custom-call | bytes 16777216 | tf_op jit(solution)/shard_map/pallas_call | solution.py:190
  37.0 1.8 %shard_map.143 = (bf16[128,4096]{1,0:T(8,128)(2,1)S(1)}, bf16[16,4096]{1,0:T(8,128)(2,1)S(1)}, bf16[128,128]{1,0:T(8,128)(2,1)S(1)}, bf16[128,128]{1,0:T(8,128)(2,1)S(1)}) custom-call(bf16[32,4096]{1,0:T(8,128)(2,1)S(1)} %shard_map.136.refs_0_, bf16[32,4096]{1,0:T(8,128)(2,1)S(1)} %collective-permute-done.refs_3_.refs_1_, ...), custom_call_target="tpu_custom_call" | custom-call | flops 536870912 | bytes 1048576 | tf_op jit(solution)/shard_map/pallas_call | solution.py:165
  38.7 1.6 %collective-permute-start.8 = (bf16[128,128]{1,0:T(8,128)(2,1)S(1)}, bf16[128,128]{1,0:T(8,128)(2,1)S(1)}, u32[]{:S(2)}, u32[]{:S(2)}) collective-permute-start(bf16[128,128]{1,0:T(8,128)(2,1)S(1)} %get-tuple-element.54), channel_id=1, source_target_pairs={{0,1},{1,0},{2,3},{3,2},{4,5},{5,4},{6,7},{7,6},{8,9},{9,8},{10,11... | collective-permute-start | bytes 98312 | tf_op jit(solution)/shard_map/ppermute | solution.py:34
  40.4 2.3 %collective-permute-done.8.refs_1_ = bf16[128,128]{1,0:T(8,128)(2,1)S(1)} collective-permute-done((bf16[128,128]{1,0:T(8,128)(2,1)S(1)}, bf16[128,128]{1,0:T(8,128)(2,1)S(1)}, u32[]{:S(2)}, u32[]{:S(2)}) %collective-permute-start.8) | collective-permute-done | bytes 32800 | tf_op jit(solution)/shard_map/ppermute | solution.py:34
  42.7 2.2 %collective-permute-start.9 = (bf16[64,128]{1,0:T(8,128)(2,1)S(1)}, bf16[64,128]{1,0:T(8,128)(2,1)S(1)}, u32[]{:S(2)}, u32[]{:S(2)}) collective-permute-start(bf16[64,128]{1,0:T(8,128)(2,1)S(1)} %get-tuple-element.56), channel_id=1, source_target_pairs={{0,2},{1,3},{2,4},{3,5},{4,6},{5,7},{6,0},{7,1},{8,10},{9,11},{10,... | collective-permute-start | bytes 49160 | tf_op jit(solution)/shard_map/ppermute | solution.py:34
  46.2 2.8 %collective-permute-start.11 = (bf16[64,128]{1,0:T(8,128)(2,1)S(1)}, bf16[64,128]{1,0:T(8,128)(2,1)S(1)}, u32[]{:S(2)}, u32[]{:S(2)}) collective-permute-start(bf16[64,128]{1,0:T(8,128)(2,1)S(1)} %get-tuple-element.58), channel_id=1, source_target_pairs={{0,6},{1,7},{2,0},{3,1},{4,2},{5,3},{6,4},{7,5},{8,14},{9,15},{10,... | collective-permute-start | bytes 49160 | tf_op jit(solution)/shard_map/ppermute | solution.py:34
  50.5 1.7 %shard_map.146 = (bf16[16,4096]{1,0:T(8,128)(2,1)S(1)}, bf16[16,4096]{1,0:T(8,128)(2,1)S(1)}, bf16[16,4096]{1,0:T(8,128)(2,1)S(1)}, bf16[16,4096]{1,0:T(8,128)(2...) custom-call(bf16[64,128]{1,0:T(8,128)(2,1)S(1)} %get-tuple-element.55.refs_0_, ...), custom_call_target="tpu_custom_call" | custom-call | flops 536870912 | bytes 1048576 | tf_op jit(solution)/shard_map/pallas_call | solution.py:165
  54.3 3.4 %shard_map.147 = (bf16[1024,4096]{1,0:T(8,128)(2,1)S(1)}, f32[8,128]{1,0:T(8,128)S(1)}) custom-call(bf16[16,4096]{1,0:T(8,128)(2,1)S(1)} %get-tuple-element.68.refs_0_, bf16[1024,4096]{1,0:T(8,128)(2,1)} %refs_1_.6), custom_call_target="tpu_custom_call" | custom-call | bytes 16777216 | tf_op jit(solution)/shard_map/pallas_call | solution.py:190
  59.9 3.5 %collective-permute-start.14 = (bf16[16,4096]{1,0:T(8,128)(2,1)S(1)}, bf16[16,4096]{1,0:T(8,128)(2,1)S(1)}, u32[]{:S(2)}, u32[]{:S(2)}) collective-permute-start(bf16[16,4096]{1,0:T(8,128)(2,1)S(1)} %get-tuple-element.87), channel_id=1, source_target_pairs={{0,2},{1,3},{2,4},{3,5},{4,6},{5,7},{6,0},{7,1},{8,10},{9,11},{10,... | collective-permute-start | bytes 393224 | tf_op jit(solution)/shard_map/ppermute | solution.py:34
  63.5 2.2 %collective-permute-start.16 = (bf16[16,4096]{1,0:T(8,128)(2,1)S(1)}, bf16[16,4096]{1,0:T(8,128)(2,1)S(1)}, u32[]{:S(2)}, u32[]{:S(2)}) collective-permute-start(bf16[16,4096]{1,0:T(8,128)(2,1)S(1)} %add_convert_fusion.3), channel_id=1, source_target_pairs={{0,6},{1,7},{2,0},{3,1},{4,2},{5,3},{6,4},{7,5},{8,14},{9,15},{10,... | collective-permute-start | bytes 393224 | tf_op jit(solution)/shard_map/ppermute | solution.py:34
  66.4 2.4 %collective-permute-done.14 = bf16[16,4096]{1,0:T(8,128)(2,1)S(1)} collective-permute-done((bf16[16,4096]{1,0:T(8,128)(2,1)S(1)}, bf16[16,4096]{1,0:T(8,128)(2,1)S(1)}, u32[]{:S(2)}, u32[]{:S(2)}) %collective-permute-start.14) | collective-permute-done | bytes 131104 | tf_op jit(solution)/shard_map/ppermute | solution.py:34
  70.2 4.3 %collective-permute-start.22 = (bf16[16,4096]{1,0:T(8,128)(2,1)S(1)}, bf16[16,4096]{1,0:T(8,128)(2,1)S(1)}, u32[]{:S(2)}, u32[]{:S(2)}) collective-permute-start(bf16[16,4096]{1,0:T(8,128)(2,1)S(1)} %multiply_convert_fusion.refs_0_), channel_id=1, source_target_pairs={{0,6},{1,7},{2,0},{3,1},{4,2},{5,3},{6,4},{7,5},{8,14},{9,15},{10,... | collective-permute-start | bytes 393224 | tf_op jit(solution)/shard_map/ppermute | solution.py:34
  75.8 1.9 %collective-permute-start.18 = (bf16[16,4096]{1,0:T(8,128)(2,1)S(1)}, bf16[16,4096]{1,0:T(8,128)(2,1)S(1)}, u32[]{:S(2)}, u32[]{:S(2)}) collective-permute-start(bf16[16,4096]{1,0:T(8,128)(2,1)S(1)} %multiply_convert_fusion.refs_0_), channel_id=1, source_target_pairs={{0,2},{1,3},{2,4},{3,5},{4,6},{5,7},{6,0},{7,1},{8,10},{9,11},{10,... | collective-permute-start | bytes 393224 | tf_op jit(solution)/shard_map/ppermute | solution.py:34
  78.0 1.7 %collective-permute-start.23 = (bf16[16,4096]{1,0:T(8,128)(2,1)S(1)}, bf16[16,4096]{1,0:T(8,128)(2,1)S(1)}, u32[]{:S(2)}, u32[]{:S(2)}) collective-permute-start(bf16[16,4096]{1,0:T(8,128)(2,1)S(1)} %collective-permute-done.22.refs_6_), channel_id=1, source_target_pairs={{0,1},{1,0},{2,3},{3,2},{4,5},{5,4},{6,7},{7,6},{8,9},{9,8},{10,11... | collective-permute-start | bytes 393224 | tf_op jit(solution)/shard_map/ppermute | solution.py:34
  79.8 3.4 %collective-permute-done.20.refs_4_ = bf16[16,4096]{1,0:T(8,128)(2,1)S(1)} collective-permute-done((bf16[16,4096]{1,0:T(8,128)(2,1)S(1)}, bf16[16,4096]{1,0:T(8,128)(2,1)S(1)}, u32[]{:S(2)}, u32[]{:S(2)}) %collective-permute-start.20) | collective-permute-done | bytes 131104 | tf_op jit(solution)/shard_map/ppermute | solution.py:34
  83.5 1.7 %collective-permute-start.19 = (bf16[16,4096]{1,0:T(8,128)(2,1)S(1)}, bf16[16,4096]{1,0:T(8,128)(2,1)S(1)}, u32[]{:S(2)}, u32[]{:S(2)}) collective-permute-start(bf16[16,4096]{1,0:T(8,128)(2,1)S(1)} %collective-permute-done.18.refs_2_), channel_id=1, source_target_pairs={{0,1},{1,0},{2,3},{3,2},{4,5},{5,4},{6,7},{7,6},{8,9},{9,8},{10,11... | collective-permute-start | bytes 393224 | tf_op jit(solution)/shard_map/ppermute | solution.py:34
  85.2 4.0 %shard_map.149 = (bf16[4096,1024]{1,0:T(8,128)(2,1)S(1)}, f32[8,128]{1,0:T(8,128)}) custom-call(bf16[16,4096]{1,0:T(8,128)(2,1)S(1)} %multiply_convert_fusion.refs_0_, bf16[4096,1024]{1,0:T(8,128)(2,1)} %refs_1_.7), custom_call_target="tpu_custom_call" | custom-call | bytes 16777216 | tf_op jit(solution)/shard_map/pallas_call | solution.py:190
  89.5 2.8 %collective-permute-done.19.refs_3_ = bf16[16,4096]{1,0:T(8,128)(2,1)S(1)} collective-permute-done((bf16[16,4096]{1,0:T(8,128)(2,1)S(1)}, bf16[16,4096]{1,0:T(8,128)(2,1)S(1)}, u32[]{:S(2)}, u32[]{:S(2)}) %collective-permute-start.19) | collective-permute-done | bytes 131104 | tf_op jit(solution)/shard_map/ppermute | solution.py:34
  92.3 3.6 %shard_map.150 = (bf16[16,4096]{1,0:T(8,128)(2,1)S(1)}, bf16[16,4096]{1,0:T(8,128)(2,1)S(1)}, bf16[16,4096]{1,0:T(8,128)(2,1)S(1)}, bf16[16,4096]{1,0:T(8,128)(2...) custom-call(bf16[16,4096]{1,0:T(8,128)(2,1)S(1)} %multiply_convert_fusion.refs_0_, ...), custom_call_target="tpu_custom_call" | custom-call | flops 3221225472 | bytes 1048576 | tf_op jit(solution)/shard_map/pallas_call | solution.py:165
  96.2 1.8 %collective-permute-start.27 = (bf16[32,4096]{1,0:T(8,128)(2,1)S(1)}, bf16[32,4096]{1,0:T(8,128)(2,1)S(1)}, u32[]{:S(2)}, u32[]{:S(2)}) collective-permute-start(bf16[32,4096]{1,0:T(8,128)(2,1)S(1)} %get-tuple-element.77), channel_id=1, source_target_pairs={{0,1},{1,0},{2,3},{3,2},{4,5},{5,4},{6,7},{7,6},{8,9},{9,8},{10,11... | collective-permute-start | bytes 786440 | tf_op jit(solution)/shard_map/ppermute | solution.py:34
  98.0 4.3 %collective-permute-done.24 = bf16[32,4096]{1,0:T(8,128)(2,1)S(1)} collective-permute-done((bf16[32,4096]{1,0:T(8,128)(2,1)S(1)}, bf16[32,4096]{1,0:T(8,128)(2,1)S(1)}, u32[]{:S(2)}, u32[]{:S(2)}) %collective-permute-start.24) | collective-permute-done | bytes 262176 | tf_op jit(solution)/shard_map/ppermute | solution.py:34
  106.5 3.4 %collective-permute-done.25 = bf16[16,4096]{1,0:T(8,128)(2,1)S(1)} collective-permute-done((bf16[16,4096]{1,0:T(8,128)(2,1)S(1)}, bf16[16,4096]{1,0:T(8,128)(2,1)S(1)}, u32[]{:S(2)}, u32[]{:S(2)}) %collective-permute-start.25) | collective-permute-done | bytes 131104 | tf_op jit(solution)/shard_map/ppermute | solution.py:34
  (66 shorter events, 25.2 us)
Async XLA Ops:
  0.0 20.9 %copy-start.2 = (s32[128]{0:T(128)S(1)}, s32[128]{0:T(128)}, u32[]{:S(2)}) copy-start(s32[128]{0:T(128)} %param.15) | copy-start | bytes 1540
  1.6 12.8 %collective-permute-start.1 = (bf16[32,4096]{1,0:T(8,128)(2,1)S(1)}, bf16[32,4096]{1,0:T(8,128)(2,1)S(1)}, u32[]{:S(2)}, u32[]{:S(2)}) collective-permute-start(bf16[32,4096]{1,0:T(8,128)(2,1)S(1)} %shard_map.136.refs_0_), channel_id=1, source_target_pairs={{0,2},{1,3},{2,4},{3,5},{4,6},{5,7},{6,0},{7,1},{8,10},{9,11},{10,... | collective-permute-start | bytes 786440 | tf_op jit(solution)/shard_map/ppermute | solution.py:34
  4.6 13.4 %collective-permute-start.4 = (bf16[32,4096]{1,0:T(8,128)(2,1)S(1)}, bf16[32,4096]{1,0:T(8,128)(2,1)S(1)}, u32[]{:S(2)}, u32[]{:S(2)}) collective-permute-start(bf16[32,4096]{1,0:T(8,128)(2,1)S(1)} %shard_map.136.refs_0_), channel_id=1, source_target_pairs={{0,6},{1,7},{2,0},{3,1},{4,2},{5,3},{6,4},{7,5},{8,14},{9,15},{10,... | collective-permute-start | bytes 786440 | tf_op jit(solution)/shard_map/ppermute | solution.py:34
  6.7 11.3 %collective-permute-start = (bf16[32,4096]{1,0:T(8,128)(2,1)S(1)}, bf16[32,4096]{1,0:T(8,128)(2,1)S(1)}, u32[]{:S(2)}, u32[]{:S(2)}) collective-permute-start(bf16[32,4096]{1,0:T(8,128)(2,1)S(1)} %shard_map.136.refs_0_), channel_id=1, source_target_pairs={{0,1},{1,0},{2,3},{3,2},{4,5},{5,4},{6,7},{7,6},{8,9},{9,8},{10,11... | collective-permute-start | bytes 786440 | tf_op jit(solution)/shard_map/ppermute | solution.py:34
  14.4 7.1 %collective-permute-start.3 = (bf16[32,4096]{1,0:T(8,128)(2,1)S(1)}, bf16[32,4096]{1,0:T(8,128)(2,1)S(1)}, u32[]{:S(2)}, u32[]{:S(2)}) collective-permute-start(bf16[32,4096]{1,0:T(8,128)(2,1)S(1)} %collective-permute-done.1.refs_2_), channel_id=1, source_target_pairs={{2,4},{3,5},{4,6},{5,7},{10,12},{11,13},{12,14},{13,15},{18,20},{1... | collective-permute-start | bytes 786440 | tf_op jit(solution)/shard_map/ppermute | solution.py:34
  18.0 9.3 %collective-permute-start.6 = (bf16[32,4096]{1,0:T(8,128)(2,1)S(1)}, bf16[32,4096]{1,0:T(8,128)(2,1)S(1)}, u32[]{:S(2)}, u32[]{:S(2)}) collective-permute-start(bf16[32,4096]{1,0:T(8,128)(2,1)S(1)} %shard_map.139.refs_6_), channel_id=1, source_target_pairs={{0,1},{1,0},{2,3},{3,2},{4,5},{5,4},{6,7},{7,6},{8,9},{9,8},{10,11... | collective-permute-start | bytes 786440 | tf_op jit(solution)/shard_map/ppermute | solution.py:34
  19.6 10.0 %collective-permute-start.5 = (bf16[32,4096]{1,0:T(8,128)(2,1)S(1)}, bf16[32,4096]{1,0:T(8,128)(2,1)S(1)}, u32[]{:S(2)}, u32[]{:S(2)}) collective-permute-start(bf16[32,4096]{1,0:T(8,128)(2,1)S(1)} %shard_map.139.refs_6_), channel_id=1, source_target_pairs={{2,0},{3,1},{4,2},{5,3},{10,8},{11,9},{12,10},{13,11},{18,16},{19,... | collective-permute-start | bytes 786440 | tf_op jit(solution)/shard_map/ppermute | solution.py:34
  21.0 15.4 %collective-permute-start.2 = (bf16[32,4096]{1,0:T(8,128)(2,1)S(1)}, bf16[32,4096]{1,0:T(8,128)(2,1)S(1)}, u32[]{:S(2)}, u32[]{:S(2)}) collective-permute-start(bf16[32,4096]{1,0:T(8,128)(2,1)S(1)} %collective-permute-done.1.refs_2_), channel_id=1, source_target_pairs={{0,1},{1,0},{2,3},{3,2},{4,5},{5,4},{6,7},{7,6},{8,9},{9,8},{10,11... | collective-permute-start | bytes 786440 | tf_op jit(solution)/shard_map/ppermute | solution.py:34
  29.7 7.3 %collective-permute-start.7 = (bf16[32,4096]{1,0:T(8,128)(2,1)S(1)}, bf16[32,4096]{1,0:T(8,128)(2,1)S(1)}, u32[]{:S(2)}, u32[]{:S(2)}) collective-permute-start(bf16[32,4096]{1,0:T(8,128)(2,1)S(1)} %shard_map.140.refs_0_.refs_4_), channel_id=1, source_target_pairs={{0,1},{1,0},{2,3},{3,2},{4,5},{5,4},{6,7},{7,6},{8,9},{9,8},{10,11... | collective-permute-start | bytes 786440 | tf_op jit(solution)/shard_map/ppermute | solution.py:34
  38.7 4.0 %collective-permute-start.8 = (bf16[128,128]{1,0:T(8,128)(2,1)S(1)}, bf16[128,128]{1,0:T(8,128)(2,1)S(1)}, u32[]{:S(2)}, u32[]{:S(2)}) collective-permute-start(bf16[128,128]{1,0:T(8,128)(2,1)S(1)} %get-tuple-element.54), channel_id=1, source_target_pairs={{0,1},{1,0},{2,3},{3,2},{4,5},{5,4},{6,7},{7,6},{8,9},{9,8},{10,11... | collective-permute-start | bytes 98312 | tf_op jit(solution)/shard_map/ppermute | solution.py:34
  42.7 7.2 %collective-permute-start.9 = (bf16[64,128]{1,0:T(8,128)(2,1)S(1)}, bf16[64,128]{1,0:T(8,128)(2,1)S(1)}, u32[]{:S(2)}, u32[]{:S(2)}) collective-permute-start(bf16[64,128]{1,0:T(8,128)(2,1)S(1)} %get-tuple-element.56), channel_id=1, source_target_pairs={{0,2},{1,3},{2,4},{3,5},{4,6},{5,7},{6,0},{7,1},{8,10},{9,11},{10,... | collective-permute-start | bytes 49160 | tf_op jit(solution)/shard_map/ppermute | solution.py:34
  45.0 5.0 %collective-permute-start.10 = (bf16[64,128]{1,0:T(8,128)(2,1)S(1)}, bf16[64,128]{1,0:T(8,128)(2,1)S(1)}, u32[]{:S(2)}, u32[]{:S(2)}) collective-permute-start(bf16[64,128]{1,0:T(8,128)(2,1)S(1)} %get-tuple-element.57), channel_id=1, source_target_pairs={{0,4},{1,5},{2,6},{3,7},{4,0},{5,1},{6,2},{7,3},{8,12},{9,13},{10,... | collective-permute-start | bytes 49160 | tf_op jit(solution)/shard_map/ppermute | solution.py:34
  46.2 4.3 %collective-permute-start.11 = (bf16[64,128]{1,0:T(8,128)(2,1)S(1)}, bf16[64,128]{1,0:T(8,128)(2,1)S(1)}, u32[]{:S(2)}, u32[]{:S(2)}) collective-permute-start(bf16[64,128]{1,0:T(8,128)(2,1)S(1)} %get-tuple-element.58), channel_id=1, source_target_pairs={{0,6},{1,7},{2,0},{3,1},{4,2},{5,3},{6,4},{7,5},{8,14},{9,15},{10,... | collective-permute-start | bytes 49160 | tf_op jit(solution)/shard_map/ppermute | solution.py:34
  49.9 19.9 %copy-start.4 = (f32[4096]{0:T(1024)S(1)}, f32[4096]{0:T(1024)}, u32[]{:S(2)}) copy-start(f32[4096]{0:T(1024)} %param.26) | copy-start | bytes 49156
  49.9 20.1 %copy-start.5 = (f32[4096]{0:T(1024)S(1)}, f32[4096]{0:T(1024)}, u32[]{:S(2)}) copy-start(f32[4096]{0:T(1024)} %param.22) | copy-start | bytes 49156
  52.2 6.4 %collective-permute-start.12 = (bf16[32,4096]{1,0:T(8,128)(2,1)S(1)}, bf16[32,4096]{1,0:T(8,128)(2,1)S(1)}, u32[]{:S(2)}, u32[]{:S(2)}) collective-permute-start(bf16[32,4096]{1,0:T(8,128)(2,1)S(1)} %get-tuple-element.64), channel_id=1, source_target_pairs={{0,1},{1,0},{2,3},{3,2},{4,5},{5,4},{6,7},{7,6},{8,9},{9,8},{10,11... | collective-permute-start | bytes 786440 | tf_op jit(solution)/shard_map/ppermute | solution.py:34
  52.8 10.7 %collective-permute-start.15 = (bf16[32,4096]{1,0:T(8,128)(2,1)S(1)}, bf16[32,4096]{1,0:T(8,128)(2,1)S(1)}, u32[]{:S(2)}, u32[]{:S(2)}) collective-permute-start(bf16[32,4096]{1,0:T(8,128)(2,1)S(1)} %get-tuple-element.67), channel_id=1, source_target_pairs={{0,1},{1,0},{2,3},{3,2},{4,5},{5,4},{6,7},{7,6},{8,9},{9,8},{10,11... | collective-permute-start | bytes 786440 | tf_op jit(solution)/shard_map/ppermute | solution.py:34
  58.7 7.7 %collective-permute-start.13 = (bf16[16,4096]{1,0:T(8,128)(2,1)S(1)}, bf16[16,4096]{1,0:T(8,128)(2,1)S(1)}, u32[]{:S(2)}, u32[]{:S(2)}) collective-permute-start(bf16[16,4096]{1,0:T(8,128)(2,1)S(1)} %get-tuple-element.86), channel_id=1, source_target_pairs={{0,4},{1,5},{2,6},{3,7},{4,0},{5,1},{6,2},{7,3},{8,12},{9,13},{10,... | collective-permute-start | bytes 393224 | tf_op jit(solution)/shard_map/ppermute | solution.py:34
  59.9 9.0 %collective-permute-start.14 = (bf16[16,4096]{1,0:T(8,128)(2,1)S(1)}, bf16[16,4096]{1,0:T(8,128)(2,1)S(1)}, u32[]{:S(2)}, u32[]{:S(2)}) collective-permute-start(bf16[16,4096]{1,0:T(8,128)(2,1)S(1)} %get-tuple-element.87), channel_id=1, source_target_pairs={{0,2},{1,3},{2,4},{3,5},{4,6},{5,7},{6,0},{7,1},{8,10},{9,11},{10,... | collective-permute-start | bytes 393224 | tf_op jit(solution)/shard_map/ppermute | solution.py:34
  63.5 6.3 %collective-permute-start.16 = (bf16[16,4096]{1,0:T(8,128)(2,1)S(1)}, bf16[16,4096]{1,0:T(8,128)(2,1)S(1)}, u32[]{:S(2)}, u32[]{:S(2)}) collective-permute-start(bf16[16,4096]{1,0:T(8,128)(2,1)S(1)} %add_convert_fusion.3), channel_id=1, source_target_pairs={{0,6},{1,7},{2,0},{3,1},{4,2},{5,3},{6,4},{7,5},{8,14},{9,15},{10,... | collective-permute-start | bytes 393224 | tf_op jit(solution)/shard_map/ppermute | solution.py:34
  70.2 7.9 %collective-permute-start.22 = (bf16[16,4096]{1,0:T(8,128)(2,1)S(1)}, bf16[16,4096]{1,0:T(8,128)(2,1)S(1)}, u32[]{:S(2)}, u32[]{:S(2)}) collective-permute-start(bf16[16,4096]{1,0:T(8,128)(2,1)S(1)} %multiply_convert_fusion.refs_0_), channel_id=1, source_target_pairs={{0,6},{1,7},{2,0},{3,1},{4,2},{5,3},{6,4},{7,5},{8,14},{9,15},{10,... | collective-permute-start | bytes 393224 | tf_op jit(solution)/shard_map/ppermute | solution.py:34
  74.5 8.7 %collective-permute-start.20 = (bf16[16,4096]{1,0:T(8,128)(2,1)S(1)}, bf16[16,4096]{1,0:T(8,128)(2,1)S(1)}, u32[]{:S(2)}, u32[]{:S(2)}) collective-permute-start(bf16[16,4096]{1,0:T(8,128)(2,1)S(1)} %multiply_convert_fusion.refs_0_), channel_id=1, source_target_pairs={{0,4},{1,5},{2,6},{3,7},{4,0},{5,1},{6,2},{7,3},{8,12},{9,13},{10,... | collective-permute-start | bytes 393224 | tf_op jit(solution)/shard_map/ppermute | solution.py:34
  75.8 7.7 %collective-permute-start.18 = (bf16[16,4096]{1,0:T(8,128)(2,1)S(1)}, bf16[16,4096]{1,0:T(8,128)(2,1)S(1)}, u32[]{:S(2)}, u32[]{:S(2)}) collective-permute-start(bf16[16,4096]{1,0:T(8,128)(2,1)S(1)} %multiply_convert_fusion.refs_0_), channel_id=1, source_target_pairs={{0,2},{1,3},{2,4},{3,5},{4,6},{5,7},{6,0},{7,1},{8,10},{9,11},{10,... | collective-permute-start | bytes 393224 | tf_op jit(solution)/shard_map/ppermute | solution.py:34
  77.7 11.5 %collective-permute-start.17 = (bf16[16,4096]{1,0:T(8,128)(2,1)S(1)}, bf16[16,4096]{1,0:T(8,128)(2,1)S(1)}, u32[]{:S(2)}, u32[]{:S(2)}) collective-permute-start(bf16[16,4096]{1,0:T(8,128)(2,1)S(1)} %multiply_convert_fusion.refs_0_), channel_id=1, source_target_pairs={{0,1},{1,0},{2,3},{3,2},{4,5},{5,4},{6,7},{7,6},{8,9},{9,8},{10,11... | collective-permute-start | bytes 393224 | tf_op jit(solution)/shard_map/ppermute | solution.py:34
  78.0 11.2 %collective-permute-start.23 = (bf16[16,4096]{1,0:T(8,128)(2,1)S(1)}, bf16[16,4096]{1,0:T(8,128)(2,1)S(1)}, u32[]{:S(2)}, u32[]{:S(2)}) collective-permute-start(bf16[16,4096]{1,0:T(8,128)(2,1)S(1)} %collective-permute-done.22.refs_6_), channel_id=1, source_target_pairs={{0,1},{1,0},{2,3},{3,2},{4,5},{5,4},{6,7},{7,6},{8,9},{9,8},{10,11... | collective-permute-start | bytes 393224 | tf_op jit(solution)/shard_map/ppermute | solution.py:34
  83.2 6.3 %collective-permute-start.21 = (bf16[16,4096]{1,0:T(8,128)(2,1)S(1)}, bf16[16,4096]{1,0:T(8,128)(2,1)S(1)}, u32[]{:S(2)}, u32[]{:S(2)}) collective-permute-start(bf16[16,4096]{1,0:T(8,128)(2,1)S(1)} %collective-permute-done.20.refs_4_), channel_id=1, source_target_pairs={{0,1},{1,0},{2,3},{3,2},{4,5},{5,4},{6,7},{7,6},{8,9},{9,8},{10,11... | collective-permute-start | bytes 393224 | tf_op jit(solution)/shard_map/ppermute | solution.py:34
  83.5 8.8 %collective-permute-start.19 = (bf16[16,4096]{1,0:T(8,128)(2,1)S(1)}, bf16[16,4096]{1,0:T(8,128)(2,1)S(1)}, u32[]{:S(2)}, u32[]{:S(2)}) collective-permute-start(bf16[16,4096]{1,0:T(8,128)(2,1)S(1)} %collective-permute-done.18.refs_2_), channel_id=1, source_target_pairs={{0,1},{1,0},{2,3},{3,2},{4,5},{5,4},{6,7},{7,6},{8,9},{9,8},{10,11... | collective-permute-start | bytes 393224 | tf_op jit(solution)/shard_map/ppermute | solution.py:34
  95.9 6.4 %collective-permute-start.24 = (bf16[32,4096]{1,0:T(8,128)(2,1)S(1)}, bf16[32,4096]{1,0:T(8,128)(2,1)S(1)}, u32[]{:S(2)}, u32[]{:S(2)}) collective-permute-start(bf16[32,4096]{1,0:T(8,128)(2,1)S(1)} %get-tuple-element.74), channel_id=1, source_target_pairs={{0,1},{1,0},{2,3},{3,2},{4,5},{5,4},{6,7},{7,6},{8,9},{9,8},{10,11... | collective-permute-start | bytes 786440 | tf_op jit(solution)/shard_map/ppermute | solution.py:34
  96.2 8.9 %collective-permute-start.27 = (bf16[32,4096]{1,0:T(8,128)(2,1)S(1)}, bf16[32,4096]{1,0:T(8,128)(2,1)S(1)}, u32[]{:S(2)}, u32[]{:S(2)}) collective-permute-start(bf16[32,4096]{1,0:T(8,128)(2,1)S(1)} %get-tuple-element.77), channel_id=1, source_target_pairs={{0,1},{1,0},{2,3},{3,2},{4,5},{5,4},{6,7},{7,6},{8,9},{9,8},{10,11... | collective-permute-start | bytes 786440 | tf_op jit(solution)/shard_map/ppermute | solution.py:34
  102.4 7.4 %collective-permute-start.25 = (bf16[16,4096]{1,0:T(8,128)(2,1)S(1)}, bf16[16,4096]{1,0:T(8,128)(2,1)S(1)}, u32[]{:S(2)}, u32[]{:S(2)}) collective-permute-start(bf16[16,4096]{1,0:T(8,128)(2,1)S(1)} %get-tuple-element.84), channel_id=1, source_target_pairs={{0,4},{1,5},{2,6},{3,7},{4,0},{5,1},{6,2},{7,3},{8,12},{9,13},{10,... | collective-permute-start | bytes 393224 | tf_op jit(solution)/shard_map/ppermute | solution.py:34
  102.5 7.4 %collective-permute-start.26 = (bf16[16,4096]{1,0:T(8,128)(2,1)S(1)}, bf16[16,4096]{1,0:T(8,128)(2,1)S(1)}, u32[]{:S(2)}, u32[]{:S(2)}) collective-permute-start(bf16[16,4096]{1,0:T(8,128)(2,1)S(1)} %get-tuple-element.85), channel_id=1, source_target_pairs={{0,2},{1,3},{2,4},{3,5},{4,6},{5,7},{6,0},{7,1},{8,10},{9,11},{10,... | collective-permute-start | bytes 393224 | tf_op jit(solution)/shard_map/ppermute | solution.py:34
  105.2 6.0 %collective-permute-start.28 = (bf16[16,4096]{1,0:T(8,128)(2,1)S(1)}, bf16[16,4096]{1,0:T(8,128)(2,1)S(1)}, u32[]{:S(2)}, u32[]{:S(2)}) collective-permute-start(bf16[16,4096]{1,0:T(8,128)(2,1)S(1)} %add_convert_fusion), channel_id=1, source_target_pairs={{0,6},{1,7},{2,0},{3,1},{4,2},{5,3},{6,4},{7,5},{8,14},{9,15},{10,... | collective-permute-start | bytes 393224 | tf_op jit(solution)/shard_map/ppermute | solution.py:34
  (3 other events, 2.2 us)

commit v11 on v10

--- a/solution.py
+++ b/solution.py
@@ -54,16 +54,20 @@
     blocks = {(0, 0): block}
     for dy in range(1, wide):
         blocks[0, dy] = shift(block, tall, wide, 0, dy)
-    first = [*tokens, *(blocks[0, dy] for dy in range(1, wide))]
-    for dz in range(tall - 1, 0, -1):
+    early = [blocks[0, dy] for dy in range(1, wide)]
+    last = tall - 1
+    blocks[last, 0] = tie([shift(block, tall, wide, last, 0)], early)
+    for dy in range(1, wide):
+        blocks[last, dy] = shift(blocks[last, 0], tall, wide, 0, dy)
+    block = tie([block], [blocks[last, 0]])
+    for dz in range(1, last):
         if tall != 4 or dz != 2:
             blocks[dz, 0] = shift(block, tall, wide, dz, 0)
-    blocks[tall - 1, 0] = tie([blocks[tall - 1, 0]], first)
+    blocks[1, 0] = tie([blocks[1, 0]], tokens)
     if tall == 4:
-        for dy in range(1, wide):
-            blocks[3, dy] = shift(blocks[3, 0], tall, wide, 0, dy)
         up = shift(blocks[1, 0], tall, wide, 1, 0, lambda z: z in (1, 2))
-        down = shift(blocks[3, 0], tall, wide, -1, 0, lambda z: z in (1, 2))
+        held = tie([blocks[3, 0]], [blocks[1, 0]])
+        down = shift(held, tall, wide, -1, 0, lambda z: z in (1, 2))
         blocks[2, 0] = tie([up, down], [blocks[3, dy] for dy in range(1, wide)])
     for dz in range(1, tall):
         for dy in range(1, wide):

time: 112 us -> 115 us (1.027)
  waiting for transfers between devices: 36.4 us -> 38.3 us
    ppermute x29, waiting for transfers between devices: 36.4 us -> 38.3 us  [shift(): return lax.ppermute(block, 'ctx', pairs)]
    pallas_call x10 -> x13, Pallas kernels: 10.3 us -> 10.4 us  [kernel_call(): pl.pallas_call(body, out_shape=[jax.ShapeDtypeStruct(s, d) for s, d in ou...]
  transfers between devices with their start and end apart: 29 -> 29, of which waited for: 17 -> 18; matrix products, arithmetic and copies ran while one was open for 1% -> 1% of each run, Pallas kernels for 16% -> 15%
where the time goes in v11:
time: 115 us
  starting transfers between devices  45.6 us (40%)
  waiting for transfers between devices  38.3 us (33%)
  Pallas kernels  26.3 us (23%)
  local copies, waits for them, and re-layouts  2.23 us (2%)
  other arithmetic  1.89 us (2%)
    ppermute x29, starting transfers between devices, shift(): return lax.ppermute(block, 'ctx', pairs)  45.6 us
    ppermute x29, waiting for transfers between devices, shift(): return lax.ppermute(block, 'ctx', pairs)  38.3 us
    pallas_call x5, Pallas kernels, load(): pl.pallas_call(functools.partial(load_body, len(arrays)), out_shape=[pltp...  15.9 us
    pallas_call x13, Pallas kernels, kernel_call(): pl.pallas_call(body, out_shape=[jax.ShapeDtypeStruct(s, d) for s, d in ou...  10.4 us
  transfers between devices with their start and end apart: 29, of which 18 were waited for; matrix products, arithmetic and copies ran while one was open for 1% of the time, Pallas kernels for 15%

profile of v11, /device:TPU:0, one launch (start us, length us, event | category | flops | bytes accessed | tf_op | source)
XLA Modules:
  0.0 114.6 jit_solution(17884108380466096019)
XLA Ops:
  1.6 5.1 %collective-permute-start.1 = (bf16[32,4096]{1,0:T(8,128)(2,1)S(1)}, bf16[32,4096]{1,0:T(8,128)(2,1)S(1)}, u32[]{:S(2)}, u32[]{:S(2)}) collective-permute-start(bf16[32,4096]{1,0:T(8,128)(2,1)S(1)} %shard_map.136.refs_0_), channel_id=1, source_target_pairs={{0,6},{1,7},{2,0},{3,1},{4,2},{5,3},{6,4},{7,5},{8,14},{9,15},{10,... | collective-permute-start | bytes 786440 | tf_op jit(solution)/shard_map/ppermute | solution.py:34
  8.2 4.0 %collective-permute-done.1.refs_0_ = bf16[32,4096]{1,0:T(8,128)(2,1)S(1)} collective-permute-done((bf16[32,4096]{1,0:T(8,128)(2,1)S(1)}, bf16[32,4096]{1,0:T(8,128)(2,1)S(1)}, u32[]{:S(2)}, u32[]{:S(2)}) %collective-permute-start.1) | collective-permute-done | bytes 262176 | tf_op jit(solution)/shard_map/ppermute | solution.py:34
  12.2 2.2 %collective-permute-done.refs_1_ = bf16[32,4096]{1,0:T(8,128)(2,1)S(1)} collective-permute-done((bf16[32,4096]{1,0:T(8,128)(2,1)S(1)}, bf16[32,4096]{1,0:T(8,128)(2,1)S(1)}, u32[]{:S(2)}, u32[]{:S(2)}) %collective-permute-start) | collective-permute-done | bytes 262176 | tf_op jit(solution)/shard_map/ppermute | solution.py:34
  17.6 2.9 %shard_map.139 = (f32[1,4096]{1,0:T(1,128)S(1)}, bf16[4096,128]{1,0:T(8,128)(2,1)S(1)}, bf16[4096,128]{1,0:T(8,128)(2,1)S(1)}, bf16[4096,512]{1,0:T(8,128)(2,1)S(1)}, f32[8,128]{1,0:T(8,128)S(1)}) custom-call(bf16[32,4096]{1,0:T(8,128)(2,1)S(1)} %shard_map.136.refs_0_, f32[1,4096]{1,0:T(1,128)} %bitcast.8, bf16[4096,128]{1,0:T(8,128)(2,1)} %refs_2_.1, ...), custom_call_target="tpu_custom_call" | custom-call | bytes 12615680 | tf_op jit(solution)/shard_map/pallas_call | solution.py:194
  20.5 1.6 %collective-permute-start.6 = (bf16[32,4096]{1,0:T(8,128)(2,1)S(1)}, bf16[32,4096]{1,0:T(8,128)(2,1)S(1)}, u32[]{:S(2)}, u32[]{:S(2)}) collective-permute-start(bf16[32,4096]{1,0:T(8,128)(2,1)S(1)} %shard_map.137.refs_1_.refs_0_.refs_6_), channel_id=1, source_target_pairs={{0,1},{1,0},{2,3},{3,2},{4,5},{5,4},{6,7},{7,6},{8,9},{9,8},{10,11... | collective-permute-start | bytes 786440 | tf_op jit(solution)/shard_map/ppermute | solution.py:34
  25.3 1.6 %collective-permute-start.3 = (bf16[32,4096]{1,0:T(8,128)(2,1)S(1)}, bf16[32,4096]{1,0:T(8,128)(2,1)S(1)}, u32[]{:S(2)}, u32[]{:S(2)}) collective-permute-start(bf16[32,4096]{1,0:T(8,128)(2,1)S(1)} %shard_map.141.refs_1_.refs_2_), channel_id=1, source_target_pairs={{0,1},{1,0},{2,3},{3,2},{4,5},{5,4},{6,7},{7,6},{8,9},{9,8},{10,11... | collective-permute-start | bytes 786440 | tf_op jit(solution)/shard_map/ppermute | solution.py:34
  26.8 2.4 %collective-permute-done.6.refs_2_.refs_7_ = bf16[32,4096]{1,0:T(8,128)(2,1)S(1)} collective-permute-done((bf16[32,4096]{1,0:T(8,128)(2,1)S(1)}, bf16[32,4096]{1,0:T(8,128)(2,1)S(1)}, u32[]{:S(2)}, u32[]{:S(2)}) %collective-permute-start.6) | collective-permute-done | bytes 262176 | tf_op jit(solution)/shard_map/ppermute | solution.py:34
  29.2 2.3 %collective-permute-done.5.refs_1_ = bf16[32,4096]{1,0:T(8,128)(2,1)S(1)} collective-permute-done((bf16[32,4096]{1,0:T(8,128)(2,1)S(1)}, bf16[32,4096]{1,0:T(8,128)(2,1)S(1)}, u32[]{:S(2)}, u32[]{:S(2)}) %collective-permute-start.5) | collective-permute-done | bytes 262176 | tf_op jit(solution)/shard_map/ppermute | solution.py:34
  31.5 1.6 %collective-permute-start.7 = (bf16[32,4096]{1,0:T(8,128)(2,1)S(1)}, bf16[32,4096]{1,0:T(8,128)(2,1)S(1)}, u32[]{:S(2)}, u32[]{:S(2)}) collective-permute-start(bf16[32,4096]{1,0:T(8,128)(2,1)S(1)} %shard_map.143.refs_0_.refs_4_), channel_id=1, source_target_pairs={{0,1},{1,0},{2,3},{3,2},{4,5},{5,4},{6,7},{7,6},{8,9},{9,8},{10,11... | collective-permute-start | bytes 786440 | tf_op jit(solution)/shard_map/ppermute | solution.py:34
  33.6 2.2 %shard_map.144 = (bf16[512,4096]{1,0:T(8,128)(2,1)S(1)}, f32[8,128]{1,0:T(8,128)S(1)}) custom-call(bf16[32,4096]{1,0:T(8,128)(2,1)S(1)} %shard_map.143.refs_0_.refs_4_, bf16[512,4096]{1,0:T(8,128)(2,1)} %refs_1_.4), custom_call_target="tpu_custom_call" | custom-call | bytes 8388608 | tf_op jit(solution)/shard_map/pallas_call | solution.py:194
  35.8 3.4 %shard_map.145 = (bf16[4096,1024]{1,0:T(8,128)(2,1)S(1)}, f32[8,128]{1,0:T(8,128)S(1)}) custom-call(bf16[32,4096]{1,0:T(8,128)(2,1)S(1)} %shard_map.143.refs_0_.refs_4_, bf16[4096,1024]{1,0:T(8,128)(2,1)} %refs_1_.5), custom_call_target="tpu_custom_call" | custom-call | bytes 16777216 | tf_op jit(solution)/shard_map/pallas_call | solution.py:194
  39.2 1.8 %shard_map.146 = (bf16[128,4096]{1,0:T(8,128)(2,1)S(1)}, bf16[16,4096]{1,0:T(8,128)(2,1)S(1)}, bf16[128,128]{1,0:T(8,128)(2,1)S(1)}, bf16[128,128]{1,0:T(8,128)(2,1)S(1)}) custom-call(bf16[32,4096]{1,0:T(8,128)(2,1)S(1)} %shard_map.136.refs_0_, bf16[32,4096]{1,0:T(8,128)(2,1)S(1)} %collective-permute-done.refs_1_, ...), custom_call_target="tpu_custom_call" | custom-call | flops 536870912 | bytes 1048576 | tf_op jit(solution)/shard_map/pallas_call | solution.py:169
  42.2 2.8 %collective-permute-done.8.refs_1_ = bf16[128,128]{1,0:T(8,128)(2,1)S(1)} collective-permute-done((bf16[128,128]{1,0:T(8,128)(2,1)S(1)}, bf16[128,128]{1,0:T(8,128)(2,1)S(1)}, u32[]{:S(2)}, u32[]{:S(2)}) %collective-permute-start.8) | collective-permute-done | bytes 32800 | tf_op jit(solution)/shard_map/ppermute | solution.py:34
  46.5 2.1 %collective-permute-start.10 = (bf16[64,128]{1,0:T(8,128)(2,1)S(1)}, bf16[64,128]{1,0:T(8,128)(2,1)S(1)}, u32[]{:S(2)}, u32[]{:S(2)}) collective-permute-start(bf16[64,128]{1,0:T(8,128)(2,1)S(1)} %get-tuple-element.57), channel_id=1, source_target_pairs={{0,4},{1,5},{2,6},{3,7},{4,0},{5,1},{6,2},{7,3},{8,12},{9,13},{10,... | collective-permute-start | bytes 49160 | tf_op jit(solution)/shard_map/ppermute | solution.py:34
  48.6 2.1 %collective-permute-start.11 = (bf16[64,128]{1,0:T(8,128)(2,1)S(1)}, bf16[64,128]{1,0:T(8,128)(2,1)S(1)}, u32[]{:S(2)}, u32[]{:S(2)}) collective-permute-start(bf16[64,128]{1,0:T(8,128)(2,1)S(1)} %get-tuple-element.58), channel_id=1, source_target_pairs={{0,6},{1,7},{2,0},{3,1},{4,2},{5,3},{6,4},{7,5},{8,14},{9,15},{10,... | collective-permute-start | bytes 49160 | tf_op jit(solution)/shard_map/ppermute | solution.py:34
  52.4 1.7 %shard_map.149 = (bf16[16,4096]{1,0:T(8,128)(2,1)S(1)}, bf16[16,4096]{1,0:T(8,128)(2,1)S(1)}, bf16[16,4096]{1,0:T(8,128)(2,1)S(1)}, bf16[16,4096]{1,0:T(8,128)(2...) custom-call(bf16[64,128]{1,0:T(8,128)(2,1)S(1)} %get-tuple-element.55.refs_0_, ...), custom_call_target="tpu_custom_call" | custom-call | flops 536870912 | bytes 1048576 | tf_op jit(solution)/shard_map/pallas_call | solution.py:169
  54.0 1.6 %collective-permute-start.12 = (bf16[32,4096]{1,0:T(8,128)(2,1)S(1)}, bf16[32,4096]{1,0:T(8,128)(2,1)S(1)}, u32[]{:S(2)}, u32[]{:S(2)}) collective-permute-start(bf16[32,4096]{1,0:T(8,128)(2,1)S(1)} %get-tuple-element.64), channel_id=1, source_target_pairs={{0,1},{1,0},{2,3},{3,2},{4,5},{5,4},{6,7},{7,6},{8,9},{9,8},{10,11... | collective-permute-start | bytes 786440 | tf_op jit(solution)/shard_map/ppermute | solution.py:34
  56.1 3.4 %shard_map.150 = (bf16[1024,4096]{1,0:T(8,128)(2,1)S(1)}, f32[8,128]{1,0:T(8,128)S(1)}) custom-call(bf16[16,4096]{1,0:T(8,128)(2,1)S(1)} %get-tuple-element.68.refs_0_, bf16[1024,4096]{1,0:T(8,128)(2,1)} %refs_1_.6), custom_call_target="tpu_custom_call" | custom-call | bytes 16777216 | tf_op jit(solution)/shard_map/pallas_call | solution.py:194
  61.6 3.4 %collective-permute-start.14 = (bf16[16,4096]{1,0:T(8,128)(2,1)S(1)}, bf16[16,4096]{1,0:T(8,128)(2,1)S(1)}, u32[]{:S(2)}, u32[]{:S(2)}) collective-permute-start(bf16[16,4096]{1,0:T(8,128)(2,1)S(1)} %get-tuple-element.87), channel_id=1, source_target_pairs={{0,2},{1,3},{2,4},{3,5},{4,6},{5,7},{6,0},{7,1},{8,10},{9,11},{10,... | collective-permute-start | bytes 393224 | tf_op jit(solution)/shard_map/ppermute | solution.py:34
  65.1 2.2 %collective-permute-start.16 = (bf16[16,4096]{1,0:T(8,128)(2,1)S(1)}, bf16[16,4096]{1,0:T(8,128)(2,1)S(1)}, u32[]{:S(2)}, u32[]{:S(2)}) collective-permute-start(bf16[16,4096]{1,0:T(8,128)(2,1)S(1)} %add_convert_fusion.3), channel_id=1, source_target_pairs={{0,6},{1,7},{2,0},{3,1},{4,2},{5,3},{6,4},{7,5},{8,14},{9,15},{10,... | collective-permute-start | bytes 393224 | tf_op jit(solution)/shard_map/ppermute | solution.py:34
  68.5 2.0 %collective-permute-done.14 = bf16[16,4096]{1,0:T(8,128)(2,1)S(1)} collective-permute-done((bf16[16,4096]{1,0:T(8,128)(2,1)S(1)}, bf16[16,4096]{1,0:T(8,128)(2,1)S(1)}, u32[]{:S(2)}, u32[]{:S(2)}) %collective-permute-start.14) | collective-permute-done | bytes 131104 | tf_op jit(solution)/shard_map/ppermute | solution.py:34
  71.9 4.3 %collective-permute-start.22 = (bf16[16,4096]{1,0:T(8,128)(2,1)S(1)}, bf16[16,4096]{1,0:T(8,128)(2,1)S(1)}, u32[]{:S(2)}, u32[]{:S(2)}) collective-permute-start(bf16[16,4096]{1,0:T(8,128)(2,1)S(1)} %multiply_convert_fusion.refs_0_), channel_id=1, source_target_pairs={{0,6},{1,7},{2,0},{3,1},{4,2},{5,3},{6,4},{7,5},{8,14},{9,15},{10,... | collective-permute-start | bytes 393224 | tf_op jit(solution)/shard_map/ppermute | solution.py:34
  77.6 1.8 %collective-permute-start.18 = (bf16[16,4096]{1,0:T(8,128)(2,1)S(1)}, bf16[16,4096]{1,0:T(8,128)(2,1)S(1)}, u32[]{:S(2)}, u32[]{:S(2)}) collective-permute-start(bf16[16,4096]{1,0:T(8,128)(2,1)S(1)} %multiply_convert_fusion.refs_0_), channel_id=1, source_target_pairs={{0,2},{1,3},{2,4},{3,5},{4,6},{5,7},{6,0},{7,1},{8,10},{9,11},{10,... | collective-permute-start | bytes 393224 | tf_op jit(solution)/shard_map/ppermute | solution.py:34
  79.8 1.7 %collective-permute-start.23 = (bf16[16,4096]{1,0:T(8,128)(2,1)S(1)}, bf16[16,4096]{1,0:T(8,128)(2,1)S(1)}, u32[]{:S(2)}, u32[]{:S(2)}) collective-permute-start(bf16[16,4096]{1,0:T(8,128)(2,1)S(1)} %collective-permute-done.22.refs_6_), channel_id=1, source_target_pairs={{0,1},{1,0},{2,3},{3,2},{4,5},{5,4},{6,7},{7,6},{8,9},{9,8},{10,11... | collective-permute-start | bytes 393224 | tf_op jit(solution)/shard_map/ppermute | solution.py:34
  81.5 3.4 %collective-permute-done.20.refs_4_ = bf16[16,4096]{1,0:T(8,128)(2,1)S(1)} collective-permute-done((bf16[16,4096]{1,0:T(8,128)(2,1)S(1)}, bf16[16,4096]{1,0:T(8,128)(2,1)S(1)}, u32[]{:S(2)}, u32[]{:S(2)}) %collective-permute-start.20) | collective-permute-done | bytes 131104 | tf_op jit(solution)/shard_map/ppermute | solution.py:34
  84.9 2.0 %collective-permute-start.21 = (bf16[16,4096]{1,0:T(8,128)(2,1)S(1)}, bf16[16,4096]{1,0:T(8,128)(2,1)S(1)}, u32[]{:S(2)}, u32[]{:S(2)}) collective-permute-start(bf16[16,4096]{1,0:T(8,128)(2,1)S(1)} %collective-permute-done.20.refs_4_), channel_id=1, source_target_pairs={{0,1},{1,0},{2,3},{3,2},{4,5},{5,4},{6,7},{7,6},{8,9},{9,8},{10,11... | collective-permute-start | bytes 393224 | tf_op jit(solution)/shard_map/ppermute | solution.py:34
  87.0 4.0 %shard_map.152 = (bf16[4096,1024]{1,0:T(8,128)(2,1)S(1)}, f32[8,128]{1,0:T(8,128)}) custom-call(bf16[16,4096]{1,0:T(8,128)(2,1)S(1)} %multiply_convert_fusion.refs_0_, bf16[4096,1024]{1,0:T(8,128)(2,1)} %refs_1_.7), custom_call_target="tpu_custom_call" | custom-call | bytes 16777216 | tf_op jit(solution)/shard_map/pallas_call | solution.py:194
  91.2 2.8 %collective-permute-done.19.refs_3_ = bf16[16,4096]{1,0:T(8,128)(2,1)S(1)} collective-permute-done((bf16[16,4096]{1,0:T(8,128)(2,1)S(1)}, bf16[16,4096]{1,0:T(8,128)(2,1)S(1)}, u32[]{:S(2)}, u32[]{:S(2)}) %collective-permute-start.19) | collective-permute-done | bytes 131104 | tf_op jit(solution)/shard_map/ppermute | solution.py:34
  94.0 3.6 %shard_map.153 = (bf16[16,4096]{1,0:T(8,128)(2,1)S(1)}, bf16[16,4096]{1,0:T(8,128)(2,1)S(1)}, bf16[16,4096]{1,0:T(8,128)(2,1)S(1)}, bf16[16,4096]{1,0:T(8,128)(2...) custom-call(bf16[16,4096]{1,0:T(8,128)(2,1)S(1)} %multiply_convert_fusion.refs_0_, ...), custom_call_target="tpu_custom_call" | custom-call | flops 3221225472 | bytes 1048576 | tf_op jit(solution)/shard_map/pallas_call | solution.py:169
  97.6 2.2 %collective-permute-start.24 = (bf16[32,4096]{1,0:T(8,128)(2,1)S(1)}, bf16[32,4096]{1,0:T(8,128)(2,1)S(1)}, u32[]{:S(2)}, u32[]{:S(2)}) collective-permute-start(bf16[32,4096]{1,0:T(8,128)(2,1)S(1)} %get-tuple-element.74), channel_id=1, source_target_pairs={{0,1},{1,0},{2,3},{3,2},{4,5},{5,4},{6,7},{7,6},{8,9},{9,8},{10,11... | collective-permute-start | bytes 786440 | tf_op jit(solution)/shard_map/ppermute | solution.py:34
  99.9 4.3 %collective-permute-done.24 = bf16[32,4096]{1,0:T(8,128)(2,1)S(1)} collective-permute-done((bf16[32,4096]{1,0:T(8,128)(2,1)S(1)}, bf16[32,4096]{1,0:T(8,128)(2,1)S(1)}, u32[]{:S(2)}, u32[]{:S(2)}) %collective-permute-start.24) | collective-permute-done | bytes 262176 | tf_op jit(solution)/shard_map/ppermute | solution.py:34
  108.3 4.3 %collective-permute-done.25 = bf16[16,4096]{1,0:T(8,128)(2,1)S(1)} collective-permute-done((bf16[16,4096]{1,0:T(8,128)(2,1)S(1)}, bf16[16,4096]{1,0:T(8,128)(2,1)S(1)}, u32[]{:S(2)}, u32[]{:S(2)}) %collective-permute-start.25) | collective-permute-done | bytes 131104 | tf_op jit(solution)/shard_map/ppermute | solution.py:34
  (69 shorter events, 27.7 us)
Async XLA Ops:
  0.0 25.2 %copy-start.2 = (s32[128]{0:T(128)S(1)}, s32[128]{0:T(128)}, u32[]{:S(2)}) copy-start(s32[128]{0:T(128)} %param.15) | copy-start | bytes 1540
  1.6 10.7 %collective-permute-start.1 = (bf16[32,4096]{1,0:T(8,128)(2,1)S(1)}, bf16[32,4096]{1,0:T(8,128)(2,1)S(1)}, u32[]{:S(2)}, u32[]{:S(2)}) collective-permute-start(bf16[32,4096]{1,0:T(8,128)(2,1)S(1)} %shard_map.136.refs_0_), channel_id=1, source_target_pairs={{0,6},{1,7},{2,0},{3,1},{4,2},{5,3},{6,4},{7,5},{8,14},{9,15},{10,... | collective-permute-start | bytes 786440 | tf_op jit(solution)/shard_map/ppermute | solution.py:34
  6.7 7.8 %collective-permute-start = (bf16[32,4096]{1,0:T(8,128)(2,1)S(1)}, bf16[32,4096]{1,0:T(8,128)(2,1)S(1)}, u32[]{:S(2)}, u32[]{:S(2)}) collective-permute-start(bf16[32,4096]{1,0:T(8,128)(2,1)S(1)} %shard_map.136.refs_0_), channel_id=1, source_target_pairs={{0,1},{1,0},{2,3},{3,2},{4,5},{5,4},{6,7},{7,6},{8,9},{9,8},{10,11... | collective-permute-start | bytes 786440 | tf_op jit(solution)/shard_map/ppermute | solution.py:34
  14.5 8.7 %collective-permute-start.2 = (bf16[32,4096]{1,0:T(8,128)(2,1)S(1)}, bf16[32,4096]{1,0:T(8,128)(2,1)S(1)}, u32[]{:S(2)}, u32[]{:S(2)}) collective-permute-start(bf16[32,4096]{1,0:T(8,128)(2,1)S(1)} %shard_map.138), channel_id=1, source_target_pairs={{0,2},{1,3},{2,4},{3,5},{4,6},{5,7},{6,0},{7,1},{8,10},{9,11},{10,... | collective-permute-start | bytes 786440 | tf_op jit(solution)/shard_map/ppermute | solution.py:34
  20.5 8.7 %collective-permute-start.6 = (bf16[32,4096]{1,0:T(8,128)(2,1)S(1)}, bf16[32,4096]{1,0:T(8,128)(2,1)S(1)}, u32[]{:S(2)}, u32[]{:S(2)}) collective-permute-start(bf16[32,4096]{1,0:T(8,128)(2,1)S(1)} %shard_map.137.refs_1_.refs_0_.refs_6_), channel_id=1, source_target_pairs={{0,1},{1,0},{2,3},{3,2},{4,5},{5,4},{6,7},{7,6},{8,9},{9,8},{10,11... | collective-permute-start | bytes 786440 | tf_op jit(solution)/shard_map/ppermute | solution.py:34
  23.2 8.3 %collective-permute-start.5 = (bf16[32,4096]{1,0:T(8,128)(2,1)S(1)}, bf16[32,4096]{1,0:T(8,128)(2,1)S(1)}, u32[]{:S(2)}, u32[]{:S(2)}) collective-permute-start(bf16[32,4096]{1,0:T(8,128)(2,1)S(1)} %shard_map.142), channel_id=1, source_target_pairs={{2,0},{3,1},{4,2},{5,3},{10,8},{11,9},{12,10},{13,11},{18,16},{19,... | collective-permute-start | bytes 786440 | tf_op jit(solution)/shard_map/ppermute | solution.py:34
  24.5 7.0 %collective-permute-start.4 = (bf16[32,4096]{1,0:T(8,128)(2,1)S(1)}, bf16[32,4096]{1,0:T(8,128)(2,1)S(1)}, u32[]{:S(2)}, u32[]{:S(2)}) collective-permute-start(bf16[32,4096]{1,0:T(8,128)(2,1)S(1)} %shard_map.141.refs_1_.refs_2_), channel_id=1, source_target_pairs={{2,4},{3,5},{4,6},{5,7},{10,12},{11,13},{12,14},{13,15},{18,20},{1... | collective-permute-start | bytes 786440 | tf_op jit(solution)/shard_map/ppermute | solution.py:34
  25.3 13.9 %collective-permute-start.3 = (bf16[32,4096]{1,0:T(8,128)(2,1)S(1)}, bf16[32,4096]{1,0:T(8,128)(2,1)S(1)}, u32[]{:S(2)}, u32[]{:S(2)}) collective-permute-start(bf16[32,4096]{1,0:T(8,128)(2,1)S(1)} %shard_map.141.refs_1_.refs_2_), channel_id=1, source_target_pairs={{0,1},{1,0},{2,3},{3,2},{4,5},{5,4},{6,7},{7,6},{8,9},{9,8},{10,11... | collective-permute-start | bytes 786440 | tf_op jit(solution)/shard_map/ppermute | solution.py:34
  31.5 7.7 %collective-permute-start.7 = (bf16[32,4096]{1,0:T(8,128)(2,1)S(1)}, bf16[32,4096]{1,0:T(8,128)(2,1)S(1)}, u32[]{:S(2)}, u32[]{:S(2)}) collective-permute-start(bf16[32,4096]{1,0:T(8,128)(2,1)S(1)} %shard_map.143.refs_0_.refs_4_), channel_id=1, source_target_pairs={{0,1},{1,0},{2,3},{3,2},{4,5},{5,4},{6,7},{7,6},{8,9},{9,8},{10,11... | collective-permute-start | bytes 786440 | tf_op jit(solution)/shard_map/ppermute | solution.py:34
  41.0 4.0 %collective-permute-start.8 = (bf16[128,128]{1,0:T(8,128)(2,1)S(1)}, bf16[128,128]{1,0:T(8,128)(2,1)S(1)}, u32[]{:S(2)}, u32[]{:S(2)}) collective-permute-start(bf16[128,128]{1,0:T(8,128)(2,1)S(1)} %get-tuple-element.54), channel_id=1, source_target_pairs={{0,1},{1,0},{2,3},{3,2},{4,5},{5,4},{6,7},{7,6},{8,9},{9,8},{10,11... | collective-permute-start | bytes 98312 | tf_op jit(solution)/shard_map/ppermute | solution.py:34
  45.0 6.6 %collective-permute-start.9 = (bf16[64,128]{1,0:T(8,128)(2,1)S(1)}, bf16[64,128]{1,0:T(8,128)(2,1)S(1)}, u32[]{:S(2)}, u32[]{:S(2)}) collective-permute-start(bf16[64,128]{1,0:T(8,128)(2,1)S(1)} %get-tuple-element.56), channel_id=1, source_target_pairs={{0,2},{1,3},{2,4},{3,5},{4,6},{5,7},{6,0},{7,1},{8,10},{9,11},{10,... | collective-permute-start | bytes 49160 | tf_op jit(solution)/shard_map/ppermute | solution.py:34
  46.5 5.0 %collective-permute-start.10 = (bf16[64,128]{1,0:T(8,128)(2,1)S(1)}, bf16[64,128]{1,0:T(8,128)(2,1)S(1)}, u32[]{:S(2)}, u32[]{:S(2)}) collective-permute-start(bf16[64,128]{1,0:T(8,128)(2,1)S(1)} %get-tuple-element.57), channel_id=1, source_target_pairs={{0,4},{1,5},{2,6},{3,7},{4,0},{5,1},{6,2},{7,3},{8,12},{9,13},{10,... | collective-permute-start | bytes 49160 | tf_op jit(solution)/shard_map/ppermute | solution.py:34
  48.6 3.7 %collective-permute-start.11 = (bf16[64,128]{1,0:T(8,128)(2,1)S(1)}, bf16[64,128]{1,0:T(8,128)(2,1)S(1)}, u32[]{:S(2)}, u32[]{:S(2)}) collective-permute-start(bf16[64,128]{1,0:T(8,128)(2,1)S(1)} %get-tuple-element.58), channel_id=1, source_target_pairs={{0,6},{1,7},{2,0},{3,1},{4,2},{5,3},{6,4},{7,5},{8,14},{9,15},{10,... | collective-permute-start | bytes 49160 | tf_op jit(solution)/shard_map/ppermute | solution.py:34
  51.5 20.0 %copy-start.4 = (f32[4096]{0:T(1024)S(1)}, f32[4096]{0:T(1024)}, u32[]{:S(2)}) copy-start(f32[4096]{0:T(1024)} %param.26) | copy-start | bytes 49156
  51.6 20.2 %copy-start.5 = (f32[4096]{0:T(1024)S(1)}, f32[4096]{0:T(1024)}, u32[]{:S(2)}) copy-start(f32[4096]{0:T(1024)} %param.22) | copy-start | bytes 49156
  54.0 6.4 %collective-permute-start.12 = (bf16[32,4096]{1,0:T(8,128)(2,1)S(1)}, bf16[32,4096]{1,0:T(8,128)(2,1)S(1)}, u32[]{:S(2)}, u32[]{:S(2)}) collective-permute-start(bf16[32,4096]{1,0:T(8,128)(2,1)S(1)} %get-tuple-element.64), channel_id=1, source_target_pairs={{0,1},{1,0},{2,3},{3,2},{4,5},{5,4},{6,7},{7,6},{8,9},{9,8},{10,11... | collective-permute-start | bytes 786440 | tf_op jit(solution)/shard_map/ppermute | solution.py:34
  55.6 9.4 %collective-permute-start.15 = (bf16[32,4096]{1,0:T(8,128)(2,1)S(1)}, bf16[32,4096]{1,0:T(8,128)(2,1)S(1)}, u32[]{:S(2)}, u32[]{:S(2)}) collective-permute-start(bf16[32,4096]{1,0:T(8,128)(2,1)S(1)} %get-tuple-element.67), channel_id=1, source_target_pairs={{0,1},{1,0},{2,3},{3,2},{4,5},{5,4},{6,7},{7,6},{8,9},{9,8},{10,11... | collective-permute-start | bytes 786440 | tf_op jit(solution)/shard_map/ppermute | solution.py:34
  60.5 8.0 %collective-permute-start.13 = (bf16[16,4096]{1,0:T(8,128)(2,1)S(1)}, bf16[16,4096]{1,0:T(8,128)(2,1)S(1)}, u32[]{:S(2)}, u32[]{:S(2)}) collective-permute-start(bf16[16,4096]{1,0:T(8,128)(2,1)S(1)} %get-tuple-element.86), channel_id=1, source_target_pairs={{0,4},{1,5},{2,6},{3,7},{4,0},{5,1},{6,2},{7,3},{8,12},{9,13},{10,... | collective-permute-start | bytes 393224 | tf_op jit(solution)/shard_map/ppermute | solution.py:34
  61.6 9.0 %collective-permute-start.14 = (bf16[16,4096]{1,0:T(8,128)(2,1)S(1)}, bf16[16,4096]{1,0:T(8,128)(2,1)S(1)}, u32[]{:S(2)}, u32[]{:S(2)}) collective-permute-start(bf16[16,4096]{1,0:T(8,128)(2,1)S(1)} %get-tuple-element.87), channel_id=1, source_target_pairs={{0,2},{1,3},{2,4},{3,5},{4,6},{5,7},{6,0},{7,1},{8,10},{9,11},{10,... | collective-permute-start | bytes 393224 | tf_op jit(solution)/shard_map/ppermute | solution.py:34
  65.1 6.4 %collective-permute-start.16 = (bf16[16,4096]{1,0:T(8,128)(2,1)S(1)}, bf16[16,4096]{1,0:T(8,128)(2,1)S(1)}, u32[]{:S(2)}, u32[]{:S(2)}) collective-permute-start(bf16[16,4096]{1,0:T(8,128)(2,1)S(1)} %add_convert_fusion.3), channel_id=1, source_target_pairs={{0,6},{1,7},{2,0},{3,1},{4,2},{5,3},{6,4},{7,5},{8,14},{9,15},{10,... | collective-permute-start | bytes 393224 | tf_op jit(solution)/shard_map/ppermute | solution.py:34
  71.9 7.9 %collective-permute-start.22 = (bf16[16,4096]{1,0:T(8,128)(2,1)S(1)}, bf16[16,4096]{1,0:T(8,128)(2,1)S(1)}, u32[]{:S(2)}, u32[]{:S(2)}) collective-permute-start(bf16[16,4096]{1,0:T(8,128)(2,1)S(1)} %multiply_convert_fusion.refs_0_), channel_id=1, source_target_pairs={{0,6},{1,7},{2,0},{3,1},{4,2},{5,3},{6,4},{7,5},{8,14},{9,15},{10,... | collective-permute-start | bytes 393224 | tf_op jit(solution)/shard_map/ppermute | solution.py:34
  76.2 8.7 %collective-permute-start.20 = (bf16[16,4096]{1,0:T(8,128)(2,1)S(1)}, bf16[16,4096]{1,0:T(8,128)(2,1)S(1)}, u32[]{:S(2)}, u32[]{:S(2)}) collective-permute-start(bf16[16,4096]{1,0:T(8,128)(2,1)S(1)} %multiply_convert_fusion.refs_0_), channel_id=1, source_target_pairs={{0,4},{1,5},{2,6},{3,7},{4,0},{5,1},{6,2},{7,3},{8,12},{9,13},{10,... | collective-permute-start | bytes 393224 | tf_op jit(solution)/shard_map/ppermute | solution.py:34
  77.6 9.3 %collective-permute-start.18 = (bf16[16,4096]{1,0:T(8,128)(2,1)S(1)}, bf16[16,4096]{1,0:T(8,128)(2,1)S(1)}, u32[]{:S(2)}, u32[]{:S(2)}) collective-permute-start(bf16[16,4096]{1,0:T(8,128)(2,1)S(1)} %multiply_convert_fusion.refs_0_), channel_id=1, source_target_pairs={{0,2},{1,3},{2,4},{3,5},{4,6},{5,7},{6,0},{7,1},{8,10},{9,11},{10,... | collective-permute-start | bytes 393224 | tf_op jit(solution)/shard_map/ppermute | solution.py:34
  79.4 11.5 %collective-permute-start.17 = (bf16[16,4096]{1,0:T(8,128)(2,1)S(1)}, bf16[16,4096]{1,0:T(8,128)(2,1)S(1)}, u32[]{:S(2)}, u32[]{:S(2)}) collective-permute-start(bf16[16,4096]{1,0:T(8,128)(2,1)S(1)} %multiply_convert_fusion.refs_0_), channel_id=1, source_target_pairs={{0,1},{1,0},{2,3},{3,2},{4,5},{5,4},{6,7},{7,6},{8,9},{9,8},{10,11... | collective-permute-start | bytes 393224 | tf_op jit(solution)/shard_map/ppermute | solution.py:34
  79.8 11.2 %collective-permute-start.23 = (bf16[16,4096]{1,0:T(8,128)(2,1)S(1)}, bf16[16,4096]{1,0:T(8,128)(2,1)S(1)}, u32[]{:S(2)}, u32[]{:S(2)}) collective-permute-start(bf16[16,4096]{1,0:T(8,128)(2,1)S(1)} %collective-permute-done.22.refs_6_), channel_id=1, source_target_pairs={{0,1},{1,0},{2,3},{3,2},{4,5},{5,4},{6,7},{7,6},{8,9},{9,8},{10,11... | collective-permute-start | bytes 393224 | tf_op jit(solution)/shard_map/ppermute | solution.py:34
  84.9 6.3 %collective-permute-start.21 = (bf16[16,4096]{1,0:T(8,128)(2,1)S(1)}, bf16[16,4096]{1,0:T(8,128)(2,1)S(1)}, u32[]{:S(2)}, u32[]{:S(2)}) collective-permute-start(bf16[16,4096]{1,0:T(8,128)(2,1)S(1)} %collective-permute-done.20.refs_4_), channel_id=1, source_target_pairs={{0,1},{1,0},{2,3},{3,2},{4,5},{5,4},{6,7},{7,6},{8,9},{9,8},{10,11... | collective-permute-start | bytes 393224 | tf_op jit(solution)/shard_map/ppermute | solution.py:34
  86.9 7.1 %collective-permute-start.19 = (bf16[16,4096]{1,0:T(8,128)(2,1)S(1)}, bf16[16,4096]{1,0:T(8,128)(2,1)S(1)}, u32[]{:S(2)}, u32[]{:S(2)}) collective-permute-start(bf16[16,4096]{1,0:T(8,128)(2,1)S(1)} %collective-permute-done.18.refs_2_), channel_id=1, source_target_pairs={{0,1},{1,0},{2,3},{3,2},{4,5},{5,4},{6,7},{7,6},{8,9},{9,8},{10,11... | collective-permute-start | bytes 393224 | tf_op jit(solution)/shard_map/ppermute | solution.py:34
  97.6 6.5 %collective-permute-start.24 = (bf16[32,4096]{1,0:T(8,128)(2,1)S(1)}, bf16[32,4096]{1,0:T(8,128)(2,1)S(1)}, u32[]{:S(2)}, u32[]{:S(2)}) collective-permute-start(bf16[32,4096]{1,0:T(8,128)(2,1)S(1)} %get-tuple-element.74), channel_id=1, source_target_pairs={{0,1},{1,0},{2,3},{3,2},{4,5},{5,4},{6,7},{7,6},{8,9},{9,8},{10,11... | collective-permute-start | bytes 786440 | tf_op jit(solution)/shard_map/ppermute | solution.py:34
  99.8 7.2 %collective-permute-start.27 = (bf16[32,4096]{1,0:T(8,128)(2,1)S(1)}, bf16[32,4096]{1,0:T(8,128)(2,1)S(1)}, u32[]{:S(2)}, u32[]{:S(2)}) collective-permute-start(bf16[32,4096]{1,0:T(8,128)(2,1)S(1)} %get-tuple-element.77), channel_id=1, source_target_pairs={{0,1},{1,0},{2,3},{3,2},{4,5},{5,4},{6,7},{7,6},{8,9},{9,8},{10,11... | collective-permute-start | bytes 786440 | tf_op jit(solution)/shard_map/ppermute | solution.py:34
  104.2 8.3 %collective-permute-start.25 = (bf16[16,4096]{1,0:T(8,128)(2,1)S(1)}, bf16[16,4096]{1,0:T(8,128)(2,1)S(1)}, u32[]{:S(2)}, u32[]{:S(2)}) collective-permute-start(bf16[16,4096]{1,0:T(8,128)(2,1)S(1)} %get-tuple-element.84), channel_id=1, source_target_pairs={{0,4},{1,5},{2,6},{3,7},{4,0},{5,1},{6,2},{7,3},{8,12},{9,13},{10,... | collective-permute-start | bytes 393224 | tf_op jit(solution)/shard_map/ppermute | solution.py:34
  104.3 8.2 %collective-permute-start.26 = (bf16[16,4096]{1,0:T(8,128)(2,1)S(1)}, bf16[16,4096]{1,0:T(8,128)(2,1)S(1)}, u32[]{:S(2)}, u32[]{:S(2)}) collective-permute-start(bf16[16,4096]{1,0:T(8,128)(2,1)S(1)} %get-tuple-element.85), channel_id=1, source_target_pairs={{0,2},{1,3},{2,4},{3,5},{4,6},{5,7},{6,0},{7,1},{8,10},{9,11},{10,... | collective-permute-start | bytes 393224 | tf_op jit(solution)/shard_map/ppermute | solution.py:34
  107.0 6.8 %collective-permute-start.28 = (bf16[16,4096]{1,0:T(8,128)(2,1)S(1)}, bf16[16,4096]{1,0:T(8,128)(2,1)S(1)}, u32[]{:S(2)}, u32[]{:S(2)}) collective-permute-start(bf16[16,4096]{1,0:T(8,128)(2,1)S(1)} %add_convert_fusion), channel_id=1, source_target_pairs={{0,6},{1,7},{2,0},{3,1},{4,2},{5,3},{6,4},{7,5},{8,14},{9,15},{10,... | collective-permute-start | bytes 393224 | tf_op jit(solution)/shard_map/ppermute | solution.py:34
  (3 other events, 2.2 us)

commit v12 on v10

--- a/solution.py
+++ b/solution.py
@@ -89,20 +89,18 @@
 
 def gather_blocks(block, tall, wide):
     blocks = {(dz, 0): shift(block, tall, wide, dz, 0) if dz else block for dz in range(tall)}
-    for dz in range(tall):
+    for dy in range(1, wide):
+        blocks[0, dy] = shift(block, tall, wide, 0, dy)
+    blocks[1, 0] = tie([blocks[1, 0]], [blocks[0, dy] for dy in range(1, wide)])
+    for dz in range(1, tall):
         for dy in range(1, wide):
             blocks[dz, dy] = shift(blocks[dz, 0], tall, wide, 0, dy)
     return [blocks[dz, dy] for dz in range(tall) for dy in range(wide)]
 
 
-def sum_order(tall):
-    order = [tall // 2, *range(1, tall // 2), *range(tall // 2 + 1, tall), 0]
-    return order[: tall // 2], order[tall // 2 :]
-
-
 def sum_shapes(tall, wide, share, model):
     kept = [((share, model), bf16)] * tall
-    return kept + [((tall // 2 * share, model), bf16)] * (2 * (wide - 1))
+    return kept + [((tall * share, model), bf16)] * (wide - 1)
 
 
 def store_parts(parts, tall, wide, span, product, back):
@@ -115,37 +113,25 @@
 
     for dz in range(tall):
         parts[dz][:, span] = rows(dz, 0)
-    for dy in range(1, wide):
-        for which, group in enumerate(sum_order(tall)):
-            out = parts[tall + 2 * (dy - 1) + which]
-            for place, dz in enumerate(group):
-                out[place * share : (place + 1) * share, span] = rows(dz, dy)
+        for dy in range(1, wide):
+            parts[tall + dy - 1][dz * share : (dz + 1) * share, span] = rows(dz, dy)
 
 
 def scatter_sum(parts, tall, wide, loads=()):
     share = parts[0].shape[0]
     loaded = []
-    crossed = [shift(p, tall, wide, 0, i // 2 + 1) for i, p in enumerate(parts[tall:])]
+    crossed = [shift(p, tall, wide, 0, dy) for dy, p in enumerate(parts[tall:], 1)]
     if loads:
-        *copy, token = load(parts[0], loads[0])
-        loaded += copy
-        crossed[1] = tie([crossed[1]], [token])
+        *loaded, token = load(parts[0], *loads)
+        crossed[0] = tie([crossed[0]], [token])
     total = None
-    for which, group in enumerate(sum_order(tall)):
-        for place, dz in enumerate(group):
-            lane = parts[dz].astype(f32)
-            for dy in range(1, wide):
-                other = crossed[2 * (dy - 1) + which]
-                lane = lane + other[place * share : (place + 1) * share].astype(f32)
-            if dz:
-                sent = lane.astype(bf16)
-                lane = shift(sent, tall, wide, dz, 0)
-                if len(loads) > 1 and dz == tall - 1:
-                    *copy, token = load(sent, loads[1])
-                    loaded += copy
-                    lane = tie([lane], [token])
-                lane = lane.astype(f32)
-            total = lane if total is None else total + lane
+    for dz in [tall // 2, *range(1, tall // 2), *range(tall // 2 + 1, tall), 0]:
+        lane = parts[dz].astype(f32)
+        for other in crossed:
+            lane = lane + other[dz * share : (dz + 1) * share].astype(f32)
+        if dz:
+            lane = shift(lane.astype(bf16), tall, wide, dz, 0).astype(f32)
+        total = lane if total is None else total + lane
     return (total, *loaded) if loads else total
 
 

time: 112 us -> 120 us (1.071)
  waiting for transfers between devices: 36.4 us -> 52 us
  starting transfers between devices: 44.9 us -> 36.9 us
    ppermute x29 -> x27, waiting for transfers between devices: 36.4 us -> 52 us  [shift(): return lax.ppermute(block, 'ctx', pairs)]
    ppermute x29 -> x27, starting transfers between devices: 44.9 us -> 36.9 us  [shift(): return lax.ppermute(block, 'ctx', pairs)]
    pallas_call x10 -> x11, Pallas kernels: 10.3 us -> 10.4 us  [kernel_call(): pl.pallas_call(body, out_shape=[jax.ShapeDtypeStruct(s, d) for s, d in ou...]
  transfers between devices with their start and end apart: 29 -> 27, of which waited for: 17 -> 18; matrix products, arithmetic and copies ran while one was open for 1% -> 0% of each run, Pallas kernels for 16% -> 15%
where the time goes in v12:
time: 120 us; the launch traced here: 119 us
  waiting for transfers between devices  52 us (43%)
  starting transfers between devices  36.9 us (31%)
  Pallas kernels  26.2 us (22%)
  local copies, waits for them, and re-layouts  2.23 us (2%)
  other arithmetic  1.88 us (2%)
    ppermute x27, waiting for transfers between devices, shift(): return lax.ppermute(block, 'ctx', pairs)  52 us
    ppermute x27, starting transfers between devices, shift(): return lax.ppermute(block, 'ctx', pairs)  36.9 us
    pallas_call x5, Pallas kernels, load(): pl.pallas_call(functools.partial(load_body, len(arrays)), out_shape=[pltp...  15.9 us
    pallas_call x11, Pallas kernels, kernel_call(): pl.pallas_call(body, out_shape=[jax.ShapeDtypeStruct(s, d) for s, d in ou...  10.4 us
  transfers between devices with their start and end apart: 27, of which 18 were waited for; matrix products, arithmetic and copies ran while one was open for 0% of the time, Pallas kernels for 15%

profile of v12, /device:TPU:0, one launch (start us, length us, event | category | flops | bytes accessed | tf_op | source)
XLA Modules:
  0.0 119.5 jit_solution(17941038371828333634)
XLA Ops:
  1.6 3.1 %collective-permute-start.1 = (bf16[32,4096]{1,0:T(8,128)(2,1)S(1)}, bf16[32,4096]{1,0:T(8,128)(2,1)S(1)}, u32[]{:S(2)}, u32[]{:S(2)}) collective-permute-start(bf16[32,4096]{1,0:T(8,128)(2,1)S(1)} %shard_map.136.refs_0_), channel_id=1, source_target_pairs={{0,2},{1,3},{2,4},{3,5},{4,6},{5,7},{6,0},{7,1},{8,10},{9,11},{10,... | collective-permute-start | bytes 786440 | tf_op jit(solution)/shard_map/ppermute | solution.py:34
  4.6 2.1 %collective-permute-start.4 = (bf16[32,4096]{1,0:T(8,128)(2,1)S(1)}, bf16[32,4096]{1,0:T(8,128)(2,1)S(1)}, u32[]{:S(2)}, u32[]{:S(2)}) collective-permute-start(bf16[32,4096]{1,0:T(8,128)(2,1)S(1)} %shard_map.136.refs_0_), channel_id=1, source_target_pairs={{0,6},{1,7},{2,0},{3,1},{4,2},{5,3},{6,4},{7,5},{8,14},{9,15},{10,... | collective-permute-start | bytes 786440 | tf_op jit(solution)/shard_map/ppermute | solution.py:34
  6.7 1.7 %collective-permute-start = (bf16[32,4096]{1,0:T(8,128)(2,1)S(1)}, bf16[32,4096]{1,0:T(8,128)(2,1)S(1)}, u32[]{:S(2)}, u32[]{:S(2)}) collective-permute-start(bf16[32,4096]{1,0:T(8,128)(2,1)S(1)} %shard_map.136.refs_0_), channel_id=1, source_target_pairs={{0,1},{1,0},{2,3},{3,2},{4,5},{5,4},{6,7},{7,6},{8,9},{9,8},{10,11... | collective-permute-start | bytes 786440 | tf_op jit(solution)/shard_map/ppermute | solution.py:34
  11.5 2.9 %shard_map.137 = (f32[1,4096]{1,0:T(1,128)S(1)}, bf16[4096,128]{1,0:T(8,128)(2,1)S(1)}, bf16[4096,128]{1,0:T(8,128)(2,1)S(1)}, bf16[4096,512]{1,0:T(8,128)(2,1)S(1)}, f32[8,128]{1,0:T(8,128)S(1)}) custom-call(bf16[32,4096]{1,0:T(8,128)(2,1)S(1)} %shard_map.136.refs_0_, f32[1,4096]{1,0:T(1,128)} %bitcast.8, bf16[4096,128]{1,0:T(8,128)(2,1)} %refs_2_.1, ...), custom_call_target="tpu_custom_call" | custom-call | bytes 12615680 | tf_op jit(solution)/shard_map/pallas_call | solution.py:176
  15.1 2.9 %collective-permute-done.4.refs_0_ = bf16[32,4096]{1,0:T(8,128)(2,1)S(1)} collective-permute-done((bf16[32,4096]{1,0:T(8,128)(2,1)S(1)}, bf16[32,4096]{1,0:T(8,128)(2,1)S(1)}, u32[]{:S(2)}, u32[]{:S(2)}) %collective-permute-start.4) | collective-permute-done | bytes 262176 | tf_op jit(solution)/shard_map/ppermute | solution.py:34
  18.0 1.6 %collective-permute-start.6 = (bf16[32,4096]{1,0:T(8,128)(2,1)S(1)}, bf16[32,4096]{1,0:T(8,128)(2,1)S(1)}, u32[]{:S(2)}, u32[]{:S(2)}) collective-permute-start(bf16[32,4096]{1,0:T(8,128)(2,1)S(1)} %shard_map.139.refs_6_), channel_id=1, source_target_pairs={{0,1},{1,0},{2,3},{3,2},{4,5},{5,4},{6,7},{7,6},{8,9},{9,8},{10,11... | collective-permute-start | bytes 786440 | tf_op jit(solution)/shard_map/ppermute | solution.py:34
  21.5 5.8 %collective-permute-done.6.refs_2_.refs_7_ = bf16[32,4096]{1,0:T(8,128)(2,1)S(1)} collective-permute-done((bf16[32,4096]{1,0:T(8,128)(2,1)S(1)}, bf16[32,4096]{1,0:T(8,128)(2,1)S(1)}, u32[]{:S(2)}, u32[]{:S(2)}) %collective-permute-start.6) | collective-permute-done | bytes 262176 | tf_op jit(solution)/shard_map/ppermute | solution.py:34
  27.4 2.3 %collective-permute-done.5.refs_1_ = bf16[32,4096]{1,0:T(8,128)(2,1)S(1)} collective-permute-done((bf16[32,4096]{1,0:T(8,128)(2,1)S(1)}, bf16[32,4096]{1,0:T(8,128)(2,1)S(1)}, u32[]{:S(2)}, u32[]{:S(2)}) %collective-permute-start.5) | collective-permute-done | bytes 262176 | tf_op jit(solution)/shard_map/ppermute | solution.py:34
  30.7 2.2 %shard_map.141 = (bf16[512,4096]{1,0:T(8,128)(2,1)S(1)}, f32[8,128]{1,0:T(8,128)S(1)}) custom-call(bf16[32,4096]{1,0:T(8,128)(2,1)S(1)} %shard_map.140.refs_0_.refs_4_, bf16[512,4096]{1,0:T(8,128)(2,1)} %refs_1_.4), custom_call_target="tpu_custom_call" | custom-call | bytes 8388608 | tf_op jit(solution)/shard_map/pallas_call | solution.py:176
  32.9 3.4 %shard_map.142 = (bf16[4096,1024]{1,0:T(8,128)(2,1)S(1)}, f32[8,128]{1,0:T(8,128)S(1)}) custom-call(bf16[32,4096]{1,0:T(8,128)(2,1)S(1)} %shard_map.140.refs_0_.refs_4_, bf16[4096,1024]{1,0:T(8,128)(2,1)} %refs_1_.5), custom_call_target="tpu_custom_call" | custom-call | bytes 16777216 | tf_op jit(solution)/shard_map/pallas_call | solution.py:176
  37.0 1.8 %shard_map.143 = (bf16[128,4096]{1,0:T(8,128)(2,1)S(1)}, bf16[16,4096]{1,0:T(8,128)(2,1)S(1)}, bf16[128,128]{1,0:T(8,128)(2,1)S(1)}, bf16[128,128]{1,0:T(8,128)(2,1)S(1)}) custom-call(bf16[32,4096]{1,0:T(8,128)(2,1)S(1)} %shard_map.136.refs_0_, bf16[32,4096]{1,0:T(8,128)(2,1)S(1)} %collective-permute-done.refs_3_.refs_1_, ...), custom_call_target="tpu_custom_call" | custom-call | flops 536870912 | bytes 1048576 | tf_op jit(solution)/shard_map/pallas_call | solution.py:151
  38.7 1.6 %collective-permute-start.8 = (bf16[128,128]{1,0:T(8,128)(2,1)S(1)}, bf16[128,128]{1,0:T(8,128)(2,1)S(1)}, u32[]{:S(2)}, u32[]{:S(2)}) collective-permute-start(bf16[128,128]{1,0:T(8,128)(2,1)S(1)} %get-tuple-element.52), channel_id=1, source_target_pairs={{0,1},{1,0},{2,3},{3,2},{4,5},{5,4},{6,7},{7,6},{8,9},{9,8},{10,11... | collective-permute-start | bytes 98312 | tf_op jit(solution)/shard_map/ppermute | solution.py:34
  40.4 2.3 %collective-permute-done.8.refs_1_ = bf16[128,128]{1,0:T(8,128)(2,1)S(1)} collective-permute-done((bf16[128,128]{1,0:T(8,128)(2,1)S(1)}, bf16[128,128]{1,0:T(8,128)(2,1)S(1)}, u32[]{:S(2)}, u32[]{:S(2)}) %collective-permute-start.8) | collective-permute-done | bytes 32800 | tf_op jit(solution)/shard_map/ppermute | solution.py:34
  42.7 2.3 %collective-permute-start.9 = (bf16[64,128]{1,0:T(8,128)(2,1)S(1)}, bf16[64,128]{1,0:T(8,128)(2,1)S(1)}, u32[]{:S(2)}, u32[]{:S(2)}) collective-permute-start(bf16[64,128]{1,0:T(8,128)(2,1)S(1)} %get-tuple-element.54), channel_id=1, source_target_pairs={{0,2},{1,3},{2,4},{3,5},{4,6},{5,7},{6,0},{7,1},{8,10},{9,11},{10,... | collective-permute-start | bytes 49160 | tf_op jit(solution)/shard_map/ppermute | solution.py:34
  46.3 2.8 %collective-permute-start.11 = (bf16[64,128]{1,0:T(8,128)(2,1)S(1)}, bf16[64,128]{1,0:T(8,128)(2,1)S(1)}, u32[]{:S(2)}, u32[]{:S(2)}) collective-permute-start(bf16[64,128]{1,0:T(8,128)(2,1)S(1)} %get-tuple-element.56), channel_id=1, source_target_pairs={{0,6},{1,7},{2,0},{3,1},{4,2},{5,3},{6,4},{7,5},{8,14},{9,15},{10,... | collective-permute-start | bytes 49160 | tf_op jit(solution)/shard_map/ppermute | solution.py:34
  50.5 1.7 %shard_map.146 = (bf16[16,4096]{1,0:T(8,128)(2,1)S(1)}, bf16[16,4096]{1,0:T(8,128)(2,1)S(1)}, bf16[16,4096]{1,0:T(8,128)(2,1)S(1)}, bf16[16,4096]{1,0:T(8,128)(2,1)S(1)}, bf16[64,4096]{1,0:T(8,128)(2,1)S(1)}) custom-call(bf16[64,128]{1,0:T(8,128)(2,1)S(1)} %get-tuple-element.53.refs_0_, bf16[64,128]{1,0:T(8,128)(2,1)S(1)} %collective-permute-done.9.refs_1_, ...), custom_call_target="tpu_custom_call" | custom-call | flops 536870912 | bytes 1048576 | tf_op jit(solution)/shard_map/pallas_call | solution.py:151
  52.8 3.4 %shard_map.147 = (bf16[1024,4096]{1,0:T(8,128)(2,1)S(1)}, f32[8,128]{1,0:T(8,128)S(1)}) custom-call(bf16[16,4096]{1,0:T(8,128)(2,1)S(1)} %get-tuple-element.63.refs_0_, bf16[1024,4096]{1,0:T(8,128)(2,1)} %refs_1_.6), custom_call_target="tpu_custom_call" | custom-call | bytes 16777216 | tf_op jit(solution)/shard_map/pallas_call | solution.py:176
  56.2 5.3 %collective-permute-done.12.refs_0_ = bf16[64,4096]{1,0:T(8,128)(2,1)S(1)} collective-permute-done((bf16[64,4096]{1,0:T(8,128)(2,1)S(1)}, bf16[64,4096]{1,0:T(8,128)(2,1)S(1)}, u32[]{:S(2)}, u32[]{:S(2)}) %collective-permute-start.12) | collective-permute-done | bytes 524320 | tf_op jit(solution)/shard_map/ppermute | solution.py:34
  62.8 3.0 %collective-permute-start.15 = (bf16[16,4096]{1,0:T(8,128)(2,1)S(1)}, bf16[16,4096]{1,0:T(8,128)(2,1)S(1)}, u32[]{:S(2)}, u32[]{:S(2)}) collective-permute-start(bf16[16,4096]{1,0:T(8,128)(2,1)S(1)} %get-tuple-element.84), channel_id=1, source_target_pairs={{0,6},{1,7},{2,0},{3,1},{4,2},{5,3},{6,4},{7,5},{8,14},{9,15},{10,... | collective-permute-start | bytes 393224 | tf_op jit(solution)/shard_map/ppermute | solution.py:34
  66.3 3.4 %collective-permute-done.13 = bf16[16,4096]{1,0:T(8,128)(2,1)S(1)} collective-permute-done((bf16[16,4096]{1,0:T(8,128)(2,1)S(1)}, bf16[16,4096]{1,0:T(8,128)(2,1)S(1)}, u32[]{:S(2)}, u32[]{:S(2)}) %collective-permute-start.13) | collective-permute-done | bytes 131104 | tf_op jit(solution)/shard_map/ppermute | solution.py:34
  70.6 4.6 %collective-permute-done.14 = bf16[16,4096]{1,0:T(8,128)(2,1)S(1)} collective-permute-done((bf16[16,4096]{1,0:T(8,128)(2,1)S(1)}, bf16[16,4096]{1,0:T(8,128)(2,1)S(1)}, u32[]{:S(2)}, u32[]{:S(2)}) %collective-permute-start.14) | collective-permute-done | bytes 131104 | tf_op jit(solution)/shard_map/ppermute | solution.py:34
  75.5 3.5 %collective-permute-start.21 = (bf16[16,4096]{1,0:T(8,128)(2,1)S(1)}, bf16[16,4096]{1,0:T(8,128)(2,1)S(1)}, u32[]{:S(2)}, u32[]{:S(2)}) collective-permute-start(bf16[16,4096]{1,0:T(8,128)(2,1)S(1)} %multiply_convert_fusion.refs_0_), channel_id=1, source_target_pairs={{0,6},{1,7},{2,0},{3,1},{4,2},{5,3},{6,4},{7,5},{8,14},{9,15},{10,... | collective-permute-start | bytes 393224 | tf_op jit(solution)/shard_map/ppermute | solution.py:34
  79.4 1.9 %collective-permute-start.17 = (bf16[16,4096]{1,0:T(8,128)(2,1)S(1)}, bf16[16,4096]{1,0:T(8,128)(2,1)S(1)}, u32[]{:S(2)}, u32[]{:S(2)}) collective-permute-start(bf16[16,4096]{1,0:T(8,128)(2,1)S(1)} %multiply_convert_fusion.refs_0_), channel_id=1, source_target_pairs={{0,2},{1,3},{2,4},{3,5},{4,6},{5,7},{6,0},{7,1},{8,10},{9,11},{10,... | collective-permute-start | bytes 393224 | tf_op jit(solution)/shard_map/ppermute | solution.py:34
  81.5 1.8 %collective-permute-start.22 = (bf16[16,4096]{1,0:T(8,128)(2,1)S(1)}, bf16[16,4096]{1,0:T(8,128)(2,1)S(1)}, u32[]{:S(2)}, u32[]{:S(2)}) collective-permute-start(bf16[16,4096]{1,0:T(8,128)(2,1)S(1)} %collective-permute-done.21.refs_6_), channel_id=1, source_target_pairs={{0,1},{1,0},{2,3},{3,2},{4,5},{5,4},{6,7},{7,6},{8,9},{9,8},{10,11... | collective-permute-start | bytes 393224 | tf_op jit(solution)/shard_map/ppermute | solution.py:34
  83.3 4.3 %collective-permute-done.19.refs_4_ = bf16[16,4096]{1,0:T(8,128)(2,1)S(1)} collective-permute-done((bf16[16,4096]{1,0:T(8,128)(2,1)S(1)}, bf16[16,4096]{1,0:T(8,128)(2,1)S(1)}, u32[]{:S(2)}, u32[]{:S(2)}) %collective-permute-start.19) | collective-permute-done | bytes 131104 | tf_op jit(solution)/shard_map/ppermute | solution.py:34
  87.9 1.9 %collective-permute-start.18 = (bf16[16,4096]{1,0:T(8,128)(2,1)S(1)}, bf16[16,4096]{1,0:T(8,128)(2,1)S(1)}, u32[]{:S(2)}, u32[]{:S(2)}) collective-permute-start(bf16[16,4096]{1,0:T(8,128)(2,1)S(1)} %shard_map.149.refs_2_), channel_id=1, source_target_pairs={{0,1},{1,0},{2,3},{3,2},{4,5},{5,4},{6,7},{7,6},{8,9},{9,8},{10,11... | collective-permute-start | bytes 393224 | tf_op jit(solution)/shard_map/ppermute | solution.py:34
  89.8 4.0 %shard_map.150 = (bf16[4096,1024]{1,0:T(8,128)(2,1)S(1)}, f32[8,128]{1,0:T(8,128)}) custom-call(bf16[16,4096]{1,0:T(8,128)(2,1)S(1)} %multiply_convert_fusion.refs_0_, bf16[4096,1024]{1,0:T(8,128)(2,1)} %refs_1_.7), custom_call_target="tpu_custom_call" | custom-call | bytes 16777216 | tf_op jit(solution)/shard_map/pallas_call | solution.py:176
  94.1 2.8 %collective-permute-done.18.refs_3_ = bf16[16,4096]{1,0:T(8,128)(2,1)S(1)} collective-permute-done((bf16[16,4096]{1,0:T(8,128)(2,1)S(1)}, bf16[16,4096]{1,0:T(8,128)(2,1)S(1)}, u32[]{:S(2)}, u32[]{:S(2)}) %collective-permute-start.18) | collective-permute-done | bytes 131104 | tf_op jit(solution)/shard_map/ppermute | solution.py:34
  96.9 3.6 %shard_map.151 = (bf16[16,4096]{1,0:T(8,128)(2,1)S(1)}, bf16[16,4096]{1,0:T(8,128)(2,1)S(1)}, bf16[16,4096]{1,0:T(8,128)(2,1)S(1)}, bf16[16,4096]{1,0:T(8,128)(2,1)S(1)}, bf16[64,4096]{1,0:T(8,128)(2,1)S(1)}) custom-call(bf16[16,4096]{1,0:T(8,128)(2,1)S(1)} %multiply_convert_fusion.refs_0_, bf16[16,4096]{1,0:T(8,128)(2,1)S(1)} %collective-permute-done.16.refs_1_, ...), custom_call_target="tpu_custom_call" | custom-call | flops 3221225472 | bytes 1048576 | tf_op jit(solution)/shard_map/pallas_call | solution.py:151
  100.8 9.0 %collective-permute-done.23 = bf16[64,4096]{1,0:T(8,128)(2,1)S(1)} collective-permute-done((bf16[64,4096]{1,0:T(8,128)(2,1)S(1)}, bf16[64,4096]{1,0:T(8,128)(2,1)S(1)}, u32[]{:S(2)}, u32[]{:S(2)}) %collective-permute-start.23) | collective-permute-done | bytes 524320 | tf_op jit(solution)/shard_map/ppermute | solution.py:34
  112.0 3.9 %collective-permute-done.24 = bf16[16,4096]{1,0:T(8,128)(2,1)S(1)} collective-permute-done((bf16[16,4096]{1,0:T(8,128)(2,1)S(1)}, bf16[16,4096]{1,0:T(8,128)(2,1)S(1)}, u32[]{:S(2)}, u32[]{:S(2)}) %collective-permute-start.24) | collective-permute-done | bytes 131104 | tf_op jit(solution)/shard_map/ppermute | solution.py:34
  116.4 2.3 %collective-permute-done.25 = bf16[16,4096]{1,0:T(8,128)(2,1)S(1)} collective-permute-done((bf16[16,4096]{1,0:T(8,128)(2,1)S(1)}, bf16[16,4096]{1,0:T(8,128)(2,1)S(1)}, u32[]{:S(2)}, u32[]{:S(2)}) %collective-permute-start.25) | collective-permute-done | bytes 131104 | tf_op jit(solution)/shard_map/ppermute | solution.py:34
  (61 shorter events, 20.2 us)
Async XLA Ops:
  0.0 20.9 %copy-start.2 = (s32[128]{0:T(128)S(1)}, s32[128]{0:T(128)}, u32[]{:S(2)}) copy-start(s32[128]{0:T(128)} %param.15) | copy-start | bytes 1540
  1.6 12.8 %collective-permute-start.1 = (bf16[32,4096]{1,0:T(8,128)(2,1)S(1)}, bf16[32,4096]{1,0:T(8,128)(2,1)S(1)}, u32[]{:S(2)}, u32[]{:S(2)}) collective-permute-start(bf16[32,4096]{1,0:T(8,128)(2,1)S(1)} %shard_map.136.refs_0_), channel_id=1, source_target_pairs={{0,2},{1,3},{2,4},{3,5},{4,6},{5,7},{6,0},{7,1},{8,10},{9,11},{10,... | collective-permute-start | bytes 786440 | tf_op jit(solution)/shard_map/ppermute | solution.py:34
  4.6 13.4 %collective-permute-start.4 = (bf16[32,4096]{1,0:T(8,128)(2,1)S(1)}, bf16[32,4096]{1,0:T(8,128)(2,1)S(1)}, u32[]{:S(2)}, u32[]{:S(2)}) collective-permute-start(bf16[32,4096]{1,0:T(8,128)(2,1)S(1)} %shard_map.136.refs_0_), channel_id=1, source_target_pairs={{0,6},{1,7},{2,0},{3,1},{4,2},{5,3},{6,4},{7,5},{8,14},{9,15},{10,... | collective-permute-start | bytes 786440 | tf_op jit(solution)/shard_map/ppermute | solution.py:34
  6.7 11.3 %collective-permute-start = (bf16[32,4096]{1,0:T(8,128)(2,1)S(1)}, bf16[32,4096]{1,0:T(8,128)(2,1)S(1)}, u32[]{:S(2)}, u32[]{:S(2)}) collective-permute-start(bf16[32,4096]{1,0:T(8,128)(2,1)S(1)} %shard_map.136.refs_0_), channel_id=1, source_target_pairs={{0,1},{1,0},{2,3},{3,2},{4,5},{5,4},{6,7},{7,6},{8,9},{9,8},{10,11... | collective-permute-start | bytes 786440 | tf_op jit(solution)/shard_map/ppermute | solution.py:34
  8.4 0.9 copy-start
  9.3 0.7 copy-start.1
  14.4 7.1 %collective-permute-start.3 = (bf16[32,4096]{1,0:T(8,128)(2,1)S(1)}, bf16[32,4096]{1,0:T(8,128)(2,1)S(1)}, u32[]{:S(2)}, u32[]{:S(2)}) collective-permute-start(bf16[32,4096]{1,0:T(8,128)(2,1)S(1)} %collective-permute-done.1.refs_2_), channel_id=1, source_target_pairs={{2,4},{3,5},{4,6},{5,7},{10,12},{11,13},{12,14},{13,15},{18,20},{1... | collective-permute-start | bytes 786440 | tf_op jit(solution)/shard_map/ppermute | solution.py:34
  18.0 9.3 %collective-permute-start.6 = (bf16[32,4096]{1,0:T(8,128)(2,1)S(1)}, bf16[32,4096]{1,0:T(8,128)(2,1)S(1)}, u32[]{:S(2)}, u32[]{:S(2)}) collective-permute-start(bf16[32,4096]{1,0:T(8,128)(2,1)S(1)} %shard_map.139.refs_6_), channel_id=1, source_target_pairs={{0,1},{1,0},{2,3},{3,2},{4,5},{5,4},{6,7},{7,6},{8,9},{9,8},{10,11... | collective-permute-start | bytes 786440 | tf_op jit(solution)/shard_map/ppermute | solution.py:34
  19.6 10.0 %collective-permute-start.5 = (bf16[32,4096]{1,0:T(8,128)(2,1)S(1)}, bf16[32,4096]{1,0:T(8,128)(2,1)S(1)}, u32[]{:S(2)}, u32[]{:S(2)}) collective-permute-start(bf16[32,4096]{1,0:T(8,128)(2,1)S(1)} %shard_map.139.refs_6_), channel_id=1, source_target_pairs={{2,0},{3,1},{4,2},{5,3},{10,8},{11,9},{12,10},{13,11},{18,16},{19,... | collective-permute-start | bytes 786440 | tf_op jit(solution)/shard_map/ppermute | solution.py:34
  21.0 15.4 %collective-permute-start.2 = (bf16[32,4096]{1,0:T(8,128)(2,1)S(1)}, bf16[32,4096]{1,0:T(8,128)(2,1)S(1)}, u32[]{:S(2)}, u32[]{:S(2)}) collective-permute-start(bf16[32,4096]{1,0:T(8,128)(2,1)S(1)} %collective-permute-done.1.refs_2_), channel_id=1, source_target_pairs={{0,1},{1,0},{2,3},{3,2},{4,5},{5,4},{6,7},{7,6},{8,9},{9,8},{10,11... | collective-permute-start | bytes 786440 | tf_op jit(solution)/shard_map/ppermute | solution.py:34
  29.7 7.2 %collective-permute-start.7 = (bf16[32,4096]{1,0:T(8,128)(2,1)S(1)}, bf16[32,4096]{1,0:T(8,128)(2,1)S(1)}, u32[]{:S(2)}, u32[]{:S(2)}) collective-permute-start(bf16[32,4096]{1,0:T(8,128)(2,1)S(1)} %shard_map.140.refs_0_.refs_4_), channel_id=1, source_target_pairs={{0,1},{1,0},{2,3},{3,2},{4,5},{5,4},{6,7},{7,6},{8,9},{9,8},{10,11... | collective-permute-start | bytes 786440 | tf_op jit(solution)/shard_map/ppermute | solution.py:34
  38.7 4.0 %collective-permute-start.8 = (bf16[128,128]{1,0:T(8,128)(2,1)S(1)}, bf16[128,128]{1,0:T(8,128)(2,1)S(1)}, u32[]{:S(2)}, u32[]{:S(2)}) collective-permute-start(bf16[128,128]{1,0:T(8,128)(2,1)S(1)} %get-tuple-element.52), channel_id=1, source_target_pairs={{0,1},{1,0},{2,3},{3,2},{4,5},{5,4},{6,7},{7,6},{8,9},{9,8},{10,11... | collective-permute-start | bytes 98312 | tf_op jit(solution)/shard_map/ppermute | solution.py:34
  42.7 7.2 %collective-permute-start.9 = (bf16[64,128]{1,0:T(8,128)(2,1)S(1)}, bf16[64,128]{1,0:T(8,128)(2,1)S(1)}, u32[]{:S(2)}, u32[]{:S(2)}) collective-permute-start(bf16[64,128]{1,0:T(8,128)(2,1)S(1)} %get-tuple-element.54), channel_id=1, source_target_pairs={{0,2},{1,3},{2,4},{3,5},{4,6},{5,7},{6,0},{7,1},{8,10},{9,11},{10,... | collective-permute-start | bytes 49160 | tf_op jit(solution)/shard_map/ppermute | solution.py:34
  45.0 5.0 %collective-permute-start.10 = (bf16[64,128]{1,0:T(8,128)(2,1)S(1)}, bf16[64,128]{1,0:T(8,128)(2,1)S(1)}, u32[]{:S(2)}, u32[]{:S(2)}) collective-permute-start(bf16[64,128]{1,0:T(8,128)(2,1)S(1)} %get-tuple-element.55), channel_id=1, source_target_pairs={{0,4},{1,5},{2,6},{3,7},{4,0},{5,1},{6,2},{7,3},{8,12},{9,13},{10,... | collective-permute-start | bytes 49160 | tf_op jit(solution)/shard_map/ppermute | solution.py:34
  46.3 4.3 %collective-permute-start.11 = (bf16[64,128]{1,0:T(8,128)(2,1)S(1)}, bf16[64,128]{1,0:T(8,128)(2,1)S(1)}, u32[]{:S(2)}, u32[]{:S(2)}) collective-permute-start(bf16[64,128]{1,0:T(8,128)(2,1)S(1)} %get-tuple-element.56), channel_id=1, source_target_pairs={{0,6},{1,7},{2,0},{3,1},{4,2},{5,3},{6,4},{7,5},{8,14},{9,15},{10,... | collective-permute-start | bytes 49160 | tf_op jit(solution)/shard_map/ppermute | solution.py:34
  49.9 25.2 %copy-start.4 = (f32[4096]{0:T(1024)S(1)}, f32[4096]{0:T(1024)}, u32[]{:S(2)}) copy-start(f32[4096]{0:T(1024)} %param.26) | copy-start | bytes 49156
  49.9 25.5 %copy-start.5 = (f32[4096]{0:T(1024)S(1)}, f32[4096]{0:T(1024)}, u32[]{:S(2)}) copy-start(f32[4096]{0:T(1024)} %param.22) | copy-start | bytes 49156
  52.2 9.2 %collective-permute-start.12 = (bf16[64,4096]{1,0:T(8,128)(2,1)S(1)}, bf16[64,4096]{1,0:T(8,128)(2,1)S(1)}, u32[]{:S(2)}, u32[]{:S(2)}) collective-permute-start(bf16[64,4096]{1,0:T(8,128)(2,1)S(1)} %get-tuple-element.62), channel_id=1, source_target_pairs={{0,1},{1,0},{2,3},{3,2},{4,5},{5,4},{6,7},{7,6},{8,9},{9,8},{10,11... | collective-permute-start | bytes 1572872 | tf_op jit(solution)/shard_map/ppermute | solution.py:34
  61.6 8.1 %collective-permute-start.13 = (bf16[16,4096]{1,0:T(8,128)(2,1)S(1)}, bf16[16,4096]{1,0:T(8,128)(2,1)S(1)}, u32[]{:S(2)}, u32[]{:S(2)}) collective-permute-start(bf16[16,4096]{1,0:T(8,128)(2,1)S(1)} %get-tuple-element.83), channel_id=1, source_target_pairs={{0,4},{1,5},{2,6},{3,7},{4,0},{5,1},{6,2},{7,3},{8,12},{9,13},{10,... | collective-permute-start | bytes 393224 | tf_op jit(solution)/shard_map/ppermute | solution.py:34
  62.8 7.8 %collective-permute-start.15 = (bf16[16,4096]{1,0:T(8,128)(2,1)S(1)}, bf16[16,4096]{1,0:T(8,128)(2,1)S(1)}, u32[]{:S(2)}, u32[]{:S(2)}) collective-permute-start(bf16[16,4096]{1,0:T(8,128)(2,1)S(1)} %get-tuple-element.84), channel_id=1, source_target_pairs={{0,6},{1,7},{2,0},{3,1},{4,2},{5,3},{6,4},{7,5},{8,14},{9,15},{10,... | collective-permute-start | bytes 393224 | tf_op jit(solution)/shard_map/ppermute | solution.py:34
  65.8 9.3 %collective-permute-start.14 = (bf16[16,4096]{1,0:T(8,128)(2,1)S(1)}, bf16[16,4096]{1,0:T(8,128)(2,1)S(1)}, u32[]{:S(2)}, u32[]{:S(2)}) collective-permute-start(bf16[16,4096]{1,0:T(8,128)(2,1)S(1)} %get-tuple-element.85), channel_id=1, source_target_pairs={{0,2},{1,3},{2,4},{3,5},{4,6},{5,7},{6,0},{7,1},{8,10},{9,11},{10,... | collective-permute-start | bytes 393224 | tf_op jit(solution)/shard_map/ppermute | solution.py:34
  75.5 6.0 %collective-permute-start.21 = (bf16[16,4096]{1,0:T(8,128)(2,1)S(1)}, bf16[16,4096]{1,0:T(8,128)(2,1)S(1)}, u32[]{:S(2)}, u32[]{:S(2)}) collective-permute-start(bf16[16,4096]{1,0:T(8,128)(2,1)S(1)} %multiply_convert_fusion.refs_0_), channel_id=1, source_target_pairs={{0,6},{1,7},{2,0},{3,1},{4,2},{5,3},{6,4},{7,5},{8,14},{9,15},{10,... | collective-permute-start | bytes 393224 | tf_op jit(solution)/shard_map/ppermute | solution.py:34
  79.0 8.7 %collective-permute-start.19 = (bf16[16,4096]{1,0:T(8,128)(2,1)S(1)}, bf16[16,4096]{1,0:T(8,128)(2,1)S(1)}, u32[]{:S(2)}, u32[]{:S(2)}) collective-permute-start(bf16[16,4096]{1,0:T(8,128)(2,1)S(1)} %multiply_convert_fusion.refs_0_), channel_id=1, source_target_pairs={{0,4},{1,5},{2,6},{3,7},{4,0},{5,1},{6,2},{7,3},{8,12},{9,13},{10,... | collective-permute-start | bytes 393224 | tf_op jit(solution)/shard_map/ppermute | solution.py:34
  79.4 8.5 %collective-permute-start.17 = (bf16[16,4096]{1,0:T(8,128)(2,1)S(1)}, bf16[16,4096]{1,0:T(8,128)(2,1)S(1)}, u32[]{:S(2)}, u32[]{:S(2)}) collective-permute-start(bf16[16,4096]{1,0:T(8,128)(2,1)S(1)} %multiply_convert_fusion.refs_0_), channel_id=1, source_target_pairs={{0,2},{1,3},{2,4},{3,5},{4,6},{5,7},{6,0},{7,1},{8,10},{9,11},{10,... | collective-permute-start | bytes 393224 | tf_op jit(solution)/shard_map/ppermute | solution.py:34
  81.3 6.6 %collective-permute-start.16 = (bf16[16,4096]{1,0:T(8,128)(2,1)S(1)}, bf16[16,4096]{1,0:T(8,128)(2,1)S(1)}, u32[]{:S(2)}, u32[]{:S(2)}) collective-permute-start(bf16[16,4096]{1,0:T(8,128)(2,1)S(1)} %multiply_convert_fusion.refs_0_), channel_id=1, source_target_pairs={{0,1},{1,0},{2,3},{3,2},{4,5},{5,4},{6,7},{7,6},{8,9},{9,8},{10,11... | collective-permute-start | bytes 393224 | tf_op jit(solution)/shard_map/ppermute | solution.py:34
  81.5 12.3 %collective-permute-start.22 = (bf16[16,4096]{1,0:T(8,128)(2,1)S(1)}, bf16[16,4096]{1,0:T(8,128)(2,1)S(1)}, u32[]{:S(2)}, u32[]{:S(2)}) collective-permute-start(bf16[16,4096]{1,0:T(8,128)(2,1)S(1)} %collective-permute-done.21.refs_6_), channel_id=1, source_target_pairs={{0,1},{1,0},{2,3},{3,2},{4,5},{5,4},{6,7},{7,6},{8,9},{9,8},{10,11... | collective-permute-start | bytes 393224 | tf_op jit(solution)/shard_map/ppermute | solution.py:34
  87.7 6.4 %collective-permute-start.20 = (bf16[16,4096]{1,0:T(8,128)(2,1)S(1)}, bf16[16,4096]{1,0:T(8,128)(2,1)S(1)}, u32[]{:S(2)}, u32[]{:S(2)}) collective-permute-start(bf16[16,4096]{1,0:T(8,128)(2,1)S(1)} %collective-permute-done.19.refs_4_), channel_id=1, source_target_pairs={{0,1},{1,0},{2,3},{3,2},{4,5},{5,4},{6,7},{7,6},{8,9},{9,8},{10,11... | collective-permute-start | bytes 393224 | tf_op jit(solution)/shard_map/ppermute | solution.py:34
  87.9 9.0 %collective-permute-start.18 = (bf16[16,4096]{1,0:T(8,128)(2,1)S(1)}, bf16[16,4096]{1,0:T(8,128)(2,1)S(1)}, u32[]{:S(2)}, u32[]{:S(2)}) collective-permute-start(bf16[16,4096]{1,0:T(8,128)(2,1)S(1)} %shard_map.149.refs_2_), channel_id=1, source_target_pairs={{0,1},{1,0},{2,3},{3,2},{4,5},{5,4},{6,7},{7,6},{8,9},{9,8},{10,11... | collective-permute-start | bytes 393224 | tf_op jit(solution)/shard_map/ppermute | solution.py:34
  100.5 9.2 %collective-permute-start.23 = (bf16[64,4096]{1,0:T(8,128)(2,1)S(1)}, bf16[64,4096]{1,0:T(8,128)(2,1)S(1)}, u32[]{:S(2)}, u32[]{:S(2)}) collective-permute-start(bf16[64,4096]{1,0:T(8,128)(2,1)S(1)} %get-tuple-element.71), channel_id=1, source_target_pairs={{0,1},{1,0},{2,3},{3,2},{4,5},{5,4},{6,7},{7,6},{8,9},{9,8},{10,11... | collective-permute-start | bytes 1572872 | tf_op jit(solution)/shard_map/ppermute | solution.py:34
  109.9 6.0 %collective-permute-start.24 = (bf16[16,4096]{1,0:T(8,128)(2,1)S(1)}, bf16[16,4096]{1,0:T(8,128)(2,1)S(1)}, u32[]{:S(2)}, u32[]{:S(2)}) collective-permute-start(bf16[16,4096]{1,0:T(8,128)(2,1)S(1)} %get-tuple-element.80), channel_id=1, source_target_pairs={{0,4},{1,5},{2,6},{3,7},{4,0},{5,1},{6,2},{7,3},{8,12},{9,13},{10,... | collective-permute-start | bytes 393224 | tf_op jit(solution)/shard_map/ppermute | solution.py:34
  110.0 6.4 %collective-permute-start.26 = (bf16[16,4096]{1,0:T(8,128)(2,1)S(1)}, bf16[16,4096]{1,0:T(8,128)(2,1)S(1)}, u32[]{:S(2)}, u32[]{:S(2)}) collective-permute-start(bf16[16,4096]{1,0:T(8,128)(2,1)S(1)} %get-tuple-element.81), channel_id=1, source_target_pairs={{0,6},{1,7},{2,0},{3,1},{4,2},{5,3},{6,4},{7,5},{8,14},{9,15},{10,... | collective-permute-start | bytes 393224 | tf_op jit(solution)/shard_map/ppermute | solution.py:34
  111.0 7.7 %collective-permute-start.25 = (bf16[16,4096]{1,0:T(8,128)(2,1)S(1)}, bf16[16,4096]{1,0:T(8,128)(2,1)S(1)}, u32[]{:S(2)}, u32[]{:S(2)}) collective-permute-start(bf16[16,4096]{1,0:T(8,128)(2,1)S(1)} %get-tuple-element.82), channel_id=1, source_target_pairs={{0,2},{1,3},{2,4},{3,5},{4,6},{5,7},{6,0},{7,1},{8,10},{9,11},{10,... | collective-permute-start | bytes 393224 | tf_op jit(solution)/shard_map/ppermute | solution.py:34
  (1 other events, 0.7 us)

commit v13 on v10

--- a/solution.py
+++ b/solution.py
@@ -84,7 +84,11 @@
     shape = ((parts[0].shape[0] // tall * wide, parts[0].shape[1]), bf16)
     crossed = [parts[0]] + [shift(parts[dy], tall, wide, 0, dy) for dy in range(1, wide)]
     packed = kernel_call(functools.partial(pack_body, tall), [shape] * tall, crossed)
-    return [packed[0]] + [shift(packed[dz], tall, wide, dz, 0) for dz in range(1, tall)]
+    pairs = [
+        [(z * wide + y, (z ^ kz) * wide + y) for z in range(tall) for y in range(wide)]
+        for kz in range(tall)
+    ]
+    return [packed[0]] + [lax.ppermute(packed[k], "ctx", pairs[k]) for k in range(1, tall)]
 
 
 def gather_blocks(block, tall, wide):
@@ -95,19 +99,22 @@
     return [blocks[dz, dy] for dz in range(tall) for dy in range(wide)]
 
 
-def sum_order(tall):
+def sum_groups(tall, fine):
     order = [tall // 2, *range(1, tall // 2), *range(tall // 2 + 1, tall), 0]
-    return order[: tall // 2], order[tall // 2 :]
-
-
-def sum_shapes(tall, wide, share, model):
-    kept = [((share, model), bf16)] * tall
-    return kept + [((tall // 2 * share, model), bf16)] * (2 * (wide - 1))
-
-
-def store_parts(parts, tall, wide, span, product, back):
+    half = [order[: tall // 2], order[tall // 2 :]]
+    return [[dz] for dz in half[0]] + half[1:] if fine else half
+
+
+def sum_shapes(tall, wide, share, model, fine):
+    shapes = [((share, model), bf16)] * tall
+    for group in sum_groups(tall, fine):
+        shapes += [((len(group) * share, model), bf16)] * (wide - 1)
+    return shapes
+
+
+def store_parts(parts, tall, wide, span, product, last):
     share = parts[0].shape[0]
-    sign = -1 if back else 1
+    sign = -1 if last else 1
 
     def rows(dz, dy):
         at = sign * dz % tall * wide + sign * dy % wide
@@ -115,36 +122,29 @@
 
     for dz in range(tall):
         parts[dz][:, span] = rows(dz, 0)
-    for dy in range(1, wide):
-        for which, group in enumerate(sum_order(tall)):
-            out = parts[tall + 2 * (dy - 1) + which]
+    for which, group in enumerate(sum_groups(tall, last)):
+        for dy in range(1, wide):
+            out = parts[tall + which * (wide - 1) + dy - 1]
             for place, dz in enumerate(group):
                 out[place * share : (place + 1) * share, span] = rows(dz, dy)
 
 
-def scatter_sum(parts, tall, wide, loads=()):
+def scatter_sum(parts, tall, wide, last, loads=()):
     share = parts[0].shape[0]
+    others = wide - 1
     loaded = []
-    crossed = [shift(p, tall, wide, 0, i // 2 + 1) for i, p in enumerate(parts[tall:])]
+    crossed = [shift(p, tall, wide, 0, i % others + 1) for i, p in enumerate(parts[tall:])]
     if loads:
-        *copy, token = load(parts[0], loads[0])
-        loaded += copy
-        crossed[1] = tie([crossed[1]], [token])
+        *loaded, token = load(parts[0], *loads)
+        crossed[others] = tie([crossed[others]], [token])
     total = None
-    for which, group in enumerate(sum_order(tall)):
+    for which, group in enumerate(sum_groups(tall, last)):
         for place, dz in enumerate(group):
             lane = parts[dz].astype(f32)
-            for dy in range(1, wide):
-                other = crossed[2 * (dy - 1) + which]
+            for other in crossed[which * others : (which + 1) * others]:
                 lane = lane + other[place * share : (place + 1) * share].astype(f32)
             if dz:
-                sent = lane.astype(bf16)
-                lane = shift(sent, tall, wide, dz, 0)
-                if len(loads) > 1 and dz == tall - 1:
-                    *copy, token = load(sent, loads[1])
-                    loaded += copy
-                    lane = tie([lane], [token])
-                lane = lane.astype(f32)
+                lane = shift(lane.astype(bf16), tall, wide, dz, 0).astype(f32)
             total = lane if total is None else total + lane
     return (total, *loaded) if loads else total
 
@@ -250,7 +250,8 @@
         z, y = divmod(s, wide)
         from_block = lax.rem(my_z - z + tall, tall) * wide + lax.rem(my_y - y + wide, wide)
         to_block = lax.rem(z - my_z + tall, tall) * wide + lax.rem(y - my_y + wide, wide)
-        peer = lax.rem(my_z + z, tall) * wide + lax.rem(my_y + y, wide)
+        peer = (my_z ^ z) * wide + lax.rem(my_y + y, wide)
+        lot = (my_z ^ z) * wide + lax.rem(my_y - y + wide, wide)
         before = where < s * tokens
         first = jnp.sum(jnp.where(before, 1.0, 0.0), axis=1, keepdims=True)
         inside = (where < (s + 1) * tokens) & jnp.logical_not(before)
@@ -258,7 +259,7 @@
         slot += jnp.where(inside, lane - first + start, 0.0)
         place += jnp.where(owner == s, (to_block * share).astype(f32), 0.0)
         out_base += jnp.where(out_block == y * tall + z, heads_of(peer).astype(f32), 0.0)
-        in_base += jnp.where(in_source == s, (from_block * (outbound // count)).astype(f32), 0.0)
+        in_base += jnp.where(in_source == s, (lot * (outbound // count)).astype(f32), 0.0)
     mine = owner == iota((count, total), 0)
     earlier = jnp.where(iota((total, total), 0) < iota((total, total), 1), 1.0, 0.0)
     rank = dot(jnp.where(mine, 1.0, 0.0).astype(bf16), earlier.astype(bf16))
@@ -470,15 +471,14 @@
         [normed, w_query, q_cos, q_sin],
         flops=2 * total * model * heads_wide,
     )
-    part_shapes = sum_shapes(tall, wide, share, model)
     attn_parts = kernel_call(
         functools.partial(attend_body, plane, kv_local),
-        part_shapes,
+        sum_shapes(tall, wide, share, model, False),
         [*arrived, query, unmix, k_cos, k_sin, routed, positions, w_output],
         [pltpu.VMEM((total, heads_wide), bf16)],
         flops=2 * total * model * heads_wide,
     )
-    attn_own, w_down = scatter_sum(attn_parts, tall, wide, [w_down])
+    attn_own, w_down = scatter_sum(attn_parts, tall, wide, False, [w_down])
     own_rows = own.astype(f32)
     hidden = own_rows + attn_own
     mean_sq = jnp.mean(hidden * hidden, axis=-1, keepdims=True)
@@ -488,12 +488,12 @@
     hidden_units = w_gate.shape[1]
     mlp_parts = kernel_call(
         functools.partial(mlp_body, plane),
-        part_shapes,
+        sum_shapes(tall, wide, share, model, True),
         [*pieces, w_gate, w_up, w_down],
         [pltpu.VMEM((total, model), bf16), pltpu.VMEM((total, hidden_units), bf16)],
         flops=6 * total * model * hidden_units,
     )
-    mlp_own = scatter_sum(mlp_parts, tall, wide)
+    mlp_own = scatter_sum(mlp_parts, tall, wide, True)
     router_score = jnp.sum(own_rows * w_router[None, :], axis=1, keepdims=True)
     return (own_rows + router_score * (attn_own + mlp_own)).astype(bf16)
 

time: 112 us -> 114 us (1.018)
  waiting for transfers between devices: 36.4 us -> 46.3 us
  starting transfers between devices: 44.9 us -> 36.6 us
    ppermute x29 -> x27, starting transfers between devices: 44.9 us -> 31.7 us  [shift(): return lax.ppermute(block, 'ctx', pairs)]
    ppermute x29 -> x27, waiting for transfers between devices: 36.4 us -> 43.1 us  [shift(): return lax.ppermute(block, 'ctx', pairs)]
    ppermute x0 -> x3, starting transfers between devices: none -> 4.9 us  [exchange(): lax.ppermute(packed[k], 'ctx', pairs[k])]
    ppermute x0 -> x3, waiting for transfers between devices: none -> 3.29 us  [exchange(): lax.ppermute(packed[k], 'ctx', pairs[k])]
  transfers between devices with their start and end apart: 29 -> 30, of which waited for: 17 -> 19; matrix products, arithmetic and copies ran while one was open for 1% -> 1% of each run, Pallas kernels for 16% -> 16%
where the time goes in v13:
time: 114 us
  waiting for transfers between devices  46.3 us (41%)
  starting transfers between devices  36.6 us (32%)
  Pallas kernels  26.2 us (23%)
  local copies, waits for them, and re-layouts  2.23 us (2%)
  other arithmetic  1.9 us (2%)
    ppermute x27, waiting for transfers between devices, shift(): return lax.ppermute(block, 'ctx', pairs)  43.1 us
    ppermute x27, starting transfers between devices, shift(): return lax.ppermute(block, 'ctx', pairs)  31.7 us
    pallas_call x5, Pallas kernels, load(): pl.pallas_call(functools.partial(load_body, len(arrays)), out_shape=[pltp...  15.9 us
    pallas_call x10, Pallas kernels, kernel_call(): pl.pallas_call(body, out_shape=[jax.ShapeDtypeStruct(s, d) for s, d in ou...  10.4 us
    ppermute x3, starting transfers between devices, exchange(): lax.ppermute(packed[k], 'ctx', pairs[k])  4.9 us
    ppermute x3, waiting for transfers between devices, exchange(): lax.ppermute(packed[k], 'ctx', pairs[k])  3.29 us
  transfers between devices with their start and end apart: 30, of which 19 were waited for; matrix products, arithmetic and copies ran while one was open for 1% of the time, Pallas kernels for 16%

profile of v13, /device:TPU:0, one launch (start us, length us, event | category | flops | bytes accessed | tf_op | source)
XLA Modules:
  0.0 113.6 jit_solution(10517754735807671245)
XLA Ops:
  0.0 1.6 %shard_map.136.refs_0_ = bf16[32,4096]{1,0:T(8,128)(2,1)S(1)} custom-call(s32[1]{0:T(128)} %bitcast.me, s32[1,128]{1,0:T(1,128)} %bitcast.4, bf16[128,4096]{1,0:T(8,128)(2,1)} %activations_in.1), custom_call_target="tpu_custom_call" | custom-call | flops 33554432 | bytes 1048576 | tf_op jit(solution)/shard_map/pallas_call | solution.py:165
  1.6 3.1 %collective-permute-start.1 = (bf16[32,4096]{1,0:T(8,128)(2,1)S(1)}, bf16[32,4096]{1,0:T(8,128)(2,1)S(1)}, u32[]{:S(2)}, u32[]{:S(2)}) collective-permute-start(bf16[32,4096]{1,0:T(8,128)(2,1)S(1)} %shard_map.136.refs_0_), channel_id=1, source_target_pairs={{0,2},{1,3},{2,4},{3,5},{4,6},{5,7},{6,0},{7,1},{8,10},{9,11},{10,... | collective-permute-start | bytes 786440 | tf_op jit(solution)/shard_map/ppermute | solution.py:34
  4.6 2.1 %collective-permute-start.4 = (bf16[32,4096]{1,0:T(8,128)(2,1)S(1)}, bf16[32,4096]{1,0:T(8,128)(2,1)S(1)}, u32[]{:S(2)}, u32[]{:S(2)}) collective-permute-start(bf16[32,4096]{1,0:T(8,128)(2,1)S(1)} %shard_map.136.refs_0_), channel_id=1, source_target_pairs={{0,6},{1,7},{2,0},{3,1},{4,2},{5,3},{6,4},{7,5},{8,14},{9,15},{10,... | collective-permute-start | bytes 786440 | tf_op jit(solution)/shard_map/ppermute | solution.py:34
  6.7 1.7 %collective-permute-start = (bf16[32,4096]{1,0:T(8,128)(2,1)S(1)}, bf16[32,4096]{1,0:T(8,128)(2,1)S(1)}, u32[]{:S(2)}, u32[]{:S(2)}) collective-permute-start(bf16[32,4096]{1,0:T(8,128)(2,1)S(1)} %shard_map.136.refs_0_), channel_id=1, source_target_pairs={{0,1},{1,0},{2,3},{3,2},{4,5},{5,4},{6,7},{7,6},{8,9},{9,8},{10,11... | collective-permute-start | bytes 786440 | tf_op jit(solution)/shard_map/ppermute | solution.py:34
  11.5 2.9 %shard_map.137 = (f32[1,4096]{1,0:T(1,128)S(1)}, bf16[4096,128]{1,0:T(8,128)(2,1)S(1)}, bf16[4096,128]{1,0:T(8,128)(2,1)S(1)}, bf16[4096,512]{1,0:T(8,128)(2,1)S(1)}, f32[8,128]{1,0:T(8,128)S(1)}) custom-call(bf16[32,4096]{1,0:T(8,128)(2,1)S(1)} %shard_map.136.refs_0_, f32[1,4096]{1,0:T(1,128)} %bitcast.8, bf16[4096,128]{1,0:T(8,128)(2,1)} %refs_2_.1, ...), custom_call_target="tpu_custom_call" | custom-call | bytes 12615680 | tf_op jit(solution)/shard_map/pallas_call | solution.py:190
  15.1 2.9 %collective-permute-done.4.refs_0_ = bf16[32,4096]{1,0:T(8,128)(2,1)S(1)} collective-permute-done((bf16[32,4096]{1,0:T(8,128)(2,1)S(1)}, bf16[32,4096]{1,0:T(8,128)(2,1)S(1)}, u32[]{:S(2)}, u32[]{:S(2)}) %collective-permute-start.4) | collective-permute-done | bytes 262176 | tf_op jit(solution)/shard_map/ppermute | solution.py:34
  18.0 1.6 %collective-permute-start.6 = (bf16[32,4096]{1,0:T(8,128)(2,1)S(1)}, bf16[32,4096]{1,0:T(8,128)(2,1)S(1)}, u32[]{:S(2)}, u32[]{:S(2)}) collective-permute-start(bf16[32,4096]{1,0:T(8,128)(2,1)S(1)} %shard_map.139.refs_6_), channel_id=1, source_target_pairs={{0,1},{1,0},{2,3},{3,2},{4,5},{5,4},{6,7},{7,6},{8,9},{9,8},{10,11... | collective-permute-start | bytes 786440 | tf_op jit(solution)/shard_map/ppermute | solution.py:34
  21.5 5.8 %collective-permute-done.6.refs_2_.refs_7_ = bf16[32,4096]{1,0:T(8,128)(2,1)S(1)} collective-permute-done((bf16[32,4096]{1,0:T(8,128)(2,1)S(1)}, bf16[32,4096]{1,0:T(8,128)(2,1)S(1)}, u32[]{:S(2)}, u32[]{:S(2)}) %collective-permute-start.6) | collective-permute-done | bytes 262176 | tf_op jit(solution)/shard_map/ppermute | solution.py:34
  27.4 2.3 %collective-permute-done.5.refs_1_ = bf16[32,4096]{1,0:T(8,128)(2,1)S(1)} collective-permute-done((bf16[32,4096]{1,0:T(8,128)(2,1)S(1)}, bf16[32,4096]{1,0:T(8,128)(2,1)S(1)}, u32[]{:S(2)}, u32[]{:S(2)}) %collective-permute-start.5) | collective-permute-done | bytes 262176 | tf_op jit(solution)/shard_map/ppermute | solution.py:34
  30.7 2.2 %shard_map.141 = (bf16[512,4096]{1,0:T(8,128)(2,1)S(1)}, f32[8,128]{1,0:T(8,128)S(1)}) custom-call(bf16[32,4096]{1,0:T(8,128)(2,1)S(1)} %shard_map.140.refs_0_.refs_4_, bf16[512,4096]{1,0:T(8,128)(2,1)} %refs_1_.4), custom_call_target="tpu_custom_call" | custom-call | bytes 8388608 | tf_op jit(solution)/shard_map/pallas_call | solution.py:190
  32.9 3.4 %shard_map.142 = (bf16[4096,1024]{1,0:T(8,128)(2,1)S(1)}, f32[8,128]{1,0:T(8,128)S(1)}) custom-call(bf16[32,4096]{1,0:T(8,128)(2,1)S(1)} %shard_map.140.refs_0_.refs_4_, bf16[4096,1024]{1,0:T(8,128)(2,1)} %refs_1_.5), custom_call_target="tpu_custom_call" | custom-call | bytes 16777216 | tf_op jit(solution)/shard_map/pallas_call | solution.py:190
  37.0 1.8 %shard_map.143 = (bf16[128,4096]{1,0:T(8,128)(2,1)S(1)}, bf16[16,4096]{1,0:T(8,128)(2,1)S(1)}, bf16[128,128]{1,0:T(8,128)(2,1)S(1)}, bf16[128,128]{1,0:T(8,128)(2,1)S(1)}) custom-call(bf16[32,4096]{1,0:T(8,128)(2,1)S(1)} %shard_map.136.refs_0_, bf16[32,4096]{1,0:T(8,128)(2,1)S(1)} %collective-permute-done.refs_3_.refs_1_, ...), custom_call_target="tpu_custom_call" | custom-call | flops 536870912 | bytes 1048576 | tf_op jit(solution)/shard_map/pallas_call | solution.py:165
  38.7 1.6 %collective-permute-start.8 = (bf16[128,128]{1,0:T(8,128)(2,1)S(1)}, bf16[128,128]{1,0:T(8,128)(2,1)S(1)}, u32[]{:S(2)}, u32[]{:S(2)}) collective-permute-start(bf16[128,128]{1,0:T(8,128)(2,1)S(1)} %get-tuple-element.55), channel_id=1, source_target_pairs={{0,1},{1,0},{2,3},{3,2},{4,5},{5,4},{6,7},{7,6},{8,9},{9,8},{10,11... | collective-permute-start | bytes 98312 | tf_op jit(solution)/shard_map/ppermute | solution.py:34
  40.4 2.3 %collective-permute-done.8.refs_1_ = bf16[128,128]{1,0:T(8,128)(2,1)S(1)} collective-permute-done((bf16[128,128]{1,0:T(8,128)(2,1)S(1)}, bf16[128,128]{1,0:T(8,128)(2,1)S(1)}, u32[]{:S(2)}, u32[]{:S(2)}) %collective-permute-start.8) | collective-permute-done | bytes 32800 | tf_op jit(solution)/shard_map/ppermute | solution.py:34
  42.7 2.3 %collective-permute-start.9 = (bf16[64,128]{1,0:T(8,128)(2,1)S(1)}, bf16[64,128]{1,0:T(8,128)(2,1)S(1)}, u32[]{:S(2)}, u32[]{:S(2)}) collective-permute-start(bf16[64,128]{1,0:T(8,128)(2,1)S(1)} %get-tuple-element.57), channel_id=1, source_target_pairs={{0,2},{1,3},{2,0},{3,1},{4,6},{5,7},{6,4},{7,5},{8,10},{9,11},{10,... | collective-permute-start | bytes 49160 | tf_op jit(solution)/shard_map/ppermute | solution.py:91
  49.7 2.1 %collective-permute-done.11.refs_3_ = bf16[64,128]{1,0:T(8,128)(2,1)S(1)} collective-permute-done((bf16[64,128]{1,0:T(8,128)(2,1)S(1)}, bf16[64,128]{1,0:T(8,128)(2,1)S(1)}, u32[]{:S(2)}, u32[]{:S(2)}) %collective-permute-start.11) | collective-permute-done | bytes 16416 | tf_op jit(solution)/shard_map/ppermute | solution.py:91
  51.8 1.7 %shard_map.146 = (bf16[16,4096]{1,0:T(8,128)(2,1)S(1)}, bf16[16,4096]{1,0:T(8,128)(2,1)S(1)}, bf16[16,4096]{1,0:T(8,128)(2,1)S(1)}, bf16[16,4096]{1,0:T(8,128)(2...) custom-call(bf16[64,128]{1,0:T(8,128)(2,1)S(1)} %get-tuple-element.56.refs_0_, ...), custom_call_target="tpu_custom_call" | custom-call | flops 536870912 | bytes 1048576 | tf_op jit(solution)/shard_map/pallas_call | solution.py:165
  54.0 1.5 %collective-permute-start.15 = (bf16[32,4096]{1,0:T(8,128)(2,1)S(1)}, bf16[32,4096]{1,0:T(8,128)(2,1)S(1)}, u32[]{:S(2)}, u32[]{:S(2)}) collective-permute-start(bf16[32,4096]{1,0:T(8,128)(2,1)S(1)} %get-tuple-element.68), channel_id=1, source_target_pairs={{0,1},{1,0},{2,3},{3,2},{4,5},{5,4},{6,7},{7,6},{8,9},{9,8},{10,11... | collective-permute-start | bytes 786440 | tf_op jit(solution)/shard_map/ppermute | solution.py:34
  55.5 3.4 %shard_map.147 = (bf16[1024,4096]{1,0:T(8,128)(2,1)S(1)}, f32[8,128]{1,0:T(8,128)S(1)}) custom-call(bf16[16,4096]{1,0:T(8,128)(2,1)S(1)} %get-tuple-element.69.refs_0_, bf16[1024,4096]{1,0:T(8,128)(2,1)} %refs_1_.6), custom_call_target="tpu_custom_call" | custom-call | bytes 16777216 | tf_op jit(solution)/shard_map/pallas_call | solution.py:190
  60.0 1.9 %collective-permute-start.14 = (bf16[16,4096]{1,0:T(8,128)(2,1)S(1)}, bf16[16,4096]{1,0:T(8,128)(2,1)S(1)}, u32[]{:S(2)}, u32[]{:S(2)}) collective-permute-start(bf16[16,4096]{1,0:T(8,128)(2,1)S(1)} %get-tuple-element.87), channel_id=1, source_target_pairs={{0,2},{1,3},{2,4},{3,5},{4,6},{5,7},{6,0},{7,1},{8,10},{9,11},{10,... | collective-permute-start | bytes 393224 | tf_op jit(solution)/shard_map/ppermute | solution.py:34
  62.8 1.4 %collective-permute-start.16 = (bf16[16,4096]{1,0:T(8,128)(2,1)S(1)}, bf16[16,4096]{1,0:T(8,128)(2,1)S(1)}, u32[]{:S(2)}, u32[]{:S(2)}) collective-permute-start(bf16[16,4096]{1,0:T(8,128)(2,1)S(1)} %add_convert_fusion.3), channel_id=1, source_target_pairs={{0,6},{1,7},{2,0},{3,1},{4,2},{5,3},{6,4},{7,5},{8,14},{9,15},{10,... | collective-permute-start | bytes 393224 | tf_op jit(solution)/shard_map/ppermute | solution.py:34
  64.2 7.4 %collective-permute-done.13 = bf16[16,4096]{1,0:T(8,128)(2,1)S(1)} collective-permute-done((bf16[16,4096]{1,0:T(8,128)(2,1)S(1)}, bf16[16,4096]{1,0:T(8,128)(2,1)S(1)}, u32[]{:S(2)}, u32[]{:S(2)}) %collective-permute-start.13) | collective-permute-done | bytes 131104 | tf_op jit(solution)/shard_map/ppermute | solution.py:34
  73.2 4.5 %collective-permute-start.20 = (bf16[16,4096]{1,0:T(8,128)(2,1)S(1)}, bf16[16,4096]{1,0:T(8,128)(2,1)S(1)}, u32[]{:S(2)}, u32[]{:S(2)}) collective-permute-start(bf16[16,4096]{1,0:T(8,128)(2,1)S(1)} %multiply_convert_fusion.refs_0_), channel_id=1, source_target_pairs={{0,4},{1,5},{2,6},{3,7},{4,0},{5,1},{6,2},{7,3},{8,12},{9,13},{10,... | collective-permute-start | bytes 393224 | tf_op jit(solution)/shard_map/ppermute | solution.py:34
  79.7 5.1 %collective-permute-done.20.refs_4_ = bf16[16,4096]{1,0:T(8,128)(2,1)S(1)} collective-permute-done((bf16[16,4096]{1,0:T(8,128)(2,1)S(1)}, bf16[16,4096]{1,0:T(8,128)(2,1)S(1)}, u32[]{:S(2)}, u32[]{:S(2)}) %collective-permute-start.20) | collective-permute-done | bytes 131104 | tf_op jit(solution)/shard_map/ppermute | solution.py:34
  85.3 1.6 %collective-permute-start.19 = (bf16[16,4096]{1,0:T(8,128)(2,1)S(1)}, bf16[16,4096]{1,0:T(8,128)(2,1)S(1)}, u32[]{:S(2)}, u32[]{:S(2)}) collective-permute-start(bf16[16,4096]{1,0:T(8,128)(2,1)S(1)} %collective-permute-done.18.refs_2_), channel_id=1, source_target_pairs={{0,1},{1,0},{2,3},{3,2},{4,5},{5,4},{6,7},{7,6},{8,9},{9,8},{10,11... | collective-permute-start | bytes 393224 | tf_op jit(solution)/shard_map/ppermute | solution.py:34
  86.9 4.0 %shard_map.149 = (bf16[4096,1024]{1,0:T(8,128)(2,1)S(1)}, f32[8,128]{1,0:T(8,128)}) custom-call(bf16[16,4096]{1,0:T(8,128)(2,1)S(1)} %multiply_convert_fusion.refs_0_, bf16[4096,1024]{1,0:T(8,128)(2,1)} %refs_1_.7), custom_call_target="tpu_custom_call" | custom-call | bytes 16777216 | tf_op jit(solution)/shard_map/pallas_call | solution.py:190
  91.3 2.8 %collective-permute-done.19.refs_3_ = bf16[16,4096]{1,0:T(8,128)(2,1)S(1)} collective-permute-done((bf16[16,4096]{1,0:T(8,128)(2,1)S(1)}, bf16[16,4096]{1,0:T(8,128)(2,1)S(1)}, u32[]{:S(2)}, u32[]{:S(2)}) %collective-permute-start.19) | collective-permute-done | bytes 131104 | tf_op jit(solution)/shard_map/ppermute | solution.py:34
  94.1 3.6 %shard_map.150 = (bf16[16,4096]{1,0:T(8,128)(2,1)S(1)}, bf16[16,4096]{1,0:T(8,128)(2,1)S(1)}, bf16[16,4096]{1,0:T(8,128)(2,1)S(1)}, bf16[16,4096]{1,0:T(8,128)(2...) custom-call(bf16[16,4096]{1,0:T(8,128)(2,1)S(1)} %multiply_convert_fusion.refs_0_,, ...), custom_call_target="tpu_custom_call" | custom-call | flops 3221225472 | bytes 1048576 | tf_op jit(solution)/shard_map/pallas_call | solution.py:165
  98.2 1.6 %collective-permute-start.26 = (bf16[16,4096]{1,0:T(8,128)(2,1)S(1)}, bf16[16,4096]{1,0:T(8,128)(2,1)S(1)}, u32[]{:S(2)}, u32[]{:S(2)}) collective-permute-start(bf16[16,4096]{1,0:T(8,128)(2,1)S(1)} %get-tuple-element.77), channel_id=1, source_target_pairs={{0,1},{1,0},{2,3},{3,2},{4,5},{5,4},{6,7},{7,6},{8,9},{9,8},{10,11... | collective-permute-start | bytes 393224 | tf_op jit(solution)/shard_map/ppermute | solution.py:34
  100.3 2.5 %collective-permute-done.24 = bf16[16,4096]{1,0:T(8,128)(2,1)S(1)} collective-permute-done((bf16[16,4096]{1,0:T(8,128)(2,1)S(1)}, bf16[16,4096]{1,0:T(8,128)(2,1)S(1)}, u32[]{:S(2)}, u32[]{:S(2)}) %collective-permute-start.24) | collective-permute-done | bytes 131104 | tf_op jit(solution)/shard_map/ppermute | solution.py:34
  104.7 2.3 %collective-permute-done.28 = bf16[32,4096]{1,0:T(8,128)(2,1)S(1)} collective-permute-done((bf16[32,4096]{1,0:T(8,128)(2,1)S(1)}, bf16[32,4096]{1,0:T(8,128)(2,1)S(1)}, u32[]{:S(2)}, u32[]{:S(2)}) %collective-permute-start.28) | collective-permute-done | bytes 262176 | tf_op jit(solution)/shard_map/ppermute | solution.py:34
  108.2 3.3 %collective-permute-done.25 = bf16[16,4096]{1,0:T(8,128)(2,1)S(1)} collective-permute-done((bf16[16,4096]{1,0:T(8,128)(2,1)S(1)}, bf16[16,4096]{1,0:T(8,128)(2,1)S(1)}, u32[]{:S(2)}, u32[]{:S(2)}) %collective-permute-start.25) | collective-permute-done | bytes 131104 | tf_op jit(solution)/shard_map/ppermute | solution.py:34
  (69 shorter events, 25.2 us)
Async XLA Ops:
  1.6 12.8 %collective-permute-start.1 = (bf16[32,4096]{1,0:T(8,128)(2,1)S(1)}, bf16[32,4096]{1,0:T(8,128)(2,1)S(1)}, u32[]{:S(2)}, u32[]{:S(2)}) collective-permute-start(bf16[32,4096]{1,0:T(8,128)(2,1)S(1)} %shard_map.136.refs_0_), channel_id=1, source_target_pairs={{0,2},{1,3},{2,4},{3,5},{4,6},{5,7},{6,0},{7,1},{8,10},{9,11},{10,... | collective-permute-start | bytes 786440 | tf_op jit(solution)/shard_map/ppermute | solution.py:34
  4.6 13.4 %collective-permute-start.4 = (bf16[32,4096]{1,0:T(8,128)(2,1)S(1)}, bf16[32,4096]{1,0:T(8,128)(2,1)S(1)}, u32[]{:S(2)}, u32[]{:S(2)}) collective-permute-start(bf16[32,4096]{1,0:T(8,128)(2,1)S(1)} %shard_map.136.refs_0_), channel_id=1, source_target_pairs={{0,6},{1,7},{2,0},{3,1},{4,2},{5,3},{6,4},{7,5},{8,14},{9,15},{10,... | collective-permute-start | bytes 786440 | tf_op jit(solution)/shard_map/ppermute | solution.py:34
  6.7 11.3 %collective-permute-start = (bf16[32,4096]{1,0:T(8,128)(2,1)S(1)}, bf16[32,4096]{1,0:T(8,128)(2,1)S(1)}, u32[]{:S(2)}, u32[]{:S(2)}) collective-permute-start(bf16[32,4096]{1,0:T(8,128)(2,1)S(1)} %shard_map.136.refs_0_), channel_id=1, source_target_pairs={{0,1},{1,0},{2,3},{3,2},{4,5},{5,4},{6,7},{7,6},{8,9},{9,8},{10,11... | collective-permute-start | bytes 786440 | tf_op jit(solution)/shard_map/ppermute | solution.py:34
  14.4 7.1 %collective-permute-start.3 = (bf16[32,4096]{1,0:T(8,128)(2,1)S(1)}, bf16[32,4096]{1,0:T(8,128)(2,1)S(1)}, u32[]{:S(2)}, u32[]{:S(2)}) collective-permute-start(bf16[32,4096]{1,0:T(8,128)(2,1)S(1)} %collective-permute-done.1.refs_2_), channel_id=1, source_target_pairs={{2,4},{3,5},{4,6},{5,7},{10,12},{11,13},{12,14},{13,15},{18,20},{1... | collective-permute-start | bytes 786440 | tf_op jit(solution)/shard_map/ppermute | solution.py:34
  18.0 9.3 %collective-permute-start.6 = (bf16[32,4096]{1,0:T(8,128)(2,1)S(1)}, bf16[32,4096]{1,0:T(8,128)(2,1)S(1)}, u32[]{:S(2)}, u32[]{:S(2)}) collective-permute-start(bf16[32,4096]{1,0:T(8,128)(2,1)S(1)} %shard_map.139.refs_6_), channel_id=1, source_target_pairs={{0,1},{1,0},{2,3},{3,2},{4,5},{5,4},{6,7},{7,6},{8,9},{9,8},{10,11... | collective-permute-start | bytes 786440 | tf_op jit(solution)/shard_map/ppermute | solution.py:34
  19.6 10.0 %collective-permute-start.5 = (bf16[32,4096]{1,0:T(8,128)(2,1)S(1)}, bf16[32,4096]{1,0:T(8,128)(2,1)S(1)}, u32[]{:S(2)}, u32[]{:S(2)}) collective-permute-start(bf16[32,4096]{1,0:T(8,128)(2,1)S(1)} %shard_map.139.refs_6_), channel_id=1, source_target_pairs={{2,0},{3,1},{4,2},{5,3},{10,8},{11,9},{12,10},{13,11},{18,16},{19,... | collective-permute-start | bytes 786440 | tf_op jit(solution)/shard_map/ppermute | solution.py:34
  21.0 15.4 %collective-permute-start.2 = (bf16[32,4096]{1,0:T(8,128)(2,1)S(1)}, bf16[32,4096]{1,0:T(8,128)(2,1)S(1)}, u32[]{:S(2)}, u32[]{:S(2)}) collective-permute-start(bf16[32,4096]{1,0:T(8,128)(2,1)S(1)} %collective-permute-done.1.refs_2_), channel_id=1, source_target_pairs={{0,1},{1,0},{2,3},{3,2},{4,5},{5,4},{6,7},{7,6},{8,9},{9,8},{10,11... | collective-permute-start | bytes 786440 | tf_op jit(solution)/shard_map/ppermute | solution.py:34
  29.7 7.3 %collective-permute-start.7 = (bf16[32,4096]{1,0:T(8,128)(2,1)S(1)}, bf16[32,4096]{1,0:T(8,128)(2,1)S(1)}, u32[]{:S(2)}, u32[]{:S(2)}) collective-permute-start(bf16[32,4096]{1,0:T(8,128)(2,1)S(1)} %shard_map.140.refs_0_.refs_4_), channel_id=1, source_target_pairs={{0,1},{1,0},{2,3},{3,2},{4,5},{5,4},{6,7},{7,6},{8,9},{9,8},{10,11... | collective-permute-start | bytes 786440 | tf_op jit(solution)/shard_map/ppermute | solution.py:34
  38.7 4.0 %collective-permute-start.8 = (bf16[128,128]{1,0:T(8,128)(2,1)S(1)}, bf16[128,128]{1,0:T(8,128)(2,1)S(1)}, u32[]{:S(2)}, u32[]{:S(2)}) collective-permute-start(bf16[128,128]{1,0:T(8,128)(2,1)S(1)} %get-tuple-element.55), channel_id=1, source_target_pairs={{0,1},{1,0},{2,3},{3,2},{4,5},{5,4},{6,7},{7,6},{8,9},{9,8},{10,11... | collective-permute-start | bytes 98312 | tf_op jit(solution)/shard_map/ppermute | solution.py:34
  42.7 5.8 %collective-permute-start.9 = (bf16[64,128]{1,0:T(8,128)(2,1)S(1)}, bf16[64,128]{1,0:T(8,128)(2,1)S(1)}, u32[]{:S(2)}, u32[]{:S(2)}) collective-permute-start(bf16[64,128]{1,0:T(8,128)(2,1)S(1)} %get-tuple-element.57), channel_id=1, source_target_pairs={{0,2},{1,3},{2,0},{3,1},{4,6},{5,7},{6,4},{7,5},{8,10},{9,11},{10,... | collective-permute-start | bytes 49160 | tf_op jit(solution)/shard_map/ppermute | solution.py:91
  45.0 4.7 %collective-permute-start.10 = (bf16[64,128]{1,0:T(8,128)(2,1)S(1)}, bf16[64,128]{1,0:T(8,128)(2,1)S(1)}, u32[]{:S(2)}, u32[]{:S(2)}) collective-permute-start(bf16[64,128]{1,0:T(8,128)(2,1)S(1)} %get-tuple-element.58), channel_id=1, source_target_pairs={{0,4},{1,5},{2,6},{3,7},{4,0},{5,1},{6,2},{7,3},{8,12},{9,13},{10,... | collective-permute-start | bytes 49160 | tf_op jit(solution)/shard_map/ppermute | solution.py:91
  46.2 5.5 %collective-permute-start.11 = (bf16[64,128]{1,0:T(8,128)(2,1)S(1)}, bf16[64,128]{1,0:T(8,128)(2,1)S(1)}, u32[]{:S(2)}, u32[]{:S(2)}) collective-permute-start(bf16[64,128]{1,0:T(8,128)(2,1)S(1)} %get-tuple-element.59), channel_id=1, source_target_pairs={{0,6},{1,7},{2,4},{3,5},{4,2},{5,3},{6,0},{7,1},{8,14},{9,15},{10,... | collective-permute-start | bytes 49160 | tf_op jit(solution)/shard_map/ppermute | solution.py:91
  48.5 23.1 %copy-start.4 = (f32[4096]{0:T(1024)S(1)}, f32[4096]{0:T(1024)}, u32[]{:S(2)}) copy-start(f32[4096]{0:T(1024)} %param.26) | copy-start | bytes 49156
  48.5 23.4 %copy-start.5 = (f32[4096]{0:T(1024)S(1)}, f32[4096]{0:T(1024)}, u32[]{:S(2)}) copy-start(f32[4096]{0:T(1024)} %param.22) | copy-start | bytes 49156
  53.5 6.4 %collective-permute-start.12 = (bf16[32,4096]{1,0:T(8,128)(2,1)S(1)}, bf16[32,4096]{1,0:T(8,128)(2,1)S(1)}, u32[]{:S(2)}, u32[]{:S(2)}) collective-permute-start(bf16[32,4096]{1,0:T(8,128)(2,1)S(1)} %get-tuple-element.65), channel_id=1, source_target_pairs={{0,1},{1,0},{2,3},{3,2},{4,5},{5,4},{6,7},{7,6},{8,9},{9,8},{10,11... | collective-permute-start | bytes 786440 | tf_op jit(solution)/shard_map/ppermute | solution.py:34
  54.0 8.7 %collective-permute-start.15 = (bf16[32,4096]{1,0:T(8,128)(2,1)S(1)}, bf16[32,4096]{1,0:T(8,128)(2,1)S(1)}, u32[]{:S(2)}, u32[]{:S(2)}) collective-permute-start(bf16[32,4096]{1,0:T(8,128)(2,1)S(1)} %get-tuple-element.68), channel_id=1, source_target_pairs={{0,1},{1,0},{2,3},{3,2},{4,5},{5,4},{6,7},{7,6},{8,9},{9,8},{10,11... | collective-permute-start | bytes 786440 | tf_op jit(solution)/shard_map/ppermute | solution.py:34
  60.0 11.6 %collective-permute-start.13 = (bf16[16,4096]{1,0:T(8,128)(2,1)S(1)}, bf16[16,4096]{1,0:T(8,128)(2,1)S(1)}, u32[]{:S(2)}, u32[]{:S(2)}) collective-permute-start(bf16[16,4096]{1,0:T(8,128)(2,1)S(1)} %get-tuple-element.86), channel_id=1, source_target_pairs={{0,4},{1,5},{2,6},{3,7},{4,0},{5,1},{6,2},{7,3},{8,12},{9,13},{10,... | collective-permute-start | bytes 393224 | tf_op jit(solution)/shard_map/ppermute | solution.py:34
  60.0 11.5 %collective-permute-start.14 = (bf16[16,4096]{1,0:T(8,128)(2,1)S(1)}, bf16[16,4096]{1,0:T(8,128)(2,1)S(1)}, u32[]{:S(2)}, u32[]{:S(2)}) collective-permute-start(bf16[16,4096]{1,0:T(8,128)(2,1)S(1)} %get-tuple-element.87), channel_id=1, source_target_pairs={{0,2},{1,3},{2,4},{3,5},{4,6},{5,7},{6,0},{7,1},{8,10},{9,11},{10,... | collective-permute-start | bytes 393224 | tf_op jit(solution)/shard_map/ppermute | solution.py:34
  62.8 8.8 %collective-permute-start.16 = (bf16[16,4096]{1,0:T(8,128)(2,1)S(1)}, bf16[16,4096]{1,0:T(8,128)(2,1)S(1)}, u32[]{:S(2)}, u32[]{:S(2)}) collective-permute-start(bf16[16,4096]{1,0:T(8,128)(2,1)S(1)} %add_convert_fusion.3), channel_id=1, source_target_pairs={{0,6},{1,7},{2,0},{3,1},{4,2},{5,3},{6,4},{7,5},{8,14},{9,15},{10,... | collective-permute-start | bytes 393224 | tf_op jit(solution)/shard_map/ppermute | solution.py:34
  72.0 7.2 %collective-permute-start.22 = (bf16[16,4096]{1,0:T(8,128)(2,1)S(1)}, bf16[16,4096]{1,0:T(8,128)(2,1)S(1)}, u32[]{:S(2)}, u32[]{:S(2)}) collective-permute-start(bf16[16,4096]{1,0:T(8,128)(2,1)S(1)} %multiply_convert_fusion.refs_0_), channel_id=1, source_target_pairs={{0,6},{1,7},{2,0},{3,1},{4,2},{5,3},{6,4},{7,5},{8,14},{9,15},{10,... | collective-permute-start | bytes 393224 | tf_op jit(solution)/shard_map/ppermute | solution.py:34
  73.2 11.7 %collective-permute-start.20 = (bf16[16,4096]{1,0:T(8,128)(2,1)S(1)}, bf16[16,4096]{1,0:T(8,128)(2,1)S(1)}, u32[]{:S(2)}, u32[]{:S(2)}) collective-permute-start(bf16[16,4096]{1,0:T(8,128)(2,1)S(1)} %multiply_convert_fusion.refs_0_), channel_id=1, source_target_pairs={{0,4},{1,5},{2,6},{3,7},{4,0},{5,1},{6,2},{7,3},{8,12},{9,13},{10,... | collective-permute-start | bytes 393224 | tf_op jit(solution)/shard_map/ppermute | solution.py:34
  77.7 7.6 %collective-permute-start.18 = (bf16[16,4096]{1,0:T(8,128)(2,1)S(1)}, bf16[16,4096]{1,0:T(8,128)(2,1)S(1)}, u32[]{:S(2)}, u32[]{:S(2)}) collective-permute-start(bf16[16,4096]{1,0:T(8,128)(2,1)S(1)} %multiply_convert_fusion.refs_0_), channel_id=1, source_target_pairs={{0,2},{1,3},{2,4},{3,5},{4,6},{5,7},{6,0},{7,1},{8,10},{9,11},{10,... | collective-permute-start | bytes 393224 | tf_op jit(solution)/shard_map/ppermute | solution.py:34
  77.7 13.2 %collective-permute-start.17 = (bf16[16,4096]{1,0:T(8,128)(2,1)S(1)}, bf16[16,4096]{1,0:T(8,128)(2,1)S(1)}, u32[]{:S(2)}, u32[]{:S(2)}) collective-permute-start(bf16[16,4096]{1,0:T(8,128)(2,1)S(1)} %multiply_convert_fusion.refs_0_), channel_id=1, source_target_pairs={{0,1},{1,0},{2,3},{3,2},{4,5},{5,4},{6,7},{7,6},{8,9},{9,8},{10,11... | collective-permute-start | bytes 393224 | tf_op jit(solution)/shard_map/ppermute | solution.py:34
  79.2 11.7 %collective-permute-start.23 = (bf16[16,4096]{1,0:T(8,128)(2,1)S(1)}, bf16[16,4096]{1,0:T(8,128)(2,1)S(1)}, u32[]{:S(2)}, u32[]{:S(2)}) collective-permute-start(bf16[16,4096]{1,0:T(8,128)(2,1)S(1)} %collective-permute-done.22.refs_6_), channel_id=1, source_target_pairs={{0,1},{1,0},{2,3},{3,2},{4,5},{5,4},{6,7},{7,6},{8,9},{9,8},{10,11... | collective-permute-start | bytes 393224 | tf_op jit(solution)/shard_map/ppermute | solution.py:34
  84.9 6.4 %collective-permute-start.21 = (bf16[16,4096]{1,0:T(8,128)(2,1)S(1)}, bf16[16,4096]{1,0:T(8,128)(2,1)S(1)}, u32[]{:S(2)}, u32[]{:S(2)}) collective-permute-start(bf16[16,4096]{1,0:T(8,128)(2,1)S(1)} %collective-permute-done.20.refs_4_), channel_id=1, source_target_pairs={{0,1},{1,0},{2,3},{3,2},{4,5},{5,4},{6,7},{7,6},{8,9},{9,8},{10,11... | collective-permute-start | bytes 393224 | tf_op jit(solution)/shard_map/ppermute | solution.py:34
  85.3 8.8 %collective-permute-start.19 = (bf16[16,4096]{1,0:T(8,128)(2,1)S(1)}, bf16[16,4096]{1,0:T(8,128)(2,1)S(1)}, u32[]{:S(2)}, u32[]{:S(2)}) collective-permute-start(bf16[16,4096]{1,0:T(8,128)(2,1)S(1)} %collective-permute-done.18.refs_2_), channel_id=1, source_target_pairs={{0,1},{1,0},{2,3},{3,2},{4,5},{5,4},{6,7},{7,6},{8,9},{9,8},{10,11... | collective-permute-start | bytes 393224 | tf_op jit(solution)/shard_map/ppermute | solution.py:34
  97.7 5.0 %collective-permute-start.24 = (bf16[16,4096]{1,0:T(8,128)(2,1)S(1)}, bf16[16,4096]{1,0:T(8,128)(2,1)S(1)}, u32[]{:S(2)}, u32[]{:S(2)}) collective-permute-start(bf16[16,4096]{1,0:T(8,128)(2,1)S(1)} %get-tuple-element.75), channel_id=1, source_target_pairs={{0,1},{1,0},{2,3},{3,2},{4,5},{5,4},{6,7},{7,6},{8,9},{9,8},{10,11... | collective-permute-start | bytes 393224 | tf_op jit(solution)/shard_map/ppermute | solution.py:34
  98.2 5.9 %collective-permute-start.26 = (bf16[16,4096]{1,0:T(8,128)(2,1)S(1)}, bf16[16,4096]{1,0:T(8,128)(2,1)S(1)}, u32[]{:S(2)}, u32[]{:S(2)}) collective-permute-start(bf16[16,4096]{1,0:T(8,128)(2,1)S(1)} %get-tuple-element.77), channel_id=1, source_target_pairs={{0,1},{1,0},{2,3},{3,2},{4,5},{5,4},{6,7},{7,6},{8,9},{9,8},{10,11... | collective-permute-start | bytes 393224 | tf_op jit(solution)/shard_map/ppermute | solution.py:34
  99.8 7.2 %collective-permute-start.28 = (bf16[32,4096]{1,0:T(8,128)(2,1)S(1)}, bf16[32,4096]{1,0:T(8,128)(2,1)S(1)}, u32[]{:S(2)}, u32[]{:S(2)}) collective-permute-start(bf16[32,4096]{1,0:T(8,128)(2,1)S(1)} %get-tuple-element.79), channel_id=1, source_target_pairs={{0,1},{1,0},{2,3},{3,2},{4,5},{5,4},{6,7},{7,6},{8,9},{9,8},{10,11... | collective-permute-start | bytes 786440 | tf_op jit(solution)/shard_map/ppermute | solution.py:34
  102.8 8.7 %collective-permute-start.25 = (bf16[16,4096]{1,0:T(8,128)(2,1)S(1)}, bf16[16,4096]{1,0:T(8,128)(2,1)S(1)}, u32[]{:S(2)}, u32[]{:S(2)}) collective-permute-start(bf16[16,4096]{1,0:T(8,128)(2,1)S(1)} %add_convert_fusion.2), channel_id=1, source_target_pairs={{0,4},{1,5},{2,6},{3,7},{4,0},{5,1},{6,2},{7,3},{8,12},{9,13},{10,... | collective-permute-start | bytes 393224 | tf_op jit(solution)/shard_map/ppermute | solution.py:34
  104.2 7.3 %collective-permute-start.27 = (bf16[16,4096]{1,0:T(8,128)(2,1)S(1)}, bf16[16,4096]{1,0:T(8,128)(2,1)S(1)}, u32[]{:S(2)}, u32[]{:S(2)}) collective-permute-start(bf16[16,4096]{1,0:T(8,128)(2,1)S(1)} %add_convert_fusion.1), channel_id=1, source_target_pairs={{0,2},{1,3},{2,4},{3,5},{4,6},{5,7},{6,0},{7,1},{8,10},{9,11},{10,... | collective-permute-start | bytes 393224 | tf_op jit(solution)/shard_map/ppermute | solution.py:34
  107.0 5.8 %collective-permute-start.29 = (bf16[16,4096]{1,0:T(8,128)(2,1)S(1)}, bf16[16,4096]{1,0:T(8,128)(2,1)S(1)}, u32[]{:S(2)}, u32[]{:S(2)}) collective-permute-start(bf16[16,4096]{1,0:T(8,128)(2,1)S(1)} %add_convert_fusion), channel_id=1, source_target_pairs={{0,6},{1,7},{2,0},{3,1},{4,2},{5,3},{6,4},{7,5},{8,14},{9,15},{10,... | collective-permute-start | bytes 393224 | tf_op jit(solution)/shard_map/ppermute | solution.py:34
  (4 other events, 23.1 us)

commit v14 on v10

--- a/solution.py
+++ b/solution.py
@@ -50,26 +50,51 @@
     )[0]
 
 
+def lots_of(tall):
+    return 5 if tall == 4 else tall
+
+
+def lot_of(tall, my_z, z):
+    if tall != 4:
+        return lax.rem(my_z - z + tall, tall)
+    ahead = z - my_z
+    far = jnp.maximum(2 * jnp.abs(ahead) - 2, 0)
+    return jnp.where(ahead == -1, 1, jnp.where(ahead == 1, 3, far))
+
+
+def send(block, wide, moves, ky=0):
+    pairs = [(a * wide + y, b * wide + (y + ky) % wide) for a, b in moves for y in range(wide)]
+    return lax.ppermute(block, "ctx", pairs)
+
+
 def gather_rows(block, tall, wide, tokens):
     blocks = {(0, 0): block}
-    for dy in range(1, wide):
+    across = range(1, wide)
+    for dy in across:
         blocks[0, dy] = shift(block, tall, wide, 0, dy)
-    first = [*tokens, *(blocks[0, dy] for dy in range(1, wide))]
-    for dz in range(tall - 1, 0, -1):
-        if tall != 4 or dz != 2:
+    first = [*tokens, *(blocks[0, dy] for dy in across)]
+    if tall != 4:
+        for dz in range(1, tall):
             blocks[dz, 0] = shift(block, tall, wide, dz, 0)
-    blocks[tall - 1, 0] = tie([blocks[tall - 1, 0]], first)
-    if tall == 4:
-        for dy in range(1, wide):
-            blocks[3, dy] = shift(blocks[3, 0], tall, wide, 0, dy)
-        up = shift(blocks[1, 0], tall, wide, 1, 0, lambda z: z in (1, 2))
-        down = shift(blocks[3, 0], tall, wide, -1, 0, lambda z: z in (1, 2))
-        blocks[2, 0] = tie([up, down], [blocks[3, dy] for dy in range(1, wide)])
-    for dz in range(1, tall):
-        for dy in range(1, wide):
-            if (dz, dy) not in blocks:
+        blocks[1, 0] = tie([blocks[1, 0]], first)
+        for dz in range(1, tall):
+            for dy in across:
                 blocks[dz, dy] = shift(blocks[dz, 0], tall, wide, 0, dy)
-    return [blocks[dz, dy] for dz in range(tall) for dy in range(wide)]
+    else:
+        blocks[1, 0] = send(block, wide, [(0, 1), (1, 2), (2, 3)])
+        blocks[3, 0] = tie([send(block, wide, [(1, 0), (2, 1), (3, 2)])], first)
+        for dy in across:
+            blocks[3, dy] = send(blocks[3, 0], wide, [(0, 0), (1, 1), (2, 2)], dy)
+        down = send(blocks[3, 0], wide, [(1, 0), (2, 1)])
+        for dy in across:
+            blocks[1, dy] = send(blocks[1, 0], wide, [(1, 1), (2, 2), (3, 3)], dy)
+        up = send(blocks[1, 0], wide, [(1, 2), (2, 3)])
+        blocks[4, 0] = send(tie([block], [blocks[1, 0]]), wide, [(0, 3), (3, 0)])
+        blocks[2, 0] = tie([up, down], [blocks[3, dy] for dy in across])
+        for dy in across:
+            blocks[2, dy] = shift(blocks[2, 0], tall, wide, 0, dy)
+            blocks[4, dy] = send(blocks[4, 0], wide, [(0, 0), (3, 3)], dy)
+    return [blocks[lot, dy] for lot in range(lots_of(tall)) for dy in range(wide)]
 
 
 def pack_body(tall, *refs):
@@ -238,7 +263,7 @@
 def map_body(tall, wide, tokens, heads_of, me, routed, balance, notes, *outs):
     pick_rows, in_order, columns, unmix, positions = outs
     count, total = tall * wide, routed.shape[1]
-    share, capacity = total // count, pick_rows.shape[1] // count
+    share, capacity = total // count, pick_rows.shape[1] // (lots_of(tall) * wide)
     outbound, inbound = columns.shape[0], unmix.shape[0]
     my_z, my_y = lax.div(me[0], wide), lax.rem(me[0], wide)
     where, owner = routed[...].astype(f32), balance[...].astype(f32)
@@ -254,7 +279,8 @@
         before = where < s * tokens
         first = jnp.sum(jnp.where(before, 1.0, 0.0), axis=1, keepdims=True)
         inside = (where < (s + 1) * tokens) & jnp.logical_not(before)
-        start = (from_block * capacity).astype(f32)
+        lot = lot_of(tall, my_z, z) * wide + lax.rem(my_y - y + wide, wide)
+        start = (lot * capacity).astype(f32)
         slot += jnp.where(inside, lane - first + start, 0.0)
         place += jnp.where(owner == s, (to_block * share).astype(f32), 0.0)
         out_base += jnp.where(out_block == y * tall + z, heads_of(peer).astype(f32), 0.0)
@@ -430,7 +456,7 @@
             map_body, tall, wide, tokens, lambda peer: lax.div(peer * local_heads, group_size)
         ),
         [
-            ((total, count * capacity), bf16),
+            ((total, lots_of(tall) * wide * capacity), bf16),
             ((total, total), bf16),
             ((count * each, 2 * key_cols), bf16),
             ((2 * kv_local * HEAD_DIM, count * each), bf16),
@@ -440,7 +466,7 @@
         specs=[scalar, VMEM, VMEM, VMEM],
     )
     blocks = gather_rows(outgoing, tall, wide, [token_1, positions])
-    near = blocks[2 * wide]
+    near = blocks[wide]
     w_output, *token_2 = load(near, w_output)
     w_gate, *token_3 = load(near, w_gate)
     loaded = token_2 + token_3
@@ -456,7 +482,7 @@
     k_cos, k_sin = jnp.cos(k_angles), jnp.sin(k_angles)
 
     normed, own, *sent = kernel_call(
-        functools.partial(kv_body, count, len(loaded)),
+        functools.partial(kv_body, len(blocks), len(loaded)),
         [((total, model), bf16), ((share, model), bf16)] + [((tall * each, total), bf16)] * wide,
         [*blocks, pick_rows, in_order, columns, attn_gain, w_key, w_value, *loaded],
         [pltpu.VMEM((total, model), bf16)],

time: 112 us -> 125 us (1.12)
  waiting for transfers between devices: 36.4 us -> 44.4 us
  starting transfers between devices: 44.9 us -> 49.1 us
    ppermute x0 -> x8, starting transfers between devices: none -> 18.5 us  [send(): return lax.ppermute(block, 'ctx', pairs)]
    ppermute x0 -> x8, waiting for transfers between devices: none -> 14.6 us  [send(): return lax.ppermute(block, 'ctx', pairs)]
    ppermute x29 -> x23, starting transfers between devices: 44.9 us -> 30.6 us  [shift(): return lax.ppermute(block, 'ctx', pairs)]
    ppermute x29 -> x23, waiting for transfers between devices: 36.4 us -> 29.8 us  [shift(): return lax.ppermute(block, 'ctx', pairs)]
    pallas_call x10 -> x11, Pallas kernels: 10.3 us -> 10.6 us  [kernel_call(): pl.pallas_call(body, out_shape=[jax.ShapeDtypeStruct(s, d) for s, d in ou...]
  transfers between devices with their start and end apart: 29 -> 31, of which waited for: 17 -> 17; matrix products, arithmetic and copies ran while one was open for 1% -> 1% of each run, Pallas kernels for 16% -> 14%
where the time goes in v14:
time: 125 us; the launch traced here: 124 us
  starting transfers between devices  49.1 us (39%)
  waiting for transfers between devices  44.4 us (36%)
  Pallas kernels  26.5 us (21%)
  local copies, waits for them, and re-layouts  2.23 us (2%)
  other arithmetic  1.89 us (2%)
    ppermute x23, starting transfers between devices, shift(): return lax.ppermute(block, 'ctx', pairs)  30.6 us
    ppermute x23, waiting for transfers between devices, shift(): return lax.ppermute(block, 'ctx', pairs)  29.8 us
    ppermute x8, starting transfers between devices, send(): return lax.ppermute(block, 'ctx', pairs)  18.5 us
    pallas_call x5, Pallas kernels, load(): pl.pallas_call(functools.partial(load_body, len(arrays)), out_shape=[pltp...  15.9 us
    ppermute x8, waiting for transfers between devices, send(): return lax.ppermute(block, 'ctx', pairs)  14.6 us
    pallas_call x11, Pallas kernels, kernel_call(): pl.pallas_call(body, out_shape=[jax.ShapeDtypeStruct(s, d) for s, d in ou...  10.6 us
  transfers between devices with their start and end apart: 31, of which 17 were waited for; matrix products, arithmetic and copies ran while one was open for 1% of the time, Pallas kernels for 14%

profile of v14, /device:TPU:0, one launch (start us, length us, event | category | flops | bytes accessed | tf_op | source)
XLA Modules:
  0.0 124.5 jit_solution(4244615923930583040)
XLA Ops:
  1.6 4.9 %collective-permute-start.1 = (bf16[32,4096]{1,0:T(8,128)(2,1)S(1)}, bf16[32,4096]{1,0:T(8,128)(2,1)S(1)}, u32[]{:S(2)}, u32[]{:S(2)}) collective-permute-start(bf16[32,4096]{1,0:T(8,128)(2,1)S(1)} %shard_map.136.refs_0_), channel_id=1, source_target_pairs={{0,2},{1,3},{2,4},{3,5},{4,6},{5,7},{8,10},{9,11},{10,12},{11,13},... | collective-permute-start | bytes 786440 | tf_op jit(solution)/shard_map/ppermute | solution.py:67
  12.5 2.9 %shard_map.137 = (f32[1,4096]{1,0:T(1,128)S(1)}, bf16[4096,128]{1,0:T(8,128)(2,1)S(1)}, bf16[4096,128]{1,0:T(8,128)(2,1)S(1)}, bf16[4096,512]{1,0:T(8,128)(2,1)S(1)}, f32[8,128]{1,0:T(8,128)S(1)}) custom-call(bf16[32,4096]{1,0:T(8,128)(2,1)S(1)} %shard_map.136.refs_0_, f32[1,4096]{1,0:T(1,128)} %bitcast.8, bf16[4096,128]{1,0:T(8,128)(2,1)} %refs_2_.1, ...), custom_call_target="tpu_custom_call" | custom-call | bytes 12615680 | tf_op jit(solution)/shard_map/pallas_call | solution.py:215
  16.2 3.4 %collective-permute-start.6 = (bf16[32,4096]{1,0:T(8,128)(2,1)S(1)}, bf16[32,4096]{1,0:T(8,128)(2,1)S(1)}, u32[]{:S(2)}, u32[]{:S(2)}) collective-permute-start(bf16[32,4096]{1,0:T(8,128)(2,1)S(1)} %shard_map.139.refs_6_), channel_id=1, source_target_pairs={{0,1},{1,0},{2,3},{3,2},{4,5},{5,4},{8,9},{9,8},{10,11},{11,10},{1... | collective-permute-start | bytes 786440 | tf_op jit(solution)/shard_map/ppermute | solution.py:67
  21.0 3.8 %collective-permute-start.8 = (bf16[32,4096]{1,0:T(8,128)(2,1)S(1)}, bf16[32,4096]{1,0:T(8,128)(2,1)S(1)}, u32[]{:S(2)}, u32[]{:S(2)}) collective-permute-start(bf16[32,4096]{1,0:T(8,128)(2,1)S(1)} %shard_map.141), channel_id=1, source_target_pairs={{0,6},{1,7},{6,0},{7,1},{8,14},{9,15},{14,8},{15,9},{16,22},{17,23... | collective-permute-start | bytes 786440 | tf_op jit(solution)/shard_map/ppermute | solution.py:67
  25.5 10.9 %collective-permute-done.5.refs_1_ = bf16[32,4096]{1,0:T(8,128)(2,1)S(1)} collective-permute-done((bf16[32,4096]{1,0:T(8,128)(2,1)S(1)}, bf16[32,4096]{1,0:T(8,128)(2,1)S(1)}, u32[]{:S(2)}, u32[]{:S(2)}) %collective-permute-start.5) | collective-permute-done | bytes 262176 | tf_op jit(solution)/shard_map/ppermute | solution.py:67
  38.0 2.4 %collective-permute-start.9 = (bf16[32,4096]{1,0:T(8,128)(2,1)S(1)}, bf16[32,4096]{1,0:T(8,128)(2,1)S(1)}, u32[]{:S(2)}, u32[]{:S(2)}) collective-permute-start(bf16[32,4096]{1,0:T(8,128)(2,1)S(1)} %collective-permute-done.8.refs_8_), channel_id=1, source_target_pairs={{0,1},{1,0},{6,7},{7,6},{8,9},{9,8},{14,15},{15,14},{16,17},{17,16... | collective-permute-start | bytes 786440 | tf_op jit(solution)/shard_map/ppermute | solution.py:67
  40.9 2.2 %shard_map.142 = (bf16[512,4096]{1,0:T(8,128)(2,1)S(1)}, f32[8,128]{1,0:T(8,128)S(1)}) custom-call(bf16[32,4096]{1,0:T(8,128)(2,1)S(1)} %collective-permute-done.1.refs_1_.refs_0_.refs_2_, bf16[512,4096]{1,0:T(8,128)(2,1)} %refs_1_.4), custom_call_target="tpu_custom_call" | custom-call | bytes 8388608 | tf_op jit(solution)/shard_map/pallas_call | solution.py:215
  43.1 3.4 %shard_map.143 = (bf16[4096,1024]{1,0:T(8,128)(2,1)S(1)}, f32[8,128]{1,0:T(8,128)S(1)}) custom-call(bf16[32,4096]{1,0:T(8,128)(2,1)S(1)} %collective-permute-done.1.refs_1_.refs_0_.refs_2_, bf16[4096,1024]{1,0:T(8,128)(2,1)} %refs_1_.5), custom_call_target="tpu_custom_call" | custom-call | bytes 16777216 | tf_op jit(solution)/shard_map/pallas_call | solution.py:215
  46.5 3.5 %collective-permute-done.9.refs_9_ = bf16[32,4096]{1,0:T(8,128)(2,1)S(1)} collective-permute-done((bf16[32,4096]{1,0:T(8,128)(2,1)S(1)}, bf16[32,4096]{1,0:T(8,128)(2,1)S(1)}, u32[]{:S(2)}, u32[]{:S(2)}) %collective-permute-start.9) | collective-permute-done | bytes 262176 | tf_op jit(solution)/shard_map/ppermute | solution.py:67
  50.1 2.0 %shard_map.144 = (bf16[128,4096]{1,0:T(8,128)(2,1)S(1)}, bf16[16,4096]{1,0:T(8,128)(2,1)S(1)}, bf16[128,128]{1,0:T(8,128)(2,1)S(1)}, bf16[128,128]{1,0:T(8,128)(2,1)S(1)}) custom-call(bf16[32,4096]{1,0:T(8,128)(2,1)S(1)} %shard_map.136.refs_0_, bf16[32,4096]{1,0:T(8,128)(2,1)S(1)} %collective-permute-done.refs_3_.refs_1_, ...), custom_call_target="tpu_custom_call" | custom-call | flops 536870912 | bytes 1048576 | tf_op jit(solution)/shard_map/pallas_call | solution.py:190
  52.1 1.8 %collective-permute-start.10 = (bf16[128,128]{1,0:T(8,128)(2,1)S(1)}, bf16[128,128]{1,0:T(8,128)(2,1)S(1)}, u32[]{:S(2)}, u32[]{:S(2)}) collective-permute-start(bf16[128,128]{1,0:T(8,128)(2,1)S(1)} %get-tuple-element.54), channel_id=1, source_target_pairs={{0,1},{1,0},{2,3},{3,2},{4,5},{5,4},{6,7},{7,6},{8,9},{9,8},{10,11... | collective-permute-start | bytes 98312 | tf_op jit(solution)/shard_map/ppermute | solution.py:34
  54.0 2.1 %collective-permute-done.10.refs_1_ = bf16[128,128]{1,0:T(8,128)(2,1)S(1)} collective-permute-done((bf16[128,128]{1,0:T(8,128)(2,1)S(1)}, bf16[128,128]{1,0:T(8,128)(2,1)S(1)}, u32[]{:S(2)}, u32[]{:S(2)}) %collective-permute-start.10) | collective-permute-done | bytes 32800 | tf_op jit(solution)/shard_map/ppermute | solution.py:34
  56.3 3.7 %collective-permute-start.13 = (bf16[64,128]{1,0:T(8,128)(2,1)S(1)}, bf16[64,128]{1,0:T(8,128)(2,1)S(1)}, u32[]{:S(2)}, u32[]{:S(2)}) collective-permute-start(bf16[64,128]{1,0:T(8,128)(2,1)S(1)} %get-tuple-element.58), channel_id=1, source_target_pairs={{0,6},{1,7},{2,0},{3,1},{4,2},{5,3},{6,4},{7,5},{8,14},{9,15},{10,... | collective-permute-start | bytes 49160 | tf_op jit(solution)/shard_map/ppermute | solution.py:34
  62.3 1.7 %shard_map.147 = (bf16[16,4096]{1,0:T(8,128)(2,1)S(1)}, bf16[16,4096]{1,0:T(8,128)(2,1)S(1)}, bf16[16,4096]{1,0:T(8,128)(2,1)S(1)}, bf16[16,4096]{1,0:T(8,128)(2...) custom-call(bf16[64,128]{1,0:T(8,128)(2,1)S(1)} %get-tuple-element.55.refs_0_, ...), custom_call_target="tpu_custom_call" | custom-call | flops 536870912 | bytes 1048576 | tf_op jit(solution)/shard_map/pallas_call | solution.py:190
  63.9 1.8 %collective-permute-start.14 = (bf16[32,4096]{1,0:T(8,128)(2,1)S(1)}, bf16[32,4096]{1,0:T(8,128)(2,1)S(1)}, u32[]{:S(2)}, u32[]{:S(2)}) collective-permute-start(bf16[32,4096]{1,0:T(8,128)(2,1)S(1)} %get-tuple-element.64), channel_id=1, source_target_pairs={{0,1},{1,0},{2,3},{3,2},{4,5},{5,4},{6,7},{7,6},{8,9},{9,8},{10,11... | collective-permute-start | bytes 786440 | tf_op jit(solution)/shard_map/ppermute | solution.py:34
  66.0 3.4 %shard_map.148 = (bf16[1024,4096]{1,0:T(8,128)(2,1)S(1)}, f32[8,128]{1,0:T(8,128)S(1)}) custom-call(bf16[16,4096]{1,0:T(8,128)(2,1)S(1)} %get-tuple-element.68.refs_0_, bf16[1024,4096]{1,0:T(8,128)(2,1)} %refs_1_.6), custom_call_target="tpu_custom_call" | custom-call | bytes 16777216 | tf_op jit(solution)/shard_map/pallas_call | solution.py:215
  69.4 2.1 %collective-permute-done.14 = bf16[32,4096]{1,0:T(8,128)(2,1)S(1)} collective-permute-done((bf16[32,4096]{1,0:T(8,128)(2,1)S(1)}, bf16[32,4096]{1,0:T(8,128)(2,1)S(1)}, u32[]{:S(2)}, u32[]{:S(2)}) %collective-permute-start.14) | collective-permute-done | bytes 262176 | tf_op jit(solution)/shard_map/ppermute | solution.py:34
  72.9 2.6 %collective-permute-start.16 = (bf16[16,4096]{1,0:T(8,128)(2,1)S(1)}, bf16[16,4096]{1,0:T(8,128)(2,1)S(1)}, u32[]{:S(2)}, u32[]{:S(2)}) collective-permute-start(bf16[16,4096]{1,0:T(8,128)(2,1)S(1)} %get-tuple-element.87), channel_id=1, source_target_pairs={{0,2},{1,3},{2,4},{3,5},{4,6},{5,7},{6,0},{7,1},{8,10},{9,11},{10,... | collective-permute-start | bytes 393224 | tf_op jit(solution)/shard_map/ppermute | solution.py:34
  75.6 2.2 %collective-permute-start.18 = (bf16[16,4096]{1,0:T(8,128)(2,1)S(1)}, bf16[16,4096]{1,0:T(8,128)(2,1)S(1)}, u32[]{:S(2)}, u32[]{:S(2)}) collective-permute-start(bf16[16,4096]{1,0:T(8,128)(2,1)S(1)} %add_convert_fusion.3), channel_id=1, source_target_pairs={{0,6},{1,7},{2,0},{3,1},{4,2},{5,3},{6,4},{7,5},{8,14},{9,15},{10,... | collective-permute-start | bytes 393224 | tf_op jit(solution)/shard_map/ppermute | solution.py:34
  77.7 2.7 %collective-permute-done.15 = bf16[16,4096]{1,0:T(8,128)(2,1)S(1)} collective-permute-done((bf16[16,4096]{1,0:T(8,128)(2,1)S(1)}, bf16[16,4096]{1,0:T(8,128)(2,1)S(1)}, u32[]{:S(2)}, u32[]{:S(2)}) %collective-permute-start.15) | collective-permute-done | bytes 131104 | tf_op jit(solution)/shard_map/ppermute | solution.py:34
  80.5 2.7 %collective-permute-done.18 = bf16[16,4096]{1,0:T(8,128)(2,1)S(1)} collective-permute-done((bf16[16,4096]{1,0:T(8,128)(2,1)S(1)}, bf16[16,4096]{1,0:T(8,128)(2,1)S(1)}, u32[]{:S(2)}, u32[]{:S(2)}) %collective-permute-start.18) | collective-permute-done | bytes 131104 | tf_op jit(solution)/shard_map/ppermute | solution.py:34
  85.0 3.5 %collective-permute-start.22 = (bf16[16,4096]{1,0:T(8,128)(2,1)S(1)}, bf16[16,4096]{1,0:T(8,128)(2,1)S(1)}, u32[]{:S(2)}, u32[]{:S(2)}) collective-permute-start(bf16[16,4096]{1,0:T(8,128)(2,1)S(1)} %multiply_convert_fusion.refs_0_), channel_id=1, source_target_pairs={{0,4},{1,5},{2,6},{3,7},{4,0},{5,1},{6,2},{7,3},{8,12},{9,13},{10,... | collective-permute-start | bytes 393224 | tf_op jit(solution)/shard_map/ppermute | solution.py:34
  89.2 1.7 %collective-permute-start.19 = (bf16[16,4096]{1,0:T(8,128)(2,1)S(1)}, bf16[16,4096]{1,0:T(8,128)(2,1)S(1)}, u32[]{:S(2)}, u32[]{:S(2)}) collective-permute-start(bf16[16,4096]{1,0:T(8,128)(2,1)S(1)} %multiply_convert_fusion.refs_0_), channel_id=1, source_target_pairs={{0,1},{1,0},{2,3},{3,2},{4,5},{5,4},{6,7},{7,6},{8,9},{9,8},{10,11... | collective-permute-start | bytes 393224 | tf_op jit(solution)/shard_map/ppermute | solution.py:34
  91.7 3.9 %collective-permute-done.22.refs_4_ = bf16[16,4096]{1,0:T(8,128)(2,1)S(1)} collective-permute-done((bf16[16,4096]{1,0:T(8,128)(2,1)S(1)}, bf16[16,4096]{1,0:T(8,128)(2,1)S(1)}, u32[]{:S(2)}, u32[]{:S(2)}) %collective-permute-start.22) | collective-permute-done | bytes 131104 | tf_op jit(solution)/shard_map/ppermute | solution.py:34
  95.7 1.7 %collective-permute-start.23 = (bf16[16,4096]{1,0:T(8,128)(2,1)S(1)}, bf16[16,4096]{1,0:T(8,128)(2,1)S(1)}, u32[]{:S(2)}, u32[]{:S(2)}) collective-permute-start(bf16[16,4096]{1,0:T(8,128)(2,1)S(1)} %collective-permute-done.22.refs_4_), channel_id=1, source_target_pairs={{0,1},{1,0},{2,3},{3,2},{4,5},{5,4},{6,7},{7,6},{8,9},{9,8},{10,11... | collective-permute-start | bytes 393224 | tf_op jit(solution)/shard_map/ppermute | solution.py:34
  97.7 4.0 %shard_map.150 = (bf16[4096,1024]{1,0:T(8,128)(2,1)S(1)}, f32[8,128]{1,0:T(8,128)}) custom-call(bf16[16,4096]{1,0:T(8,128)(2,1)S(1)} %multiply_convert_fusion.refs_0_, bf16[4096,1024]{1,0:T(8,128)(2,1)} %refs_1_.7), custom_call_target="tpu_custom_call" | custom-call | bytes 16777216 | tf_op jit(solution)/shard_map/pallas_call | solution.py:215
  102.0 2.8 %collective-permute-done.21.refs_3_ = bf16[16,4096]{1,0:T(8,128)(2,1)S(1)} collective-permute-done((bf16[16,4096]{1,0:T(8,128)(2,1)S(1)}, bf16[16,4096]{1,0:T(8,128)(2,1)S(1)}, u32[]{:S(2)}, u32[]{:S(2)}) %collective-permute-start.21) | collective-permute-done | bytes 131104 | tf_op jit(solution)/shard_map/ppermute | solution.py:34
  104.8 3.6 %shard_map.151 = (bf16[16,4096]{1,0:T(8,128)(2,1)S(1)}, bf16[16,4096]{1,0:T(8,128)(2,1)S(1)}, bf16[16,4096]{1,0:T(8,128)(2,1)S(1)}, bf16[16,4096]{1,0:T(8,128)(2...) custom-call(bf16[16,4096]{1,0:T(8,128)(2,1)S(1)} %multiply_convert_fusion.refs_0_, ...), custom_call_target="tpu_custom_call" | custom-call | flops 3221225472 | bytes 1048576 | tf_op jit(solution)/shard_map/pallas_call | solution.py:190
  108.4 1.8 %collective-permute-start.26 = (bf16[32,4096]{1,0:T(8,128)(2,1)S(1)}, bf16[32,4096]{1,0:T(8,128)(2,1)S(1)}, u32[]{:S(2)}, u32[]{:S(2)}) collective-permute-start(bf16[32,4096]{1,0:T(8,128)(2,1)S(1)} %get-tuple-element.74), channel_id=1, source_target_pairs={{0,1},{1,0},{2,3},{3,2},{4,5},{5,4},{6,7},{7,6},{8,9},{9,8},{10,11... | collective-permute-start | bytes 786440 | tf_op jit(solution)/shard_map/ppermute | solution.py:34
  110.5 4.3 %collective-permute-done.26 = bf16[32,4096]{1,0:T(8,128)(2,1)S(1)} collective-permute-done((bf16[32,4096]{1,0:T(8,128)(2,1)S(1)}, bf16[32,4096]{1,0:T(8,128)(2,1)S(1)}, u32[]{:S(2)}, u32[]{:S(2)}) %collective-permute-start.26) | collective-permute-done | bytes 262176 | tf_op jit(solution)/shard_map/ppermute | solution.py:34
  115.1 2.6 %collective-permute-done.29 = bf16[32,4096]{1,0:T(8,128)(2,1)S(1)} collective-permute-done((bf16[32,4096]{1,0:T(8,128)(2,1)S(1)}, bf16[32,4096]{1,0:T(8,128)(2,1)S(1)}, u32[]{:S(2)}, u32[]{:S(2)}) %collective-permute-start.29) | collective-permute-done | bytes 262176 | tf_op jit(solution)/shard_map/ppermute | solution.py:34
  119.0 3.4 %collective-permute-done.27 = bf16[16,4096]{1,0:T(8,128)(2,1)S(1)} collective-permute-done((bf16[16,4096]{1,0:T(8,128)(2,1)S(1)}, bf16[16,4096]{1,0:T(8,128)(2,1)S(1)}, u32[]{:S(2)}, u32[]{:S(2)}) %collective-permute-start.27) | collective-permute-done | bytes 131104 | tf_op jit(solution)/shard_map/ppermute | solution.py:34
  (71 shorter events, 24.4 us)
Async XLA Ops:
  0.0 24.7 %copy-start.2 = (s32[128]{0:T(128)S(1)}, s32[128]{0:T(128)}, u32[]{:S(2)}) copy-start(s32[128]{0:T(128)} %param.15) | copy-start | bytes 1540
  1.6 13.8 %collective-permute-start.1 = (bf16[32,4096]{1,0:T(8,128)(2,1)S(1)}, bf16[32,4096]{1,0:T(8,128)(2,1)S(1)}, u32[]{:S(2)}, u32[]{:S(2)}) collective-permute-start(bf16[32,4096]{1,0:T(8,128)(2,1)S(1)} %shard_map.136.refs_0_), channel_id=1, source_target_pairs={{0,2},{1,3},{2,4},{3,5},{4,6},{5,7},{8,10},{9,11},{10,12},{11,13},... | collective-permute-start | bytes 786440 | tf_op jit(solution)/shard_map/ppermute | solution.py:67
  6.5 9.7 %collective-permute-start.4 = (bf16[32,4096]{1,0:T(8,128)(2,1)S(1)}, bf16[32,4096]{1,0:T(8,128)(2,1)S(1)}, u32[]{:S(2)}, u32[]{:S(2)}) collective-permute-start(bf16[32,4096]{1,0:T(8,128)(2,1)S(1)} %shard_map.136.refs_0_), channel_id=1, source_target_pairs={{2,0},{3,1},{4,2},{5,3},{6,4},{7,5},{10,8},{11,9},{12,10},{13,11},... | collective-permute-start | bytes 786440 | tf_op jit(solution)/shard_map/ppermute | solution.py:67
  7.8 8.4 %collective-permute-start = (bf16[32,4096]{1,0:T(8,128)(2,1)S(1)}, bf16[32,4096]{1,0:T(8,128)(2,1)S(1)}, u32[]{:S(2)}, u32[]{:S(2)}) collective-permute-start(bf16[32,4096]{1,0:T(8,128)(2,1)S(1)} %shard_map.136.refs_0_), channel_id=1, source_target_pairs={{0,1},{1,0},{2,3},{3,2},{4,5},{5,4},{6,7},{7,6},{8,9},{9,8},{10,11... | collective-permute-start | bytes 786440 | tf_op jit(solution)/shard_map/ppermute | solution.py:34
  15.4 10.1 %collective-permute-start.3 = (bf16[32,4096]{1,0:T(8,128)(2,1)S(1)}, bf16[32,4096]{1,0:T(8,128)(2,1)S(1)}, u32[]{:S(2)}, u32[]{:S(2)}) collective-permute-start(bf16[32,4096]{1,0:T(8,128)(2,1)S(1)} %collective-permute-done.1.refs_1_.refs_0_.refs_2_), channel_id=1, source_target_pairs={{2,4},{3,5},{4,6},{5,7},{10,12},{11,13},{12,14},{13,15},{18,20},{1... | collective-permute-start | bytes 786440 | tf_op jit(solution)/shard_map/ppermute | solution.py:67
  16.2 9.3 %collective-permute-start.6 = (bf16[32,4096]{1,0:T(8,128)(2,1)S(1)}, bf16[32,4096]{1,0:T(8,128)(2,1)S(1)}, u32[]{:S(2)}, u32[]{:S(2)}) collective-permute-start(bf16[32,4096]{1,0:T(8,128)(2,1)S(1)} %shard_map.139.refs_6_), channel_id=1, source_target_pairs={{0,1},{1,0},{2,3},{3,2},{4,5},{5,4},{8,9},{9,8},{10,11},{11,10},{1... | collective-permute-start | bytes 786440 | tf_op jit(solution)/shard_map/ppermute | solution.py:67
  19.6 16.8 %collective-permute-start.5 = (bf16[32,4096]{1,0:T(8,128)(2,1)S(1)}, bf16[32,4096]{1,0:T(8,128)(2,1)S(1)}, u32[]{:S(2)}, u32[]{:S(2)}) collective-permute-start(bf16[32,4096]{1,0:T(8,128)(2,1)S(1)} %shard_map.139.refs_6_), channel_id=1, source_target_pairs={{2,0},{3,1},{4,2},{5,3},{10,8},{11,9},{12,10},{13,11},{18,16},{19,... | collective-permute-start | bytes 786440 | tf_op jit(solution)/shard_map/ppermute | solution.py:67
  21.0 17.1 %collective-permute-start.8 = (bf16[32,4096]{1,0:T(8,128)(2,1)S(1)}, bf16[32,4096]{1,0:T(8,128)(2,1)S(1)}, u32[]{:S(2)}, u32[]{:S(2)}) collective-permute-start(bf16[32,4096]{1,0:T(8,128)(2,1)S(1)} %shard_map.141), channel_id=1, source_target_pairs={{0,6},{1,7},{6,0},{7,1},{8,14},{9,15},{14,8},{15,9},{16,22},{17,23... | collective-permute-start | bytes 786440 | tf_op jit(solution)/shard_map/ppermute | solution.py:67
  24.8 21.8 %collective-permute-start.2 = (bf16[32,4096]{1,0:T(8,128)(2,1)S(1)}, bf16[32,4096]{1,0:T(8,128)(2,1)S(1)}, u32[]{:S(2)}, u32[]{:S(2)}) collective-permute-start(bf16[32,4096]{1,0:T(8,128)(2,1)S(1)} %collective-permute-done.1.refs_1_.refs_0_.refs_2_), channel_id=1, source_target_pairs={{2,3},{3,2},{4,5},{5,4},{6,7},{7,6},{10,11},{11,10},{12,13},{13,12... | collective-permute-start | bytes 786440 | tf_op jit(solution)/shard_map/ppermute | solution.py:67
  36.5 13.6 %collective-permute-start.7 = (bf16[32,4096]{1,0:T(8,128)(2,1)S(1)}, bf16[32,4096]{1,0:T(8,128)(2,1)S(1)}, u32[]{:S(2)}, u32[]{:S(2)}) collective-permute-start(bf16[32,4096]{1,0:T(8,128)(2,1)S(1)} %shard_map.140.refs_4_), channel_id=1, source_target_pairs={{0,1},{1,0},{2,3},{3,2},{4,5},{5,4},{6,7},{7,6},{8,9},{9,8},{10,11... | collective-permute-start | bytes 786440 | tf_op jit(solution)/shard_map/ppermute | solution.py:34
  38.0 12.0 %collective-permute-start.9 = (bf16[32,4096]{1,0:T(8,128)(2,1)S(1)}, bf16[32,4096]{1,0:T(8,128)(2,1)S(1)}, u32[]{:S(2)}, u32[]{:S(2)}) collective-permute-start(bf16[32,4096]{1,0:T(8,128)(2,1)S(1)} %collective-permute-done.8.refs_8_), channel_id=1, source_target_pairs={{0,1},{1,0},{6,7},{7,6},{8,9},{9,8},{14,15},{15,14},{16,17},{17,16... | collective-permute-start | bytes 786440 | tf_op jit(solution)/shard_map/ppermute | solution.py:67
  52.1 4.0 %collective-permute-start.10 = (bf16[128,128]{1,0:T(8,128)(2,1)S(1)}, bf16[128,128]{1,0:T(8,128)(2,1)S(1)}, u32[]{:S(2)}, u32[]{:S(2)}) collective-permute-start(bf16[128,128]{1,0:T(8,128)(2,1)S(1)} %get-tuple-element.54), channel_id=1, source_target_pairs={{0,1},{1,0},{2,3},{3,2},{4,5},{5,4},{6,7},{7,6},{8,9},{9,8},{10,11... | collective-permute-start | bytes 98312 | tf_op jit(solution)/shard_map/ppermute | solution.py:34
  56.1 5.6 %collective-permute-start.11 = (bf16[64,128]{1,0:T(8,128)(2,1)S(1)}, bf16[64,128]{1,0:T(8,128)(2,1)S(1)}, u32[]{:S(2)}, u32[]{:S(2)}) collective-permute-start(bf16[64,128]{1,0:T(8,128)(2,1)S(1)} %get-tuple-element.56), channel_id=1, source_target_pairs={{0,2},{1,3},{2,4},{3,5},{4,6},{5,7},{6,0},{7,1},{8,10},{9,11},{10,... | collective-permute-start | bytes 49160 | tf_op jit(solution)/shard_map/ppermute | solution.py:34
  56.2 5.5 %collective-permute-start.12 = (bf16[64,128]{1,0:T(8,128)(2,1)S(1)}, bf16[64,128]{1,0:T(8,128)(2,1)S(1)}, u32[]{:S(2)}, u32[]{:S(2)}) collective-permute-start(bf16[64,128]{1,0:T(8,128)(2,1)S(1)} %get-tuple-element.57), channel_id=1, source_target_pairs={{0,4},{1,5},{2,6},{3,7},{4,0},{5,1},{6,2},{7,3},{8,12},{9,13},{10,... | collective-permute-start | bytes 49160 | tf_op jit(solution)/shard_map/ppermute | solution.py:34
  56.3 6.0 %collective-permute-start.13 = (bf16[64,128]{1,0:T(8,128)(2,1)S(1)}, bf16[64,128]{1,0:T(8,128)(2,1)S(1)}, u32[]{:S(2)}, u32[]{:S(2)}) collective-permute-start(bf16[64,128]{1,0:T(8,128)(2,1)S(1)} %get-tuple-element.58), channel_id=1, source_target_pairs={{0,6},{1,7},{2,0},{3,1},{4,2},{5,3},{6,4},{7,5},{8,14},{9,15},{10,... | collective-permute-start | bytes 49160 | tf_op jit(solution)/shard_map/ppermute | solution.py:34
  63.9 7.6 %collective-permute-start.14 = (bf16[32,4096]{1,0:T(8,128)(2,1)S(1)}, bf16[32,4096]{1,0:T(8,128)(2,1)S(1)}, u32[]{:S(2)}, u32[]{:S(2)}) collective-permute-start(bf16[32,4096]{1,0:T(8,128)(2,1)S(1)} %get-tuple-element.64), channel_id=1, source_target_pairs={{0,1},{1,0},{2,3},{3,2},{4,5},{5,4},{6,7},{7,6},{8,9},{9,8},{10,11... | collective-permute-start | bytes 786440 | tf_op jit(solution)/shard_map/ppermute | solution.py:34
  65.8 9.8 %collective-permute-start.17 = (bf16[32,4096]{1,0:T(8,128)(2,1)S(1)}, bf16[32,4096]{1,0:T(8,128)(2,1)S(1)}, u32[]{:S(2)}, u32[]{:S(2)}) collective-permute-start(bf16[32,4096]{1,0:T(8,128)(2,1)S(1)} %get-tuple-element.67), channel_id=1, source_target_pairs={{0,1},{1,0},{2,3},{3,2},{4,5},{5,4},{6,7},{7,6},{8,9},{9,8},{10,11... | collective-permute-start | bytes 786440 | tf_op jit(solution)/shard_map/ppermute | solution.py:34
  71.6 8.8 %collective-permute-start.15 = (bf16[16,4096]{1,0:T(8,128)(2,1)S(1)}, bf16[16,4096]{1,0:T(8,128)(2,1)S(1)}, u32[]{:S(2)}, u32[]{:S(2)}) collective-permute-start(bf16[16,4096]{1,0:T(8,128)(2,1)S(1)} %get-tuple-element.86), channel_id=1, source_target_pairs={{0,4},{1,5},{2,6},{3,7},{4,0},{5,1},{6,2},{7,3},{8,12},{9,13},{10,... | collective-permute-start | bytes 393224 | tf_op jit(solution)/shard_map/ppermute | solution.py:34
  72.9 7.6 %collective-permute-start.16 = (bf16[16,4096]{1,0:T(8,128)(2,1)S(1)}, bf16[16,4096]{1,0:T(8,128)(2,1)S(1)}, u32[]{:S(2)}, u32[]{:S(2)}) collective-permute-start(bf16[16,4096]{1,0:T(8,128)(2,1)S(1)} %get-tuple-element.87), channel_id=1, source_target_pairs={{0,2},{1,3},{2,4},{3,5},{4,6},{5,7},{6,0},{7,1},{8,10},{9,11},{10,... | collective-permute-start | bytes 393224 | tf_op jit(solution)/shard_map/ppermute | solution.py:34
  75.6 7.6 %collective-permute-start.18 = (bf16[16,4096]{1,0:T(8,128)(2,1)S(1)}, bf16[16,4096]{1,0:T(8,128)(2,1)S(1)}, u32[]{:S(2)}, u32[]{:S(2)}) collective-permute-start(bf16[16,4096]{1,0:T(8,128)(2,1)S(1)} %add_convert_fusion.3), channel_id=1, source_target_pairs={{0,6},{1,7},{2,0},{3,1},{4,2},{5,3},{6,4},{7,5},{8,14},{9,15},{10,... | collective-permute-start | bytes 393224 | tf_op jit(solution)/shard_map/ppermute | solution.py:34
  83.5 7.4 %collective-permute-start.24 = (bf16[16,4096]{1,0:T(8,128)(2,1)S(1)}, bf16[16,4096]{1,0:T(8,128)(2,1)S(1)}, u32[]{:S(2)}, u32[]{:S(2)}) collective-permute-start(bf16[16,4096]{1,0:T(8,128)(2,1)S(1)} %multiply_convert_fusion.refs_0_), channel_id=1, source_target_pairs={{0,6},{1,7},{2,0},{3,1},{4,2},{5,3},{6,4},{7,5},{8,14},{9,15},{10,... | collective-permute-start | bytes 393224 | tf_op jit(solution)/shard_map/ppermute | solution.py:34
  85.0 10.6 %collective-permute-start.22 = (bf16[16,4096]{1,0:T(8,128)(2,1)S(1)}, bf16[16,4096]{1,0:T(8,128)(2,1)S(1)}, u32[]{:S(2)}, u32[]{:S(2)}) collective-permute-start(bf16[16,4096]{1,0:T(8,128)(2,1)S(1)} %multiply_convert_fusion.refs_0_), channel_id=1, source_target_pairs={{0,4},{1,5},{2,6},{3,7},{4,0},{5,1},{6,2},{7,3},{8,12},{9,13},{10,... | collective-permute-start | bytes 393224 | tf_op jit(solution)/shard_map/ppermute | solution.py:34
  88.5 8.9 %collective-permute-start.20 = (bf16[16,4096]{1,0:T(8,128)(2,1)S(1)}, bf16[16,4096]{1,0:T(8,128)(2,1)S(1)}, u32[]{:S(2)}, u32[]{:S(2)}) collective-permute-start(bf16[16,4096]{1,0:T(8,128)(2,1)S(1)} %multiply_convert_fusion.refs_0_), channel_id=1, source_target_pairs={{0,2},{1,3},{2,4},{3,5},{4,6},{5,7},{6,0},{7,1},{8,10},{9,11},{10,... | collective-permute-start | bytes 393224 | tf_op jit(solution)/shard_map/ppermute | solution.py:34
  89.2 12.5 %collective-permute-start.19 = (bf16[16,4096]{1,0:T(8,128)(2,1)S(1)}, bf16[16,4096]{1,0:T(8,128)(2,1)S(1)}, u32[]{:S(2)}, u32[]{:S(2)}) collective-permute-start(bf16[16,4096]{1,0:T(8,128)(2,1)S(1)} %multiply_convert_fusion.refs_0_), channel_id=1, source_target_pairs={{0,1},{1,0},{2,3},{3,2},{4,5},{5,4},{6,7},{7,6},{8,9},{9,8},{10,11... | collective-permute-start | bytes 393224 | tf_op jit(solution)/shard_map/ppermute | solution.py:34
  90.9 10.7 %collective-permute-start.25 = (bf16[16,4096]{1,0:T(8,128)(2,1)S(1)}, bf16[16,4096]{1,0:T(8,128)(2,1)S(1)}, u32[]{:S(2)}, u32[]{:S(2)}) collective-permute-start(bf16[16,4096]{1,0:T(8,128)(2,1)S(1)} %collective-permute-done.24.refs_6_), channel_id=1, source_target_pairs={{0,1},{1,0},{2,3},{3,2},{4,5},{5,4},{6,7},{7,6},{8,9},{9,8},{10,11... | collective-permute-start | bytes 393224 | tf_op jit(solution)/shard_map/ppermute | solution.py:34
  95.7 6.4 %collective-permute-start.23 = (bf16[16,4096]{1,0:T(8,128)(2,1)S(1)}, bf16[16,4096]{1,0:T(8,128)(2,1)S(1)}, u32[]{:S(2)}, u32[]{:S(2)}) collective-permute-start(bf16[16,4096]{1,0:T(8,128)(2,1)S(1)} %collective-permute-done.22.refs_4_), channel_id=1, source_target_pairs={{0,1},{1,0},{2,3},{3,2},{4,5},{5,4},{6,7},{7,6},{8,9},{9,8},{10,11... | collective-permute-start | bytes 393224 | tf_op jit(solution)/shard_map/ppermute | solution.py:34
  97.4 7.4 %collective-permute-start.21 = (bf16[16,4096]{1,0:T(8,128)(2,1)S(1)}, bf16[16,4096]{1,0:T(8,128)(2,1)S(1)}, u32[]{:S(2)}, u32[]{:S(2)}) collective-permute-start(bf16[16,4096]{1,0:T(8,128)(2,1)S(1)} %collective-permute-done.20.refs_2_), channel_id=1, source_target_pairs={{0,1},{1,0},{2,3},{3,2},{4,5},{5,4},{6,7},{7,6},{8,9},{9,8},{10,11... | collective-permute-start | bytes 393224 | tf_op jit(solution)/shard_map/ppermute | solution.py:34
  108.4 6.4 %collective-permute-start.26 = (bf16[32,4096]{1,0:T(8,128)(2,1)S(1)}, bf16[32,4096]{1,0:T(8,128)(2,1)S(1)}, u32[]{:S(2)}, u32[]{:S(2)}) collective-permute-start(bf16[32,4096]{1,0:T(8,128)(2,1)S(1)} %get-tuple-element.74), channel_id=1, source_target_pairs={{0,1},{1,0},{2,3},{3,2},{4,5},{5,4},{6,7},{7,6},{8,9},{9,8},{10,11... | collective-permute-start | bytes 786440 | tf_op jit(solution)/shard_map/ppermute | solution.py:34
  110.2 7.4 %collective-permute-start.29 = (bf16[32,4096]{1,0:T(8,128)(2,1)S(1)}, bf16[32,4096]{1,0:T(8,128)(2,1)S(1)}, u32[]{:S(2)}, u32[]{:S(2)}) collective-permute-start(bf16[32,4096]{1,0:T(8,128)(2,1)S(1)} %get-tuple-element.77), channel_id=1, source_target_pairs={{0,1},{1,0},{2,3},{3,2},{4,5},{5,4},{6,7},{7,6},{8,9},{9,8},{10,11... | collective-permute-start | bytes 786440 | tf_op jit(solution)/shard_map/ppermute | solution.py:34
  114.9 7.4 %collective-permute-start.27 = (bf16[16,4096]{1,0:T(8,128)(2,1)S(1)}, bf16[16,4096]{1,0:T(8,128)(2,1)S(1)}, u32[]{:S(2)}, u32[]{:S(2)}) collective-permute-start(bf16[16,4096]{1,0:T(8,128)(2,1)S(1)} %get-tuple-element.84), channel_id=1, source_target_pairs={{0,4},{1,5},{2,6},{3,7},{4,0},{5,1},{6,2},{7,3},{8,12},{9,13},{10,... | collective-permute-start | bytes 393224 | tf_op jit(solution)/shard_map/ppermute | solution.py:34
  115.0 7.4 %collective-permute-start.28 = (bf16[16,4096]{1,0:T(8,128)(2,1)S(1)}, bf16[16,4096]{1,0:T(8,128)(2,1)S(1)}, u32[]{:S(2)}, u32[]{:S(2)}) collective-permute-start(bf16[16,4096]{1,0:T(8,128)(2,1)S(1)} %get-tuple-element.85), channel_id=1, source_target_pairs={{0,2},{1,3},{2,4},{3,5},{4,6},{5,7},{6,0},{7,1},{8,10},{9,11},{10,... | collective-permute-start | bytes 393224 | tf_op jit(solution)/shard_map/ppermute | solution.py:34
  117.7 6.0 %collective-permute-start.30 = (bf16[16,4096]{1,0:T(8,128)(2,1)S(1)}, bf16[16,4096]{1,0:T(8,128)(2,1)S(1)}, u32[]{:S(2)}, u32[]{:S(2)}) collective-permute-start(bf16[16,4096]{1,0:T(8,128)(2,1)S(1)} %add_convert_fusion), channel_id=1, source_target_pairs={{0,6},{1,7},{2,0},{3,1},{4,2},{5,3},{6,4},{7,5},{8,14},{9,15},{10,... | collective-permute-start | bytes 393224 | tf_op jit(solution)/shard_map/ppermute | solution.py:34
  (5 other events, 47.2 us)

commit v15 on v13

--- a/solution.py
+++ b/solution.py
@@ -101,8 +101,7 @@
 
 def sum_groups(tall, fine):
     order = [tall // 2, *range(1, tall // 2), *range(tall // 2 + 1, tall), 0]
-    half = [order[: tall // 2], order[tall // 2 :]]
-    return [[dz] for dz in half[0]] + half[1:] if fine else half
+    return [[dz] for dz in order] if fine else [order[: tall // 2], order[tall // 2 :]]
 
 
 def sum_shapes(tall, wide, share, model, fine):
@@ -214,9 +213,15 @@
 
 def send_body(me, routed_in, activations_in, outgoing, routed, activations, sems):
     first_move = pltpu.make_async_copy(routed_in, routed, sems.at[0])
-    second_move = pltpu.make_async_copy(activations_in, activations, sems.at[1])
     first_move.start()
-    second_move.start()
+    width = activations.shape[1]
+    tile = width // 4
+    moves = []
+    for index in range(4):
+        piece = pl.ds(index * tile, tile)
+        source, target = activations_in.at[:, piece], activations.at[:, piece]
+        moves.append(pltpu.make_async_copy(source, target, sems.at[1 + index]))
+        moves[-1].start()
     first_move.wait()
     capacity, tokens, total = outgoing.shape[0], activations.shape[0], routed.shape[1]
     low = (me[0] * tokens).astype(f32)
@@ -227,11 +232,9 @@
     hit = slot == iota((capacity, total), 0)
     token = jnp.sum(jnp.where(hit, where - low + 1.0, 0.0), axis=1, keepdims=True) - 1.0
     onehot = jnp.where(token == iota((capacity, tokens), 1), 1.0, 0.0).astype(bf16)
-    second_move.wait()
-    width = activations.shape[1]
-    tile = tile_of(width, 1024)
-    for start in range(0, width, tile):
-        span = slice(start, start + tile)
+    for index, move in enumerate(moves):
+        move.wait()
+        span = slice(index * tile, (index + 1) * tile)
         outgoing[:, span] = pick(onehot, activations[:, span])
 
 
@@ -409,7 +412,7 @@
         [
             pltpu.VMEM(routed.shape, i32),
             pltpu.VMEM(activations.shape, bf16),
-            pltpu.SemaphoreType.DMA((2,)),
+            pltpu.SemaphoreType.DMA((5,)),
         ],
         specs=[scalar, in_hbm, in_hbm],
         flops=2 * capacity * tokens * model,

time: 114 us -> 114 us (level)
  starting transfers between devices: 36.6 us -> 39.5 us
  waiting for transfers between devices: 46.3 us -> 43.4 us
    ppermute x27 -> x28, waiting for transfers between devices: 43.1 us -> 40.1 us  [shift(): return lax.ppermute(block, 'ctx', pairs)]
    ppermute x27 -> x28, starting transfers between devices: 31.7 us -> 34.6 us  [shift(): return lax.ppermute(block, 'ctx', pairs)]
  transfers between devices with their start and end apart: 30 -> 31, of which waited for: 19 -> 19; matrix products, arithmetic and copies ran while one was open for 1% -> 1% of each run, Pallas kernels for 16% -> 15%
where the time goes in v15:
time: 114 us
  waiting for transfers between devices  43.4 us (38%)
  starting transfers between devices  39.5 us (35%)
  Pallas kernels  26.3 us (23%)
  local copies, waits for them, and re-layouts  2.23 us (2%)
  other arithmetic  1.9 us (2%)
    ppermute x28, waiting for transfers between devices, shift(): return lax.ppermute(block, 'ctx', pairs)  40.1 us
    ppermute x28, starting transfers between devices, shift(): return lax.ppermute(block, 'ctx', pairs)  34.6 us
    pallas_call x5, Pallas kernels, load(): pl.pallas_call(functools.partial(load_body, len(arrays)), out_shape=[pltp...  15.9 us
    pallas_call x10, Pallas kernels, kernel_call(): pl.pallas_call(body, out_shape=[jax.ShapeDtypeStruct(s, d) for s, d in ou...  10.5 us
    ppermute x3, starting transfers between devices, exchange(): lax.ppermute(packed[k], 'ctx', pairs[k])  4.9 us
    ppermute x3, waiting for transfers between devices, exchange(): lax.ppermute(packed[k], 'ctx', pairs[k])  3.29 us
  transfers between devices with their start and end apart: 31, of which 19 were waited for; matrix products, arithmetic and copies ran while one was open for 1% of the time, Pallas kernels for 15%

profile of v15, /device:TPU:0, one launch (start us, length us, event | category | flops | bytes accessed | tf_op | source)
XLA Modules:
  0.0 113.7 jit_solution(4121976382480437793)
XLA Ops:
  0.0 1.7 %shard_map.136.refs_0_ = bf16[32,4096]{1,0:T(8,128)(2,1)S(1)} custom-call(s32[1]{0:T(128)} %bitcast.me, s32[1,128]{1,0:T(1,128)} %bitcast.4, bf16[128,4096]{1,0:T(8,128)(2,1)} %activations_in.1), custom_call_target="tpu_custom_call" | custom-call | flops 33554432 | bytes 1048576 | tf_op jit(solution)/shard_map/pallas_call | solution.py:164
  1.7 3.1 %collective-permute-start.1 = (bf16[32,4096]{1,0:T(8,128)(2,1)S(1)}, bf16[32,4096]{1,0:T(8,128)(2,1)S(1)}, u32[]{:S(2)}, u32[]{:S(2)}) collective-permute-start(bf16[32,4096]{1,0:T(8,128)(2,1)S(1)} %shard_map.136.refs_0_), channel_id=1, source_target_pairs={{0,2},{1,3},{2,4},{3,5},{4,6},{5,7},{6,0},{7,1},{8,10},{9,11},{10,... | collective-permute-start | bytes 786440 | tf_op jit(solution)/shard_map/ppermute | solution.py:34
  4.8 2.1 %collective-permute-start.4 = (bf16[32,4096]{1,0:T(8,128)(2,1)S(1)}, bf16[32,4096]{1,0:T(8,128)(2,1)S(1)}, u32[]{:S(2)}, u32[]{:S(2)}) collective-permute-start(bf16[32,4096]{1,0:T(8,128)(2,1)S(1)} %shard_map.136.refs_0_), channel_id=1, source_target_pairs={{0,6},{1,7},{2,0},{3,1},{4,2},{5,3},{6,4},{7,5},{8,14},{9,15},{10,... | collective-permute-start | bytes 786440 | tf_op jit(solution)/shard_map/ppermute | solution.py:34
  6.9 1.7 %collective-permute-start = (bf16[32,4096]{1,0:T(8,128)(2,1)S(1)}, bf16[32,4096]{1,0:T(8,128)(2,1)S(1)}, u32[]{:S(2)}, u32[]{:S(2)}) collective-permute-start(bf16[32,4096]{1,0:T(8,128)(2,1)S(1)} %shard_map.136.refs_0_), channel_id=1, source_target_pairs={{0,1},{1,0},{2,3},{3,2},{4,5},{5,4},{6,7},{7,6},{8,9},{9,8},{10,11... | collective-permute-start | bytes 786440 | tf_op jit(solution)/shard_map/ppermute | solution.py:34
  11.6 2.9 %shard_map.137 = (f32[1,4096]{1,0:T(1,128)S(1)}, bf16[4096,128]{1,0:T(8,128)(2,1)S(1)}, bf16[4096,128]{1,0:T(8,128)(2,1)S(1)}, bf16[4096,512]{1,0:T(8,128)(2,1)S(1)}, f32[8,128]{1,0:T(8,128)S(1)}) custom-call(bf16[32,4096]{1,0:T(8,128)(2,1)S(1)} %shard_map.136.refs_0_, f32[1,4096]{1,0:T(1,128)} %bitcast.8, bf16[4096,128]{1,0:T(8,128)(2,1)} %refs_2_.1, ...), custom_call_target="tpu_custom_call" | custom-call | bytes 12615680 | tf_op jit(solution)/shard_map/pallas_call | solution.py:189
  15.2 2.9 %collective-permute-done.4.refs_0_ = bf16[32,4096]{1,0:T(8,128)(2,1)S(1)} collective-permute-done((bf16[32,4096]{1,0:T(8,128)(2,1)S(1)}, bf16[32,4096]{1,0:T(8,128)(2,1)S(1)}, u32[]{:S(2)}, u32[]{:S(2)}) %collective-permute-start.4) | collective-permute-done | bytes 262176 | tf_op jit(solution)/shard_map/ppermute | solution.py:34
  18.2 1.6 %collective-permute-start.6 = (bf16[32,4096]{1,0:T(8,128)(2,1)S(1)}, bf16[32,4096]{1,0:T(8,128)(2,1)S(1)}, u32[]{:S(2)}, u32[]{:S(2)}) collective-permute-start(bf16[32,4096]{1,0:T(8,128)(2,1)S(1)} %shard_map.139.refs_6_), channel_id=1, source_target_pairs={{0,1},{1,0},{2,3},{3,2},{4,5},{5,4},{6,7},{7,6},{8,9},{9,8},{10,11... | collective-permute-start | bytes 786440 | tf_op jit(solution)/shard_map/ppermute | solution.py:34
  21.7 5.8 %collective-permute-done.6.refs_2_.refs_7_ = bf16[32,4096]{1,0:T(8,128)(2,1)S(1)} collective-permute-done((bf16[32,4096]{1,0:T(8,128)(2,1)S(1)}, bf16[32,4096]{1,0:T(8,128)(2,1)S(1)}, u32[]{:S(2)}, u32[]{:S(2)}) %collective-permute-start.6) | collective-permute-done | bytes 262176 | tf_op jit(solution)/shard_map/ppermute | solution.py:34
  27.5 2.3 %collective-permute-done.5.refs_1_ = bf16[32,4096]{1,0:T(8,128)(2,1)S(1)} collective-permute-done((bf16[32,4096]{1,0:T(8,128)(2,1)S(1)}, bf16[32,4096]{1,0:T(8,128)(2,1)S(1)}, u32[]{:S(2)}, u32[]{:S(2)}) %collective-permute-start.5) | collective-permute-done | bytes 262176 | tf_op jit(solution)/shard_map/ppermute | solution.py:34
  30.9 2.2 %shard_map.141 = (bf16[512,4096]{1,0:T(8,128)(2,1)S(1)}, f32[8,128]{1,0:T(8,128)S(1)}) custom-call(bf16[32,4096]{1,0:T(8,128)(2,1)S(1)} %shard_map.140.refs_0_.refs_4_, bf16[512,4096]{1,0:T(8,128)(2,1)} %refs_1_.4), custom_call_target="tpu_custom_call" | custom-call | bytes 8388608 | tf_op jit(solution)/shard_map/pallas_call | solution.py:189
  33.1 3.4 %shard_map.142 = (bf16[4096,1024]{1,0:T(8,128)(2,1)S(1)}, f32[8,128]{1,0:T(8,128)S(1)}) custom-call(bf16[32,4096]{1,0:T(8,128)(2,1)S(1)} %shard_map.140.refs_0_.refs_4_, bf16[4096,1024]{1,0:T(8,128)(2,1)} %refs_1_.5), custom_call_target="tpu_custom_call" | custom-call | bytes 16777216 | tf_op jit(solution)/shard_map/pallas_call | solution.py:189
  37.1 1.8 %shard_map.143 = (bf16[128,4096]{1,0:T(8,128)(2,1)S(1)}, bf16[16,4096]{1,0:T(8,128)(2,1)S(1)}, bf16[128,128]{1,0:T(8,128)(2,1)S(1)}, bf16[128,128]{1,0:T(8,128)(2,1)S(1)}) custom-call(bf16[32,4096]{1,0:T(8,128)(2,1)S(1)} %shard_map.136.refs_0_, bf16[32,4096]{1,0:T(8,128)(2,1)S(1)} %collective-permute-done.refs_3_.refs_1_, ...), custom_call_target="tpu_custom_call" | custom-call | flops 536870912 | bytes 1048576 | tf_op jit(solution)/shard_map/pallas_call | solution.py:164
  38.9 1.6 %collective-permute-start.8 = (bf16[128,128]{1,0:T(8,128)(2,1)S(1)}, bf16[128,128]{1,0:T(8,128)(2,1)S(1)}, u32[]{:S(2)}, u32[]{:S(2)}) collective-permute-start(bf16[128,128]{1,0:T(8,128)(2,1)S(1)} %get-tuple-element.56), channel_id=1, source_target_pairs={{0,1},{1,0},{2,3},{3,2},{4,5},{5,4},{6,7},{7,6},{8,9},{9,8},{10,11... | collective-permute-start | bytes 98312 | tf_op jit(solution)/shard_map/ppermute | solution.py:34
  40.6 2.3 %collective-permute-done.8.refs_1_ = bf16[128,128]{1,0:T(8,128)(2,1)S(1)} collective-permute-done((bf16[128,128]{1,0:T(8,128)(2,1)S(1)}, bf16[128,128]{1,0:T(8,128)(2,1)S(1)}, u32[]{:S(2)}, u32[]{:S(2)}) %collective-permute-start.8) | collective-permute-done | bytes 32800 | tf_op jit(solution)/shard_map/ppermute | solution.py:34
  42.9 2.3 %collective-permute-start.9 = (bf16[64,128]{1,0:T(8,128)(2,1)S(1)}, bf16[64,128]{1,0:T(8,128)(2,1)S(1)}, u32[]{:S(2)}, u32[]{:S(2)}) collective-permute-start(bf16[64,128]{1,0:T(8,128)(2,1)S(1)} %get-tuple-element.58), channel_id=1, source_target_pairs={{0,2},{1,3},{2,0},{3,1},{4,6},{5,7},{6,4},{7,5},{8,10},{9,11},{10,... | collective-permute-start | bytes 49160 | tf_op jit(solution)/shard_map/ppermute | solution.py:91
  49.8 2.1 %collective-permute-done.11.refs_3_ = bf16[64,128]{1,0:T(8,128)(2,1)S(1)} collective-permute-done((bf16[64,128]{1,0:T(8,128)(2,1)S(1)}, bf16[64,128]{1,0:T(8,128)(2,1)S(1)}, u32[]{:S(2)}, u32[]{:S(2)}) %collective-permute-start.11) | collective-permute-done | bytes 16416 | tf_op jit(solution)/shard_map/ppermute | solution.py:91
  51.9 1.7 %shard_map.146 = (bf16[16,4096]{1,0:T(8,128)(2,1)S(1)}, bf16[16,4096]{1,0:T(8,128)(2,1)S(1)}, bf16[16,4096]{1,0:T(8,128)(2,1)S(1)}, bf16[16,4096]{1,0:T(8,128)(2...) custom-call(bf16[64,128]{1,0:T(8,128)(2,1)S(1)} %get-tuple-element.57.refs_0_, ...), custom_call_target="tpu_custom_call" | custom-call | flops 536870912 | bytes 1048576 | tf_op jit(solution)/shard_map/pallas_call | solution.py:164
  54.2 1.5 %collective-permute-start.15 = (bf16[32,4096]{1,0:T(8,128)(2,1)S(1)}, bf16[32,4096]{1,0:T(8,128)(2,1)S(1)}, u32[]{:S(2)}, u32[]{:S(2)}) collective-permute-start(bf16[32,4096]{1,0:T(8,128)(2,1)S(1)} %get-tuple-element.69), channel_id=1, source_target_pairs={{0,1},{1,0},{2,3},{3,2},{4,5},{5,4},{6,7},{7,6},{8,9},{9,8},{10,11... | collective-permute-start | bytes 786440 | tf_op jit(solution)/shard_map/ppermute | solution.py:34
  55.7 3.4 %shard_map.147 = (bf16[1024,4096]{1,0:T(8,128)(2,1)S(1)}, f32[8,128]{1,0:T(8,128)S(1)}) custom-call(bf16[16,4096]{1,0:T(8,128)(2,1)S(1)} %get-tuple-element.70.refs_0_, bf16[1024,4096]{1,0:T(8,128)(2,1)} %refs_1_.6), custom_call_target="tpu_custom_call" | custom-call | bytes 16777216 | tf_op jit(solution)/shard_map/pallas_call | solution.py:189
  60.2 1.9 %collective-permute-start.14 = (bf16[16,4096]{1,0:T(8,128)(2,1)S(1)}, bf16[16,4096]{1,0:T(8,128)(2,1)S(1)}, u32[]{:S(2)}, u32[]{:S(2)}) collective-permute-start(bf16[16,4096]{1,0:T(8,128)(2,1)S(1)} %get-tuple-element.89), channel_id=1, source_target_pairs={{0,2},{1,3},{2,4},{3,5},{4,6},{5,7},{6,0},{7,1},{8,10},{9,11},{10,... | collective-permute-start | bytes 393224 | tf_op jit(solution)/shard_map/ppermute | solution.py:34
  62.9 1.4 %collective-permute-start.16 = (bf16[16,4096]{1,0:T(8,128)(2,1)S(1)}, bf16[16,4096]{1,0:T(8,128)(2,1)S(1)}, u32[]{:S(2)}, u32[]{:S(2)}) collective-permute-start(bf16[16,4096]{1,0:T(8,128)(2,1)S(1)} %add_convert_fusion.3), channel_id=1, source_target_pairs={{0,6},{1,7},{2,0},{3,1},{4,2},{5,3},{6,4},{7,5},{8,14},{9,15},{10,... | collective-permute-start | bytes 393224 | tf_op jit(solution)/shard_map/ppermute | solution.py:34
  64.3 7.4 %collective-permute-done.13 = bf16[16,4096]{1,0:T(8,128)(2,1)S(1)} collective-permute-done((bf16[16,4096]{1,0:T(8,128)(2,1)S(1)}, bf16[16,4096]{1,0:T(8,128)(2,1)S(1)}, u32[]{:S(2)}, u32[]{:S(2)}) %collective-permute-start.13) | collective-permute-done | bytes 131104 | tf_op jit(solution)/shard_map/ppermute | solution.py:34
  73.4 4.5 %collective-permute-start.20 = (bf16[16,4096]{1,0:T(8,128)(2,1)S(1)}, bf16[16,4096]{1,0:T(8,128)(2,1)S(1)}, u32[]{:S(2)}, u32[]{:S(2)}) collective-permute-start(bf16[16,4096]{1,0:T(8,128)(2,1)S(1)} %multiply_convert_fusion.refs_0_), channel_id=1, source_target_pairs={{0,4},{1,5},{2,6},{3,7},{4,0},{5,1},{6,2},{7,3},{8,12},{9,13},{10,... | collective-permute-start | bytes 393224 | tf_op jit(solution)/shard_map/ppermute | solution.py:34
  79.9 5.1 %collective-permute-done.20.refs_4_ = bf16[16,4096]{1,0:T(8,128)(2,1)S(1)} collective-permute-done((bf16[16,4096]{1,0:T(8,128)(2,1)S(1)}, bf16[16,4096]{1,0:T(8,128)(2,1)S(1)}, u32[]{:S(2)}, u32[]{:S(2)}) %collective-permute-start.20) | collective-permute-done | bytes 131104 | tf_op jit(solution)/shard_map/ppermute | solution.py:34
  85.5 1.6 %collective-permute-start.19 = (bf16[16,4096]{1,0:T(8,128)(2,1)S(1)}, bf16[16,4096]{1,0:T(8,128)(2,1)S(1)}, u32[]{:S(2)}, u32[]{:S(2)}) collective-permute-start(bf16[16,4096]{1,0:T(8,128)(2,1)S(1)} %collective-permute-done.18.refs_2_), channel_id=1, source_target_pairs={{0,1},{1,0},{2,3},{3,2},{4,5},{5,4},{6,7},{7,6},{8,9},{9,8},{10,11... | collective-permute-start | bytes 393224 | tf_op jit(solution)/shard_map/ppermute | solution.py:34
  87.0 4.0 %shard_map.149 = (bf16[4096,1024]{1,0:T(8,128)(2,1)S(1)}, f32[8,128]{1,0:T(8,128)}) custom-call(bf16[16,4096]{1,0:T(8,128)(2,1)S(1)} %multiply_convert_fusion.refs_0_, bf16[4096,1024]{1,0:T(8,128)(2,1)} %refs_1_.7), custom_call_target="tpu_custom_call" | custom-call | bytes 16777216 | tf_op jit(solution)/shard_map/pallas_call | solution.py:189
  91.4 2.8 %collective-permute-done.19.refs_3_ = bf16[16,4096]{1,0:T(8,128)(2,1)S(1)} collective-permute-done((bf16[16,4096]{1,0:T(8,128)(2,1)S(1)}, bf16[16,4096]{1,0:T(8,128)(2,1)S(1)}, u32[]{:S(2)}, u32[]{:S(2)}) %collective-permute-start.19) | collective-permute-done | bytes 131104 | tf_op jit(solution)/shard_map/ppermute | solution.py:34
  94.3 3.6 %shard_map.150 = (bf16[16,4096]{1,0:T(8,128)(2,1)S(1)}, bf16[16,4096]{1,0:T(8,128)(2,1)S(1)}, bf16[16,4096]{1,0:T(8,128)(2,1)S(1)}, bf16[16,4096]{1,0:T(8,128)(2...) custom-call(bf16[16,4096]{1,0:T(8,128)(2,1)S(1)} %multiply_convert_f, ...), custom_call_target="tpu_custom_call" | custom-call | flops 3221225472 | bytes 1048576 | tf_op jit(solution)/shard_map/pallas_call | solution.py:164
  98.4 1.6 %collective-permute-start.26 = (bf16[16,4096]{1,0:T(8,128)(2,1)S(1)}, bf16[16,4096]{1,0:T(8,128)(2,1)S(1)}, u32[]{:S(2)}, u32[]{:S(2)}) collective-permute-start(bf16[16,4096]{1,0:T(8,128)(2,1)S(1)} %get-tuple-element.78), channel_id=1, source_target_pairs={{0,1},{1,0},{2,3},{3,2},{4,5},{5,4},{6,7},{7,6},{8,9},{9,8},{10,11... | collective-permute-start | bytes 393224 | tf_op jit(solution)/shard_map/ppermute | solution.py:34
  100.4 1.6 %collective-permute-start.30 = (bf16[16,4096]{1,0:T(8,128)(2,1)S(1)}, bf16[16,4096]{1,0:T(8,128)(2,1)S(1)}, u32[]{:S(2)}, u32[]{:S(2)}) collective-permute-start(bf16[16,4096]{1,0:T(8,128)(2,1)S(1)} %get-tuple-element.82), channel_id=1, source_target_pairs={{0,1},{1,0},{2,3},{3,2},{4,5},{5,4},{6,7},{7,6},{8,9},{9,8},{10,11... | collective-permute-start | bytes 393224 | tf_op jit(solution)/shard_map/ppermute | solution.py:34
  105.7 2.6 %collective-permute-start.29 = (bf16[16,4096]{1,0:T(8,128)(2,1)S(1)}, bf16[16,4096]{1,0:T(8,128)(2,1)S(1)}, u32[]{:S(2)}, u32[]{:S(2)}) collective-permute-start(bf16[16,4096]{1,0:T(8,128)(2,1)S(1)} %add_convert_fusion), channel_id=1, source_target_pairs={{0,6},{1,7},{2,0},{3,1},{4,2},{5,3},{6,4},{7,5},{8,14},{9,15},{10,... | collective-permute-start | bytes 393224 | tf_op jit(solution)/shard_map/ppermute | solution.py:34
  108.3 3.3 %collective-permute-done.25 = bf16[16,4096]{1,0:T(8,128)(2,1)S(1)} collective-permute-done((bf16[16,4096]{1,0:T(8,128)(2,1)S(1)}, bf16[16,4096]{1,0:T(8,128)(2,1)S(1)}, u32[]{:S(2)}, u32[]{:S(2)}) %collective-permute-start.25) | collective-permute-done | bytes 131104 | tf_op jit(solution)/shard_map/ppermute | solution.py:34
  (71 shorter events, 25.9 us)
Async XLA Ops:
  1.7 12.8 %collective-permute-start.1 = (bf16[32,4096]{1,0:T(8,128)(2,1)S(1)}, bf16[32,4096]{1,0:T(8,128)(2,1)S(1)}, u32[]{:S(2)}, u32[]{:S(2)}) collective-permute-start(bf16[32,4096]{1,0:T(8,128)(2,1)S(1)} %shard_map.136.refs_0_), channel_id=1, source_target_pairs={{0,2},{1,3},{2,4},{3,5},{4,6},{5,7},{6,0},{7,1},{8,10},{9,11},{10,... | collective-permute-start | bytes 786440 | tf_op jit(solution)/shard_map/ppermute | solution.py:34
  4.8 13.4 %collective-permute-start.4 = (bf16[32,4096]{1,0:T(8,128)(2,1)S(1)}, bf16[32,4096]{1,0:T(8,128)(2,1)S(1)}, u32[]{:S(2)}, u32[]{:S(2)}) collective-permute-start(bf16[32,4096]{1,0:T(8,128)(2,1)S(1)} %shard_map.136.refs_0_), channel_id=1, source_target_pairs={{0,6},{1,7},{2,0},{3,1},{4,2},{5,3},{6,4},{7,5},{8,14},{9,15},{10,... | collective-permute-start | bytes 786440 | tf_op jit(solution)/shard_map/ppermute | solution.py:34
  6.9 11.3 %collective-permute-start = (bf16[32,4096]{1,0:T(8,128)(2,1)S(1)}, bf16[32,4096]{1,0:T(8,128)(2,1)S(1)}, u32[]{:S(2)}, u32[]{:S(2)}) collective-permute-start(bf16[32,4096]{1,0:T(8,128)(2,1)S(1)} %shard_map.136.refs_0_), channel_id=1, source_target_pairs={{0,1},{1,0},{2,3},{3,2},{4,5},{5,4},{6,7},{7,6},{8,9},{9,8},{10,11... | collective-permute-start | bytes 786440 | tf_op jit(solution)/shard_map/ppermute | solution.py:34
  14.6 7.1 %collective-permute-start.3 = (bf16[32,4096]{1,0:T(8,128)(2,1)S(1)}, bf16[32,4096]{1,0:T(8,128)(2,1)S(1)}, u32[]{:S(2)}, u32[]{:S(2)}) collective-permute-start(bf16[32,4096]{1,0:T(8,128)(2,1)S(1)} %collective-permute-done.1.refs_2_), channel_id=1, source_target_pairs={{2,4},{3,5},{4,6},{5,7},{10,12},{11,13},{12,14},{13,15},{18,20},{1... | collective-permute-start | bytes 786440 | tf_op jit(solution)/shard_map/ppermute | solution.py:34
  18.2 9.3 %collective-permute-start.6 = (bf16[32,4096]{1,0:T(8,128)(2,1)S(1)}, bf16[32,4096]{1,0:T(8,128)(2,1)S(1)}, u32[]{:S(2)}, u32[]{:S(2)}) collective-permute-start(bf16[32,4096]{1,0:T(8,128)(2,1)S(1)} %shard_map.139.refs_6_), channel_id=1, source_target_pairs={{0,1},{1,0},{2,3},{3,2},{4,5},{5,4},{6,7},{7,6},{8,9},{9,8},{10,11... | collective-permute-start | bytes 786440 | tf_op jit(solution)/shard_map/ppermute | solution.py:34
  19.8 10.0 %collective-permute-start.5 = (bf16[32,4096]{1,0:T(8,128)(2,1)S(1)}, bf16[32,4096]{1,0:T(8,128)(2,1)S(1)}, u32[]{:S(2)}, u32[]{:S(2)}) collective-permute-start(bf16[32,4096]{1,0:T(8,128)(2,1)S(1)} %shard_map.139.refs_6_), channel_id=1, source_target_pairs={{2,0},{3,1},{4,2},{5,3},{10,8},{11,9},{12,10},{13,11},{18,16},{19,... | collective-permute-start | bytes 786440 | tf_op jit(solution)/shard_map/ppermute | solution.py:34
  21.1 15.4 %collective-permute-start.2 = (bf16[32,4096]{1,0:T(8,128)(2,1)S(1)}, bf16[32,4096]{1,0:T(8,128)(2,1)S(1)}, u32[]{:S(2)}, u32[]{:S(2)}) collective-permute-start(bf16[32,4096]{1,0:T(8,128)(2,1)S(1)} %collective-permute-done.1.refs_2_), channel_id=1, source_target_pairs={{0,1},{1,0},{2,3},{3,2},{4,5},{5,4},{6,7},{7,6},{8,9},{9,8},{10,11... | collective-permute-start | bytes 786440 | tf_op jit(solution)/shard_map/ppermute | solution.py:34
  29.8 7.3 %collective-permute-start.7 = (bf16[32,4096]{1,0:T(8,128)(2,1)S(1)}, bf16[32,4096]{1,0:T(8,128)(2,1)S(1)}, u32[]{:S(2)}, u32[]{:S(2)}) collective-permute-start(bf16[32,4096]{1,0:T(8,128)(2,1)S(1)} %shard_map.140.refs_0_.refs_4_), channel_id=1, source_target_pairs={{0,1},{1,0},{2,3},{3,2},{4,5},{5,4},{6,7},{7,6},{8,9},{9,8},{10,11... | collective-permute-start | bytes 786440 | tf_op jit(solution)/shard_map/ppermute | solution.py:34
  38.9 4.0 %collective-permute-start.8 = (bf16[128,128]{1,0:T(8,128)(2,1)S(1)}, bf16[128,128]{1,0:T(8,128)(2,1)S(1)}, u32[]{:S(2)}, u32[]{:S(2)}) collective-permute-start(bf16[128,128]{1,0:T(8,128)(2,1)S(1)} %get-tuple-element.56), channel_id=1, source_target_pairs={{0,1},{1,0},{2,3},{3,2},{4,5},{5,4},{6,7},{7,6},{8,9},{9,8},{10,11... | collective-permute-start | bytes 98312 | tf_op jit(solution)/shard_map/ppermute | solution.py:34
  42.9 5.8 %collective-permute-start.9 = (bf16[64,128]{1,0:T(8,128)(2,1)S(1)}, bf16[64,128]{1,0:T(8,128)(2,1)S(1)}, u32[]{:S(2)}, u32[]{:S(2)}) collective-permute-start(bf16[64,128]{1,0:T(8,128)(2,1)S(1)} %get-tuple-element.58), channel_id=1, source_target_pairs={{0,2},{1,3},{2,0},{3,1},{4,6},{5,7},{6,4},{7,5},{8,10},{9,11},{10,... | collective-permute-start | bytes 49160 | tf_op jit(solution)/shard_map/ppermute | solution.py:91
  45.1 4.7 %collective-permute-start.10 = (bf16[64,128]{1,0:T(8,128)(2,1)S(1)}, bf16[64,128]{1,0:T(8,128)(2,1)S(1)}, u32[]{:S(2)}, u32[]{:S(2)}) collective-permute-start(bf16[64,128]{1,0:T(8,128)(2,1)S(1)} %get-tuple-element.59), channel_id=1, source_target_pairs={{0,4},{1,5},{2,6},{3,7},{4,0},{5,1},{6,2},{7,3},{8,12},{9,13},{10,... | collective-permute-start | bytes 49160 | tf_op jit(solution)/shard_map/ppermute | solution.py:91
  46.4 5.5 %collective-permute-start.11 = (bf16[64,128]{1,0:T(8,128)(2,1)S(1)}, bf16[64,128]{1,0:T(8,128)(2,1)S(1)}, u32[]{:S(2)}, u32[]{:S(2)}) collective-permute-start(bf16[64,128]{1,0:T(8,128)(2,1)S(1)} %get-tuple-element.60), channel_id=1, source_target_pairs={{0,6},{1,7},{2,4},{3,5},{4,2},{5,3},{6,0},{7,1},{8,14},{9,15},{10,... | collective-permute-start | bytes 49160 | tf_op jit(solution)/shard_map/ppermute | solution.py:91
  48.6 23.4 %copy-start.5 = (f32[4096]{0:T(1024)S(1)}, f32[4096]{0:T(1024)}, u32[]{:S(2)}) copy-start(f32[4096]{0:T(1024)} %param.22) | copy-start | bytes 49156
  53.6 6.4 %collective-permute-start.12 = (bf16[32,4096]{1,0:T(8,128)(2,1)S(1)}, bf16[32,4096]{1,0:T(8,128)(2,1)S(1)}, u32[]{:S(2)}, u32[]{:S(2)}) collective-permute-start(bf16[32,4096]{1,0:T(8,128)(2,1)S(1)} %get-tuple-element.66), channel_id=1, source_target_pairs={{0,1},{1,0},{2,3},{3,2},{4,5},{5,4},{6,7},{7,6},{8,9},{9,8},{10,11... | collective-permute-start | bytes 786440 | tf_op jit(solution)/shard_map/ppermute | solution.py:34
  54.2 8.7 %collective-permute-start.15 = (bf16[32,4096]{1,0:T(8,128)(2,1)S(1)}, bf16[32,4096]{1,0:T(8,128)(2,1)S(1)}, u32[]{:S(2)}, u32[]{:S(2)}) collective-permute-start(bf16[32,4096]{1,0:T(8,128)(2,1)S(1)} %get-tuple-element.69), channel_id=1, source_target_pairs={{0,1},{1,0},{2,3},{3,2},{4,5},{5,4},{6,7},{7,6},{8,9},{9,8},{10,11... | collective-permute-start | bytes 786440 | tf_op jit(solution)/shard_map/ppermute | solution.py:34
  60.1 11.6 %collective-permute-start.13 = (bf16[16,4096]{1,0:T(8,128)(2,1)S(1)}, bf16[16,4096]{1,0:T(8,128)(2,1)S(1)}, u32[]{:S(2)}, u32[]{:S(2)}) collective-permute-start(bf16[16,4096]{1,0:T(8,128)(2,1)S(1)} %get-tuple-element.88), channel_id=1, source_target_pairs={{0,4},{1,5},{2,6},{3,7},{4,0},{5,1},{6,2},{7,3},{8,12},{9,13},{10,... | collective-permute-start | bytes 393224 | tf_op jit(solution)/shard_map/ppermute | solution.py:34
  60.2 11.6 %collective-permute-start.14 = (bf16[16,4096]{1,0:T(8,128)(2,1)S(1)}, bf16[16,4096]{1,0:T(8,128)(2,1)S(1)}, u32[]{:S(2)}, u32[]{:S(2)}) collective-permute-start(bf16[16,4096]{1,0:T(8,128)(2,1)S(1)} %get-tuple-element.89), channel_id=1, source_target_pairs={{0,2},{1,3},{2,4},{3,5},{4,6},{5,7},{6,0},{7,1},{8,10},{9,11},{10,... | collective-permute-start | bytes 393224 | tf_op jit(solution)/shard_map/ppermute | solution.py:34
  62.9 8.8 %collective-permute-start.16 = (bf16[16,4096]{1,0:T(8,128)(2,1)S(1)}, bf16[16,4096]{1,0:T(8,128)(2,1)S(1)}, u32[]{:S(2)}, u32[]{:S(2)}) collective-permute-start(bf16[16,4096]{1,0:T(8,128)(2,1)S(1)} %add_convert_fusion.3), channel_id=1, source_target_pairs={{0,6},{1,7},{2,0},{3,1},{4,2},{5,3},{6,4},{7,5},{8,14},{9,15},{10,... | collective-permute-start | bytes 393224 | tf_op jit(solution)/shard_map/ppermute | solution.py:34
  72.1 7.2 %collective-permute-start.22 = (bf16[16,4096]{1,0:T(8,128)(2,1)S(1)}, bf16[16,4096]{1,0:T(8,128)(2,1)S(1)}, u32[]{:S(2)}, u32[]{:S(2)}) collective-permute-start(bf16[16,4096]{1,0:T(8,128)(2,1)S(1)} %multiply_convert_fusion.refs_0_), channel_id=1, source_target_pairs={{0,6},{1,7},{2,0},{3,1},{4,2},{5,3},{6,4},{7,5},{8,14},{9,15},{10,... | collective-permute-start | bytes 393224 | tf_op jit(solution)/shard_map/ppermute | solution.py:34
  73.4 11.6 %collective-permute-start.20 = (bf16[16,4096]{1,0:T(8,128)(2,1)S(1)}, bf16[16,4096]{1,0:T(8,128)(2,1)S(1)}, u32[]{:S(2)}, u32[]{:S(2)}) collective-permute-start(bf16[16,4096]{1,0:T(8,128)(2,1)S(1)} %multiply_convert_fusion.refs_0_), channel_id=1, source_target_pairs={{0,4},{1,5},{2,6},{3,7},{4,0},{5,1},{6,2},{7,3},{8,12},{9,13},{10,... | collective-permute-start | bytes 393224 | tf_op jit(solution)/shard_map/ppermute | solution.py:34
  77.9 7.6 %collective-permute-start.18 = (bf16[16,4096]{1,0:T(8,128)(2,1)S(1)}, bf16[16,4096]{1,0:T(8,128)(2,1)S(1)}, u32[]{:S(2)}, u32[]{:S(2)}) collective-permute-start(bf16[16,4096]{1,0:T(8,128)(2,1)S(1)} %multiply_convert_fusion.refs_0_), channel_id=1, source_target_pairs={{0,2},{1,3},{2,4},{3,5},{4,6},{5,7},{6,0},{7,1},{8,10},{9,11},{10,... | collective-permute-start | bytes 393224 | tf_op jit(solution)/shard_map/ppermute | solution.py:34
  77.9 13.2 %collective-permute-start.17 = (bf16[16,4096]{1,0:T(8,128)(2,1)S(1)}, bf16[16,4096]{1,0:T(8,128)(2,1)S(1)}, u32[]{:S(2)}, u32[]{:S(2)}) collective-permute-start(bf16[16,4096]{1,0:T(8,128)(2,1)S(1)} %multiply_convert_fusion.refs_0_), channel_id=1, source_target_pairs={{0,1},{1,0},{2,3},{3,2},{4,5},{5,4},{6,7},{7,6},{8,9},{9,8},{10,11... | collective-permute-start | bytes 393224 | tf_op jit(solution)/shard_map/ppermute | solution.py:34
  79.3 11.7 %collective-permute-start.23 = (bf16[16,4096]{1,0:T(8,128)(2,1)S(1)}, bf16[16,4096]{1,0:T(8,128)(2,1)S(1)}, u32[]{:S(2)}, u32[]{:S(2)}) collective-permute-start(bf16[16,4096]{1,0:T(8,128)(2,1)S(1)} %collective-permute-done.22.refs_6_), channel_id=1, source_target_pairs={{0,1},{1,0},{2,3},{3,2},{4,5},{5,4},{6,7},{7,6},{8,9},{9,8},{10,11... | collective-permute-start | bytes 393224 | tf_op jit(solution)/shard_map/ppermute | solution.py:34
  85.0 6.4 %collective-permute-start.21 = (bf16[16,4096]{1,0:T(8,128)(2,1)S(1)}, bf16[16,4096]{1,0:T(8,128)(2,1)S(1)}, u32[]{:S(2)}, u32[]{:S(2)}) collective-permute-start(bf16[16,4096]{1,0:T(8,128)(2,1)S(1)} %collective-permute-done.20.refs_4_), channel_id=1, source_target_pairs={{0,1},{1,0},{2,3},{3,2},{4,5},{5,4},{6,7},{7,6},{8,9},{9,8},{10,11... | collective-permute-start | bytes 393224 | tf_op jit(solution)/shard_map/ppermute | solution.py:34
  85.5 8.8 %collective-permute-start.19 = (bf16[16,4096]{1,0:T(8,128)(2,1)S(1)}, bf16[16,4096]{1,0:T(8,128)(2,1)S(1)}, u32[]{:S(2)}, u32[]{:S(2)}) collective-permute-start(bf16[16,4096]{1,0:T(8,128)(2,1)S(1)} %collective-permute-done.18.refs_2_), channel_id=1, source_target_pairs={{0,1},{1,0},{2,3},{3,2},{4,5},{5,4},{6,7},{7,6},{8,9},{9,8},{10,11... | collective-permute-start | bytes 393224 | tf_op jit(solution)/shard_map/ppermute | solution.py:34
  97.9 5.0 %collective-permute-start.24 = (bf16[16,4096]{1,0:T(8,128)(2,1)S(1)}, bf16[16,4096]{1,0:T(8,128)(2,1)S(1)}, u32[]{:S(2)}, u32[]{:S(2)}) collective-permute-start(bf16[16,4096]{1,0:T(8,128)(2,1)S(1)} %get-tuple-element.76), channel_id=1, source_target_pairs={{0,1},{1,0},{2,3},{3,2},{4,5},{5,4},{6,7},{7,6},{8,9},{9,8},{10,11... | collective-permute-start | bytes 393224 | tf_op jit(solution)/shard_map/ppermute | solution.py:34
  98.4 5.9 %collective-permute-start.26 = (bf16[16,4096]{1,0:T(8,128)(2,1)S(1)}, bf16[16,4096]{1,0:T(8,128)(2,1)S(1)}, u32[]{:S(2)}, u32[]{:S(2)}) collective-permute-start(bf16[16,4096]{1,0:T(8,128)(2,1)S(1)} %get-tuple-element.78), channel_id=1, source_target_pairs={{0,1},{1,0},{2,3},{3,2},{4,5},{5,4},{6,7},{7,6},{8,9},{9,8},{10,11... | collective-permute-start | bytes 393224 | tf_op jit(solution)/shard_map/ppermute | solution.py:34
  100.0 5.8 %collective-permute-start.28 = (bf16[16,4096]{1,0:T(8,128)(2,1)S(1)}, bf16[16,4096]{1,0:T(8,128)(2,1)S(1)}, u32[]{:S(2)}, u32[]{:S(2)}) collective-permute-start(bf16[16,4096]{1,0:T(8,128)(2,1)S(1)} %get-tuple-element.80), channel_id=1, source_target_pairs={{0,1},{1,0},{2,3},{3,2},{4,5},{5,4},{6,7},{7,6},{8,9},{9,8},{10,11... | collective-permute-start | bytes 393224 | tf_op jit(solution)/shard_map/ppermute | solution.py:34
  100.4 7.9 %collective-permute-start.30 = (bf16[16,4096]{1,0:T(8,128)(2,1)S(1)}, bf16[16,4096]{1,0:T(8,128)(2,1)S(1)}, u32[]{:S(2)}, u32[]{:S(2)}) collective-permute-start(bf16[16,4096]{1,0:T(8,128)(2,1)S(1)} %get-tuple-element.82), channel_id=1, source_target_pairs={{0,1},{1,0},{2,3},{3,2},{4,5},{5,4},{6,7},{7,6},{8,9},{9,8},{10,11... | collective-permute-start | bytes 393224 | tf_op jit(solution)/shard_map/ppermute | solution.py:34
  102.9 8.7 %collective-permute-start.25 = (bf16[16,4096]{1,0:T(8,128)(2,1)S(1)}, bf16[16,4096]{1,0:T(8,128)(2,1)S(1)}, u32[]{:S(2)}, u32[]{:S(2)}) collective-permute-start(bf16[16,4096]{1,0:T(8,128)(2,1)S(1)} %add_convert_fusion.2), channel_id=1, source_target_pairs={{0,4},{1,5},{2,6},{3,7},{4,0},{5,1},{6,2},{7,3},{8,12},{9,13},{10,... | collective-permute-start | bytes 393224 | tf_op jit(solution)/shard_map/ppermute | solution.py:34
  104.3 7.3 %collective-permute-start.27 = (bf16[16,4096]{1,0:T(8,128)(2,1)S(1)}, bf16[16,4096]{1,0:T(8,128)(2,1)S(1)}, u32[]{:S(2)}, u32[]{:S(2)}) collective-permute-start(bf16[16,4096]{1,0:T(8,128)(2,1)S(1)} %add_convert_fusion.1), channel_id=1, source_target_pairs={{0,2},{1,3},{2,4},{3,5},{4,6},{5,7},{6,0},{7,1},{8,10},{9,11},{10,... | collective-permute-start | bytes 393224 | tf_op jit(solution)/shard_map/ppermute | solution.py:34
  105.7 7.2 %collective-permute-start.29 = (bf16[16,4096]{1,0:T(8,128)(2,1)S(1)}, bf16[16,4096]{1,0:T(8,128)(2,1)S(1)}, u32[]{:S(2)}, u32[]{:S(2)}) collective-permute-start(bf16[16,4096]{1,0:T(8,128)(2,1)S(1)} %add_convert_fusion), channel_id=1, source_target_pairs={{0,6},{1,7},{2,0},{3,1},{4,2},{5,3},{6,4},{7,5},{8,14},{9,15},{10,... | collective-permute-start | bytes 393224 | tf_op jit(solution)/shard_map/ppermute | solution.py:34
  (5 other events, 46.4 us)

commit v16 on v12

--- a/solution.py
+++ b/solution.py
@@ -84,55 +84,44 @@
     shape = ((parts[0].shape[0] // tall * wide, parts[0].shape[1]), bf16)
     crossed = [parts[0]] + [shift(parts[dy], tall, wide, 0, dy) for dy in range(1, wide)]
     packed = kernel_call(functools.partial(pack_body, tall), [shape] * tall, crossed)
-    return [packed[0]] + [shift(packed[dz], tall, wide, dz, 0) for dz in range(1, tall)]
+    pairs = [
+        [(z * wide + y, (z ^ kz) * wide + y) for z in range(tall) for y in range(wide)]
+        for kz in range(tall)
+    ]
+    return [packed[0]] + [lax.ppermute(packed[k], "ctx", pairs[k]) for k in range(1, tall)]
 
 
 def gather_blocks(block, tall, wide):
     blocks = {(dz, 0): shift(block, tall, wide, dz, 0) if dz else block for dz in range(tall)}
-    for dy in range(1, wide):
-        blocks[0, dy] = shift(block, tall, wide, 0, dy)
-    blocks[1, 0] = tie([blocks[1, 0]], [blocks[0, dy] for dy in range(1, wide)])
-    for dz in range(1, tall):
+    for dz in range(tall):
         for dy in range(1, wide):
             blocks[dz, dy] = shift(blocks[dz, 0], tall, wide, 0, dy)
     return [blocks[dz, dy] for dz in range(tall) for dy in range(wide)]
 
 
-def sum_shapes(tall, wide, share, model):
-    kept = [((share, model), bf16)] * tall
-    return kept + [((tall * share, model), bf16)] * (wide - 1)
+def sum_order(tall):
+    return [tall // 2, *range(1, tall // 2), *range(tall // 2 + 1, tall), 0]
 
 
 def store_parts(parts, tall, wide, span, product, back):
     share = parts[0].shape[0]
     sign = -1 if back else 1
-
-    def rows(dz, dy):
-        at = sign * dz % tall * wide + sign * dy % wide
-        return product[at * share : (at + 1) * share, :]
-
     for dz in range(tall):
-        parts[dz][:, span] = rows(dz, 0)
+        for dy in range(wide):
+            at = sign * dz % tall * wide + sign * dy % wide
+            parts[dz * wide + dy][:, span] = product[at * share : (at + 1) * share, :]
+
+
+def scatter_sum(parts, tall, wide):
+    total = None
+    for dz in sum_order(tall):
+        lane = parts[dz * wide].astype(f32)
         for dy in range(1, wide):
-            parts[tall + dy - 1][dz * share : (dz + 1) * share, span] = rows(dz, dy)
-
-
-def scatter_sum(parts, tall, wide, loads=()):
-    share = parts[0].shape[0]
-    loaded = []
-    crossed = [shift(p, tall, wide, 0, dy) for dy, p in enumerate(parts[tall:], 1)]
-    if loads:
-        *loaded, token = load(parts[0], *loads)
-        crossed[0] = tie([crossed[0]], [token])
-    total = None
-    for dz in [tall // 2, *range(1, tall // 2), *range(tall // 2 + 1, tall), 0]:
-        lane = parts[dz].astype(f32)
-        for other in crossed:
-            lane = lane + other[dz * share : (dz + 1) * share].astype(f32)
+            lane = lane + shift(parts[dz * wide + dy], tall, wide, 0, dy).astype(f32)
         if dz:
             lane = shift(lane.astype(bf16), tall, wide, dz, 0).astype(f32)
         total = lane if total is None else total + lane
-    return (total, *loaded) if loads else total
+    return total
 
 
 def dot(a, b):
@@ -236,7 +225,8 @@
         z, y = divmod(s, wide)
         from_block = lax.rem(my_z - z + tall, tall) * wide + lax.rem(my_y - y + wide, wide)
         to_block = lax.rem(z - my_z + tall, tall) * wide + lax.rem(y - my_y + wide, wide)
-        peer = lax.rem(my_z + z, tall) * wide + lax.rem(my_y + y, wide)
+        peer = (my_z ^ z) * wide + lax.rem(my_y + y, wide)
+        lot = (my_z ^ z) * wide + lax.rem(my_y - y + wide, wide)
         before = where < s * tokens
         first = jnp.sum(jnp.where(before, 1.0, 0.0), axis=1, keepdims=True)
         inside = (where < (s + 1) * tokens) & jnp.logical_not(before)
@@ -244,7 +234,7 @@
         slot += jnp.where(inside, lane - first + start, 0.0)
         place += jnp.where(owner == s, (to_block * share).astype(f32), 0.0)
         out_base += jnp.where(out_block == y * tall + z, heads_of(peer).astype(f32), 0.0)
-        in_base += jnp.where(in_source == s, (from_block * (outbound // count)).astype(f32), 0.0)
+        in_base += jnp.where(in_source == s, (lot * (outbound // count)).astype(f32), 0.0)
     mine = owner == iota((count, total), 0)
     earlier = jnp.where(iota((total, total), 0) < iota((total, total), 1), 1.0, 0.0)
     rank = dot(jnp.where(mine, 1.0, 0.0).astype(bf16), earlier.astype(bf16))
@@ -402,6 +392,7 @@
     attn_gain, w_key, w_value, w_query, token_1 = load(
         outgoing, attn_gain.reshape(1, model), w_key, w_value, w_query
     )
+    w_down, token_5 = load(token_1, w_down)
 
     each = kv_local * 2 * depth
     notes = np.zeros((max(count * each, 2 * kv_local * HEAD_DIM), 4), np.float32)
@@ -425,7 +416,7 @@
         [me, routed, balance, notes],
         specs=[scalar, VMEM, VMEM, VMEM],
     )
-    blocks = gather_rows(outgoing, tall, wide, [token_1, positions])
+    blocks = gather_rows(outgoing, tall, wide, [token_1, token_5, positions])
     near = blocks[2 * wide]
     w_output, *token_2 = load(near, w_output)
     w_gate, *token_3 = load(near, w_gate)
@@ -456,15 +447,14 @@
         [normed, w_query, q_cos, q_sin],
         flops=2 * total * model * heads_wide,
     )
-    part_shapes = sum_shapes(tall, wide, share, model)
     attn_parts = kernel_call(
         functools.partial(attend_body, plane, kv_local),
-        part_shapes,
+        [((share, model), bf16)] * count,
         [*arrived, query, unmix, k_cos, k_sin, routed, positions, w_output],
         [pltpu.VMEM((total, heads_wide), bf16)],
         flops=2 * total * model * heads_wide,
     )
-    attn_own, w_down = scatter_sum(attn_parts, tall, wide, [w_down])
+    attn_own = scatter_sum(attn_parts, tall, wide)
     own_rows = own.astype(f32)
     hidden = own_rows + attn_own
     mean_sq = jnp.mean(hidden * hidden, axis=-1, keepdims=True)
@@ -474,7 +464,7 @@
     hidden_units = w_gate.shape[1]
     mlp_parts = kernel_call(
         functools.partial(mlp_body, plane),
-        part_shapes,
+        [((share, model), bf16)] * count,
         [*pieces, w_gate, w_up, w_down],
         [pltpu.VMEM((total, model), bf16), pltpu.VMEM((total, hidden_units), bf16)],
         flops=6 * total * model * hidden_units,

time: 120 us -> 108 us (0.900)
  waiting for transfers between devices: 52 us -> 34.8 us
  starting transfers between devices: 36.9 us -> 44.1 us
  local copies, waits for them, and re-layouts: 2.23 us -> 0.02 us
    ppermute x27 -> x30, waiting for transfers between devices: 52 us -> 32.2 us  [shift(): return lax.ppermute(block, 'ctx', pairs)]
    ppermute x0 -> x3, starting transfers between devices: none -> 4.17 us  [exchange(): lax.ppermute(packed[k], 'ctx', pairs[k])]
    ppermute x27 -> x30, starting transfers between devices: 36.9 us -> 39.9 us  [shift(): return lax.ppermute(block, 'ctx', pairs)]
    ppermute x0 -> x3, waiting for transfers between devices: none -> 2.66 us  [exchange(): lax.ppermute(packed[k], 'ctx', pairs[k])]
    unnamed x12 -> x10, local copies, waits for them, and re-layouts: 2.23 us -> 0.02 us
    pallas_call x11 -> x9, Pallas kernels: 10.4 us -> 10.5 us  [kernel_call(): pl.pallas_call(body, out_shape=[jax.ShapeDtypeStruct(s, d) for s, d in ou...]
  transfers between devices with their start and end apart: 27 -> 33, of which waited for: 18 -> 18; matrix products, arithmetic and copies ran while one was open for 0% -> 1% of each run, Pallas kernels for 15% -> 16%
where the time goes in v16:
time: 108 us; the launch traced here: 107 us
  starting transfers between devices  44.1 us (41%)
  waiting for transfers between devices  34.8 us (32%)
  Pallas kernels  26.3 us (24%)
  other arithmetic  1.91 us (2%)
    ppermute x30, starting transfers between devices, shift(): return lax.ppermute(block, 'ctx', pairs)  39.9 us
    ppermute x30, waiting for transfers between devices, shift(): return lax.ppermute(block, 'ctx', pairs)  32.2 us
    pallas_call x5, Pallas kernels, load(): pl.pallas_call(functools.partial(load_body, len(arrays)), out_shape=[pltp...  15.9 us
    pallas_call x9, Pallas kernels, kernel_call(): pl.pallas_call(body, out_shape=[jax.ShapeDtypeStruct(s, d) for s, d in ou...  10.5 us
    ppermute x3, starting transfers between devices, exchange(): lax.ppermute(packed[k], 'ctx', pairs[k])  4.17 us
    ppermute x3, waiting for transfers between devices, exchange(): lax.ppermute(packed[k], 'ctx', pairs[k])  2.66 us
  transfers between devices with their start and end apart: 33, of which 18 were waited for; matrix products, arithmetic and copies ran while one was open for 1% of the time, Pallas kernels for 16%

profile of v16, /device:TPU:0, one launch (start us, length us, event | category | flops | bytes accessed | tf_op | source)
XLA Modules:
  0.0 107.4 jit_solution(3167307625216764238)
XLA Ops:
  0.0 1.6 %shard_map.136.refs_0_ = bf16[32,4096]{1,0:T(8,128)(2,1)S(1)} custom-call(s32[1]{0:T(128)} %bitcast.me, s32[1,128]{1,0:T(1,128)} %bitcast.4, bf16[128,4096]{1,0:T(8,128)(2,1)} %activations_in.1), custom_call_target="tpu_custom_call" | custom-call | flops 33554432 | bytes 1048576 | tf_op jit(solution)/shard_map/pallas_call | solution.py:140
  1.6 3.0 %collective-permute-start = (bf16[32,4096]{1,0:T(8,128)(2,1)S(1)}, bf16[32,4096]{1,0:T(8,128)(2,1)S(1)}, u32[]{:S(2)}, u32[]{:S(2)}) collective-permute-start(bf16[32,4096]{1,0:T(8,128)(2,1)S(1)} %shard_map.136.refs_0_), channel_id=1, source_target_pairs={{0,1},{1,0},{2,3},{3,2},{4,5},{5,4},{6,7},{7,6},{8,9},{9,8},{10,11... | collective-permute-start | bytes 786440 | tf_op jit(solution)/shard_map/ppermute | solution.py:34
  4.6 3.6 %collective-permute-start.4 = (bf16[32,4096]{1,0:T(8,128)(2,1)S(1)}, bf16[32,4096]{1,0:T(8,128)(2,1)S(1)}, u32[]{:S(2)}, u32[]{:S(2)}) collective-permute-start(bf16[32,4096]{1,0:T(8,128)(2,1)S(1)} %shard_map.136.refs_0_), channel_id=1, source_target_pairs={{0,6},{1,7},{2,0},{3,1},{4,2},{5,3},{6,4},{7,5},{8,14},{9,15},{10,... | collective-permute-start | bytes 786440 | tf_op jit(solution)/shard_map/ppermute | solution.py:34
  8.2 2.9 %shard_map.137 = (f32[1,4096]{1,0:T(1,128)S(1)}, bf16[4096,128]{1,0:T(8,128)(2,1)S(1)}, bf16[4096,128]{1,0:T(8,128)(2,1)S(1)}, bf16[4096,512]{1,0:T(8,128)(2,1)S(1)}, f32[8,128]{1,0:T(8,128)S(1)}) custom-call(bf16[32,4096]{1,0:T(8,128)(2,1)S(1)} %shard_map.136.refs_0_, f32[1,4096]{1,0:T(1,128)} %bitcast.8, bf16[4096,128]{1,0:T(8,128)(2,1)} %refs_2_.1, ...), custom_call_target="tpu_custom_call" | custom-call | bytes 12615680 | tf_op jit(solution)/shard_map/pallas_call | solution.py:165
  11.1 3.4 %shard_map.138 = (bf16[1024,4096]{1,0:T(8,128)(2,1)S(1)}, f32[8,128]{1,0:T(8,128)S(1)}) custom-call(f32[8,128]{1,0:T(8,128)S(1)} %get-tuple-element.46.refs_0_.refs_1_, bf16[1024,4096]{1,0:T(8,128)(2,1)} %refs_1_.4), custom_call_target="tpu_custom_call" | custom-call | bytes 16777216 | tf_op jit(solution)/shard_map/pallas_call | solution.py:165
  17.3 2.8 %collective-permute-done.1.refs_2_ = bf16[32,4096]{1,0:T(8,128)(2,1)S(1)} collective-permute-done((bf16[32,4096]{1,0:T(8,128)(2,1)S(1)}, bf16[32,4096]{1,0:T(8,128)(2,1)S(1)}, u32[]{:S(2)}, u32[]{:S(2)}) %collective-permute-start.1) | collective-permute-done | bytes 262176 | tf_op jit(solution)/shard_map/ppermute | solution.py:34
  21.3 2.6 %collective-permute-done.6.refs_2_.refs_7_ = bf16[32,4096]{1,0:T(8,128)(2,1)S(1)} collective-permute-done((bf16[32,4096]{1,0:T(8,128)(2,1)S(1)}, bf16[32,4096]{1,0:T(8,128)(2,1)S(1)}, u32[]{:S(2)}, u32[]{:S(2)}) %collective-permute-start.6) | collective-permute-done | bytes 262176 | tf_op jit(solution)/shard_map/ppermute | solution.py:34
  24.0 1.8 %collective-permute-done.5.refs_1_ = bf16[32,4096]{1,0:T(8,128)(2,1)S(1)} collective-permute-done((bf16[32,4096]{1,0:T(8,128)(2,1)S(1)}, bf16[32,4096]{1,0:T(8,128)(2,1)S(1)}, u32[]{:S(2)}, u32[]{:S(2)}) %collective-permute-start.5) | collective-permute-done | bytes 262176 | tf_op jit(solution)/shard_map/ppermute | solution.py:34
  27.2 3.4 %shard_map.143 = (bf16[4096,1024]{1,0:T(8,128)(2,1)S(1)}, f32[8,128]{1,0:T(8,128)S(1)}) custom-call(bf16[32,4096]{1,0:T(8,128)(2,1)S(1)} %shard_map.141.refs_0_.refs_4_, bf16[4096,1024]{1,0:T(8,128)(2,1)} %refs_1_.6), custom_call_target="tpu_custom_call" | custom-call | bytes 16777216 | tf_op jit(solution)/shard_map/pallas_call | solution.py:165
  30.6 2.2 %shard_map.142 = (bf16[512,4096]{1,0:T(8,128)(2,1)S(1)}, f32[8,128]{1,0:T(8,128)S(1)}) custom-call(bf16[32,4096]{1,0:T(8,128)(2,1)S(1)} %shard_map.141.refs_0_.refs_4_, bf16[512,4096]{1,0:T(8,128)(2,1)} %refs_1_.5), custom_call_target="tpu_custom_call" | custom-call | bytes 8388608 | tf_op jit(solution)/shard_map/pallas_call | solution.py:165
  34.3 1.8 %shard_map.144 = (bf16[128,4096]{1,0:T(8,128)(2,1)S(1)}, bf16[16,4096]{1,0:T(8,128)(2,1)S(1)}, bf16[128,128]{1,0:T(8,128)(2,1)S(1)}, bf16[128,128]{1,0:T(8,128)(2,1)S(1)}) custom-call(bf16[32,4096]{1,0:T(8,128)(2,1)S(1)} %shard_map.136.refs_0_, bf16[32,4096]{1,0:T(8,128)(2,1)S(1)} %collective-permute-done.refs_4_.refs_1_, ...), custom_call_target="tpu_custom_call" | custom-call | flops 536870912 | bytes 1048576 | tf_op jit(solution)/shard_map/pallas_call | solution.py:140
  36.7 3.3 %collective-permute-done.8.refs_1_ = bf16[128,128]{1,0:T(8,128)(2,1)S(1)} collective-permute-done((bf16[128,128]{1,0:T(8,128)(2,1)S(1)}, bf16[128,128]{1,0:T(8,128)(2,1)S(1)}, u32[]{:S(2)}, u32[]{:S(2)}) %collective-permute-start.8) | collective-permute-done | bytes 32800 | tf_op jit(solution)/shard_map/ppermute | solution.py:34
  40.1 2.1 %collective-permute-start.10 = (bf16[64,128]{1,0:T(8,128)(2,1)S(1)}, bf16[64,128]{1,0:T(8,128)(2,1)S(1)}, u32[]{:S(2)}, u32[]{:S(2)}) collective-permute-start(bf16[64,128]{1,0:T(8,128)(2,1)S(1)} %get-tuple-element.62), channel_id=1, source_target_pairs={{0,4},{1,5},{2,6},{3,7},{4,0},{5,1},{6,2},{7,3},{8,12},{9,13},{10,... | collective-permute-start | bytes 49160 | tf_op jit(solution)/shard_map/ppermute | solution.py:91
  42.2 1.6 %collective-permute-start.11 = (bf16[64,128]{1,0:T(8,128)(2,1)S(1)}, bf16[64,128]{1,0:T(8,128)(2,1)S(1)}, u32[]{:S(2)}, u32[]{:S(2)}) collective-permute-start(bf16[64,128]{1,0:T(8,128)(2,1)S(1)} %get-tuple-element.63), channel_id=1, source_target_pairs={{0,6},{1,7},{2,4},{3,5},{4,2},{5,3},{6,0},{7,1},{8,14},{9,15},{10,... | collective-permute-start | bytes 49160 | tf_op jit(solution)/shard_map/ppermute | solution.py:91
  45.1 2.7 %collective-permute-done.11.refs_3_ = bf16[64,128]{1,0:T(8,128)(2,1)S(1)} collective-permute-done((bf16[64,128]{1,0:T(8,128)(2,1)S(1)}, bf16[64,128]{1,0:T(8,128)(2,1)S(1)}, u32[]{:S(2)}, u32[]{:S(2)}) %collective-permute-start.11) | collective-permute-done | bytes 16416 | tf_op jit(solution)/shard_map/ppermute | solution.py:91
  47.7 1.7 %shard_map.147 = (bf16[16,4096]{1,0:T(8,128)(2,1)S(1)}, bf16[16,4096]{1,0:T(8,128)(2,1)S(1)}, bf16[16,4096]{1,0:T(8,128)(2,1)S(1)}, bf16[16,4096]{1,0:T(8,128)(2...) custom-call(bf16[64,128]{1,0:T(8,128)(2,1)S(1)} %get-tuple-element.6, ...), custom_call_target="tpu_custom_call" | custom-call | flops 536870912 | bytes 1048576 | tf_op jit(solution)/shard_map/pallas_call | solution.py:140
  54.7 1.7 %collective-permute-start.13 = (bf16[16,4096]{1,0:T(8,128)(2,1)S(1)}, bf16[16,4096]{1,0:T(8,128)(2,1)S(1)}, u32[]{:S(2)}, u32[]{:S(2)}) collective-permute-start(bf16[16,4096]{1,0:T(8,128)(2,1)S(1)} %add_convert_fusion.5), channel_id=1, source_target_pairs={{0,4},{1,5},{2,6},{3,7},{4,0},{5,1},{6,2},{7,3},{8,12},{9,13},{10,... | collective-permute-start | bytes 393224 | tf_op jit(solution)/shard_map/ppermute | solution.py:34
  57.5 2.9 %collective-permute-start.17 = (bf16[16,4096]{1,0:T(8,128)(2,1)S(1)}, bf16[16,4096]{1,0:T(8,128)(2,1)S(1)}, u32[]{:S(2)}, u32[]{:S(2)}) collective-permute-start(bf16[16,4096]{1,0:T(8,128)(2,1)S(1)} %add_convert_fusion.3), channel_id=1, source_target_pairs={{0,6},{1,7},{2,0},{3,1},{4,2},{5,3},{6,4},{7,5},{8,14},{9,15},{10,... | collective-permute-start | bytes 393224 | tf_op jit(solution)/shard_map/ppermute | solution.py:34
  60.4 1.6 %collective-permute-done.13 = bf16[16,4096]{1,0:T(8,128)(2,1)S(1)} collective-permute-done((bf16[16,4096]{1,0:T(8,128)(2,1)S(1)}, bf16[16,4096]{1,0:T(8,128)(2,1)S(1)}, u32[]{:S(2)}, u32[]{:S(2)}) %collective-permute-start.13) | collective-permute-done | bytes 131104 | tf_op jit(solution)/shard_map/ppermute | solution.py:34
  62.1 1.8 %collective-permute-done.15 = bf16[16,4096]{1,0:T(8,128)(2,1)S(1)} collective-permute-done((bf16[16,4096]{1,0:T(8,128)(2,1)S(1)}, bf16[16,4096]{1,0:T(8,128)(2,1)S(1)}, u32[]{:S(2)}, u32[]{:S(2)}) %collective-permute-start.15) | collective-permute-done | bytes 131104 | tf_op jit(solution)/shard_map/ppermute | solution.py:34
  63.9 4.8 %collective-permute-done.17 = bf16[16,4096]{1,0:T(8,128)(2,1)S(1)} collective-permute-done((bf16[16,4096]{1,0:T(8,128)(2,1)S(1)}, bf16[16,4096]{1,0:T(8,128)(2,1)S(1)}, u32[]{:S(2)}, u32[]{:S(2)}) %collective-permute-start.17) | collective-permute-done | bytes 131104 | tf_op jit(solution)/shard_map/ppermute | solution.py:34
  69.9 1.6 %collective-permute-start.22 = (bf16[16,4096]{1,0:T(8,128)(2,1)S(1)}, bf16[16,4096]{1,0:T(8,128)(2,1)S(1)}, u32[]{:S(2)}, u32[]{:S(2)}) collective-permute-start(bf16[16,4096]{1,0:T(8,128)(2,1)S(1)} %multiply_convert_fusion.refs_0_), channel_id=1, source_target_pairs={{0,4},{1,5},{2,6},{3,7},{4,0},{5,1},{6,2},{7,3},{8,12},{9,13},{10,... | collective-permute-start | bytes 393224 | tf_op jit(solution)/shard_map/ppermute | solution.py:34
  71.5 2.8 %collective-permute-start.24 = (bf16[16,4096]{1,0:T(8,128)(2,1)S(1)}, bf16[16,4096]{1,0:T(8,128)(2,1)S(1)}, u32[]{:S(2)}, u32[]{:S(2)}) collective-permute-start(bf16[16,4096]{1,0:T(8,128)(2,1)S(1)} %multiply_convert_fusion.refs_0_), channel_id=1, source_target_pairs={{0,6},{1,7},{2,0},{3,1},{4,2},{5,3},{6,4},{7,5},{8,14},{9,15},{10,... | collective-permute-start | bytes 393224 | tf_op jit(solution)/shard_map/ppermute | solution.py:34
  74.3 1.5 %collective-permute-start.19 = (bf16[16,4096]{1,0:T(8,128)(2,1)S(1)}, bf16[16,4096]{1,0:T(8,128)(2,1)S(1)}, u32[]{:S(2)}, u32[]{:S(2)}) collective-permute-start(bf16[16,4096]{1,0:T(8,128)(2,1)S(1)} %multiply_convert_fusion.refs_0_), channel_id=1, source_target_pairs={{0,1},{1,0},{2,3},{3,2},{4,5},{5,4},{6,7},{7,6},{8,9},{9,8},{10,11... | collective-permute-start | bytes 393224 | tf_op jit(solution)/shard_map/ppermute | solution.py:34
  76.4 2.2 %collective-permute-done.22.refs_4_ = bf16[16,4096]{1,0:T(8,128)(2,1)S(1)} collective-permute-done((bf16[16,4096]{1,0:T(8,128)(2,1)S(1)}, bf16[16,4096]{1,0:T(8,128)(2,1)S(1)}, u32[]{:S(2)}, u32[]{:S(2)}) %collective-permute-start.22) | collective-permute-done | bytes 131104 | tf_op jit(solution)/shard_map/ppermute | solution.py:34
  78.6 2.0 %collective-permute-start.25 = (bf16[16,4096]{1,0:T(8,128)(2,1)S(1)}, bf16[16,4096]{1,0:T(8,128)(2,1)S(1)}, u32[]{:S(2)}, u32[]{:S(2)}) collective-permute-start(bf16[16,4096]{1,0:T(8,128)(2,1)S(1)} %collective-permute-done.24.refs_6_), channel_id=1, source_target_pairs={{0,1},{1,0},{2,3},{3,2},{4,5},{5,4},{6,7},{7,6},{8,9},{9,8},{10,11... | collective-permute-start | bytes 393224 | tf_op jit(solution)/shard_map/ppermute | solution.py:34
  80.6 4.0 %shard_map.148 = (bf16[4096,1024]{1,0:T(8,128)(2,1)S(1)}, f32[8,128]{1,0:T(8,128)}) custom-call(bf16[16,4096]{1,0:T(8,128)(2,1)S(1)} %multiply_convert_fusion.refs_0_, bf16[4096,1024]{1,0:T(8,128)(2,1)} %refs_1_.7), custom_call_target="tpu_custom_call" | custom-call | bytes 16777216 | tf_op jit(solution)/shard_map/pallas_call | solution.py:165
  85.0 2.8 %collective-permute-done.25.refs_7_ = bf16[16,4096]{1,0:T(8,128)(2,1)S(1)} collective-permute-done((bf16[16,4096]{1,0:T(8,128)(2,1)S(1)}, bf16[16,4096]{1,0:T(8,128)(2,1)S(1)}, u32[]{:S(2)}, u32[]{:S(2)}) %collective-permute-start.25) | collective-permute-done | bytes 131104 | tf_op jit(solution)/shard_map/ppermute | solution.py:34
  87.8 3.7 %shard_map.149 = (bf16[16,4096]{1,0:T(8,128)(2,1)S(1)}, bf16[16,4096]{1,0:T(8,128)(2,1)S(1)}, bf16[16,4096]{1,0:T(8,128)(2,1)S(1)}, bf16[16,4096]{1,0:T(8,128)(2...) custom-call(bf16[16,4096]{1,0:T(8,128)(2,1)S(1)} %multiply_convert_f, ...), custom_call_target="tpu_custom_call" | custom-call | flops 3221225472 | bytes 1048576 | tf_op jit(solution)/shard_map/pallas_call | solution.py:140
  97.9 2.2 %collective-permute-start.29 = (bf16[16,4096]{1,0:T(8,128)(2,1)S(1)}, bf16[16,4096]{1,0:T(8,128)(2,1)S(1)}, u32[]{:S(2)}, u32[]{:S(2)}) collective-permute-start(bf16[16,4096]{1,0:T(8,128)(2,1)S(1)} %add_convert_fusion.1), channel_id=1, source_target_pairs={{0,2},{1,3},{2,4},{3,5},{4,6},{5,7},{6,0},{7,1},{8,10},{9,11},{10,... | collective-permute-start | bytes 393224 | tf_op jit(solution)/shard_map/ppermute | solution.py:34
  100.2 2.3 %collective-permute-start.31 = (bf16[16,4096]{1,0:T(8,128)(2,1)S(1)}, bf16[16,4096]{1,0:T(8,128)(2,1)S(1)}, u32[]{:S(2)}, u32[]{:S(2)}) collective-permute-start(bf16[16,4096]{1,0:T(8,128)(2,1)S(1)} %add_convert_fusion), channel_id=1, source_target_pairs={{0,6},{1,7},{2,0},{3,1},{4,2},{5,3},{6,4},{7,5},{8,14},{9,15},{10,... | collective-permute-start | bytes 393224 | tf_op jit(solution)/shard_map/ppermute | solution.py:34
  102.5 2.9 %collective-permute-done.27 = bf16[16,4096]{1,0:T(8,128)(2,1)S(1)} collective-permute-done((bf16[16,4096]{1,0:T(8,128)(2,1)S(1)}, bf16[16,4096]{1,0:T(8,128)(2,1)S(1)}, u32[]{:S(2)}, u32[]{:S(2)}) %collective-permute-start.27) | collective-permute-done | bytes 131104 | tf_op jit(solution)/shard_map/ppermute | solution.py:34
  (73 shorter events, 25.8 us)
Async XLA Ops:
  1.6 13.8 %collective-permute-start = (bf16[32,4096]{1,0:T(8,128)(2,1)S(1)}, bf16[32,4096]{1,0:T(8,128)(2,1)S(1)}, u32[]{:S(2)}, u32[]{:S(2)}) collective-permute-start(bf16[32,4096]{1,0:T(8,128)(2,1)S(1)} %shard_map.136.refs_0_), channel_id=1, source_target_pairs={{0,1},{1,0},{2,3},{3,2},{4,5},{5,4},{6,7},{7,6},{8,9},{9,8},{10,11... | collective-permute-start | bytes 786440 | tf_op jit(solution)/shard_map/ppermute | solution.py:34
  4.6 10.8 %collective-permute-start.4 = (bf16[32,4096]{1,0:T(8,128)(2,1)S(1)}, bf16[32,4096]{1,0:T(8,128)(2,1)S(1)}, u32[]{:S(2)}, u32[]{:S(2)}) collective-permute-start(bf16[32,4096]{1,0:T(8,128)(2,1)S(1)} %shard_map.136.refs_0_), channel_id=1, source_target_pairs={{0,6},{1,7},{2,0},{3,1},{4,2},{5,3},{6,4},{7,5},{8,14},{9,15},{10,... | collective-permute-start | bytes 786440 | tf_op jit(solution)/shard_map/ppermute | solution.py:34
  8.2 12.0 %collective-permute-start.1 = (bf16[32,4096]{1,0:T(8,128)(2,1)S(1)}, bf16[32,4096]{1,0:T(8,128)(2,1)S(1)}, u32[]{:S(2)}, u32[]{:S(2)}) collective-permute-start(bf16[32,4096]{1,0:T(8,128)(2,1)S(1)} %shard_map.136.refs_0_), channel_id=1, source_target_pairs={{0,2},{1,3},{2,4},{3,5},{4,6},{5,7},{6,0},{7,1},{8,10},{9,11},{10,... | collective-permute-start | bytes 786440 | tf_op jit(solution)/shard_map/ppermute | solution.py:34
  15.5 8.5 %collective-permute-start.6 = (bf16[32,4096]{1,0:T(8,128)(2,1)S(1)}, bf16[32,4096]{1,0:T(8,128)(2,1)S(1)}, u32[]{:S(2)}, u32[]{:S(2)}) collective-permute-start(bf16[32,4096]{1,0:T(8,128)(2,1)S(1)} %shard_map.140.refs_6_), channel_id=1, source_target_pairs={{0,1},{1,0},{2,3},{3,2},{4,5},{5,4},{6,7},{7,6},{8,9},{9,8},{10,11... | collective-permute-start | bytes 786440 | tf_op jit(solution)/shard_map/ppermute | solution.py:34
  16.1 9.7 %collective-permute-start.5 = (bf16[32,4096]{1,0:T(8,128)(2,1)S(1)}, bf16[32,4096]{1,0:T(8,128)(2,1)S(1)}, u32[]{:S(2)}, u32[]{:S(2)}) collective-permute-start(bf16[32,4096]{1,0:T(8,128)(2,1)S(1)} %shard_map.140.refs_6_), channel_id=1, source_target_pairs={{2,0},{3,1},{4,2},{5,3},{10,8},{11,9},{12,10},{13,11},{18,16},{19,... | collective-permute-start | bytes 786440 | tf_op jit(solution)/shard_map/ppermute | solution.py:34
  20.2 5.6 %collective-permute-start.3 = (bf16[32,4096]{1,0:T(8,128)(2,1)S(1)}, bf16[32,4096]{1,0:T(8,128)(2,1)S(1)}, u32[]{:S(2)}, u32[]{:S(2)}) collective-permute-start(bf16[32,4096]{1,0:T(8,128)(2,1)S(1)} %collective-permute-done.1.refs_2_), channel_id=1, source_target_pairs={{2,4},{3,5},{4,6},{5,7},{10,12},{11,13},{12,14},{13,15},{18,20},{1... | collective-permute-start | bytes 786440 | tf_op jit(solution)/shard_map/ppermute | solution.py:34
  20.9 12.0 %collective-permute-start.2 = (bf16[32,4096]{1,0:T(8,128)(2,1)S(1)}, bf16[32,4096]{1,0:T(8,128)(2,1)S(1)}, u32[]{:S(2)}, u32[]{:S(2)}) collective-permute-start(bf16[32,4096]{1,0:T(8,128)(2,1)S(1)} %collective-permute-done.1.refs_2_), channel_id=1, source_target_pairs={{0,1},{1,0},{2,3},{3,2},{4,5},{5,4},{6,7},{7,6},{8,9},{9,8},{10,11... | collective-permute-start | bytes 786440 | tf_op jit(solution)/shard_map/ppermute | solution.py:34
  25.8 8.5 %collective-permute-start.7 = (bf16[32,4096]{1,0:T(8,128)(2,1)S(1)}, bf16[32,4096]{1,0:T(8,128)(2,1)S(1)}, u32[]{:S(2)}, u32[]{:S(2)}) collective-permute-start(bf16[32,4096]{1,0:T(8,128)(2,1)S(1)} %shard_map.141.refs_0_.refs_4_), channel_id=1, source_target_pairs={{0,1},{1,0},{2,3},{3,2},{4,5},{5,4},{6,7},{7,6},{8,9},{9,8},{10,11... | collective-permute-start | bytes 786440 | tf_op jit(solution)/shard_map/ppermute | solution.py:34
  36.1 4.0 %collective-permute-start.8 = (bf16[128,128]{1,0:T(8,128)(2,1)S(1)}, bf16[128,128]{1,0:T(8,128)(2,1)S(1)}, u32[]{:S(2)}, u32[]{:S(2)}) collective-permute-start(bf16[128,128]{1,0:T(8,128)(2,1)S(1)} %get-tuple-element.59), channel_id=1, source_target_pairs={{0,1},{1,0},{2,3},{3,2},{4,5},{5,4},{6,7},{7,6},{8,9},{9,8},{10,11... | collective-permute-start | bytes 98312 | tf_op jit(solution)/shard_map/ppermute | solution.py:34
  40.1 5.0 %collective-permute-start.10 = (bf16[64,128]{1,0:T(8,128)(2,1)S(1)}, bf16[64,128]{1,0:T(8,128)(2,1)S(1)}, u32[]{:S(2)}, u32[]{:S(2)}) collective-permute-start(bf16[64,128]{1,0:T(8,128)(2,1)S(1)} %get-tuple-element.62), channel_id=1, source_target_pairs={{0,4},{1,5},{2,6},{3,7},{4,0},{5,1},{6,2},{7,3},{8,12},{9,13},{10,... | collective-permute-start | bytes 49160 | tf_op jit(solution)/shard_map/ppermute | solution.py:91
  42.2 5.5 %collective-permute-start.11 = (bf16[64,128]{1,0:T(8,128)(2,1)S(1)}, bf16[64,128]{1,0:T(8,128)(2,1)S(1)}, u32[]{:S(2)}, u32[]{:S(2)}) collective-permute-start(bf16[64,128]{1,0:T(8,128)(2,1)S(1)} %get-tuple-element.63), channel_id=1, source_target_pairs={{0,6},{1,7},{2,4},{3,5},{4,2},{5,3},{6,0},{7,1},{8,14},{9,15},{10,... | collective-permute-start | bytes 49160 | tf_op jit(solution)/shard_map/ppermute | solution.py:91
  49.5 5.2 %collective-permute-start.12 = (bf16[16,4096]{1,0:T(8,128)(2,1)S(1)}, bf16[16,4096]{1,0:T(8,128)(2,1)S(1)}, u32[]{:S(2)}, u32[]{:S(2)}) collective-permute-start(bf16[16,4096]{1,0:T(8,128)(2,1)S(1)} %get-tuple-element.69), channel_id=1, source_target_pairs={{0,1},{1,0},{2,3},{3,2},{4,5},{5,4},{6,7},{7,6},{8,9},{9,8},{10,11... | collective-permute-start | bytes 393224 | tf_op jit(solution)/shard_map/ppermute | solution.py:34
  51.0 5.5 %collective-permute-start.14 = (bf16[16,4096]{1,0:T(8,128)(2,1)S(1)}, bf16[16,4096]{1,0:T(8,128)(2,1)S(1)}, u32[]{:S(2)}, u32[]{:S(2)}) collective-permute-start(bf16[16,4096]{1,0:T(8,128)(2,1)S(1)} %get-tuple-element.71), channel_id=1, source_target_pairs={{0,1},{1,0},{2,3},{3,2},{4,5},{5,4},{6,7},{7,6},{8,9},{9,8},{10,11... | collective-permute-start | bytes 393224 | tf_op jit(solution)/shard_map/ppermute | solution.py:34
  51.5 6.0 %collective-permute-start.16 = (bf16[16,4096]{1,0:T(8,128)(2,1)S(1)}, bf16[16,4096]{1,0:T(8,128)(2,1)S(1)}, u32[]{:S(2)}, u32[]{:S(2)}) collective-permute-start(bf16[16,4096]{1,0:T(8,128)(2,1)S(1)} %get-tuple-element.73), channel_id=1, source_target_pairs={{0,1},{1,0},{2,3},{3,2},{4,5},{5,4},{6,7},{7,6},{8,9},{9,8},{10,11... | collective-permute-start | bytes 393224 | tf_op jit(solution)/shard_map/ppermute | solution.py:34
  53.0 7.5 %collective-permute-start.18 = (bf16[16,4096]{1,0:T(8,128)(2,1)S(1)}, bf16[16,4096]{1,0:T(8,128)(2,1)S(1)}, u32[]{:S(2)}, u32[]{:S(2)}) collective-permute-start(bf16[16,4096]{1,0:T(8,128)(2,1)S(1)} %get-tuple-element.75), channel_id=1, source_target_pairs={{0,1},{1,0},{2,3},{3,2},{4,5},{5,4},{6,7},{7,6},{8,9},{9,8},{10,11... | collective-permute-start | bytes 393224 | tf_op jit(solution)/shard_map/ppermute | solution.py:34
  54.7 7.4 %collective-permute-start.13 = (bf16[16,4096]{1,0:T(8,128)(2,1)S(1)}, bf16[16,4096]{1,0:T(8,128)(2,1)S(1)}, u32[]{:S(2)}, u32[]{:S(2)}) collective-permute-start(bf16[16,4096]{1,0:T(8,128)(2,1)S(1)} %add_convert_fusion.5), channel_id=1, source_target_pairs={{0,4},{1,5},{2,6},{3,7},{4,0},{5,1},{6,2},{7,3},{8,12},{9,13},{10,... | collective-permute-start | bytes 393224 | tf_op jit(solution)/shard_map/ppermute | solution.py:34
  56.5 7.4 %collective-permute-start.15 = (bf16[16,4096]{1,0:T(8,128)(2,1)S(1)}, bf16[16,4096]{1,0:T(8,128)(2,1)S(1)}, u32[]{:S(2)}, u32[]{:S(2)}) collective-permute-start(bf16[16,4096]{1,0:T(8,128)(2,1)S(1)} %add_convert_fusion.4), channel_id=1, source_target_pairs={{0,2},{1,3},{2,4},{3,5},{4,6},{5,7},{6,0},{7,1},{8,10},{9,11},{10,... | collective-permute-start | bytes 393224 | tf_op jit(solution)/shard_map/ppermute | solution.py:34
  57.5 11.1 %collective-permute-start.17 = (bf16[16,4096]{1,0:T(8,128)(2,1)S(1)}, bf16[16,4096]{1,0:T(8,128)(2,1)S(1)}, u32[]{:S(2)}, u32[]{:S(2)}) collective-permute-start(bf16[16,4096]{1,0:T(8,128)(2,1)S(1)} %add_convert_fusion.3), channel_id=1, source_target_pairs={{0,6},{1,7},{2,0},{3,1},{4,2},{5,3},{6,4},{7,5},{8,14},{9,15},{10,... | collective-permute-start | bytes 393224 | tf_op jit(solution)/shard_map/ppermute | solution.py:34
  69.1 7.0 %collective-permute-start.20 = (bf16[16,4096]{1,0:T(8,128)(2,1)S(1)}, bf16[16,4096]{1,0:T(8,128)(2,1)S(1)}, u32[]{:S(2)}, u32[]{:S(2)}) collective-permute-start(bf16[16,4096]{1,0:T(8,128)(2,1)S(1)} %multiply_convert_fusion.refs_0_), channel_id=1, source_target_pairs={{0,2},{1,3},{2,4},{3,5},{4,6},{5,7},{6,0},{7,1},{8,10},{9,11},{10,... | collective-permute-start | bytes 393224 | tf_op jit(solution)/shard_map/ppermute | solution.py:34
  69.9 8.7 %collective-permute-start.22 = (bf16[16,4096]{1,0:T(8,128)(2,1)S(1)}, bf16[16,4096]{1,0:T(8,128)(2,1)S(1)}, u32[]{:S(2)}, u32[]{:S(2)}) collective-permute-start(bf16[16,4096]{1,0:T(8,128)(2,1)S(1)} %multiply_convert_fusion.refs_0_), channel_id=1, source_target_pairs={{0,4},{1,5},{2,6},{3,7},{4,0},{5,1},{6,2},{7,3},{8,12},{9,13},{10,... | collective-permute-start | bytes 393224 | tf_op jit(solution)/shard_map/ppermute | solution.py:34
  71.5 7.0 %collective-permute-start.24 = (bf16[16,4096]{1,0:T(8,128)(2,1)S(1)}, bf16[16,4096]{1,0:T(8,128)(2,1)S(1)}, u32[]{:S(2)}, u32[]{:S(2)}) collective-permute-start(bf16[16,4096]{1,0:T(8,128)(2,1)S(1)} %multiply_convert_fusion.refs_0_), channel_id=1, source_target_pairs={{0,6},{1,7},{2,0},{3,1},{4,2},{5,3},{6,4},{7,5},{8,14},{9,15},{10,... | collective-permute-start | bytes 393224 | tf_op jit(solution)/shard_map/ppermute | solution.py:34
  74.3 10.2 %collective-permute-start.19 = (bf16[16,4096]{1,0:T(8,128)(2,1)S(1)}, bf16[16,4096]{1,0:T(8,128)(2,1)S(1)}, u32[]{:S(2)}, u32[]{:S(2)}) collective-permute-start(bf16[16,4096]{1,0:T(8,128)(2,1)S(1)} %multiply_convert_fusion.refs_0_), channel_id=1, source_target_pairs={{0,1},{1,0},{2,3},{3,2},{4,5},{5,4},{6,7},{7,6},{8,9},{9,8},{10,11... | collective-permute-start | bytes 393224 | tf_op jit(solution)/shard_map/ppermute | solution.py:34
  76.1 8.5 %collective-permute-start.21 = (bf16[16,4096]{1,0:T(8,128)(2,1)S(1)}, bf16[16,4096]{1,0:T(8,128)(2,1)S(1)}, u32[]{:S(2)}, u32[]{:S(2)}) collective-permute-start(bf16[16,4096]{1,0:T(8,128)(2,1)S(1)} %collective-permute-done.20.refs_2_), channel_id=1, source_target_pairs={{0,1},{1,0},{2,3},{3,2},{4,5},{5,4},{6,7},{7,6},{8,9},{9,8},{10,11... | collective-permute-start | bytes 393224 | tf_op jit(solution)/shard_map/ppermute | solution.py:34
  78.5 6.4 %collective-permute-start.23 = (bf16[16,4096]{1,0:T(8,128)(2,1)S(1)}, bf16[16,4096]{1,0:T(8,128)(2,1)S(1)}, u32[]{:S(2)}, u32[]{:S(2)}) collective-permute-start(bf16[16,4096]{1,0:T(8,128)(2,1)S(1)} %collective-permute-done.22.refs_4_), channel_id=1, source_target_pairs={{0,1},{1,0},{2,3},{3,2},{4,5},{5,4},{6,7},{7,6},{8,9},{9,8},{10,11... | collective-permute-start | bytes 393224 | tf_op jit(solution)/shard_map/ppermute | solution.py:34
  78.6 9.2 %collective-permute-start.25 = (bf16[16,4096]{1,0:T(8,128)(2,1)S(1)}, bf16[16,4096]{1,0:T(8,128)(2,1)S(1)}, u32[]{:S(2)}, u32[]{:S(2)}) collective-permute-start(bf16[16,4096]{1,0:T(8,128)(2,1)S(1)} %collective-permute-done.24.refs_6_), channel_id=1, source_target_pairs={{0,1},{1,0},{2,3},{3,2},{4,5},{5,4},{6,7},{7,6},{8,9},{9,8},{10,11... | collective-permute-start | bytes 393224 | tf_op jit(solution)/shard_map/ppermute | solution.py:34
  91.5 5.0 %collective-permute-start.26 = (bf16[16,4096]{1,0:T(8,128)(2,1)S(1)}, bf16[16,4096]{1,0:T(8,128)(2,1)S(1)}, u32[]{:S(2)}, u32[]{:S(2)}) collective-permute-start(bf16[16,4096]{1,0:T(8,128)(2,1)S(1)} %get-tuple-element.80), channel_id=1, source_target_pairs={{0,1},{1,0},{2,3},{3,2},{4,5},{5,4},{6,7},{7,6},{8,9},{9,8},{10,11... | collective-permute-start | bytes 393224 | tf_op jit(solution)/shard_map/ppermute | solution.py:34
  92.4 5.4 %collective-permute-start.28 = (bf16[16,4096]{1,0:T(8,128)(2,1)S(1)}, bf16[16,4096]{1,0:T(8,128)(2,1)S(1)}, u32[]{:S(2)}, u32[]{:S(2)}) collective-permute-start(bf16[16,4096]{1,0:T(8,128)(2,1)S(1)} %get-tuple-element.82), channel_id=1, source_target_pairs={{0,1},{1,0},{2,3},{3,2},{4,5},{5,4},{6,7},{7,6},{8,9},{9,8},{10,11... | collective-permute-start | bytes 393224 | tf_op jit(solution)/shard_map/ppermute | solution.py:34
  93.5 6.6 %collective-permute-start.30 = (bf16[16,4096]{1,0:T(8,128)(2,1)S(1)}, bf16[16,4096]{1,0:T(8,128)(2,1)S(1)}, u32[]{:S(2)}, u32[]{:S(2)}) collective-permute-start(bf16[16,4096]{1,0:T(8,128)(2,1)S(1)} %get-tuple-element.84), channel_id=1, source_target_pairs={{0,1},{1,0},{2,3},{3,2},{4,5},{5,4},{6,7},{7,6},{8,9},{9,8},{10,11... | collective-permute-start | bytes 393224 | tf_op jit(solution)/shard_map/ppermute | solution.py:34
  94.5 8.0 %collective-permute-start.32 = (bf16[16,4096]{1,0:T(8,128)(2,1)S(1)}, bf16[16,4096]{1,0:T(8,128)(2,1)S(1)}, u32[]{:S(2)}, u32[]{:S(2)}) collective-permute-start(bf16[16,4096]{1,0:T(8,128)(2,1)S(1)} %get-tuple-element.86), channel_id=1, source_target_pairs={{0,1},{1,0},{2,3},{3,2},{4,5},{5,4},{6,7},{7,6},{8,9},{9,8},{10,11... | collective-permute-start | bytes 393224 | tf_op jit(solution)/shard_map/ppermute | solution.py:34
  96.5 8.8 %collective-permute-start.27 = (bf16[16,4096]{1,0:T(8,128)(2,1)S(1)}, bf16[16,4096]{1,0:T(8,128)(2,1)S(1)}, u32[]{:S(2)}, u32[]{:S(2)}) collective-permute-start(bf16[16,4096]{1,0:T(8,128)(2,1)S(1)} %add_convert_fusion.2), channel_id=1, source_target_pairs={{0,4},{1,5},{2,6},{3,7},{4,0},{5,1},{6,2},{7,3},{8,12},{9,13},{10,... | collective-permute-start | bytes 393224 | tf_op jit(solution)/shard_map/ppermute | solution.py:34
  97.9 7.4 %collective-permute-start.29 = (bf16[16,4096]{1,0:T(8,128)(2,1)S(1)}, bf16[16,4096]{1,0:T(8,128)(2,1)S(1)}, u32[]{:S(2)}, u32[]{:S(2)}) collective-permute-start(bf16[16,4096]{1,0:T(8,128)(2,1)S(1)} %add_convert_fusion.1), channel_id=1, source_target_pairs={{0,2},{1,3},{2,4},{3,5},{4,6},{5,7},{6,0},{7,1},{8,10},{9,11},{10,... | collective-permute-start | bytes 393224 | tf_op jit(solution)/shard_map/ppermute | solution.py:34
  100.2 6.5 %collective-permute-start.31 = (bf16[16,4096]{1,0:T(8,128)(2,1)S(1)}, bf16[16,4096]{1,0:T(8,128)(2,1)S(1)}, u32[]{:S(2)}, u32[]{:S(2)}) collective-permute-start(bf16[16,4096]{1,0:T(8,128)(2,1)S(1)} %add_convert_fusion), channel_id=1, source_target_pairs={{0,6},{1,7},{2,0},{3,1},{4,2},{5,3},{6,4},{7,5},{8,14},{9,15},{10,... | collective-permute-start | bytes 393224 | tf_op jit(solution)/shard_map/ppermute | solution.py:34
  (6 other events, 118.1 us)

commit v17 on v16

--- a/solution.py
+++ b/solution.py
@@ -84,11 +84,7 @@
     shape = ((parts[0].shape[0] // tall * wide, parts[0].shape[1]), bf16)
     crossed = [parts[0]] + [shift(parts[dy], tall, wide, 0, dy) for dy in range(1, wide)]
     packed = kernel_call(functools.partial(pack_body, tall), [shape] * tall, crossed)
-    pairs = [
-        [(z * wide + y, (z ^ kz) * wide + y) for z in range(tall) for y in range(wide)]
-        for kz in range(tall)
-    ]
-    return [packed[0]] + [lax.ppermute(packed[k], "ctx", pairs[k]) for k in range(1, tall)]
+    return [packed[0]] + [shift(packed[dz], tall, wide, dz, 0) for dz in range(1, tall)]
 
 
 def gather_blocks(block, tall, wide):
@@ -225,8 +221,7 @@
         z, y = divmod(s, wide)
         from_block = lax.rem(my_z - z + tall, tall) * wide + lax.rem(my_y - y + wide, wide)
         to_block = lax.rem(z - my_z + tall, tall) * wide + lax.rem(y - my_y + wide, wide)
-        peer = (my_z ^ z) * wide + lax.rem(my_y + y, wide)
-        lot = (my_z ^ z) * wide + lax.rem(my_y - y + wide, wide)
+        peer = lax.rem(my_z + z, tall) * wide + lax.rem(my_y + y, wide)
         before = where < s * tokens
         first = jnp.sum(jnp.where(before, 1.0, 0.0), axis=1, keepdims=True)
         inside = (where < (s + 1) * tokens) & jnp.logical_not(before)
@@ -234,7 +229,7 @@
         slot += jnp.where(inside, lane - first + start, 0.0)
         place += jnp.where(owner == s, (to_block * share).astype(f32), 0.0)
         out_base += jnp.where(out_block == y * tall + z, heads_of(peer).astype(f32), 0.0)
-        in_base += jnp.where(in_source == s, (lot * (outbound // count)).astype(f32), 0.0)
+        in_base += jnp.where(in_source == s, (from_block * (outbound // count)).astype(f32), 0.0)
     mine = owner == iota((count, total), 0)
     earlier = jnp.where(iota((total, total), 0) < iota((total, total), 1), 1.0, 0.0)
     rank = dot(jnp.where(mine, 1.0, 0.0).astype(bf16), earlier.astype(bf16))

time: 108 us -> 108 us (level)
  waiting for transfers between devices: 34.8 us -> 41.8 us
  starting transfers between devices: 44.1 us -> 37.8 us
    ppermute x30 -> x33, waiting for transfers between devices: 32.2 us -> 41.8 us  [shift(): return lax.ppermute(block, 'ctx', pairs)]
    ppermute x3 -> x0, starting transfers between devices: 4.17 us -> none  [exchange(): lax.ppermute(packed[k], 'ctx', pairs[k])]
    ppermute x3 -> x0, waiting for transfers between devices: 2.66 us -> none  [exchange(): lax.ppermute(packed[k], 'ctx', pairs[k])]
    ppermute x30 -> x33, starting transfers between devices: 39.9 us -> 37.8 us  [shift(): return lax.ppermute(block, 'ctx', pairs)]
  transfers between devices with their start and end apart: 33 -> 33, of which waited for: 18 -> 21; matrix products, arithmetic and copies ran while one was open for 1% -> 1% of each run, Pallas kernels for 16% -> 16%
where the time goes in v17:
time: 108 us
  waiting for transfers between devices  41.8 us (39%)
  starting transfers between devices  37.8 us (35%)
  Pallas kernels  26.3 us (24%)
  other arithmetic  1.91 us (2%)
    ppermute x33, waiting for transfers between devices, shift(): return lax.ppermute(block, 'ctx', pairs)  41.8 us
    ppermute x33, starting transfers between devices, shift(): return lax.ppermute(block, 'ctx', pairs)  37.8 us
    pallas_call x5, Pallas kernels, load(): pl.pallas_call(functools.partial(load_body, len(arrays)), out_shape=[pltp...  15.9 us
    pallas_call x9, Pallas kernels, kernel_call(): pl.pallas_call(body, out_shape=[jax.ShapeDtypeStruct(s, d) for s, d in ou...  10.5 us
  transfers between devices with their start and end apart: 33, of which 21 were waited for; matrix products, arithmetic and copies ran while one was open for 1% of the time, Pallas kernels for 16%

profile of v17, /device:TPU:0, one launch (start us, length us, event | category | flops | bytes accessed | tf_op | source)
XLA Modules:
  0.0 108.2 jit_solution(8690644858898928405)
XLA Ops:
  0.0 1.6 %shard_map.136.refs_0_ = bf16[32,4096]{1,0:T(8,128)(2,1)S(1)} custom-call(s32[1]{0:T(128)} %bitcast.me, s32[1,128]{1,0:T(1,128)} %bitcast.4, bf16[128,4096]{1,0:T(8,128)(2,1)} %activations_in.1), custom_call_target="tpu_custom_call" | custom-call | flops 33554432 | bytes 1048576 | tf_op jit(solution)/shard_map/pallas_call | solution.py:136
  1.6 3.0 %collective-permute-start = (bf16[32,4096]{1,0:T(8,128)(2,1)S(1)}, bf16[32,4096]{1,0:T(8,128)(2,1)S(1)}, u32[]{:S(2)}, u32[]{:S(2)}) collective-permute-start(bf16[32,4096]{1,0:T(8,128)(2,1)S(1)} %shard_map.136.refs_0_), channel_id=1, source_target_pairs={{0,1},{1,0},{2,3},{3,2},{4,5},{5,4},{6,7},{7,6},{8,9},{9,8},{10,11... | collective-permute-start | bytes 786440 | tf_op jit(solution)/shard_map/ppermute | solution.py:34
  4.6 3.6 %collective-permute-start.4 = (bf16[32,4096]{1,0:T(8,128)(2,1)S(1)}, bf16[32,4096]{1,0:T(8,128)(2,1)S(1)}, u32[]{:S(2)}, u32[]{:S(2)}) collective-permute-start(bf16[32,4096]{1,0:T(8,128)(2,1)S(1)} %shard_map.136.refs_0_), channel_id=1, source_target_pairs={{0,6},{1,7},{2,0},{3,1},{4,2},{5,3},{6,4},{7,5},{8,14},{9,15},{10,... | collective-permute-start | bytes 786440 | tf_op jit(solution)/shard_map/ppermute | solution.py:34
  8.2 2.9 %shard_map.137 = (f32[1,4096]{1,0:T(1,128)S(1)}, bf16[4096,128]{1,0:T(8,128)(2,1)S(1)}, bf16[4096,128]{1,0:T(8,128)(2,1)S(1)}, bf16[4096,512]{1,0:T(8,128)(2,1)S(1)}, f32[8,128]{1,0:T(8,128)S(1)}) custom-call(bf16[32,4096]{1,0:T(8,128)(2,1)S(1)} %shard_map.136.refs_0_, f32[1,4096]{1,0:T(1,128)} %bitcast.8, bf16[4096,128]{1,0:T(8,128)(2,1)} %refs_2_.1, ...), custom_call_target="tpu_custom_call" | custom-call | bytes 12615680 | tf_op jit(solution)/shard_map/pallas_call | solution.py:161
  11.1 3.4 %shard_map.138 = (bf16[1024,4096]{1,0:T(8,128)(2,1)S(1)}, f32[8,128]{1,0:T(8,128)S(1)}) custom-call(f32[8,128]{1,0:T(8,128)S(1)} %get-tuple-element.46.refs_0_.refs_1_, bf16[1024,4096]{1,0:T(8,128)(2,1)} %refs_1_.4), custom_call_target="tpu_custom_call" | custom-call | bytes 16777216 | tf_op jit(solution)/shard_map/pallas_call | solution.py:161
  17.3 2.8 %collective-permute-done.1.refs_2_ = bf16[32,4096]{1,0:T(8,128)(2,1)S(1)} collective-permute-done((bf16[32,4096]{1,0:T(8,128)(2,1)S(1)}, bf16[32,4096]{1,0:T(8,128)(2,1)S(1)}, u32[]{:S(2)}, u32[]{:S(2)}) %collective-permute-start.1) | collective-permute-done | bytes 262176 | tf_op jit(solution)/shard_map/ppermute | solution.py:34
  21.3 2.6 %collective-permute-done.6.refs_2_.refs_7_ = bf16[32,4096]{1,0:T(8,128)(2,1)S(1)} collective-permute-done((bf16[32,4096]{1,0:T(8,128)(2,1)S(1)}, bf16[32,4096]{1,0:T(8,128)(2,1)S(1)}, u32[]{:S(2)}, u32[]{:S(2)}) %collective-permute-start.6) | collective-permute-done | bytes 262176 | tf_op jit(solution)/shard_map/ppermute | solution.py:34
  24.0 1.8 %collective-permute-done.5.refs_1_ = bf16[32,4096]{1,0:T(8,128)(2,1)S(1)} collective-permute-done((bf16[32,4096]{1,0:T(8,128)(2,1)S(1)}, bf16[32,4096]{1,0:T(8,128)(2,1)S(1)}, u32[]{:S(2)}, u32[]{:S(2)}) %collective-permute-start.5) | collective-permute-done | bytes 262176 | tf_op jit(solution)/shard_map/ppermute | solution.py:34
  27.2 3.4 %shard_map.143 = (bf16[4096,1024]{1,0:T(8,128)(2,1)S(1)}, f32[8,128]{1,0:T(8,128)S(1)}) custom-call(bf16[32,4096]{1,0:T(8,128)(2,1)S(1)} %shard_map.141.refs_0_.refs_4_, bf16[4096,1024]{1,0:T(8,128)(2,1)} %refs_1_.6), custom_call_target="tpu_custom_call" | custom-call | bytes 16777216 | tf_op jit(solution)/shard_map/pallas_call | solution.py:161
  30.6 2.2 %shard_map.142 = (bf16[512,4096]{1,0:T(8,128)(2,1)S(1)}, f32[8,128]{1,0:T(8,128)S(1)}) custom-call(bf16[32,4096]{1,0:T(8,128)(2,1)S(1)} %shard_map.141.refs_0_.refs_4_, bf16[512,4096]{1,0:T(8,128)(2,1)} %refs_1_.5), custom_call_target="tpu_custom_call" | custom-call | bytes 8388608 | tf_op jit(solution)/shard_map/pallas_call | solution.py:161
  34.3 1.8 %shard_map.144 = (bf16[128,4096]{1,0:T(8,128)(2,1)S(1)}, bf16[16,4096]{1,0:T(8,128)(2,1)S(1)}, bf16[128,128]{1,0:T(8,128)(2,1)S(1)}, bf16[128,128]{1,0:T(8,128)(2,1)S(1)}) custom-call(bf16[32,4096]{1,0:T(8,128)(2,1)S(1)} %shard_map.136.refs_0_, bf16[32,4096]{1,0:T(8,128)(2,1)S(1)} %collective-permute-done.refs_4_.refs_1_, ...), custom_call_target="tpu_custom_call" | custom-call | flops 536870912 | bytes 1048576 | tf_op jit(solution)/shard_map/pallas_call | solution.py:136
  36.7 3.3 %collective-permute-done.8.refs_1_ = bf16[128,128]{1,0:T(8,128)(2,1)S(1)} collective-permute-done((bf16[128,128]{1,0:T(8,128)(2,1)S(1)}, bf16[128,128]{1,0:T(8,128)(2,1)S(1)}, u32[]{:S(2)}, u32[]{:S(2)}) %collective-permute-start.8) | collective-permute-done | bytes 32800 | tf_op jit(solution)/shard_map/ppermute | solution.py:34
  40.1 2.1 %collective-permute-start.10 = (bf16[64,128]{1,0:T(8,128)(2,1)S(1)}, bf16[64,128]{1,0:T(8,128)(2,1)S(1)}, u32[]{:S(2)}, u32[]{:S(2)}) collective-permute-start(bf16[64,128]{1,0:T(8,128)(2,1)S(1)} %get-tuple-element.62), channel_id=1, source_target_pairs={{0,4},{1,5},{2,6},{3,7},{4,0},{5,1},{6,2},{7,3},{8,12},{9,13},{10,... | collective-permute-start | bytes 49160 | tf_op jit(solution)/shard_map/ppermute | solution.py:34
  42.2 1.6 %collective-permute-start.11 = (bf16[64,128]{1,0:T(8,128)(2,1)S(1)}, bf16[64,128]{1,0:T(8,128)(2,1)S(1)}, u32[]{:S(2)}, u32[]{:S(2)}) collective-permute-start(bf16[64,128]{1,0:T(8,128)(2,1)S(1)} %get-tuple-element.63), channel_id=1, source_target_pairs={{0,6},{1,7},{2,0},{3,1},{4,2},{5,3},{6,4},{7,5},{8,14},{9,15},{10,... | collective-permute-start | bytes 49160 | tf_op jit(solution)/shard_map/ppermute | solution.py:34
  45.9 3.4 %collective-permute-done.9.refs_1_ = bf16[64,128]{1,0:T(8,128)(2,1)S(1)} collective-permute-done((bf16[64,128]{1,0:T(8,128)(2,1)S(1)}, bf16[64,128]{1,0:T(8,128)(2,1)S(1)}, u32[]{:S(2)}, u32[]{:S(2)}) %collective-permute-start.9) | collective-permute-done | bytes 16416 | tf_op jit(solution)/shard_map/ppermute | solution.py:34
  49.3 1.7 %shard_map.147 = (bf16[16,4096]{1,0:T(8,128)(2,1)S(1)}, bf16[16,4096]{1,0:T(8,128)(2,1)S(1)}, bf16[16,4096]{1,0:T(8,128)(2,1)S(1)}, bf16[16,4096]{1,0:T(8,128)(2...) custom-call(bf16[64,128]{1,0:T(8,128)(2,1)S(1)} %get-tuple-element.6, ...), custom_call_target="tpu_custom_call" | custom-call | flops 536870912 | bytes 1048576 | tf_op jit(solution)/shard_map/pallas_call | solution.py:136
  59.3 2.6 %collective-permute-start.17 = (bf16[16,4096]{1,0:T(8,128)(2,1)S(1)}, bf16[16,4096]{1,0:T(8,128)(2,1)S(1)}, u32[]{:S(2)}, u32[]{:S(2)}) collective-permute-start(bf16[16,4096]{1,0:T(8,128)(2,1)S(1)} %add_convert_fusion.3), channel_id=1, source_target_pairs={{0,6},{1,7},{2,0},{3,1},{4,2},{5,3},{6,4},{7,5},{8,14},{9,15},{10,... | collective-permute-start | bytes 393224 | tf_op jit(solution)/shard_map/ppermute | solution.py:34
  62.4 3.3 %collective-permute-done.15 = bf16[16,4096]{1,0:T(8,128)(2,1)S(1)} collective-permute-done((bf16[16,4096]{1,0:T(8,128)(2,1)S(1)}, bf16[16,4096]{1,0:T(8,128)(2,1)S(1)}, u32[]{:S(2)}, u32[]{:S(2)}) %collective-permute-start.15) | collective-permute-done | bytes 131104 | tf_op jit(solution)/shard_map/ppermute | solution.py:34
  65.7 3.6 %collective-permute-done.17 = bf16[16,4096]{1,0:T(8,128)(2,1)S(1)} collective-permute-done((bf16[16,4096]{1,0:T(8,128)(2,1)S(1)}, bf16[16,4096]{1,0:T(8,128)(2,1)S(1)}, u32[]{:S(2)}, u32[]{:S(2)}) %collective-permute-start.17) | collective-permute-done | bytes 131104 | tf_op jit(solution)/shard_map/ppermute | solution.py:34
  69.7 1.5 %collective-permute-start.20 = (bf16[16,4096]{1,0:T(8,128)(2,1)S(1)}, bf16[16,4096]{1,0:T(8,128)(2,1)S(1)}, u32[]{:S(2)}, u32[]{:S(2)}) collective-permute-start(bf16[16,4096]{1,0:T(8,128)(2,1)S(1)} %multiply_convert_fusion.refs_0_), channel_id=1, source_target_pairs={{0,2},{1,3},{2,4},{3,5},{4,6},{5,7},{6,0},{7,1},{8,10},{9,11},{10,... | collective-permute-start | bytes 393224 | tf_op jit(solution)/shard_map/ppermute | solution.py:34
  71.2 2.8 %collective-permute-start.24 = (bf16[16,4096]{1,0:T(8,128)(2,1)S(1)}, bf16[16,4096]{1,0:T(8,128)(2,1)S(1)}, u32[]{:S(2)}, u32[]{:S(2)}) collective-permute-start(bf16[16,4096]{1,0:T(8,128)(2,1)S(1)} %multiply_convert_fusion.refs_0_), channel_id=1, source_target_pairs={{0,6},{1,7},{2,0},{3,1},{4,2},{5,3},{6,4},{7,5},{8,14},{9,15},{10,... | collective-permute-start | bytes 393224 | tf_op jit(solution)/shard_map/ppermute | solution.py:34
  74.5 2.2 %collective-permute-done.20.refs_2_ = bf16[16,4096]{1,0:T(8,128)(2,1)S(1)} collective-permute-done((bf16[16,4096]{1,0:T(8,128)(2,1)S(1)}, bf16[16,4096]{1,0:T(8,128)(2,1)S(1)}, u32[]{:S(2)}, u32[]{:S(2)}) %collective-permute-start.20) | collective-permute-done | bytes 131104 | tf_op jit(solution)/shard_map/ppermute | solution.py:34
  77.1 2.3 %collective-permute-done.22.refs_4_ = bf16[16,4096]{1,0:T(8,128)(2,1)S(1)} collective-permute-done((bf16[16,4096]{1,0:T(8,128)(2,1)S(1)}, bf16[16,4096]{1,0:T(8,128)(2,1)S(1)}, u32[]{:S(2)}, u32[]{:S(2)}) %collective-permute-start.22) | collective-permute-done | bytes 131104 | tf_op jit(solution)/shard_map/ppermute | solution.py:34
  79.7 1.7 %collective-permute-start.25 = (bf16[16,4096]{1,0:T(8,128)(2,1)S(1)}, bf16[16,4096]{1,0:T(8,128)(2,1)S(1)}, u32[]{:S(2)}, u32[]{:S(2)}) collective-permute-start(bf16[16,4096]{1,0:T(8,128)(2,1)S(1)} %collective-permute-done.24.refs_6_), channel_id=1, source_target_pairs={{0,1},{1,0},{2,3},{3,2},{4,5},{5,4},{6,7},{7,6},{8,9},{9,8},{10,11... | collective-permute-start | bytes 393224 | tf_op jit(solution)/shard_map/ppermute | solution.py:34
  81.4 4.0 %shard_map.148 = (bf16[4096,1024]{1,0:T(8,128)(2,1)S(1)}, f32[8,128]{1,0:T(8,128)}) custom-call(bf16[16,4096]{1,0:T(8,128)(2,1)S(1)} %multiply_convert_fusion.refs_0_, bf16[4096,1024]{1,0:T(8,128)(2,1)} %refs_1_.7), custom_call_target="tpu_custom_call" | custom-call | bytes 16777216 | tf_op jit(solution)/shard_map/pallas_call | solution.py:161
  85.8 2.8 %collective-permute-done.25.refs_7_ = bf16[16,4096]{1,0:T(8,128)(2,1)S(1)} collective-permute-done((bf16[16,4096]{1,0:T(8,128)(2,1)S(1)}, bf16[16,4096]{1,0:T(8,128)(2,1)S(1)}, u32[]{:S(2)}, u32[]{:S(2)}) %collective-permute-start.25) | collective-permute-done | bytes 131104 | tf_op jit(solution)/shard_map/ppermute | solution.py:34
  88.6 3.7 %shard_map.149 = (bf16[16,4096]{1,0:T(8,128)(2,1)S(1)}, bf16[16,4096]{1,0:T(8,128)(2,1)S(1)}, bf16[16,4096]{1,0:T(8,128)(2,1)S(1)}, bf16[16,4096]{1,0:T(8,128)(2...) custom-call(bf16[16,4096]{1,0:T(8,128)(2,1)S(1)} %multiply_convert_f, ...), custom_call_target="tpu_custom_call" | custom-call | flops 3221225472 | bytes 1048576 | tf_op jit(solution)/shard_map/pallas_call | solution.py:136
  92.6 1.7 %collective-permute-start.28 = (bf16[16,4096]{1,0:T(8,128)(2,1)S(1)}, bf16[16,4096]{1,0:T(8,128)(2,1)S(1)}, u32[]{:S(2)}, u32[]{:S(2)}) collective-permute-start(bf16[16,4096]{1,0:T(8,128)(2,1)S(1)} %get-tuple-element.82), channel_id=1, source_target_pairs={{0,1},{1,0},{2,3},{3,2},{4,5},{5,4},{6,7},{7,6},{8,9},{9,8},{10,11... | collective-permute-start | bytes 393224 | tf_op jit(solution)/shard_map/ppermute | solution.py:34
  94.7 1.7 %collective-permute-start.32 = (bf16[16,4096]{1,0:T(8,128)(2,1)S(1)}, bf16[16,4096]{1,0:T(8,128)(2,1)S(1)}, u32[]{:S(2)}, u32[]{:S(2)}) collective-permute-start(bf16[16,4096]{1,0:T(8,128)(2,1)S(1)} %get-tuple-element.86), channel_id=1, source_target_pairs={{0,1},{1,0},{2,3},{3,2},{4,5},{5,4},{6,7},{7,6},{8,9},{9,8},{10,11... | collective-permute-start | bytes 393224 | tf_op jit(solution)/shard_map/ppermute | solution.py:34
  98.7 2.2 %collective-permute-start.29 = (bf16[16,4096]{1,0:T(8,128)(2,1)S(1)}, bf16[16,4096]{1,0:T(8,128)(2,1)S(1)}, u32[]{:S(2)}, u32[]{:S(2)}) collective-permute-start(bf16[16,4096]{1,0:T(8,128)(2,1)S(1)} %add_convert_fusion.1), channel_id=1, source_target_pairs={{0,2},{1,3},{2,4},{3,5},{4,6},{5,7},{6,0},{7,1},{8,10},{9,11},{10,... | collective-permute-start | bytes 393224 | tf_op jit(solution)/shard_map/ppermute | solution.py:34
  100.9 2.1 %collective-permute-start.31 = (bf16[16,4096]{1,0:T(8,128)(2,1)S(1)}, bf16[16,4096]{1,0:T(8,128)(2,1)S(1)}, u32[]{:S(2)}, u32[]{:S(2)}) collective-permute-start(bf16[16,4096]{1,0:T(8,128)(2,1)S(1)} %add_convert_fusion), channel_id=1, source_target_pairs={{0,6},{1,7},{2,0},{3,1},{4,2},{5,3},{6,4},{7,5},{8,14},{9,15},{10,... | collective-permute-start | bytes 393224 | tf_op jit(solution)/shard_map/ppermute | solution.py:34
  103.0 3.1 %collective-permute-done.27 = bf16[16,4096]{1,0:T(8,128)(2,1)S(1)} collective-permute-done((bf16[16,4096]{1,0:T(8,128)(2,1)S(1)}, bf16[16,4096]{1,0:T(8,128)(2,1)S(1)}, u32[]{:S(2)}, u32[]{:S(2)}) %collective-permute-start.27) | collective-permute-done | bytes 131104 | tf_op jit(solution)/shard_map/ppermute | solution.py:34
  (73 shorter events, 25.6 us)
Async XLA Ops:
  1.6 13.8 %collective-permute-start = (bf16[32,4096]{1,0:T(8,128)(2,1)S(1)}, bf16[32,4096]{1,0:T(8,128)(2,1)S(1)}, u32[]{:S(2)}, u32[]{:S(2)}) collective-permute-start(bf16[32,4096]{1,0:T(8,128)(2,1)S(1)} %shard_map.136.refs_0_), channel_id=1, source_target_pairs={{0,1},{1,0},{2,3},{3,2},{4,5},{5,4},{6,7},{7,6},{8,9},{9,8},{10,11... | collective-permute-start | bytes 786440 | tf_op jit(solution)/shard_map/ppermute | solution.py:34
  4.6 10.8 %collective-permute-start.4 = (bf16[32,4096]{1,0:T(8,128)(2,1)S(1)}, bf16[32,4096]{1,0:T(8,128)(2,1)S(1)}, u32[]{:S(2)}, u32[]{:S(2)}) collective-permute-start(bf16[32,4096]{1,0:T(8,128)(2,1)S(1)} %shard_map.136.refs_0_), channel_id=1, source_target_pairs={{0,6},{1,7},{2,0},{3,1},{4,2},{5,3},{6,4},{7,5},{8,14},{9,15},{10,... | collective-permute-start | bytes 786440 | tf_op jit(solution)/shard_map/ppermute | solution.py:34
  8.2 12.0 %collective-permute-start.1 = (bf16[32,4096]{1,0:T(8,128)(2,1)S(1)}, bf16[32,4096]{1,0:T(8,128)(2,1)S(1)}, u32[]{:S(2)}, u32[]{:S(2)}) collective-permute-start(bf16[32,4096]{1,0:T(8,128)(2,1)S(1)} %shard_map.136.refs_0_), channel_id=1, source_target_pairs={{0,2},{1,3},{2,4},{3,5},{4,6},{5,7},{6,0},{7,1},{8,10},{9,11},{10,... | collective-permute-start | bytes 786440 | tf_op jit(solution)/shard_map/ppermute | solution.py:34
  15.5 8.5 %collective-permute-start.6 = (bf16[32,4096]{1,0:T(8,128)(2,1)S(1)}, bf16[32,4096]{1,0:T(8,128)(2,1)S(1)}, u32[]{:S(2)}, u32[]{:S(2)}) collective-permute-start(bf16[32,4096]{1,0:T(8,128)(2,1)S(1)} %shard_map.140.refs_6_), channel_id=1, source_target_pairs={{0,1},{1,0},{2,3},{3,2},{4,5},{5,4},{6,7},{7,6},{8,9},{9,8},{10,11... | collective-permute-start | bytes 786440 | tf_op jit(solution)/shard_map/ppermute | solution.py:34
  16.1 9.7 %collective-permute-start.5 = (bf16[32,4096]{1,0:T(8,128)(2,1)S(1)}, bf16[32,4096]{1,0:T(8,128)(2,1)S(1)}, u32[]{:S(2)}, u32[]{:S(2)}) collective-permute-start(bf16[32,4096]{1,0:T(8,128)(2,1)S(1)} %shard_map.140.refs_6_), channel_id=1, source_target_pairs={{2,0},{3,1},{4,2},{5,3},{10,8},{11,9},{12,10},{13,11},{18,16},{19,... | collective-permute-start | bytes 786440 | tf_op jit(solution)/shard_map/ppermute | solution.py:34
  20.2 5.6 %collective-permute-start.3 = (bf16[32,4096]{1,0:T(8,128)(2,1)S(1)}, bf16[32,4096]{1,0:T(8,128)(2,1)S(1)}, u32[]{:S(2)}, u32[]{:S(2)}) collective-permute-start(bf16[32,4096]{1,0:T(8,128)(2,1)S(1)} %collective-permute-done.1.refs_2_), channel_id=1, source_target_pairs={{2,4},{3,5},{4,6},{5,7},{10,12},{11,13},{12,14},{13,15},{18,20},{1... | collective-permute-start | bytes 786440 | tf_op jit(solution)/shard_map/ppermute | solution.py:34
  20.9 12.0 %collective-permute-start.2 = (bf16[32,4096]{1,0:T(8,128)(2,1)S(1)}, bf16[32,4096]{1,0:T(8,128)(2,1)S(1)}, u32[]{:S(2)}, u32[]{:S(2)}) collective-permute-start(bf16[32,4096]{1,0:T(8,128)(2,1)S(1)} %collective-permute-done.1.refs_2_), channel_id=1, source_target_pairs={{0,1},{1,0},{2,3},{3,2},{4,5},{5,4},{6,7},{7,6},{8,9},{9,8},{10,11... | collective-permute-start | bytes 786440 | tf_op jit(solution)/shard_map/ppermute | solution.py:34
  25.8 8.5 %collective-permute-start.7 = (bf16[32,4096]{1,0:T(8,128)(2,1)S(1)}, bf16[32,4096]{1,0:T(8,128)(2,1)S(1)}, u32[]{:S(2)}, u32[]{:S(2)}) collective-permute-start(bf16[32,4096]{1,0:T(8,128)(2,1)S(1)} %shard_map.141.refs_0_.refs_4_), channel_id=1, source_target_pairs={{0,1},{1,0},{2,3},{3,2},{4,5},{5,4},{6,7},{7,6},{8,9},{9,8},{10,11... | collective-permute-start | bytes 786440 | tf_op jit(solution)/shard_map/ppermute | solution.py:34
  36.1 4.0 %collective-permute-start.8 = (bf16[128,128]{1,0:T(8,128)(2,1)S(1)}, bf16[128,128]{1,0:T(8,128)(2,1)S(1)}, u32[]{:S(2)}, u32[]{:S(2)}) collective-permute-start(bf16[128,128]{1,0:T(8,128)(2,1)S(1)} %get-tuple-element.59), channel_id=1, source_target_pairs={{0,1},{1,0},{2,3},{3,2},{4,5},{5,4},{6,7},{7,6},{8,9},{9,8},{10,11... | collective-permute-start | bytes 98312 | tf_op jit(solution)/shard_map/ppermute | solution.py:34
  40.1 5.0 %collective-permute-start.10 = (bf16[64,128]{1,0:T(8,128)(2,1)S(1)}, bf16[64,128]{1,0:T(8,128)(2,1)S(1)}, u32[]{:S(2)}, u32[]{:S(2)}) collective-permute-start(bf16[64,128]{1,0:T(8,128)(2,1)S(1)} %get-tuple-element.62), channel_id=1, source_target_pairs={{0,4},{1,5},{2,6},{3,7},{4,0},{5,1},{6,2},{7,3},{8,12},{9,13},{10,... | collective-permute-start | bytes 49160 | tf_op jit(solution)/shard_map/ppermute | solution.py:34
  43.8 5.5 %collective-permute-start.9 = (bf16[64,128]{1,0:T(8,128)(2,1)S(1)}, bf16[64,128]{1,0:T(8,128)(2,1)S(1)}, u32[]{:S(2)}, u32[]{:S(2)}) collective-permute-start(bf16[64,128]{1,0:T(8,128)(2,1)S(1)} %get-tuple-element.61), channel_id=1, source_target_pairs={{0,2},{1,3},{2,4},{3,5},{4,6},{5,7},{6,0},{7,1},{8,10},{9,11},{10,... | collective-permute-start | bytes 49160 | tf_op jit(solution)/shard_map/ppermute | solution.py:34
  51.0 5.4 %collective-permute-start.12 = (bf16[16,4096]{1,0:T(8,128)(2,1)S(1)}, bf16[16,4096]{1,0:T(8,128)(2,1)S(1)}, u32[]{:S(2)}, u32[]{:S(2)}) collective-permute-start(bf16[16,4096]{1,0:T(8,128)(2,1)S(1)} %get-tuple-element.69), channel_id=1, source_target_pairs={{0,1},{1,0},{2,3},{3,2},{4,5},{5,4},{6,7},{7,6},{8,9},{9,8},{10,11... | collective-permute-start | bytes 393224 | tf_op jit(solution)/shard_map/ppermute | solution.py:34
  51.7 6.1 %collective-permute-start.14 = (bf16[16,4096]{1,0:T(8,128)(2,1)S(1)}, bf16[16,4096]{1,0:T(8,128)(2,1)S(1)}, u32[]{:S(2)}, u32[]{:S(2)}) collective-permute-start(bf16[16,4096]{1,0:T(8,128)(2,1)S(1)} %get-tuple-element.71), channel_id=1, source_target_pairs={{0,1},{1,0},{2,3},{3,2},{4,5},{5,4},{6,7},{7,6},{8,9},{9,8},{10,11... | collective-permute-start | bytes 393224 | tf_op jit(solution)/shard_map/ppermute | solution.py:34
  53.1 6.1 %collective-permute-start.16 = (bf16[16,4096]{1,0:T(8,128)(2,1)S(1)}, bf16[16,4096]{1,0:T(8,128)(2,1)S(1)}, u32[]{:S(2)}, u32[]{:S(2)}) collective-permute-start(bf16[16,4096]{1,0:T(8,128)(2,1)S(1)} %get-tuple-element.73), channel_id=1, source_target_pairs={{0,1},{1,0},{2,3},{3,2},{4,5},{5,4},{6,7},{7,6},{8,9},{9,8},{10,11... | collective-permute-start | bytes 393224 | tf_op jit(solution)/shard_map/ppermute | solution.py:34
  53.7 8.1 %collective-permute-start.18 = (bf16[16,4096]{1,0:T(8,128)(2,1)S(1)}, bf16[16,4096]{1,0:T(8,128)(2,1)S(1)}, u32[]{:S(2)}, u32[]{:S(2)}) collective-permute-start(bf16[16,4096]{1,0:T(8,128)(2,1)S(1)} %get-tuple-element.75), channel_id=1, source_target_pairs={{0,1},{1,0},{2,3},{3,2},{4,5},{5,4},{6,7},{7,6},{8,9},{9,8},{10,11... | collective-permute-start | bytes 393224 | tf_op jit(solution)/shard_map/ppermute | solution.py:34
  56.5 5.9 %collective-permute-start.13 = (bf16[16,4096]{1,0:T(8,128)(2,1)S(1)}, bf16[16,4096]{1,0:T(8,128)(2,1)S(1)}, u32[]{:S(2)}, u32[]{:S(2)}) collective-permute-start(bf16[16,4096]{1,0:T(8,128)(2,1)S(1)} %add_convert_fusion.5), channel_id=1, source_target_pairs={{0,4},{1,5},{2,6},{3,7},{4,0},{5,1},{6,2},{7,3},{8,12},{9,13},{10,... | collective-permute-start | bytes 393224 | tf_op jit(solution)/shard_map/ppermute | solution.py:34
  57.9 7.9 %collective-permute-start.15 = (bf16[16,4096]{1,0:T(8,128)(2,1)S(1)}, bf16[16,4096]{1,0:T(8,128)(2,1)S(1)}, u32[]{:S(2)}, u32[]{:S(2)}) collective-permute-start(bf16[16,4096]{1,0:T(8,128)(2,1)S(1)} %add_convert_fusion.4), channel_id=1, source_target_pairs={{0,2},{1,3},{2,4},{3,5},{4,6},{5,7},{6,0},{7,1},{8,10},{9,11},{10,... | collective-permute-start | bytes 393224 | tf_op jit(solution)/shard_map/ppermute | solution.py:34
  59.3 10.0 %collective-permute-start.17 = (bf16[16,4096]{1,0:T(8,128)(2,1)S(1)}, bf16[16,4096]{1,0:T(8,128)(2,1)S(1)}, u32[]{:S(2)}, u32[]{:S(2)}) collective-permute-start(bf16[16,4096]{1,0:T(8,128)(2,1)S(1)} %add_convert_fusion.3), channel_id=1, source_target_pairs={{0,6},{1,7},{2,0},{3,1},{4,2},{5,3},{6,4},{7,5},{8,14},{9,15},{10,... | collective-permute-start | bytes 393224 | tf_op jit(solution)/shard_map/ppermute | solution.py:34
  69.7 7.0 %collective-permute-start.20 = (bf16[16,4096]{1,0:T(8,128)(2,1)S(1)}, bf16[16,4096]{1,0:T(8,128)(2,1)S(1)}, u32[]{:S(2)}, u32[]{:S(2)}) collective-permute-start(bf16[16,4096]{1,0:T(8,128)(2,1)S(1)} %multiply_convert_fusion.refs_0_), channel_id=1, source_target_pairs={{0,2},{1,3},{2,4},{3,5},{4,6},{5,7},{6,0},{7,1},{8,10},{9,11},{10,... | collective-permute-start | bytes 393224 | tf_op jit(solution)/shard_map/ppermute | solution.py:34
  71.2 8.1 %collective-permute-start.22 = (bf16[16,4096]{1,0:T(8,128)(2,1)S(1)}, bf16[16,4096]{1,0:T(8,128)(2,1)S(1)}, u32[]{:S(2)}, u32[]{:S(2)}) collective-permute-start(bf16[16,4096]{1,0:T(8,128)(2,1)S(1)} %multiply_convert_fusion.refs_0_), channel_id=1, source_target_pairs={{0,4},{1,5},{2,6},{3,7},{4,0},{5,1},{6,2},{7,3},{8,12},{9,13},{10,... | collective-permute-start | bytes 393224 | tf_op jit(solution)/shard_map/ppermute | solution.py:34
  71.2 8.4 %collective-permute-start.24 = (bf16[16,4096]{1,0:T(8,128)(2,1)S(1)}, bf16[16,4096]{1,0:T(8,128)(2,1)S(1)}, u32[]{:S(2)}, u32[]{:S(2)}) collective-permute-start(bf16[16,4096]{1,0:T(8,128)(2,1)S(1)} %multiply_convert_fusion.refs_0_), channel_id=1, source_target_pairs={{0,6},{1,7},{2,0},{3,1},{4,2},{5,3},{6,4},{7,5},{8,14},{9,15},{10,... | collective-permute-start | bytes 393224 | tf_op jit(solution)/shard_map/ppermute | solution.py:34
  74.0 11.3 %collective-permute-start.19 = (bf16[16,4096]{1,0:T(8,128)(2,1)S(1)}, bf16[16,4096]{1,0:T(8,128)(2,1)S(1)}, u32[]{:S(2)}, u32[]{:S(2)}) collective-permute-start(bf16[16,4096]{1,0:T(8,128)(2,1)S(1)} %multiply_convert_fusion.refs_0_), channel_id=1, source_target_pairs={{0,1},{1,0},{2,3},{3,2},{4,5},{5,4},{6,7},{7,6},{8,9},{9,8},{10,11... | collective-permute-start | bytes 393224 | tf_op jit(solution)/shard_map/ppermute | solution.py:34
  76.7 8.7 %collective-permute-start.21 = (bf16[16,4096]{1,0:T(8,128)(2,1)S(1)}, bf16[16,4096]{1,0:T(8,128)(2,1)S(1)}, u32[]{:S(2)}, u32[]{:S(2)}) collective-permute-start(bf16[16,4096]{1,0:T(8,128)(2,1)S(1)} %collective-permute-done.20.refs_2_), channel_id=1, source_target_pairs={{0,1},{1,0},{2,3},{3,2},{4,5},{5,4},{6,7},{7,6},{8,9},{9,8},{10,11... | collective-permute-start | bytes 393224 | tf_op jit(solution)/shard_map/ppermute | solution.py:34
  79.3 6.4 %collective-permute-start.23 = (bf16[16,4096]{1,0:T(8,128)(2,1)S(1)}, bf16[16,4096]{1,0:T(8,128)(2,1)S(1)}, u32[]{:S(2)}, u32[]{:S(2)}) collective-permute-start(bf16[16,4096]{1,0:T(8,128)(2,1)S(1)} %collective-permute-done.22.refs_4_), channel_id=1, source_target_pairs={{0,1},{1,0},{2,3},{3,2},{4,5},{5,4},{6,7},{7,6},{8,9},{9,8},{10,11... | collective-permute-start | bytes 393224 | tf_op jit(solution)/shard_map/ppermute | solution.py:34
  79.7 8.9 %collective-permute-start.25 = (bf16[16,4096]{1,0:T(8,128)(2,1)S(1)}, bf16[16,4096]{1,0:T(8,128)(2,1)S(1)}, u32[]{:S(2)}, u32[]{:S(2)}) collective-permute-start(bf16[16,4096]{1,0:T(8,128)(2,1)S(1)} %collective-permute-done.24.refs_6_), channel_id=1, source_target_pairs={{0,1},{1,0},{2,3},{3,2},{4,5},{5,4},{6,7},{7,6},{8,9},{9,8},{10,11... | collective-permute-start | bytes 393224 | tf_op jit(solution)/shard_map/ppermute | solution.py:34
  92.2 5.0 %collective-permute-start.26 = (bf16[16,4096]{1,0:T(8,128)(2,1)S(1)}, bf16[16,4096]{1,0:T(8,128)(2,1)S(1)}, u32[]{:S(2)}, u32[]{:S(2)}) collective-permute-start(bf16[16,4096]{1,0:T(8,128)(2,1)S(1)} %get-tuple-element.80), channel_id=1, source_target_pairs={{0,1},{1,0},{2,3},{3,2},{4,5},{5,4},{6,7},{7,6},{8,9},{9,8},{10,11... | collective-permute-start | bytes 393224 | tf_op jit(solution)/shard_map/ppermute | solution.py:34
  92.6 6.0 %collective-permute-start.28 = (bf16[16,4096]{1,0:T(8,128)(2,1)S(1)}, bf16[16,4096]{1,0:T(8,128)(2,1)S(1)}, u32[]{:S(2)}, u32[]{:S(2)}) collective-permute-start(bf16[16,4096]{1,0:T(8,128)(2,1)S(1)} %get-tuple-element.82), channel_id=1, source_target_pairs={{0,1},{1,0},{2,3},{3,2},{4,5},{5,4},{6,7},{7,6},{8,9},{9,8},{10,11... | collective-permute-start | bytes 393224 | tf_op jit(solution)/shard_map/ppermute | solution.py:34
  94.3 6.6 %collective-permute-start.30 = (bf16[16,4096]{1,0:T(8,128)(2,1)S(1)}, bf16[16,4096]{1,0:T(8,128)(2,1)S(1)}, u32[]{:S(2)}, u32[]{:S(2)}) collective-permute-start(bf16[16,4096]{1,0:T(8,128)(2,1)S(1)} %get-tuple-element.84), channel_id=1, source_target_pairs={{0,1},{1,0},{2,3},{3,2},{4,5},{5,4},{6,7},{7,6},{8,9},{9,8},{10,11... | collective-permute-start | bytes 393224 | tf_op jit(solution)/shard_map/ppermute | solution.py:34
  94.7 8.4 %collective-permute-start.32 = (bf16[16,4096]{1,0:T(8,128)(2,1)S(1)}, bf16[16,4096]{1,0:T(8,128)(2,1)S(1)}, u32[]{:S(2)}, u32[]{:S(2)}) collective-permute-start(bf16[16,4096]{1,0:T(8,128)(2,1)S(1)} %get-tuple-element.86), channel_id=1, source_target_pairs={{0,1},{1,0},{2,3},{3,2},{4,5},{5,4},{6,7},{7,6},{8,9},{9,8},{10,11... | collective-permute-start | bytes 393224 | tf_op jit(solution)/shard_map/ppermute | solution.py:34
  97.3 8.8 %collective-permute-start.27 = (bf16[16,4096]{1,0:T(8,128)(2,1)S(1)}, bf16[16,4096]{1,0:T(8,128)(2,1)S(1)}, u32[]{:S(2)}, u32[]{:S(2)}) collective-permute-start(bf16[16,4096]{1,0:T(8,128)(2,1)S(1)} %add_convert_fusion.2), channel_id=1, source_target_pairs={{0,4},{1,5},{2,6},{3,7},{4,0},{5,1},{6,2},{7,3},{8,12},{9,13},{10,... | collective-permute-start | bytes 393224 | tf_op jit(solution)/shard_map/ppermute | solution.py:34
  98.7 7.4 %collective-permute-start.29 = (bf16[16,4096]{1,0:T(8,128)(2,1)S(1)}, bf16[16,4096]{1,0:T(8,128)(2,1)S(1)}, u32[]{:S(2)}, u32[]{:S(2)}) collective-permute-start(bf16[16,4096]{1,0:T(8,128)(2,1)S(1)} %add_convert_fusion.1), channel_id=1, source_target_pairs={{0,2},{1,3},{2,4},{3,5},{4,6},{5,7},{6,0},{7,1},{8,10},{9,11},{10,... | collective-permute-start | bytes 393224 | tf_op jit(solution)/shard_map/ppermute | solution.py:34
  100.9 6.5 %collective-permute-start.31 = (bf16[16,4096]{1,0:T(8,128)(2,1)S(1)}, bf16[16,4096]{1,0:T(8,128)(2,1)S(1)}, u32[]{:S(2)}, u32[]{:S(2)}) collective-permute-start(bf16[16,4096]{1,0:T(8,128)(2,1)S(1)} %add_convert_fusion), channel_id=1, source_target_pairs={{0,6},{1,7},{2,0},{3,1},{4,2},{5,3},{6,4},{7,5},{8,14},{9,15},{10,... | collective-permute-start | bytes 393224 | tf_op jit(solution)/shard_map/ppermute | solution.py:34
  (6 other events, 119.2 us)

commit v18 on v16

--- a/solution.py
+++ b/solution.py
@@ -253,23 +253,20 @@
     blocks = refs[:count]
     pick_rows, order, columns, gain, w_key, w_value = refs[count : count + 6]
     wide = len(refs) - count - 9 - extra
-    normed, own, *sent, rows = refs[-3 - wide :]
-    total, width = normed.shape
+    scaled, own, factor, *sent = refs[-3 - wide :]
+    total, width = scaled.shape
     tile = tile_of(width, 512)
     square = jnp.zeros((total, 1), f32)
     for start in range(0, width, tile):
         span = slice(start, start + tile)
         part = dot(pick_rows[...], jnp.concatenate([b[:, span] for b in blocks], axis=0))
-        rows[:, span] = part.astype(bf16)
+        own[:, span] = part[: own.shape[0], :].astype(bf16)
+        scaled[:, span] = (part * gain[:, span]).astype(bf16)
         square += jnp.sum(part * part, axis=1, keepdims=True)
-    own[...] = rows[: own.shape[0], :]
-    factor = lax.rsqrt(square / width + norm_eps)
-    for start in range(0, width, tile):
-        span = slice(start, start + tile)
-        part = rows[:, span].astype(f32) * factor * gain[:, span]
-        normed[:, span] = part.astype(bf16)
-    keys = dot(normed[...], w_key[...]).astype(bf16)
-    values = dot(normed[...], w_value[...]).astype(bf16)
+    rooted = lax.rsqrt(square / width + norm_eps)
+    factor[...] = jnp.broadcast_to(rooted, factor.shape)
+    keys = (dot(scaled[...], w_key[...]) * rooted).astype(bf16)
+    values = (dot(scaled[...], w_value[...]) * rooted).astype(bf16)
     both = jnp.concatenate([keys, values], axis=1)
     turned = lax.dot_general(
         columns[...], both, (((1,), (1,)), ((), ())), preferred_element_type=f32
@@ -280,8 +277,8 @@
         sent[dy][...] = turned[dy * each : (dy + 1) * each].astype(bf16)
 
 
-def query_body(normed, w_query, cosine, sine, query):
-    raw = dot(normed[...], w_query[...])
+def query_body(scaled, factor, w_query, cosine, sine, query):
+    raw = dot(scaled[...], w_query[...]) * factor[:, 0:1]
     for head in range(query.shape[1] // HEAD_DIM):
         span = slice(head * HEAD_DIM, (head + 1) * HEAD_DIM)
         one = raw[:, span]
@@ -432,11 +429,11 @@
     k_angles = freqs[:, None] * routed.astype(f32)
     k_cos, k_sin = jnp.cos(k_angles), jnp.sin(k_angles)
 
-    normed, own, *sent = kernel_call(
+    scaled, own, factor, *sent = kernel_call(
         functools.partial(kv_body, count, len(loaded)),
-        [((total, model), bf16), ((share, model), bf16)] + [((tall * each, total), bf16)] * wide,
+        [((total, model), bf16), ((share, model), bf16), ((total, 128), f32)]
+        + [((tall * each, total), bf16)] * wide,
         [*blocks, pick_rows, in_order, columns, attn_gain, w_key, w_value, *loaded],
-        [pltpu.VMEM((total, model), bf16)],
         flops=2 * total * model * 512,
     )
     arrived = exchange(sent, tall, wide)
@@ -444,7 +441,7 @@
     (query,) = kernel_call(
         query_body,
         [((total, heads_wide), bf16)],
-        [normed, w_query, q_cos, q_sin],
+        [scaled, factor, w_query, q_cos, q_sin],
         flops=2 * total * model * heads_wide,
     )
     attn_parts = kernel_call(

time: 108 us -> 107 us (level)
  transfers between devices with their start and end apart: 33 -> 33, of which waited for: 18 -> 17; matrix products, arithmetic and copies ran while one was open for 1% -> 1% of each run, Pallas kernels for 16% -> 16%
where the time goes in v18:
time: 107 us
  starting transfers between devices  44.4 us (41%)
  waiting for transfers between devices  34.5 us (32%)
  Pallas kernels  26 us (24%)
  other arithmetic  1.91 us (2%)
    ppermute x30, starting transfers between devices, shift(): return lax.ppermute(block, 'ctx', pairs)  40.2 us
    ppermute x30, waiting for transfers between devices, shift(): return lax.ppermute(block, 'ctx', pairs)  31.8 us
    pallas_call x5, Pallas kernels, load(): pl.pallas_call(functools.partial(load_body, len(arrays)), out_shape=[pltp...  15.9 us
    pallas_call x9, Pallas kernels, kernel_call(): pl.pallas_call(body, out_shape=[jax.ShapeDtypeStruct(s, d) for s, d in ou...  10.1 us
    ppermute x3, starting transfers between devices, exchange(): lax.ppermute(packed[k], 'ctx', pairs[k])  4.18 us
    ppermute x3, waiting for transfers between devices, exchange(): lax.ppermute(packed[k], 'ctx', pairs[k])  2.66 us
  transfers between devices with their start and end apart: 33, of which 17 were waited for; matrix products, arithmetic and copies ran while one was open for 1% of the time, Pallas kernels for 16%

profile of v18, /device:TPU:0, one launch (start us, length us, event | category | flops | bytes accessed | tf_op | source)
XLA Modules:
  0.0 107.0 jit_solution(12874609183512885198)
XLA Ops:
  0.0 1.6 %shard_map.136.refs_0_ = bf16[32,4096]{1,0:T(8,128)(2,1)S(1)} custom-call(s32[1]{0:T(128)} %bitcast.me, s32[1,128]{1,0:T(1,128)} %bitcast.4, bf16[128,4096]{1,0:T(8,128)(2,1)} %activations_in.1), custom_call_target="tpu_custom_call" | custom-call | flops 33554432 | bytes 1048576 | tf_op jit(solution)/shard_map/pallas_call | solution.py:140
  1.6 3.0 %collective-permute-start = (bf16[32,4096]{1,0:T(8,128)(2,1)S(1)}, bf16[32,4096]{1,0:T(8,128)(2,1)S(1)}, u32[]{:S(2)}, u32[]{:S(2)}) collective-permute-start(bf16[32,4096]{1,0:T(8,128)(2,1)S(1)} %shard_map.136.refs_0_), channel_id=1, source_target_pairs={{0,1},{1,0},{2,3},{3,2},{4,5},{5,4},{6,7},{7,6},{8,9},{9,8},{10,11... | collective-permute-start | bytes 786440 | tf_op jit(solution)/shard_map/ppermute | solution.py:34
  4.6 3.6 %collective-permute-start.4 = (bf16[32,4096]{1,0:T(8,128)(2,1)S(1)}, bf16[32,4096]{1,0:T(8,128)(2,1)S(1)}, u32[]{:S(2)}, u32[]{:S(2)}) collective-permute-start(bf16[32,4096]{1,0:T(8,128)(2,1)S(1)} %shard_map.136.refs_0_), channel_id=1, source_target_pairs={{0,6},{1,7},{2,0},{3,1},{4,2},{5,3},{6,4},{7,5},{8,14},{9,15},{10,... | collective-permute-start | bytes 786440 | tf_op jit(solution)/shard_map/ppermute | solution.py:34
  8.2 2.9 %shard_map.137 = (f32[1,4096]{1,0:T(1,128)S(1)}, bf16[4096,128]{1,0:T(8,128)(2,1)S(1)}, bf16[4096,128]{1,0:T(8,128)(2,1)S(1)}, bf16[4096,512]{1,0:T(8,128)(2,1)S(1)}, f32[8,128]{1,0:T(8,128)S(1)}) custom-call(bf16[32,4096]{1,0:T(8,128)(2,1)S(1)} %shard_map.136.refs_0_, f32[1,4096]{1,0:T(1,128)} %bitcast.8, bf16[4096,128]{1,0:T(8,128)(2,1)} %refs_2_.1, ...), custom_call_target="tpu_custom_call" | custom-call | bytes 12615680 | tf_op jit(solution)/shard_map/pallas_call | solution.py:165
  11.1 3.4 %shard_map.138 = (bf16[1024,4096]{1,0:T(8,128)(2,1)S(1)}, f32[8,128]{1,0:T(8,128)S(1)}) custom-call(f32[8,128]{1,0:T(8,128)S(1)} %get-tuple-element.47.refs_0_.refs_1_, bf16[1024,4096]{1,0:T(8,128)(2,1)} %refs_1_.4), custom_call_target="tpu_custom_call" | custom-call | bytes 16777216 | tf_op jit(solution)/shard_map/pallas_call | solution.py:165
  17.3 2.8 %collective-permute-done.1.refs_2_ = bf16[32,4096]{1,0:T(8,128)(2,1)S(1)} collective-permute-done((bf16[32,4096]{1,0:T(8,128)(2,1)S(1)}, bf16[32,4096]{1,0:T(8,128)(2,1)S(1)}, u32[]{:S(2)}, u32[]{:S(2)}) %collective-permute-start.1) | collective-permute-done | bytes 262176 | tf_op jit(solution)/shard_map/ppermute | solution.py:34
  21.3 2.6 %collective-permute-done.6.refs_2_.refs_7_ = bf16[32,4096]{1,0:T(8,128)(2,1)S(1)} collective-permute-done((bf16[32,4096]{1,0:T(8,128)(2,1)S(1)}, bf16[32,4096]{1,0:T(8,128)(2,1)S(1)}, u32[]{:S(2)}, u32[]{:S(2)}) %collective-permute-start.6) | collective-permute-done | bytes 262176 | tf_op jit(solution)/shard_map/ppermute | solution.py:34
  24.0 1.8 %collective-permute-done.5.refs_1_ = bf16[32,4096]{1,0:T(8,128)(2,1)S(1)} collective-permute-done((bf16[32,4096]{1,0:T(8,128)(2,1)S(1)}, bf16[32,4096]{1,0:T(8,128)(2,1)S(1)}, u32[]{:S(2)}, u32[]{:S(2)}) %collective-permute-start.5) | collective-permute-done | bytes 262176 | tf_op jit(solution)/shard_map/ppermute | solution.py:34
  27.2 3.4 %shard_map.143 = (bf16[4096,1024]{1,0:T(8,128)(2,1)S(1)}, f32[8,128]{1,0:T(8,128)S(1)}) custom-call(bf16[32,4096]{1,0:T(8,128)(2,1)S(1)} %shard_map.141.refs_0_.refs_4_, bf16[4096,1024]{1,0:T(8,128)(2,1)} %refs_1_.6), custom_call_target="tpu_custom_call" | custom-call | bytes 16777216 | tf_op jit(solution)/shard_map/pallas_call | solution.py:165
  30.6 2.2 %shard_map.142 = (bf16[512,4096]{1,0:T(8,128)(2,1)S(1)}, f32[8,128]{1,0:T(8,128)S(1)}) custom-call(bf16[32,4096]{1,0:T(8,128)(2,1)S(1)} %shard_map.141.refs_0_.refs_4_, bf16[512,4096]{1,0:T(8,128)(2,1)} %refs_1_.5), custom_call_target="tpu_custom_call" | custom-call | bytes 8388608 | tf_op jit(solution)/shard_map/pallas_call | solution.py:165
  36.4 3.3 %collective-permute-done.8.refs_1_ = bf16[128,128]{1,0:T(8,128)(2,1)S(1)} collective-permute-done((bf16[128,128]{1,0:T(8,128)(2,1)S(1)}, bf16[128,128]{1,0:T(8,128)(2,1)S(1)}, u32[]{:S(2)}, u32[]{:S(2)}) %collective-permute-start.8) | collective-permute-done | bytes 32800 | tf_op jit(solution)/shard_map/ppermute | solution.py:34
  39.7 2.1 %collective-permute-start.10 = (bf16[64,128]{1,0:T(8,128)(2,1)S(1)}, bf16[64,128]{1,0:T(8,128)(2,1)S(1)}, u32[]{:S(2)}, u32[]{:S(2)}) collective-permute-start(bf16[64,128]{1,0:T(8,128)(2,1)S(1)} %get-tuple-element.63), channel_id=1, source_target_pairs={{0,4},{1,5},{2,6},{3,7},{4,0},{5,1},{6,2},{7,3},{8,12},{9,13},{10,... | collective-permute-start | bytes 49160 | tf_op jit(solution)/shard_map/ppermute | solution.py:91
  41.8 1.6 %collective-permute-start.11 = (bf16[64,128]{1,0:T(8,128)(2,1)S(1)}, bf16[64,128]{1,0:T(8,128)(2,1)S(1)}, u32[]{:S(2)}, u32[]{:S(2)}) collective-permute-start(bf16[64,128]{1,0:T(8,128)(2,1)S(1)} %get-tuple-element.64), channel_id=1, source_target_pairs={{0,6},{1,7},{2,4},{3,5},{4,2},{5,3},{6,0},{7,1},{8,14},{9,15},{10,... | collective-permute-start | bytes 49160 | tf_op jit(solution)/shard_map/ppermute | solution.py:91
  44.7 2.7 %collective-permute-done.11.refs_3_ = bf16[64,128]{1,0:T(8,128)(2,1)S(1)} collective-permute-done((bf16[64,128]{1,0:T(8,128)(2,1)S(1)}, bf16[64,128]{1,0:T(8,128)(2,1)S(1)}, u32[]{:S(2)}, u32[]{:S(2)}) %collective-permute-start.11) | collective-permute-done | bytes 16416 | tf_op jit(solution)/shard_map/ppermute | solution.py:91
  47.4 1.7 %shard_map.147 = (bf16[16,4096]{1,0:T(8,128)(2,1)S(1)}, bf16[16,4096]{1,0:T(8,128)(2,1)S(1)}, bf16[16,4096]{1,0:T(8,128)(2,1)S(1)}, bf16[16,4096]{1,0:T(8,128)(2...) custom-call(bf16[64,128]{1,0:T(8,128)(2,1)S(1)} %get-tuple-element.6, ...), custom_call_target="tpu_custom_call" | custom-call | flops 536870912 | bytes 1048576 | tf_op jit(solution)/shard_map/pallas_call | solution.py:140
  49.0 1.5 %collective-permute-start.12 = (bf16[16,4096]{1,0:T(8,128)(2,1)S(1)}, bf16[16,4096]{1,0:T(8,128)(2,1)S(1)}, u32[]{:S(2)}, u32[]{:S(2)}) collective-permute-start(bf16[16,4096]{1,0:T(8,128)(2,1)S(1)} %get-tuple-element.71), channel_id=1, source_target_pairs={{0,1},{1,0},{2,3},{3,2},{4,5},{5,4},{6,7},{7,6},{8,9},{9,8},{10,11... | collective-permute-start | bytes 393224 | tf_op jit(solution)/shard_map/ppermute | solution.py:34
  54.3 1.7 %collective-permute-start.13 = (bf16[16,4096]{1,0:T(8,128)(2,1)S(1)}, bf16[16,4096]{1,0:T(8,128)(2,1)S(1)}, u32[]{:S(2)}, u32[]{:S(2)}) collective-permute-start(bf16[16,4096]{1,0:T(8,128)(2,1)S(1)} %add_convert_fusion.5), channel_id=1, source_target_pairs={{0,4},{1,5},{2,6},{3,7},{4,0},{5,1},{6,2},{7,3},{8,12},{9,13},{10,... | collective-permute-start | bytes 393224 | tf_op jit(solution)/shard_map/ppermute | solution.py:34
  57.1 2.9 %collective-permute-start.17 = (bf16[16,4096]{1,0:T(8,128)(2,1)S(1)}, bf16[16,4096]{1,0:T(8,128)(2,1)S(1)}, u32[]{:S(2)}, u32[]{:S(2)}) collective-permute-start(bf16[16,4096]{1,0:T(8,128)(2,1)S(1)} %add_convert_fusion.3), channel_id=1, source_target_pairs={{0,6},{1,7},{2,0},{3,1},{4,2},{5,3},{6,4},{7,5},{8,14},{9,15},{10,... | collective-permute-start | bytes 393224 | tf_op jit(solution)/shard_map/ppermute | solution.py:34
  60.0 1.6 %collective-permute-done.13 = bf16[16,4096]{1,0:T(8,128)(2,1)S(1)} collective-permute-done((bf16[16,4096]{1,0:T(8,128)(2,1)S(1)}, bf16[16,4096]{1,0:T(8,128)(2,1)S(1)}, u32[]{:S(2)}, u32[]{:S(2)}) %collective-permute-start.13) | collective-permute-done | bytes 131104 | tf_op jit(solution)/shard_map/ppermute | solution.py:34
  61.7 1.8 %collective-permute-done.15 = bf16[16,4096]{1,0:T(8,128)(2,1)S(1)} collective-permute-done((bf16[16,4096]{1,0:T(8,128)(2,1)S(1)}, bf16[16,4096]{1,0:T(8,128)(2,1)S(1)}, u32[]{:S(2)}, u32[]{:S(2)}) %collective-permute-start.15) | collective-permute-done | bytes 131104 | tf_op jit(solution)/shard_map/ppermute | solution.py:34
  63.5 4.8 %collective-permute-done.17 = bf16[16,4096]{1,0:T(8,128)(2,1)S(1)} collective-permute-done((bf16[16,4096]{1,0:T(8,128)(2,1)S(1)}, bf16[16,4096]{1,0:T(8,128)(2,1)S(1)}, u32[]{:S(2)}, u32[]{:S(2)}) %collective-permute-start.17) | collective-permute-done | bytes 131104 | tf_op jit(solution)/shard_map/ppermute | solution.py:34
  69.5 1.6 %collective-permute-start.22 = (bf16[16,4096]{1,0:T(8,128)(2,1)S(1)}, bf16[16,4096]{1,0:T(8,128)(2,1)S(1)}, u32[]{:S(2)}, u32[]{:S(2)}) collective-permute-start(bf16[16,4096]{1,0:T(8,128)(2,1)S(1)} %multiply_convert_fusion.refs_0_), channel_id=1, source_target_pairs={{0,4},{1,5},{2,6},{3,7},{4,0},{5,1},{6,2},{7,3},{8,12},{9,13},{10,... | collective-permute-start | bytes 393224 | tf_op jit(solution)/shard_map/ppermute | solution.py:34
  71.1 2.8 %collective-permute-start.24 = (bf16[16,4096]{1,0:T(8,128)(2,1)S(1)}, bf16[16,4096]{1,0:T(8,128)(2,1)S(1)}, u32[]{:S(2)}, u32[]{:S(2)}) collective-permute-start(bf16[16,4096]{1,0:T(8,128)(2,1)S(1)} %multiply_convert_fusion.refs_0_), channel_id=1, source_target_pairs={{0,6},{1,7},{2,0},{3,1},{4,2},{5,3},{6,4},{7,5},{8,14},{9,15},{10,... | collective-permute-start | bytes 393224 | tf_op jit(solution)/shard_map/ppermute | solution.py:34
  73.9 1.6 %collective-permute-start.19 = (bf16[16,4096]{1,0:T(8,128)(2,1)S(1)}, bf16[16,4096]{1,0:T(8,128)(2,1)S(1)}, u32[]{:S(2)}, u32[]{:S(2)}) collective-permute-start(bf16[16,4096]{1,0:T(8,128)(2,1)S(1)} %multiply_convert_fusion.refs_0_), channel_id=1, source_target_pairs={{0,1},{1,0},{2,3},{3,2},{4,5},{5,4},{6,7},{7,6},{8,9},{9,8},{10,11... | collective-permute-start | bytes 393224 | tf_op jit(solution)/shard_map/ppermute | solution.py:34
  76.0 2.2 %collective-permute-done.22.refs_4_ = bf16[16,4096]{1,0:T(8,128)(2,1)S(1)} collective-permute-done((bf16[16,4096]{1,0:T(8,128)(2,1)S(1)}, bf16[16,4096]{1,0:T(8,128)(2,1)S(1)}, u32[]{:S(2)}, u32[]{:S(2)}) %collective-permute-start.22) | collective-permute-done | bytes 131104 | tf_op jit(solution)/shard_map/ppermute | solution.py:34
  78.2 2.0 %collective-permute-start.25 = (bf16[16,4096]{1,0:T(8,128)(2,1)S(1)}, bf16[16,4096]{1,0:T(8,128)(2,1)S(1)}, u32[]{:S(2)}, u32[]{:S(2)}) collective-permute-start(bf16[16,4096]{1,0:T(8,128)(2,1)S(1)} %collective-permute-done.24.refs_6_), channel_id=1, source_target_pairs={{0,1},{1,0},{2,3},{3,2},{4,5},{5,4},{6,7},{7,6},{8,9},{9,8},{10,11... | collective-permute-start | bytes 393224 | tf_op jit(solution)/shard_map/ppermute | solution.py:34
  80.2 4.0 %shard_map.148 = (bf16[4096,1024]{1,0:T(8,128)(2,1)S(1)}, f32[8,128]{1,0:T(8,128)}) custom-call(bf16[16,4096]{1,0:T(8,128)(2,1)S(1)} %multiply_convert_fusion.refs_0_, bf16[4096,1024]{1,0:T(8,128)(2,1)} %refs_1_.7), custom_call_target="tpu_custom_call" | custom-call | bytes 16777216 | tf_op jit(solution)/shard_map/pallas_call | solution.py:165
  84.6 2.8 %collective-permute-done.25.refs_7_ = bf16[16,4096]{1,0:T(8,128)(2,1)S(1)} collective-permute-done((bf16[16,4096]{1,0:T(8,128)(2,1)S(1)}, bf16[16,4096]{1,0:T(8,128)(2,1)S(1)}, u32[]{:S(2)}, u32[]{:S(2)}) %collective-permute-start.25) | collective-permute-done | bytes 131104 | tf_op jit(solution)/shard_map/ppermute | solution.py:34
  87.4 3.7 %shard_map.149 = (bf16[16,4096]{1,0:T(8,128)(2,1)S(1)}, bf16[16,4096]{1,0:T(8,128)(2,1)S(1)}, bf16[16,4096]{1,0:T(8,128)(2,1)S(1)}, bf16[16,4096]{1,0:T(8,128)(2...) custom-call(bf16[16,4096]{1,0:T(8,128)(2,1)S(1)} %multiply_convert_f, ...), custom_call_target="tpu_custom_call" | custom-call | flops 3221225472 | bytes 1048576 | tf_op jit(solution)/shard_map/pallas_call | solution.py:140
  97.6 2.2 %collective-permute-start.29 = (bf16[16,4096]{1,0:T(8,128)(2,1)S(1)}, bf16[16,4096]{1,0:T(8,128)(2,1)S(1)}, u32[]{:S(2)}, u32[]{:S(2)}) collective-permute-start(bf16[16,4096]{1,0:T(8,128)(2,1)S(1)} %add_convert_fusion.1), channel_id=1, source_target_pairs={{0,2},{1,3},{2,4},{3,5},{4,6},{5,7},{6,0},{7,1},{8,10},{9,11},{10,... | collective-permute-start | bytes 393224 | tf_op jit(solution)/shard_map/ppermute | solution.py:34
  99.8 2.4 %collective-permute-start.31 = (bf16[16,4096]{1,0:T(8,128)(2,1)S(1)}, bf16[16,4096]{1,0:T(8,128)(2,1)S(1)}, u32[]{:S(2)}, u32[]{:S(2)}) collective-permute-start(bf16[16,4096]{1,0:T(8,128)(2,1)S(1)} %add_convert_fusion), channel_id=1, source_target_pairs={{0,6},{1,7},{2,0},{3,1},{4,2},{5,3},{6,4},{7,5},{8,14},{9,15},{10,... | collective-permute-start | bytes 393224 | tf_op jit(solution)/shard_map/ppermute | solution.py:34
  102.2 2.8 %collective-permute-done.27 = bf16[16,4096]{1,0:T(8,128)(2,1)S(1)} collective-permute-done((bf16[16,4096]{1,0:T(8,128)(2,1)S(1)}, bf16[16,4096]{1,0:T(8,128)(2,1)S(1)}, u32[]{:S(2)}, u32[]{:S(2)}) %collective-permute-start.27) | collective-permute-done | bytes 131104 | tf_op jit(solution)/shard_map/ppermute | solution.py:34
  (73 shorter events, 25.7 us)
Async XLA Ops:
  1.6 13.8 %collective-permute-start = (bf16[32,4096]{1,0:T(8,128)(2,1)S(1)}, bf16[32,4096]{1,0:T(8,128)(2,1)S(1)}, u32[]{:S(2)}, u32[]{:S(2)}) collective-permute-start(bf16[32,4096]{1,0:T(8,128)(2,1)S(1)} %shard_map.136.refs_0_), channel_id=1, source_target_pairs={{0,1},{1,0},{2,3},{3,2},{4,5},{5,4},{6,7},{7,6},{8,9},{9,8},{10,11... | collective-permute-start | bytes 786440 | tf_op jit(solution)/shard_map/ppermute | solution.py:34
  4.6 10.8 %collective-permute-start.4 = (bf16[32,4096]{1,0:T(8,128)(2,1)S(1)}, bf16[32,4096]{1,0:T(8,128)(2,1)S(1)}, u32[]{:S(2)}, u32[]{:S(2)}) collective-permute-start(bf16[32,4096]{1,0:T(8,128)(2,1)S(1)} %shard_map.136.refs_0_), channel_id=1, source_target_pairs={{0,6},{1,7},{2,0},{3,1},{4,2},{5,3},{6,4},{7,5},{8,14},{9,15},{10,... | collective-permute-start | bytes 786440 | tf_op jit(solution)/shard_map/ppermute | solution.py:34
  8.2 12.0 %collective-permute-start.1 = (bf16[32,4096]{1,0:T(8,128)(2,1)S(1)}, bf16[32,4096]{1,0:T(8,128)(2,1)S(1)}, u32[]{:S(2)}, u32[]{:S(2)}) collective-permute-start(bf16[32,4096]{1,0:T(8,128)(2,1)S(1)} %shard_map.136.refs_0_), channel_id=1, source_target_pairs={{0,2},{1,3},{2,4},{3,5},{4,6},{5,7},{6,0},{7,1},{8,10},{9,11},{10,... | collective-permute-start | bytes 786440 | tf_op jit(solution)/shard_map/ppermute | solution.py:34
  15.5 8.5 %collective-permute-start.6 = (bf16[32,4096]{1,0:T(8,128)(2,1)S(1)}, bf16[32,4096]{1,0:T(8,128)(2,1)S(1)}, u32[]{:S(2)}, u32[]{:S(2)}) collective-permute-start(bf16[32,4096]{1,0:T(8,128)(2,1)S(1)} %shard_map.140.refs_6_), channel_id=1, source_target_pairs={{0,1},{1,0},{2,3},{3,2},{4,5},{5,4},{6,7},{7,6},{8,9},{9,8},{10,11... | collective-permute-start | bytes 786440 | tf_op jit(solution)/shard_map/ppermute | solution.py:34
  16.1 9.7 %collective-permute-start.5 = (bf16[32,4096]{1,0:T(8,128)(2,1)S(1)}, bf16[32,4096]{1,0:T(8,128)(2,1)S(1)}, u32[]{:S(2)}, u32[]{:S(2)}) collective-permute-start(bf16[32,4096]{1,0:T(8,128)(2,1)S(1)} %shard_map.140.refs_6_), channel_id=1, source_target_pairs={{2,0},{3,1},{4,2},{5,3},{10,8},{11,9},{12,10},{13,11},{18,16},{19,... | collective-permute-start | bytes 786440 | tf_op jit(solution)/shard_map/ppermute | solution.py:34
  20.2 5.6 %collective-permute-start.3 = (bf16[32,4096]{1,0:T(8,128)(2,1)S(1)}, bf16[32,4096]{1,0:T(8,128)(2,1)S(1)}, u32[]{:S(2)}, u32[]{:S(2)}) collective-permute-start(bf16[32,4096]{1,0:T(8,128)(2,1)S(1)} %collective-permute-done.1.refs_2_), channel_id=1, source_target_pairs={{2,4},{3,5},{4,6},{5,7},{10,12},{11,13},{12,14},{13,15},{18,20},{1... | collective-permute-start | bytes 786440 | tf_op jit(solution)/shard_map/ppermute | solution.py:34
  20.9 12.0 %collective-permute-start.2 = (bf16[32,4096]{1,0:T(8,128)(2,1)S(1)}, bf16[32,4096]{1,0:T(8,128)(2,1)S(1)}, u32[]{:S(2)}, u32[]{:S(2)}) collective-permute-start(bf16[32,4096]{1,0:T(8,128)(2,1)S(1)} %collective-permute-done.1.refs_2_), channel_id=1, source_target_pairs={{0,1},{1,0},{2,3},{3,2},{4,5},{5,4},{6,7},{7,6},{8,9},{9,8},{10,11... | collective-permute-start | bytes 786440 | tf_op jit(solution)/shard_map/ppermute | solution.py:34
  25.8 8.5 %collective-permute-start.7 = (bf16[32,4096]{1,0:T(8,128)(2,1)S(1)}, bf16[32,4096]{1,0:T(8,128)(2,1)S(1)}, u32[]{:S(2)}, u32[]{:S(2)}) collective-permute-start(bf16[32,4096]{1,0:T(8,128)(2,1)S(1)} %shard_map.141.refs_0_.refs_4_), channel_id=1, source_target_pairs={{0,1},{1,0},{2,3},{3,2},{4,5},{5,4},{6,7},{7,6},{8,9},{9,8},{10,11... | collective-permute-start | bytes 786440 | tf_op jit(solution)/shard_map/ppermute | solution.py:34
  35.7 4.0 %collective-permute-start.8 = (bf16[128,128]{1,0:T(8,128)(2,1)S(1)}, bf16[128,128]{1,0:T(8,128)(2,1)S(1)}, u32[]{:S(2)}, u32[]{:S(2)}) collective-permute-start(bf16[128,128]{1,0:T(8,128)(2,1)S(1)} %get-tuple-element.60), channel_id=1, source_target_pairs={{0,1},{1,0},{2,3},{3,2},{4,5},{5,4},{6,7},{7,6},{8,9},{9,8},{10,11... | collective-permute-start | bytes 98312 | tf_op jit(solution)/shard_map/ppermute | solution.py:34
  39.7 5.0 %collective-permute-start.10 = (bf16[64,128]{1,0:T(8,128)(2,1)S(1)}, bf16[64,128]{1,0:T(8,128)(2,1)S(1)}, u32[]{:S(2)}, u32[]{:S(2)}) collective-permute-start(bf16[64,128]{1,0:T(8,128)(2,1)S(1)} %get-tuple-element.63), channel_id=1, source_target_pairs={{0,4},{1,5},{2,6},{3,7},{4,0},{5,1},{6,2},{7,3},{8,12},{9,13},{10,... | collective-permute-start | bytes 49160 | tf_op jit(solution)/shard_map/ppermute | solution.py:91
  41.8 5.5 %collective-permute-start.11 = (bf16[64,128]{1,0:T(8,128)(2,1)S(1)}, bf16[64,128]{1,0:T(8,128)(2,1)S(1)}, u32[]{:S(2)}, u32[]{:S(2)}) collective-permute-start(bf16[64,128]{1,0:T(8,128)(2,1)S(1)} %get-tuple-element.64), channel_id=1, source_target_pairs={{0,6},{1,7},{2,4},{3,5},{4,2},{5,3},{6,0},{7,1},{8,14},{9,15},{10,... | collective-permute-start | bytes 49160 | tf_op jit(solution)/shard_map/ppermute | solution.py:91
  49.0 5.2 %collective-permute-start.12 = (bf16[16,4096]{1,0:T(8,128)(2,1)S(1)}, bf16[16,4096]{1,0:T(8,128)(2,1)S(1)}, u32[]{:S(2)}, u32[]{:S(2)}) collective-permute-start(bf16[16,4096]{1,0:T(8,128)(2,1)S(1)} %get-tuple-element.71), channel_id=1, source_target_pairs={{0,1},{1,0},{2,3},{3,2},{4,5},{5,4},{6,7},{7,6},{8,9},{9,8},{10,11... | collective-permute-start | bytes 393224 | tf_op jit(solution)/shard_map/ppermute | solution.py:34
  50.5 5.5 %collective-permute-start.14 = (bf16[16,4096]{1,0:T(8,128)(2,1)S(1)}, bf16[16,4096]{1,0:T(8,128)(2,1)S(1)}, u32[]{:S(2)}, u32[]{:S(2)}) collective-permute-start(bf16[16,4096]{1,0:T(8,128)(2,1)S(1)} %get-tuple-element.73), channel_id=1, source_target_pairs={{0,1},{1,0},{2,3},{3,2},{4,5},{5,4},{6,7},{7,6},{8,9},{9,8},{10,11... | collective-permute-start | bytes 393224 | tf_op jit(solution)/shard_map/ppermute | solution.py:34
  51.1 6.0 %collective-permute-start.16 = (bf16[16,4096]{1,0:T(8,128)(2,1)S(1)}, bf16[16,4096]{1,0:T(8,128)(2,1)S(1)}, u32[]{:S(2)}, u32[]{:S(2)}) collective-permute-start(bf16[16,4096]{1,0:T(8,128)(2,1)S(1)} %get-tuple-element.75), channel_id=1, source_target_pairs={{0,1},{1,0},{2,3},{3,2},{4,5},{5,4},{6,7},{7,6},{8,9},{9,8},{10,11... | collective-permute-start | bytes 393224 | tf_op jit(solution)/shard_map/ppermute | solution.py:34
  52.6 7.5 %collective-permute-start.18 = (bf16[16,4096]{1,0:T(8,128)(2,1)S(1)}, bf16[16,4096]{1,0:T(8,128)(2,1)S(1)}, u32[]{:S(2)}, u32[]{:S(2)}) collective-permute-start(bf16[16,4096]{1,0:T(8,128)(2,1)S(1)} %get-tuple-element.77), channel_id=1, source_target_pairs={{0,1},{1,0},{2,3},{3,2},{4,5},{5,4},{6,7},{7,6},{8,9},{9,8},{10,11... | collective-permute-start | bytes 393224 | tf_op jit(solution)/shard_map/ppermute | solution.py:34
  54.3 7.4 %collective-permute-start.13 = (bf16[16,4096]{1,0:T(8,128)(2,1)S(1)}, bf16[16,4096]{1,0:T(8,128)(2,1)S(1)}, u32[]{:S(2)}, u32[]{:S(2)}) collective-permute-start(bf16[16,4096]{1,0:T(8,128)(2,1)S(1)} %add_convert_fusion.5), channel_id=1, source_target_pairs={{0,4},{1,5},{2,6},{3,7},{4,0},{5,1},{6,2},{7,3},{8,12},{9,13},{10,... | collective-permute-start | bytes 393224 | tf_op jit(solution)/shard_map/ppermute | solution.py:34
  56.1 7.4 %collective-permute-start.15 = (bf16[16,4096]{1,0:T(8,128)(2,1)S(1)}, bf16[16,4096]{1,0:T(8,128)(2,1)S(1)}, u32[]{:S(2)}, u32[]{:S(2)}) collective-permute-start(bf16[16,4096]{1,0:T(8,128)(2,1)S(1)} %add_convert_fusion.4), channel_id=1, source_target_pairs={{0,2},{1,3},{2,4},{3,5},{4,6},{5,7},{6,0},{7,1},{8,10},{9,11},{10,... | collective-permute-start | bytes 393224 | tf_op jit(solution)/shard_map/ppermute | solution.py:34
  57.1 11.1 %collective-permute-start.17 = (bf16[16,4096]{1,0:T(8,128)(2,1)S(1)}, bf16[16,4096]{1,0:T(8,128)(2,1)S(1)}, u32[]{:S(2)}, u32[]{:S(2)}) collective-permute-start(bf16[16,4096]{1,0:T(8,128)(2,1)S(1)} %add_convert_fusion.3), channel_id=1, source_target_pairs={{0,6},{1,7},{2,0},{3,1},{4,2},{5,3},{6,4},{7,5},{8,14},{9,15},{10,... | collective-permute-start | bytes 393224 | tf_op jit(solution)/shard_map/ppermute | solution.py:34
  68.7 7.0 %collective-permute-start.20 = (bf16[16,4096]{1,0:T(8,128)(2,1)S(1)}, bf16[16,4096]{1,0:T(8,128)(2,1)S(1)}, u32[]{:S(2)}, u32[]{:S(2)}) collective-permute-start(bf16[16,4096]{1,0:T(8,128)(2,1)S(1)} %multiply_convert_fusion.refs_0_), channel_id=1, source_target_pairs={{0,2},{1,3},{2,4},{3,5},{4,6},{5,7},{6,0},{7,1},{8,10},{9,11},{10,... | collective-permute-start | bytes 393224 | tf_op jit(solution)/shard_map/ppermute | solution.py:34
  69.5 8.7 %collective-permute-start.22 = (bf16[16,4096]{1,0:T(8,128)(2,1)S(1)}, bf16[16,4096]{1,0:T(8,128)(2,1)S(1)}, u32[]{:S(2)}, u32[]{:S(2)}) collective-permute-start(bf16[16,4096]{1,0:T(8,128)(2,1)S(1)} %multiply_convert_fusion.refs_0_), channel_id=1, source_target_pairs={{0,4},{1,5},{2,6},{3,7},{4,0},{5,1},{6,2},{7,3},{8,12},{9,13},{10,... | collective-permute-start | bytes 393224 | tf_op jit(solution)/shard_map/ppermute | solution.py:34
  71.1 7.1 %collective-permute-start.24 = (bf16[16,4096]{1,0:T(8,128)(2,1)S(1)}, bf16[16,4096]{1,0:T(8,128)(2,1)S(1)}, u32[]{:S(2)}, u32[]{:S(2)}) collective-permute-start(bf16[16,4096]{1,0:T(8,128)(2,1)S(1)} %multiply_convert_fusion.refs_0_), channel_id=1, source_target_pairs={{0,6},{1,7},{2,0},{3,1},{4,2},{5,3},{6,4},{7,5},{8,14},{9,15},{10,... | collective-permute-start | bytes 393224 | tf_op jit(solution)/shard_map/ppermute | solution.py:34
  73.9 10.2 %collective-permute-start.19 = (bf16[16,4096]{1,0:T(8,128)(2,1)S(1)}, bf16[16,4096]{1,0:T(8,128)(2,1)S(1)}, u32[]{:S(2)}, u32[]{:S(2)}) collective-permute-start(bf16[16,4096]{1,0:T(8,128)(2,1)S(1)} %multiply_convert_fusion.refs_0_), channel_id=1, source_target_pairs={{0,1},{1,0},{2,3},{3,2},{4,5},{5,4},{6,7},{7,6},{8,9},{9,8},{10,11... | collective-permute-start | bytes 393224 | tf_op jit(solution)/shard_map/ppermute | solution.py:34
  75.7 8.5 %collective-permute-start.21 = (bf16[16,4096]{1,0:T(8,128)(2,1)S(1)}, bf16[16,4096]{1,0:T(8,128)(2,1)S(1)}, u32[]{:S(2)}, u32[]{:S(2)}) collective-permute-start(bf16[16,4096]{1,0:T(8,128)(2,1)S(1)} %collective-permute-done.20.refs_2_), channel_id=1, source_target_pairs={{0,1},{1,0},{2,3},{3,2},{4,5},{5,4},{6,7},{7,6},{8,9},{9,8},{10,11... | collective-permute-start | bytes 393224 | tf_op jit(solution)/shard_map/ppermute | solution.py:34
  78.2 6.4 %collective-permute-start.23 = (bf16[16,4096]{1,0:T(8,128)(2,1)S(1)}, bf16[16,4096]{1,0:T(8,128)(2,1)S(1)}, u32[]{:S(2)}, u32[]{:S(2)}) collective-permute-start(bf16[16,4096]{1,0:T(8,128)(2,1)S(1)} %collective-permute-done.22.refs_4_), channel_id=1, source_target_pairs={{0,1},{1,0},{2,3},{3,2},{4,5},{5,4},{6,7},{7,6},{8,9},{9,8},{10,11... | collective-permute-start | bytes 393224 | tf_op jit(solution)/shard_map/ppermute | solution.py:34
  78.2 9.2 %collective-permute-start.25 = (bf16[16,4096]{1,0:T(8,128)(2,1)S(1)}, bf16[16,4096]{1,0:T(8,128)(2,1)S(1)}, u32[]{:S(2)}, u32[]{:S(2)}) collective-permute-start(bf16[16,4096]{1,0:T(8,128)(2,1)S(1)} %collective-permute-done.24.refs_6_), channel_id=1, source_target_pairs={{0,1},{1,0},{2,3},{3,2},{4,5},{5,4},{6,7},{7,6},{8,9},{9,8},{10,11... | collective-permute-start | bytes 393224 | tf_op jit(solution)/shard_map/ppermute | solution.py:34
  91.1 5.0 %collective-permute-start.26 = (bf16[16,4096]{1,0:T(8,128)(2,1)S(1)}, bf16[16,4096]{1,0:T(8,128)(2,1)S(1)}, u32[]{:S(2)}, u32[]{:S(2)}) collective-permute-start(bf16[16,4096]{1,0:T(8,128)(2,1)S(1)} %get-tuple-element.82), channel_id=1, source_target_pairs={{0,1},{1,0},{2,3},{3,2},{4,5},{5,4},{6,7},{7,6},{8,9},{9,8},{10,11... | collective-permute-start | bytes 393224 | tf_op jit(solution)/shard_map/ppermute | solution.py:34
  92.2 5.3 %collective-permute-start.28 = (bf16[16,4096]{1,0:T(8,128)(2,1)S(1)}, bf16[16,4096]{1,0:T(8,128)(2,1)S(1)}, u32[]{:S(2)}, u32[]{:S(2)}) collective-permute-start(bf16[16,4096]{1,0:T(8,128)(2,1)S(1)} %get-tuple-element.84), channel_id=1, source_target_pairs={{0,1},{1,0},{2,3},{3,2},{4,5},{5,4},{6,7},{7,6},{8,9},{9,8},{10,11... | collective-permute-start | bytes 393224 | tf_op jit(solution)/shard_map/ppermute | solution.py:34
  93.2 6.6 %collective-permute-start.30 = (bf16[16,4096]{1,0:T(8,128)(2,1)S(1)}, bf16[16,4096]{1,0:T(8,128)(2,1)S(1)}, u32[]{:S(2)}, u32[]{:S(2)}) collective-permute-start(bf16[16,4096]{1,0:T(8,128)(2,1)S(1)} %get-tuple-element.86), channel_id=1, source_target_pairs={{0,1},{1,0},{2,3},{3,2},{4,5},{5,4},{6,7},{7,6},{8,9},{9,8},{10,11... | collective-permute-start | bytes 393224 | tf_op jit(solution)/shard_map/ppermute | solution.py:34
  94.3 7.9 %collective-permute-start.32 = (bf16[16,4096]{1,0:T(8,128)(2,1)S(1)}, bf16[16,4096]{1,0:T(8,128)(2,1)S(1)}, u32[]{:S(2)}, u32[]{:S(2)}) collective-permute-start(bf16[16,4096]{1,0:T(8,128)(2,1)S(1)} %get-tuple-element.88), channel_id=1, source_target_pairs={{0,1},{1,0},{2,3},{3,2},{4,5},{5,4},{6,7},{7,6},{8,9},{9,8},{10,11... | collective-permute-start | bytes 393224 | tf_op jit(solution)/shard_map/ppermute | solution.py:34
  96.2 8.8 %collective-permute-start.27 = (bf16[16,4096]{1,0:T(8,128)(2,1)S(1)}, bf16[16,4096]{1,0:T(8,128)(2,1)S(1)}, u32[]{:S(2)}, u32[]{:S(2)}) collective-permute-start(bf16[16,4096]{1,0:T(8,128)(2,1)S(1)} %add_convert_fusion.2), channel_id=1, source_target_pairs={{0,4},{1,5},{2,6},{3,7},{4,0},{5,1},{6,2},{7,3},{8,12},{9,13},{10,... | collective-permute-start | bytes 393224 | tf_op jit(solution)/shard_map/ppermute | solution.py:34
  97.6 7.4 %collective-permute-start.29 = (bf16[16,4096]{1,0:T(8,128)(2,1)S(1)}, bf16[16,4096]{1,0:T(8,128)(2,1)S(1)}, u32[]{:S(2)}, u32[]{:S(2)}) collective-permute-start(bf16[16,4096]{1,0:T(8,128)(2,1)S(1)} %add_convert_fusion.1), channel_id=1, source_target_pairs={{0,2},{1,3},{2,4},{3,5},{4,6},{5,7},{6,0},{7,1},{8,10},{9,11},{10,... | collective-permute-start | bytes 393224 | tf_op jit(solution)/shard_map/ppermute | solution.py:34
  99.8 6.5 %collective-permute-start.31 = (bf16[16,4096]{1,0:T(8,128)(2,1)S(1)}, bf16[16,4096]{1,0:T(8,128)(2,1)S(1)}, u32[]{:S(2)}, u32[]{:S(2)}) collective-permute-start(bf16[16,4096]{1,0:T(8,128)(2,1)S(1)} %add_convert_fusion), channel_id=1, source_target_pairs={{0,6},{1,7},{2,0},{3,1},{4,2},{5,3},{6,4},{7,5},{8,14},{9,15},{10,... | collective-permute-start | bytes 393224 | tf_op jit(solution)/shard_map/ppermute | solution.py:34
  (6 other events, 117.3 us)

commit v19 on v18

--- a/solution.py
+++ b/solution.py
@@ -100,7 +100,7 @@
 
 
 def sum_order(tall):
-    return [tall // 2, *range(1, tall // 2), *range(tall // 2 + 1, tall), 0]
+    return [tall // 2, *range(tall - 1, tall // 2, -1), *range(tall // 2 - 1, -1, -1)]
 
 
 def store_parts(parts, tall, wide, span, product, back):

time: 107 us -> 109 us (1.019)
  transfers between devices with their start and end apart: 33 -> 33, of which waited for: 17 -> 18; matrix products, arithmetic and copies ran while one was open for 1% -> 1% of each run, Pallas kernels for 16% -> 16%
where the time goes in v19:
time: 109 us; the launch traced here: 108 us
  starting transfers between devices  44.6 us (41%)
  waiting for transfers between devices  35.5 us (33%)
  Pallas kernels  26 us (24%)
  other arithmetic  1.91 us (2%)
    ppermute x30, starting transfers between devices, shift(): return lax.ppermute(block, 'ctx', pairs)  40.5 us
    ppermute x30, waiting for transfers between devices, shift(): return lax.ppermute(block, 'ctx', pairs)  32.8 us
    pallas_call x5, Pallas kernels, load(): pl.pallas_call(functools.partial(load_body, len(arrays)), out_shape=[pltp...  15.9 us
    pallas_call x9, Pallas kernels, kernel_call(): pl.pallas_call(body, out_shape=[jax.ShapeDtypeStruct(s, d) for s, d in ou...  10.1 us
    ppermute x3, starting transfers between devices, exchange(): lax.ppermute(packed[k], 'ctx', pairs[k])  4.18 us
    ppermute x3, waiting for transfers between devices, exchange(): lax.ppermute(packed[k], 'ctx', pairs[k])  2.66 us
  transfers between devices with their start and end apart: 33, of which 18 were waited for; matrix products, arithmetic and copies ran while one was open for 1% of the time, Pallas kernels for 16%

profile of v19, /device:TPU:0, one launch (start us, length us, event | category | flops | bytes accessed | tf_op | source)
XLA Modules:
  0.0 108.3 jit_solution(3230842183922883688)
XLA Ops:
  0.0 1.6 %shard_map.136.refs_0_ = bf16[32,4096]{1,0:T(8,128)(2,1)S(1)} custom-call(s32[1]{0:T(128)} %bitcast.me, s32[1,128]{1,0:T(1,128)} %bitcast.4, bf16[128,4096]{1,0:T(8,128)(2,1)} %activations_in.1), custom_call_target="tpu_custom_call" | custom-call | flops 33554432 | bytes 1048576 | tf_op jit(solution)/shard_map/pallas_call | solution.py:140
  1.6 3.0 %collective-permute-start = (bf16[32,4096]{1,0:T(8,128)(2,1)S(1)}, bf16[32,4096]{1,0:T(8,128)(2,1)S(1)}, u32[]{:S(2)}, u32[]{:S(2)}) collective-permute-start(bf16[32,4096]{1,0:T(8,128)(2,1)S(1)} %shard_map.136.refs_0_), channel_id=1, source_target_pairs={{0,1},{1,0},{2,3},{3,2},{4,5},{5,4},{6,7},{7,6},{8,9},{9,8},{10,11... | collective-permute-start | bytes 786440 | tf_op jit(solution)/shard_map/ppermute | solution.py:34
  4.6 3.6 %collective-permute-start.4 = (bf16[32,4096]{1,0:T(8,128)(2,1)S(1)}, bf16[32,4096]{1,0:T(8,128)(2,1)S(1)}, u32[]{:S(2)}, u32[]{:S(2)}) collective-permute-start(bf16[32,4096]{1,0:T(8,128)(2,1)S(1)} %shard_map.136.refs_0_), channel_id=1, source_target_pairs={{0,6},{1,7},{2,0},{3,1},{4,2},{5,3},{6,4},{7,5},{8,14},{9,15},{10,... | collective-permute-start | bytes 786440 | tf_op jit(solution)/shard_map/ppermute | solution.py:34
  8.2 2.9 %shard_map.137 = (f32[1,4096]{1,0:T(1,128)S(1)}, bf16[4096,128]{1,0:T(8,128)(2,1)S(1)}, bf16[4096,128]{1,0:T(8,128)(2,1)S(1)}, bf16[4096,512]{1,0:T(8,128)(2,1)S(1)}, f32[8,128]{1,0:T(8,128)S(1)}) custom-call(bf16[32,4096]{1,0:T(8,128)(2,1)S(1)} %shard_map.136.refs_0_, f32[1,4096]{1,0:T(1,128)} %bitcast.8, bf16[4096,128]{1,0:T(8,128)(2,1)} %refs_2_.1, ...), custom_call_target="tpu_custom_call" | custom-call | bytes 12615680 | tf_op jit(solution)/shard_map/pallas_call | solution.py:165
  11.1 3.4 %shard_map.138 = (bf16[1024,4096]{1,0:T(8,128)(2,1)S(1)}, f32[8,128]{1,0:T(8,128)S(1)}) custom-call(f32[8,128]{1,0:T(8,128)S(1)} %get-tuple-element.47.refs_0_.refs_1_, bf16[1024,4096]{1,0:T(8,128)(2,1)} %refs_1_.4), custom_call_target="tpu_custom_call" | custom-call | bytes 16777216 | tf_op jit(solution)/shard_map/pallas_call | solution.py:165
  17.3 2.8 %collective-permute-done.1.refs_2_ = bf16[32,4096]{1,0:T(8,128)(2,1)S(1)} collective-permute-done((bf16[32,4096]{1,0:T(8,128)(2,1)S(1)}, bf16[32,4096]{1,0:T(8,128)(2,1)S(1)}, u32[]{:S(2)}, u32[]{:S(2)}) %collective-permute-start.1) | collective-permute-done | bytes 262176 | tf_op jit(solution)/shard_map/ppermute | solution.py:34
  21.3 2.6 %collective-permute-done.6.refs_2_.refs_7_ = bf16[32,4096]{1,0:T(8,128)(2,1)S(1)} collective-permute-done((bf16[32,4096]{1,0:T(8,128)(2,1)S(1)}, bf16[32,4096]{1,0:T(8,128)(2,1)S(1)}, u32[]{:S(2)}, u32[]{:S(2)}) %collective-permute-start.6) | collective-permute-done | bytes 262176 | tf_op jit(solution)/shard_map/ppermute | solution.py:34
  24.0 1.8 %collective-permute-done.5.refs_1_ = bf16[32,4096]{1,0:T(8,128)(2,1)S(1)} collective-permute-done((bf16[32,4096]{1,0:T(8,128)(2,1)S(1)}, bf16[32,4096]{1,0:T(8,128)(2,1)S(1)}, u32[]{:S(2)}, u32[]{:S(2)}) %collective-permute-start.5) | collective-permute-done | bytes 262176 | tf_op jit(solution)/shard_map/ppermute | solution.py:34
  27.2 3.4 %shard_map.143 = (bf16[4096,1024]{1,0:T(8,128)(2,1)S(1)}, f32[8,128]{1,0:T(8,128)S(1)}) custom-call(bf16[32,4096]{1,0:T(8,128)(2,1)S(1)} %shard_map.141.refs_0_.refs_4_, bf16[4096,1024]{1,0:T(8,128)(2,1)} %refs_1_.6), custom_call_target="tpu_custom_call" | custom-call | bytes 16777216 | tf_op jit(solution)/shard_map/pallas_call | solution.py:165
  30.6 2.2 %shard_map.142 = (bf16[512,4096]{1,0:T(8,128)(2,1)S(1)}, f32[8,128]{1,0:T(8,128)S(1)}) custom-call(bf16[32,4096]{1,0:T(8,128)(2,1)S(1)} %shard_map.141.refs_0_.refs_4_, bf16[512,4096]{1,0:T(8,128)(2,1)} %refs_1_.5), custom_call_target="tpu_custom_call" | custom-call | bytes 8388608 | tf_op jit(solution)/shard_map/pallas_call | solution.py:165
  36.4 3.3 %collective-permute-done.8.refs_1_ = bf16[128,128]{1,0:T(8,128)(2,1)S(1)} collective-permute-done((bf16[128,128]{1,0:T(8,128)(2,1)S(1)}, bf16[128,128]{1,0:T(8,128)(2,1)S(1)}, u32[]{:S(2)}, u32[]{:S(2)}) %collective-permute-start.8) | collective-permute-done | bytes 32800 | tf_op jit(solution)/shard_map/ppermute | solution.py:34
  39.7 2.1 %collective-permute-start.10 = (bf16[64,128]{1,0:T(8,128)(2,1)S(1)}, bf16[64,128]{1,0:T(8,128)(2,1)S(1)}, u32[]{:S(2)}, u32[]{:S(2)}) collective-permute-start(bf16[64,128]{1,0:T(8,128)(2,1)S(1)} %get-tuple-element.63), channel_id=1, source_target_pairs={{0,4},{1,5},{2,6},{3,7},{4,0},{5,1},{6,2},{7,3},{8,12},{9,13},{10,... | collective-permute-start | bytes 49160 | tf_op jit(solution)/shard_map/ppermute | solution.py:91
  41.8 1.6 %collective-permute-start.11 = (bf16[64,128]{1,0:T(8,128)(2,1)S(1)}, bf16[64,128]{1,0:T(8,128)(2,1)S(1)}, u32[]{:S(2)}, u32[]{:S(2)}) collective-permute-start(bf16[64,128]{1,0:T(8,128)(2,1)S(1)} %get-tuple-element.64), channel_id=1, source_target_pairs={{0,6},{1,7},{2,4},{3,5},{4,2},{5,3},{6,0},{7,1},{8,14},{9,15},{10,... | collective-permute-start | bytes 49160 | tf_op jit(solution)/shard_map/ppermute | solution.py:91
  44.7 2.7 %collective-permute-done.11.refs_3_ = bf16[64,128]{1,0:T(8,128)(2,1)S(1)} collective-permute-done((bf16[64,128]{1,0:T(8,128)(2,1)S(1)}, bf16[64,128]{1,0:T(8,128)(2,1)S(1)}, u32[]{:S(2)}, u32[]{:S(2)}) %collective-permute-start.11) | collective-permute-done | bytes 16416 | tf_op jit(solution)/shard_map/ppermute | solution.py:91
  47.4 1.7 %shard_map.147 = (bf16[16,4096]{1,0:T(8,128)(2,1)S(1)}, bf16[16,4096]{1,0:T(8,128)(2,1)S(1)}, bf16[16,4096]{1,0:T(8,128)(2,1)S(1)}, bf16[16,4096]{1,0:T(8,128)(2...) custom-call(bf16[64,128]{1,0:T(8,128)(2,1)S(1)} %get-tuple-element.6, ...), custom_call_target="tpu_custom_call" | custom-call | flops 536870912 | bytes 1048576 | tf_op jit(solution)/shard_map/pallas_call | solution.py:140
  54.3 1.7 %collective-permute-start.13 = (bf16[16,4096]{1,0:T(8,128)(2,1)S(1)}, bf16[16,4096]{1,0:T(8,128)(2,1)S(1)}, u32[]{:S(2)}, u32[]{:S(2)}) collective-permute-start(bf16[16,4096]{1,0:T(8,128)(2,1)S(1)} %add_convert_fusion.5), channel_id=1, source_target_pairs={{0,4},{1,5},{2,6},{3,7},{4,0},{5,1},{6,2},{7,3},{8,12},{9,13},{10,... | collective-permute-start | bytes 393224 | tf_op jit(solution)/shard_map/ppermute | solution.py:34
  56.1 1.8 %collective-permute-start.15 = (bf16[16,4096]{1,0:T(8,128)(2,1)S(1)}, bf16[16,4096]{1,0:T(8,128)(2,1)S(1)}, u32[]{:S(2)}, u32[]{:S(2)}) collective-permute-start(bf16[16,4096]{1,0:T(8,128)(2,1)S(1)} %add_convert_fusion.4), channel_id=1, source_target_pairs={{0,6},{1,7},{2,0},{3,1},{4,2},{5,3},{6,4},{7,5},{8,14},{9,15},{10,... | collective-permute-start | bytes 393224 | tf_op jit(solution)/shard_map/ppermute | solution.py:34
  58.5 3.2 %collective-permute-done.13 = bf16[16,4096]{1,0:T(8,128)(2,1)S(1)} collective-permute-done((bf16[16,4096]{1,0:T(8,128)(2,1)S(1)}, bf16[16,4096]{1,0:T(8,128)(2,1)S(1)}, u32[]{:S(2)}, u32[]{:S(2)}) %collective-permute-start.13) | collective-permute-done | bytes 131104 | tf_op jit(solution)/shard_map/ppermute | solution.py:34
  61.7 4.1 %collective-permute-done.15 = bf16[16,4096]{1,0:T(8,128)(2,1)S(1)} collective-permute-done((bf16[16,4096]{1,0:T(8,128)(2,1)S(1)}, bf16[16,4096]{1,0:T(8,128)(2,1)S(1)}, u32[]{:S(2)}, u32[]{:S(2)}) %collective-permute-start.15) | collective-permute-done | bytes 131104 | tf_op jit(solution)/shard_map/ppermute | solution.py:34
  66.5 3.1 %collective-permute-start.20 = (bf16[16,4096]{1,0:T(8,128)(2,1)S(1)}, bf16[16,4096]{1,0:T(8,128)(2,1)S(1)}, u32[]{:S(2)}, u32[]{:S(2)}) collective-permute-start(bf16[16,4096]{1,0:T(8,128)(2,1)S(1)} %multiply_convert_fusion.refs_0_), channel_id=1, source_target_pairs={{0,2},{1,3},{2,4},{3,5},{4,6},{5,7},{6,0},{7,1},{8,10},{9,11},{10,... | collective-permute-start | bytes 393224 | tf_op jit(solution)/shard_map/ppermute | solution.py:34
  71.0 2.8 %collective-permute-start.24 = (bf16[16,4096]{1,0:T(8,128)(2,1)S(1)}, bf16[16,4096]{1,0:T(8,128)(2,1)S(1)}, u32[]{:S(2)}, u32[]{:S(2)}) collective-permute-start(bf16[16,4096]{1,0:T(8,128)(2,1)S(1)} %multiply_convert_fusion.refs_0_), channel_id=1, source_target_pairs={{0,6},{1,7},{2,0},{3,1},{4,2},{5,3},{6,4},{7,5},{8,14},{9,15},{10,... | collective-permute-start | bytes 393224 | tf_op jit(solution)/shard_map/ppermute | solution.py:34
  73.8 1.6 %collective-permute-start.19 = (bf16[16,4096]{1,0:T(8,128)(2,1)S(1)}, bf16[16,4096]{1,0:T(8,128)(2,1)S(1)}, u32[]{:S(2)}, u32[]{:S(2)}) collective-permute-start(bf16[16,4096]{1,0:T(8,128)(2,1)S(1)} %multiply_convert_fusion.refs_0_), channel_id=1, source_target_pairs={{0,1},{1,0},{2,3},{3,2},{4,5},{5,4},{6,7},{7,6},{8,9},{9,8},{10,11... | collective-permute-start | bytes 393224 | tf_op jit(solution)/shard_map/ppermute | solution.py:34
  77.5 1.5 %collective-permute-start.25 = (bf16[16,4096]{1,0:T(8,128)(2,1)S(1)}, bf16[16,4096]{1,0:T(8,128)(2,1)S(1)}, u32[]{:S(2)}, u32[]{:S(2)}) collective-permute-start(bf16[16,4096]{1,0:T(8,128)(2,1)S(1)} %collective-permute-done.24.refs_6_), channel_id=1, source_target_pairs={{0,1},{1,0},{2,3},{3,2},{4,5},{5,4},{6,7},{7,6},{8,9},{9,8},{10,11... | collective-permute-start | bytes 393224 | tf_op jit(solution)/shard_map/ppermute | solution.py:34
  79.0 4.0 %shard_map.148 = (bf16[4096,1024]{1,0:T(8,128)(2,1)S(1)}, f32[8,128]{1,0:T(8,128)}) custom-call(bf16[16,4096]{1,0:T(8,128)(2,1)S(1)} %multiply_convert_fusion.refs_0_, bf16[4096,1024]{1,0:T(8,128)(2,1)} %refs_1_.7), custom_call_target="tpu_custom_call" | custom-call | bytes 16777216 | tf_op jit(solution)/shard_map/pallas_call | solution.py:165
  83.3 2.8 %collective-permute-done.25.refs_7_ = bf16[16,4096]{1,0:T(8,128)(2,1)S(1)} collective-permute-done((bf16[16,4096]{1,0:T(8,128)(2,1)S(1)}, bf16[16,4096]{1,0:T(8,128)(2,1)S(1)}, u32[]{:S(2)}, u32[]{:S(2)}) %collective-permute-start.25) | collective-permute-done | bytes 131104 | tf_op jit(solution)/shard_map/ppermute | solution.py:34
  86.1 3.7 %shard_map.149 = (bf16[16,4096]{1,0:T(8,128)(2,1)S(1)}, bf16[16,4096]{1,0:T(8,128)(2,1)S(1)}, bf16[16,4096]{1,0:T(8,128)(2,1)S(1)}, bf16[16,4096]{1,0:T(8,128)(2...) custom-call(bf16[16,4096]{1,0:T(8,128)(2,1)S(1)} %multiply_convert_f, ...), custom_call_target="tpu_custom_call" | custom-call | flops 3221225472 | bytes 1048576 | tf_op jit(solution)/shard_map/pallas_call | solution.py:140
  89.8 2.3 %collective-permute-start.26 = (bf16[16,4096]{1,0:T(8,128)(2,1)S(1)}, bf16[16,4096]{1,0:T(8,128)(2,1)S(1)}, u32[]{:S(2)}, u32[]{:S(2)}) collective-permute-start(bf16[16,4096]{1,0:T(8,128)(2,1)S(1)} %get-tuple-element.82), channel_id=1, source_target_pairs={{0,1},{1,0},{2,3},{3,2},{4,5},{5,4},{6,7},{7,6},{8,9},{9,8},{10,11... | collective-permute-start | bytes 393224 | tf_op jit(solution)/shard_map/ppermute | solution.py:34
  92.2 1.9 %collective-permute-start.30 = (bf16[16,4096]{1,0:T(8,128)(2,1)S(1)}, bf16[16,4096]{1,0:T(8,128)(2,1)S(1)}, u32[]{:S(2)}, u32[]{:S(2)}) collective-permute-start(bf16[16,4096]{1,0:T(8,128)(2,1)S(1)} %get-tuple-element.86), channel_id=1, source_target_pairs={{0,1},{1,0},{2,3},{3,2},{4,5},{5,4},{6,7},{7,6},{8,9},{9,8},{10,11... | collective-permute-start | bytes 393224 | tf_op jit(solution)/shard_map/ppermute | solution.py:34
  95.1 2.0 %collective-permute-start.27 = (bf16[16,4096]{1,0:T(8,128)(2,1)S(1)}, bf16[16,4096]{1,0:T(8,128)(2,1)S(1)}, u32[]{:S(2)}, u32[]{:S(2)}) collective-permute-start(bf16[16,4096]{1,0:T(8,128)(2,1)S(1)} %add_convert_fusion.2), channel_id=1, source_target_pairs={{0,4},{1,5},{2,6},{3,7},{4,0},{5,1},{6,2},{7,3},{8,12},{9,13},{10,... | collective-permute-start | bytes 393224 | tf_op jit(solution)/shard_map/ppermute | solution.py:34
  97.2 3.4 %collective-permute-start.29 = (bf16[16,4096]{1,0:T(8,128)(2,1)S(1)}, bf16[16,4096]{1,0:T(8,128)(2,1)S(1)}, u32[]{:S(2)}, u32[]{:S(2)}) collective-permute-start(bf16[16,4096]{1,0:T(8,128)(2,1)S(1)} %add_convert_fusion.1), channel_id=1, source_target_pairs={{0,6},{1,7},{2,0},{3,1},{4,2},{5,3},{6,4},{7,5},{8,14},{9,15},{10,... | collective-permute-start | bytes 393224 | tf_op jit(solution)/shard_map/ppermute | solution.py:34
  100.8 1.8 %collective-permute-done.27 = bf16[16,4096]{1,0:T(8,128)(2,1)S(1)} collective-permute-done((bf16[16,4096]{1,0:T(8,128)(2,1)S(1)}, bf16[16,4096]{1,0:T(8,128)(2,1)S(1)}, u32[]{:S(2)}, u32[]{:S(2)}) %collective-permute-start.27) | collective-permute-done | bytes 131104 | tf_op jit(solution)/shard_map/ppermute | solution.py:34
  103.2 4.3 %collective-permute-done.31 = bf16[16,4096]{1,0:T(8,128)(2,1)S(1)} collective-permute-done((bf16[16,4096]{1,0:T(8,128)(2,1)S(1)}, bf16[16,4096]{1,0:T(8,128)(2,1)S(1)}, u32[]{:S(2)}, u32[]{:S(2)}) %collective-permute-start.31) | collective-permute-done | bytes 131104 | tf_op jit(solution)/shard_map/ppermute | solution.py:34
  (73 shorter events, 23.0 us)
Async XLA Ops:
  1.6 13.8 %collective-permute-start = (bf16[32,4096]{1,0:T(8,128)(2,1)S(1)}, bf16[32,4096]{1,0:T(8,128)(2,1)S(1)}, u32[]{:S(2)}, u32[]{:S(2)}) collective-permute-start(bf16[32,4096]{1,0:T(8,128)(2,1)S(1)} %shard_map.136.refs_0_), channel_id=1, source_target_pairs={{0,1},{1,0},{2,3},{3,2},{4,5},{5,4},{6,7},{7,6},{8,9},{9,8},{10,11... | collective-permute-start | bytes 786440 | tf_op jit(solution)/shard_map/ppermute | solution.py:34
  4.6 10.8 %collective-permute-start.4 = (bf16[32,4096]{1,0:T(8,128)(2,1)S(1)}, bf16[32,4096]{1,0:T(8,128)(2,1)S(1)}, u32[]{:S(2)}, u32[]{:S(2)}) collective-permute-start(bf16[32,4096]{1,0:T(8,128)(2,1)S(1)} %shard_map.136.refs_0_), channel_id=1, source_target_pairs={{0,6},{1,7},{2,0},{3,1},{4,2},{5,3},{6,4},{7,5},{8,14},{9,15},{10,... | collective-permute-start | bytes 786440 | tf_op jit(solution)/shard_map/ppermute | solution.py:34
  8.2 12.0 %collective-permute-start.1 = (bf16[32,4096]{1,0:T(8,128)(2,1)S(1)}, bf16[32,4096]{1,0:T(8,128)(2,1)S(1)}, u32[]{:S(2)}, u32[]{:S(2)}) collective-permute-start(bf16[32,4096]{1,0:T(8,128)(2,1)S(1)} %shard_map.136.refs_0_), channel_id=1, source_target_pairs={{0,2},{1,3},{2,4},{3,5},{4,6},{5,7},{6,0},{7,1},{8,10},{9,11},{10,... | collective-permute-start | bytes 786440 | tf_op jit(solution)/shard_map/ppermute | solution.py:34
  15.5 8.5 %collective-permute-start.6 = (bf16[32,4096]{1,0:T(8,128)(2,1)S(1)}, bf16[32,4096]{1,0:T(8,128)(2,1)S(1)}, u32[]{:S(2)}, u32[]{:S(2)}) collective-permute-start(bf16[32,4096]{1,0:T(8,128)(2,1)S(1)} %shard_map.140.refs_6_), channel_id=1, source_target_pairs={{0,1},{1,0},{2,3},{3,2},{4,5},{5,4},{6,7},{7,6},{8,9},{9,8},{10,11... | collective-permute-start | bytes 786440 | tf_op jit(solution)/shard_map/ppermute | solution.py:34
  16.1 9.7 %collective-permute-start.5 = (bf16[32,4096]{1,0:T(8,128)(2,1)S(1)}, bf16[32,4096]{1,0:T(8,128)(2,1)S(1)}, u32[]{:S(2)}, u32[]{:S(2)}) collective-permute-start(bf16[32,4096]{1,0:T(8,128)(2,1)S(1)} %shard_map.140.refs_6_), channel_id=1, source_target_pairs={{2,0},{3,1},{4,2},{5,3},{10,8},{11,9},{12,10},{13,11},{18,16},{19,... | collective-permute-start | bytes 786440 | tf_op jit(solution)/shard_map/ppermute | solution.py:34
  20.2 5.6 %collective-permute-start.3 = (bf16[32,4096]{1,0:T(8,128)(2,1)S(1)}, bf16[32,4096]{1,0:T(8,128)(2,1)S(1)}, u32[]{:S(2)}, u32[]{:S(2)}) collective-permute-start(bf16[32,4096]{1,0:T(8,128)(2,1)S(1)} %collective-permute-done.1.refs_2_), channel_id=1, source_target_pairs={{2,4},{3,5},{4,6},{5,7},{10,12},{11,13},{12,14},{13,15},{18,20},{1... | collective-permute-start | bytes 786440 | tf_op jit(solution)/shard_map/ppermute | solution.py:34
  20.9 12.0 %collective-permute-start.2 = (bf16[32,4096]{1,0:T(8,128)(2,1)S(1)}, bf16[32,4096]{1,0:T(8,128)(2,1)S(1)}, u32[]{:S(2)}, u32[]{:S(2)}) collective-permute-start(bf16[32,4096]{1,0:T(8,128)(2,1)S(1)} %collective-permute-done.1.refs_2_), channel_id=1, source_target_pairs={{0,1},{1,0},{2,3},{3,2},{4,5},{5,4},{6,7},{7,6},{8,9},{9,8},{10,11... | collective-permute-start | bytes 786440 | tf_op jit(solution)/shard_map/ppermute | solution.py:34
  25.8 8.5 %collective-permute-start.7 = (bf16[32,4096]{1,0:T(8,128)(2,1)S(1)}, bf16[32,4096]{1,0:T(8,128)(2,1)S(1)}, u32[]{:S(2)}, u32[]{:S(2)}) collective-permute-start(bf16[32,4096]{1,0:T(8,128)(2,1)S(1)} %shard_map.141.refs_0_.refs_4_), channel_id=1, source_target_pairs={{0,1},{1,0},{2,3},{3,2},{4,5},{5,4},{6,7},{7,6},{8,9},{9,8},{10,11... | collective-permute-start | bytes 786440 | tf_op jit(solution)/shard_map/ppermute | solution.py:34
  35.7 4.0 %collective-permute-start.8 = (bf16[128,128]{1,0:T(8,128)(2,1)S(1)}, bf16[128,128]{1,0:T(8,128)(2,1)S(1)}, u32[]{:S(2)}, u32[]{:S(2)}) collective-permute-start(bf16[128,128]{1,0:T(8,128)(2,1)S(1)} %get-tuple-element.60), channel_id=1, source_target_pairs={{0,1},{1,0},{2,3},{3,2},{4,5},{5,4},{6,7},{7,6},{8,9},{9,8},{10,11... | collective-permute-start | bytes 98312 | tf_op jit(solution)/shard_map/ppermute | solution.py:34
  39.7 5.0 %collective-permute-start.10 = (bf16[64,128]{1,0:T(8,128)(2,1)S(1)}, bf16[64,128]{1,0:T(8,128)(2,1)S(1)}, u32[]{:S(2)}, u32[]{:S(2)}) collective-permute-start(bf16[64,128]{1,0:T(8,128)(2,1)S(1)} %get-tuple-element.63), channel_id=1, source_target_pairs={{0,4},{1,5},{2,6},{3,7},{4,0},{5,1},{6,2},{7,3},{8,12},{9,13},{10,... | collective-permute-start | bytes 49160 | tf_op jit(solution)/shard_map/ppermute | solution.py:91
  41.8 5.5 %collective-permute-start.11 = (bf16[64,128]{1,0:T(8,128)(2,1)S(1)}, bf16[64,128]{1,0:T(8,128)(2,1)S(1)}, u32[]{:S(2)}, u32[]{:S(2)}) collective-permute-start(bf16[64,128]{1,0:T(8,128)(2,1)S(1)} %get-tuple-element.64), channel_id=1, source_target_pairs={{0,6},{1,7},{2,4},{3,5},{4,2},{5,3},{6,0},{7,1},{8,14},{9,15},{10,... | collective-permute-start | bytes 49160 | tf_op jit(solution)/shard_map/ppermute | solution.py:91
  49.0 5.2 %collective-permute-start.12 = (bf16[16,4096]{1,0:T(8,128)(2,1)S(1)}, bf16[16,4096]{1,0:T(8,128)(2,1)S(1)}, u32[]{:S(2)}, u32[]{:S(2)}) collective-permute-start(bf16[16,4096]{1,0:T(8,128)(2,1)S(1)} %get-tuple-element.71), channel_id=1, source_target_pairs={{0,1},{1,0},{2,3},{3,2},{4,5},{5,4},{6,7},{7,6},{8,9},{9,8},{10,11... | collective-permute-start | bytes 393224 | tf_op jit(solution)/shard_map/ppermute | solution.py:34
  50.5 5.5 %collective-permute-start.14 = (bf16[16,4096]{1,0:T(8,128)(2,1)S(1)}, bf16[16,4096]{1,0:T(8,128)(2,1)S(1)}, u32[]{:S(2)}, u32[]{:S(2)}) collective-permute-start(bf16[16,4096]{1,0:T(8,128)(2,1)S(1)} %get-tuple-element.73), channel_id=1, source_target_pairs={{0,1},{1,0},{2,3},{3,2},{4,5},{5,4},{6,7},{7,6},{8,9},{9,8},{10,11... | collective-permute-start | bytes 393224 | tf_op jit(solution)/shard_map/ppermute | solution.py:34
  51.1 6.7 %collective-permute-start.16 = (bf16[16,4096]{1,0:T(8,128)(2,1)S(1)}, bf16[16,4096]{1,0:T(8,128)(2,1)S(1)}, u32[]{:S(2)}, u32[]{:S(2)}) collective-permute-start(bf16[16,4096]{1,0:T(8,128)(2,1)S(1)} %get-tuple-element.75), channel_id=1, source_target_pairs={{0,1},{1,0},{2,3},{3,2},{4,5},{5,4},{6,7},{7,6},{8,9},{9,8},{10,11... | collective-permute-start | bytes 393224 | tf_op jit(solution)/shard_map/ppermute | solution.py:34
  52.6 5.9 %collective-permute-start.18 = (bf16[16,4096]{1,0:T(8,128)(2,1)S(1)}, bf16[16,4096]{1,0:T(8,128)(2,1)S(1)}, u32[]{:S(2)}, u32[]{:S(2)}) collective-permute-start(bf16[16,4096]{1,0:T(8,128)(2,1)S(1)} %get-tuple-element.77), channel_id=1, source_target_pairs={{0,1},{1,0},{2,3},{3,2},{4,5},{5,4},{6,7},{7,6},{8,9},{9,8},{10,11... | collective-permute-start | bytes 393224 | tf_op jit(solution)/shard_map/ppermute | solution.py:34
  54.3 7.4 %collective-permute-start.13 = (bf16[16,4096]{1,0:T(8,128)(2,1)S(1)}, bf16[16,4096]{1,0:T(8,128)(2,1)S(1)}, u32[]{:S(2)}, u32[]{:S(2)}) collective-permute-start(bf16[16,4096]{1,0:T(8,128)(2,1)S(1)} %add_convert_fusion.5), channel_id=1, source_target_pairs={{0,4},{1,5},{2,6},{3,7},{4,0},{5,1},{6,2},{7,3},{8,12},{9,13},{10,... | collective-permute-start | bytes 393224 | tf_op jit(solution)/shard_map/ppermute | solution.py:34
  56.1 9.8 %collective-permute-start.15 = (bf16[16,4096]{1,0:T(8,128)(2,1)S(1)}, bf16[16,4096]{1,0:T(8,128)(2,1)S(1)}, u32[]{:S(2)}, u32[]{:S(2)}) collective-permute-start(bf16[16,4096]{1,0:T(8,128)(2,1)S(1)} %add_convert_fusion.4), channel_id=1, source_target_pairs={{0,6},{1,7},{2,0},{3,1},{4,2},{5,3},{6,4},{7,5},{8,14},{9,15},{10,... | collective-permute-start | bytes 393224 | tf_op jit(solution)/shard_map/ppermute | solution.py:34
  57.9 8.3 %collective-permute-start.17 = (bf16[16,4096]{1,0:T(8,128)(2,1)S(1)}, bf16[16,4096]{1,0:T(8,128)(2,1)S(1)}, u32[]{:S(2)}, u32[]{:S(2)}) collective-permute-start(bf16[16,4096]{1,0:T(8,128)(2,1)S(1)} %add_convert_fusion.3), channel_id=1, source_target_pairs={{0,2},{1,3},{2,4},{3,5},{4,6},{5,7},{6,0},{7,1},{8,10},{9,11},{10,... | collective-permute-start | bytes 393224 | tf_op jit(solution)/shard_map/ppermute | solution.py:34
  66.5 8.9 %collective-permute-start.20 = (bf16[16,4096]{1,0:T(8,128)(2,1)S(1)}, bf16[16,4096]{1,0:T(8,128)(2,1)S(1)}, u32[]{:S(2)}, u32[]{:S(2)}) collective-permute-start(bf16[16,4096]{1,0:T(8,128)(2,1)S(1)} %multiply_convert_fusion.refs_0_), channel_id=1, source_target_pairs={{0,2},{1,3},{2,4},{3,5},{4,6},{5,7},{6,0},{7,1},{8,10},{9,11},{10,... | collective-permute-start | bytes 393224 | tf_op jit(solution)/shard_map/ppermute | solution.py:34
  69.7 7.3 %collective-permute-start.22 = (bf16[16,4096]{1,0:T(8,128)(2,1)S(1)}, bf16[16,4096]{1,0:T(8,128)(2,1)S(1)}, u32[]{:S(2)}, u32[]{:S(2)}) collective-permute-start(bf16[16,4096]{1,0:T(8,128)(2,1)S(1)} %multiply_convert_fusion.refs_0_), channel_id=1, source_target_pairs={{0,4},{1,5},{2,6},{3,7},{4,0},{5,1},{6,2},{7,3},{8,12},{9,13},{10,... | collective-permute-start | bytes 393224 | tf_op jit(solution)/shard_map/ppermute | solution.py:34
  71.0 6.5 %collective-permute-start.24 = (bf16[16,4096]{1,0:T(8,128)(2,1)S(1)}, bf16[16,4096]{1,0:T(8,128)(2,1)S(1)}, u32[]{:S(2)}, u32[]{:S(2)}) collective-permute-start(bf16[16,4096]{1,0:T(8,128)(2,1)S(1)} %multiply_convert_fusion.refs_0_), channel_id=1, source_target_pairs={{0,6},{1,7},{2,0},{3,1},{4,2},{5,3},{6,4},{7,5},{8,14},{9,15},{10,... | collective-permute-start | bytes 393224 | tf_op jit(solution)/shard_map/ppermute | solution.py:34
  73.8 9.2 %collective-permute-start.19 = (bf16[16,4096]{1,0:T(8,128)(2,1)S(1)}, bf16[16,4096]{1,0:T(8,128)(2,1)S(1)}, u32[]{:S(2)}, u32[]{:S(2)}) collective-permute-start(bf16[16,4096]{1,0:T(8,128)(2,1)S(1)} %multiply_convert_fusion.refs_0_), channel_id=1, source_target_pairs={{0,1},{1,0},{2,3},{3,2},{4,5},{5,4},{6,7},{7,6},{8,9},{9,8},{10,11... | collective-permute-start | bytes 393224 | tf_op jit(solution)/shard_map/ppermute | solution.py:34
  75.4 7.6 %collective-permute-start.21 = (bf16[16,4096]{1,0:T(8,128)(2,1)S(1)}, bf16[16,4096]{1,0:T(8,128)(2,1)S(1)}, u32[]{:S(2)}, u32[]{:S(2)}) collective-permute-start(bf16[16,4096]{1,0:T(8,128)(2,1)S(1)} %collective-permute-done.20.refs_2_), channel_id=1, source_target_pairs={{0,1},{1,0},{2,3},{3,2},{4,5},{5,4},{6,7},{7,6},{8,9},{9,8},{10,11... | collective-permute-start | bytes 393224 | tf_op jit(solution)/shard_map/ppermute | solution.py:34
  77.0 6.4 %collective-permute-start.23 = (bf16[16,4096]{1,0:T(8,128)(2,1)S(1)}, bf16[16,4096]{1,0:T(8,128)(2,1)S(1)}, u32[]{:S(2)}, u32[]{:S(2)}) collective-permute-start(bf16[16,4096]{1,0:T(8,128)(2,1)S(1)} %collective-permute-done.22.refs_4_), channel_id=1, source_target_pairs={{0,1},{1,0},{2,3},{3,2},{4,5},{5,4},{6,7},{7,6},{8,9},{9,8},{10,11... | collective-permute-start | bytes 393224 | tf_op jit(solution)/shard_map/ppermute | solution.py:34
  77.5 8.7 %collective-permute-start.25 = (bf16[16,4096]{1,0:T(8,128)(2,1)S(1)}, bf16[16,4096]{1,0:T(8,128)(2,1)S(1)}, u32[]{:S(2)}, u32[]{:S(2)}) collective-permute-start(bf16[16,4096]{1,0:T(8,128)(2,1)S(1)} %collective-permute-done.24.refs_6_), channel_id=1, source_target_pairs={{0,1},{1,0},{2,3},{3,2},{4,5},{5,4},{6,7},{7,6},{8,9},{9,8},{10,11... | collective-permute-start | bytes 393224 | tf_op jit(solution)/shard_map/ppermute | solution.py:34
  89.8 5.3 %collective-permute-start.26 = (bf16[16,4096]{1,0:T(8,128)(2,1)S(1)}, bf16[16,4096]{1,0:T(8,128)(2,1)S(1)}, u32[]{:S(2)}, u32[]{:S(2)}) collective-permute-start(bf16[16,4096]{1,0:T(8,128)(2,1)S(1)} %get-tuple-element.82), channel_id=1, source_target_pairs={{0,1},{1,0},{2,3},{3,2},{4,5},{5,4},{6,7},{7,6},{8,9},{9,8},{10,11... | collective-permute-start | bytes 393224 | tf_op jit(solution)/shard_map/ppermute | solution.py:34
  92.2 5.0 %collective-permute-start.28 = (bf16[16,4096]{1,0:T(8,128)(2,1)S(1)}, bf16[16,4096]{1,0:T(8,128)(2,1)S(1)}, u32[]{:S(2)}, u32[]{:S(2)}) collective-permute-start(bf16[16,4096]{1,0:T(8,128)(2,1)S(1)} %get-tuple-element.84), channel_id=1, source_target_pairs={{0,1},{1,0},{2,3},{3,2},{4,5},{5,4},{6,7},{7,6},{8,9},{9,8},{10,11... | collective-permute-start | bytes 393224 | tf_op jit(solution)/shard_map/ppermute | solution.py:34
  92.2 8.4 %collective-permute-start.30 = (bf16[16,4096]{1,0:T(8,128)(2,1)S(1)}, bf16[16,4096]{1,0:T(8,128)(2,1)S(1)}, u32[]{:S(2)}, u32[]{:S(2)}) collective-permute-start(bf16[16,4096]{1,0:T(8,128)(2,1)S(1)} %get-tuple-element.86), channel_id=1, source_target_pairs={{0,1},{1,0},{2,3},{3,2},{4,5},{5,4},{6,7},{7,6},{8,9},{9,8},{10,11... | collective-permute-start | bytes 393224 | tf_op jit(solution)/shard_map/ppermute | solution.py:34
  94.2 6.6 %collective-permute-start.32 = (bf16[16,4096]{1,0:T(8,128)(2,1)S(1)}, bf16[16,4096]{1,0:T(8,128)(2,1)S(1)}, u32[]{:S(2)}, u32[]{:S(2)}) collective-permute-start(bf16[16,4096]{1,0:T(8,128)(2,1)S(1)} %get-tuple-element.88), channel_id=1, source_target_pairs={{0,1},{1,0},{2,3},{3,2},{4,5},{5,4},{6,7},{7,6},{8,9},{9,8},{10,11... | collective-permute-start | bytes 393224 | tf_op jit(solution)/shard_map/ppermute | solution.py:34
  95.1 7.4 %collective-permute-start.27 = (bf16[16,4096]{1,0:T(8,128)(2,1)S(1)}, bf16[16,4096]{1,0:T(8,128)(2,1)S(1)}, u32[]{:S(2)}, u32[]{:S(2)}) collective-permute-start(bf16[16,4096]{1,0:T(8,128)(2,1)S(1)} %add_convert_fusion.2), channel_id=1, source_target_pairs={{0,4},{1,5},{2,6},{3,7},{4,0},{5,1},{6,2},{7,3},{8,12},{9,13},{10,... | collective-permute-start | bytes 393224 | tf_op jit(solution)/shard_map/ppermute | solution.py:34
  97.2 6.0 %collective-permute-start.29 = (bf16[16,4096]{1,0:T(8,128)(2,1)S(1)}, bf16[16,4096]{1,0:T(8,128)(2,1)S(1)}, u32[]{:S(2)}, u32[]{:S(2)}) collective-permute-start(bf16[16,4096]{1,0:T(8,128)(2,1)S(1)} %add_convert_fusion.1), channel_id=1, source_target_pairs={{0,6},{1,7},{2,0},{3,1},{4,2},{5,3},{6,4},{7,5},{8,14},{9,15},{10,... | collective-permute-start | bytes 393224 | tf_op jit(solution)/shard_map/ppermute | solution.py:34
  100.7 6.8 %collective-permute-start.31 = (bf16[16,4096]{1,0:T(8,128)(2,1)S(1)}, bf16[16,4096]{1,0:T(8,128)(2,1)S(1)}, u32[]{:S(2)}, u32[]{:S(2)}) collective-permute-start(bf16[16,4096]{1,0:T(8,128)(2,1)S(1)} %add_convert_fusion), channel_id=1, source_target_pairs={{0,2},{1,3},{2,4},{3,5},{4,6},{5,7},{6,0},{7,1},{8,10},{9,11},{10,... | collective-permute-start | bytes 393224 | tf_op jit(solution)/shard_map/ppermute | solution.py:34
  (6 other events, 113.1 us)
